TPU v7x, 32 devices: a whole 2x2x4 slice. The times are simulated.
32 devices in a mesh: row: 8 (over z, y), col: 4 (over x, core).
Axes of the slice: x: 2, y: 2, z: 4, core: 2. Of those that a mesh axis runs over, the one named last changes fastest.
Arguments:
- features: bfloat16 [8192, 256], P(('row', 'col')), may hold values from -6 to 6
- weight: bfloat16 [256, 256], replicated, may hold values from -0.375 to 0.375
- adj_tiles: bfloat16 [8, 4, 256, 128, 128], P('row', 'col'), may hold values from -0.078125 to 0.078125
- tile_rows: int32 [8, 4, 256], P('row', 'col'), may hold values from 0 to 7, as said below
- tile_cols: int32 [8, 4, 256], P('row', 'col'), may hold values from 0 to 15
- tile_counts: int32 [8, 4], P('row', 'col'), may hold values from 21 to 256, as said below
- out_grad: bfloat16 [8192, 256], P(('row', 'col')), may hold values from -6 to 6
Outputs:
- activations: bfloat16 [8192, 256], P(('row', 'col'))
- grad_features: bfloat16 [8192, 256], P(('row', 'col'))
- grad_weight: float32 [256, 256], replicated
Inputs may be any that keep to these rules, and one draw needn't show every extreme that they name: `tile_counts`: some device holds exactly 256 live slots in every draw. `tile_rows`: slots may name the same block pair; their values then add.
All inputs are finite; a program needn't handle non-finite values.
Results may differ from a plain program's by a relative error of at most 0.025.
Values may be sent and summed in bfloat16 or wider, within the bound.
No kernel may reach another device: no remote copies, remote signals or barrier semaphores. Data moves between devices by JAX's collectives and lax.ppermute only.
A program may use at most 128 MiB of HBM per device.

v0:
```python
import math

import jax
import jax.numpy as jnp
from jax import lax
from jax.sharding import PartitionSpec as P

tile_group = 16


def forward_tiles(total, tiles, rows, cols, count, blocks):
    groups = (count + tile_group - 1) // tile_group
    lanes = jnp.arange(tile_group, dtype=jnp.int32)

    def forward_step(index, acc):
        first = index * tile_group
        part_tiles = lax.dynamic_slice_in_dim(tiles, first, tile_group, 0)
        part_rows = lax.dynamic_slice_in_dim(rows, first, tile_group, 0)
        part_cols = lax.dynamic_slice_in_dim(cols, first, tile_group, 0)
        live = (first + lanes < count).astype(jnp.float32)
        prod = jnp.einsum(
            "gij,gjf->gif", part_tiles, blocks[part_cols], preferred_element_type=jnp.float32
        )
        return acc.at[part_rows].add(prod * live[:, None, None])

    return lax.fori_loop(0, groups, forward_step, total)


def backward_tiles(total, tiles, rows, cols, count, blocks):
    groups = (count + tile_group - 1) // tile_group
    lanes = jnp.arange(tile_group, dtype=jnp.int32)

    def backward_step(index, acc):
        first = index * tile_group
        part_tiles = lax.dynamic_slice_in_dim(tiles, first, tile_group, 0)
        part_rows = lax.dynamic_slice_in_dim(rows, first, tile_group, 0)
        part_cols = lax.dynamic_slice_in_dim(cols, first, tile_group, 0)
        live = (first + lanes < count).astype(jnp.float32)
        prod = jnp.einsum(
            "gji,gjf->gif", part_tiles, blocks[part_rows], preferred_element_type=jnp.float32
        )
        return acc.at[part_cols].add(prod * live[:, None, None])

    return lax.fori_loop(0, groups, backward_step, total)


def per_device(features, weight, adj_tiles, tile_rows, tile_cols, tile_counts, out_grad):
    node_rows, width = features.shape
    capacity = adj_tiles.shape[2]
    side = adj_tiles.shape[3]
    tiles = adj_tiles.reshape(capacity, side, side)
    rows = tile_rows.reshape(capacity)
    cols = tile_cols.reshape(capacity)
    count = tile_counts.reshape(())
    row_count = lax.axis_size("row")
    col_count = lax.axis_size("col")
    total_nodes = node_rows * row_count * col_count
    projected = jnp.dot(features, weight, preferred_element_type=jnp.float32).astype(jnp.bfloat16)
    gathered = lax.all_gather(projected, "row", axis=0, tiled=True)
    column_blocks = gathered.reshape(-1, side, width)
    row_blocks = col_count * node_rows // side
    empty_rows = jnp.zeros((row_blocks, side, width), jnp.float32)
    empty_cols = jnp.zeros((column_blocks.shape[0], side, width), jnp.float32)
    partial_value = forward_tiles(empty_rows, tiles, rows, cols, count, column_blocks)
    pre = lax.psum_scatter(
        partial_value.reshape(-1, width).astype(jnp.bfloat16),
        "col",
        scatter_dimension=0,
        tiled=True,
    ).astype(jnp.float32)
    sig = jax.nn.sigmoid(pre)
    activations = (pre * sig).astype(jnp.bfloat16)
    grad_pre = (out_grad.astype(jnp.float32) * sig * (1.0 + pre * (1.0 - sig))).astype(jnp.bfloat16)
    grad_group = lax.all_gather(grad_pre, "col", axis=0, tiled=True)
    grad_blocks = grad_group.reshape(-1, side, width)
    col_part = backward_tiles(empty_cols, tiles, rows, cols, count, grad_blocks)
    grad_proj = lax.psum_scatter(
        col_part.reshape(-1, width).astype(jnp.bfloat16), "row", scatter_dimension=0, tiled=True
    )
    grad_features = lax.dot_general(
        grad_proj, weight, (((1,), (1,)), ((), ())), preferred_element_type=jnp.float32
    ).astype(jnp.bfloat16)
    local_weight = lax.dot_general(
        features, grad_proj, (((0,), (0,)), ((), ())), preferred_element_type=jnp.float32
    ) * (1.0 / math.sqrt(total_nodes))
    grad_weight = lax.psum(local_weight, ("row", "col"))
    return (activations, grad_features, grad_weight)


def solution(mesh):
    placed = (
        P(("row", "col"), None),
        P(),
        P("row", "col", None, None, None),
        P("row", "col", None),
        P("row", "col", None),
        P("row", "col"),
        P(("row", "col"), None),
    )
    return jax.shard_map(
        per_device,
        mesh=mesh,
        in_specs=placed,
        out_specs=(P(("row", "col"), None), P(("row", "col"), None), P()),
        check_vma=False,
    )
```

profile of v0, /device:TPU:0, one launch (start us, length us, event | category | flops | bytes accessed | tf_op | source)
XLA Modules:
  0.0 554.9 jit_solution(6164200459092089226)
XLA Ops:
  8.1 1.7 convolution_convert_fusion.1
  10.6 43.0 %all-gather.2.cloned.1.call-done = bf16[2048,256]{1,0:T(8,128)(2,1)} async-done(((bf16[256,256]{1,0:T(8,128)(2,1)}), bf16[2048,256]{1,0:T(8,128)(2,1)}) %all-gather.2.cloned.1.call-update) | async-done | bytes 1048592 | tf_op jit(solution)/shard_map/all_gather | solution.py:59
  53.7 66.8 %while.22 = (s32[]{:T(128)}, f32[8,128,256]{2,1,0:T(8,128)S(1)}, s32[]{:T(128)}, s32[256]{0:T(256)}, bf16[256,128,128]{2,1,0:T(8,128)(2,1)}, /*index=5*/s32[256]...) while((s32[]{:T(128)}, f32[8,128,256]{2,1,0:T(8,128)S(1)}, ...), condition=%wide.region_2.3_spmd.clone, body=%wide.region_0.2_spmd.clone.sunk | while | flops 135267472 | bytes 12063475 | solution.py:26
  55.2 2.9 gather_fusion
  58.0 1.8 convolution_multiply_fusion.5
  59.8 2.2 scatter_fusion
  63.5 2.9 gather_fusion
  66.4 1.8 convolution_multiply_fusion.5
  68.2 2.2 scatter_fusion
  71.9 2.9 gather_fusion
  74.7 1.8 convolution_multiply_fusion.5
  76.5 2.2 scatter_fusion
  80.2 2.9 gather_fusion
  83.1 1.8 convolution_multiply_fusion.5
  84.9 2.2 scatter_fusion
  88.6 2.9 gather_fusion
  91.4 1.8 convolution_multiply_fusion.5
  93.2 2.2 scatter_fusion
  96.9 2.9 gather_fusion
  99.8 1.8 convolution_multiply_fusion.5
  101.6 2.2 scatter_fusion
  105.3 2.9 gather_fusion
  108.1 1.8 convolution_multiply_fusion.5
  109.9 2.2 scatter_fusion
  113.6 2.9 gather_fusion
  116.5 1.8 convolution_multiply_fusion.5
  118.3 2.2 scatter_fusion
  120.5 0.9 convert_element_type.45
  121.5 12.0 %copy.10 = bf16[1,1,256,128,128]{3,4,2,1,0:T(8,128)(2,1)} copy(bf16[1,1,256,128,128]{4,3,2,1,0:T(8,128)(2,1)} %bitcast.26) | data formatting | bytes 16777216 | tf_op args[2]
  133.5 73.8 %reduce-scatter.3.cloned.1.call-done = bf16[256,256]{1,0:T(8,128)(2,1)} async-done(((bf16[1024,256]{1,0:T(8,128)(2,1)}), bf16[256,256]{1,0:T(8,128)(2,1)}) %reduce-scatter.3.cloned.1.call-update) | async-done | bytes 131088 | tf_op jit(solution)/shard_map/reduce_scatter | solution.py:65
  207.3 1.7 fusion.15
  209.0 7.2 %all_gather.7 = bf16[1024,256]{1,0:T(8,128)(2,1)} all-gather(bf16[256,256]{1,0:T(8,128)(2,1)S(1)} %get-tuple-element.186), channel_id=1, replica_groups=mesh['row'=8,'col'=4] {'col'}, dimensions={0}, use_global_device_ids=true | all-gather | bytes 655360 | tf_op jit(solution)/shard_map/all_gather | solution.py:74
  216.2 1.6 broadcast_in_dim.21
  217.8 66.3 %while.23 = (s32[]{:T(128)}, f32[16,128,256]{2,1,0:T(8,128)}, s32[]{:T(128)}, s32[256]{0:T(256)S(1)}, bf16[256,128,128]{1,2,0:T(8,128)(2,1)}, /*index=5*/s32[256...) while((s32[]{:T(128)}, f32[16,128,256]{2,1,0:T(8,128)}, ...), condition=%wide.region_6.7_spmd.clone, body=%wide.region_4.6_spmd.clone.sunk | while | flops 135267472 | bytes 12063475 | solution.py:44
  218.5 1.7 gather_fusion.1
  220.2 1.5 convolution_multiply_fusion.6
  221.7 4.4 scatter_fusion.1
  226.8 1.7 gather_fusion.1
  228.5 1.5 convolution_multiply_fusion.6
  230.0 4.4 scatter_fusion.1
  235.1 1.7 gather_fusion.1
  236.8 1.5 convolution_multiply_fusion.6
  238.3 4.3 scatter_fusion.1
  243.4 1.7 gather_fusion.1
  245.0 1.5 convolution_multiply_fusion.6
  246.5 4.3 scatter_fusion.1
  251.6 1.7 gather_fusion.1
  253.2 1.5 convolution_multiply_fusion.6
  254.7 4.4 scatter_fusion.1
  259.8 1.7 gather_fusion.1
  261.5 1.5 convolution_multiply_fusion.6
  263.0 4.4 scatter_fusion.1
  268.1 1.7 gather_fusion.1
  269.8 1.5 convolution_multiply_fusion.6
  271.3 4.4 scatter_fusion.1
  276.4 1.7 gather_fusion.1
  278.1 1.5 convolution_multiply_fusion.6
  279.6 4.5 scatter_fusion.1
  284.0 2.7 convert_element_type.51
  286.8 129.7 %reduce-scatter.5.cloned.1.call-done = bf16[256,256]{1,0:T(8,128)(2,1)} async-done(((bf16[2048,256]{1,0:T(8,128)(2,1)}), bf16[256,256]{1,0:T(8,128)(2,1)}) %reduce-scatter.5.cloned.1.call-update) | async-done | bytes 131088 | tf_op jit(solution)/shard_map/reduce_scatter | solution.py:77
  416.5 1.8 fusion.8
  418.4 1.8 convolution_convert_fusion
  420.2 126.3 %all-reduce.2.cloned.1.call-done = f32[256,256]{0,1:T(8,128)} async-done(((f32[256,256]{0,1:T(8,128)}), f32[256,256]{0,1:T(8,128)}) %all-reduce.2.cloned.1.call-update) | async-done | bytes 262160 | tf_op jit(solution)/shard_map/psum | solution.py:86
  546.5 1.8 copy.12
  (67 shorter events, 18.5 us)
Async XLA Ops:
  7.2 0.9 copy-start
  7.2 46.4 %all-gather.2.cloned.1.call-start = ((), (), s32[]{:S(2)}) async-start(), calls=%async_computation.2 | async-start | bytes 1179648 | tf_op jit(solution)/shard_map/all_gather | solution.py:59
  9.8 197.4 %reduce-scatter.3.cloned.1.call-start = ((), (), s32[]{:S(2)}) async-start(), calls=%async_computation.3 | async-start | bytes 655360 | tf_op jit(solution)/shard_map/reduce_scatter | solution.py:65
  121.4 295.1 %reduce-scatter.5.cloned.1.call-start = ((), (), s32[]{:S(2)}) async-start(), calls=%async_computation.4 | async-start | bytes 1179648 | tf_op jit(solution)/shard_map/reduce_scatter | solution.py:77
  121.5 85.8 %copy-start.2 = (bf16[256,256]{1,0:T(8,128)(2,1)S(1)}, bf16[256,256]{1,0:T(8,128)(2,1)}, u32[]{:S(2)}) copy-start(bf16[256,256]{1,0:T(8,128)(2,1)} %param.17) | copy-start | bytes 393220
  133.5 84.3 %copy-start.3 = (s32[256]{0:T(256)S(1)}, s32[256]{0:T(256)}, u32[]{:S(2)}) copy-start(s32[256]{0:T(256)} %get-tuple-element.385) | copy-start | bytes 3076
  133.5 84.3 %copy-start.4 = (s32[256]{0:T(256)S(1)}, s32[256]{0:T(256)}, u32[]{:S(2)}) copy-start(s32[256]{0:T(256)} %get-tuple-element.386) | copy-start | bytes 3076
  284.0 134.4 %copy-start.1 = (bf16[256,256]{1,0:T(8,128)(2,1)S(1)}, bf16[256,256]{1,0:T(8,128)(2,1)}, u32[]{:S(2)}) copy-start(bf16[256,256]{1,0:T(8,128)(2,1)} %param.12) | copy-start | bytes 393220
  286.8 259.8 %all-reduce.2.cloned.1.call-start = ((), (), s32[]{:S(2)}) async-start(), calls=%async_computation.5 | async-start | bytes 524288 | tf_op jit(solution)/shard_map/psum | solution.py:86
Sparse Core Ops, SparseCore 0:
  10.7 42.8 all-gather.1
  121.6 85.6 reduce-scatter.2
  286.9 129.5 reduce-scatter.4
  422.5 124.0 all-reduce.1
where the time goes:
time: 559 us; the launch traced here: 555 us
  waiting for transfers between devices  373 us (67%)
  other arithmetic  75.4 us (13%)
  local copies, waits for them, and re-layouts  52.5 us (9%)
  matrix products  31.5 us (6%)
  between operations  14.5 us (3%)
  blocking collectives  7.22 us (1%)
    reduce_scatter x1, waiting for transfers between devices, per_device(): lax.psum_scatter(col_part.reshape(-1, width).astype(jnp.bfloat16), 'row',...  130 us
    psum x1, waiting for transfers between devices, per_device(): grad_weight = lax.psum(local_weight, ('row', 'col'))  126 us
    reduce_scatter x1, waiting for transfers between devices, per_device(): lax.psum_scatter(partial_value.reshape(-1, width).astype(jnp.bfloat16), '...  73.8 us
    all_gather x1, waiting for transfers between devices, per_device(): gathered = lax.all_gather(projected, 'row', axis=0, tiled=True)  43 us
    scatter-add x8, other arithmetic, backward_step(): return acc.at[part_cols].add(prod * live[:, None, None])  35.2 us
    gather x8, local copies, waits for them, and re-layouts, forward_step(): blocks[part_cols]  23 us
    scatter-add x8, other arithmetic, forward_step(): return acc.at[part_rows].add(prod * live[:, None, None])  17.6 us
    unnamed x12, local copies, waits for them, and re-layouts  14.7 us
  transfers between devices with their start and end apart: 4, of which 4 were waited for; matrix products, arithmetic and copies ran while one was open for 2% of the time, Pallas kernels for 0%

commit v1 on v0

v1 whole, which is shorter than its diff:
```python
import functools
import math

import jax
import jax.numpy as jnp
from jax import lax
from jax.experimental import pallas as pl
from jax.experimental.pallas import tpu as pltpu
from jax.sharding import PartitionSpec as P

chunk_tiles = 16
chunk_slots = 4
strips_per_step = 8
strip_slots = 8
vmem_bytes = 56 * 1024 * 1024


def build_kernel(rows_ref, cols_ref, count_ref, tiles_ref, dense_ref, total, held, sems, *, per_strip, strips, steps):
    side = tiles_ref.shape[1]
    first_strip = pl.program_id(0) * strips
    count = count_ref[0]
    chunks = (count + chunk_tiles - 1) // chunk_tiles

    def fetch(index):
        slot = lax.rem(index, chunk_slots)
        return pltpu.make_async_copy(
            tiles_ref.at[pl.ds(index * chunk_tiles, chunk_tiles)], held.at[slot], sems.at[slot]
        )

    for ahead in range(chunk_slots - 1):
        @pl.when(ahead < chunks)
        def _():
            fetch(ahead).start()

    def clear(strip, carry):
        total[strip] = jnp.zeros(total.shape[1:], jnp.float32)
        return carry

    lax.fori_loop(0, strips, clear, 0)

    def chunk_step(index, carry):
        @pl.when(index + chunk_slots - 1 < chunks)
        def _():
            fetch(index + chunk_slots - 1).start()

        fetch(index).wait()
        slot = lax.rem(index, chunk_slots)
        for lane in range(chunk_tiles):
            place = index * chunk_tiles + lane
            col = cols_ref[place]
            strip = col // per_strip - first_strip
            live = place < count
            if steps > 1:
                live = live & (strip >= 0) & (strip < strips)
            strip = jnp.where(live, strip, strips)
            down = pl.ds(pl.multiple_of(rows_ref[place] * side, side), side)
            along = pl.ds(pl.multiple_of(lax.rem(col, per_strip) * side, side), side)
            total[strip, down, along] += held[slot, lane].astype(jnp.float32)
        return carry

    lax.fori_loop(0, chunks, chunk_step, 0)

    def round_strip(strip, carry):
        dense_ref[strip] = total[strip].astype(jnp.bfloat16)
        return carry

    lax.fori_loop(0, strips, round_strip, 0)


def build_dense(rows, cols, count, tiles, row_blocks, col_strips, per_strip):
    capacity, side, _ = tiles.shape
    strips = min(strips_per_step, col_strips)
    steps = col_strips // strips
    high, wide = row_blocks * side, per_strip * side
    return pl.pallas_call(
        functools.partial(build_kernel, per_strip=per_strip, strips=strips, steps=steps),
        out_shape=jax.ShapeDtypeStruct((col_strips, high, wide), jnp.bfloat16),
        grid_spec=pltpu.PrefetchScalarGridSpec(
            num_scalar_prefetch=3,
            grid=(steps,),
            in_specs=[pl.BlockSpec(memory_space=pl.ANY)],
            out_specs=pl.BlockSpec((strips, high, wide), lambda i, *_: (i, 0, 0)),
            scratch_shapes=[
                pltpu.VMEM((strips + 1, high, wide), jnp.float32),
                pltpu.VMEM((chunk_slots, chunk_tiles, side, side), jnp.bfloat16),
                pltpu.SemaphoreType.DMA((chunk_slots,)),
            ],
        ),
        compiler_params=pltpu.CompilerParams(vmem_limit_bytes=vmem_bytes),
        cost_estimate=pl.CostEstimate(
            flops=capacity * side * side,
            bytes_accessed=2 * (capacity * side * side + col_strips * high * wide),
            transcendentals=0,
        ),
        name="build_dense",
    )(rows, cols, count, tiles)


def forward_kernel(source_ref, dense_ref, *refs):
    shards, (out_ref, held, total, sems) = refs[:-4], refs[-4:]
    slots = held.shape[0]

    def fetch(index):
        slot = index % slots
        return pltpu.make_async_copy(dense_ref.at[source_ref[index]], held.at[slot], sems.at[slot])

    for index in range(slots):
        fetch(index).start()
    for index, shard in enumerate(shards):
        fetch(index).wait()
        part = jnp.dot(held[index % slots], shard[...], preferred_element_type=jnp.float32)
        if index + slots < len(shards):
            fetch(index + slots).start()
        if index == 0:
            total[...] = part
        elif index < len(shards) - 1:
            total[...] += part
        else:
            out_ref[...] = (total[...] + part).astype(jnp.bfloat16)


def forward_product(source, dense, shards):
    strips, high, wide = dense.shape
    slots = min(strips, strip_slots)
    width = shards[0].shape[1]
    return pl.pallas_call(
        forward_kernel,
        out_shape=jax.ShapeDtypeStruct((high, width), jnp.bfloat16),
        in_specs=[pl.BlockSpec(memory_space=pltpu.SMEM), pl.BlockSpec(memory_space=pl.ANY)]
        + [pl.BlockSpec(memory_space=pltpu.VMEM)] * len(shards),
        out_specs=pl.BlockSpec(memory_space=pltpu.VMEM),
        scratch_shapes=[
            pltpu.VMEM((slots, high, wide), jnp.bfloat16),
            pltpu.VMEM((high, width), jnp.float32),
            pltpu.SemaphoreType.DMA((slots,)),
        ],
        compiler_params=pltpu.CompilerParams(vmem_limit_bytes=vmem_bytes),
        cost_estimate=pl.CostEstimate(
            flops=2 * strips * high * wide * width,
            bytes_accessed=2 * (strips * high * wide + strips * wide * width + high * width),
            transcendentals=0,
        ),
        name="forward_product",
    )(source, dense, *shards)


def middle_kernel(place_ref, parts_ref, weight_ref, cotangent_ref, act_ref, back_ref, *refs, scale):
    chunk_refs, product = refs[:-1], refs[-1]
    width = weight_ref.shape[0]
    aggregate = parts_ref[0].astype(jnp.float32)
    for index in range(1, parts_ref.shape[0]):
        aggregate += parts_ref[index].astype(jnp.float32)
    high = aggregate.astype(jnp.bfloat16)
    low = (aggregate - high.astype(jnp.float32)).astype(jnp.bfloat16)
    weight = weight_ref[...]
    pre = jnp.dot(high, weight, preferred_element_type=jnp.float32)
    pre += jnp.dot(low, weight, preferred_element_type=jnp.float32)
    sig = jax.nn.sigmoid(pre)
    act_ref[...] = (pre * sig).astype(jnp.bfloat16)
    grad = (cotangent_ref[...].astype(jnp.float32) * sig * (1.0 + pre * (1.0 - sig))).astype(jnp.bfloat16)
    back_ref[...] = lax.dot_general(
        grad, weight, (((1,), (1,)), ((), ())), preferred_element_type=jnp.float32
    ).astype(jnp.bfloat16)
    over_nodes = (((0,), (0,)), ((), ()))
    terms = lax.dot_general(high, grad, over_nodes, preferred_element_type=jnp.float32)
    terms += lax.dot_general(low, grad, over_nodes, preferred_element_type=jnp.float32)
    product[...] = terms * scale
    count = len(chunk_refs)
    rows = width // count
    for index, chunk_ref in enumerate(chunk_refs):
        first = lax.rem(place_ref[0] + index, count) * rows
        chunk_ref[...] = product[pl.ds(pl.multiple_of(first, rows), rows), :]


def middle(place, parts, weight, cotangent, total_nodes):
    count, rows, width = parts.shape
    return pl.pallas_call(
        functools.partial(middle_kernel, scale=1.0 / math.sqrt(total_nodes)),
        out_shape=[
            jax.ShapeDtypeStruct((rows, width), jnp.bfloat16),
            jax.ShapeDtypeStruct((rows, width), jnp.bfloat16),
        ]
        + [jax.ShapeDtypeStruct((width // count, width), jnp.float32)] * count,
        in_specs=[pl.BlockSpec(memory_space=pltpu.SMEM)] + [pl.BlockSpec(memory_space=pltpu.VMEM)] * 3,
        out_specs=[pl.BlockSpec(memory_space=pltpu.VMEM)] * (2 + count),
        scratch_shapes=[pltpu.VMEM((width, width), jnp.float32)],
        compiler_params=pltpu.CompilerParams(vmem_limit_bytes=vmem_bytes),
        cost_estimate=pl.CostEstimate(
            flops=10 * rows * width * width, bytes_accessed=2 * (count + 5) * rows * width, transcendentals=rows * width
        ),
        name="middle",
    )(place, parts, weight, cotangent)


def backward_kernel(dense_ref, grads_ref, out_ref, held, sems):
    strips, slots = dense_ref.shape[0], held.shape[0]

    def fetch(index):
        slot = index % slots
        return pltpu.make_async_copy(dense_ref.at[index], held.at[slot], sems.at[slot])

    for index in range(slots):
        fetch(index).start()
    grads = grads_ref[...].T
    for index in range(strips):
        fetch(index).wait()
        part = jnp.dot(grads, held[index % slots], preferred_element_type=jnp.float32)
        if index + slots < strips:
            fetch(index + slots).start()
        out_ref[index] = part.T.astype(jnp.bfloat16)


def backward_product(dense, grads):
    strips, high, wide = dense.shape
    slots = min(strips, strip_slots)
    width = grads.shape[1]
    return pl.pallas_call(
        backward_kernel,
        out_shape=jax.ShapeDtypeStruct((strips, wide, width), jnp.bfloat16),
        in_specs=[pl.BlockSpec(memory_space=pl.ANY), pl.BlockSpec(memory_space=pltpu.VMEM)],
        out_specs=pl.BlockSpec(memory_space=pltpu.VMEM),
        scratch_shapes=[
            pltpu.VMEM((slots, high, wide), jnp.bfloat16),
            pltpu.SemaphoreType.DMA((slots,)),
        ],
        compiler_params=pltpu.CompilerParams(vmem_limit_bytes=vmem_bytes),
        cost_estimate=pl.CostEstimate(
            flops=2 * strips * high * wide * width,
            bytes_accessed=2 * (strips * high * wide + strips * wide * width + high * width),
            transcendentals=0,
        ),
        name="backward_product",
    )(dense, grads)


def finish_kernel(place_ref, parts_ref, *refs):
    chunk_refs, (features_ref, weight_ref) = refs[:-2], refs[-2:]
    total = parts_ref[0].astype(jnp.float32)
    for index in range(1, parts_ref.shape[0]):
        total += parts_ref[index].astype(jnp.float32)
    features_ref[...] = total.astype(jnp.bfloat16)
    count = len(chunk_refs)
    rows = chunk_refs[0].shape[0]
    for index, chunk_ref in enumerate(chunk_refs):
        first = lax.rem(place_ref[0] + (count - index), count) * rows
        weight_ref[pl.ds(pl.multiple_of(first, rows), rows), :] = chunk_ref[...]


def finish(place, parts, chunks):
    count, rows, width = parts.shape
    return pl.pallas_call(
        finish_kernel,
        out_shape=[
            jax.ShapeDtypeStruct((rows, width), jnp.bfloat16),
            jax.ShapeDtypeStruct((len(chunks) * chunks[0].shape[0], width), jnp.float32),
        ],
        in_specs=[pl.BlockSpec(memory_space=pltpu.SMEM)] + [pl.BlockSpec(memory_space=pltpu.VMEM)] * (1 + len(chunks)),
        out_specs=[pl.BlockSpec(memory_space=pltpu.VMEM)] * 2,
        compiler_params=pltpu.CompilerParams(vmem_limit_bytes=vmem_bytes),
        cost_estimate=pl.CostEstimate(
            flops=count * rows * width, bytes_accessed=2 * (count + 5) * rows * width, transcendentals=0
        ),
        name="finish",
    )(place, parts, *chunks)


def shifted(value, axis, step):
    size = lax.axis_size(axis)
    return lax.ppermute(value, axis, [(i, (i + step) % size) for i in range(size)])


def per_device(features, weight, adj_tiles, tile_rows, tile_cols, tile_counts, out_grad):
    node_rows, width = features.shape
    capacity, side = adj_tiles.shape[2:4]
    tiles = adj_tiles.reshape(capacity, side, side)
    rows = tile_rows.reshape(capacity)
    cols = tile_cols.reshape(capacity)
    count = tile_counts.reshape(1)
    row_count = lax.axis_size("row")
    col_count = lax.axis_size("col")
    per_strip = node_rows // side
    row_place = lax.axis_index("row")
    col_place = lax.axis_index("col").astype(jnp.int32).reshape(1)

    shards = [features] + [shifted(features, "row", step) for step in range(1, row_count)]
    source = lax.rem(row_place + row_count - jnp.arange(row_count, dtype=jnp.int32), row_count)
    dense = build_dense(rows, cols, count, tiles, col_count * per_strip, row_count, per_strip)

    cell = forward_product(source, dense, shards)
    parts = lax.all_to_all(cell, "col", 0, 0, tiled=True).reshape(col_count, node_rows, width)
    activations, back, *terms = middle(col_place, parts, weight, out_grad, node_rows * row_count * col_count)
    grads = lax.all_gather(back, "col", axis=0, tiled=True)

    owned = terms[0]
    for step in range(1, col_count):
        owned = owned + shifted(terms[step], "col", step)
    low = owned.astype(jnp.bfloat16)
    row_terms = jnp.stack([low] + [shifted(low, "row", step) for step in range(1, row_count)])
    ordered = jnp.take(row_terms, lax.rem(row_place + row_count - jnp.arange(row_count), row_count), axis=0)
    owned = jnp.sum(ordered.astype(jnp.float32), axis=0)
    chunks = [owned] + [shifted(owned, "col", step) for step in range(1, col_count)]

    cell_back = backward_product(dense, grads)
    back_parts = lax.all_to_all(cell_back, "row", 0, 0, tiled=True)
    grad_features, grad_weight = finish(col_place, back_parts, chunks)
    return (activations, grad_features, grad_weight)


def solution(mesh):
    placed = (
        P(("row", "col"), None),
        P(),
        P("row", "col", None, None, None),
        P("row", "col", None),
        P("row", "col", None),
        P("row", "col"),
        P(("row", "col"), None),
    )
    return jax.shard_map(
        per_device,
        mesh=mesh,
        in_specs=placed,
        out_specs=(P(("row", "col"), None), P(("row", "col"), None), P()),
        check_vma=False,
    )
```

time: 559 us -> 123 us (0.22)
  waiting for transfers between devices: 373 us -> 41 us
  other arithmetic: 75.4 us -> 0.68 us
  local copies, waits for them, and re-layouts: 52.5 us -> 3.66 us
  starting transfers between devices: 0.16 us -> 42.7 us
  matrix products: 31.5 us -> 0 us
  Pallas kernels: 0 us -> 23.1 us
  between operations: 14.5 us -> 1.51 us
    reduce_scatter x2 -> x0, waiting for transfers between devices: 204 us -> none  [the longest x1 130 us: per_device(): lax.psum_scatter(col_part.reshape(-1, width).astype(jnp.bfloat16), 'row',...]
    psum x1 -> x0, waiting for transfers between devices: 126 us -> none  [per_device(): grad_weight = lax.psum(local_weight, ('row', 'col'))]
    scatter-add x16 -> x0, other arithmetic: 52.8 us -> none  [the longest x8 35.2 us: backward_step(): return acc.at[part_cols].add(prod * live[:, None, None])]
    all_gather x1 -> x0, waiting for transfers between devices: 43 us -> none  [per_device(): gathered = lax.all_gather(projected, 'row', axis=0, tiled=True)]
    gather x16 -> x1, local copies, waits for them, and re-layouts: 36.2 us -> 0.56 us  [per_device(): jnp.take(row_terms, lax.rem(row_place + row_count - jnp.arange(row_count)...]
    ppermute x0 -> x20, starting transfers between devices: none -> 32.7 us  [shifted(): lax.ppermute(value, axis, [(i, (i + step) % size) for i in range(size)])]
    ppermute x0 -> x20, waiting for transfers between devices: none -> 32.2 us  [shifted(): lax.ppermute(value, axis, [(i, (i + step) % size) for i in range(size)])]
    dot_general x19 -> x0, matrix products: 31.5 us -> none  [the longest x8 14.4 us: forward_step(): jnp.einsum('gij,gjf->gif', part_tiles, blocks[part_cols], preferred_eleme...]
  transfers between devices with their start and end apart: 4 -> 22, of which waited for: 4 -> 10; matrix products, arithmetic and copies ran while one was open for 2% -> 1% of each run, Pallas kernels for 0% -> 11%
where the time goes in v1:
time: 123 us; the launch traced here: 121 us
  starting transfers between devices  42.7 us (35%)
  waiting for transfers between devices  41 us (33%)
  Pallas kernels  23.1 us (19%)
  blocking collectives  8.33 us (7%)
  local copies, waits for them, and re-layouts  3.66 us (3%)
  between operations  1.51 us (1%)
    ppermute x20, starting transfers between devices, shifted(): lax.ppermute(value, axis, [(i, (i + step) % size) for i in range(size)])  32.7 us
    ppermute x20, waiting for transfers between devices, shifted(): lax.ppermute(value, axis, [(i, (i + step) % size) for i in range(size)])  32.2 us
    all_to_all x1, waiting for transfers between devices, per_device(): lax.all_to_all(cell, 'col', 0, 0, tiled=True)  8.78 us
    all_gather x1, blocking collectives, per_device(): grads = lax.all_gather(back, 'col', axis=0, tiled=True)  8.33 us
    pallas_call x1, Pallas kernels, backward_product(): pl.pallas_call(backward_kernel, out_shape=jax.ShapeDtypeStruct((strips, w...  7.11 us
    all_to_all x1, starting transfers between devices, per_device(): back_parts = lax.all_to_all(cell_back, 'row', 0, 0, tiled=True)  6.46 us
    pallas_call x1, Pallas kernels, forward_product(): pl.pallas_call(forward_kernel, out_shape=jax.ShapeDtypeStruct((high, widt...  5.87 us
    pallas_call x1, Pallas kernels, build_dense(): pl.pallas_call(functools.partial(build_kernel, per_strip=per_strip, strip...  5.59 us
  transfers between devices with their start and end apart: 22, of which 10 were waited for; matrix products, arithmetic and copies ran while one was open for 1% of the time, Pallas kernels for 11%

profile of v1, /device:TPU:0, one launch (start us, length us, event | category | flops | bytes accessed | tf_op | source)
XLA Modules:
  0.0 120.9 jit_solution(271411541754966938)
XLA Ops:
  0.6 5.1 %collective-permute-start.5 = (bf16[256,256]{1,0:T(8,128)(2,1)}, bf16[256,256]{1,0:T(8,128)(2,1)S(1)}, u32[]{:S(2)}, u32[]{:S(2)}) collective-permute-start(bf16[256,256]{1,0:T(8,128)(2,1)} %refs_0_.1), channel_id=1, source_target_pairs={{0,24},{4,28},{8,0},{12,4},{16,8},{20,12},{24,16},{28,20},{1,25},{... | collective-permute-start | bytes 393224 | tf_op jit(solution)/shard_map/ppermute | solution.py:269
  5.7 0.4 collective-permute-start.4
  6.1 3.5 %collective-permute-start.3 = (bf16[256,256]{1,0:T(8,128)(2,1)}, bf16[256,256]{1,0:T(8,128)(2,1)S(1)}, u32[]{:S(2)}, u32[]{:S(2)}) collective-permute-start(bf16[256,256]{1,0:T(8,128)(2,1)} %refs_0_.1), channel_id=1, source_target_pairs={{0,16},{4,20},{8,24},{12,28},{16,0},{20,4},{24,8},{28,12},{1,17},{... | collective-permute-start | bytes 393224 | tf_op jit(solution)/shard_map/ppermute | solution.py:269
  9.6 0.0 collective-permute-start.2
  9.6 1.0 collective-permute-start.1
  10.6 0.0 collective-permute-done.5.refs_6_
  10.6 1.5 %collective-permute-start = (bf16[256,256]{1,0:T(8,128)(2,1)}, bf16[256,256]{1,0:T(8,128)(2,1)S(1)}, u32[]{:S(2)}, u32[]{:S(2)}) collective-permute-start(bf16[256,256]{1,0:T(8,128)(2,1)} %refs_0_.1), channel_id=1, source_target_pairs={{0,4},{4,8},{8,12},{12,16},{16,20},{20,24},{24,28},{28,0},{1,5},{5... | collective-permute-start | bytes 393224 | tf_op jit(solution)/shard_map/ppermute | solution.py:269
  12.1 0.7 collective-permute-done.4.refs_5_
  12.8 9.7 %collective-permute-start.6 = (bf16[256,256]{1,0:T(8,128)(2,1)}, bf16[256,256]{1,0:T(8,128)(2,1)S(1)}, u32[]{:S(2)}, u32[]{:S(2)}) collective-permute-start(bf16[256,256]{1,0:T(8,128)(2,1)} %refs_0_.1), channel_id=1, source_target_pairs={{0,28},{4,0},{8,4},{12,8},{16,12},{20,16},{24,20},{28,24},{1,29},{... | collective-permute-start | bytes 393224 | tf_op jit(solution)/shard_map/ppermute | solution.py:269
  23.2 5.6 %build_dense.1.dense_ref = bf16[8,1024,256]{2,1,0:T(8,128)(2,1)} custom-call(s32[256]{0:T(256)} %bitcast.27, s32[256]{0:T(256)} %bitcast.28, s32[1]{0:T(128)} %bitcast.24.count_ref, bf16[256,128,128]{2,1,0:T(8,128)(2,1)} %bitcast.25), custom_call_target="tpu_custom_call" | custom-call | flops 4194304 | bytes 12582912 | tf_op jit(solution)/shard_map/build_dense/pallas_call | solution.py:75
  28.8 0.5 compare_select_fusion.4.source_ref
  29.3 0.0 collective-permute-done.3.refs_4_
  29.3 0.0 collective-permute-done.2.refs_3_
  29.3 0.0 collective-permute-done.1.refs_2_
  29.3 0.0 collective-permute-done.refs_1_
  29.3 0.0 copy-start.8
  29.3 1.6 %collective-permute-done.6.refs_7_ = bf16[256,256]{1,0:T(8,128)(2,1)S(1)} collective-permute-done((bf16[256,256]{1,0:T(8,128)(2,1)}, bf16[256,256]{1,0:T(8,128)(2,1)S(1)}, u32[]{:S(2)}, u32[]{:S(2)}) %collective-permute-start.6) | collective-permute-done | bytes 131104 | tf_op jit(solution)/shard_map/ppermute | solution.py:269
  30.9 0.0 copy-done.3
  30.9 0.0 copy-done.4
  30.9 0.0 copy-done.5
  30.9 0.0 copy-done.6
  31.0 0.7 copy-done.9
  31.6 5.9 %forward_product.1 = bf16[1024,256]{1,0:T(8,128)(2,1)} custom-call(s32[8]{0:T(128)} %compare_select_fusion.4.source_ref, bf16[8,1024,256]{2,1,0:T(8,128)(2,1)} %build_dense.1.dense_ref, bf16[256,256]{1,0:T(8,128)(2,1)} %refs_0_.1, bf16[256,256]{1,0:T(8,128)(2,1)} %copy-done.8, bf16[256,256]{1,0:T(8,128)(2,1)} %copy-done.7, bf16[256,256]{1,0:T(8,128)(2,1)} %copy-done.6, ...), custom_call_target="tpu_custom_call" | custom-call | flops 1073741824 | bytes 5767168 | tf_op jit(solution)/shard_map/forward_product/pallas_call | solution.py:126
  37.5 3.5 %all-to-all-start = ((bf16[4,256,256]{2,1,0:T(8,128)(2,1)}), bf16[4,256,256]{2,1,0:T(8,128)(2,1)S(1)}, u32[]{:S(2)}, u32[]{:S(2)}) async-start(bf16[4,256,256]{2,1,0:T(8,128)(2,1)} %bitcast.26), calls=%async_computation | async-start | bytes 1048576 | tf_op jit(solution)/shard_map/all_to_all | solution.py:290
  41.0 8.8 %all-to-all-done.parts_ref = bf16[4,256,256]{2,1,0:T(8,128)(2,1)S(1)} async-done(((bf16[4,256,256]{2,1,0:T(8,128)(2,1)}), bf16[4,256,256]{2,1,0:T(8,128)(2,1)S(1)}, u32[]{:S(2)}, u32[]{:S(2)}) %all-to-all-start) | async-done | bytes 524320 | tf_op jit(solution)/shard_map/all_to_all | solution.py:290
  49.8 0.8 copy-done.1
  50.6 2.4 %middle.1 = (bf16[256,256]{1,0:T(8,128)(2,1)}, bf16[256,256]{1,0:T(8,128)(2,1)}, f32[64,256]{1,0:T(8,128)}, f32[64,256]{1,0:T(8,128)}, f32[64,256]{1,0:T(8,128)}, /*index=5*/f32[64,256]{1,0:T(8,128)}) custom-call(s32[1]{0:T(128)} %bitcast.place_ref, bf16[4,256,256]{2,1,0:T(8,128)(2,1)} %copy-done.1, bf16[256,256]{1,0:T(8,128)(2,1)} %weight_ref.1, ...), custom_call_target="tpu_custom_call" | custom-call | flops 167772160 | bytes 1179648 | tf_op jit(solution)/shard_map/middle/pallas_call | solution.py:177
  53.0 0.0 collective-permute-start.7
  53.0 0.4 collective-permute-start.8
  53.4 1.4 %collective-permute-start.9 = (f32[64,256]{1,0:T(8,128)}, f32[64,256]{1,0:T(8,128)S(1)}, u32[]{:S(2)}, u32[]{:S(2)}) collective-permute-start(f32[64,256]{1,0:T(8,128)} %get-tuple-element.16), channel_id=1, source_target_pairs={{0,3},{1,0},{2,1},{3,2},{4,7},{5,4},{6,5},{7,6},{8,11},{9,8},{10,9... | collective-permute-start | bytes 196616 | tf_op jit(solution)/shard_map/ppermute | solution.py:269
  54.8 8.3 %all_gather.3.grads_ref = bf16[1024,256]{1,0:T(8,128)(2,1)} all-gather(bf16[256,256]{1,0:T(8,128)(2,1)} %get-tuple-element.12), channel_id=1, replica_groups=mesh['row'=8,'col'=4] {'col'}, dimensions={0}, use_global_device_ids=true | all-gather | bytes 655360 | tf_op jit(solution)/shard_map/all_gather | solution.py:292
  63.2 7.1 %backward_product.1 = bf16[8,256,256]{2,1,0:T(8,128)(2,1)} custom-call(bf16[8,1024,256]{2,1,0:T(8,128)(2,1)} %build_dense.1.dense_ref, bf16[1024,256]{1,0:T(8,128)(2,1)} %all_gather.3.grads_ref), custom_call_target="tpu_custom_call" | custom-call | flops 1073741824 | bytes 5767168 | tf_op jit(solution)/shard_map/backward_product/pallas_call | solution.py:217
  70.3 6.5 %all-to-all-start.1 = ((bf16[8,256,256]{2,1,0:T(8,128)(2,1)}), bf16[8,256,256]{2,1,0:T(8,128)(2,1)S(1)}, u32[]{:S(2)}, u32[]{:S(2)}) async-start(bf16[8,256,256]{2,1,0:T(8,128)(2,1)} %backward_product.1), calls=%async_computation.1 | async-start | bytes 2097152 | tf_op jit(solution)/shard_map/all_to_all | solution.py:304
  76.7 0.0 collective-permute-done.7
  76.7 0.0 collective-permute-done.8
  76.7 0.0 collective-permute-done.9
  76.8 2.3 %collective-permute-start.10 = (bf16[64,256]{1,0:T(8,128)(2,1)S(1)}, bf16[64,256]{1,0:T(8,128)(2,1)S(1)}, u32[]{:S(2)}, u32[]{:S(2)}) collective-permute-start(bf16[64,256]{1,0:T(8,128)(2,1)S(1)} %get-tuple-element.20), channel_id=1, source_target_pairs={{0,4},{4,8},{8,12},{12,16},{16,20},{20,24},{24,28},{28,0},{1,5},{5... | collective-permute-start | bytes 98312 | tf_op jit(solution)/shard_map/ppermute | solution.py:269
  79.1 3.1 %collective-permute-start.15 = (bf16[64,256]{1,0:T(8,128)(2,1)S(1)}, bf16[64,256]{1,0:T(8,128)(2,1)S(1)}, u32[]{:S(2)}, u32[]{:S(2)}) collective-permute-start(bf16[64,256]{1,0:T(8,128)(2,1)S(1)} %get-tuple-element.20), channel_id=1, source_target_pairs={{0,24},{4,28},{8,0},{12,4},{16,8},{20,12},{24,16},{28,20},{1,25},{... | collective-permute-start | bytes 98312 | tf_op jit(solution)/shard_map/ppermute | solution.py:269
  82.2 0.6 collective-permute-start.14
  82.8 1.8 %collective-permute-start.13 = (bf16[64,256]{1,0:T(8,128)(2,1)S(1)}, bf16[64,256]{1,0:T(8,128)(2,1)S(1)}, u32[]{:S(2)}, u32[]{:S(2)}) collective-permute-start(bf16[64,256]{1,0:T(8,128)(2,1)S(1)} %get-tuple-element.20), channel_id=1, source_target_pairs={{0,16},{4,20},{8,24},{12,28},{16,0},{20,4},{24,8},{28,12},{1,17},{... | collective-permute-start | bytes 98312 | tf_op jit(solution)/shard_map/ppermute | solution.py:269
  84.6 0.5 collective-permute-start.12
  85.1 15.8 %collective-permute-done.10 = bf16[64,256]{1,0:T(8,128)(2,1)S(1)} collective-permute-done((bf16[64,256]{1,0:T(8,128)(2,1)S(1)}, bf16[64,256]{1,0:T(8,128)(2,1)S(1)}, u32[]{:S(2)}, u32[]{:S(2)}) %collective-permute-start.10) | collective-permute-done | bytes 32800 | tf_op jit(solution)/shard_map/ppermute | solution.py:269
  100.9 0.0 collective-permute-start.11
  100.9 5.8 %collective-permute-done.11 = bf16[64,256]{1,0:T(8,128)(2,1)S(1)} collective-permute-done((bf16[64,256]{1,0:T(8,128)(2,1)S(1)}, bf16[64,256]{1,0:T(8,128)(2,1)S(1)}, u32[]{:S(2)}, u32[]{:S(2)}) %collective-permute-start.11) | collective-permute-done | bytes 32800 | tf_op jit(solution)/shard_map/ppermute | solution.py:269
  106.7 0.0 collective-permute-start.16
  106.7 2.8 %collective-permute-done.12 = bf16[64,256]{1,0:T(8,128)(2,1)S(1)} collective-permute-done((bf16[64,256]{1,0:T(8,128)(2,1)S(1)}, bf16[64,256]{1,0:T(8,128)(2,1)S(1)}, u32[]{:S(2)}, u32[]{:S(2)}) %collective-permute-start.12) | collective-permute-done | bytes 32800 | tf_op jit(solution)/shard_map/ppermute | solution.py:269
  109.5 0.0 collective-permute-done.13
  109.5 0.0 collective-permute-done.14
  109.5 0.0 collective-permute-done.15
  109.5 1.4 %collective-permute-done.16 = bf16[64,256]{1,0:T(8,128)(2,1)S(1)} collective-permute-done((bf16[64,256]{1,0:T(8,128)(2,1)S(1)}, bf16[64,256]{1,0:T(8,128)(2,1)S(1)}, u32[]{:S(2)}, u32[]{:S(2)}) %collective-permute-start.16) | collective-permute-done | bytes 32800 | tf_op jit(solution)/shard_map/ppermute | solution.py:269
  110.9 0.6 gather_fusion
  111.5 0.1 convert_reduce_fusion.refs_0_
  111.6 0.1 collective-permute-start.19
  111.7 1.2 collective-permute-start.18
  112.9 0.2 collective-permute-start.17
  113.0 0.6 collective-permute-done.19.refs_3_
  113.6 3.2 %collective-permute-done.18.refs_2_ = f32[64,256]{1,0:T(8,128)S(1)} collective-permute-done((f32[64,256]{1,0:T(8,128)S(1)}, f32[64,256]{1,0:T(8,128)S(1)}, u32[]{:S(2)}, u32[]{:S(2)}) %collective-permute-start.18) | collective-permute-done | bytes 65568 | tf_op jit(solution)/shard_map/ppermute | solution.py:269
  116.8 0.4 collective-permute-done.17.refs_1_
  117.2 0.0 all-to-all-done.1.parts_ref
  117.2 0.0 copy-done.11
  117.2 0.2 copy-done.12
  117.4 0.4 copy-done.13
  117.8 1.0 copy-done
  118.7 2.1 %finish.1 = (bf16[256,256]{1,0:T(8,128)(2,1)}, f32[256,256]{1,0:T(8,128)}) custom-call(s32[1]{0:T(128)} %bitcast.place_ref, bf16[8,256,256]{2,1,0:T(8,128)(2,1)} %copy-done, f32[64,256]{1,0:T(8,128)} %copy-done.2, f32[64,256]{1,0:T(8,128)} %copy-done.13, f32[64,256]{1,0:T(8,128)} %copy-done.12, f32[64,256]{1,0:T(8,128)} %copy-done.11), custom_call_target="tpu_custom_call" | custom-call | flops 524288 | bytes 1703936 | tf_op jit(solution)/shard_map/finish/pallas_call | solution.py:251
  (28 shorter events, 0.1 us)
Async XLA Ops:
  0.6 9.9 %collective-permute-start.5 = (bf16[256,256]{1,0:T(8,128)(2,1)}, bf16[256,256]{1,0:T(8,128)(2,1)S(1)}, u32[]{:S(2)}, u32[]{:S(2)}) collective-permute-start(bf16[256,256]{1,0:T(8,128)(2,1)} %refs_0_.1), channel_id=1, source_target_pairs={{0,24},{4,28},{8,0},{12,4},{16,8},{20,12},{24,16},{28,20},{1,25},{... | collective-permute-start | bytes 393224 | tf_op jit(solution)/shard_map/ppermute | solution.py:269
  5.7 7.1 %collective-permute-start.4 = (bf16[256,256]{1,0:T(8,128)(2,1)}, bf16[256,256]{1,0:T(8,128)(2,1)S(1)}, u32[]{:S(2)}, u32[]{:S(2)}) collective-permute-start(bf16[256,256]{1,0:T(8,128)(2,1)} %refs_0_.1), channel_id=1, source_target_pairs={{0,20},{4,24},{8,28},{12,0},{16,4},{20,8},{24,12},{28,16},{1,21},{... | collective-permute-start | bytes 393224 | tf_op jit(solution)/shard_map/ppermute | solution.py:269
  6.1 23.1 %collective-permute-start.3 = (bf16[256,256]{1,0:T(8,128)(2,1)}, bf16[256,256]{1,0:T(8,128)(2,1)S(1)}, u32[]{:S(2)}, u32[]{:S(2)}) collective-permute-start(bf16[256,256]{1,0:T(8,128)(2,1)} %refs_0_.1), channel_id=1, source_target_pairs={{0,16},{4,20},{8,24},{12,28},{16,0},{20,4},{24,8},{28,12},{1,17},{... | collective-permute-start | bytes 393224 | tf_op jit(solution)/shard_map/ppermute | solution.py:269
  9.6 19.7 %collective-permute-start.2 = (bf16[256,256]{1,0:T(8,128)(2,1)}, bf16[256,256]{1,0:T(8,128)(2,1)S(1)}, u32[]{:S(2)}, u32[]{:S(2)}) collective-permute-start(bf16[256,256]{1,0:T(8,128)(2,1)} %refs_0_.1), channel_id=1, source_target_pairs={{0,12},{4,16},{8,20},{12,24},{16,28},{20,0},{24,4},{28,8},{1,13},{... | collective-permute-start | bytes 393224 | tf_op jit(solution)/shard_map/ppermute | solution.py:269
  9.6 19.7 %collective-permute-start.1 = (bf16[256,256]{1,0:T(8,128)(2,1)}, bf16[256,256]{1,0:T(8,128)(2,1)S(1)}, u32[]{:S(2)}, u32[]{:S(2)}) collective-permute-start(bf16[256,256]{1,0:T(8,128)(2,1)} %refs_0_.1), channel_id=1, source_target_pairs={{0,8},{4,12},{8,16},{12,20},{16,24},{20,28},{24,0},{28,4},{1,9},{5... | collective-permute-start | bytes 393224 | tf_op jit(solution)/shard_map/ppermute | solution.py:269
  10.6 20.3 %copy-start.3 = (bf16[256,256]{1,0:T(8,128)(2,1)}, bf16[256,256]{1,0:T(8,128)(2,1)S(1)}, u32[]{:S(2)}) copy-start(bf16[256,256]{1,0:T(8,128)(2,1)S(1)} %collective-permute-done.5.refs_6_) | copy-start | bytes 393220
  10.6 18.7 %collective-permute-start = (bf16[256,256]{1,0:T(8,128)(2,1)}, bf16[256,256]{1,0:T(8,128)(2,1)S(1)}, u32[]{:S(2)}, u32[]{:S(2)}) collective-permute-start(bf16[256,256]{1,0:T(8,128)(2,1)} %refs_0_.1), channel_id=1, source_target_pairs={{0,4},{4,8},{8,12},{12,16},{16,20},{20,24},{24,28},{28,0},{1,5},{5... | collective-permute-start | bytes 393224 | tf_op jit(solution)/shard_map/ppermute | solution.py:269
  12.8 18.1 %copy-start.4 = (bf16[256,256]{1,0:T(8,128)(2,1)}, bf16[256,256]{1,0:T(8,128)(2,1)S(1)}, u32[]{:S(2)}) copy-start(bf16[256,256]{1,0:T(8,128)(2,1)S(1)} %collective-permute-done.4.refs_5_) | copy-start | bytes 393220
  12.8 18.1 %collective-permute-start.6 = (bf16[256,256]{1,0:T(8,128)(2,1)}, bf16[256,256]{1,0:T(8,128)(2,1)S(1)}, u32[]{:S(2)}, u32[]{:S(2)}) collective-permute-start(bf16[256,256]{1,0:T(8,128)(2,1)} %refs_0_.1), channel_id=1, source_target_pairs={{0,28},{4,0},{8,4},{12,8},{16,12},{20,16},{24,20},{28,24},{1,29},{... | collective-permute-start | bytes 393224 | tf_op jit(solution)/shard_map/ppermute | solution.py:269
  29.3 1.6 %copy-start.5 = (bf16[256,256]{1,0:T(8,128)(2,1)}, bf16[256,256]{1,0:T(8,128)(2,1)S(1)}, u32[]{:S(2)}) copy-start(bf16[256,256]{1,0:T(8,128)(2,1)S(1)} %collective-permute-done.3.refs_4_) | copy-start | bytes 393220
  29.3 1.6 %copy-start.6 = (bf16[256,256]{1,0:T(8,128)(2,1)}, bf16[256,256]{1,0:T(8,128)(2,1)S(1)}, u32[]{:S(2)}) copy-start(bf16[256,256]{1,0:T(8,128)(2,1)S(1)} %collective-permute-done.2.refs_3_) | copy-start | bytes 393220
  29.3 1.6 %copy-start.7 = (bf16[256,256]{1,0:T(8,128)(2,1)}, bf16[256,256]{1,0:T(8,128)(2,1)S(1)}, u32[]{:S(2)}) copy-start(bf16[256,256]{1,0:T(8,128)(2,1)S(1)} %collective-permute-done.1.refs_2_) | copy-start | bytes 393220
  29.3 1.6 %copy-start.8 = (bf16[256,256]{1,0:T(8,128)(2,1)}, bf16[256,256]{1,0:T(8,128)(2,1)S(1)}, u32[]{:S(2)}) copy-start(bf16[256,256]{1,0:T(8,128)(2,1)S(1)} %collective-permute-done.refs_1_) | copy-start | bytes 393220
  30.9 0.7 copy-start.9
  37.5 12.3 %all-to-all-start = ((bf16[4,256,256]{2,1,0:T(8,128)(2,1)}), bf16[4,256,256]{2,1,0:T(8,128)(2,1)S(1)}, u32[]{:S(2)}, u32[]{:S(2)}) async-start(bf16[4,256,256]{2,1,0:T(8,128)(2,1)} %bitcast.26), calls=%async_computation | async-start | bytes 1048576 | tf_op jit(solution)/shard_map/all_to_all | solution.py:290
  49.8 0.8 copy-start.1
  53.0 23.8 %copy-start.10 = (f32[64,256]{1,0:T(8,128)S(1)}, f32[64,256]{1,0:T(8,128)}, u32[]{:S(2)}) copy-start(f32[64,256]{1,0:T(8,128)} %get-tuple-element.13) | copy-start | bytes 196612
  53.0 23.8 %collective-permute-start.7 = (f32[64,256]{1,0:T(8,128)}, f32[64,256]{1,0:T(8,128)S(1)}, u32[]{:S(2)}, u32[]{:S(2)}) collective-permute-start(f32[64,256]{1,0:T(8,128)} %get-tuple-element.14), channel_id=1, source_target_pairs={{0,1},{1,2},{2,3},{3,0},{4,5},{5,6},{6,7},{7,4},{8,9},{9,10},{10,1... | collective-permute-start | bytes 196616 | tf_op jit(solution)/shard_map/ppermute | solution.py:269
  53.0 23.8 %collective-permute-start.8 = (f32[64,256]{1,0:T(8,128)}, f32[64,256]{1,0:T(8,128)S(1)}, u32[]{:S(2)}, u32[]{:S(2)}) collective-permute-start(f32[64,256]{1,0:T(8,128)} %get-tuple-element.15), channel_id=1, source_target_pairs={{0,2},{1,3},{2,0},{3,1},{4,6},{5,7},{6,4},{7,5},{8,10},{9,11},{10,... | collective-permute-start | bytes 196616 | tf_op jit(solution)/shard_map/ppermute | solution.py:269
  53.4 23.3 %collective-permute-start.9 = (f32[64,256]{1,0:T(8,128)}, f32[64,256]{1,0:T(8,128)S(1)}, u32[]{:S(2)}, u32[]{:S(2)}) collective-permute-start(f32[64,256]{1,0:T(8,128)} %get-tuple-element.16), channel_id=1, source_target_pairs={{0,3},{1,0},{2,1},{3,2},{4,7},{5,4},{6,5},{7,6},{8,11},{9,8},{10,9... | collective-permute-start | bytes 196616 | tf_op jit(solution)/shard_map/ppermute | solution.py:269
  70.3 46.9 %all-to-all-start.1 = ((bf16[8,256,256]{2,1,0:T(8,128)(2,1)}), bf16[8,256,256]{2,1,0:T(8,128)(2,1)S(1)}, u32[]{:S(2)}, u32[]{:S(2)}) async-start(bf16[8,256,256]{2,1,0:T(8,128)(2,1)} %backward_product.1), calls=%async_computation.1 | async-start | bytes 2097152 | tf_op jit(solution)/shard_map/all_to_all | solution.py:304
  76.8 24.1 %collective-permute-start.10 = (bf16[64,256]{1,0:T(8,128)(2,1)S(1)}, bf16[64,256]{1,0:T(8,128)(2,1)S(1)}, u32[]{:S(2)}, u32[]{:S(2)}) collective-permute-start(bf16[64,256]{1,0:T(8,128)(2,1)S(1)} %get-tuple-element.20), channel_id=1, source_target_pairs={{0,4},{4,8},{8,12},{12,16},{16,20},{20,24},{24,28},{28,0},{1,5},{5... | collective-permute-start | bytes 98312 | tf_op jit(solution)/shard_map/ppermute | solution.py:269
  79.1 30.4 %collective-permute-start.15 = (bf16[64,256]{1,0:T(8,128)(2,1)S(1)}, bf16[64,256]{1,0:T(8,128)(2,1)S(1)}, u32[]{:S(2)}, u32[]{:S(2)}) collective-permute-start(bf16[64,256]{1,0:T(8,128)(2,1)S(1)} %get-tuple-element.20), channel_id=1, source_target_pairs={{0,24},{4,28},{8,0},{12,4},{16,8},{20,12},{24,16},{28,20},{1,25},{... | collective-permute-start | bytes 98312 | tf_op jit(solution)/shard_map/ppermute | solution.py:269
  82.2 27.3 %collective-permute-start.14 = (bf16[64,256]{1,0:T(8,128)(2,1)S(1)}, bf16[64,256]{1,0:T(8,128)(2,1)S(1)}, u32[]{:S(2)}, u32[]{:S(2)}) collective-permute-start(bf16[64,256]{1,0:T(8,128)(2,1)S(1)} %get-tuple-element.20), channel_id=1, source_target_pairs={{0,20},{4,24},{8,28},{12,0},{16,4},{20,8},{24,12},{28,16},{1,21},{... | collective-permute-start | bytes 98312 | tf_op jit(solution)/shard_map/ppermute | solution.py:269
  82.8 26.7 %collective-permute-start.13 = (bf16[64,256]{1,0:T(8,128)(2,1)S(1)}, bf16[64,256]{1,0:T(8,128)(2,1)S(1)}, u32[]{:S(2)}, u32[]{:S(2)}) collective-permute-start(bf16[64,256]{1,0:T(8,128)(2,1)S(1)} %get-tuple-element.20), channel_id=1, source_target_pairs={{0,16},{4,20},{8,24},{12,28},{16,0},{20,4},{24,8},{28,12},{1,17},{... | collective-permute-start | bytes 98312 | tf_op jit(solution)/shard_map/ppermute | solution.py:269
  84.6 24.9 %collective-permute-start.12 = (bf16[64,256]{1,0:T(8,128)(2,1)S(1)}, bf16[64,256]{1,0:T(8,128)(2,1)S(1)}, u32[]{:S(2)}, u32[]{:S(2)}) collective-permute-start(bf16[64,256]{1,0:T(8,128)(2,1)S(1)} %get-tuple-element.20), channel_id=1, source_target_pairs={{0,12},{4,16},{8,20},{12,24},{16,28},{20,0},{24,4},{28,8},{1,13},{... | collective-permute-start | bytes 98312 | tf_op jit(solution)/shard_map/ppermute | solution.py:269
  100.9 5.8 %collective-permute-start.11 = (bf16[64,256]{1,0:T(8,128)(2,1)S(1)}, bf16[64,256]{1,0:T(8,128)(2,1)S(1)}, u32[]{:S(2)}, u32[]{:S(2)}) collective-permute-start(bf16[64,256]{1,0:T(8,128)(2,1)S(1)} %get-tuple-element.20), channel_id=1, source_target_pairs={{0,8},{4,12},{8,16},{12,20},{16,24},{20,28},{24,0},{28,4},{1,9},{5... | collective-permute-start | bytes 98312 | tf_op jit(solution)/shard_map/ppermute | solution.py:269
  106.7 4.2 %collective-permute-start.16 = (bf16[64,256]{1,0:T(8,128)(2,1)S(1)}, bf16[64,256]{1,0:T(8,128)(2,1)S(1)}, u32[]{:S(2)}, u32[]{:S(2)}) collective-permute-start(bf16[64,256]{1,0:T(8,128)(2,1)S(1)} %get-tuple-element.20), channel_id=1, source_target_pairs={{0,28},{4,0},{8,4},{12,8},{16,12},{20,16},{24,20},{28,24},{1,29},{... | collective-permute-start | bytes 98312 | tf_op jit(solution)/shard_map/ppermute | solution.py:269
  111.6 5.5 %copy-start.2 = (f32[64,256]{1,0:T(8,128)}, f32[64,256]{1,0:T(8,128)S(1)}, u32[]{:S(2)}) copy-start(f32[64,256]{1,0:T(8,128)S(1)} %convert_reduce_fusion.refs_0_) | copy-start | bytes 196612
  111.6 2.0 %collective-permute-start.19 = (f32[64,256]{1,0:T(8,128)S(1)}, f32[64,256]{1,0:T(8,128)S(1)}, u32[]{:S(2)}, u32[]{:S(2)}) collective-permute-start(f32[64,256]{1,0:T(8,128)S(1)} %convert_reduce_fusion.refs_0_), channel_id=1, source_target_pairs={{0,3},{1,0},{2,1},{3,2},{4,7},{5,4},{6,5},{7,6},{8,11},{9,8},{10,9... | collective-permute-start | bytes 196616 | tf_op jit(solution)/shard_map/ppermute | solution.py:269
  111.7 5.1 %collective-permute-start.18 = (f32[64,256]{1,0:T(8,128)S(1)}, f32[64,256]{1,0:T(8,128)S(1)}, u32[]{:S(2)}, u32[]{:S(2)}) collective-permute-start(f32[64,256]{1,0:T(8,128)S(1)} %convert_reduce_fusion.refs_0_), channel_id=1, source_target_pairs={{0,2},{1,3},{2,0},{3,1},{4,6},{5,7},{6,4},{7,5},{8,10},{9,11},{10,... | collective-permute-start | bytes 196616 | tf_op jit(solution)/shard_map/ppermute | solution.py:269
  112.9 4.3 %collective-permute-start.17 = (f32[64,256]{1,0:T(8,128)S(1)}, f32[64,256]{1,0:T(8,128)S(1)}, u32[]{:S(2)}, u32[]{:S(2)}) collective-permute-start(f32[64,256]{1,0:T(8,128)S(1)} %convert_reduce_fusion.refs_0_), channel_id=1, source_target_pairs={{0,1},{1,2},{2,3},{3,0},{4,5},{5,6},{6,7},{7,4},{8,9},{9,10},{10,1... | collective-permute-start | bytes 196616 | tf_op jit(solution)/shard_map/ppermute | solution.py:269
  113.6 3.6 %copy-start.11 = (f32[64,256]{1,0:T(8,128)}, f32[64,256]{1,0:T(8,128)S(1)}, u32[]{:S(2)}) copy-start(f32[64,256]{1,0:T(8,128)S(1)} %collective-permute-done.19.refs_3_) | copy-start | bytes 196612
  116.8 0.6 copy-start.12
  117.2 0.6 copy-start.13
  117.8 1.0 copy-start

commit v2 on v1

v2 whole, which is shorter than its diff:
```python
import functools
import math

import jax
import jax.numpy as jnp
from jax import lax
from jax.experimental import pallas as pl
from jax.experimental.pallas import tpu as pltpu
from jax.sharding import PartitionSpec as P

chunk_tiles = 16
chunk_slots = 4
strips_per_step = 8
part_slots = 4
mib = 1024 * 1024


def scratch_bytes(*shapes):
    return sum(math.prod(shape) * jnp.dtype(kind).itemsize for shape, kind in shapes)


def build_kernel(rows_ref, cols_ref, count_ref, tiles_ref, dense_ref, total, held, sems, *, blocks, steps):
    side = tiles_ref.shape[1]
    first_block = pl.program_id(0) * blocks
    count = count_ref[0]
    chunks = (count + chunk_tiles - 1) // chunk_tiles

    def fetch(index):
        slot = lax.rem(index, chunk_slots)
        return pltpu.make_async_copy(
            tiles_ref.at[pl.ds(index * chunk_tiles, chunk_tiles)], held.at[slot], sems.at[slot]
        )

    for ahead in range(chunk_slots - 1):
        @pl.when(ahead < chunks)
        def _():
            fetch(ahead).start()

    row_blocks = dense_ref.shape[0] // side

    def clear(block, carry):
        down = pl.ds(pl.multiple_of(block * side, side), side)
        total[down, :] = jnp.zeros((side, total.shape[1]), jnp.float32)
        return carry

    lax.fori_loop(0, row_blocks, clear, 0)

    def chunk_step(index, carry):
        @pl.when(index + chunk_slots - 1 < chunks)
        def _():
            fetch(index + chunk_slots - 1).start()

        fetch(index).wait()
        slot = lax.rem(index, chunk_slots)
        for lane in range(chunk_tiles):
            place = index * chunk_tiles + lane
            col = cols_ref[place] - first_block
            live = place < count
            if steps > 1:
                live = live & (col >= 0) & (col < blocks)
                col = jnp.where(live, col, 0)
            row = jnp.where(live, rows_ref[place], row_blocks)
            down = pl.ds(pl.multiple_of(row * side, side), side)
            along = pl.ds(pl.multiple_of(col * side, side), side)
            total[down, along] += held[slot, lane].astype(jnp.float32)
        return carry

    lax.fori_loop(0, chunks, chunk_step, 0)

    def round_block(block, carry):
        down = pl.ds(pl.multiple_of(block * side, side), side)
        dense_ref[down, :] = total[down, :].astype(jnp.bfloat16)
        return carry

    lax.fori_loop(0, row_blocks, round_block, 0)


def build_dense(rows, cols, count, tiles, row_blocks, col_blocks, per_strip):
    capacity, side, _ = tiles.shape
    blocks = min(strips_per_step * per_strip, col_blocks)
    steps = col_blocks // blocks
    high, wide = row_blocks * side, blocks * side
    total = ((high + side, wide), jnp.float32)
    held = ((chunk_slots, chunk_tiles, side, side), jnp.bfloat16)
    block = ((high, wide), jnp.bfloat16)
    return pl.pallas_call(
        functools.partial(build_kernel, blocks=blocks, steps=steps),
        out_shape=jax.ShapeDtypeStruct((high, col_blocks * side), jnp.bfloat16),
        grid_spec=pltpu.PrefetchScalarGridSpec(
            num_scalar_prefetch=3,
            grid=(steps,),
            in_specs=[pl.BlockSpec(memory_space=pl.ANY)],
            out_specs=pl.BlockSpec((high, wide), lambda i, *_: (0, i)),
            scratch_shapes=[
                pltpu.VMEM(*total),
                pltpu.VMEM(*held),
                pltpu.SemaphoreType.DMA((chunk_slots,)),
            ],
        ),
        compiler_params=pltpu.CompilerParams(vmem_limit_bytes=scratch_bytes(total, held, block, block) + 4 * mib),
        cost_estimate=pl.CostEstimate(
            flops=capacity * side * side,
            bytes_accessed=2 * (capacity * side * side + high * col_blocks * side),
            transcendentals=0,
        ),
        name="build_dense",
    )(rows, cols, count, tiles)


def forward_kernel(place_ref, dense_ref, *refs, halves):
    half_refs, refs = refs[:halves], refs[halves:]
    *out_refs, held, depth, sems, depth_sems = refs
    count = len(out_refs)
    rows = held.shape[1]
    slots = held.shape[0]
    wide = depth.shape[1] // halves

    def fetch(order):
        first = lax.rem(place_ref[0] + 1 + order, count) * rows
        slot = order % slots
        return pltpu.make_async_copy(
            dense_ref.at[pl.ds(pl.multiple_of(first, rows), rows)], held.at[slot], sems.at[slot]
        )

    copies = []
    for index, half in enumerate(half_refs):
        copy = pltpu.make_async_copy(half, depth.at[:, pl.ds(index * wide, wide)], depth_sems.at[index])
        copy.start()
        copies.append(copy)
    for order in range(slots):
        fetch(order).start()
    for copy in copies:
        copy.wait()
    for order in range(count):
        fetch(order).wait()
        part = jnp.dot(held[order % slots], depth[...], preferred_element_type=jnp.float32)
        if order + slots < count:
            fetch(order + slots).start()
        out_refs[(order + 1) % count][...] = part.astype(jnp.bfloat16)


def forward_product(place, dense, halves, count):
    high, deep = dense.shape
    width = sum(half.shape[1] for half in halves)
    rows = high // count
    slots = min(count, part_slots)
    held = ((slots, rows, deep), jnp.bfloat16)
    depth = ((deep, width), jnp.bfloat16)
    out = ((high, width), jnp.float32)
    return pl.pallas_call(
        functools.partial(forward_kernel, halves=len(halves)),
        out_shape=[jax.ShapeDtypeStruct((rows, width), jnp.bfloat16)] * count,
        in_specs=[pl.BlockSpec(memory_space=pltpu.SMEM)] + [pl.BlockSpec(memory_space=pl.ANY)] * (1 + len(halves)),
        out_specs=[pl.BlockSpec(memory_space=pltpu.VMEM)] * count,
        scratch_shapes=[
            pltpu.VMEM(*held),
            pltpu.VMEM(*depth),
            pltpu.SemaphoreType.DMA((slots,)),
            pltpu.SemaphoreType.DMA((len(halves),)),
        ],
        compiler_params=pltpu.CompilerParams(vmem_limit_bytes=scratch_bytes(held, depth, out) + 6 * mib),
        cost_estimate=pl.CostEstimate(
            flops=2 * high * deep * width,
            bytes_accessed=2 * (high * deep + deep * width + high * width),
            transcendentals=0,
        ),
        name="forward_product",
    )(place, dense, *halves)


def middle_kernel(*refs, count, scale):
    parts = refs[:count]
    weight_ref, cotangent_ref, act_ref, back_ref, terms_ref = refs[count:]
    aggregate = parts[0][...].astype(jnp.float32)
    for part in parts[1:]:
        aggregate += part[...].astype(jnp.float32)
    high = aggregate.astype(jnp.bfloat16)
    low = (aggregate - high.astype(jnp.float32)).astype(jnp.bfloat16)
    weight = weight_ref[...]
    pre = jnp.dot(high, weight, preferred_element_type=jnp.float32)
    pre += jnp.dot(low, weight, preferred_element_type=jnp.float32)
    sig = jax.nn.sigmoid(pre)
    grad = (cotangent_ref[...].astype(jnp.float32) * sig * (1.0 + pre * (1.0 - sig))).astype(jnp.bfloat16)
    back_ref[...] = lax.dot_general(
        grad, weight, (((1,), (1,)), ((), ())), preferred_element_type=jnp.float32
    ).astype(jnp.bfloat16)
    act_ref[...] = (pre * sig).astype(jnp.bfloat16)
    over_nodes = (((0,), (0,)), ((), ()))
    terms = lax.dot_general(high, grad, over_nodes, preferred_element_type=jnp.float32)
    terms += lax.dot_general(low, grad, over_nodes, preferred_element_type=jnp.float32)
    terms_ref[...] = terms * scale


def middle(parts, weight, cotangent, total_nodes):
    rows, width = cotangent.shape
    count = len(parts)
    return pl.pallas_call(
        functools.partial(middle_kernel, count=count, scale=1.0 / math.sqrt(total_nodes)),
        out_shape=[
            jax.ShapeDtypeStruct((rows, width), jnp.bfloat16),
            jax.ShapeDtypeStruct((rows, width), jnp.bfloat16),
            jax.ShapeDtypeStruct((width, width), jnp.float32),
        ],
        in_specs=[pl.BlockSpec(memory_space=pltpu.VMEM)] * (count + 2),
        out_specs=[pl.BlockSpec(memory_space=pltpu.VMEM)] * 3,
        compiler_params=pltpu.CompilerParams(vmem_limit_bytes=12 * mib),
        cost_estimate=pl.CostEstimate(
            flops=10 * rows * width * width, bytes_accessed=2 * (count + 6) * rows * width, transcendentals=rows * width
        ),
        name="middle",
    )(*parts, weight, cotangent)


def backward_kernel(dense_ref, grads_ref, out_ref, held, results, sems, out_sems):
    strips, wide, _ = out_ref.shape
    slots = held.shape[0]
    per_part = held.shape[2] // wide

    def fetch(part):
        along = pl.ds(part * per_part * wide, per_part * wide)
        slot = part % slots
        return pltpu.make_async_copy(dense_ref.at[:, along], held.at[slot], sems.at[slot])

    def store(part):
        strips_of = pl.ds(part * per_part, per_part)
        return pltpu.make_async_copy(results.at[strips_of], out_ref.at[strips_of], out_sems.at[part])

    parts = strips // per_part
    for part in range(slots):
        fetch(part).start()
    grads = grads_ref[...].T
    for part in range(parts):
        fetch(part).wait()
        for index in range(per_part):
            product = jnp.dot(
                grads, held[part % slots, :, index * wide : (index + 1) * wide], preferred_element_type=jnp.float32
            )
            results[part * per_part + index] = product.astype(jnp.bfloat16).T
        store(part).start()
        if part + slots < parts:
            fetch(part + slots).start()
    for part in range(parts):
        store(part).wait()


def backward_product(dense, grads, strips):
    high, deep = dense.shape
    width = grads.shape[1]
    wide = deep // strips
    per_part = 2 if strips % 2 == 0 else 1
    parts = strips // per_part
    slots = min(parts, part_slots)
    held = ((slots, high, per_part * wide), jnp.bfloat16)
    results = ((strips, wide, width), jnp.bfloat16)
    return pl.pallas_call(
        backward_kernel,
        out_shape=jax.ShapeDtypeStruct((strips, wide, width), jnp.bfloat16),
        in_specs=[pl.BlockSpec(memory_space=pl.ANY), pl.BlockSpec(memory_space=pltpu.VMEM)],
        out_specs=pl.BlockSpec(memory_space=pl.ANY),
        scratch_shapes=[
            pltpu.VMEM(*held),
            pltpu.VMEM(*results),
            pltpu.SemaphoreType.DMA((slots,)),
            pltpu.SemaphoreType.DMA((parts,)),
        ],
        compiler_params=pltpu.CompilerParams(vmem_limit_bytes=scratch_bytes(held, results, results) + 8 * mib),
        cost_estimate=pl.CostEstimate(
            flops=2 * high * deep * width,
            bytes_accessed=2 * (high * deep + deep * width + high * width),
            transcendentals=0,
        ),
        name="backward_product",
    )(dense, grads)


def shifted(value, axis, step):
    size = lax.axis_size(axis)
    return lax.ppermute(value, axis, [(i, (i + step) % size) for i in range(size)])


def summed_everywhere(terms):
    devices = lax.axis_size("row") * lax.axis_size("col")
    height, width = terms.shape
    rows = height // devices
    if rows < 8:
        return lax.psum(terms, ("row", "col"))
    sent = lax.all_to_all(terms.reshape(devices, rows, width), ("row", "col"), 0, 0, tiled=True)
    owned = jnp.sum(sent, axis=0)
    copies = jnp.broadcast_to(owned[None], (devices, rows, width))
    return lax.all_to_all(copies, ("row", "col"), 0, 0, tiled=True).reshape(height, width)


def per_device(features, weight, adj_tiles, tile_rows, tile_cols, tile_counts, out_grad):
    node_rows, width = features.shape
    capacity, side = adj_tiles.shape[2:4]
    tiles = adj_tiles.reshape(capacity, side, side)
    rows = tile_rows.reshape(capacity)
    cols = tile_cols.reshape(capacity)
    count = tile_counts.reshape(1)
    row_count = lax.axis_size("row")
    col_count = lax.axis_size("col")
    per_strip = node_rows // side
    col_place = lax.axis_index("col").astype(jnp.int32).reshape(1)

    half = width // 2
    halves = [lax.all_gather(features[:, at : at + half], "row", axis=0, tiled=True) for at in (0, half)]
    dense = build_dense(rows, cols, count, tiles, col_count * per_strip, row_count * per_strip, per_strip)

    cells = forward_product(col_place, dense, halves, col_count)
    parts = [cells[0]] + [shifted(cells[step], "col", step) for step in range(1, col_count)]
    activations, back, terms = middle(parts, weight, out_grad, node_rows * row_count * col_count)
    grad_weight = summed_everywhere(terms)
    grads = lax.all_gather(back, "col", axis=0, tiled=True)

    cell_back = backward_product(dense, grads, row_count)
    back_parts = lax.all_to_all(cell_back, "row", 0, 0, tiled=True)
    grad_features = jnp.sum(back_parts.astype(jnp.float32), axis=0).astype(jnp.bfloat16)
    return (activations, grad_features, grad_weight)


def solution(mesh):
    placed = (
        P(("row", "col"), None),
        P(),
        P("row", "col", None, None, None),
        P("row", "col", None),
        P("row", "col", None),
        P("row", "col"),
        P(("row", "col"), None),
    )
    return jax.shard_map(
        per_device,
        mesh=mesh,
        in_specs=placed,
        out_specs=(P(("row", "col"), None), P(("row", "col"), None), P()),
        check_vma=False,
    )
```

time: 123 us -> 157 us (1.28)
  blocking collectives: 8.33 us -> 88.2 us
  starting transfers between devices: 42.7 us -> 11.7 us
  Pallas kernels: 23.1 us -> 11.8 us
  waiting for transfers between devices: 41 us -> 30.9 us
  local copies, waits for them, and re-layouts: 3.66 us -> 11.2 us
    all_gather x0 -> x2, blocking collectives: none -> 64.3 us  [per_device(): lax.all_gather(features[:, at:at + half], 'row', axis=0, tiled=True)]
    ppermute x20 -> x3, starting transfers between devices: 32.7 us -> 3.25 us  [shifted(): lax.ppermute(value, axis, [(i, (i + step) % size) for i in range(size)])]
    ppermute x20 -> x3, waiting for transfers between devices: 32.2 us -> 4.66 us  [shifted(): lax.ppermute(value, axis, [(i, (i + step) % size) for i in range(size)])]
    all_to_all x1, waiting for transfers between devices: 0.01 us -> 26.3 us  [per_device(): back_parts = lax.all_to_all(cell_back, 'row', 0, 0, tiled=True)]
    all_to_all x0 -> x1, blocking collectives: none -> 15 us  [summed_everywhere(): lax.all_to_all(terms.reshape(devices, rows, width), ('row', 'col'), 0, 0,...]
    all_to_all x1, waiting for transfers between devices: 8.78 us -> 0.01 us  [summed_everywhere(): lax.all_to_all(copies, ('row', 'col'), 0, 0, tiled=True)]
    pallas_call x4 -> x3, Pallas kernels: 16 us -> 8.18 us  [the longest x1 3.89 us: build_dense(): pl.pallas_call(functools.partial(build_kernel, blocks=blocks, steps=steps...]
    unnamed x34 -> x15, local copies, waits for them, and re-layouts: 3.09 us -> 9.58 us
  transfers between devices with their start and end apart: 22 -> 5, of which waited for: 10 -> 4; matrix products, arithmetic and copies ran while one was open for 1% -> 0% of each run, Pallas kernels for 11% -> 2%
where the time goes in v2:
time: 157 us; the launch traced here: 156 us
  blocking collectives  88.2 us (56%)
  waiting for transfers between devices  30.9 us (20%)
  Pallas kernels  11.8 us (8%)
  starting transfers between devices  11.7 us (7%)
  local copies, waits for them, and re-layouts  11.2 us (7%)
    all_gather x2, blocking collectives, per_device(): lax.all_gather(features[:, at:at + half], 'row', axis=0, tiled=True)  64.3 us
    all_to_all x1, waiting for transfers between devices, per_device(): back_parts = lax.all_to_all(cell_back, 'row', 0, 0, tiled=True)  26.3 us
    all_to_all x1, blocking collectives, summed_everywhere(): lax.all_to_all(terms.reshape(devices, rows, width), ('row', 'col'), 0, 0,...  15 us
    unnamed x15, local copies, waits for them, and re-layouts  9.58 us
    all_gather x1, blocking collectives, per_device(): grads = lax.all_gather(back, 'col', axis=0, tiled=True)  8.99 us
    all_to_all x1, starting transfers between devices, per_device(): back_parts = lax.all_to_all(cell_back, 'row', 0, 0, tiled=True)  5.91 us
    ppermute x3, waiting for transfers between devices, shifted(): lax.ppermute(value, axis, [(i, (i + step) % size) for i in range(size)])  4.66 us
    pallas_call x1, Pallas kernels, build_dense(): pl.pallas_call(functools.partial(build_kernel, blocks=blocks, steps=steps...  3.89 us
  transfers between devices with their start and end apart: 5, of which 4 were waited for; matrix products, arithmetic and copies ran while one was open for 0% of the time, Pallas kernels for 2%

profile of v2, /device:TPU:0, one launch (start us, length us, event | category | flops | bytes accessed | tf_op | source)
XLA Modules:
  0.0 156.1 jit_solution(9623361558497404564)
XLA Ops:
  1.3 0.9 fusion
  2.2 33.0 %all_gather.10.refs_1_ = bf16[2048,128]{1,0:T(8,128)(2,1)S(1)} all-gather(bf16[256,128]{1,0:T(8,128)(2,1)S(1)} %get-tuple-element.17), channel_id=1, replica_groups=mesh['row'=8,'col'=4] {'row'}, dimensions={0}, use_global_device_ids=true | all-gather | bytes 589824 | tf_op jit(solution)/shard_map/all_gather | solution.py:306
  35.2 31.3 %all_gather.9.refs_0_ = bf16[2048,128]{1,0:T(8,128)(2,1)S(1)} all-gather(bf16[256,128]{1,0:T(8,128)(2,1)S(1)} %get-tuple-element.18), channel_id=1, replica_groups=mesh['row'=8,'col'=4] {'row'}, dimensions={0}, use_global_device_ids=true | all-gather | bytes 589824 | tf_op jit(solution)/shard_map/all_gather | solution.py:306
  66.4 0.0 copy-start.2
  66.4 3.4 %copy-done.2 = bf16[1,1,256,128,128]{4,3,2,1,0:T(8,128)(2,1)S(1)} copy-done((bf16[1,1,256,128,128]{4,3,2,1,0:T(8,128)(2,1)S(1)}, bf16[1,1,256,128,128]{4,3,2,1,0:T(8,128)(2,1)}, u32[]{:S(2)}) %copy-start.2) | copy-done | bytes 8388632
  69.8 0.0 copy-start.5
  69.8 0.7 copy-done.5
  70.5 0.0 copy-start.6
  70.5 0.7 copy-done.6
  71.2 0.0 copy-start.3
  71.2 0.0 copy-start.4
  71.2 3.9 %build_dense.1.dense_ref = bf16[1024,2048]{1,0:T(8,128)(2,1)S(1)} custom-call(s32[256]{0:T(256)S(1)} %bitcast.10, s32[256]{0:T(256)S(1)} %bitcast.11, s32[1]{0:T(128)} %bitcast.7.count_ref, bf16[256,128,128]{2,1,0:T(8,128)(2,1)S(1)} %bitcast.8), custom_call_target="tpu_custom_call" | custom-call | flops 4194304 | bytes 12582912 | tf_op jit(solution)/shard_map/build_dense/pallas_call | solution.py:86
  75.1 3.3 %forward_product.1 = (bf16[256,256]{1,0:T(8,128)(2,1)S(1)}, bf16[256,256]{1,0:T(8,128)(2,1)S(1)}, bf16[256,256]{1,0:T(8,128)(2,1)S(1)}, bf16[256,256]{1,0:T(8,128)(2,1)S(1)}) custom-call(s32[1]{0:T(128)} %bitcast.place_ref, bf16[1024,2048]{1,0:T(8,128)(2,1)S(1)} %build_dense.1.dense_ref, bf16[2048,128]{1,0:T(8,128)(2,1)S(1)} %all_gather.9.refs_0_, ...), custom_call_target="tpu_custom_call" | custom-call | flops 1073741824 | bytes 5767168 | tf_op jit(solution)/shard_map/forward_product/pallas_call | solution.py:150
  78.4 0.0 copy-start
  78.4 1.9 %copy-done = bf16[1024,2048]{1,0:T(8,128)(2,1)} copy-done((bf16[1024,2048]{1,0:T(8,128)(2,1)}, bf16[1024,2048]{1,0:T(8,128)(2,1)S(1)}, u32[]{:S(2)}) %copy-start) | copy-done | bytes 4194328
  80.4 0.0 collective-permute-start
  80.4 1.8 %collective-permute-start.1 = (bf16[256,256]{1,0:T(8,128)(2,1)S(1)}, bf16[256,256]{1,0:T(8,128)(2,1)S(1)}, u32[]{:S(2)}, u32[]{:S(2)}) collective-permute-start(bf16[256,256]{1,0:T(8,128)(2,1)S(1)} %get-tuple-element.12), channel_id=1, source_target_pairs={{0,2},{1,3},{2,0},{3,1},{4,6},{5,7},{6,4},{7,5},{8,10},{9,11},{10,... | collective-permute-start | bytes 393224 | tf_op jit(solution)/shard_map/ppermute | solution.py:278
  82.2 1.4 collective-permute-start.2
  83.6 2.0 %collective-permute-done.refs_1_ = bf16[256,256]{1,0:T(8,128)(2,1)S(1)} collective-permute-done((bf16[256,256]{1,0:T(8,128)(2,1)S(1)}, bf16[256,256]{1,0:T(8,128)(2,1)S(1)}, u32[]{:S(2)}, u32[]{:S(2)}) %collective-permute-start) | collective-permute-done | bytes 131104 | tf_op jit(solution)/shard_map/ppermute | solution.py:278
  85.6 1.1 collective-permute-done.1.refs_2_
  86.7 1.6 %collective-permute-done.2.refs_3_ = bf16[256,256]{1,0:T(8,128)(2,1)S(1)} collective-permute-done((bf16[256,256]{1,0:T(8,128)(2,1)S(1)}, bf16[256,256]{1,0:T(8,128)(2,1)S(1)}, u32[]{:S(2)}, u32[]{:S(2)}) %collective-permute-start.2) | collective-permute-done | bytes 131104 | tf_op jit(solution)/shard_map/ppermute | solution.py:278
  88.3 0.0 copy-done.3
  88.3 0.0 copy-done.4
  88.3 1.0 middle.1
  89.2 15.0 %all_to_all.15 = f32[32,8,256]{2,1,0:T(8,128)S(1)} all-to-all(f32[32,8,256]{2,1,0:T(8,128)S(1)} %bitcast.9), channel_id=1, replica_groups=mesh['row'=8,'col'=4] {'row','col'}, dimensions={0} | all-to-all | bytes 524288 | tf_op jit(solution)/shard_map/all_to_all | solution.py:287
  104.3 0.7 broadcast_in_dim.2
  105.0 2.6 %all-to-all-start.2 = ((f32[32,8,256]{2,1,0:T(8,128)}), f32[32,8,256]{2,1,0:T(8,128)S(1)}, u32[]{:S(2)}, u32[]{:S(2)}) async-start(f32[32,8,256]{2,1,0:T(8,128)} %broadcast_in_dim.2), calls=%async_computation.2 | async-start | bytes 524288 | tf_op jit(solution)/shard_map/all_to_all | solution.py:290
  107.6 9.0 %all_gather.11.grads_ref = bf16[1024,256]{1,0:T(8,128)(2,1)S(1)} all-gather(bf16[256,256]{1,0:T(8,128)(2,1)S(1)} %get-tuple-element.15), channel_id=1, replica_groups=mesh['row'=8,'col'=4] {'col'}, dimensions={0}, use_global_device_ids=true | all-gather | bytes 655360 | tf_op jit(solution)/shard_map/all_gather | solution.py:313
  116.6 0.0 copy-start.1
  116.6 2.2 %copy-done.1 = bf16[1024,2048]{1,0:T(8,128)(2,1)S(1)} copy-done((bf16[1024,2048]{1,0:T(8,128)(2,1)S(1)}, bf16[1024,2048]{1,0:T(8,128)(2,1)}, u32[]{:S(2)}) %copy-start.1) | copy-done | bytes 4194328
  118.7 3.7 %backward_product.1 = bf16[8,256,256]{2,1,0:T(8,128)(2,1)} custom-call(bf16[1024,2048]{1,0:T(8,128)(2,1)S(1)} %copy-done.1, bf16[1024,256]{1,0:T(8,128)(2,1)S(1)} %all_gather.11.grads_ref), custom_call_target="tpu_custom_call" | custom-call | flops 1073741824 | bytes 5767168 | tf_op jit(solution)/shard_map/backward_product/pallas_call | solution.py:255
  122.4 0.0 all-to-all-done.2
  122.4 5.9 %all-to-all-start = ((bf16[8,256,256]{2,1,0:T(8,128)(2,1)}), bf16[8,256,256]{2,1,0:T(8,128)(2,1)S(1)}, u32[]{:S(2)}, u32[]{:S(2)}) async-start(bf16[8,256,256]{2,1,0:T(8,128)(2,1)} %backward_product.1), calls=%async_computation | async-start | bytes 2097152 | tf_op jit(solution)/shard_map/all_to_all | solution.py:316
  128.3 26.3 %all-to-all-done = bf16[8,256,256]{2,1,0:T(8,128)(2,1)S(1)} async-done(((bf16[8,256,256]{2,1,0:T(8,128)(2,1)}), bf16[8,256,256]{2,1,0:T(8,128)(2,1)S(1)}, u32[]{:S(2)}, u32[]{:S(2)}) %all-to-all-start) | async-done | bytes 1048608 | tf_op jit(solution)/shard_map/all_to_all | solution.py:316
  154.6 0.8 reduce_sum.21
  155.4 0.7 copy.12
  (1 shorter events, 0.0 us)
Async XLA Ops:
  66.4 3.4 %copy-start.2 = (bf16[1,1,256,128,128]{4,3,2,1,0:T(8,128)(2,1)S(1)}, bf16[1,1,256,128,128]{4,3,2,1,0:T(8,128)(2,1)}, u32[]{:S(2)}) copy-start(bf16[1,1,256,128,128]{4,3,2,1,0:T(8,128)(2,1)} %param.9) | copy-start | bytes 25165828
  69.8 0.7 copy-start.5
  70.5 0.7 copy-start.6
  71.2 17.1 %copy-start.3 = (bf16[256,256]{1,0:T(8,128)(2,1)S(1)}, bf16[256,256]{1,0:T(8,128)(2,1)}, u32[]{:S(2)}) copy-start(bf16[256,256]{1,0:T(8,128)(2,1)} %refs_4_.1) | copy-start | bytes 393220
  71.2 17.1 %copy-start.4 = (bf16[256,256]{1,0:T(8,128)(2,1)S(1)}, bf16[256,256]{1,0:T(8,128)(2,1)}, u32[]{:S(2)}) copy-start(bf16[256,256]{1,0:T(8,128)(2,1)} %refs_5_.1) | copy-start | bytes 393220
  78.4 2.0 %copy-start = (bf16[1024,2048]{1,0:T(8,128)(2,1)}, bf16[1024,2048]{1,0:T(8,128)(2,1)S(1)}, u32[]{:S(2)}) copy-start(bf16[1024,2048]{1,0:T(8,128)(2,1)S(1)} %build_dense.1.dense_ref) | copy-start | bytes 12582916
  80.4 5.2 %collective-permute-start = (bf16[256,256]{1,0:T(8,128)(2,1)S(1)}, bf16[256,256]{1,0:T(8,128)(2,1)S(1)}, u32[]{:S(2)}, u32[]{:S(2)}) collective-permute-start(bf16[256,256]{1,0:T(8,128)(2,1)S(1)} %get-tuple-element.11), channel_id=1, source_target_pairs={{0,1},{1,2},{2,3},{3,0},{4,5},{5,6},{6,7},{7,4},{8,9},{9,10},{10,1... | collective-permute-start | bytes 393224 | tf_op jit(solution)/shard_map/ppermute | solution.py:278
  80.4 6.3 %collective-permute-start.1 = (bf16[256,256]{1,0:T(8,128)(2,1)S(1)}, bf16[256,256]{1,0:T(8,128)(2,1)S(1)}, u32[]{:S(2)}, u32[]{:S(2)}) collective-permute-start(bf16[256,256]{1,0:T(8,128)(2,1)S(1)} %get-tuple-element.12), channel_id=1, source_target_pairs={{0,2},{1,3},{2,0},{3,1},{4,6},{5,7},{6,4},{7,5},{8,10},{9,11},{10,... | collective-permute-start | bytes 393224 | tf_op jit(solution)/shard_map/ppermute | solution.py:278
  82.2 6.1 %collective-permute-start.2 = (bf16[256,256]{1,0:T(8,128)(2,1)S(1)}, bf16[256,256]{1,0:T(8,128)(2,1)S(1)}, u32[]{:S(2)}, u32[]{:S(2)}) collective-permute-start(bf16[256,256]{1,0:T(8,128)(2,1)S(1)} %get-tuple-element.13), channel_id=1, source_target_pairs={{0,3},{1,0},{2,1},{3,2},{4,7},{5,4},{6,5},{7,6},{8,11},{9,8},{10,9... | collective-permute-start | bytes 393224 | tf_op jit(solution)/shard_map/ppermute | solution.py:278
  105.0 17.4 %all-to-all-start.2 = ((f32[32,8,256]{2,1,0:T(8,128)}), f32[32,8,256]{2,1,0:T(8,128)S(1)}, u32[]{:S(2)}, u32[]{:S(2)}) async-start(f32[32,8,256]{2,1,0:T(8,128)} %broadcast_in_dim.2), calls=%async_computation.2 | async-start | bytes 524288 | tf_op jit(solution)/shard_map/all_to_all | solution.py:290
  116.6 2.2 %copy-start.1 = (bf16[1024,2048]{1,0:T(8,128)(2,1)S(1)}, bf16[1024,2048]{1,0:T(8,128)(2,1)}, u32[]{:S(2)}) copy-start(bf16[1024,2048]{1,0:T(8,128)(2,1)} %copy-done) | copy-start | bytes 12582916
  122.4 32.2 %all-to-all-start = ((bf16[8,256,256]{2,1,0:T(8,128)(2,1)}), bf16[8,256,256]{2,1,0:T(8,128)(2,1)S(1)}, u32[]{:S(2)}, u32[]{:S(2)}) async-start(bf16[8,256,256]{2,1,0:T(8,128)(2,1)} %backward_product.1), calls=%async_computation | async-start | bytes 2097152 | tf_op jit(solution)/shard_map/all_to_all | solution.py:316

commit v3 on v2

v3 whole, which is shorter than its diff:
```python
import functools
import math

import jax
import jax.numpy as jnp
from jax import lax
from jax.experimental import pallas as pl
from jax.experimental.pallas import tpu as pltpu
from jax.sharding import PartitionSpec as P

chunk_tiles = 16
chunk_slots = 4
strips_per_step = 8
mib = 1024 * 1024


def scratch_bytes(*shapes):
    return sum(math.prod(shape) * jnp.dtype(kind).itemsize for shape, kind in shapes)


def build_kernel(rows_ref, cols_ref, count_ref, tiles_ref, dense_ref, total, held, sems, *, blocks, steps):
    side = tiles_ref.shape[1]
    first_block = pl.program_id(0) * blocks
    count = count_ref[0]
    chunks = (count + chunk_tiles - 1) // chunk_tiles

    def fetch(index):
        slot = lax.rem(index, chunk_slots)
        return pltpu.make_async_copy(
            tiles_ref.at[pl.ds(index * chunk_tiles, chunk_tiles)], held.at[slot], sems.at[slot]
        )

    for ahead in range(chunk_slots - 1):
        @pl.when(ahead < chunks)
        def _():
            fetch(ahead).start()

    row_blocks = dense_ref.shape[0] // side

    def clear(block, carry):
        down = pl.ds(pl.multiple_of(block * side, side), side)
        total[down, :] = jnp.zeros((side, total.shape[1]), jnp.float32)
        return carry

    lax.fori_loop(0, row_blocks, clear, 0)

    def chunk_step(index, carry):
        @pl.when(index + chunk_slots - 1 < chunks)
        def _():
            fetch(index + chunk_slots - 1).start()

        fetch(index).wait()
        slot = lax.rem(index, chunk_slots)
        for lane in range(chunk_tiles):
            place = index * chunk_tiles + lane
            col = cols_ref[place] - first_block
            live = place < count
            if steps > 1:
                live = live & (col >= 0) & (col < blocks)
                col = jnp.where(live, col, 0)
            row = jnp.where(live, rows_ref[place], row_blocks)
            down = pl.ds(pl.multiple_of(row * side, side), side)
            along = pl.ds(pl.multiple_of(col * side, side), side)
            total[down, along] += held[slot, lane].astype(jnp.float32)
        return carry

    lax.fori_loop(0, chunks, chunk_step, 0)

    def round_block(block, carry):
        down = pl.ds(pl.multiple_of(block * side, side), side)
        dense_ref[down, :] = total[down, :].astype(jnp.bfloat16)
        return carry

    lax.fori_loop(0, row_blocks, round_block, 0)


def build_dense(rows, cols, count, tiles, row_blocks, col_blocks, per_strip):
    capacity, side, _ = tiles.shape
    blocks = min(strips_per_step * per_strip, col_blocks)
    steps = col_blocks // blocks
    high, wide = row_blocks * side, blocks * side
    total = ((high + side, wide), jnp.float32)
    held = ((chunk_slots, chunk_tiles, side, side), jnp.bfloat16)
    block = ((high, wide), jnp.bfloat16)
    return pl.pallas_call(
        functools.partial(build_kernel, blocks=blocks, steps=steps),
        out_shape=jax.ShapeDtypeStruct((high, col_blocks * side), jnp.bfloat16),
        grid_spec=pltpu.PrefetchScalarGridSpec(
            num_scalar_prefetch=3,
            grid=(steps,),
            in_specs=[pl.BlockSpec(memory_space=pltpu.HBM)],
            out_specs=pl.BlockSpec((high, wide), lambda i, *_: (0, i)),
            scratch_shapes=[
                pltpu.VMEM(*total),
                pltpu.VMEM(*held),
                pltpu.SemaphoreType.DMA((chunk_slots,)),
            ],
        ),
        compiler_params=pltpu.CompilerParams(vmem_limit_bytes=46 * mib),
        cost_estimate=pl.CostEstimate(
            flops=capacity * side * side,
            bytes_accessed=2 * (capacity * side * side + high * col_blocks * side),
            transcendentals=0,
        ),
        name="build_dense",
    )(rows, cols, count, tiles)


def ring_place(row, count):
    return jnp.where(lax.rem(row, 2) == 0, row // 2, count - 1 - row // 2)


def ring_row(place, count):
    place = lax.rem(place + 2 * count, count)
    return jnp.where(place < count // 2, 2 * place, 2 * (count - 1 - place) + 1)


def forward_kernel(row_ref, col_ref, dense_ref, *refs, offsets, partners, row_count):
    piece_refs, refs = refs[: len(offsets)], refs[len(offsets) :]
    out_refs, (depth, sems) = refs[:-2], refs[-2:]
    rows = out_refs[0].shape[0]
    place = ring_place(row_ref[0], row_count)
    copies = []
    for index, (offset, piece) in enumerate(zip(offsets, piece_refs)):
        high = piece.shape[0]
        down = pl.ds(pl.multiple_of(ring_row(place + offset, row_count) * high, high), high)
        copy = pltpu.make_async_copy(piece, depth.at[down], sems.at[index])
        copy.start()
        copies.append(copy)
    for copy in copies:
        copy.wait()
    for partner, out_ref in zip(partners, out_refs):
        down = pl.ds(pl.multiple_of((col_ref[0] ^ partner) * rows, rows), rows)
        part = jnp.dot(dense_ref[down, :], depth[...], preferred_element_type=jnp.float32)
        out_ref[...] = part.astype(jnp.bfloat16)


def forward_product(row_place, col_place, dense, shards, partners, row_count, col_count):
    offsets = tuple(offset for offset, _ in shards)
    arrays = [array for _, array in shards]
    high, deep = dense.shape
    width = arrays[0].shape[1]
    rows = high // col_count
    cell = ((high, deep), jnp.bfloat16)
    depth = ((deep, width), jnp.bfloat16)
    out = ((high, width), jnp.float32)
    return pl.pallas_call(
        functools.partial(forward_kernel, offsets=offsets, partners=partners, row_count=row_count),
        out_shape=[jax.ShapeDtypeStruct((rows, width), jnp.bfloat16)] * len(partners),
        in_specs=[pl.BlockSpec(memory_space=pltpu.SMEM)] * 2
        + [pl.BlockSpec(memory_space=pltpu.VMEM)]
        + [pl.BlockSpec(memory_space=pl.ANY)] * len(arrays),
        out_specs=[pl.BlockSpec(memory_space=pltpu.VMEM)] * len(partners),
        scratch_shapes=[pltpu.VMEM(*depth), pltpu.SemaphoreType.DMA((len(arrays),))],
        compiler_params=pltpu.CompilerParams(vmem_limit_bytes=scratch_bytes(cell, depth, out) + 6 * mib),
        cost_estimate=pl.CostEstimate(
            flops=2 * rows * len(partners) * deep * width,
            bytes_accessed=2 * (rows * len(partners) * deep + deep * width + rows * len(partners) * width),
            transcendentals=0,
        ),
        name="forward_product",
    )(row_place, col_place, dense, *arrays)


def middle_kernel(*refs, count, scale):
    parts = refs[:count]
    weight_ref, cotangent_ref, act_ref, back_ref, terms_ref = refs[count:]
    aggregate = parts[0][...].astype(jnp.float32)
    for part in parts[1:]:
        aggregate += part[...].astype(jnp.float32)
    high = aggregate.astype(jnp.bfloat16)
    low = (aggregate - high.astype(jnp.float32)).astype(jnp.bfloat16)
    weight = weight_ref[...]
    pre = jnp.dot(high, weight, preferred_element_type=jnp.float32)
    pre += jnp.dot(low, weight, preferred_element_type=jnp.float32)
    sig = jax.nn.sigmoid(pre)
    grad = (cotangent_ref[...].astype(jnp.float32) * sig * (1.0 + pre * (1.0 - sig))).astype(jnp.bfloat16)
    back_ref[...] = lax.dot_general(
        weight, grad, (((1,), (1,)), ((), ())), preferred_element_type=jnp.float32
    ).astype(jnp.bfloat16)
    act_ref[...] = (pre * sig).astype(jnp.bfloat16)
    over_nodes = (((0,), (0,)), ((), ()))
    terms = lax.dot_general(high, grad, over_nodes, preferred_element_type=jnp.float32)
    terms += lax.dot_general(low, grad, over_nodes, preferred_element_type=jnp.float32)
    terms_ref[...] = terms * scale


def middle(parts, weight, cotangent, total_nodes):
    rows, width = cotangent.shape
    count = len(parts)
    return pl.pallas_call(
        functools.partial(middle_kernel, count=count, scale=1.0 / math.sqrt(total_nodes)),
        out_shape=[
            jax.ShapeDtypeStruct((rows, width), jnp.bfloat16),
            jax.ShapeDtypeStruct((width, rows), jnp.bfloat16),
            jax.ShapeDtypeStruct((width, width), jnp.float32),
        ],
        in_specs=[pl.BlockSpec(memory_space=pltpu.VMEM)] * (count + 2),
        out_specs=[pl.BlockSpec(memory_space=pltpu.VMEM)] * 3,
        compiler_params=pltpu.CompilerParams(vmem_limit_bytes=12 * mib),
        cost_estimate=pl.CostEstimate(
            flops=10 * rows * width * width, bytes_accessed=2 * (count + 6) * rows * width, transcendentals=rows * width
        ),
        name="middle",
    )(*parts, weight, cotangent)


def backward_kernel(row_ref, col_ref, dense_ref, *refs, count, offsets, row_count):
    grad_refs, refs = refs[:count], refs[count:]
    out_refs, (depth, sems) = refs[:-2], refs[-2:]
    width, rows = grad_refs[0].shape
    wide = dense_ref.shape[1] // row_count
    copies = []
    for partner, grad in enumerate(grad_refs):
        along = pl.ds(pl.multiple_of((col_ref[0] ^ partner) * rows, rows), rows)
        copy = pltpu.make_async_copy(grad, depth.at[:, along], sems.at[partner])
        copy.start()
        copies.append(copy)
    for copy in copies:
        copy.wait()
    place = ring_place(row_ref[0], row_count)
    for index, offset in enumerate(offsets):
        along = pl.ds(pl.multiple_of(ring_row(place + offset, row_count) * wide, wide), wide)
        part = jnp.dot(depth[...], dense_ref[:, along], preferred_element_type=jnp.float32)
        out_refs[index][...] = part.astype(jnp.bfloat16)


def backward_product(row_place, col_place, dense, grads, offsets, row_count):
    high, deep = dense.shape
    width = grads[0].shape[0]
    wide = deep // row_count
    cell = ((high, deep), jnp.bfloat16)
    depth = ((width, high), jnp.bfloat16)
    out = ((len(offsets), width, wide), jnp.float32)
    return pl.pallas_call(
        functools.partial(backward_kernel, count=len(grads), offsets=offsets, row_count=row_count),
        out_shape=[jax.ShapeDtypeStruct((width, wide), jnp.bfloat16)] * len(offsets),
        in_specs=[pl.BlockSpec(memory_space=pltpu.SMEM)] * 2
        + [pl.BlockSpec(memory_space=pltpu.VMEM)]
        + [pl.BlockSpec(memory_space=pl.ANY)] * len(grads),
        out_specs=[pl.BlockSpec(memory_space=pltpu.VMEM)] * len(offsets),
        scratch_shapes=[pltpu.VMEM(*depth), pltpu.SemaphoreType.DMA((len(grads),))],
        compiler_params=pltpu.CompilerParams(vmem_limit_bytes=scratch_bytes(cell, depth, out) + 6 * mib),
        cost_estimate=pl.CostEstimate(
            flops=2 * high * wide * width, bytes_accessed=2 * wide * len(offsets) * width, transcendentals=0
        ),
        name="backward_product",
    )(row_place, col_place, dense, *grads)


def finish_kernel(first_ref, second_ref, third_ref, out_ref):
    total = first_ref[...].astype(jnp.float32) + second_ref[...].astype(jnp.float32) + third_ref[...].astype(jnp.float32)
    out_ref[...] = total.astype(jnp.bfloat16).T


def finish(first, second, third):
    width, rows = first.shape
    return pl.pallas_call(
        finish_kernel,
        out_shape=jax.ShapeDtypeStruct((rows, width), jnp.bfloat16),
        in_specs=[pl.BlockSpec(memory_space=pltpu.VMEM)] * 3,
        out_specs=pl.BlockSpec(memory_space=pltpu.VMEM),
        compiler_params=pltpu.CompilerParams(vmem_limit_bytes=8 * mib),
        cost_estimate=pl.CostEstimate(flops=3 * rows * width, bytes_accessed=8 * rows * width, transcendentals=0),
        name="finish",
    )(first, second, third)


def around(value, step):
    count = lax.axis_size("row")
    order = list(range(0, count, 2)) + list(range(count - 1, 0, -2))
    return lax.ppermute(value, "row", [(order[i], order[(i + step) % count]) for i in range(count)])


def swapped(value, axis, partner):
    return lax.ppermute(value, axis, [(i, i ^ partner) for i in range(lax.axis_size(axis))])


def gathered_shards(own, beside):
    reach = lax.axis_size("row") // 2
    shards = [(0, own)]
    up = down = own
    for step in range(1, reach + 1):
        up = around(up, 1)
        shards.append((-step, up))
        if step < reach:
            down = around(down, -1)
            shards.append((step, down))
        if step == 1:
            up, down, beside = lax.optimization_barrier((up, down, beside))
    return shards, beside


def added(first, second):
    return (first.astype(jnp.float32) + second.astype(jnp.float32)).astype(jnp.bfloat16)


def summed_everywhere(terms):
    place = lax.axis_index("col")
    bits = [1 << bit for bit in range((lax.axis_size("col") - 1).bit_length())]
    for bit in bits:
        half = terms.shape[0] // 2
        upper = (place & bit) != 0
        kept = jnp.where(upper, terms[half:], terms[:half])
        sent = jnp.where(upper, terms[:half], terms[half:])
        terms = kept + swapped(sent, "col", bit)
    for bit in [1 << bit for bit in range((lax.axis_size("row") - 1).bit_length())]:
        terms = terms + swapped(terms, "row", bit)
    for bit in reversed(bits):
        other = swapped(terms, "col", bit)
        upper = (place & bit) != 0
        terms = jnp.concatenate([jnp.where(upper, other, terms), jnp.where(upper, terms, other)])
    return terms


def per_device(features, weight, adj_tiles, tile_rows, tile_cols, tile_counts, out_grad):
    node_rows, width = features.shape
    capacity, side = adj_tiles.shape[2:4]
    tiles = adj_tiles.reshape(capacity, side, side)
    rows = tile_rows.reshape(capacity)
    cols = tile_cols.reshape(capacity)
    count = tile_counts.reshape(1)
    row_count = lax.axis_size("row")
    col_count = lax.axis_size("col")
    per_strip = node_rows // side
    row_place = lax.axis_index("row").astype(jnp.int32).reshape(1)
    col_place = lax.axis_index("col").astype(jnp.int32).reshape(1)

    dense = build_dense(rows, cols, count, tiles, col_count * per_strip, row_count * per_strip, per_strip)
    shards, dense = gathered_shards(features, dense)

    far = tuple(range(col_count // 2, col_count))
    near = tuple(range(col_count // 2))
    sent = forward_product(row_place, col_place, dense, shards, far, row_count, col_count)
    parts = [swapped(part, "col", partner) for partner, part in zip(far, sent)]
    own, *sent = forward_product(row_place, col_place, dense, shards, near, row_count, col_count)
    parts += [own] + [swapped(part, "col", partner) for partner, part in zip(near[1:], sent)]

    activations, back, terms = middle(parts, weight, out_grad, node_rows * row_count * col_count)
    grads = [back] + [swapped(back, "col", partner) for partner in range(1, col_count)]
    grad_weight = summed_everywhere(terms)

    reach = row_count // 2
    (opposite,) = backward_product(row_place, col_place, dense, grads, (reach,), row_count)
    opposite, cell = lax.optimization_barrier((opposite, dense))
    up, down = around(opposite, 1), None
    offsets = tuple(sign * step for step in range(reach - 1, 0, -1) for sign in (1, -1)) + (0,)
    *strips, own = backward_product(row_place, col_place, cell, grads, offsets, row_count)
    for step in range(reach - 1):
        above, below = strips[2 * step : 2 * step + 2]
        up = around(added(above, up), 1)
        down = around(below if down is None else added(below, down), -1)
    grad_features = finish(own, up, down)
    return (activations, grad_features, grad_weight)


def solution(mesh):
    placed = (
        P(("row", "col"), None),
        P(),
        P("row", "col", None, None, None),
        P("row", "col", None),
        P("row", "col", None),
        P("row", "col"),
        P(("row", "col"), None),
    )
    return jax.shard_map(
        per_device,
        mesh=mesh,
        in_specs=placed,
        out_specs=(P(("row", "col"), None), P(("row", "col"), None), P()),
        check_vma=False,
    )
```

time: 157 us -> 91.3 us (0.58)
  blocking collectives: 88.2 us -> 0 us
  starting transfers between devices: 11.7 us -> 34.1 us
  waiting for transfers between devices: 30.9 us -> 32.6 us
    all_gather x3 -> x0, blocking collectives: 73.2 us -> none  [the longest x2 64.3 us: per_device(): lax.all_gather(features[:, at:at + half], 'row', axis=0, tiled=True)]
    ppermute x3 -> x27, starting transfers between devices: 3.25 us -> 34.1 us  [the longest x14 19.7 us: around(): lax.ppermute(value, 'row', [(order[i], order[(i + step) % count]) for i i...]
    ppermute x3 -> x27, waiting for transfers between devices: 4.66 us -> 32.6 us  [the longest x13 17.2 us: swapped(): lax.ppermute(value, axis, [(i, i ^ partner) for i in range(lax.axis_size(...]
    all_to_all x2 -> x0, waiting for transfers between devices: 26.3 us -> none  [the longest x1 26.3 us: per_device(): back_parts = lax.all_to_all(cell_back, 'row', 0, 0, tiled=True)]
    all_to_all x1 -> x0, blocking collectives: 15 us -> none  [summed_everywhere(): lax.all_to_all(terms.reshape(devices, rows, width), ('row', 'col'), 0, 0,...]
    all_to_all x2 -> x0, starting transfers between devices: 8.49 us -> none  [the longest x1 5.91 us: per_device(): back_parts = lax.all_to_all(cell_back, 'row', 0, 0, tiled=True)]
    unnamed x15 -> x18, local copies, waits for them, and re-layouts: 9.58 us -> 9.89 us
    pallas_call x2 -> x5, Pallas kernels: 6.98 us -> 6.81 us  [the longest x2 4.34 us: forward_product(): pl.pallas_call(functools.partial(forward_kernel, offsets=offsets, partner...]
  transfers between devices with their start and end apart: 5 -> 27, of which waited for: 4 -> 13; matrix products, arithmetic and copies ran while one was open for 0% -> 1% of each run, Pallas kernels for 2% -> 9%
where the time goes in v3:
time: 91.3 us; the launch traced here: 90.9 us
  starting transfers between devices  34.1 us (37%)
  waiting for transfers between devices  32.6 us (36%)
  Pallas kernels  11.8 us (13%)
  local copies, waits for them, and re-layouts  9.89 us (11%)
  between operations  1.47 us (2%)
  other arithmetic  1.03 us (1%)
    ppermute x14, starting transfers between devices, around(): lax.ppermute(value, 'row', [(order[i], order[(i + step) % count]) for i i...  19.7 us
    ppermute x13, waiting for transfers between devices, swapped(): lax.ppermute(value, axis, [(i, i ^ partner) for i in range(lax.axis_size(...  17.2 us
    ppermute x14, waiting for transfers between devices, around(): lax.ppermute(value, 'row', [(order[i], order[(i + step) % count]) for i i...  15.4 us
    ppermute x13, starting transfers between devices, swapped(): lax.ppermute(value, axis, [(i, i ^ partner) for i in range(lax.axis_size(...  14.4 us
    unnamed x18, local copies, waits for them, and re-layouts  9.89 us
    pallas_call x2, Pallas kernels, forward_product(): pl.pallas_call(functools.partial(forward_kernel, offsets=offsets, partner...  4.34 us
    pallas_call x1, Pallas kernels, build_dense(): pl.pallas_call(functools.partial(build_kernel, blocks=blocks, steps=steps...  4.04 us
  transfers between devices with their start and end apart: 27, of which 13 were waited for; matrix products, arithmetic and copies ran while one was open for 1% of the time, Pallas kernels for 9%

profile of v3, /device:TPU:0, one launch (start us, length us, event | category | flops | bytes accessed | tf_op | source)
XLA Modules:
  0.0 90.9 jit_solution(12798151170209202286)
XLA Ops:
  0.6 3.0 %collective-permute-start.1 = (bf16[256,256]{1,0:T(8,128)(2,1)}, bf16[256,256]{1,0:T(8,128)(2,1)S(1)}, u32[]{:S(2)}, u32[]{:S(2)}) collective-permute-start(bf16[256,256]{1,0:T(8,128)(2,1)} %refs_0_.3), channel_id=1, source_target_pairs={{0,4},{8,0},{16,8},{24,16},{28,24},{20,28},{12,20},{4,12},{1,5},{9... | collective-permute-start | bytes 393224 | tf_op jit(solution)/shard_map/ppermute | solution.py:272
  3.7 0.1 collective-permute-start
  4.4 0.7 copy-done.7
  5.1 0.7 copy-done.8
  5.8 4.0 %build_dense.1.dense_ref = bf16[1024,2048]{1,0:T(8,128)(2,1)S(1)} custom-call(s32[256]{0:T(256)S(1)} %bitcast.7, s32[256]{0:T(256)S(1)} %bitcast.8, s32[1]{0:T(128)} %bitcast.6.count_ref, bf16[256,128,128]{2,1,0:T(8,128)(2,1)} %bitcast.9), custom_call_target="tpu_custom_call" | custom-call | flops 4194304 | bytes 12582912 | tf_op jit(solution)/shard_map/build_dense/pallas_call | solution.py:85
  9.9 2.0 %copy-done = bf16[1024,2048]{1,0:T(8,128)(2,1)} copy-done((bf16[1024,2048]{1,0:T(8,128)(2,1)}, bf16[1024,2048]{1,0:T(8,128)(2,1)S(1)}, u32[]{:S(2)}) %copy-start) | copy-done | bytes 4194328
  11.8 0.0 collective-permute-done.1.refs_2_
  11.8 0.0 collective-permute-done.refs_1_
  11.8 1.8 %collective-permute-start.2 = (bf16[256,256]{1,0:T(8,128)(2,1)S(1)}, bf16[256,256]{1,0:T(8,128)(2,1)S(1)}, u32[]{:S(2)}, u32[]{:S(2)}) collective-permute-start(bf16[256,256]{1,0:T(8,128)(2,1)S(1)} %collective-permute-done.refs_1_), channel_id=1, source_target_pairs={{0,8},{8,16},{16,24},{24,28},{28,20},{20,12},{12,4},{4,0},{1,9},{9... | collective-permute-start | bytes 393224 | tf_op jit(solution)/shard_map/ppermute | solution.py:272
  13.6 0.3 collective-permute-start.3
  13.9 3.8 %collective-permute-done.2.refs_3_ = bf16[256,256]{1,0:T(8,128)(2,1)S(1)} collective-permute-done((bf16[256,256]{1,0:T(8,128)(2,1)S(1)}, bf16[256,256]{1,0:T(8,128)(2,1)S(1)}, u32[]{:S(2)}, u32[]{:S(2)}) %collective-permute-start.2) | collective-permute-done | bytes 131104 | tf_op jit(solution)/shard_map/ppermute | solution.py:272
  17.7 2.3 %collective-permute-start.4 = (bf16[256,256]{1,0:T(8,128)(2,1)S(1)}, bf16[256,256]{1,0:T(8,128)(2,1)S(1)}, u32[]{:S(2)}, u32[]{:S(2)}) collective-permute-start(bf16[256,256]{1,0:T(8,128)(2,1)S(1)} %collective-permute-done.2.refs_3_), channel_id=1, source_target_pairs={{0,8},{8,16},{16,24},{24,28},{28,20},{20,12},{12,4},{4,0},{1,9},{9... | collective-permute-start | bytes 393224 | tf_op jit(solution)/shard_map/ppermute | solution.py:272
  19.9 0.0 collective-permute-done.3.refs_4_
  19.9 0.0 collective-permute-start.5
  19.9 3.0 %collective-permute-done.4.refs_5_ = bf16[256,256]{1,0:T(8,128)(2,1)S(1)} collective-permute-done((bf16[256,256]{1,0:T(8,128)(2,1)S(1)}, bf16[256,256]{1,0:T(8,128)(2,1)S(1)}, u32[]{:S(2)}, u32[]{:S(2)}) %collective-permute-start.4) | collective-permute-done | bytes 131104 | tf_op jit(solution)/shard_map/ppermute | solution.py:272
  23.0 2.7 %collective-permute-start.6 = (bf16[256,256]{1,0:T(8,128)(2,1)S(1)}, bf16[256,256]{1,0:T(8,128)(2,1)S(1)}, u32[]{:S(2)}, u32[]{:S(2)}) collective-permute-start(bf16[256,256]{1,0:T(8,128)(2,1)S(1)} %collective-permute-done.4.refs_5_), channel_id=1, source_target_pairs={{0,8},{8,16},{16,24},{24,28},{28,20},{20,12},{12,4},{4,0},{1,9},{9... | collective-permute-start | bytes 393224 | tf_op jit(solution)/shard_map/ppermute | solution.py:272
  25.7 0.0 collective-permute-done.5.refs_6_
  25.7 2.5 %collective-permute-done.6.refs_7_ = bf16[256,256]{1,0:T(8,128)(2,1)S(1)} collective-permute-done((bf16[256,256]{1,0:T(8,128)(2,1)S(1)}, bf16[256,256]{1,0:T(8,128)(2,1)S(1)}, u32[]{:S(2)}, u32[]{:S(2)}) %collective-permute-start.6) | collective-permute-done | bytes 131104 | tf_op jit(solution)/shard_map/ppermute | solution.py:272
  28.2 2.2 %copy-done.1 = bf16[1024,2048]{1,0:T(8,128)(2,1)S(1)} copy-done((bf16[1024,2048]{1,0:T(8,128)(2,1)S(1)}, bf16[1024,2048]{1,0:T(8,128)(2,1)}, u32[]{:S(2)}) %copy-start.1) | copy-done | bytes 4194328
  30.4 2.1 %forward_product.3 = (bf16[256,256]{1,0:T(8,128)(2,1)S(1)}, bf16[256,256]{1,0:T(8,128)(2,1)S(1)}) custom-call(s32[1]{0:T(128)} %bitcast.row_ref, s32[1]{0:T(128)} %bitcast.1.col_ref, bf16[1024,2048]{1,0:T(8,128)(2,1)S(1)} %copy-done.1, bf16[256,256]{1,0:T(8,128)(2,1)S(1)} %copy-done.4, bf16[256,256]{1,0:T(8,128)(2,1)S(1)} %collective-permute-done.refs_1_, ...), custom_call_target="tpu_custom_call" | custom-call | flops 536870912 | bytes 3407872 | tf_op jit(solution)/shard_map/forward_product/pallas_call | solution.py:147
  32.5 0.1 collective-permute-start.9
  32.6 2.2 %forward_product.2 = (bf16[256,256]{1,0:T(8,128)(2,1)S(1)}, bf16[256,256]{1,0:T(8,128)(2,1)S(1)}) custom-call(s32[1]{0:T(128)} %bitcast.row_ref, s32[1]{0:T(128)} %bitcast.1.col_ref, bf16[1024,2048]{1,0:T(8,128)(2,1)S(1)} %copy-done.1, bf16[256,256]{1,0:T(8,128)(2,1)S(1)} %copy-done.4, bf16[256,256]{1,0:T(8,128)(2,1)S(1)} %collective-permute-done.refs_1_, ...), custom_call_target="tpu_custom_call" | custom-call | flops 536870912 | bytes 3407872 | tf_op jit(solution)/shard_map/forward_product/pallas_call | solution.py:147
  34.8 3.2 %collective-permute-start.7 = (bf16[256,256]{1,0:T(8,128)(2,1)S(1)}, bf16[256,256]{1,0:T(8,128)(2,1)S(1)}, u32[]{:S(2)}, u32[]{:S(2)}) collective-permute-start(bf16[256,256]{1,0:T(8,128)(2,1)S(1)} %get-tuple-element.25), channel_id=1, source_target_pairs={{0,2},{1,3},{2,0},{3,1},{4,6},{5,7},{6,4},{7,5},{8,10},{9,11},{10,... | collective-permute-start | bytes 393224 | tf_op jit(solution)/shard_map/ppermute | solution.py:276
  38.1 0.1 collective-permute-start.8
  38.2 0.0 collective-permute-done.9.refs_3_
  38.2 4.2 %collective-permute-done.7.refs_0_ = bf16[256,256]{1,0:T(8,128)(2,1)S(1)} collective-permute-done((bf16[256,256]{1,0:T(8,128)(2,1)S(1)}, bf16[256,256]{1,0:T(8,128)(2,1)S(1)}, u32[]{:S(2)}, u32[]{:S(2)}) %collective-permute-start.7) | collective-permute-done | bytes 131104 | tf_op jit(solution)/shard_map/ppermute | solution.py:276
  42.4 2.3 %collective-permute-done.8.refs_1_ = bf16[256,256]{1,0:T(8,128)(2,1)S(1)} collective-permute-done((bf16[256,256]{1,0:T(8,128)(2,1)S(1)}, bf16[256,256]{1,0:T(8,128)(2,1)S(1)}, u32[]{:S(2)}, u32[]{:S(2)}) %collective-permute-start.8) | collective-permute-done | bytes 131104 | tf_op jit(solution)/shard_map/ppermute | solution.py:276
  44.7 1.0 %middle.1 = (bf16[256,256]{1,0:T(8,128)(2,1)}, bf16[256,256]{1,0:T(8,128)(2,1)S(1)}, f32[256,256]{1,0:T(8,128)S(1)}) custom-call(bf16[256,256]{1,0:T(8,128)(2,1)S(1)} %collective-permute-done.7.refs_0_, bf16[256,256]{1,0:T(8,128)(2,1)S(1)} %collective-permute-done.8.refs_1_, bf16[256,256]{1,0:T(8,128)(2,1)S(1)} %get-tuple-element.27.refs_2_, ...), custom_call_target="tpu_custom_call" | custom-call | flops 167772160 | bytes 1310720 | tf_op jit(solution)/shard_map/middle/pallas_call | solution.py:191
  45.7 0.2 collective-permute-start.20
  45.9 1.5 %collective-permute-start.12 = (bf16[256,256]{1,0:T(8,128)(2,1)S(1)}, bf16[256,256]{1,0:T(8,128)(2,1)S(1)}, u32[]{:S(2)}, u32[]{:S(2)}) collective-permute-start(bf16[256,256]{1,0:T(8,128)(2,1)S(1)} %get-tuple-element.30.refs_0_), channel_id=1, source_target_pairs={{0,3},{1,2},{2,1},{3,0},{4,7},{5,6},{6,5},{7,4},{8,11},{9,10},{10,... | collective-permute-start | bytes 393224 | tf_op jit(solution)/shard_map/ppermute | solution.py:276
  47.4 0.5 collective-permute-start.11
  47.9 0.0 collective-permute-start.10
  47.9 0.0 collective-permute-done.20
  48.0 1.6 %collective-permute-start.21 = (f32[64,256]{1,0:T(8,128)S(1)}, f32[64,256]{1,0:T(8,128)S(1)}, u32[]{:S(2)}, u32[]{:S(2)}) collective-permute-start(f32[64,256]{1,0:T(8,128)S(1)} %slice_select_fusion.1), channel_id=1, source_target_pairs={{0,2},{1,3},{2,0},{3,1},{4,6},{5,7},{6,4},{7,5},{8,10},{9,11},{10,... | collective-permute-start | bytes 196616 | tf_op jit(solution)/shard_map/ppermute | solution.py:276
  49.6 1.7 %collective-permute-done.12.refs_3_ = bf16[256,256]{1,0:T(8,128)(2,1)S(1)} collective-permute-done((bf16[256,256]{1,0:T(8,128)(2,1)S(1)}, bf16[256,256]{1,0:T(8,128)(2,1)S(1)}, u32[]{:S(2)}, u32[]{:S(2)}) %collective-permute-start.12) | collective-permute-done | bytes 131104 | tf_op jit(solution)/shard_map/ppermute | solution.py:276
  51.3 3.8 %collective-permute-done.11.refs_2_ = bf16[256,256]{1,0:T(8,128)(2,1)S(1)} collective-permute-done((bf16[256,256]{1,0:T(8,128)(2,1)S(1)}, bf16[256,256]{1,0:T(8,128)(2,1)S(1)}, u32[]{:S(2)}, u32[]{:S(2)}) %collective-permute-start.11) | collective-permute-done | bytes 131104 | tf_op jit(solution)/shard_map/ppermute | solution.py:276
  55.0 2.2 %copy-done.2 = bf16[1024,2048]{1,0:T(8,128)(2,1)S(1)} copy-done((bf16[1024,2048]{1,0:T(8,128)(2,1)S(1)}, bf16[1024,2048]{1,0:T(8,128)(2,1)}, u32[]{:S(2)}) %copy-start.2) | copy-done | bytes 4194328
  57.2 0.4 backward_product.2
  57.7 2.2 %copy-done.3 = bf16[1024,2048]{1,0:T(8,128)(2,1)S(1)} copy-done((bf16[1024,2048]{1,0:T(8,128)(2,1)S(1)}, bf16[1024,2048]{1,0:T(8,128)(2,1)}, u32[]{:S(2)}) %copy-start.3) | copy-done | bytes 4194328
  59.8 1.3 %backward_product.3 = (bf16[256,256]{1,0:T(8,128)(2,1)S(1)}, bf16[256,256]{1,0:T(8,128)(2,1)S(1)}, bf16[256,256]{1,0:T(8,128)(2,1)S(1)}, bf16[256,256]{1,0:T(8,1...) custom-call(s32[1]{0:T(128)} %bitcast.row_ref, ...), custom_call_target="tpu_custom_call" | custom-call | flops 134217728 | bytes 917504 | tf_op jit(solution)/shard_map/backward_product/pallas_call | solution.py:235
  61.1 1.7 %collective-permute-start.17 = (bf16[256,256]{1,0:T(8,128)(2,1)S(1)}, bf16[256,256]{1,0:T(8,128)(2,1)S(1)}, u32[]{:S(2)}, u32[]{:S(2)}) collective-permute-start(bf16[256,256]{1,0:T(8,128)(2,1)S(1)} %get-tuple-element.39), channel_id=1, source_target_pairs={{0,4},{8,0},{16,8},{24,16},{28,24},{20,28},{12,20},{4,12},{1,5},{9... | collective-permute-start | bytes 393224 | tf_op jit(solution)/shard_map/ppermute | solution.py:272
  62.8 1.2 %collective-permute-start.22 = (f32[64,256]{1,0:T(8,128)S(1)}, f32[64,256]{1,0:T(8,128)S(1)}, u32[]{:S(2)}, u32[]{:S(2)}) collective-permute-start(f32[64,256]{1,0:T(8,128)S(1)} %select_add_fusion.1), channel_id=1, source_target_pairs={{0,4},{4,0},{8,12},{12,8},{16,20},{20,16},{24,28},{28,24},{1,5},{5... | collective-permute-start | bytes 196616 | tf_op jit(solution)/shard_map/ppermute | solution.py:276
  64.1 1.7 %collective-permute-start.13 = (bf16[256,256]{1,0:T(8,128)(2,1)S(1)}, bf16[256,256]{1,0:T(8,128)(2,1)S(1)}, u32[]{:S(2)}, u32[]{:S(2)}) collective-permute-start(bf16[256,256]{1,0:T(8,128)(2,1)S(1)} %backward_product.2), channel_id=1, source_target_pairs={{0,8},{8,16},{16,24},{24,28},{28,20},{20,12},{12,4},{4,0},{1,9},{9... | collective-permute-start | bytes 393224 | tf_op jit(solution)/shard_map/ppermute | solution.py:272
  65.8 1.6 %collective-permute-done.22 = f32[64,256]{1,0:T(8,128)S(1)} collective-permute-done((f32[64,256]{1,0:T(8,128)S(1)}, f32[64,256]{1,0:T(8,128)S(1)}, u32[]{:S(2)}, u32[]{:S(2)}) %collective-permute-start.22) | collective-permute-done | bytes 65568 | tf_op jit(solution)/shard_map/ppermute | solution.py:276
  67.4 0.7 collective-permute-start.23
  68.1 0.0 collective-permute-done.17
  68.1 2.1 %collective-permute-start.18 = (bf16[256,256]{1,0:T(8,128)(2,1)S(1)}, bf16[256,256]{1,0:T(8,128)(2,1)S(1)}, u32[]{:S(2)}, u32[]{:S(2)}) collective-permute-start(bf16[256,256]{1,0:T(8,128)(2,1)S(1)} %add_convert_fusion.1), channel_id=1, source_target_pairs={{0,4},{8,0},{16,8},{24,16},{28,24},{20,28},{12,20},{4,12},{1,5},{9... | collective-permute-start | bytes 393224 | tf_op jit(solution)/shard_map/ppermute | solution.py:272
  70.2 0.0 collective-permute-done.13
  70.3 0.6 collective-permute-start.14
  70.9 0.8 collective-permute-done.23
  71.7 3.0 %collective-permute-start.24 = (f32[64,256]{1,0:T(8,128)S(1)}, f32[64,256]{1,0:T(8,128)S(1)}, u32[]{:S(2)}, u32[]{:S(2)}) collective-permute-start(f32[64,256]{1,0:T(8,128)S(1)} %add.38), channel_id=1, source_target_pairs={{0,16},{4,20},{8,24},{12,28},{16,0},{20,4},{24,8},{28,12},{1,17},{... | collective-permute-start | bytes 196616 | tf_op jit(solution)/shard_map/ppermute | solution.py:276
  74.7 0.8 collective-permute-start.19
  75.5 2.1 %collective-permute-done.24 = f32[64,256]{1,0:T(8,128)S(1)} collective-permute-done((f32[64,256]{1,0:T(8,128)S(1)}, f32[64,256]{1,0:T(8,128)S(1)}, u32[]{:S(2)}, u32[]{:S(2)}) %collective-permute-start.24) | collective-permute-done | bytes 65568 | tf_op jit(solution)/shard_map/ppermute | solution.py:276
  77.6 2.2 %collective-permute-start.25 = (f32[64,256]{1,0:T(8,128)S(1)}, f32[64,256]{1,0:T(8,128)S(1)}, u32[]{:S(2)}, u32[]{:S(2)}) collective-permute-start(f32[64,256]{1,0:T(8,128)S(1)} %add.39), channel_id=1, source_target_pairs={{0,2},{1,3},{2,0},{3,1},{4,6},{5,7},{6,4},{7,5},{8,10},{9,11},{10,... | collective-permute-start | bytes 196616 | tf_op jit(solution)/shard_map/ppermute | solution.py:276
  79.8 0.0 collective-permute-done.14
  79.8 1.5 %collective-permute-start.15 = (bf16[256,256]{1,0:T(8,128)(2,1)S(1)}, bf16[256,256]{1,0:T(8,128)(2,1)S(1)}, u32[]{:S(2)}, u32[]{:S(2)}) collective-permute-start(bf16[256,256]{1,0:T(8,128)(2,1)S(1)} %add_convert_fusion.3), channel_id=1, source_target_pairs={{0,8},{8,16},{16,24},{24,28},{28,20},{20,12},{12,4},{4,0},{1,9},{9... | collective-permute-start | bytes 393224 | tf_op jit(solution)/shard_map/ppermute | solution.py:272
  81.3 0.7 collective-permute-done.25
  82.0 0.1 collective-permute-start.26
  82.1 3.0 %collective-permute-done.15 = bf16[256,256]{1,0:T(8,128)(2,1)S(1)} collective-permute-done((bf16[256,256]{1,0:T(8,128)(2,1)S(1)}, bf16[256,256]{1,0:T(8,128)(2,1)S(1)}, u32[]{:S(2)}, u32[]{:S(2)}) %collective-permute-start.15) | collective-permute-done | bytes 131104 | tf_op jit(solution)/shard_map/ppermute | solution.py:272
  85.1 1.2 %collective-permute-start.16 = (bf16[256,256]{1,0:T(8,128)(2,1)S(1)}, bf16[256,256]{1,0:T(8,128)(2,1)S(1)}, u32[]{:S(2)}, u32[]{:S(2)}) collective-permute-start(bf16[256,256]{1,0:T(8,128)(2,1)S(1)} %add_convert_fusion.2), channel_id=1, source_target_pairs={{0,8},{8,16},{16,24},{24,28},{28,20},{20,12},{12,4},{4,0},{1,9},{9... | collective-permute-start | bytes 393224 | tf_op jit(solution)/shard_map/ppermute | solution.py:272
  86.3 0.0 collective-permute-done.26
  86.4 0.7 pad_maximum_fusion
  87.1 3.1 %collective-permute-done.16.second_ref = bf16[256,256]{1,0:T(8,128)(2,1)S(1)} collective-permute-done((bf16[256,256]{1,0:T(8,128)(2,1)S(1)}, bf16[256,256]{1,0:T(8,128)(2,1)S(1)}, u32[]{:S(2)}, u32[]{:S(2)}) %collective-permute-start.16) | collective-permute-done | bytes 131104 | tf_op jit(solution)/shard_map/ppermute | solution.py:272
  90.1 0.8 finish.1
  (31 shorter events, 0.3 us)
Async XLA Ops:
  0.6 27.6 %copy-start.4 = (bf16[256,256]{1,0:T(8,128)(2,1)S(1)}, bf16[256,256]{1,0:T(8,128)(2,1)}, u32[]{:S(2)}) copy-start(bf16[256,256]{1,0:T(8,128)(2,1)} %refs_0_.3) | copy-start | bytes 393220
  0.6 11.2 %collective-permute-start.1 = (bf16[256,256]{1,0:T(8,128)(2,1)}, bf16[256,256]{1,0:T(8,128)(2,1)S(1)}, u32[]{:S(2)}, u32[]{:S(2)}) collective-permute-start(bf16[256,256]{1,0:T(8,128)(2,1)} %refs_0_.3), channel_id=1, source_target_pairs={{0,4},{8,0},{16,8},{24,16},{28,24},{20,28},{12,20},{4,12},{1,5},{9... | collective-permute-start | bytes 393224 | tf_op jit(solution)/shard_map/ppermute | solution.py:272
  3.7 8.2 %collective-permute-start = (bf16[256,256]{1,0:T(8,128)(2,1)}, bf16[256,256]{1,0:T(8,128)(2,1)S(1)}, u32[]{:S(2)}, u32[]{:S(2)}) collective-permute-start(bf16[256,256]{1,0:T(8,128)(2,1)} %refs_0_.3), channel_id=1, source_target_pairs={{0,8},{8,16},{16,24},{24,28},{28,20},{20,12},{12,4},{4,0},{1,9},{9... | collective-permute-start | bytes 393224 | tf_op jit(solution)/shard_map/ppermute | solution.py:272
  4.4 0.7 copy-start.7
  5.1 0.7 copy-start.8
  5.8 38.9 %copy-start.5 = (bf16[256,256]{1,0:T(8,128)(2,1)S(1)}, bf16[256,256]{1,0:T(8,128)(2,1)}, u32[]{:S(2)}) copy-start(bf16[256,256]{1,0:T(8,128)(2,1)} %refs_4_.1) | copy-start | bytes 393220
  5.8 38.9 %copy-start.6 = (bf16[256,256]{1,0:T(8,128)(2,1)S(1)}, bf16[256,256]{1,0:T(8,128)(2,1)}, u32[]{:S(2)}) copy-start(bf16[256,256]{1,0:T(8,128)(2,1)} %refs_5_.1) | copy-start | bytes 393220
  9.8 2.0 %copy-start = (bf16[1024,2048]{1,0:T(8,128)(2,1)}, bf16[1024,2048]{1,0:T(8,128)(2,1)S(1)}, u32[]{:S(2)}) copy-start(bf16[1024,2048]{1,0:T(8,128)(2,1)S(1)} %build_dense.1.dense_ref) | copy-start | bytes 12582916
  11.8 5.9 %collective-permute-start.2 = (bf16[256,256]{1,0:T(8,128)(2,1)S(1)}, bf16[256,256]{1,0:T(8,128)(2,1)S(1)}, u32[]{:S(2)}, u32[]{:S(2)}) collective-permute-start(bf16[256,256]{1,0:T(8,128)(2,1)S(1)} %collective-permute-done.refs_1_), channel_id=1, source_target_pairs={{0,8},{8,16},{16,24},{24,28},{28,20},{20,12},{12,4},{4,0},{1,9},{9... | collective-permute-start | bytes 393224 | tf_op jit(solution)/shard_map/ppermute | solution.py:272
  13.6 6.4 %collective-permute-start.3 = (bf16[256,256]{1,0:T(8,128)(2,1)S(1)}, bf16[256,256]{1,0:T(8,128)(2,1)S(1)}, u32[]{:S(2)}, u32[]{:S(2)}) collective-permute-start(bf16[256,256]{1,0:T(8,128)(2,1)S(1)} %collective-permute-done.1.refs_2_), channel_id=1, source_target_pairs={{0,4},{8,0},{16,8},{24,16},{28,24},{20,28},{12,20},{4,12},{1,5},{9... | collective-permute-start | bytes 393224 | tf_op jit(solution)/shard_map/ppermute | solution.py:272
  17.7 5.3 %collective-permute-start.4 = (bf16[256,256]{1,0:T(8,128)(2,1)S(1)}, bf16[256,256]{1,0:T(8,128)(2,1)S(1)}, u32[]{:S(2)}, u32[]{:S(2)}) collective-permute-start(bf16[256,256]{1,0:T(8,128)(2,1)S(1)} %collective-permute-done.2.refs_3_), channel_id=1, source_target_pairs={{0,8},{8,16},{16,24},{24,28},{28,20},{20,12},{12,4},{4,0},{1,9},{9... | collective-permute-start | bytes 393224 | tf_op jit(solution)/shard_map/ppermute | solution.py:272
  19.9 5.7 %collective-permute-start.5 = (bf16[256,256]{1,0:T(8,128)(2,1)S(1)}, bf16[256,256]{1,0:T(8,128)(2,1)S(1)}, u32[]{:S(2)}, u32[]{:S(2)}) collective-permute-start(bf16[256,256]{1,0:T(8,128)(2,1)S(1)} %collective-permute-done.3.refs_4_), channel_id=1, source_target_pairs={{0,4},{8,0},{16,8},{24,16},{28,24},{20,28},{12,20},{4,12},{1,5},{9... | collective-permute-start | bytes 393224 | tf_op jit(solution)/shard_map/ppermute | solution.py:272
  23.0 5.2 %collective-permute-start.6 = (bf16[256,256]{1,0:T(8,128)(2,1)S(1)}, bf16[256,256]{1,0:T(8,128)(2,1)S(1)}, u32[]{:S(2)}, u32[]{:S(2)}) collective-permute-start(bf16[256,256]{1,0:T(8,128)(2,1)S(1)} %collective-permute-done.4.refs_5_), channel_id=1, source_target_pairs={{0,8},{8,16},{16,24},{24,28},{28,20},{20,12},{12,4},{4,0},{1,9},{9... | collective-permute-start | bytes 393224 | tf_op jit(solution)/shard_map/ppermute | solution.py:272
  28.2 2.2 %copy-start.1 = (bf16[1024,2048]{1,0:T(8,128)(2,1)S(1)}, bf16[1024,2048]{1,0:T(8,128)(2,1)}, u32[]{:S(2)}) copy-start(bf16[1024,2048]{1,0:T(8,128)(2,1)} %copy-done) | copy-start | bytes 12582916
  32.5 5.7 %collective-permute-start.9 = (bf16[256,256]{1,0:T(8,128)(2,1)S(1)}, bf16[256,256]{1,0:T(8,128)(2,1)S(1)}, u32[]{:S(2)}, u32[]{:S(2)}) collective-permute-start(bf16[256,256]{1,0:T(8,128)(2,1)S(1)} %get-tuple-element.28), channel_id=1, source_target_pairs={{0,1},{1,0},{2,3},{3,2},{4,5},{5,4},{6,7},{7,6},{8,9},{9,8},{10,11... | collective-permute-start | bytes 393224 | tf_op jit(solution)/shard_map/ppermute | solution.py:276
  34.8 7.6 %collective-permute-start.7 = (bf16[256,256]{1,0:T(8,128)(2,1)S(1)}, bf16[256,256]{1,0:T(8,128)(2,1)S(1)}, u32[]{:S(2)}, u32[]{:S(2)}) collective-permute-start(bf16[256,256]{1,0:T(8,128)(2,1)S(1)} %get-tuple-element.25), channel_id=1, source_target_pairs={{0,2},{1,3},{2,0},{3,1},{4,6},{5,7},{6,4},{7,5},{8,10},{9,11},{10,... | collective-permute-start | bytes 393224 | tf_op jit(solution)/shard_map/ppermute | solution.py:276
  38.1 6.7 %collective-permute-start.8 = (bf16[256,256]{1,0:T(8,128)(2,1)S(1)}, bf16[256,256]{1,0:T(8,128)(2,1)S(1)}, u32[]{:S(2)}, u32[]{:S(2)}) collective-permute-start(bf16[256,256]{1,0:T(8,128)(2,1)S(1)} %get-tuple-element.26), channel_id=1, source_target_pairs={{0,3},{1,2},{2,1},{3,0},{4,7},{5,6},{6,5},{7,4},{8,11},{9,10},{10,... | collective-permute-start | bytes 393224 | tf_op jit(solution)/shard_map/ppermute | solution.py:276
  45.7 2.2 %collective-permute-start.20 = (f32[128,256]{1,0:T(8,128)S(1)}, f32[128,256]{1,0:T(8,128)S(1)}, u32[]{:S(2)}, u32[]{:S(2)}) collective-permute-start(f32[128,256]{1,0:T(8,128)S(1)} %slice_select_fusion), channel_id=1, source_target_pairs={{0,1},{1,0},{2,3},{3,2},{4,5},{5,4},{6,7},{7,6},{8,9},{9,8},{10,11... | collective-permute-start | bytes 393224 | tf_op jit(solution)/shard_map/ppermute | solution.py:276
  45.9 5.4 %collective-permute-start.12 = (bf16[256,256]{1,0:T(8,128)(2,1)S(1)}, bf16[256,256]{1,0:T(8,128)(2,1)S(1)}, u32[]{:S(2)}, u32[]{:S(2)}) collective-permute-start(bf16[256,256]{1,0:T(8,128)(2,1)S(1)} %get-tuple-element.30.refs_0_), channel_id=1, source_target_pairs={{0,3},{1,2},{2,1},{3,0},{4,7},{5,6},{6,5},{7,4},{8,11},{9,10},{10,... | collective-permute-start | bytes 393224 | tf_op jit(solution)/shard_map/ppermute | solution.py:276
  47.4 7.6 %collective-permute-start.11 = (bf16[256,256]{1,0:T(8,128)(2,1)S(1)}, bf16[256,256]{1,0:T(8,128)(2,1)S(1)}, u32[]{:S(2)}, u32[]{:S(2)}) collective-permute-start(bf16[256,256]{1,0:T(8,128)(2,1)S(1)} %get-tuple-element.30.refs_0_), channel_id=1, source_target_pairs={{0,2},{1,3},{2,0},{3,1},{4,6},{5,7},{6,4},{7,5},{8,10},{9,11},{10,... | collective-permute-start | bytes 393224 | tf_op jit(solution)/shard_map/ppermute | solution.py:276
  47.9 7.1 %collective-permute-start.10 = (bf16[256,256]{1,0:T(8,128)(2,1)S(1)}, bf16[256,256]{1,0:T(8,128)(2,1)S(1)}, u32[]{:S(2)}, u32[]{:S(2)}) collective-permute-start(bf16[256,256]{1,0:T(8,128)(2,1)S(1)} %get-tuple-element.30.refs_0_), channel_id=1, source_target_pairs={{0,1},{1,0},{2,3},{3,2},{4,5},{5,4},{6,7},{7,6},{8,9},{9,8},{10,11... | collective-permute-start | bytes 393224 | tf_op jit(solution)/shard_map/ppermute | solution.py:276
  48.0 14.8 %collective-permute-start.21 = (f32[64,256]{1,0:T(8,128)S(1)}, f32[64,256]{1,0:T(8,128)S(1)}, u32[]{:S(2)}, u32[]{:S(2)}) collective-permute-start(f32[64,256]{1,0:T(8,128)S(1)} %slice_select_fusion.1), channel_id=1, source_target_pairs={{0,2},{1,3},{2,0},{3,1},{4,6},{5,7},{6,4},{7,5},{8,10},{9,11},{10,... | collective-permute-start | bytes 196616 | tf_op jit(solution)/shard_map/ppermute | solution.py:276
  55.0 2.2 %copy-start.2 = (bf16[1024,2048]{1,0:T(8,128)(2,1)S(1)}, bf16[1024,2048]{1,0:T(8,128)(2,1)}, u32[]{:S(2)}) copy-start(bf16[1024,2048]{1,0:T(8,128)(2,1)} %copy-done) | copy-start | bytes 12582916
  57.7 2.2 %copy-start.3 = (bf16[1024,2048]{1,0:T(8,128)(2,1)S(1)}, bf16[1024,2048]{1,0:T(8,128)(2,1)}, u32[]{:S(2)}) copy-start(bf16[1024,2048]{1,0:T(8,128)(2,1)} %copy-done) | copy-start | bytes 12582916
  61.1 7.0 %collective-permute-start.17 = (bf16[256,256]{1,0:T(8,128)(2,1)S(1)}, bf16[256,256]{1,0:T(8,128)(2,1)S(1)}, u32[]{:S(2)}, u32[]{:S(2)}) collective-permute-start(bf16[256,256]{1,0:T(8,128)(2,1)S(1)} %get-tuple-element.39), channel_id=1, source_target_pairs={{0,4},{8,0},{16,8},{24,16},{28,24},{20,28},{12,20},{4,12},{1,5},{9... | collective-permute-start | bytes 393224 | tf_op jit(solution)/shard_map/ppermute | solution.py:272
  62.8 4.5 %collective-permute-start.22 = (f32[64,256]{1,0:T(8,128)S(1)}, f32[64,256]{1,0:T(8,128)S(1)}, u32[]{:S(2)}, u32[]{:S(2)}) collective-permute-start(f32[64,256]{1,0:T(8,128)S(1)} %select_add_fusion.1), channel_id=1, source_target_pairs={{0,4},{4,0},{8,12},{12,8},{16,20},{20,16},{24,28},{28,24},{1,5},{5... | collective-permute-start | bytes 196616 | tf_op jit(solution)/shard_map/ppermute | solution.py:276
  64.1 6.2 %collective-permute-start.13 = (bf16[256,256]{1,0:T(8,128)(2,1)S(1)}, bf16[256,256]{1,0:T(8,128)(2,1)S(1)}, u32[]{:S(2)}, u32[]{:S(2)}) collective-permute-start(bf16[256,256]{1,0:T(8,128)(2,1)S(1)} %backward_product.2), channel_id=1, source_target_pairs={{0,8},{8,16},{16,24},{24,28},{28,20},{20,12},{12,4},{4,0},{1,9},{9... | collective-permute-start | bytes 393224 | tf_op jit(solution)/shard_map/ppermute | solution.py:272
  67.4 4.3 %collective-permute-start.23 = (f32[64,256]{1,0:T(8,128)S(1)}, f32[64,256]{1,0:T(8,128)S(1)}, u32[]{:S(2)}, u32[]{:S(2)}) collective-permute-start(f32[64,256]{1,0:T(8,128)S(1)} %add.37), channel_id=1, source_target_pairs={{0,8},{4,12},{8,0},{12,4},{16,24},{20,28},{24,16},{28,20},{1,9},{5... | collective-permute-start | bytes 196616 | tf_op jit(solution)/shard_map/ppermute | solution.py:276
  68.1 6.5 %collective-permute-start.18 = (bf16[256,256]{1,0:T(8,128)(2,1)S(1)}, bf16[256,256]{1,0:T(8,128)(2,1)S(1)}, u32[]{:S(2)}, u32[]{:S(2)}) collective-permute-start(bf16[256,256]{1,0:T(8,128)(2,1)S(1)} %add_convert_fusion.1), channel_id=1, source_target_pairs={{0,4},{8,0},{16,8},{24,16},{28,24},{20,28},{12,20},{4,12},{1,5},{9... | collective-permute-start | bytes 393224 | tf_op jit(solution)/shard_map/ppermute | solution.py:272
  70.3 9.5 %collective-permute-start.14 = (bf16[256,256]{1,0:T(8,128)(2,1)S(1)}, bf16[256,256]{1,0:T(8,128)(2,1)S(1)}, u32[]{:S(2)}, u32[]{:S(2)}) collective-permute-start(bf16[256,256]{1,0:T(8,128)(2,1)S(1)} %add_convert_fusion.4), channel_id=1, source_target_pairs={{0,8},{8,16},{16,24},{24,28},{28,20},{20,12},{12,4},{4,0},{1,9},{9... | collective-permute-start | bytes 393224 | tf_op jit(solution)/shard_map/ppermute | solution.py:272
  71.7 5.9 %collective-permute-start.24 = (f32[64,256]{1,0:T(8,128)S(1)}, f32[64,256]{1,0:T(8,128)S(1)}, u32[]{:S(2)}, u32[]{:S(2)}) collective-permute-start(f32[64,256]{1,0:T(8,128)S(1)} %add.38), channel_id=1, source_target_pairs={{0,16},{4,20},{8,24},{12,28},{16,0},{20,4},{24,8},{28,12},{1,17},{... | collective-permute-start | bytes 196616 | tf_op jit(solution)/shard_map/ppermute | solution.py:276
  74.7 12.4 %collective-permute-start.19 = (bf16[256,256]{1,0:T(8,128)(2,1)S(1)}, bf16[256,256]{1,0:T(8,128)(2,1)S(1)}, u32[]{:S(2)}, u32[]{:S(2)}) collective-permute-start(bf16[256,256]{1,0:T(8,128)(2,1)S(1)} %add_convert_fusion), channel_id=1, source_target_pairs={{0,4},{8,0},{16,8},{24,16},{28,24},{20,28},{12,20},{4,12},{1,5},{9... | collective-permute-start | bytes 393224 | tf_op jit(solution)/shard_map/ppermute | solution.py:272
  77.6 4.4 %collective-permute-start.25 = (f32[64,256]{1,0:T(8,128)S(1)}, f32[64,256]{1,0:T(8,128)S(1)}, u32[]{:S(2)}, u32[]{:S(2)}) collective-permute-start(f32[64,256]{1,0:T(8,128)S(1)} %add.39), channel_id=1, source_target_pairs={{0,2},{1,3},{2,0},{3,1},{4,6},{5,7},{6,4},{7,5},{8,10},{9,11},{10,... | collective-permute-start | bytes 196616 | tf_op jit(solution)/shard_map/ppermute | solution.py:276
  79.8 5.3 %collective-permute-start.15 = (bf16[256,256]{1,0:T(8,128)(2,1)S(1)}, bf16[256,256]{1,0:T(8,128)(2,1)S(1)}, u32[]{:S(2)}, u32[]{:S(2)}) collective-permute-start(bf16[256,256]{1,0:T(8,128)(2,1)S(1)} %add_convert_fusion.3), channel_id=1, source_target_pairs={{0,8},{8,16},{16,24},{24,28},{28,20},{20,12},{12,4},{4,0},{1,9},{9... | collective-permute-start | bytes 393224 | tf_op jit(solution)/shard_map/ppermute | solution.py:272
  82.0 4.3 %collective-permute-start.26 = (f32[128,256]{1,0:T(8,128)S(1)}, f32[128,256]{1,0:T(8,128)S(1)}, u32[]{:S(2)}, u32[]{:S(2)}) collective-permute-start(f32[128,256]{1,0:T(8,128)S(1)} %pad_maximum_fusion.1), channel_id=1, source_target_pairs={{0,1},{1,0},{2,3},{3,2},{4,5},{5,4},{6,7},{7,6},{8,9},{9,8},{10,11... | collective-permute-start | bytes 393224 | tf_op jit(solution)/shard_map/ppermute | solution.py:276
  85.1 5.0 %collective-permute-start.16 = (bf16[256,256]{1,0:T(8,128)(2,1)S(1)}, bf16[256,256]{1,0:T(8,128)(2,1)S(1)}, u32[]{:S(2)}, u32[]{:S(2)}) collective-permute-start(bf16[256,256]{1,0:T(8,128)(2,1)S(1)} %add_convert_fusion.2), channel_id=1, source_target_pairs={{0,8},{8,16},{16,24},{24,28},{28,20},{20,12},{12,4},{4,0},{1,9},{9... | collective-permute-start | bytes 393224 | tf_op jit(solution)/shard_map/ppermute | solution.py:272

commit v4 on v3

--- a/solution.py
+++ b/solution.py
@@ -115,27 +115,27 @@
     return jnp.where(place < count // 2, 2 * place, 2 * (count - 1 - place) + 1)
 
 
-def forward_kernel(row_ref, col_ref, dense_ref, *refs, offsets, partners, row_count):
-    piece_refs, refs = refs[: len(offsets)], refs[len(offsets) :]
-    out_refs, (depth, sems) = refs[:-2], refs[-2:]
+def forward_kernel(dense_ref, *refs, offsets, partners, row_count):
+    piece_refs, out_refs = refs[: len(offsets)], refs[len(offsets) :]
     rows = out_refs[0].shape[0]
-    place = ring_place(row_ref[0], row_count)
-    copies = []
-    for index, (offset, piece) in enumerate(zip(offsets, piece_refs)):
+    place = ring_place(lax.axis_index("row"), row_count)
+    col = lax.axis_index("col")
+    starts = []
+    for offset, piece in zip(offsets, piece_refs):
         high = piece.shape[0]
-        down = pl.ds(pl.multiple_of(ring_row(place + offset, row_count) * high, high), high)
-        copy = pltpu.make_async_copy(piece, depth.at[down], sems.at[index])
-        copy.start()
-        copies.append(copy)
-    for copy in copies:
-        copy.wait()
+        starts.append(pl.multiple_of(ring_row(place + offset, row_count) * high, high))
     for partner, out_ref in zip(partners, out_refs):
-        down = pl.ds(pl.multiple_of((col_ref[0] ^ partner) * rows, rows), rows)
-        part = jnp.dot(dense_ref[down, :], depth[...], preferred_element_type=jnp.float32)
-        out_ref[...] = part.astype(jnp.bfloat16)
-
-
-def forward_product(row_place, col_place, dense, shards, partners, row_count, col_count):
+        down = pl.ds(pl.multiple_of((col ^ partner) * rows, rows), rows)
+        total = None
+        for start, piece in zip(starts, piece_refs):
+            part = jnp.dot(
+                dense_ref[down, pl.ds(start, piece.shape[0])], piece[...], preferred_element_type=jnp.float32
+            )
+            total = part if total is None else total + part
+        out_ref[...] = total.astype(jnp.bfloat16)
+
+
+def forward_product(dense, shards, partners, row_count, col_count):
     offsets = tuple(offset for offset, _ in shards)
     arrays = [array for _, array in shards]
     high, deep = dense.shape
@@ -147,11 +147,8 @@
     return pl.pallas_call(
         functools.partial(forward_kernel, offsets=offsets, partners=partners, row_count=row_count),
         out_shape=[jax.ShapeDtypeStruct((rows, width), jnp.bfloat16)] * len(partners),
-        in_specs=[pl.BlockSpec(memory_space=pltpu.SMEM)] * 2
-        + [pl.BlockSpec(memory_space=pltpu.VMEM)]
-        + [pl.BlockSpec(memory_space=pl.ANY)] * len(arrays),
+        in_specs=[pl.BlockSpec(memory_space=pltpu.VMEM)] * (1 + len(arrays)),
         out_specs=[pl.BlockSpec(memory_space=pltpu.VMEM)] * len(partners),
-        scratch_shapes=[pltpu.VMEM(*depth), pltpu.SemaphoreType.DMA((len(arrays),))],
         compiler_params=pltpu.CompilerParams(vmem_limit_bytes=scratch_bytes(cell, depth, out) + 6 * mib),
         cost_estimate=pl.CostEstimate(
             flops=2 * rows * len(partners) * deep * width,
@@ -159,12 +156,12 @@
             transcendentals=0,
         ),
         name="forward_product",
-    )(row_place, col_place, dense, *arrays)
+    )(dense, *arrays)
 
 
 def middle_kernel(*refs, count, scale):
     parts = refs[:count]
-    weight_ref, cotangent_ref, act_ref, back_ref, terms_ref = refs[count:]
+    weight_ref, cotangent_ref, act_ref, back_ref, *chunk_refs, product = refs[count:]
     aggregate = parts[0][...].astype(jnp.float32)
     for part in parts[1:]:
         aggregate += part[...].astype(jnp.float32)
@@ -182,7 +179,11 @@
     over_nodes = (((0,), (0,)), ((), ()))
     terms = lax.dot_general(high, grad, over_nodes, preferred_element_type=jnp.float32)
     terms += lax.dot_general(low, grad, over_nodes, preferred_element_type=jnp.float32)
-    terms_ref[...] = terms * scale
+    product[...] = terms * scale
+    rows = product.shape[0] // count
+    col = lax.axis_index("col")
+    for partner, chunk_ref in enumerate(chunk_refs):
+        chunk_ref[...] = product[pl.ds(pl.multiple_of((col ^ partner) * rows, rows), rows), :]
 
 
 def middle(parts, weight, cotangent, total_nodes):
@@ -193,10 +194,11 @@
         out_shape=[
             jax.ShapeDtypeStruct((rows, width), jnp.bfloat16),
             jax.ShapeDtypeStruct((width, rows), jnp.bfloat16),
-            jax.ShapeDtypeStruct((width, width), jnp.float32),
-        ],
+        ]
+        + [jax.ShapeDtypeStruct((width // count, width), jnp.float32)] * count,
         in_specs=[pl.BlockSpec(memory_space=pltpu.VMEM)] * (count + 2),
-        out_specs=[pl.BlockSpec(memory_space=pltpu.VMEM)] * 3,
+        out_specs=[pl.BlockSpec(memory_space=pltpu.VMEM)] * (2 + count),
+        scratch_shapes=[pltpu.VMEM((width, width), jnp.float32)],
         compiler_params=pltpu.CompilerParams(vmem_limit_bytes=12 * mib),
         cost_estimate=pl.CostEstimate(
             flops=10 * rows * width * width, bytes_accessed=2 * (count + 6) * rows * width, transcendentals=rows * width
@@ -205,27 +207,28 @@
     )(*parts, weight, cotangent)
 
 
-def backward_kernel(row_ref, col_ref, dense_ref, *refs, count, offsets, row_count):
+def backward_kernel(dense_ref, *refs, count, offsets, row_count):
     grad_refs, refs = refs[:count], refs[count:]
     out_refs, (depth, sems) = refs[:-2], refs[-2:]
     width, rows = grad_refs[0].shape
     wide = dense_ref.shape[1] // row_count
+    col = lax.axis_index("col")
     copies = []
     for partner, grad in enumerate(grad_refs):
-        along = pl.ds(pl.multiple_of((col_ref[0] ^ partner) * rows, rows), rows)
+        along = pl.ds(pl.multiple_of((col ^ partner) * rows, rows), rows)
         copy = pltpu.make_async_copy(grad, depth.at[:, along], sems.at[partner])
         copy.start()
         copies.append(copy)
     for copy in copies:
         copy.wait()
-    place = ring_place(row_ref[0], row_count)
+    place = ring_place(lax.axis_index("row"), row_count)
     for index, offset in enumerate(offsets):
         along = pl.ds(pl.multiple_of(ring_row(place + offset, row_count) * wide, wide), wide)
         part = jnp.dot(depth[...], dense_ref[:, along], preferred_element_type=jnp.float32)
         out_refs[index][...] = part.astype(jnp.bfloat16)
 
 
-def backward_product(row_place, col_place, dense, grads, offsets, row_count):
+def backward_product(dense, grads, offsets, row_count):
     high, deep = dense.shape
     width = grads[0].shape[0]
     wide = deep // row_count
@@ -235,9 +238,7 @@
     return pl.pallas_call(
         functools.partial(backward_kernel, count=len(grads), offsets=offsets, row_count=row_count),
         out_shape=[jax.ShapeDtypeStruct((width, wide), jnp.bfloat16)] * len(offsets),
-        in_specs=[pl.BlockSpec(memory_space=pltpu.SMEM)] * 2
-        + [pl.BlockSpec(memory_space=pltpu.VMEM)]
-        + [pl.BlockSpec(memory_space=pl.ANY)] * len(grads),
+        in_specs=[pl.BlockSpec(memory_space=pltpu.VMEM)] + [pl.BlockSpec(memory_space=pl.ANY)] * len(grads),
         out_specs=[pl.BlockSpec(memory_space=pltpu.VMEM)] * len(offsets),
         scratch_shapes=[pltpu.VMEM(*depth), pltpu.SemaphoreType.DMA((len(grads),))],
         compiler_params=pltpu.CompilerParams(vmem_limit_bytes=scratch_bytes(cell, depth, out) + 6 * mib),
@@ -245,25 +246,33 @@
             flops=2 * high * wide * width, bytes_accessed=2 * wide * len(offsets) * width, transcendentals=0
         ),
         name="backward_product",
-    )(row_place, col_place, dense, *grads)
-
-
-def finish_kernel(first_ref, second_ref, third_ref, out_ref):
+    )(dense, *grads)
+
+
+def finish_kernel(first_ref, second_ref, third_ref, *refs):
+    chunk_refs, (features_ref, weight_ref) = refs[:-2], refs[-2:]
     total = first_ref[...].astype(jnp.float32) + second_ref[...].astype(jnp.float32) + third_ref[...].astype(jnp.float32)
-    out_ref[...] = total.astype(jnp.bfloat16).T
-
-
-def finish(first, second, third):
+    features_ref[...] = total.astype(jnp.bfloat16).T
+    rows = chunk_refs[0].shape[0]
+    col = lax.axis_index("col")
+    for partner, chunk_ref in enumerate(chunk_refs):
+        weight_ref[pl.ds(pl.multiple_of((col ^ partner) * rows, rows), rows), :] = chunk_ref[...]
+
+
+def finish(first, second, third, chunks):
     width, rows = first.shape
     return pl.pallas_call(
         finish_kernel,
-        out_shape=jax.ShapeDtypeStruct((rows, width), jnp.bfloat16),
-        in_specs=[pl.BlockSpec(memory_space=pltpu.VMEM)] * 3,
-        out_specs=pl.BlockSpec(memory_space=pltpu.VMEM),
+        out_shape=[
+            jax.ShapeDtypeStruct((rows, width), jnp.bfloat16),
+            jax.ShapeDtypeStruct((width, width), jnp.float32),
+        ],
+        in_specs=[pl.BlockSpec(memory_space=pltpu.VMEM)] * (3 + len(chunks)),
+        out_specs=[pl.BlockSpec(memory_space=pltpu.VMEM)] * 2,
         compiler_params=pltpu.CompilerParams(vmem_limit_bytes=8 * mib),
-        cost_estimate=pl.CostEstimate(flops=3 * rows * width, bytes_accessed=8 * rows * width, transcendentals=0),
+        cost_estimate=pl.CostEstimate(flops=3 * rows * width, bytes_accessed=16 * rows * width, transcendentals=0),
         name="finish",
-    )(first, second, third)
+    )(first, second, third, *chunks)
 
 
 def around(value, step):
@@ -295,22 +304,10 @@
     return (first.astype(jnp.float32) + second.astype(jnp.float32)).astype(jnp.bfloat16)
 
 
-def summed_everywhere(terms):
-    place = lax.axis_index("col")
-    bits = [1 << bit for bit in range((lax.axis_size("col") - 1).bit_length())]
-    for bit in bits:
-        half = terms.shape[0] // 2
-        upper = (place & bit) != 0
-        kept = jnp.where(upper, terms[half:], terms[:half])
-        sent = jnp.where(upper, terms[:half], terms[half:])
-        terms = kept + swapped(sent, "col", bit)
-    for bit in [1 << bit for bit in range((lax.axis_size("row") - 1).bit_length())]:
-        terms = terms + swapped(terms, "row", bit)
-    for bit in reversed(bits):
-        other = swapped(terms, "col", bit)
-        upper = (place & bit) != 0
-        terms = jnp.concatenate([jnp.where(upper, other, terms), jnp.where(upper, terms, other)])
-    return terms
+def partners_sum(values):
+    while len(values) > 1:
+        values = [values[i] + values[i + 1] for i in range(0, len(values), 2)]
+    return values[0]
 
 
 def per_device(features, weight, adj_tiles, tile_rows, tile_cols, tile_counts, out_grad):
@@ -323,34 +320,50 @@
     row_count = lax.axis_size("row")
     col_count = lax.axis_size("col")
     per_strip = node_rows // side
-    row_place = lax.axis_index("row").astype(jnp.int32).reshape(1)
-    col_place = lax.axis_index("col").astype(jnp.int32).reshape(1)
-
     dense = build_dense(rows, cols, count, tiles, col_count * per_strip, row_count * per_strip, per_strip)
     shards, dense = gathered_shards(features, dense)
 
     far = tuple(range(col_count // 2, col_count))
     near = tuple(range(col_count // 2))
-    sent = forward_product(row_place, col_place, dense, shards, far, row_count, col_count)
+    sent = forward_product(dense, shards, far, row_count, col_count)
     parts = [swapped(part, "col", partner) for partner, part in zip(far, sent)]
-    own, *sent = forward_product(row_place, col_place, dense, shards, near, row_count, col_count)
+    own, *sent = forward_product(dense, shards, near, row_count, col_count)
     parts += [own] + [swapped(part, "col", partner) for partner, part in zip(near[1:], sent)]
 
-    activations, back, terms = middle(parts, weight, out_grad, node_rows * row_count * col_count)
+    activations, back, *terms = middle(parts, weight, out_grad, node_rows * row_count * col_count)
     grads = [back] + [swapped(back, "col", partner) for partner in range(1, col_count)]
-    grad_weight = summed_everywhere(terms)
+    terms = terms[:1] + [swapped(terms[partner], "col", partner) for partner in range(1, col_count)]
+    grads, terms = lax.optimization_barrier((grads, terms))
 
     reach = row_count // 2
-    (opposite,) = backward_product(row_place, col_place, dense, grads, (reach,), row_count)
+    chunk = partners_sum(terms)
+    doublings = [1 << bit for bit in range((row_count - 1).bit_length())]
+    chunks = None
+    (opposite,) = backward_product(dense, grads, (reach,), row_count)
     opposite, cell = lax.optimization_barrier((opposite, dense))
     up, down = around(opposite, 1), None
     offsets = tuple(sign * step for step in range(reach - 1, 0, -1) for sign in (1, -1)) + (0,)
-    *strips, own = backward_product(row_place, col_place, cell, grads, offsets, row_count)
-    for step in range(reach - 1):
-        above, below = strips[2 * step : 2 * step + 2]
-        up = around(added(above, up), 1)
-        down = around(below if down is None else added(below, down), -1)
-    grad_features = finish(own, up, down)
+    *strips, own = backward_product(cell, grads, offsets, row_count)
+    for step in range(reach):
+        if doublings:
+            other = swapped(chunk, "row", doublings.pop(0))
+        elif chunks is None:
+            chunks = [chunk] + [swapped(chunk, "col", partner) for partner in range(1, col_count)]
+        if step == 0:
+            up, other = lax.optimization_barrier((up, other))
+        elif chunks is None:
+            up, down, other = lax.optimization_barrier((up, down, other))
+        if chunks is None:
+            chunk = chunk + other
+        if step < reach - 1:
+            above, below = strips[2 * step : 2 * step + 2]
+            up = around(added(above, up), 1)
+            down = around(below if down is None else added(below, down), -1)
+    while doublings:
+        chunk = chunk + swapped(chunk, "row", doublings.pop(0))
+    if chunks is None:
+        chunks = [chunk] + [swapped(chunk, "col", partner) for partner in range(1, col_count)]
+    grad_features, grad_weight = finish(own, up, down, chunks)
     return (activations, grad_features, grad_weight)
 
 

time: 91.3 us -> 80.5 us (0.88)
  local copies, waits for them, and re-layouts: 9.89 us -> 1.37 us
  waiting for transfers between devices: 32.6 us -> 38.2 us
  starting transfers between devices: 34.1 us -> 29.3 us
  Pallas kernels: 11.8 us -> 10.1 us
    ppermute x13 -> x15, waiting for transfers between devices: 17.2 us -> 25.9 us  [swapped(): lax.ppermute(value, axis, [(i, i ^ partner) for i in range(lax.axis_size(...]
    unnamed x18 -> x10, local copies, waits for them, and re-layouts: 9.89 us -> 1.37 us
    ppermute x14, waiting for transfers between devices: 15.4 us -> 12.4 us  [around(): lax.ppermute(value, 'row', [(order[i], order[(i + step) % count]) for i i...]
    pallas_call x2, Pallas kernels: 4.34 us -> 1.42 us  [forward_product(): pl.pallas_call(functools.partial(forward_kernel, offsets=offsets, partner...]
    ppermute x13 -> x15, starting transfers between devices: 14.4 us -> 12 us  [swapped(): lax.ppermute(value, axis, [(i, i ^ partner) for i in range(lax.axis_size(...]
    ppermute x14, starting transfers between devices: 19.7 us -> 17.4 us  [around(): lax.ppermute(value, 'row', [(order[i], order[(i + step) % count]) for i i...]
  transfers between devices with their start and end apart: 27 -> 29, of which waited for: 13 -> 15; matrix products, arithmetic and copies ran while one was open for 1% -> 0% of each run, Pallas kernels for 9% -> 9%
where the time goes in v4:
time: 80.5 us; the launch traced here: 80.7 us
  waiting for transfers between devices  38.2 us (47%)
  starting transfers between devices  29.3 us (36%)
  Pallas kernels  10.1 us (13%)
  between operations  1.47 us (2%)
  local copies, waits for them, and re-layouts  1.37 us (2%)
    ppermute x15, waiting for transfers between devices, swapped(): lax.ppermute(value, axis, [(i, i ^ partner) for i in range(lax.axis_size(...  25.9 us
    ppermute x14, starting transfers between devices, around(): lax.ppermute(value, 'row', [(order[i], order[(i + step) % count]) for i i...  17.4 us
    ppermute x14, waiting for transfers between devices, around(): lax.ppermute(value, 'row', [(order[i], order[(i + step) % count]) for i i...  12.4 us
    ppermute x15, starting transfers between devices, swapped(): lax.ppermute(value, axis, [(i, i ^ partner) for i in range(lax.axis_size(...  12 us
    pallas_call x1, Pallas kernels, build_dense(): pl.pallas_call(functools.partial(build_kernel, blocks=blocks, steps=steps...  4.93 us
    pallas_call x2, Pallas kernels, backward_product(): pl.pallas_call(functools.partial(backward_kernel, count=len(grads), offse...  1.73 us
  transfers between devices with their start and end apart: 29, of which 15 were waited for; matrix products, arithmetic and copies ran while one was open for 0% of the time, Pallas kernels for 9%

profile of v4, /device:TPU:0, one launch (start us, length us, event | category | flops | bytes accessed | tf_op | source)
XLA Modules:
  0.0 80.7 jit_solution(11298000422165473484)
XLA Ops:
  0.6 3.0 %collective-permute-start.1 = (bf16[256,256]{1,0:T(8,128)(2,1)}, bf16[256,256]{1,0:T(8,128)(2,1)S(1)}, u32[]{:S(2)}, u32[]{:S(2)}) collective-permute-start(bf16[256,256]{1,0:T(8,128)(2,1)} %refs_0_.3), channel_id=1, source_target_pairs={{0,4},{8,0},{16,8},{24,16},{28,24},{20,28},{12,20},{4,12},{1,5},{9... | collective-permute-start | bytes 393224 | tf_op jit(solution)/shard_map/ppermute | solution.py:281
  3.7 0.1 collective-permute-start
  4.4 0.7 copy-done.3
  5.1 0.7 copy-done.4
  5.8 4.9 %build_dense.1.dense_ref = bf16[1024,2048]{1,0:T(8,128)(2,1)S(1)} custom-call(s32[256]{0:T(256)S(1)} %bitcast.5, s32[256]{0:T(256)S(1)} %bitcast.6, s32[1]{0:T(128)} %bitcast.4.count_ref, bf16[256,128,128]{2,1,0:T(8,128)(2,1)} %bitcast.7), custom_call_target="tpu_custom_call" | custom-call | flops 4194304 | bytes 12582912 | tf_op jit(solution)/shard_map/build_dense/pallas_call | solution.py:85
  10.7 0.0 copy-start.1
  10.7 0.0 copy-start.2
  10.8 0.0 collective-permute-done.1.refs_2_
  10.8 0.1 collective-permute-start.2
  10.8 2.0 %collective-permute-start.3 = (bf16[256,256]{1,0:T(8,128)(2,1)S(1)}, bf16[256,256]{1,0:T(8,128)(2,1)S(1)}, u32[]{:S(2)}, u32[]{:S(2)}) collective-permute-start(bf16[256,256]{1,0:T(8,128)(2,1)S(1)} %collective-permute-done.1.refs_2_), channel_id=1, source_target_pairs={{0,4},{8,0},{16,8},{24,16},{28,24},{20,28},{12,20},{4,12},{1,5},{9... | collective-permute-start | bytes 393224 | tf_op jit(solution)/shard_map/ppermute | solution.py:281
  12.9 3.8 %collective-permute-done.2.refs_3_ = bf16[256,256]{1,0:T(8,128)(2,1)S(1)} collective-permute-done((bf16[256,256]{1,0:T(8,128)(2,1)S(1)}, bf16[256,256]{1,0:T(8,128)(2,1)S(1)}, u32[]{:S(2)}, u32[]{:S(2)}) %collective-permute-start.2) | collective-permute-done | bytes 131104 | tf_op jit(solution)/shard_map/ppermute | solution.py:281
  16.7 0.3 collective-permute-start.4
  17.0 2.0 %collective-permute-start.5 = (bf16[256,256]{1,0:T(8,128)(2,1)S(1)}, bf16[256,256]{1,0:T(8,128)(2,1)S(1)}, u32[]{:S(2)}, u32[]{:S(2)}) collective-permute-start(bf16[256,256]{1,0:T(8,128)(2,1)S(1)} %collective-permute-done.3.refs_4_), channel_id=1, source_target_pairs={{0,4},{8,0},{16,8},{24,16},{28,24},{20,28},{12,20},{4,12},{1,5},{9... | collective-permute-start | bytes 393224 | tf_op jit(solution)/shard_map/ppermute | solution.py:281
  18.9 3.5 %collective-permute-done.4.refs_5_ = bf16[256,256]{1,0:T(8,128)(2,1)S(1)} collective-permute-done((bf16[256,256]{1,0:T(8,128)(2,1)S(1)}, bf16[256,256]{1,0:T(8,128)(2,1)S(1)}, u32[]{:S(2)}, u32[]{:S(2)}) %collective-permute-start.4) | collective-permute-done | bytes 131104 | tf_op jit(solution)/shard_map/ppermute | solution.py:281
  22.4 0.6 collective-permute-start.6
  23.0 0.4 collective-permute-done.5.refs_6_
  23.4 4.0 %collective-permute-done.6.refs_7_ = bf16[256,256]{1,0:T(8,128)(2,1)S(1)} collective-permute-done((bf16[256,256]{1,0:T(8,128)(2,1)S(1)}, bf16[256,256]{1,0:T(8,128)(2,1)S(1)}, u32[]{:S(2)}, u32[]{:S(2)}) %collective-permute-start.6) | collective-permute-done | bytes 131104 | tf_op jit(solution)/shard_map/ppermute | solution.py:281
  27.4 0.7 forward_product.3
  28.1 0.1 collective-permute-start.9
  28.2 0.7 forward_product.2
  28.9 1.1 %collective-permute-start.7 = (bf16[256,256]{1,0:T(8,128)(2,1)S(1)}, bf16[256,256]{1,0:T(8,128)(2,1)S(1)}, u32[]{:S(2)}, u32[]{:S(2)}) collective-permute-start(bf16[256,256]{1,0:T(8,128)(2,1)S(1)} %get-tuple-element.46), channel_id=1, source_target_pairs={{0,2},{1,3},{2,0},{3,1},{4,6},{5,7},{6,4},{7,5},{8,10},{9,11},{10,... | collective-permute-start | bytes 393224 | tf_op jit(solution)/shard_map/ppermute | solution.py:285
  30.0 0.8 collective-permute-start.8
  30.8 0.0 collective-permute-done.9.refs_3_
  30.8 4.4 %collective-permute-done.7.refs_0_ = bf16[256,256]{1,0:T(8,128)(2,1)S(1)} collective-permute-done((bf16[256,256]{1,0:T(8,128)(2,1)S(1)}, bf16[256,256]{1,0:T(8,128)(2,1)S(1)}, u32[]{:S(2)}, u32[]{:S(2)}) %collective-permute-start.7) | collective-permute-done | bytes 131104 | tf_op jit(solution)/shard_map/ppermute | solution.py:285
  35.3 2.0 %collective-permute-done.8.refs_1_ = bf16[256,256]{1,0:T(8,128)(2,1)S(1)} collective-permute-done((bf16[256,256]{1,0:T(8,128)(2,1)S(1)}, bf16[256,256]{1,0:T(8,128)(2,1)S(1)}, u32[]{:S(2)}, u32[]{:S(2)}) %collective-permute-start.8) | collective-permute-done | bytes 131104 | tf_op jit(solution)/shard_map/ppermute | solution.py:285
  37.3 1.2 %middle.1 = (bf16[256,256]{1,0:T(8,128)(2,1)}, bf16[256,256]{1,0:T(8,128)(2,1)S(1)}, f32[64,256]{1,0:T(8,128)S(1)}, f32[64,256]{1,0:T(8,128)S(1)}, f32[64,256]{1,0:T(8,128)S(1)}, /*index=5*/f32[64,256]{1,0:T(8,128)S(1)}) custom-call(bf16[256,256]{1,0:T(8,128)(2,1)S(1)} %collective-permute-done.7.refs_0_, ...), custom_call_target="tpu_custom_call" | custom-call | flops 167772160 | bytes 1310720 | tf_op jit(solution)/shard_map/middle/pallas_call | solution.py:192
  38.5 0.2 collective-permute-start.13
  38.7 0.9 %collective-permute-start.12 = (bf16[256,256]{1,0:T(8,128)(2,1)S(1)}, bf16[256,256]{1,0:T(8,128)(2,1)S(1)}, u32[]{:S(2)}, u32[]{:S(2)}) collective-permute-start(bf16[256,256]{1,0:T(8,128)(2,1)S(1)} %get-tuple-element.56.refs_0_), channel_id=1, source_target_pairs={{0,3},{1,2},{2,1},{3,0},{4,7},{5,6},{6,5},{7,4},{8,11},{9,10},{10,... | collective-permute-start | bytes 393224 | tf_op jit(solution)/shard_map/ppermute | solution.py:285
  39.6 1.0 %collective-permute-start.11 = (bf16[256,256]{1,0:T(8,128)(2,1)S(1)}, bf16[256,256]{1,0:T(8,128)(2,1)S(1)}, u32[]{:S(2)}, u32[]{:S(2)}) collective-permute-start(bf16[256,256]{1,0:T(8,128)(2,1)S(1)} %get-tuple-element.56.refs_0_), channel_id=1, source_target_pairs={{0,2},{1,3},{2,0},{3,1},{4,6},{5,7},{6,4},{7,5},{8,10},{9,11},{10,... | collective-permute-start | bytes 393224 | tf_op jit(solution)/shard_map/ppermute | solution.py:285
  40.6 0.0 collective-permute-start.10
  40.6 1.1 %collective-permute-start.14 = (f32[64,256]{1,0:T(8,128)S(1)}, f32[64,256]{1,0:T(8,128)S(1)}, u32[]{:S(2)}, u32[]{:S(2)}) collective-permute-start(f32[64,256]{1,0:T(8,128)S(1)} %get-tuple-element.54), channel_id=1, source_target_pairs={{0,2},{1,3},{2,0},{3,1},{4,6},{5,7},{6,4},{7,5},{8,10},{9,11},{10,... | collective-permute-start | bytes 196616 | tf_op jit(solution)/shard_map/ppermute | solution.py:285
  41.7 0.8 %collective-permute-start.15 = (f32[64,256]{1,0:T(8,128)S(1)}, f32[64,256]{1,0:T(8,128)S(1)}, u32[]{:S(2)}, u32[]{:S(2)}) collective-permute-start(f32[64,256]{1,0:T(8,128)S(1)} %get-tuple-element.55), channel_id=1, source_target_pairs={{0,3},{1,2},{2,1},{3,0},{4,7},{5,6},{6,5},{7,4},{8,11},{9,10},{10,... | collective-permute-start | bytes 196616 | tf_op jit(solution)/shard_map/ppermute | solution.py:285
  42.5 6.6 %collective-permute-done.14 = f32[64,256]{1,0:T(8,128)S(1)} collective-permute-done((f32[64,256]{1,0:T(8,128)S(1)}, f32[64,256]{1,0:T(8,128)S(1)}, u32[]{:S(2)}, u32[]{:S(2)}) %collective-permute-start.14) | collective-permute-done | bytes 65568 | tf_op jit(solution)/shard_map/ppermute | solution.py:285
  49.1 0.6 collective-permute-done.15
  49.7 0.0 collective-permute-done.12.refs_3_
  49.7 0.0 collective-permute-done.11.refs_2_
  49.7 0.0 collective-permute-done.10.refs_1_
  49.7 0.4 backward_product.2
  50.2 1.5 %collective-permute-start.16 = (bf16[256,256]{1,0:T(8,128)(2,1)S(1)}, bf16[256,256]{1,0:T(8,128)(2,1)S(1)}, u32[]{:S(2)}, u32[]{:S(2)}) collective-permute-start(bf16[256,256]{1,0:T(8,128)(2,1)S(1)} %backward_product.2), channel_id=1, source_target_pairs={{0,8},{8,16},{16,24},{24,28},{28,20},{20,12},{12,4},{4,0},{1,9},{9... | collective-permute-start | bytes 393224 | tf_op jit(solution)/shard_map/ppermute | solution.py:281
  51.7 0.6 collective-permute-start.17
  52.3 1.3 %backward_product.3 = (bf16[256,256]{1,0:T(8,128)(2,1)S(1)}, bf16[256,256]{1,0:T(8,128)(2,1)S(1)}, bf16[256,256]{1,0:T(8,128)(2,1)S(1)}, bf16[256,256]{1,0:T(8,1...) custom-call(bf16[1024,2048]{1,0:T(8,128)(2,1)S(1)} %build_dense.1.dense_ref, ...), custom_call_target="tpu_custom_call" | custom-call | flops 134217728 | bytes 917504 | tf_op jit(solution)/shard_map/backward_product/pallas_call | solution.py:238
  53.6 1.5 %collective-permute-start.19 = (bf16[256,256]{1,0:T(8,128)(2,1)S(1)}, bf16[256,256]{1,0:T(8,128)(2,1)S(1)}, u32[]{:S(2)}, u32[]{:S(2)}) collective-permute-start(bf16[256,256]{1,0:T(8,128)(2,1)S(1)} %get-tuple-element.71), channel_id=1, source_target_pairs={{0,4},{8,0},{16,8},{24,16},{28,24},{20,28},{12,20},{4,12},{1,5},{9... | collective-permute-start | bytes 393224 | tf_op jit(solution)/shard_map/ppermute | solution.py:281
  55.2 2.1 %collective-permute-done.17 = f32[64,256]{1,0:T(8,128)S(1)} collective-permute-done((f32[64,256]{1,0:T(8,128)S(1)}, f32[64,256]{1,0:T(8,128)S(1)}, u32[]{:S(2)}, u32[]{:S(2)}) %collective-permute-start.17) | collective-permute-done | bytes 65568 | tf_op jit(solution)/shard_map/ppermute | solution.py:285
  57.3 0.0 collective-permute-done.16
  57.3 0.1 collective-permute-start.18
  57.4 1.1 %collective-permute-start.20 = (f32[64,256]{1,0:T(8,128)S(1)}, f32[64,256]{1,0:T(8,128)S(1)}, u32[]{:S(2)}, u32[]{:S(2)}) collective-permute-start(f32[64,256]{1,0:T(8,128)S(1)} %add.37), channel_id=1, source_target_pairs={{0,8},{4,12},{8,0},{12,4},{16,24},{20,28},{24,16},{28,20},{1,9},{5... | collective-permute-start | bytes 196616 | tf_op jit(solution)/shard_map/ppermute | solution.py:285
  58.6 0.2 collective-permute-done.19
  58.7 3.0 %collective-permute-done.20 = f32[64,256]{1,0:T(8,128)S(1)} collective-permute-done((f32[64,256]{1,0:T(8,128)S(1)}, f32[64,256]{1,0:T(8,128)S(1)}, u32[]{:S(2)}, u32[]{:S(2)}) %collective-permute-start.20) | collective-permute-done | bytes 65568 | tf_op jit(solution)/shard_map/ppermute | solution.py:285
  61.8 0.5 collective-permute-done.18
  62.4 1.5 %collective-permute-start.22 = (bf16[256,256]{1,0:T(8,128)(2,1)S(1)}, bf16[256,256]{1,0:T(8,128)(2,1)S(1)}, u32[]{:S(2)}, u32[]{:S(2)}) collective-permute-start(bf16[256,256]{1,0:T(8,128)(2,1)S(1)} %add_convert_fusion.2), channel_id=1, source_target_pairs={{0,4},{8,0},{16,8},{24,16},{28,24},{20,28},{12,20},{4,12},{1,5},{9... | collective-permute-start | bytes 393224 | tf_op jit(solution)/shard_map/ppermute | solution.py:281
  63.9 0.6 collective-permute-start.21
  64.5 2.3 %collective-permute-start.23 = (f32[64,256]{1,0:T(8,128)S(1)}, f32[64,256]{1,0:T(8,128)S(1)}, u32[]{:S(2)}, u32[]{:S(2)}) collective-permute-start(f32[64,256]{1,0:T(8,128)S(1)} %add.40), channel_id=1, source_target_pairs={{0,16},{4,20},{8,24},{12,28},{16,0},{20,4},{24,8},{28,12},{1,17},{... | collective-permute-start | bytes 196616 | tf_op jit(solution)/shard_map/ppermute | solution.py:285
  66.9 3.1 %collective-permute-done.23 = f32[64,256]{1,0:T(8,128)S(1)} collective-permute-done((f32[64,256]{1,0:T(8,128)S(1)}, f32[64,256]{1,0:T(8,128)S(1)}, u32[]{:S(2)}, u32[]{:S(2)}) %collective-permute-start.23) | collective-permute-done | bytes 65568 | tf_op jit(solution)/shard_map/ppermute | solution.py:285
  70.0 0.0 collective-permute-done.22
  70.0 3.9 %collective-permute-start.25 = (bf16[256,256]{1,0:T(8,128)(2,1)S(1)}, bf16[256,256]{1,0:T(8,128)(2,1)S(1)}, u32[]{:S(2)}, u32[]{:S(2)}) collective-permute-start(bf16[256,256]{1,0:T(8,128)(2,1)S(1)} %add_convert_fusion), channel_id=1, source_target_pairs={{0,4},{8,0},{16,8},{24,16},{28,24},{20,28},{12,20},{4,12},{1,5},{9... | collective-permute-start | bytes 393224 | tf_op jit(solution)/shard_map/ppermute | solution.py:281
  73.9 0.1 collective-permute-start.24
  74.0 0.1 collective-permute-start.28
  74.1 1.5 %collective-permute-start.27 = (f32[64,256]{1,0:T(8,128)S(1)}, f32[64,256]{1,0:T(8,128)S(1)}, u32[]{:S(2)}, u32[]{:S(2)}) collective-permute-start(f32[64,256]{1,0:T(8,128)S(1)} %add.43.refs_0_), channel_id=1, source_target_pairs={{0,2},{1,3},{2,0},{3,1},{4,6},{5,7},{6,4},{7,5},{8,10},{9,11},{10,... | collective-permute-start | bytes 196616 | tf_op jit(solution)/shard_map/ppermute | solution.py:285
  75.6 0.3 collective-permute-start.26
  76.0 2.5 %collective-permute-done.28.refs_3_ = f32[64,256]{1,0:T(8,128)S(1)} collective-permute-done((f32[64,256]{1,0:T(8,128)S(1)}, f32[64,256]{1,0:T(8,128)S(1)}, u32[]{:S(2)}, u32[]{:S(2)}) %collective-permute-start.28) | collective-permute-done | bytes 65568 | tf_op jit(solution)/shard_map/ppermute | solution.py:285
  78.5 1.4 %collective-permute-done.27.refs_2_ = f32[64,256]{1,0:T(8,128)S(1)} collective-permute-done((f32[64,256]{1,0:T(8,128)S(1)}, f32[64,256]{1,0:T(8,128)S(1)}, u32[]{:S(2)}, u32[]{:S(2)}) %collective-permute-start.27) | collective-permute-done | bytes 65568 | tf_op jit(solution)/shard_map/ppermute | solution.py:285
  79.9 0.0 collective-permute-done.26.refs_1_
  79.9 0.0 collective-permute-done.25.third_ref
  79.9 0.8 finish.1
  (20 shorter events, 0.2 us)
Async XLA Ops:
  0.6 26.8 %copy-start = (bf16[256,256]{1,0:T(8,128)(2,1)S(1)}, bf16[256,256]{1,0:T(8,128)(2,1)}, u32[]{:S(2)}) copy-start(bf16[256,256]{1,0:T(8,128)(2,1)} %refs_0_.3) | copy-start | bytes 393220
  0.6 10.1 %collective-permute-start.1 = (bf16[256,256]{1,0:T(8,128)(2,1)}, bf16[256,256]{1,0:T(8,128)(2,1)S(1)}, u32[]{:S(2)}, u32[]{:S(2)}) collective-permute-start(bf16[256,256]{1,0:T(8,128)(2,1)} %refs_0_.3), channel_id=1, source_target_pairs={{0,4},{8,0},{16,8},{24,16},{28,24},{20,28},{12,20},{4,12},{1,5},{9... | collective-permute-start | bytes 393224 | tf_op jit(solution)/shard_map/ppermute | solution.py:281
  3.7 7.1 %collective-permute-start = (bf16[256,256]{1,0:T(8,128)(2,1)}, bf16[256,256]{1,0:T(8,128)(2,1)S(1)}, u32[]{:S(2)}, u32[]{:S(2)}) collective-permute-start(bf16[256,256]{1,0:T(8,128)(2,1)} %refs_0_.3), channel_id=1, source_target_pairs={{0,8},{8,16},{16,24},{24,28},{28,20},{20,12},{12,4},{4,0},{1,9},{9... | collective-permute-start | bytes 393224 | tf_op jit(solution)/shard_map/ppermute | solution.py:281
  4.4 0.7 copy-start.3
  5.1 0.7 copy-start.4
  10.7 26.6 %copy-start.1 = (bf16[256,256]{1,0:T(8,128)(2,1)S(1)}, bf16[256,256]{1,0:T(8,128)(2,1)}, u32[]{:S(2)}) copy-start(bf16[256,256]{1,0:T(8,128)(2,1)} %refs_4_.1) | copy-start | bytes 393220
  10.7 26.5 %copy-start.2 = (bf16[256,256]{1,0:T(8,128)(2,1)S(1)}, bf16[256,256]{1,0:T(8,128)(2,1)}, u32[]{:S(2)}) copy-start(bf16[256,256]{1,0:T(8,128)(2,1)} %refs_5_.1) | copy-start | bytes 393220
  10.8 5.9 %collective-permute-start.2 = (bf16[256,256]{1,0:T(8,128)(2,1)S(1)}, bf16[256,256]{1,0:T(8,128)(2,1)S(1)}, u32[]{:S(2)}, u32[]{:S(2)}) collective-permute-start(bf16[256,256]{1,0:T(8,128)(2,1)S(1)} %collective-permute-done.refs_1_), channel_id=1, source_target_pairs={{0,8},{8,16},{16,24},{24,28},{28,20},{20,12},{12,4},{4,0},{1,9},{9... | collective-permute-start | bytes 393224 | tf_op jit(solution)/shard_map/ppermute | solution.py:281
  10.8 6.1 %collective-permute-start.3 = (bf16[256,256]{1,0:T(8,128)(2,1)S(1)}, bf16[256,256]{1,0:T(8,128)(2,1)S(1)}, u32[]{:S(2)}, u32[]{:S(2)}) collective-permute-start(bf16[256,256]{1,0:T(8,128)(2,1)S(1)} %collective-permute-done.1.refs_2_), channel_id=1, source_target_pairs={{0,4},{8,0},{16,8},{24,16},{28,24},{20,28},{12,20},{4,12},{1,5},{9... | collective-permute-start | bytes 393224 | tf_op jit(solution)/shard_map/ppermute | solution.py:281
  16.7 5.8 %collective-permute-start.4 = (bf16[256,256]{1,0:T(8,128)(2,1)S(1)}, bf16[256,256]{1,0:T(8,128)(2,1)S(1)}, u32[]{:S(2)}, u32[]{:S(2)}) collective-permute-start(bf16[256,256]{1,0:T(8,128)(2,1)S(1)} %collective-permute-done.2.refs_3_), channel_id=1, source_target_pairs={{0,8},{8,16},{16,24},{24,28},{28,20},{20,12},{12,4},{4,0},{1,9},{9... | collective-permute-start | bytes 393224 | tf_op jit(solution)/shard_map/ppermute | solution.py:281
  17.0 6.5 %collective-permute-start.5 = (bf16[256,256]{1,0:T(8,128)(2,1)S(1)}, bf16[256,256]{1,0:T(8,128)(2,1)S(1)}, u32[]{:S(2)}, u32[]{:S(2)}) collective-permute-start(bf16[256,256]{1,0:T(8,128)(2,1)S(1)} %collective-permute-done.3.refs_4_), channel_id=1, source_target_pairs={{0,4},{8,0},{16,8},{24,16},{28,24},{20,28},{12,20},{4,12},{1,5},{9... | collective-permute-start | bytes 393224 | tf_op jit(solution)/shard_map/ppermute | solution.py:281
  22.4 5.0 %collective-permute-start.6 = (bf16[256,256]{1,0:T(8,128)(2,1)S(1)}, bf16[256,256]{1,0:T(8,128)(2,1)S(1)}, u32[]{:S(2)}, u32[]{:S(2)}) collective-permute-start(bf16[256,256]{1,0:T(8,128)(2,1)S(1)} %collective-permute-done.4.refs_5_), channel_id=1, source_target_pairs={{0,8},{8,16},{16,24},{24,28},{28,20},{20,12},{12,4},{4,0},{1,9},{9... | collective-permute-start | bytes 393224 | tf_op jit(solution)/shard_map/ppermute | solution.py:281
  28.1 2.7 %collective-permute-start.9 = (bf16[256,256]{1,0:T(8,128)(2,1)S(1)}, bf16[256,256]{1,0:T(8,128)(2,1)S(1)}, u32[]{:S(2)}, u32[]{:S(2)}) collective-permute-start(bf16[256,256]{1,0:T(8,128)(2,1)S(1)} %get-tuple-element.49), channel_id=1, source_target_pairs={{0,1},{1,0},{2,3},{3,2},{4,5},{5,4},{6,7},{7,6},{8,9},{9,8},{10,11... | collective-permute-start | bytes 393224 | tf_op jit(solution)/shard_map/ppermute | solution.py:285
  28.9 6.4 %collective-permute-start.7 = (bf16[256,256]{1,0:T(8,128)(2,1)S(1)}, bf16[256,256]{1,0:T(8,128)(2,1)S(1)}, u32[]{:S(2)}, u32[]{:S(2)}) collective-permute-start(bf16[256,256]{1,0:T(8,128)(2,1)S(1)} %get-tuple-element.46), channel_id=1, source_target_pairs={{0,2},{1,3},{2,0},{3,1},{4,6},{5,7},{6,4},{7,5},{8,10},{9,11},{10,... | collective-permute-start | bytes 393224 | tf_op jit(solution)/shard_map/ppermute | solution.py:285
  30.0 7.3 %collective-permute-start.8 = (bf16[256,256]{1,0:T(8,128)(2,1)S(1)}, bf16[256,256]{1,0:T(8,128)(2,1)S(1)}, u32[]{:S(2)}, u32[]{:S(2)}) collective-permute-start(bf16[256,256]{1,0:T(8,128)(2,1)S(1)} %get-tuple-element.47), channel_id=1, source_target_pairs={{0,3},{1,2},{2,1},{3,0},{4,7},{5,6},{6,5},{7,4},{8,11},{9,10},{10,... | collective-permute-start | bytes 393224 | tf_op jit(solution)/shard_map/ppermute | solution.py:285
  38.5 3.2 %collective-permute-start.13 = (f32[64,256]{1,0:T(8,128)S(1)}, f32[64,256]{1,0:T(8,128)S(1)}, u32[]{:S(2)}, u32[]{:S(2)}) collective-permute-start(f32[64,256]{1,0:T(8,128)S(1)} %get-tuple-element.53), channel_id=1, source_target_pairs={{0,1},{1,0},{2,3},{3,2},{4,5},{5,4},{6,7},{7,6},{8,9},{9,8},{10,11... | collective-permute-start | bytes 196616 | tf_op jit(solution)/shard_map/ppermute | solution.py:285
  38.7 11.0 %collective-permute-start.12 = (bf16[256,256]{1,0:T(8,128)(2,1)S(1)}, bf16[256,256]{1,0:T(8,128)(2,1)S(1)}, u32[]{:S(2)}, u32[]{:S(2)}) collective-permute-start(bf16[256,256]{1,0:T(8,128)(2,1)S(1)} %get-tuple-element.56.refs_0_), channel_id=1, source_target_pairs={{0,3},{1,2},{2,1},{3,0},{4,7},{5,6},{6,5},{7,4},{8,11},{9,10},{10,... | collective-permute-start | bytes 393224 | tf_op jit(solution)/shard_map/ppermute | solution.py:285
  39.6 10.1 %collective-permute-start.11 = (bf16[256,256]{1,0:T(8,128)(2,1)S(1)}, bf16[256,256]{1,0:T(8,128)(2,1)S(1)}, u32[]{:S(2)}, u32[]{:S(2)}) collective-permute-start(bf16[256,256]{1,0:T(8,128)(2,1)S(1)} %get-tuple-element.56.refs_0_), channel_id=1, source_target_pairs={{0,2},{1,3},{2,0},{3,1},{4,6},{5,7},{6,4},{7,5},{8,10},{9,11},{10,... | collective-permute-start | bytes 393224 | tf_op jit(solution)/shard_map/ppermute | solution.py:285
  40.6 9.1 %collective-permute-start.10 = (bf16[256,256]{1,0:T(8,128)(2,1)S(1)}, bf16[256,256]{1,0:T(8,128)(2,1)S(1)}, u32[]{:S(2)}, u32[]{:S(2)}) collective-permute-start(bf16[256,256]{1,0:T(8,128)(2,1)S(1)} %get-tuple-element.56.refs_0_), channel_id=1, source_target_pairs={{0,1},{1,0},{2,3},{3,2},{4,5},{5,4},{6,7},{7,6},{8,9},{9,8},{10,11... | collective-permute-start | bytes 393224 | tf_op jit(solution)/shard_map/ppermute | solution.py:285
  40.6 8.5 %collective-permute-start.14 = (f32[64,256]{1,0:T(8,128)S(1)}, f32[64,256]{1,0:T(8,128)S(1)}, u32[]{:S(2)}, u32[]{:S(2)}) collective-permute-start(f32[64,256]{1,0:T(8,128)S(1)} %get-tuple-element.54), channel_id=1, source_target_pairs={{0,2},{1,3},{2,0},{3,1},{4,6},{5,7},{6,4},{7,5},{8,10},{9,11},{10,... | collective-permute-start | bytes 196616 | tf_op jit(solution)/shard_map/ppermute | solution.py:285
  41.7 8.0 %collective-permute-start.15 = (f32[64,256]{1,0:T(8,128)S(1)}, f32[64,256]{1,0:T(8,128)S(1)}, u32[]{:S(2)}, u32[]{:S(2)}) collective-permute-start(f32[64,256]{1,0:T(8,128)S(1)} %get-tuple-element.55), channel_id=1, source_target_pairs={{0,3},{1,2},{2,1},{3,0},{4,7},{5,6},{6,5},{7,4},{8,11},{9,10},{10,... | collective-permute-start | bytes 196616 | tf_op jit(solution)/shard_map/ppermute | solution.py:285
  50.2 7.1 %collective-permute-start.16 = (bf16[256,256]{1,0:T(8,128)(2,1)S(1)}, bf16[256,256]{1,0:T(8,128)(2,1)S(1)}, u32[]{:S(2)}, u32[]{:S(2)}) collective-permute-start(bf16[256,256]{1,0:T(8,128)(2,1)S(1)} %backward_product.2), channel_id=1, source_target_pairs={{0,8},{8,16},{16,24},{24,28},{28,20},{20,12},{12,4},{4,0},{1,9},{9... | collective-permute-start | bytes 393224 | tf_op jit(solution)/shard_map/ppermute | solution.py:281
  51.7 5.5 %collective-permute-start.17 = (f32[64,256]{1,0:T(8,128)S(1)}, f32[64,256]{1,0:T(8,128)S(1)}, u32[]{:S(2)}, u32[]{:S(2)}) collective-permute-start(f32[64,256]{1,0:T(8,128)S(1)} %add_add_fusion), channel_id=1, source_target_pairs={{0,4},{4,0},{8,12},{12,8},{16,20},{20,16},{24,28},{28,24},{1,5},{5... | collective-permute-start | bytes 196616 | tf_op jit(solution)/shard_map/ppermute | solution.py:285
  53.6 5.1 %collective-permute-start.19 = (bf16[256,256]{1,0:T(8,128)(2,1)S(1)}, bf16[256,256]{1,0:T(8,128)(2,1)S(1)}, u32[]{:S(2)}, u32[]{:S(2)}) collective-permute-start(bf16[256,256]{1,0:T(8,128)(2,1)S(1)} %get-tuple-element.71), channel_id=1, source_target_pairs={{0,4},{8,0},{16,8},{24,16},{28,24},{20,28},{12,20},{4,12},{1,5},{9... | collective-permute-start | bytes 393224 | tf_op jit(solution)/shard_map/ppermute | solution.py:281
  57.3 5.0 %collective-permute-start.18 = (bf16[256,256]{1,0:T(8,128)(2,1)S(1)}, bf16[256,256]{1,0:T(8,128)(2,1)S(1)}, u32[]{:S(2)}, u32[]{:S(2)}) collective-permute-start(bf16[256,256]{1,0:T(8,128)(2,1)S(1)} %add_convert_fusion.4), channel_id=1, source_target_pairs={{0,8},{8,16},{16,24},{24,28},{28,20},{20,12},{12,4},{4,0},{1,9},{9... | collective-permute-start | bytes 393224 | tf_op jit(solution)/shard_map/ppermute | solution.py:281
  57.4 4.3 %collective-permute-start.20 = (f32[64,256]{1,0:T(8,128)S(1)}, f32[64,256]{1,0:T(8,128)S(1)}, u32[]{:S(2)}, u32[]{:S(2)}) collective-permute-start(f32[64,256]{1,0:T(8,128)S(1)} %add.37), channel_id=1, source_target_pairs={{0,8},{4,12},{8,0},{12,4},{16,24},{20,28},{24,16},{28,20},{1,9},{5... | collective-permute-start | bytes 196616 | tf_op jit(solution)/shard_map/ppermute | solution.py:285
  62.4 7.6 %collective-permute-start.22 = (bf16[256,256]{1,0:T(8,128)(2,1)S(1)}, bf16[256,256]{1,0:T(8,128)(2,1)S(1)}, u32[]{:S(2)}, u32[]{:S(2)}) collective-permute-start(bf16[256,256]{1,0:T(8,128)(2,1)S(1)} %add_convert_fusion.2), channel_id=1, source_target_pairs={{0,4},{8,0},{16,8},{24,16},{28,24},{20,28},{12,20},{4,12},{1,5},{9... | collective-permute-start | bytes 393224 | tf_op jit(solution)/shard_map/ppermute | solution.py:281
  63.9 6.1 %collective-permute-start.21 = (bf16[256,256]{1,0:T(8,128)(2,1)S(1)}, bf16[256,256]{1,0:T(8,128)(2,1)S(1)}, u32[]{:S(2)}, u32[]{:S(2)}) collective-permute-start(bf16[256,256]{1,0:T(8,128)(2,1)S(1)} %add_convert_fusion.3), channel_id=1, source_target_pairs={{0,8},{8,16},{16,24},{24,28},{28,20},{20,12},{12,4},{4,0},{1,9},{9... | collective-permute-start | bytes 393224 | tf_op jit(solution)/shard_map/ppermute | solution.py:281
  64.5 5.4 %collective-permute-start.23 = (f32[64,256]{1,0:T(8,128)S(1)}, f32[64,256]{1,0:T(8,128)S(1)}, u32[]{:S(2)}, u32[]{:S(2)}) collective-permute-start(f32[64,256]{1,0:T(8,128)S(1)} %add.40), channel_id=1, source_target_pairs={{0,16},{4,20},{8,24},{12,28},{16,0},{20,4},{24,8},{28,12},{1,17},{... | collective-permute-start | bytes 196616 | tf_op jit(solution)/shard_map/ppermute | solution.py:285
  70.0 9.9 %collective-permute-start.25 = (bf16[256,256]{1,0:T(8,128)(2,1)S(1)}, bf16[256,256]{1,0:T(8,128)(2,1)S(1)}, u32[]{:S(2)}, u32[]{:S(2)}) collective-permute-start(bf16[256,256]{1,0:T(8,128)(2,1)S(1)} %add_convert_fusion), channel_id=1, source_target_pairs={{0,4},{8,0},{16,8},{24,16},{28,24},{20,28},{12,20},{4,12},{1,5},{9... | collective-permute-start | bytes 393224 | tf_op jit(solution)/shard_map/ppermute | solution.py:281
  73.9 6.0 %collective-permute-start.24 = (bf16[256,256]{1,0:T(8,128)(2,1)S(1)}, bf16[256,256]{1,0:T(8,128)(2,1)S(1)}, u32[]{:S(2)}, u32[]{:S(2)}) collective-permute-start(bf16[256,256]{1,0:T(8,128)(2,1)S(1)} %add_convert_fusion.1), channel_id=1, source_target_pairs={{0,8},{8,16},{16,24},{24,28},{28,20},{20,12},{12,4},{4,0},{1,9},{9... | collective-permute-start | bytes 393224 | tf_op jit(solution)/shard_map/ppermute | solution.py:281
  74.0 4.4 %collective-permute-start.28 = (f32[64,256]{1,0:T(8,128)S(1)}, f32[64,256]{1,0:T(8,128)S(1)}, u32[]{:S(2)}, u32[]{:S(2)}) collective-permute-start(f32[64,256]{1,0:T(8,128)S(1)} %add.43.refs_0_), channel_id=1, source_target_pairs={{0,3},{1,2},{2,1},{3,0},{4,7},{5,6},{6,5},{7,4},{8,11},{9,10},{10,... | collective-permute-start | bytes 196616 | tf_op jit(solution)/shard_map/ppermute | solution.py:285
  74.1 5.8 %collective-permute-start.27 = (f32[64,256]{1,0:T(8,128)S(1)}, f32[64,256]{1,0:T(8,128)S(1)}, u32[]{:S(2)}, u32[]{:S(2)}) collective-permute-start(f32[64,256]{1,0:T(8,128)S(1)} %add.43.refs_0_), channel_id=1, source_target_pairs={{0,2},{1,3},{2,0},{3,1},{4,6},{5,7},{6,4},{7,5},{8,10},{9,11},{10,... | collective-permute-start | bytes 196616 | tf_op jit(solution)/shard_map/ppermute | solution.py:285
  75.6 4.3 %collective-permute-start.26 = (f32[64,256]{1,0:T(8,128)S(1)}, f32[64,256]{1,0:T(8,128)S(1)}, u32[]{:S(2)}, u32[]{:S(2)}) collective-permute-start(f32[64,256]{1,0:T(8,128)S(1)} %add.43.refs_0_), channel_id=1, source_target_pairs={{0,1},{1,0},{2,3},{3,2},{4,5},{5,4},{6,7},{7,6},{8,9},{9,8},{10,11... | collective-permute-start | bytes 196616 | tf_op jit(solution)/shard_map/ppermute | solution.py:285

commit v5 on v4

v5 whole, which is shorter than its diff:
```python
import functools
import math

import jax
import jax.numpy as jnp
from jax import lax
from jax.experimental import pallas as pl
from jax.experimental.pallas import tpu as pltpu
from jax.sharding import PartitionSpec as P

chunk_tiles = 16
chunk_slots = 4
strips_per_step = 8
mib = 1024 * 1024


def scratch_bytes(*shapes):
    return sum(math.prod(shape) * jnp.dtype(kind).itemsize for shape, kind in shapes)


def build_kernel(rows_ref, cols_ref, count_ref, tiles_ref, dense_ref, total, held, sems, *, blocks, steps):
    side = tiles_ref.shape[1]
    first_block = pl.program_id(0) * blocks
    count = count_ref[0]
    chunks = (count + chunk_tiles - 1) // chunk_tiles

    def fetch(index):
        slot = lax.rem(index, chunk_slots)
        return pltpu.make_async_copy(
            tiles_ref.at[pl.ds(index * chunk_tiles, chunk_tiles)], held.at[slot], sems.at[slot]
        )

    for ahead in range(chunk_slots - 1):
        @pl.when(ahead < chunks)
        def _():
            fetch(ahead).start()

    row_blocks = dense_ref.shape[0] // side

    def clear(block, carry):
        down = pl.ds(pl.multiple_of(block * side, side), side)
        total[down, :] = jnp.zeros((side, total.shape[1]), jnp.float32)
        return carry

    lax.fori_loop(0, row_blocks, clear, 0)

    def chunk_step(index, carry):
        @pl.when(index + chunk_slots - 1 < chunks)
        def _():
            fetch(index + chunk_slots - 1).start()

        fetch(index).wait()
        slot = lax.rem(index, chunk_slots)
        for lane in range(chunk_tiles):
            place = index * chunk_tiles + lane
            col = cols_ref[place] - first_block
            live = place < count
            if steps > 1:
                live = live & (col >= 0) & (col < blocks)
                col = jnp.where(live, col, 0)
            row = jnp.where(live, rows_ref[place], row_blocks)
            down = pl.ds(pl.multiple_of(row * side, side), side)
            along = pl.ds(pl.multiple_of(col * side, side), side)
            total[down, along] += held[slot, lane].astype(jnp.float32)
        return carry

    lax.fori_loop(0, chunks, chunk_step, 0)

    def round_block(block, carry):
        down = pl.ds(pl.multiple_of(block * side, side), side)
        dense_ref[down, :] = total[down, :].astype(jnp.bfloat16)
        return carry

    lax.fori_loop(0, row_blocks, round_block, 0)


def build_dense(rows, cols, count, tiles, row_blocks, col_blocks, per_strip):
    capacity, side, _ = tiles.shape
    blocks = min(strips_per_step * per_strip, col_blocks)
    steps = col_blocks // blocks
    high, wide = row_blocks * side, blocks * side
    total = ((high + side, wide), jnp.float32)
    held = ((chunk_slots, chunk_tiles, side, side), jnp.bfloat16)
    block = ((high, wide), jnp.bfloat16)
    return pl.pallas_call(
        functools.partial(build_kernel, blocks=blocks, steps=steps),
        out_shape=jax.ShapeDtypeStruct((high, col_blocks * side), jnp.bfloat16),
        grid_spec=pltpu.PrefetchScalarGridSpec(
            num_scalar_prefetch=3,
            grid=(steps,),
            in_specs=[pl.BlockSpec(memory_space=pltpu.HBM)],
            out_specs=pl.BlockSpec((high, wide), lambda i, *_: (0, i)),
            scratch_shapes=[
                pltpu.VMEM(*total),
                pltpu.VMEM(*held),
                pltpu.SemaphoreType.DMA((chunk_slots,)),
            ],
        ),
        compiler_params=pltpu.CompilerParams(vmem_limit_bytes=46 * mib),
        cost_estimate=pl.CostEstimate(
            flops=capacity * side * side,
            bytes_accessed=2 * (capacity * side * side + high * col_blocks * side),
            transcendentals=0,
        ),
        name="build_dense",
    )(rows, cols, count, tiles)


def ring_place(row, count):
    return jnp.where(lax.rem(row, 2) == 0, row // 2, count - 1 - row // 2)


def ring_row(place, count):
    place = lax.rem(place + 2 * count, count)
    return jnp.where(place < count // 2, 2 * place, 2 * (count - 1 - place) + 1)


def forward_kernel(dense_ref, *refs, pieces, sibling, row_count):
    piece_refs, out_ref = refs[: len(pieces)], refs[len(pieces)]
    count = lax.axis_size("col")
    rows = dense_ref.shape[0] // count
    block = dense_ref.shape[1] // row_count
    place = ring_place(lax.axis_index("row"), row_count)
    col = lax.axis_index("col") ^ sibling
    operands = []
    for piece, ref in zip(pieces, piece_refs):
        for offset, first, start, high in piece:
            along = pl.ds(pl.multiple_of(ring_row(place + offset, row_count) * block + first, 128), high)
            operands.append((along, ref, pl.ds(start, high)))
    for index in range(count // 2):
        down = pl.ds(pl.multiple_of((col ^ (2 * index)) * rows, rows), rows)
        total = None
        for along, ref, part in operands:
            product = jnp.dot(dense_ref[down, along], ref[part, :], preferred_element_type=jnp.float32)
            total = product if total is None else total + product
        out_ref[pl.ds(index * rows, rows), :] = total.astype(jnp.bfloat16)


def forward_product(dense, shards, sibling, row_count, col_count):
    pieces = tuple(piece for piece, _ in shards)
    arrays = [array for _, array in shards]
    high, deep = dense.shape
    width = arrays[0].shape[1]
    half = high // 2
    cell = ((high, deep), jnp.bfloat16)
    depth = ((deep, width), jnp.bfloat16)
    out = ((high, width), jnp.float32)
    return pl.pallas_call(
        functools.partial(forward_kernel, pieces=pieces, sibling=sibling, row_count=row_count),
        out_shape=jax.ShapeDtypeStruct((half, width), jnp.bfloat16),
        in_specs=[pl.BlockSpec(memory_space=pltpu.VMEM)] * (1 + len(arrays)),
        out_specs=pl.BlockSpec(memory_space=pltpu.VMEM),
        compiler_params=pltpu.CompilerParams(vmem_limit_bytes=scratch_bytes(cell, depth, out) + 6 * mib),
        cost_estimate=pl.CostEstimate(
            flops=2 * half * deep * width,
            bytes_accessed=2 * (half * deep + deep * width + half * width),
            transcendentals=0,
        ),
        name="forward_product",
    )(dense, *arrays)


def middle_kernel(*refs, blocks, scale):
    sums, refs = refs[:blocks], refs[blocks:]
    weight_ref, refs = refs[0], refs[1:]
    cotangent_refs, (act_ref, message_ref, chunk_ref, sent_ref, product) = refs[:blocks], refs[blocks:]
    weight = weight_ref[...]
    rows, width = act_ref.shape
    over_nodes = (((0,), (0,)), ((), ()))
    terms = None
    for index in range(blocks):
        aggregate = sums[0][pl.ds(index * rows, rows), :].astype(jnp.float32)
        for other in range(1, blocks):
            aggregate += sums[other][pl.ds((index ^ other) * rows, rows), :].astype(jnp.float32)
        high = aggregate.astype(jnp.bfloat16)
        low = (aggregate - high.astype(jnp.float32)).astype(jnp.bfloat16)
        pre = jnp.dot(high, weight, preferred_element_type=jnp.float32)
        pre += jnp.dot(low, weight, preferred_element_type=jnp.float32)
        sig = jax.nn.sigmoid(pre)
        cotangent = cotangent_refs[index][...].astype(jnp.float32)
        grad = (cotangent * sig * (1.0 + pre * (1.0 - sig))).astype(jnp.bfloat16)
        message_ref[pl.ds(index * width, width), :] = lax.dot_general(
            weight, grad, (((1,), (1,)), ((), ())), preferred_element_type=jnp.float32
        ).astype(jnp.bfloat16)
        if index == 0:
            act_ref[...] = (pre * sig).astype(jnp.bfloat16)
        part = lax.dot_general(high, grad, over_nodes, preferred_element_type=jnp.float32)
        part += lax.dot_general(low, grad, over_nodes, preferred_element_type=jnp.float32)
        terms = part if terms is None else terms + part
    product[...] = terms * scale
    col = lax.axis_index("col")
    size = chunk_ref.shape[0]
    chunk_ref[...] = product[pl.ds(pl.multiple_of(col * size, size), size), :]
    sent = product[pl.ds(pl.multiple_of((col ^ 1) * size, size), size), :]
    high = sent.astype(jnp.bfloat16)
    low = (sent - high.astype(jnp.float32)).astype(jnp.bfloat16)
    message_ref[pl.ds(blocks * width, size), :] = high
    message_ref[pl.ds(blocks * width + size, size), :] = low
    sent_ref[...] = high.astype(jnp.float32) + low.astype(jnp.float32)


def middle(sums, weight, cotangents, total_nodes):
    rows, width = cotangents[0].shape
    blocks = len(cotangents)
    size = width // (2 * blocks)
    return pl.pallas_call(
        functools.partial(middle_kernel, blocks=blocks, scale=1.0 / math.sqrt(total_nodes)),
        out_shape=[
            jax.ShapeDtypeStruct((rows, width), jnp.bfloat16),
            jax.ShapeDtypeStruct((blocks * width + 2 * size, rows), jnp.bfloat16),
            jax.ShapeDtypeStruct((size, width), jnp.float32),
            jax.ShapeDtypeStruct((size, width), jnp.float32),
        ],
        in_specs=[pl.BlockSpec(memory_space=pltpu.VMEM)] * (2 * blocks + 1),
        out_specs=[pl.BlockSpec(memory_space=pltpu.VMEM)] * 4,
        scratch_shapes=[pltpu.VMEM((width, width), jnp.float32)],
        compiler_params=pltpu.CompilerParams(vmem_limit_bytes=12 * mib),
        cost_estimate=pl.CostEstimate(
            flops=10 * blocks * rows * width * width,
            bytes_accessed=2 * (blocks * blocks + 2 * blocks + 4) * rows * width,
            transcendentals=blocks * rows * width,
        ),
        name="middle",
    )(*sums, weight, *cotangents)


def backward_kernel(dense_ref, own_ref, sibling_ref, *refs, outputs, row_count):
    out_refs, (depth, sems) = refs[:-2], refs[-2:]
    count = lax.axis_size("col")
    width, rows = depth.shape[0], own_ref.shape[1]
    wide = dense_ref.shape[1] // row_count
    col = lax.axis_index("col")
    copies = []
    for index in range(count):
        block = pl.ds(index // 2 * width, width)
        along = pl.ds(pl.multiple_of((col ^ index) * rows, rows), rows)
        source = sibling_ref if index % 2 else own_ref
        copy = pltpu.make_async_copy(source.at[block], depth.at[:, along], sems.at[index])
        copy.start()
        copies.append(copy)
    for copy in copies:
        copy.wait()
    place = ring_place(lax.axis_index("row"), row_count)
    for offset in sorted({offset for output in outputs for offset, _, _ in output}):
        along = pl.ds(pl.multiple_of(ring_row(place + offset, row_count) * wide, wide), wide)
        part = jnp.dot(depth[...], dense_ref[:, along], preferred_element_type=jnp.float32).astype(jnp.bfloat16)
        for output, out_ref in zip(outputs, out_refs):
            start = 0
            for other, first, high in output:
                if other == offset:
                    out_ref[start : start + high, :] = part[first : first + high, :]
                start += high


def backward_product(dense, own, sibling, width, outputs, row_count, col_count):
    high, deep = dense.shape
    wide = deep // row_count
    offsets = {offset for output in outputs for offset, _, _ in output}
    cell = ((high, deep), jnp.bfloat16)
    depth = ((width, high), jnp.bfloat16)
    out = ((len(offsets), width, wide), jnp.float32)
    return pl.pallas_call(
        functools.partial(backward_kernel, outputs=outputs, row_count=row_count),
        out_shape=[
            jax.ShapeDtypeStruct((sum(rows for _, _, rows in output), wide), jnp.bfloat16) for output in outputs
        ],
        in_specs=[pl.BlockSpec(memory_space=pltpu.VMEM)] + [pl.BlockSpec(memory_space=pl.ANY)] * 2,
        out_specs=[pl.BlockSpec(memory_space=pltpu.VMEM)] * len(outputs),
        scratch_shapes=[pltpu.VMEM(*depth), pltpu.SemaphoreType.DMA((col_count,))],
        compiler_params=pltpu.CompilerParams(vmem_limit_bytes=scratch_bytes(cell, depth, out) + 6 * mib),
        cost_estimate=pl.CostEstimate(
            flops=2 * high * wide * width, bytes_accessed=2 * wide * len(offsets) * width, transcendentals=0
        ),
        name="backward_product",
    )(dense, own, sibling)


def finish_kernel(*refs, parts):
    part_refs, chunk_refs, (features_ref, weight_ref) = refs[:parts], refs[parts:-2], refs[-2:]
    total = part_refs[0][...].astype(jnp.float32)
    for part_ref in part_refs[1:]:
        total += part_ref[...].astype(jnp.float32)
    features_ref[...] = total.astype(jnp.bfloat16).T
    rows = chunk_refs[0].shape[0]
    col = lax.axis_index("col")
    for partner, chunk_ref in enumerate(chunk_refs):
        weight_ref[pl.ds(pl.multiple_of((col ^ partner) * rows, rows), rows), :] = chunk_ref[...]


def finish(parts, chunks):
    width, rows = parts[0].shape
    return pl.pallas_call(
        functools.partial(finish_kernel, parts=len(parts)),
        out_shape=[
            jax.ShapeDtypeStruct((rows, width), jnp.bfloat16),
            jax.ShapeDtypeStruct((width, width), jnp.float32),
        ],
        in_specs=[pl.BlockSpec(memory_space=pltpu.VMEM)] * (len(parts) + len(chunks)),
        out_specs=[pl.BlockSpec(memory_space=pltpu.VMEM)] * 2,
        compiler_params=pltpu.CompilerParams(vmem_limit_bytes=8 * mib),
        cost_estimate=pl.CostEstimate(
            flops=len(parts) * rows * width, bytes_accessed=2 * (len(parts) + 5) * rows * width, transcendentals=0
        ),
        name="finish",
    )(*parts, *chunks)


def around(value, step):
    count = lax.axis_size("row")
    order = list(range(0, count, 2)) + list(range(count - 1, 0, -2))
    return lax.ppermute(value, "row", [(order[i], order[(i + step) % count]) for i in range(count)])


def swapped(value, axis, partner):
    return lax.ppermute(value, axis, [(i, i ^ partner) for i in range(lax.axis_size(axis))])


def gathered_shards(own, beside):
    count = lax.axis_size("row")
    rows = own.shape[0]
    half = rows // 2
    shards = [(((0, 0, 0, rows),), own)]
    if count == 8:
        far_up, far_down, up, down = (around(own, step) for step in (2, -2, 1, -1))
        for offset, array in ((-2, far_up), (2, far_down), (-1, up), (1, down)):
            shards.append((((offset, 0, 0, rows),), array))
        far_up, far_down, up, down, beside = lax.optimization_barrier((far_up, far_down, up, down, beside))
        up = around(jnp.concatenate([up, far_up[:half]]), 2)
        down = around(jnp.concatenate([down, far_down[half:]]), -2)
        shards.append((((-3, 0, 0, rows), (-4, 0, rows, half)), up))
        shards.append((((3, 0, 0, rows), (4, half, rows, half)), down))
        return shards, beside
    up = down = own
    for step in range(1, count // 2 + 1):
        up = around(up, 1)
        shards.append((((-step, 0, 0, rows),), up))
        if step < count // 2:
            down = around(down, -1)
            shards.append((((step, 0, 0, rows),), down))
        if step == 1:
            up, down, beside = lax.optimization_barrier((up, down, beside))
    return shards, beside


def added(first, second, at=0):
    spare = first.shape[0] - at - second.shape[0]
    second = jnp.pad(second.astype(jnp.float32), ((at, spare), (0, 0)))
    return (first.astype(jnp.float32) + second).astype(jnp.bfloat16)


def partners_sum(values):
    while len(values) > 1:
        values = [values[i] + values[i + 1] for i in range(0, len(values), 2)]
    return values[0]


def scattered_sums(dense, own, sibling, chunk):
    row_count, col_count = lax.axis_size("row"), lax.axis_size("col")
    width = chunk.shape[1]
    half = width // 2
    reach = row_count // 2

    def strips(cell, outputs):
        return backward_product(cell, own, sibling, width, outputs, row_count, col_count)

    def given_to_column(chunk):
        return [chunk] + [swapped(chunk, "col", partner) for partner in range(1, col_count)]

    if row_count == 8:
        far = strips(dense, (((3, 0, width), (4, 0, half)), ((-3, 0, width), (4, half, half))))
        far, cell = lax.optimization_barrier((far, dense))
        up, down = around(far[0], 2), around(far[1], -2)
        others = [swapped(chunk, "row", partner) for partner in (2, 4, 6)]
        up, down, others = lax.optimization_barrier((up, down, others))
        above, below, above_far, below_far, mine = strips(
            cell, tuple(((offset, 0, width),) for offset in (1, -1, 2, -2, 0))
        )
        above_far, below_far = added(above_far, up[width:]), added(below_far, down[width:], half)
        above, below = added(above, up[:width]), added(below, down[:width])
        parts = [mine, around(above_far, 2), around(below_far, -2), around(above, 1), around(below, -1)]
        return parts, given_to_column(partners_sum([chunk] + others))
    (far,) = strips(dense, (((reach, 0, width),),))
    far, cell = lax.optimization_barrier((far, dense))
    up, down = around(far, 1), None
    offsets = tuple(sign * step for step in range(reach - 1, 0, -1) for sign in (1, -1)) + (0,)
    *rest, mine = strips(cell, tuple(((offset, 0, width),) for offset in offsets))
    for step in range(reach - 1):
        above, below = rest[2 * step : 2 * step + 2]
        up = around(added(above, up), 1)
        down = around(below if down is None else added(below, down), -1)
    for bit in range(1, (row_count - 1).bit_length()):
        chunk = chunk + swapped(chunk, "row", 1 << bit)
    return [mine, up, down], given_to_column(chunk)


def per_device(features, weight, adj_tiles, tile_rows, tile_cols, tile_counts, out_grad):
    node_rows, width = features.shape
    capacity, side = adj_tiles.shape[2:4]
    tiles = adj_tiles.reshape(capacity, side, side)
    rows = tile_rows.reshape(capacity)
    cols = tile_cols.reshape(capacity)
    count = tile_counts.reshape(1)
    row_count = lax.axis_size("row")
    col_count = lax.axis_size("col")
    per_strip = node_rows // side
    dense = build_dense(rows, cols, count, tiles, col_count * per_strip, row_count * per_strip, per_strip)
    cotangents = [out_grad] + [swapped(out_grad, "col", partner) for partner in range(2, col_count, 2)]
    shards, (dense, cotangents) = gathered_shards(features, (dense, cotangents))

    for_sibling = forward_product(dense, shards, 1, row_count, col_count)
    for_sibling, cell = lax.optimization_barrier((for_sibling, dense))
    sums = added(forward_product(cell, shards, 0, row_count, col_count), swapped(for_sibling, "col", 1))
    sums = [sums] + [swapped(sums, "col", partner) for partner in range(2, col_count, 2)]
    activations, message, chunk, sent = middle(sums, weight, cotangents, node_rows * row_count * col_count)

    sibling = swapped(message, "col", 1)
    across = swapped(chunk, "row", 1)
    across_sibling = lax.ppermute(
        sent,
        ("row", "col"),
        [(r * col_count + c, (r ^ 1) * col_count + (c ^ 1)) for r in range(row_count) for c in range(col_count)],
    )
    message, sibling, across, across_sibling = lax.optimization_barrier((message, sibling, across, across_sibling))
    size = chunk.shape[0]
    high, low = sibling[-2 * size : -size], sibling[-size:]
    chunk = (chunk + (high.astype(jnp.float32) + low.astype(jnp.float32))) + (across + across_sibling)

    parts, chunks = scattered_sums(dense, message, sibling, chunk)
    grad_features, grad_weight = finish(parts, chunks)
    return (activations, grad_features, grad_weight)


def solution(mesh):
    placed = (
        P(("row", "col"), None),
        P(),
        P("row", "col", None, None, None),
        P("row", "col", None),
        P("row", "col", None),
        P("row", "col"),
        P(("row", "col"), None),
    )
    return jax.shard_map(
        per_device,
        mesh=mesh,
        in_specs=placed,
        out_specs=(P(("row", "col"), None), P(("row", "col"), None), P()),
        check_vma=False,
    )
```

time: 80.5 us -> 80.4 us (level)
  Pallas kernels: 10.1 us -> 8.74 us
    ppermute x15 -> x11, waiting for transfers between devices: 25.9 us -> 22.9 us  [swapped(): lax.ppermute(value, axis, [(i, i ^ partner) for i in range(lax.axis_size(...]
    ppermute x14 -> x12, waiting for transfers between devices: 12.4 us -> 15.2 us  [around(): lax.ppermute(value, 'row', [(order[i], order[(i + step) % count]) for i i...]
    ppermute x0 -> x1, starting transfers between devices: none -> 1.78 us  [per_device(): lax.ppermute(sent, ('row', 'col'), [(r * col_count + c, (r ^ 1) * col_cou...]
    pallas_call x1, Pallas kernels: 4.93 us -> 3.6 us  [build_dense(): pl.pallas_call(functools.partial(build_kernel, blocks=blocks, steps=steps...]
    ppermute x15 -> x11, starting transfers between devices: 12 us -> 10.8 us  [swapped(): lax.ppermute(value, axis, [(i, i ^ partner) for i in range(lax.axis_size(...]
    ppermute x14 -> x12, starting transfers between devices: 17.4 us -> 17.3 us  [around(): lax.ppermute(value, 'row', [(order[i], order[(i + step) % count]) for i i...]
  transfers between devices with their start and end apart: 29 -> 24, of which waited for: 15 -> 14; matrix products, arithmetic and copies ran while one was open for 0% -> 0% of each run, Pallas kernels for 9% -> 7%
where the time goes in v5:
time: 80.4 us; the launch traced here: 80.3 us
  waiting for transfers between devices  38.6 us (48%)
  starting transfers between devices  29.9 us (37%)
  Pallas kernels  8.74 us (11%)
  between operations  1.49 us (2%)
  local copies, waits for them, and re-layouts  1.39 us (2%)
    ppermute x11, waiting for transfers between devices, swapped(): lax.ppermute(value, axis, [(i, i ^ partner) for i in range(lax.axis_size(...  22.9 us
    ppermute x12, starting transfers between devices, around(): lax.ppermute(value, 'row', [(order[i], order[(i + step) % count]) for i i...  17.3 us
    ppermute x12, waiting for transfers between devices, around(): lax.ppermute(value, 'row', [(order[i], order[(i + step) % count]) for i i...  15.2 us
    ppermute x11, starting transfers between devices, swapped(): lax.ppermute(value, axis, [(i, i ^ partner) for i in range(lax.axis_size(...  10.8 us
    pallas_call x1, Pallas kernels, build_dense(): pl.pallas_call(functools.partial(build_kernel, blocks=blocks, steps=steps...  3.6 us
    ppermute x1, starting transfers between devices, per_device(): lax.ppermute(sent, ('row', 'col'), [(r * col_count + c, (r ^ 1) * col_cou...  1.78 us
    pallas_call x2, Pallas kernels, backward_product(): pl.pallas_call(functools.partial(backward_kernel, outputs=outputs, row_co...  1.71 us
  transfers between devices with their start and end apart: 24, of which 14 were waited for; matrix products, arithmetic and copies ran while one was open for 0% of the time, Pallas kernels for 7%

profile of v5, /device:TPU:0, one launch (start us, length us, event | category | flops | bytes accessed | tf_op | source)
XLA Modules:
  0.0 80.3 jit_solution(4739407691636181690)
XLA Ops:
  0.6 0.0 copy-start
  0.6 4.1 %collective-permute-start = (bf16[256,256]{1,0:T(8,128)(2,1)}, bf16[256,256]{1,0:T(8,128)(2,1)S(1)}, u32[]{:S(2)}, u32[]{:S(2)}) collective-permute-start(bf16[256,256]{1,0:T(8,128)(2,1)} %refs_0_.3), channel_id=1, source_target_pairs={{0,16},{8,24},{16,28},{24,20},{28,12},{20,4},{12,0},{4,8},{1,17},{... | collective-permute-start | bytes 393224 | tf_op jit(solution)/shard_map/ppermute | solution.py:311
  4.7 0.0 collective-permute-start.1
  4.7 1.9 %collective-permute-start.2 = (bf16[256,256]{1,0:T(8,128)(2,1)}, bf16[256,256]{1,0:T(8,128)(2,1)S(1)}, u32[]{:S(2)}, u32[]{:S(2)}) collective-permute-start(bf16[256,256]{1,0:T(8,128)(2,1)} %refs_0_.3), channel_id=1, source_target_pairs={{0,8},{8,16},{16,24},{24,28},{28,20},{20,12},{12,4},{4,0},{1,9},{9... | collective-permute-start | bytes 393224 | tf_op jit(solution)/shard_map/ppermute | solution.py:311
  6.6 0.1 collective-permute-start.3
  6.8 1.8 %collective-permute-start.4 = (bf16[256,256]{1,0:T(8,128)(2,1)}, bf16[256,256]{1,0:T(8,128)(2,1)S(1)}, u32[]{:S(2)}, u32[]{:S(2)}) collective-permute-start(bf16[256,256]{1,0:T(8,128)(2,1)} %refs_3_), channel_id=1, source_target_pairs={{0,2},{1,3},{2,0},{3,1},{4,6},{5,7},{6,4},{7,5},{8,10},{9,11},{10,... | collective-permute-start | bytes 393224 | tf_op jit(solution)/shard_map/ppermute | solution.py:315
  9.2 0.0 copy-start.1
  9.2 0.7 copy-done.1
  9.9 0.7 copy-done.2
  10.6 3.6 %build_dense.1.dense_ref = bf16[1024,2048]{1,0:T(8,128)(2,1)S(1)} custom-call(s32[256]{0:T(256)S(1)} %bitcast.5, s32[256]{0:T(256)S(1)} %bitcast.6, s32[1]{0:T(128)} %bitcast.4.count_ref, bf16[256,128,128]{2,1,0:T(8,128)(2,1)} %bitcast.7), custom_call_target="tpu_custom_call" | custom-call | flops 4194304 | bytes 12582912 | tf_op jit(solution)/shard_map/build_dense/pallas_call | solution.py:85
  14.2 0.0 copy-start.3
  14.2 0.0 copy-start.4
  14.2 0.0 collective-permute-done.refs_1_
  14.2 0.8 %collective-permute-done.1.refs_2_ = bf16[256,256]{1,0:T(8,128)(2,1)S(1)} collective-permute-done((bf16[256,256]{1,0:T(8,128)(2,1)}, bf16[256,256]{1,0:T(8,128)(2,1)S(1)}, u32[]{:S(2)}, u32[]{:S(2)}) %collective-permute-start.1) | collective-permute-done | bytes 131104 | tf_op jit(solution)/shard_map/ppermute | solution.py:311
  15.1 0.0 collective-permute-done.2.refs_3_
  15.1 0.4 collective-permute-done.3.refs_4_
  15.4 0.0 collective-permute-done.4.refs_4_
  15.5 1.9 %collective-permute-start.5 = (bf16[384,256]{1,0:T(8,128)(2,1)S(1)}, bf16[384,256]{1,0:T(8,128)(2,1)S(1)}, u32[]{:S(2)}, u32[]{:S(2)}) collective-permute-start(bf16[384,256]{1,0:T(8,128)(2,1)S(1)} %pad_maximum_fusion), channel_id=1, source_target_pairs={{0,16},{8,24},{16,28},{24,20},{28,12},{20,4},{12,0},{4,8},{1,17},{... | collective-permute-start | bytes 589832 | tf_op jit(solution)/shard_map/ppermute | solution.py:311
  17.4 1.1 %collective-permute-start.6 = (bf16[384,256]{1,0:T(8,128)(2,1)S(1)}, bf16[384,256]{1,0:T(8,128)(2,1)S(1)}, u32[]{:S(2)}, u32[]{:S(2)}) collective-permute-start(bf16[384,256]{1,0:T(8,128)(2,1)S(1)} %pad_maximum_fusion.1), channel_id=1, source_target_pairs={{0,12},{8,4},{16,0},{24,8},{28,16},{20,24},{12,28},{4,20},{1,13},{... | collective-permute-start | bytes 589832 | tf_op jit(solution)/shard_map/ppermute | solution.py:311
  18.5 4.2 %collective-permute-done.5.refs_5_ = bf16[384,256]{1,0:T(8,128)(2,1)S(1)} collective-permute-done((bf16[384,256]{1,0:T(8,128)(2,1)S(1)}, bf16[384,256]{1,0:T(8,128)(2,1)S(1)}, u32[]{:S(2)}, u32[]{:S(2)}) %collective-permute-start.5) | collective-permute-done | bytes 196640 | tf_op jit(solution)/shard_map/ppermute | solution.py:311
  22.8 5.8 %collective-permute-done.6.refs_6_ = bf16[384,256]{1,0:T(8,128)(2,1)S(1)} collective-permute-done((bf16[384,256]{1,0:T(8,128)(2,1)S(1)}, bf16[384,256]{1,0:T(8,128)(2,1)S(1)}, u32[]{:S(2)}, u32[]{:S(2)}) %collective-permute-start.6) | collective-permute-done | bytes 196640 | tf_op jit(solution)/shard_map/ppermute | solution.py:311
  28.6 0.0 copy-done
  28.6 0.8 forward_product.2
  29.4 0.1 collective-permute-start.7
  29.5 0.8 forward_product.3
  30.3 0.7 collective-permute-done.7
  31.0 0.1 add_convert_fusion.refs_0_
  31.1 2.5 %collective-permute-start.8 = (bf16[512,256]{1,0:T(8,128)(2,1)S(1)}, bf16[512,256]{1,0:T(8,128)(2,1)S(1)}, u32[]{:S(2)}, u32[]{:S(2)}) collective-permute-start(bf16[512,256]{1,0:T(8,128)(2,1)S(1)} %add_convert_fusion.refs_0_), channel_id=1, source_target_pairs={{0,2},{1,3},{2,0},{3,1},{4,6},{5,7},{6,4},{7,5},{8,10},{9,11},{10,... | collective-permute-start | bytes 786440 | tf_op jit(solution)/shard_map/ppermute | solution.py:315
  33.5 6.6 %collective-permute-done.8.refs_1_ = bf16[512,256]{1,0:T(8,128)(2,1)S(1)} collective-permute-done((bf16[512,256]{1,0:T(8,128)(2,1)S(1)}, bf16[512,256]{1,0:T(8,128)(2,1)S(1)}, u32[]{:S(2)}, u32[]{:S(2)}) %collective-permute-start.8) | collective-permute-done | bytes 262176 | tf_op jit(solution)/shard_map/ppermute | solution.py:315
  40.1 0.0 copy-done.3
  40.1 1.0 %middle.1 = (bf16[256,256]{1,0:T(8,128)(2,1)}, bf16[640,256]{1,0:T(8,128)(2,1)S(1)}, f32[64,256]{1,0:T(8,128)S(1)}, f32[64,256]{1,0:T(8,128)S(1)}) custom-call(bf16[512,256]{1,0:T(8,128)(2,1)S(1)} %add_convert_fusion.refs_0_, bf16[512,256]{1,0:T(8,128)(2,1)S(1)} %collective-permute-done.8.refs_1_, bf16[256,256]{1,0:T(8,128)(2,1)S(1)} %copy-done.3, ...), custom_call_target="tpu_custom_call" | custom-call | flops 335544320 | bytes 1572864 | tf_op jit(solution)/shard_map/middle/pallas_call | solution.py:206
  41.2 0.0 collective-permute-start.9
  41.2 0.1 collective-permute-start.10
  41.3 1.8 %collective-permute-start.11 = (f32[64,256]{1,0:T(8,128)S(1)}, f32[64,256]{1,0:T(8,128)S(1)}, u32[]{:S(2)}, u32[]{:S(2)}) collective-permute-start(f32[64,256]{1,0:T(8,128)S(1)} %get-tuple-element.49), channel_id=1, source_target_pairs={{0,5},{1,4},{2,7},{3,6},{4,1},{5,0},{6,3},{7,2},{8,13},{9,12},{10,... | collective-permute-start | bytes 196616 | tf_op jit(solution)/shard_map/ppermute | solution.py:418
  43.1 3.1 %collective-permute-done.10 = f32[64,256]{1,0:T(8,128)S(1)} collective-permute-done((f32[64,256]{1,0:T(8,128)S(1)}, f32[64,256]{1,0:T(8,128)S(1)}, u32[]{:S(2)}, u32[]{:S(2)}) %collective-permute-start.10) | collective-permute-done | bytes 65568 | tf_op jit(solution)/shard_map/ppermute | solution.py:315
  46.2 0.5 collective-permute-done.11
  46.7 0.0 collective-permute-done.9.sibling_ref
  46.7 0.7 backward_product.2
  47.4 0.1 collective-permute-start.12
  47.5 2.9 %collective-permute-start.13 = (bf16[384,256]{1,0:T(8,128)(2,1)S(1)}, bf16[384,256]{1,0:T(8,128)(2,1)S(1)}, u32[]{:S(2)}, u32[]{:S(2)}) collective-permute-start(bf16[384,256]{1,0:T(8,128)(2,1)S(1)} %get-tuple-element.58), channel_id=1, source_target_pairs={{0,12},{8,4},{16,0},{24,8},{28,16},{20,24},{12,28},{4,20},{1,13},{... | collective-permute-start | bytes 589832 | tf_op jit(solution)/shard_map/ppermute | solution.py:311
  50.4 0.1 collective-permute-start.14
  50.5 2.0 %collective-permute-start.15 = (f32[64,256]{1,0:T(8,128)S(1)}, f32[64,256]{1,0:T(8,128)S(1)}, u32[]{:S(2)}, u32[]{:S(2)}) collective-permute-start(f32[64,256]{1,0:T(8,128)S(1)} %add_add_fusion.1), channel_id=1, source_target_pairs={{0,16},{4,20},{8,24},{12,28},{16,0},{20,4},{24,8},{28,12},{1,17},{... | collective-permute-start | bytes 196616 | tf_op jit(solution)/shard_map/ppermute | solution.py:315
  52.5 2.4 %collective-permute-start.16 = (f32[64,256]{1,0:T(8,128)S(1)}, f32[64,256]{1,0:T(8,128)S(1)}, u32[]{:S(2)}, u32[]{:S(2)}) collective-permute-start(f32[64,256]{1,0:T(8,128)S(1)} %add_add_fusion.1), channel_id=1, source_target_pairs={{0,24},{4,28},{8,16},{12,20},{16,8},{20,12},{24,0},{28,4},{1,25},{... | collective-permute-start | bytes 196616 | tf_op jit(solution)/shard_map/ppermute | solution.py:315
  54.9 1.0 %backward_product.3 = (bf16[256,256]{1,0:T(8,128)(2,1)S(1)}, bf16[256,256]{1,0:T(8,128)(2,1)S(1)}, bf16[256,256]{1,0:T(8,128)(2,1)S(1)}, bf16[256,256]{1,0:T(8,128)(2,1)S(1)}, bf16[256,256]{1,0:T(8,128)(2,1)S(1)}) custom-call(bf16[1024,2048]{1,0:T(8,128)(2,1)S(1)} %build_dense.1.dense_ref, bf16[640,256]{1,0:T(8,128)(2,1)S(1)} %get-tuple-element.50.own_ref, ...), custom_call_target="tpu_custom_call" | custom-call | flops 134217728 | bytes 655360 | tf_op jit(solution)/shard_map/backward_product/pallas_call | solution.py:262
  55.9 4.5 %collective-permute-done.14 = f32[64,256]{1,0:T(8,128)S(1)} collective-permute-done((f32[64,256]{1,0:T(8,128)S(1)}, f32[64,256]{1,0:T(8,128)S(1)}, u32[]{:S(2)}, u32[]{:S(2)}) %collective-permute-start.14) | collective-permute-done | bytes 65568 | tf_op jit(solution)/shard_map/ppermute | solution.py:315
  60.3 4.3 %collective-permute-done.15 = f32[64,256]{1,0:T(8,128)S(1)} collective-permute-done((f32[64,256]{1,0:T(8,128)S(1)}, f32[64,256]{1,0:T(8,128)S(1)}, u32[]{:S(2)}, u32[]{:S(2)}) %collective-permute-start.15) | collective-permute-done | bytes 65568 | tf_op jit(solution)/shard_map/ppermute | solution.py:315
  64.6 0.0 collective-permute-done.16
  64.6 0.0 collective-permute-done.12
  64.6 0.0 collective-permute-done.13
  64.7 0.1 collective-permute-start.21
  64.8 1.8 %collective-permute-start.22 = (f32[64,256]{1,0:T(8,128)S(1)}, f32[64,256]{1,0:T(8,128)S(1)}, u32[]{:S(2)}, u32[]{:S(2)}) collective-permute-start(f32[64,256]{1,0:T(8,128)S(1)} %add_add_fusion.refs_5_), channel_id=1, source_target_pairs={{0,2},{1,3},{2,0},{3,1},{4,6},{5,7},{6,4},{7,5},{8,10},{9,11},{10,... | collective-permute-start | bytes 196616 | tf_op jit(solution)/shard_map/ppermute | solution.py:315
  66.6 1.0 %collective-permute-start.17 = (bf16[256,256]{1,0:T(8,128)(2,1)S(1)}, bf16[256,256]{1,0:T(8,128)(2,1)S(1)}, u32[]{:S(2)}, u32[]{:S(2)}) collective-permute-start(bf16[256,256]{1,0:T(8,128)(2,1)S(1)} %add_convert_fusion.4), channel_id=1, source_target_pairs={{0,16},{8,24},{16,28},{24,20},{28,12},{20,4},{12,0},{4,8},{1,17},{... | collective-permute-start | bytes 393224 | tf_op jit(solution)/shard_map/ppermute | solution.py:311
  67.6 2.0 %collective-permute-start.18 = (bf16[256,256]{1,0:T(8,128)(2,1)S(1)}, bf16[256,256]{1,0:T(8,128)(2,1)S(1)}, u32[]{:S(2)}, u32[]{:S(2)}) collective-permute-start(bf16[256,256]{1,0:T(8,128)(2,1)S(1)} %add_convert_fusion.3), channel_id=1, source_target_pairs={{0,12},{8,4},{16,0},{24,8},{28,16},{20,24},{12,28},{4,20},{1,13},{... | collective-permute-start | bytes 393224 | tf_op jit(solution)/shard_map/ppermute | solution.py:311
  69.7 1.4 %collective-permute-start.19 = (bf16[256,256]{1,0:T(8,128)(2,1)S(1)}, bf16[256,256]{1,0:T(8,128)(2,1)S(1)}, u32[]{:S(2)}, u32[]{:S(2)}) collective-permute-start(bf16[256,256]{1,0:T(8,128)(2,1)S(1)} %add_convert_fusion.2), channel_id=1, source_target_pairs={{0,8},{8,16},{16,24},{24,28},{28,20},{20,12},{12,4},{4,0},{1,9},{9... | collective-permute-start | bytes 393224 | tf_op jit(solution)/shard_map/ppermute | solution.py:311
  71.1 0.0 collective-permute-done.21.refs_6_
  71.1 0.8 collective-permute-start.20
  71.9 0.0 collective-permute-done.22.refs_7_
  71.9 0.0 collective-permute-start.23
  71.9 3.7 %collective-permute-done.23.refs_8_ = f32[64,256]{1,0:T(8,128)S(1)} collective-permute-done((f32[64,256]{1,0:T(8,128)S(1)}, f32[64,256]{1,0:T(8,128)S(1)}, u32[]{:S(2)}, u32[]{:S(2)}) %collective-permute-start.23) | collective-permute-done | bytes 65568 | tf_op jit(solution)/shard_map/ppermute | solution.py:315
  75.6 0.2 collective-permute-done.17.refs_1_
  75.7 2.0 %collective-permute-done.18.refs_2_ = bf16[256,256]{1,0:T(8,128)(2,1)S(1)} collective-permute-done((bf16[256,256]{1,0:T(8,128)(2,1)S(1)}, bf16[256,256]{1,0:T(8,128)(2,1)S(1)}, u32[]{:S(2)}, u32[]{:S(2)}) %collective-permute-start.18) | collective-permute-done | bytes 131104 | tf_op jit(solution)/shard_map/ppermute | solution.py:311
  77.8 0.0 collective-permute-done.19.refs_3_
  77.8 1.7 %collective-permute-done.20.refs_4_ = bf16[256,256]{1,0:T(8,128)(2,1)S(1)} collective-permute-done((bf16[256,256]{1,0:T(8,128)(2,1)S(1)}, bf16[256,256]{1,0:T(8,128)(2,1)S(1)}, u32[]{:S(2)}, u32[]{:S(2)}) %collective-permute-start.20) | collective-permute-done | bytes 131104 | tf_op jit(solution)/shard_map/ppermute | solution.py:311
  79.5 0.8 %finish.1 = (bf16[256,256]{1,0:T(8,128)(2,1)}, f32[256,256]{1,0:T(8,128)}) custom-call(bf16[256,256]{1,0:T(8,128)(2,1)S(1)} %get-tuple-element.55.refs_0_, bf16[256,256]{1,0:T(8,128)(2,1)S(1)} %collective-permute-done.17.refs_1_, bf16[256,256]{1,0:T(8,128)(2,1)S(1)} %collective-permute-done.18.refs_2_, bf16[256,256]{1,0:T(8,128)(2,1)S(1)} %collective-permute-done.19.refs_3_, ...), custom_call_target="tpu_custom_call" | custom-call | flops 327680 | bytes 1310720 | tf_op jit(solution)/shard_map/finish/pallas_call | solution.py:292
  (14 shorter events, 0.2 us)
Async XLA Ops:
  0.6 28.0 %copy-start = (bf16[256,256]{1,0:T(8,128)(2,1)S(1)}, bf16[256,256]{1,0:T(8,128)(2,1)}, u32[]{:S(2)}) copy-start(bf16[256,256]{1,0:T(8,128)(2,1)} %refs_0_.3) | copy-start | bytes 393220
  0.6 13.6 %collective-permute-start = (bf16[256,256]{1,0:T(8,128)(2,1)}, bf16[256,256]{1,0:T(8,128)(2,1)S(1)}, u32[]{:S(2)}, u32[]{:S(2)}) collective-permute-start(bf16[256,256]{1,0:T(8,128)(2,1)} %refs_0_.3), channel_id=1, source_target_pairs={{0,16},{8,24},{16,28},{24,20},{28,12},{20,4},{12,0},{4,8},{1,17},{... | collective-permute-start | bytes 393224 | tf_op jit(solution)/shard_map/ppermute | solution.py:311
  4.7 10.3 %collective-permute-start.1 = (bf16[256,256]{1,0:T(8,128)(2,1)}, bf16[256,256]{1,0:T(8,128)(2,1)S(1)}, u32[]{:S(2)}, u32[]{:S(2)}) collective-permute-start(bf16[256,256]{1,0:T(8,128)(2,1)} %refs_0_.3), channel_id=1, source_target_pairs={{0,12},{8,4},{16,0},{24,8},{28,16},{20,24},{12,28},{4,20},{1,13},{... | collective-permute-start | bytes 393224 | tf_op jit(solution)/shard_map/ppermute | solution.py:311
  4.7 10.3 %collective-permute-start.2 = (bf16[256,256]{1,0:T(8,128)(2,1)}, bf16[256,256]{1,0:T(8,128)(2,1)S(1)}, u32[]{:S(2)}, u32[]{:S(2)}) collective-permute-start(bf16[256,256]{1,0:T(8,128)(2,1)} %refs_0_.3), channel_id=1, source_target_pairs={{0,8},{8,16},{16,24},{24,28},{28,20},{20,12},{12,4},{4,0},{1,9},{9... | collective-permute-start | bytes 393224 | tf_op jit(solution)/shard_map/ppermute | solution.py:311
  6.6 8.8 %collective-permute-start.3 = (bf16[256,256]{1,0:T(8,128)(2,1)}, bf16[256,256]{1,0:T(8,128)(2,1)S(1)}, u32[]{:S(2)}, u32[]{:S(2)}) collective-permute-start(bf16[256,256]{1,0:T(8,128)(2,1)} %refs_0_.3), channel_id=1, source_target_pairs={{0,4},{8,0},{16,8},{24,16},{28,24},{20,28},{12,20},{4,12},{1,5},{9... | collective-permute-start | bytes 393224 | tf_op jit(solution)/shard_map/ppermute | solution.py:311
  6.8 8.7 %collective-permute-start.4 = (bf16[256,256]{1,0:T(8,128)(2,1)}, bf16[256,256]{1,0:T(8,128)(2,1)S(1)}, u32[]{:S(2)}, u32[]{:S(2)}) collective-permute-start(bf16[256,256]{1,0:T(8,128)(2,1)} %refs_3_), channel_id=1, source_target_pairs={{0,2},{1,3},{2,0},{3,1},{4,6},{5,7},{6,4},{7,5},{8,10},{9,11},{10,... | collective-permute-start | bytes 393224 | tf_op jit(solution)/shard_map/ppermute | solution.py:315
  9.2 0.7 copy-start.1
  9.9 0.7 copy-start.2
  14.2 25.9 %copy-start.3 = (bf16[256,256]{1,0:T(8,128)(2,1)S(1)}, bf16[256,256]{1,0:T(8,128)(2,1)}, u32[]{:S(2)}) copy-start(bf16[256,256]{1,0:T(8,128)(2,1)} %refs_2_.1) | copy-start | bytes 393220
  14.2 25.9 %copy-start.4 = (bf16[256,256]{1,0:T(8,128)(2,1)S(1)}, bf16[256,256]{1,0:T(8,128)(2,1)}, u32[]{:S(2)}) copy-start(bf16[256,256]{1,0:T(8,128)(2,1)} %refs_3_) | copy-start | bytes 393220
  15.5 7.3 %collective-permute-start.5 = (bf16[384,256]{1,0:T(8,128)(2,1)S(1)}, bf16[384,256]{1,0:T(8,128)(2,1)S(1)}, u32[]{:S(2)}, u32[]{:S(2)}) collective-permute-start(bf16[384,256]{1,0:T(8,128)(2,1)S(1)} %pad_maximum_fusion), channel_id=1, source_target_pairs={{0,16},{8,24},{16,28},{24,20},{28,12},{20,4},{12,0},{4,8},{1,17},{... | collective-permute-start | bytes 589832 | tf_op jit(solution)/shard_map/ppermute | solution.py:311
  17.4 11.2 %collective-permute-start.6 = (bf16[384,256]{1,0:T(8,128)(2,1)S(1)}, bf16[384,256]{1,0:T(8,128)(2,1)S(1)}, u32[]{:S(2)}, u32[]{:S(2)}) collective-permute-start(bf16[384,256]{1,0:T(8,128)(2,1)S(1)} %pad_maximum_fusion.1), channel_id=1, source_target_pairs={{0,12},{8,4},{16,0},{24,8},{28,16},{20,24},{12,28},{4,20},{1,13},{... | collective-permute-start | bytes 589832 | tf_op jit(solution)/shard_map/ppermute | solution.py:311
  29.4 1.6 %collective-permute-start.7 = (bf16[512,256]{1,0:T(8,128)(2,1)S(1)}, bf16[512,256]{1,0:T(8,128)(2,1)S(1)}, u32[]{:S(2)}, u32[]{:S(2)}) collective-permute-start(bf16[512,256]{1,0:T(8,128)(2,1)S(1)} %forward_product.2), channel_id=1, source_target_pairs={{0,1},{1,0},{2,3},{3,2},{4,5},{5,4},{6,7},{7,6},{8,9},{9,8},{10,11... | collective-permute-start | bytes 786440 | tf_op jit(solution)/shard_map/ppermute | solution.py:315
  31.1 9.1 %collective-permute-start.8 = (bf16[512,256]{1,0:T(8,128)(2,1)S(1)}, bf16[512,256]{1,0:T(8,128)(2,1)S(1)}, u32[]{:S(2)}, u32[]{:S(2)}) collective-permute-start(bf16[512,256]{1,0:T(8,128)(2,1)S(1)} %add_convert_fusion.refs_0_), channel_id=1, source_target_pairs={{0,2},{1,3},{2,0},{3,1},{4,6},{5,7},{6,4},{7,5},{8,10},{9,11},{10,... | collective-permute-start | bytes 786440 | tf_op jit(solution)/shard_map/ppermute | solution.py:315
  41.2 5.5 %collective-permute-start.9 = (bf16[640,256]{1,0:T(8,128)(2,1)S(1)}, bf16[640,256]{1,0:T(8,128)(2,1)S(1)}, u32[]{:S(2)}, u32[]{:S(2)}) collective-permute-start(bf16[640,256]{1,0:T(8,128)(2,1)S(1)} %get-tuple-element.50.own_ref), channel_id=1, source_target_pairs={{0,1},{1,0},{2,3},{3,2},{4,5},{5,4},{6,7},{7,6},{8,9},{9,8},{10,11... | collective-permute-start | bytes 983048 | tf_op jit(solution)/shard_map/ppermute | solution.py:315
  41.2 5.0 %collective-permute-start.10 = (f32[64,256]{1,0:T(8,128)S(1)}, f32[64,256]{1,0:T(8,128)S(1)}, u32[]{:S(2)}, u32[]{:S(2)}) collective-permute-start(f32[64,256]{1,0:T(8,128)S(1)} %get-tuple-element.48), channel_id=1, source_target_pairs={{0,4},{4,0},{8,12},{12,8},{16,20},{20,16},{24,28},{28,24},{1,5},{5... | collective-permute-start | bytes 196616 | tf_op jit(solution)/shard_map/ppermute | solution.py:315
  41.3 5.4 %collective-permute-start.11 = (f32[64,256]{1,0:T(8,128)S(1)}, f32[64,256]{1,0:T(8,128)S(1)}, u32[]{:S(2)}, u32[]{:S(2)}) collective-permute-start(f32[64,256]{1,0:T(8,128)S(1)} %get-tuple-element.49), channel_id=1, source_target_pairs={{0,5},{1,4},{2,7},{3,6},{4,1},{5,0},{6,3},{7,2},{8,13},{9,12},{10,... | collective-permute-start | bytes 196616 | tf_op jit(solution)/shard_map/ppermute | solution.py:418
  47.4 17.2 %collective-permute-start.12 = (bf16[384,256]{1,0:T(8,128)(2,1)S(1)}, bf16[384,256]{1,0:T(8,128)(2,1)S(1)}, u32[]{:S(2)}, u32[]{:S(2)}) collective-permute-start(bf16[384,256]{1,0:T(8,128)(2,1)S(1)} %get-tuple-element.57), channel_id=1, source_target_pairs={{0,16},{8,24},{16,28},{24,20},{28,12},{20,4},{12,0},{4,8},{1,17},{... | collective-permute-start | bytes 589832 | tf_op jit(solution)/shard_map/ppermute | solution.py:311
  47.5 17.2 %collective-permute-start.13 = (bf16[384,256]{1,0:T(8,128)(2,1)S(1)}, bf16[384,256]{1,0:T(8,128)(2,1)S(1)}, u32[]{:S(2)}, u32[]{:S(2)}) collective-permute-start(bf16[384,256]{1,0:T(8,128)(2,1)S(1)} %get-tuple-element.58), channel_id=1, source_target_pairs={{0,12},{8,4},{16,0},{24,8},{28,16},{20,24},{12,28},{4,20},{1,13},{... | collective-permute-start | bytes 589832 | tf_op jit(solution)/shard_map/ppermute | solution.py:311
  50.4 9.9 %collective-permute-start.14 = (f32[64,256]{1,0:T(8,128)S(1)}, f32[64,256]{1,0:T(8,128)S(1)}, u32[]{:S(2)}, u32[]{:S(2)}) collective-permute-start(f32[64,256]{1,0:T(8,128)S(1)} %add_add_fusion.1), channel_id=1, source_target_pairs={{0,8},{4,12},{8,0},{12,4},{16,24},{20,28},{24,16},{28,20},{1,9},{5... | collective-permute-start | bytes 196616 | tf_op jit(solution)/shard_map/ppermute | solution.py:315
  50.5 14.1 %collective-permute-start.15 = (f32[64,256]{1,0:T(8,128)S(1)}, f32[64,256]{1,0:T(8,128)S(1)}, u32[]{:S(2)}, u32[]{:S(2)}) collective-permute-start(f32[64,256]{1,0:T(8,128)S(1)} %add_add_fusion.1), channel_id=1, source_target_pairs={{0,16},{4,20},{8,24},{12,28},{16,0},{20,4},{24,8},{28,12},{1,17},{... | collective-permute-start | bytes 196616 | tf_op jit(solution)/shard_map/ppermute | solution.py:315
  52.5 12.1 %collective-permute-start.16 = (f32[64,256]{1,0:T(8,128)S(1)}, f32[64,256]{1,0:T(8,128)S(1)}, u32[]{:S(2)}, u32[]{:S(2)}) collective-permute-start(f32[64,256]{1,0:T(8,128)S(1)} %add_add_fusion.1), channel_id=1, source_target_pairs={{0,24},{4,28},{8,16},{12,20},{16,8},{20,12},{24,0},{28,4},{1,25},{... | collective-permute-start | bytes 196616 | tf_op jit(solution)/shard_map/ppermute | solution.py:315
  64.7 6.4 %collective-permute-start.21 = (f32[64,256]{1,0:T(8,128)S(1)}, f32[64,256]{1,0:T(8,128)S(1)}, u32[]{:S(2)}, u32[]{:S(2)}) collective-permute-start(f32[64,256]{1,0:T(8,128)S(1)} %add_add_fusion.refs_5_), channel_id=1, source_target_pairs={{0,1},{1,0},{2,3},{3,2},{4,5},{5,4},{6,7},{7,6},{8,9},{9,8},{10,11... | collective-permute-start | bytes 196616 | tf_op jit(solution)/shard_map/ppermute | solution.py:315
  64.8 7.1 %collective-permute-start.22 = (f32[64,256]{1,0:T(8,128)S(1)}, f32[64,256]{1,0:T(8,128)S(1)}, u32[]{:S(2)}, u32[]{:S(2)}) collective-permute-start(f32[64,256]{1,0:T(8,128)S(1)} %add_add_fusion.refs_5_), channel_id=1, source_target_pairs={{0,2},{1,3},{2,0},{3,1},{4,6},{5,7},{6,4},{7,5},{8,10},{9,11},{10,... | collective-permute-start | bytes 196616 | tf_op jit(solution)/shard_map/ppermute | solution.py:315
  66.6 9.1 %collective-permute-start.17 = (bf16[256,256]{1,0:T(8,128)(2,1)S(1)}, bf16[256,256]{1,0:T(8,128)(2,1)S(1)}, u32[]{:S(2)}, u32[]{:S(2)}) collective-permute-start(bf16[256,256]{1,0:T(8,128)(2,1)S(1)} %add_convert_fusion.4), channel_id=1, source_target_pairs={{0,16},{8,24},{16,28},{24,20},{28,12},{20,4},{12,0},{4,8},{1,17},{... | collective-permute-start | bytes 393224 | tf_op jit(solution)/shard_map/ppermute | solution.py:311
  67.6 10.1 %collective-permute-start.18 = (bf16[256,256]{1,0:T(8,128)(2,1)S(1)}, bf16[256,256]{1,0:T(8,128)(2,1)S(1)}, u32[]{:S(2)}, u32[]{:S(2)}) collective-permute-start(bf16[256,256]{1,0:T(8,128)(2,1)S(1)} %add_convert_fusion.3), channel_id=1, source_target_pairs={{0,12},{8,4},{16,0},{24,8},{28,16},{20,24},{12,28},{4,20},{1,13},{... | collective-permute-start | bytes 393224 | tf_op jit(solution)/shard_map/ppermute | solution.py:311
  69.7 8.1 %collective-permute-start.19 = (bf16[256,256]{1,0:T(8,128)(2,1)S(1)}, bf16[256,256]{1,0:T(8,128)(2,1)S(1)}, u32[]{:S(2)}, u32[]{:S(2)}) collective-permute-start(bf16[256,256]{1,0:T(8,128)(2,1)S(1)} %add_convert_fusion.2), channel_id=1, source_target_pairs={{0,8},{8,16},{16,24},{24,28},{28,20},{20,12},{12,4},{4,0},{1,9},{9... | collective-permute-start | bytes 393224 | tf_op jit(solution)/shard_map/ppermute | solution.py:311
  71.1 8.4 %collective-permute-start.20 = (bf16[256,256]{1,0:T(8,128)(2,1)S(1)}, bf16[256,256]{1,0:T(8,128)(2,1)S(1)}, u32[]{:S(2)}, u32[]{:S(2)}) collective-permute-start(bf16[256,256]{1,0:T(8,128)(2,1)S(1)} %add_convert_fusion.1), channel_id=1, source_target_pairs={{0,4},{8,0},{16,8},{24,16},{28,24},{20,28},{12,20},{4,12},{1,5},{9... | collective-permute-start | bytes 393224 | tf_op jit(solution)/shard_map/ppermute | solution.py:311
  71.9 3.7 %collective-permute-start.23 = (f32[64,256]{1,0:T(8,128)S(1)}, f32[64,256]{1,0:T(8,128)S(1)}, u32[]{:S(2)}, u32[]{:S(2)}) collective-permute-start(f32[64,256]{1,0:T(8,128)S(1)} %add_add_fusion.refs_5_), channel_id=1, source_target_pairs={{0,3},{1,2},{2,1},{3,0},{4,7},{5,6},{6,5},{7,4},{8,11},{9,10},{10,... | collective-permute-start | bytes 196616 | tf_op jit(solution)/shard_map/ppermute | solution.py:315

commit v6 on v5

--- a/solution.py
+++ b/solution.py
@@ -18,10 +18,10 @@
     return sum(math.prod(shape) * jnp.dtype(kind).itemsize for shape, kind in shapes)
 
 
-def build_kernel(rows_ref, cols_ref, count_ref, tiles_ref, dense_ref, total, held, sems, *, blocks, steps):
+def build_kernel(list_ref, tiles_ref, dense_ref, total, held, sems, *, blocks, steps):
     side = tiles_ref.shape[1]
     first_block = pl.program_id(0) * blocks
-    count = count_ref[0]
+    count = list_ref[0] >> 16
     chunks = (count + chunk_tiles - 1) // chunk_tiles
 
     def fetch(index):
@@ -44,6 +44,16 @@
 
     lax.fori_loop(0, row_blocks, clear, 0)
 
+    def target(place):
+        code = list_ref[place]
+        col = (code & 255) - first_block
+        live = place < count
+        if steps > 1:
+            live = live & (col >= 0) & (col < blocks)
+            col = jnp.where(live, col, 0)
+        row = jnp.where(live, (code >> 8) & 255, row_blocks)
+        return row, col
+
     def chunk_step(index, carry):
         @pl.when(index + chunk_slots - 1 < chunks)
         def _():
@@ -51,17 +61,20 @@
 
         fetch(index).wait()
         slot = lax.rem(index, chunk_slots)
-        for lane in range(chunk_tiles):
-            place = index * chunk_tiles + lane
-            col = cols_ref[place] - first_block
-            live = place < count
-            if steps > 1:
-                live = live & (col >= 0) & (col < blocks)
-                col = jnp.where(live, col, 0)
-            row = jnp.where(live, rows_ref[place], row_blocks)
-            down = pl.ds(pl.multiple_of(row * side, side), side)
-            along = pl.ds(pl.multiple_of(col * side, side), side)
-            total[down, along] += held[slot, lane].astype(jnp.float32)
+        for lane in range(0, chunk_tiles, 2):
+            spots, olds, news = [], [], []
+            for place in (index * chunk_tiles + lane, index * chunk_tiles + lane + 1):
+                row, col = target(place)
+                spots.append((row, col))
+                olds.append(
+                    (pl.ds(pl.multiple_of(row * side, side), side), pl.ds(pl.multiple_of(col * side, side), side))
+                )
+            sums = [total[at] for at in olds]
+            tiles = [held[slot, lane + turn].astype(jnp.float32) for turn in range(2)]
+            same = (spots[0][0] == spots[1][0]) & (spots[0][1] == spots[1][1])
+            news = [sums[0] + tiles[0], sums[1] + tiles[1] + jnp.where(same, tiles[0], 0.0)]
+            for at, new in zip(olds, news):
+                total[at] = new
         return carry
 
     lax.fori_loop(0, chunks, chunk_step, 0)
@@ -74,7 +87,7 @@
     lax.fori_loop(0, row_blocks, round_block, 0)
 
 
-def build_dense(rows, cols, count, tiles, row_blocks, col_blocks, per_strip):
+def build_dense(packed, tiles, row_blocks, col_blocks, per_strip):
     capacity, side, _ = tiles.shape
     blocks = min(strips_per_step * per_strip, col_blocks)
     steps = col_blocks // blocks
@@ -86,7 +99,7 @@
         functools.partial(build_kernel, blocks=blocks, steps=steps),
         out_shape=jax.ShapeDtypeStruct((high, col_blocks * side), jnp.bfloat16),
         grid_spec=pltpu.PrefetchScalarGridSpec(
-            num_scalar_prefetch=3,
+            num_scalar_prefetch=1,
             grid=(steps,),
             in_specs=[pl.BlockSpec(memory_space=pltpu.HBM)],
             out_specs=pl.BlockSpec((high, wide), lambda i, *_: (0, i)),
@@ -103,7 +116,7 @@
             transcendentals=0,
         ),
         name="build_dense",
-    )(rows, cols, count, tiles)
+    )(packed, tiles)
 
 
 def ring_place(row, count):
@@ -163,7 +176,7 @@
 def middle_kernel(*refs, blocks, scale):
     sums, refs = refs[:blocks], refs[blocks:]
     weight_ref, refs = refs[0], refs[1:]
-    cotangent_refs, (act_ref, message_ref, chunk_ref, sent_ref, product) = refs[:blocks], refs[blocks:]
+    cotangent_refs, (act_ref, message_ref, chunk_ref, product) = refs[:blocks], refs[blocks:]
     weight = weight_ref[...]
     rows, width = act_ref.shape
     over_nodes = (((0,), (0,)), ((), ()))
@@ -196,7 +209,6 @@
     low = (sent - high.astype(jnp.float32)).astype(jnp.bfloat16)
     message_ref[pl.ds(blocks * width, size), :] = high
     message_ref[pl.ds(blocks * width + size, size), :] = low
-    sent_ref[...] = high.astype(jnp.float32) + low.astype(jnp.float32)
 
 
 def middle(sums, weight, cotangents, total_nodes):
@@ -209,10 +221,9 @@
             jax.ShapeDtypeStruct((rows, width), jnp.bfloat16),
             jax.ShapeDtypeStruct((blocks * width + 2 * size, rows), jnp.bfloat16),
             jax.ShapeDtypeStruct((size, width), jnp.float32),
-            jax.ShapeDtypeStruct((size, width), jnp.float32),
         ],
         in_specs=[pl.BlockSpec(memory_space=pltpu.VMEM)] * (2 * blocks + 1),
-        out_specs=[pl.BlockSpec(memory_space=pltpu.VMEM)] * 4,
+        out_specs=[pl.BlockSpec(memory_space=pltpu.VMEM)] * 3,
         scratch_shapes=[pltpu.VMEM((width, width), jnp.float32)],
         compiler_params=pltpu.CompilerParams(vmem_limit_bytes=12 * mib),
         cost_estimate=pl.CostEstimate(
@@ -224,7 +235,7 @@
     )(*sums, weight, *cotangents)
 
 
-def backward_kernel(dense_ref, own_ref, sibling_ref, *refs, outputs, row_count):
+def backward_kernel(dense_ref, own_ref, sibling_ref, chunk_ref, *refs, outputs, row_count):
     out_refs, (depth, sems) = refs[:-2], refs[-2:]
     count = lax.axis_size("col")
     width, rows = depth.shape[0], own_ref.shape[1]
@@ -238,48 +249,87 @@
         copy = pltpu.make_async_copy(source.at[block], depth.at[:, along], sems.at[index])
         copy.start()
         copies.append(copy)
+    size = chunk_ref.shape[0]
+    from_sibling = count // 2 * width
+    high, low = (sibling_ref[pl.ds(from_sibling + turn * size, size), :].astype(jnp.float32) for turn in range(2))
+    terms = (chunk_ref[...] + (high + low)).astype(jnp.bfloat16)
     for copy in copies:
         copy.wait()
     place = ring_place(lax.axis_index("row"), row_count)
-    for offset in sorted({offset for output in outputs for offset, _, _ in output}):
-        along = pl.ds(pl.multiple_of(ring_row(place + offset, row_count) * wide, wide), wide)
-        part = jnp.dot(depth[...], dense_ref[:, along], preferred_element_type=jnp.float32).astype(jnp.bfloat16)
-        for output, out_ref in zip(outputs, out_refs):
-            start = 0
-            for other, first, high in output:
-                if other == offset:
-                    out_ref[start : start + high, :] = part[first : first + high, :]
-                start += high
-
-
-def backward_product(dense, own, sibling, width, outputs, row_count, col_count):
+    for (offset, tail), out_ref in zip(outputs, out_refs):
+        if tail != "terms alone":
+            along = pl.ds(pl.multiple_of(ring_row(place + offset, row_count) * wide, wide), wide)
+            part = jnp.dot(depth[...], dense_ref[:, along], preferred_element_type=jnp.float32)
+            out_ref[pl.ds(0, width), :] = part.astype(jnp.bfloat16)
+        if tail == "terms alone":
+            out_ref[...] = terms
+        elif tail == "terms":
+            out_ref[pl.ds(width, size), :] = terms
+        elif tail == "zeros":
+            out_ref[pl.ds(width, size), :] = jnp.zeros_like(terms)
+
+
+def backward_product(dense, own, sibling, chunk, outputs, row_count, col_count):
     high, deep = dense.shape
+    size, width = chunk.shape
     wide = deep // row_count
-    offsets = {offset for output in outputs for offset, _, _ in output}
+    heights = {"": width, "terms alone": size, "terms": width + size, "zeros": width + size}
     cell = ((high, deep), jnp.bfloat16)
     depth = ((width, high), jnp.bfloat16)
-    out = ((len(offsets), width, wide), jnp.float32)
+    out = ((len(outputs), width + size, wide), jnp.float32)
     return pl.pallas_call(
         functools.partial(backward_kernel, outputs=outputs, row_count=row_count),
-        out_shape=[
-            jax.ShapeDtypeStruct((sum(rows for _, _, rows in output), wide), jnp.bfloat16) for output in outputs
-        ],
-        in_specs=[pl.BlockSpec(memory_space=pltpu.VMEM)] + [pl.BlockSpec(memory_space=pl.ANY)] * 2,
+        out_shape=[jax.ShapeDtypeStruct((heights[tail], wide), jnp.bfloat16) for _, tail in outputs],
+        in_specs=[pl.BlockSpec(memory_space=pltpu.VMEM)] * 4,
         out_specs=[pl.BlockSpec(memory_space=pltpu.VMEM)] * len(outputs),
         scratch_shapes=[pltpu.VMEM(*depth), pltpu.SemaphoreType.DMA((col_count,))],
         compiler_params=pltpu.CompilerParams(vmem_limit_bytes=scratch_bytes(cell, depth, out) + 6 * mib),
         cost_estimate=pl.CostEstimate(
-            flops=2 * high * wide * width, bytes_accessed=2 * wide * len(offsets) * width, transcendentals=0
+            flops=2 * high * wide * width, bytes_accessed=2 * wide * len(outputs) * width, transcendentals=0
         ),
         name="backward_product",
-    )(dense, own, sibling)
+    )(dense, own, sibling, chunk)
+
+
+def terms_kernel(*refs, offsets, first_rows):
+    term_refs, out_ref, places = refs[:-2], refs[-2], refs[-1]
+    row_count, size, _ = places.shape
+    place = ring_place(lax.axis_index("row"), row_count)
+    for offset, first, ref in zip(offsets, first_rows, term_refs):
+        places[ring_row(place + offset, row_count)] = ref[pl.ds(first, size), :].astype(jnp.float32)
+    total = places[0]
+    for index in range(1, row_count):
+        total += places[index]
+    out_ref[...] = total
+
+
+def summed_terms(terms, size):
+    offsets = tuple(offset for offset, _, _ in terms)
+    first_rows = tuple(first for _, first, _ in terms)
+    arrays = [array for _, _, array in terms]
+    width = arrays[0].shape[1]
+    return pl.pallas_call(
+        functools.partial(terms_kernel, offsets=offsets, first_rows=first_rows),
+        out_shape=jax.ShapeDtypeStruct((size, width), jnp.float32),
+        in_specs=[pl.BlockSpec(memory_space=pltpu.VMEM)] * len(arrays),
+        out_specs=pl.BlockSpec(memory_space=pltpu.VMEM),
+        scratch_shapes=[pltpu.VMEM((len(arrays), size, width), jnp.float32)],
+        compiler_params=pltpu.CompilerParams(
+            vmem_limit_bytes=scratch_bytes(*((array.shape, array.dtype) for array in arrays)) + 8 * mib
+        ),
+        cost_estimate=pl.CostEstimate(
+            flops=len(arrays) * size * width, bytes_accessed=2 * len(arrays) * size * width, transcendentals=0
+        ),
+        name="summed_terms",
+    )(*arrays)
 
 
 def finish_kernel(*refs, parts):
     part_refs, chunk_refs, (features_ref, weight_ref) = refs[:parts], refs[parts:-2], refs[-2:]
-    total = part_refs[0][...].astype(jnp.float32)
+    width = features_ref.shape[1]
+    total = part_refs[0][pl.ds(0, width), :].astype(jnp.float32)
     for part_ref in part_refs[1:]:
-        total += part_ref[...].astype(jnp.float32)
+        total += part_ref[pl.ds(0, width), :].astype(jnp.float32)
     features_ref[...] = total.astype(jnp.bfloat16).T
     rows = chunk_refs[0].shape[0]
     col = lax.axis_index("col")
@@ -316,25 +366,14 @@
 
 
 def gathered_shards(own, beside):
-    count = lax.axis_size("row")
+    reach = lax.axis_size("row") // 2
     rows = own.shape[0]
-    half = rows // 2
     shards = [(((0, 0, 0, rows),), own)]
-    if count == 8:
-        far_up, far_down, up, down = (around(own, step) for step in (2, -2, 1, -1))
-        for offset, array in ((-2, far_up), (2, far_down), (-1, up), (1, down)):
-            shards.append((((offset, 0, 0, rows),), array))
-        far_up, far_down, up, down, beside = lax.optimization_barrier((far_up, far_down, up, down, beside))
-        up = around(jnp.concatenate([up, far_up[:half]]), 2)
-        down = around(jnp.concatenate([down, far_down[half:]]), -2)
-        shards.append((((-3, 0, 0, rows), (-4, 0, rows, half)), up))
-        shards.append((((3, 0, 0, rows), (4, half, rows, half)), down))
-        return shards, beside
     up = down = own
-    for step in range(1, count // 2 + 1):
+    for step in range(1, reach + 1):
         up = around(up, 1)
         shards.append((((-step, 0, 0, rows),), up))
-        if step < count // 2:
+        if step < reach:
             down = around(down, -1)
             shards.append((((step, 0, 0, rows),), down))
         if step == 1:
@@ -342,68 +381,44 @@
     return shards, beside
 
 
-def added(first, second, at=0):
-    spare = first.shape[0] - at - second.shape[0]
-    second = jnp.pad(second.astype(jnp.float32), ((at, spare), (0, 0)))
-    return (first.astype(jnp.float32) + second).astype(jnp.bfloat16)
-
-
-def partners_sum(values):
-    while len(values) > 1:
-        values = [values[i] + values[i + 1] for i in range(0, len(values), 2)]
-    return values[0]
+def added(first, second):
+    return (first.astype(jnp.float32) + second[: first.shape[0]].astype(jnp.float32)).astype(jnp.bfloat16)
 
 
 def scattered_sums(dense, own, sibling, chunk):
     row_count, col_count = lax.axis_size("row"), lax.axis_size("col")
-    width = chunk.shape[1]
-    half = width // 2
+    size, width = chunk.shape
     reach = row_count // 2
-
-    def strips(cell, outputs):
-        return backward_product(cell, own, sibling, width, outputs, row_count, col_count)
-
-    def given_to_column(chunk):
-        return [chunk] + [swapped(chunk, "col", partner) for partner in range(1, col_count)]
-
-    if row_count == 8:
-        far = strips(dense, (((3, 0, width), (4, 0, half)), ((-3, 0, width), (4, half, half))))
-        far, cell = lax.optimization_barrier((far, dense))
-        up, down = around(far[0], 2), around(far[1], -2)
-        others = [swapped(chunk, "row", partner) for partner in (2, 4, 6)]
-        up, down, others = lax.optimization_barrier((up, down, others))
-        above, below, above_far, below_far, mine = strips(
-            cell, tuple(((offset, 0, width),) for offset in (1, -1, 2, -2, 0))
-        )
-        above_far, below_far = added(above_far, up[width:]), added(below_far, down[width:], half)
-        above, below = added(above, up[:width]), added(below, down[:width])
-        parts = [mine, around(above_far, 2), around(below_far, -2), around(above, 1), around(below, -1)]
-        return parts, given_to_column(partners_sum([chunk] + others))
-    (far,) = strips(dense, (((reach, 0, width),),))
-    far, cell = lax.optimization_barrier((far, dense))
-    up, down = around(far, 1), None
-    offsets = tuple(sign * step for step in range(reach - 1, 0, -1) for sign in (1, -1)) + (0,)
-    *rest, mine = strips(cell, tuple(((offset, 0, width),) for offset in offsets))
-    for step in range(reach - 1):
-        above, below = rest[2 * step : 2 * step + 2]
-        up = around(added(above, up), 1)
-        down = around(below if down is None else added(below, down), -1)
-    for bit in range(1, (row_count - 1).bit_length()):
-        chunk = chunk + swapped(chunk, "row", 1 << bit)
-    return [mine, up, down], given_to_column(chunk)
+    first = ((reach, "terms"), (1 - reach, "terms"), (0, "terms alone"))
+    above, below, terms = backward_product(dense, own, sibling, chunk, first, row_count, col_count)
+    above, below, terms, cell = lax.optimization_barrier((above, below, terms, dense))
+    up, down = around(above, 1), around(below, -1)
+    up, down, opposite = lax.optimization_barrier((up, down, around(terms, reach)))
+    all_terms = [(0, 0, terms), (reach, 0, opposite)]
+
+    ups = tuple((offset, "zeros" if offset > 1 else "") for offset in range(reach - 1, 0, -1))
+    downs = tuple((-offset, "zeros") for offset in range(reach - 2, 0, -1))
+    strips = backward_product(cell, own, sibling, chunk, ups + downs + ((0, ""),), row_count, col_count)
+    ups, downs, mine = strips[: reach - 1], strips[reach - 1 : -1], strips[-1]
+    for step in range(1, reach):
+        all_terms += [(-step, width, up), (step, width, down)]
+        up = around(added(ups[step - 1], up), 1)
+        if step < reach - 1:
+            down = around(added(downs[step - 1], down), -1)
+    chunk = summed_terms(all_terms, size)
+    chunks = [chunk] + [swapped(chunk, "col", partner) for partner in range(1, col_count)]
+    return [mine, up, down], chunks
 
 
 def per_device(features, weight, adj_tiles, tile_rows, tile_cols, tile_counts, out_grad):
     node_rows, width = features.shape
     capacity, side = adj_tiles.shape[2:4]
     tiles = adj_tiles.reshape(capacity, side, side)
-    rows = tile_rows.reshape(capacity)
-    cols = tile_cols.reshape(capacity)
-    count = tile_counts.reshape(1)
+    packed = ((tile_counts[:, :, None] << 16) | (tile_rows << 8) | tile_cols).reshape(capacity)
     row_count = lax.axis_size("row")
     col_count = lax.axis_size("col")
     per_strip = node_rows // side
-    dense = build_dense(rows, cols, count, tiles, col_count * per_strip, row_count * per_strip, per_strip)
+    dense = build_dense(packed, tiles, col_count * per_strip, row_count * per_strip, per_strip)
     cotangents = [out_grad] + [swapped(out_grad, "col", partner) for partner in range(2, col_count, 2)]
     shards, (dense, cotangents) = gathered_shards(features, (dense, cotangents))
 
@@ -411,20 +426,8 @@
     for_sibling, cell = lax.optimization_barrier((for_sibling, dense))
     sums = added(forward_product(cell, shards, 0, row_count, col_count), swapped(for_sibling, "col", 1))
     sums = [sums] + [swapped(sums, "col", partner) for partner in range(2, col_count, 2)]
-    activations, message, chunk, sent = middle(sums, weight, cotangents, node_rows * row_count * col_count)
-
+    activations, message, chunk = middle(sums, weight, cotangents, node_rows * row_count * col_count)
     sibling = swapped(message, "col", 1)
-    across = swapped(chunk, "row", 1)
-    across_sibling = lax.ppermute(
-        sent,
-        ("row", "col"),
-        [(r * col_count + c, (r ^ 1) * col_count + (c ^ 1)) for r in range(row_count) for c in range(col_count)],
-    )
-    message, sibling, across, across_sibling = lax.optimization_barrier((message, sibling, across, across_sibling))
-    size = chunk.shape[0]
-    high, low = sibling[-2 * size : -size], sibling[-size:]
-    chunk = (chunk + (high.astype(jnp.float32) + low.astype(jnp.float32))) + (across + across_sibling)
-
     parts, chunks = scattered_sums(dense, message, sibling, chunk)
     grad_features, grad_weight = finish(parts, chunks)
     return (activations, grad_features, grad_weight)

time: 80.4 us -> 72.2 us (0.90)
  waiting for transfers between devices: 38.6 us -> 31.9 us
  local copies, waits for them, and re-layouts: 1.39 us -> 0.02 us
    ppermute x11 -> x7, waiting for transfers between devices: 22.9 us -> 12.7 us  [swapped(): lax.ppermute(value, axis, [(i, i ^ partner) for i in range(lax.axis_size(...]
    ppermute x12 -> x15, starting transfers between devices: 17.3 us -> 25 us  [around(): lax.ppermute(value, 'row', [(order[i], order[(i + step) % count]) for i i...]
    ppermute x11 -> x7, starting transfers between devices: 10.8 us -> 5.18 us  [swapped(): lax.ppermute(value, axis, [(i, i ^ partner) for i in range(lax.axis_size(...]
    ppermute x12 -> x15, waiting for transfers between devices: 15.2 us -> 19.1 us  [around(): lax.ppermute(value, 'row', [(order[i], order[(i + step) % count]) for i i...]
    ppermute x1 -> x0, starting transfers between devices: 1.78 us -> none  [per_device(): lax.ppermute(sent, ('row', 'col'), [(r * col_count + c, (r ^ 1) * col_cou...]
    unnamed x10 -> x6, local copies, waits for them, and re-layouts: 1.37 us -> 0.02 us
  transfers between devices with their start and end apart: 24 -> 22, of which waited for: 14 -> 13; matrix products, arithmetic and copies ran while one was open for 0% -> 1% of each run, Pallas kernels for 7% -> 7%
where the time goes in v6:
time: 72.2 us; the launch traced here: 72.7 us
  waiting for transfers between devices  31.9 us (44%)
  starting transfers between devices  30.2 us (42%)
  Pallas kernels  8.13 us (11%)
  between operations  1.46 us (2%)
  other arithmetic  0.98 us (1%)
    ppermute x15, starting transfers between devices, around(): lax.ppermute(value, 'row', [(order[i], order[(i + step) % count]) for i i...  25 us
    ppermute x15, waiting for transfers between devices, around(): lax.ppermute(value, 'row', [(order[i], order[(i + step) % count]) for i i...  19.1 us
    ppermute x7, waiting for transfers between devices, swapped(): lax.ppermute(value, axis, [(i, i ^ partner) for i in range(lax.axis_size(...  12.7 us
    ppermute x7, starting transfers between devices, swapped(): lax.ppermute(value, axis, [(i, i ^ partner) for i in range(lax.axis_size(...  5.18 us
    pallas_call x1, Pallas kernels, build_dense(): pl.pallas_call(functools.partial(build_kernel, blocks=blocks, steps=steps...  3.11 us
    pallas_call x2, Pallas kernels, backward_product(): pl.pallas_call(functools.partial(backward_kernel, outputs=outputs, row_co...  1.73 us
  transfers between devices with their start and end apart: 22, of which 13 were waited for; matrix products, arithmetic and copies ran while one was open for 1% of the time, Pallas kernels for 7%

profile of v6, /device:TPU:0, one launch (start us, length us, event | category | flops | bytes accessed | tf_op | source)
XLA Modules:
  0.0 72.7 jit_solution(9405380852160534815)
XLA Ops:
  0.6 0.0 copy-start
  0.6 3.0 %collective-permute-start.1 = (bf16[256,256]{1,0:T(8,128)(2,1)}, bf16[256,256]{1,0:T(8,128)(2,1)S(1)}, u32[]{:S(2)}, u32[]{:S(2)}) collective-permute-start(bf16[256,256]{1,0:T(8,128)(2,1)} %refs_0_.3), channel_id=1, source_target_pairs={{0,4},{8,0},{16,8},{24,16},{28,24},{20,28},{12,20},{4,12},{1,5},{9... | collective-permute-start | bytes 393224 | tf_op jit(solution)/shard_map/ppermute | solution.py:361
  3.7 0.1 collective-permute-start
  3.8 1.9 %collective-permute-start.2 = (bf16[256,256]{1,0:T(8,128)(2,1)}, bf16[256,256]{1,0:T(8,128)(2,1)S(1)}, u32[]{:S(2)}, u32[]{:S(2)}) collective-permute-start(bf16[256,256]{1,0:T(8,128)(2,1)} %refs_3_), channel_id=1, source_target_pairs={{0,2},{1,3},{2,0},{3,1},{4,6},{5,7},{6,4},{7,5},{8,10},{9,11},{10,... | collective-permute-start | bytes 393224 | tf_op jit(solution)/shard_map/ppermute | solution.py:365
  6.3 0.7 or_or_fusion
  7.0 3.1 %build_dense.1.dense_ref = bf16[1024,2048]{1,0:T(8,128)(2,1)S(1)} custom-call(s32[256]{0:T(256)S(1)} %bitcast.3, bf16[256,128,128]{2,1,0:T(8,128)(2,1)} %bitcast.4), custom_call_target="tpu_custom_call" | custom-call | flops 4194304 | bytes 12582912 | tf_op jit(solution)/shard_map/build_dense/pallas_call | solution.py:98
  10.1 0.0 copy-start.1
  10.1 0.0 copy-start.2
  10.2 0.0 collective-permute-done.2.refs_4_
  10.2 0.0 collective-permute-done.1.refs_2_
  10.2 0.0 collective-permute-done.refs_1_
  10.2 3.6 %collective-permute-start.3 = (bf16[256,256]{1,0:T(8,128)(2,1)S(1)}, bf16[256,256]{1,0:T(8,128)(2,1)S(1)}, u32[]{:S(2)}, u32[]{:S(2)}) collective-permute-start(bf16[256,256]{1,0:T(8,128)(2,1)S(1)} %collective-permute-done.refs_1_), channel_id=1, source_target_pairs={{0,8},{8,16},{16,24},{24,28},{28,20},{20,12},{12,4},{4,0},{1,9},{9... | collective-permute-start | bytes 393224 | tf_op jit(solution)/shard_map/ppermute | solution.py:361
  13.8 0.0 collective-permute-start.4
  13.8 3.6 %collective-permute-done.3.refs_3_ = bf16[256,256]{1,0:T(8,128)(2,1)S(1)} collective-permute-done((bf16[256,256]{1,0:T(8,128)(2,1)S(1)}, bf16[256,256]{1,0:T(8,128)(2,1)S(1)}, u32[]{:S(2)}, u32[]{:S(2)}) %collective-permute-start.3) | collective-permute-done | bytes 131104 | tf_op jit(solution)/shard_map/ppermute | solution.py:361
  17.3 2.5 %collective-permute-start.5 = (bf16[256,256]{1,0:T(8,128)(2,1)S(1)}, bf16[256,256]{1,0:T(8,128)(2,1)S(1)}, u32[]{:S(2)}, u32[]{:S(2)}) collective-permute-start(bf16[256,256]{1,0:T(8,128)(2,1)S(1)} %collective-permute-done.3.refs_3_), channel_id=1, source_target_pairs={{0,8},{8,16},{16,24},{24,28},{28,20},{20,12},{12,4},{4,0},{1,9},{9... | collective-permute-start | bytes 393224 | tf_op jit(solution)/shard_map/ppermute | solution.py:361
  19.8 0.3 collective-permute-done.4.refs_4_
  20.1 0.0 collective-permute-start.6
  20.1 3.1 %collective-permute-done.5.refs_5_ = bf16[256,256]{1,0:T(8,128)(2,1)S(1)} collective-permute-done((bf16[256,256]{1,0:T(8,128)(2,1)S(1)}, bf16[256,256]{1,0:T(8,128)(2,1)S(1)}, u32[]{:S(2)}, u32[]{:S(2)}) %collective-permute-start.5) | collective-permute-done | bytes 131104 | tf_op jit(solution)/shard_map/ppermute | solution.py:361
  23.2 2.2 %collective-permute-start.7 = (bf16[256,256]{1,0:T(8,128)(2,1)S(1)}, bf16[256,256]{1,0:T(8,128)(2,1)S(1)}, u32[]{:S(2)}, u32[]{:S(2)}) collective-permute-start(bf16[256,256]{1,0:T(8,128)(2,1)S(1)} %collective-permute-done.5.refs_5_), channel_id=1, source_target_pairs={{0,8},{8,16},{16,24},{24,28},{28,20},{20,12},{12,4},{4,0},{1,9},{9... | collective-permute-start | bytes 393224 | tf_op jit(solution)/shard_map/ppermute | solution.py:361
  25.4 0.2 collective-permute-done.6.refs_6_
  25.6 2.6 %collective-permute-done.7.refs_7_ = bf16[256,256]{1,0:T(8,128)(2,1)S(1)} collective-permute-done((bf16[256,256]{1,0:T(8,128)(2,1)S(1)}, bf16[256,256]{1,0:T(8,128)(2,1)S(1)}, u32[]{:S(2)}, u32[]{:S(2)}) %collective-permute-start.7) | collective-permute-done | bytes 131104 | tf_op jit(solution)/shard_map/ppermute | solution.py:361
  28.2 0.0 copy-done
  28.2 0.7 forward_product.2
  29.0 0.1 collective-permute-start.8
  29.0 0.7 forward_product.3
  29.8 0.8 %collective-permute-done.8 = bf16[512,256]{1,0:T(8,128)(2,1)S(1)} collective-permute-done((bf16[512,256]{1,0:T(8,128)(2,1)S(1)}, bf16[512,256]{1,0:T(8,128)(2,1)S(1)}, u32[]{:S(2)}, u32[]{:S(2)}) %collective-permute-start.8) | collective-permute-done | bytes 262176 | tf_op jit(solution)/shard_map/ppermute | solution.py:365
  30.6 0.1 add_convert_fusion.refs_0_
  30.6 1.2 %collective-permute-start.9 = (bf16[512,256]{1,0:T(8,128)(2,1)S(1)}, bf16[512,256]{1,0:T(8,128)(2,1)S(1)}, u32[]{:S(2)}, u32[]{:S(2)}) collective-permute-start(bf16[512,256]{1,0:T(8,128)(2,1)S(1)} %add_convert_fusion.refs_0_), channel_id=1, source_target_pairs={{0,2},{1,3},{2,0},{3,1},{4,6},{5,7},{6,4},{7,5},{8,10},{9,11},{10,... | collective-permute-start | bytes 786440 | tf_op jit(solution)/shard_map/ppermute | solution.py:365
  31.9 7.2 %collective-permute-done.9.refs_1_ = bf16[512,256]{1,0:T(8,128)(2,1)S(1)} collective-permute-done((bf16[512,256]{1,0:T(8,128)(2,1)S(1)}, bf16[512,256]{1,0:T(8,128)(2,1)S(1)}, u32[]{:S(2)}, u32[]{:S(2)}) %collective-permute-start.9) | collective-permute-done | bytes 262176 | tf_op jit(solution)/shard_map/ppermute | solution.py:365
  39.0 0.0 copy-done.1
  39.1 0.0 copy-done.2
  39.1 1.0 %middle.1 = (bf16[256,256]{1,0:T(8,128)(2,1)}, bf16[640,256]{1,0:T(8,128)(2,1)S(1)}, f32[64,256]{1,0:T(8,128)S(1)}) custom-call(bf16[512,256]{1,0:T(8,128)(2,1)S(1)} %add_convert_fusion.refs_0_, bf16[512,256]{1,0:T(8,128)(2,1)S(1)} %collective-permute-done.9.refs_1_, bf16[256,256]{1,0:T(8,128)(2,1)S(1)} %copy-done.1, bf16[256,256]{1,0:T(8,128)(2,1)S(1)} %copy-done.2, ...), custom_call_target="tpu_custom_call" | custom-call | flops 335544320 | bytes 1572864 | tf_op jit(solution)/shard_map/middle/pallas_call | solution.py:218
  40.1 0.1 collective-permute-start.10
  40.1 1.6 %collective-permute-done.10.sibling_ref = bf16[640,256]{1,0:T(8,128)(2,1)S(1)} collective-permute-done((bf16[640,256]{1,0:T(8,128)(2,1)S(1)}, bf16[640,256]{1,0:T(8,128)(2,1)S(1)}, u32[]{:S(2)}, u32[]{:S(2)}) %collective-permute-start.10) | collective-permute-done | bytes 327712 | tf_op jit(solution)/shard_map/ppermute | solution.py:365
  41.8 0.6 backward_product.2
  42.3 2.2 %collective-permute-start.11 = (bf16[320,256]{1,0:T(8,128)(2,1)S(1)}, bf16[320,256]{1,0:T(8,128)(2,1)S(1)}, u32[]{:S(2)}, u32[]{:S(2)}) collective-permute-start(bf16[320,256]{1,0:T(8,128)(2,1)S(1)} %get-tuple-element.49), channel_id=1, source_target_pairs={{0,8},{8,16},{16,24},{24,28},{28,20},{20,12},{12,4},{4,0},{1,9},{9... | collective-permute-start | bytes 491528 | tf_op jit(solution)/shard_map/ppermute | solution.py:361
  44.5 1.3 %collective-permute-start.12 = (bf16[320,256]{1,0:T(8,128)(2,1)S(1)}, bf16[320,256]{1,0:T(8,128)(2,1)S(1)}, u32[]{:S(2)}, u32[]{:S(2)}) collective-permute-start(bf16[320,256]{1,0:T(8,128)(2,1)S(1)} %get-tuple-element.50), channel_id=1, source_target_pairs={{0,4},{8,0},{16,8},{24,16},{28,24},{20,28},{12,20},{4,12},{1,5},{9... | collective-permute-start | bytes 491528 | tf_op jit(solution)/shard_map/ppermute | solution.py:361
  45.9 5.4 %collective-permute-start.13 = (bf16[64,256]{1,0:T(8,128)(2,1)S(1)}, bf16[64,256]{1,0:T(8,128)(2,1)S(1)}, u32[]{:S(2)}, u32[]{:S(2)}) collective-permute-start(bf16[64,256]{1,0:T(8,128)(2,1)S(1)} %get-tuple-element.51.refs_0_), channel_id=1, source_target_pairs={{0,28},{8,20},{16,12},{24,4},{28,0},{20,8},{12,16},{4,24},{1,29},{... | collective-permute-start | bytes 98312 | tf_op jit(solution)/shard_map/ppermute | solution.py:361
  51.3 1.1 %backward_product.3 = (bf16[320,256]{1,0:T(8,128)(2,1)S(1)}, bf16[320,256]{1,0:T(8,128)(2,1)S(1)}, bf16[256,256]{1,0:T(8,128)(2,1)S(1)}, bf16[320,256]{1,0:T(8,1...) custom-call(bf16[1024,2048]{1,0:T(8,128)(2,1)S(1)} %build_dense.1.dense_ref, ...), custom_call_target="tpu_custom_call" | custom-call | flops 134217728 | bytes 786432 | tf_op jit(solution)/shard_map/backward_product/pallas_call | solution.py:280
  52.5 2.4 %collective-permute-done.13.refs_1_ = bf16[64,256]{1,0:T(8,128)(2,1)S(1)} collective-permute-done((bf16[64,256]{1,0:T(8,128)(2,1)S(1)}, bf16[64,256]{1,0:T(8,128)(2,1)S(1)}, u32[]{:S(2)}, u32[]{:S(2)}) %collective-permute-start.13) | collective-permute-done | bytes 32800 | tf_op jit(solution)/shard_map/ppermute | solution.py:361
  54.8 0.0 collective-permute-done.11.refs_2_
  54.8 0.0 collective-permute-done.12.refs_3_
  54.9 0.1 collective-permute-start.14
  55.0 2.1 %collective-permute-start.17 = (bf16[320,256]{1,0:T(8,128)(2,1)S(1)}, bf16[320,256]{1,0:T(8,128)(2,1)S(1)}, u32[]{:S(2)}, u32[]{:S(2)}) collective-permute-start(bf16[320,256]{1,0:T(8,128)(2,1)S(1)} %add_convert_fusion.2), channel_id=1, source_target_pairs={{0,4},{8,0},{16,8},{24,16},{28,24},{20,28},{12,20},{4,12},{1,5},{9... | collective-permute-start | bytes 491528 | tf_op jit(solution)/shard_map/ppermute | solution.py:361
  57.1 3.2 %collective-permute-done.14.refs_4_ = bf16[320,256]{1,0:T(8,128)(2,1)S(1)} collective-permute-done((bf16[320,256]{1,0:T(8,128)(2,1)S(1)}, bf16[320,256]{1,0:T(8,128)(2,1)S(1)}, u32[]{:S(2)}, u32[]{:S(2)}) %collective-permute-start.14) | collective-permute-done | bytes 163872 | tf_op jit(solution)/shard_map/ppermute | solution.py:361
  60.3 0.1 collective-permute-start.15
  60.4 0.0 collective-permute-done.17.refs_5_
  60.5 2.0 %collective-permute-start.18 = (bf16[320,256]{1,0:T(8,128)(2,1)S(1)}, bf16[320,256]{1,0:T(8,128)(2,1)S(1)}, u32[]{:S(2)}, u32[]{:S(2)}) collective-permute-start(bf16[320,256]{1,0:T(8,128)(2,1)S(1)} %add_convert_fusion.1), channel_id=1, source_target_pairs={{0,4},{8,0},{16,8},{24,16},{28,24},{20,28},{12,20},{4,12},{1,5},{9... | collective-permute-start | bytes 491528 | tf_op jit(solution)/shard_map/ppermute | solution.py:361
  62.5 3.8 %collective-permute-done.15.refs_6_ = bf16[320,256]{1,0:T(8,128)(2,1)S(1)} collective-permute-done((bf16[320,256]{1,0:T(8,128)(2,1)S(1)}, bf16[320,256]{1,0:T(8,128)(2,1)S(1)}, u32[]{:S(2)}, u32[]{:S(2)}) %collective-permute-start.15) | collective-permute-done | bytes 163872 | tf_op jit(solution)/shard_map/ppermute | solution.py:361
  66.3 0.4 collective-permute-start.16
  66.7 0.0 collective-permute-done.18.refs_7_.refs_2_
  66.7 0.1 summed_terms.1.refs_3_
  66.8 0.1 collective-permute-start.21
  66.9 0.3 collective-permute-start.20
  67.2 1.5 %collective-permute-start.19 = (f32[64,256]{1,0:T(8,128)S(1)}, f32[64,256]{1,0:T(8,128)S(1)}, u32[]{:S(2)}, u32[]{:S(2)}) collective-permute-start(f32[64,256]{1,0:T(8,128)S(1)} %summed_terms.1.refs_3_), channel_id=1, source_target_pairs={{0,1},{1,0},{2,3},{3,2},{4,5},{5,4},{6,7},{7,6},{8,9},{9,8},{10,11... | collective-permute-start | bytes 196616 | tf_op jit(solution)/shard_map/ppermute | solution.py:365
  68.8 2.0 %collective-permute-done.21.refs_6_ = f32[64,256]{1,0:T(8,128)S(1)} collective-permute-done((f32[64,256]{1,0:T(8,128)S(1)}, f32[64,256]{1,0:T(8,128)S(1)}, u32[]{:S(2)}, u32[]{:S(2)}) %collective-permute-start.21) | collective-permute-done | bytes 65568 | tf_op jit(solution)/shard_map/ppermute | solution.py:365
  70.7 1.1 %collective-permute-done.20.refs_5_ = f32[64,256]{1,0:T(8,128)S(1)} collective-permute-done((f32[64,256]{1,0:T(8,128)S(1)}, f32[64,256]{1,0:T(8,128)S(1)}, u32[]{:S(2)}, u32[]{:S(2)}) %collective-permute-start.20) | collective-permute-done | bytes 65568 | tf_op jit(solution)/shard_map/ppermute | solution.py:365
  71.9 0.0 collective-permute-done.19.refs_4_
  71.9 0.0 collective-permute-done.16.refs_1_
  71.9 0.8 %finish.1 = (bf16[256,256]{1,0:T(8,128)(2,1)}, f32[256,256]{1,0:T(8,128)}) custom-call(bf16[256,256]{1,0:T(8,128)(2,1)S(1)} %get-tuple-element.45.refs_0_, bf16[256,256]{1,0:T(8,128)(2,1)S(1)} %collective-permute-done.16.refs_1_, bf16[320,256]{1,0:T(8,128)(2,1)S(1)} %collective-permute-done.18.refs_7_.refs_2_, f32[64,256]{1,0:T(8,128)S(1)} %summed_terms.1.refs_3_, ...), custom_call_target="tpu_custom_call" | custom-call | flops 196608 | bytes 1048576 | tf_op jit(solution)/shard_map/finish/pallas_call | solution.py:342
  (5 shorter events, 0.2 us)
Async XLA Ops:
  0.6 27.6 %copy-start = (bf16[256,256]{1,0:T(8,128)(2,1)S(1)}, bf16[256,256]{1,0:T(8,128)(2,1)}, u32[]{:S(2)}) copy-start(bf16[256,256]{1,0:T(8,128)(2,1)} %refs_0_.3) | copy-start | bytes 393220
  0.6 9.5 %collective-permute-start.1 = (bf16[256,256]{1,0:T(8,128)(2,1)}, bf16[256,256]{1,0:T(8,128)(2,1)S(1)}, u32[]{:S(2)}, u32[]{:S(2)}) collective-permute-start(bf16[256,256]{1,0:T(8,128)(2,1)} %refs_0_.3), channel_id=1, source_target_pairs={{0,4},{8,0},{16,8},{24,16},{28,24},{20,28},{12,20},{4,12},{1,5},{9... | collective-permute-start | bytes 393224 | tf_op jit(solution)/shard_map/ppermute | solution.py:361
  3.7 6.5 %collective-permute-start = (bf16[256,256]{1,0:T(8,128)(2,1)}, bf16[256,256]{1,0:T(8,128)(2,1)S(1)}, u32[]{:S(2)}, u32[]{:S(2)}) collective-permute-start(bf16[256,256]{1,0:T(8,128)(2,1)} %refs_0_.3), channel_id=1, source_target_pairs={{0,8},{8,16},{16,24},{24,28},{28,20},{20,12},{12,4},{4,0},{1,9},{9... | collective-permute-start | bytes 393224 | tf_op jit(solution)/shard_map/ppermute | solution.py:361
  3.8 6.4 %collective-permute-start.2 = (bf16[256,256]{1,0:T(8,128)(2,1)}, bf16[256,256]{1,0:T(8,128)(2,1)S(1)}, u32[]{:S(2)}, u32[]{:S(2)}) collective-permute-start(bf16[256,256]{1,0:T(8,128)(2,1)} %refs_3_), channel_id=1, source_target_pairs={{0,2},{1,3},{2,0},{3,1},{4,6},{5,7},{6,4},{7,5},{8,10},{9,11},{10,... | collective-permute-start | bytes 393224 | tf_op jit(solution)/shard_map/ppermute | solution.py:365
  10.1 28.9 %copy-start.1 = (bf16[256,256]{1,0:T(8,128)(2,1)S(1)}, bf16[256,256]{1,0:T(8,128)(2,1)}, u32[]{:S(2)}) copy-start(bf16[256,256]{1,0:T(8,128)(2,1)} %refs_2_.1) | copy-start | bytes 393220
  10.1 28.9 %copy-start.2 = (bf16[256,256]{1,0:T(8,128)(2,1)S(1)}, bf16[256,256]{1,0:T(8,128)(2,1)}, u32[]{:S(2)}) copy-start(bf16[256,256]{1,0:T(8,128)(2,1)} %refs_3_) | copy-start | bytes 393220
  10.2 7.2 %collective-permute-start.3 = (bf16[256,256]{1,0:T(8,128)(2,1)S(1)}, bf16[256,256]{1,0:T(8,128)(2,1)S(1)}, u32[]{:S(2)}, u32[]{:S(2)}) collective-permute-start(bf16[256,256]{1,0:T(8,128)(2,1)S(1)} %collective-permute-done.refs_1_), channel_id=1, source_target_pairs={{0,8},{8,16},{16,24},{24,28},{28,20},{20,12},{12,4},{4,0},{1,9},{9... | collective-permute-start | bytes 393224 | tf_op jit(solution)/shard_map/ppermute | solution.py:361
  13.8 6.3 %collective-permute-start.4 = (bf16[256,256]{1,0:T(8,128)(2,1)S(1)}, bf16[256,256]{1,0:T(8,128)(2,1)S(1)}, u32[]{:S(2)}, u32[]{:S(2)}) collective-permute-start(bf16[256,256]{1,0:T(8,128)(2,1)S(1)} %collective-permute-done.1.refs_2_), channel_id=1, source_target_pairs={{0,4},{8,0},{16,8},{24,16},{28,24},{20,28},{12,20},{4,12},{1,5},{9... | collective-permute-start | bytes 393224 | tf_op jit(solution)/shard_map/ppermute | solution.py:361
  17.3 5.8 %collective-permute-start.5 = (bf16[256,256]{1,0:T(8,128)(2,1)S(1)}, bf16[256,256]{1,0:T(8,128)(2,1)S(1)}, u32[]{:S(2)}, u32[]{:S(2)}) collective-permute-start(bf16[256,256]{1,0:T(8,128)(2,1)S(1)} %collective-permute-done.3.refs_3_), channel_id=1, source_target_pairs={{0,8},{8,16},{16,24},{24,28},{28,20},{20,12},{12,4},{4,0},{1,9},{9... | collective-permute-start | bytes 393224 | tf_op jit(solution)/shard_map/ppermute | solution.py:361
  20.1 5.5 %collective-permute-start.6 = (bf16[256,256]{1,0:T(8,128)(2,1)S(1)}, bf16[256,256]{1,0:T(8,128)(2,1)S(1)}, u32[]{:S(2)}, u32[]{:S(2)}) collective-permute-start(bf16[256,256]{1,0:T(8,128)(2,1)S(1)} %collective-permute-done.4.refs_4_), channel_id=1, source_target_pairs={{0,4},{8,0},{16,8},{24,16},{28,24},{20,28},{12,20},{4,12},{1,5},{9... | collective-permute-start | bytes 393224 | tf_op jit(solution)/shard_map/ppermute | solution.py:361
  23.2 5.1 %collective-permute-start.7 = (bf16[256,256]{1,0:T(8,128)(2,1)S(1)}, bf16[256,256]{1,0:T(8,128)(2,1)S(1)}, u32[]{:S(2)}, u32[]{:S(2)}) collective-permute-start(bf16[256,256]{1,0:T(8,128)(2,1)S(1)} %collective-permute-done.5.refs_5_), channel_id=1, source_target_pairs={{0,8},{8,16},{16,24},{24,28},{28,20},{20,12},{12,4},{4,0},{1,9},{9... | collective-permute-start | bytes 393224 | tf_op jit(solution)/shard_map/ppermute | solution.py:361
  29.0 1.6 %collective-permute-start.8 = (bf16[512,256]{1,0:T(8,128)(2,1)S(1)}, bf16[512,256]{1,0:T(8,128)(2,1)S(1)}, u32[]{:S(2)}, u32[]{:S(2)}) collective-permute-start(bf16[512,256]{1,0:T(8,128)(2,1)S(1)} %forward_product.2), channel_id=1, source_target_pairs={{0,1},{1,0},{2,3},{3,2},{4,5},{5,4},{6,7},{7,6},{8,9},{9,8},{10,11... | collective-permute-start | bytes 786440 | tf_op jit(solution)/shard_map/ppermute | solution.py:365
  30.6 8.4 %collective-permute-start.9 = (bf16[512,256]{1,0:T(8,128)(2,1)S(1)}, bf16[512,256]{1,0:T(8,128)(2,1)S(1)}, u32[]{:S(2)}, u32[]{:S(2)}) collective-permute-start(bf16[512,256]{1,0:T(8,128)(2,1)S(1)} %add_convert_fusion.refs_0_), channel_id=1, source_target_pairs={{0,2},{1,3},{2,0},{3,1},{4,6},{5,7},{6,4},{7,5},{8,10},{9,11},{10,... | collective-permute-start | bytes 786440 | tf_op jit(solution)/shard_map/ppermute | solution.py:365
  40.1 1.7 %collective-permute-start.10 = (bf16[640,256]{1,0:T(8,128)(2,1)S(1)}, bf16[640,256]{1,0:T(8,128)(2,1)S(1)}, u32[]{:S(2)}, u32[]{:S(2)}) collective-permute-start(bf16[640,256]{1,0:T(8,128)(2,1)S(1)} %get-tuple-element.39.own_ref), channel_id=1, source_target_pairs={{0,1},{1,0},{2,3},{3,2},{4,5},{5,4},{6,7},{7,6},{8,9},{9,8},{10,11... | collective-permute-start | bytes 983048 | tf_op jit(solution)/shard_map/ppermute | solution.py:365
  42.3 12.5 %collective-permute-start.11 = (bf16[320,256]{1,0:T(8,128)(2,1)S(1)}, bf16[320,256]{1,0:T(8,128)(2,1)S(1)}, u32[]{:S(2)}, u32[]{:S(2)}) collective-permute-start(bf16[320,256]{1,0:T(8,128)(2,1)S(1)} %get-tuple-element.49), channel_id=1, source_target_pairs={{0,8},{8,16},{16,24},{24,28},{28,20},{20,12},{12,4},{4,0},{1,9},{9... | collective-permute-start | bytes 491528 | tf_op jit(solution)/shard_map/ppermute | solution.py:361
  44.5 10.3 %collective-permute-start.12 = (bf16[320,256]{1,0:T(8,128)(2,1)S(1)}, bf16[320,256]{1,0:T(8,128)(2,1)S(1)}, u32[]{:S(2)}, u32[]{:S(2)}) collective-permute-start(bf16[320,256]{1,0:T(8,128)(2,1)S(1)} %get-tuple-element.50), channel_id=1, source_target_pairs={{0,4},{8,0},{16,8},{24,16},{28,24},{20,28},{12,20},{4,12},{1,5},{9... | collective-permute-start | bytes 491528 | tf_op jit(solution)/shard_map/ppermute | solution.py:361
  45.9 9.0 %collective-permute-start.13 = (bf16[64,256]{1,0:T(8,128)(2,1)S(1)}, bf16[64,256]{1,0:T(8,128)(2,1)S(1)}, u32[]{:S(2)}, u32[]{:S(2)}) collective-permute-start(bf16[64,256]{1,0:T(8,128)(2,1)S(1)} %get-tuple-element.51.refs_0_), channel_id=1, source_target_pairs={{0,28},{8,20},{16,12},{24,4},{28,0},{20,8},{12,16},{4,24},{1,29},{... | collective-permute-start | bytes 98312 | tf_op jit(solution)/shard_map/ppermute | solution.py:361
  54.9 5.4 %collective-permute-start.14 = (bf16[320,256]{1,0:T(8,128)(2,1)S(1)}, bf16[320,256]{1,0:T(8,128)(2,1)S(1)}, u32[]{:S(2)}, u32[]{:S(2)}) collective-permute-start(bf16[320,256]{1,0:T(8,128)(2,1)S(1)} %add_convert_fusion.4), channel_id=1, source_target_pairs={{0,8},{8,16},{16,24},{24,28},{28,20},{20,12},{12,4},{4,0},{1,9},{9... | collective-permute-start | bytes 491528 | tf_op jit(solution)/shard_map/ppermute | solution.py:361
  55.0 5.4 %collective-permute-start.17 = (bf16[320,256]{1,0:T(8,128)(2,1)S(1)}, bf16[320,256]{1,0:T(8,128)(2,1)S(1)}, u32[]{:S(2)}, u32[]{:S(2)}) collective-permute-start(bf16[320,256]{1,0:T(8,128)(2,1)S(1)} %add_convert_fusion.2), channel_id=1, source_target_pairs={{0,4},{8,0},{16,8},{24,16},{28,24},{20,28},{12,20},{4,12},{1,5},{9... | collective-permute-start | bytes 491528 | tf_op jit(solution)/shard_map/ppermute | solution.py:361
  60.3 6.0 %collective-permute-start.15 = (bf16[320,256]{1,0:T(8,128)(2,1)S(1)}, bf16[320,256]{1,0:T(8,128)(2,1)S(1)}, u32[]{:S(2)}, u32[]{:S(2)}) collective-permute-start(bf16[320,256]{1,0:T(8,128)(2,1)S(1)} %add_convert_fusion.3), channel_id=1, source_target_pairs={{0,8},{8,16},{16,24},{24,28},{28,20},{20,12},{12,4},{4,0},{1,9},{9... | collective-permute-start | bytes 491528 | tf_op jit(solution)/shard_map/ppermute | solution.py:361
  60.5 6.2 %collective-permute-start.18 = (bf16[320,256]{1,0:T(8,128)(2,1)S(1)}, bf16[320,256]{1,0:T(8,128)(2,1)S(1)}, u32[]{:S(2)}, u32[]{:S(2)}) collective-permute-start(bf16[320,256]{1,0:T(8,128)(2,1)S(1)} %add_convert_fusion.1), channel_id=1, source_target_pairs={{0,4},{8,0},{16,8},{24,16},{28,24},{20,28},{12,20},{4,12},{1,5},{9... | collective-permute-start | bytes 491528 | tf_op jit(solution)/shard_map/ppermute | solution.py:361
  66.3 5.5 %collective-permute-start.16 = (bf16[256,256]{1,0:T(8,128)(2,1)S(1)}, bf16[256,256]{1,0:T(8,128)(2,1)S(1)}, u32[]{:S(2)}, u32[]{:S(2)}) collective-permute-start(bf16[256,256]{1,0:T(8,128)(2,1)S(1)} %add_convert_fusion.5), channel_id=1, source_target_pairs={{0,8},{8,16},{16,24},{24,28},{28,20},{20,12},{12,4},{4,0},{1,9},{9... | collective-permute-start | bytes 393224 | tf_op jit(solution)/shard_map/ppermute | solution.py:361
  66.8 3.9 %collective-permute-start.21 = (f32[64,256]{1,0:T(8,128)S(1)}, f32[64,256]{1,0:T(8,128)S(1)}, u32[]{:S(2)}, u32[]{:S(2)}) collective-permute-start(f32[64,256]{1,0:T(8,128)S(1)} %summed_terms.1.refs_3_), channel_id=1, source_target_pairs={{0,3},{1,2},{2,1},{3,0},{4,7},{5,6},{6,5},{7,4},{8,11},{9,10},{10,... | collective-permute-start | bytes 196616 | tf_op jit(solution)/shard_map/ppermute | solution.py:365
  66.9 5.0 %collective-permute-start.20 = (f32[64,256]{1,0:T(8,128)S(1)}, f32[64,256]{1,0:T(8,128)S(1)}, u32[]{:S(2)}, u32[]{:S(2)}) collective-permute-start(f32[64,256]{1,0:T(8,128)S(1)} %summed_terms.1.refs_3_), channel_id=1, source_target_pairs={{0,2},{1,3},{2,0},{3,1},{4,6},{5,7},{6,4},{7,5},{8,10},{9,11},{10,... | collective-permute-start | bytes 196616 | tf_op jit(solution)/shard_map/ppermute | solution.py:365
  67.2 4.6 %collective-permute-start.19 = (f32[64,256]{1,0:T(8,128)S(1)}, f32[64,256]{1,0:T(8,128)S(1)}, u32[]{:S(2)}, u32[]{:S(2)}) collective-permute-start(f32[64,256]{1,0:T(8,128)S(1)} %summed_terms.1.refs_3_), channel_id=1, source_target_pairs={{0,1},{1,0},{2,3},{3,2},{4,5},{5,4},{6,7},{7,6},{8,9},{9,8},{10,11... | collective-permute-start | bytes 196616 | tf_op jit(solution)/shard_map/ppermute | solution.py:365

commit v7 on v6

--- a/solution.py
+++ b/solution.py
@@ -9,7 +9,8 @@
 from jax.sharding import PartitionSpec as P
 
 chunk_tiles = 16
-chunk_slots = 4
+chunk_slots = 8
+build_grant = 44
 strips_per_step = 8
 mib = 1024 * 1024
 
@@ -18,105 +19,179 @@
     return sum(math.prod(shape) * jnp.dtype(kind).itemsize for shape, kind in shapes)
 
 
-def build_kernel(list_ref, tiles_ref, dense_ref, total, held, sems, *, blocks, steps):
+def add_tiles(list_ref, tiles_ref, total, held, sems, begin, end, *, first_block, blocks, steps):
     side = tiles_ref.shape[1]
-    first_block = pl.program_id(0) * blocks
-    count = list_ref[0] >> 16
-    chunks = (count + chunk_tiles - 1) // chunk_tiles
+    capacity = tiles_ref.shape[0]
+    count = list_ref[2 * capacity]
+    slots = held.shape[0]
+    row_blocks = total.shape[0] // side - 1
 
     def fetch(index):
-        slot = lax.rem(index, chunk_slots)
+        slot = lax.rem(index - begin, slots)
         return pltpu.make_async_copy(
             tiles_ref.at[pl.ds(index * chunk_tiles, chunk_tiles)], held.at[slot], sems.at[slot]
         )
 
-    for ahead in range(chunk_slots - 1):
-        @pl.when(ahead < chunks)
-        def _():
-            fetch(ahead).start()
-
-    row_blocks = dense_ref.shape[0] // side
-
-    def clear(block, carry):
-        down = pl.ds(pl.multiple_of(block * side, side), side)
-        total[down, :] = jnp.zeros((side, total.shape[1]), jnp.float32)
+    def start(index, carry):
+        fetch(index).start()
         return carry
 
-    lax.fori_loop(0, row_blocks, clear, 0)
+    lax.fori_loop(begin, jnp.minimum(end, begin + slots), start, 0)
 
     def target(place):
-        code = list_ref[place]
-        col = (code & 255) - first_block
+        col = list_ref[capacity + place] - first_block
         live = place < count
         if steps > 1:
             live = live & (col >= 0) & (col < blocks)
             col = jnp.where(live, col, 0)
-        row = jnp.where(live, (code >> 8) & 255, row_blocks)
+        row = jnp.where(live, list_ref[place], row_blocks)
         return row, col
 
     def chunk_step(index, carry):
-        @pl.when(index + chunk_slots - 1 < chunks)
-        def _():
-            fetch(index + chunk_slots - 1).start()
-
         fetch(index).wait()
-        slot = lax.rem(index, chunk_slots)
+        slot = lax.rem(index - begin, slots)
         for lane in range(0, chunk_tiles, 2):
-            spots, olds, news = [], [], []
-            for place in (index * chunk_tiles + lane, index * chunk_tiles + lane + 1):
-                row, col = target(place)
-                spots.append((row, col))
-                olds.append(
-                    (pl.ds(pl.multiple_of(row * side, side), side), pl.ds(pl.multiple_of(col * side, side), side))
-                )
-            sums = [total[at] for at in olds]
+            spots = [target(index * chunk_tiles + lane + turn) for turn in range(2)]
+            at = [
+                (pl.ds(pl.multiple_of(row * side, side), side), pl.ds(pl.multiple_of(col * side, side), side))
+                for row, col in spots
+            ]
+            first, second = total[at[0]], total[at[1]]
             tiles = [held[slot, lane + turn].astype(jnp.float32) for turn in range(2)]
             same = (spots[0][0] == spots[1][0]) & (spots[0][1] == spots[1][1])
-            news = [sums[0] + tiles[0], sums[1] + tiles[1] + jnp.where(same, tiles[0], 0.0)]
-            for at, new in zip(olds, news):
-                total[at] = new
+            total[at[0]] = first + tiles[0]
+            total[at[1]] = second + tiles[1] + jnp.where(same, tiles[0], 0.0)
+
+        @pl.when(index + slots < end)
+        def _():
+            fetch(index + slots).start()
+
         return carry
 
-    lax.fori_loop(0, chunks, chunk_step, 0)
-
-    def round_block(block, carry):
-        down = pl.ds(pl.multiple_of(block * side, side), side)
+    return lambda: lax.fori_loop(begin, end, chunk_step, 0)
+
+
+def each_row_block(total, side, action):
+    def step(block, carry):
+        action(pl.ds(pl.multiple_of(block * side, side), side))
+        return carry
+
+    lax.fori_loop(0, total.shape[0] // side - 1, step, 0)
+
+
+def live_chunks(list_ref, tiles_ref):
+    return (list_ref[2 * tiles_ref.shape[0]] + chunk_tiles - 1) // chunk_tiles
+
+
+def build_first_kernel(list_ref, tiles_ref, dense_ref, total, held, sems, *, blocks):
+    half = (live_chunks(list_ref, tiles_ref) + 1) // 2
+    run = add_tiles(list_ref, tiles_ref, total, held, sems, 0, half, first_block=0, blocks=blocks, steps=1)
+
+    def clear(down):
+        total[down, :] = jnp.zeros((down.size, total.shape[1]), jnp.float32)
+
+    def rounded(down):
         dense_ref[down, :] = total[down, :].astype(jnp.bfloat16)
-        return carry
-
-    lax.fori_loop(0, row_blocks, round_block, 0)
-
-
-def build_dense(packed, tiles, row_blocks, col_blocks, per_strip):
+
+    each_row_block(total, tiles_ref.shape[1], clear)
+    run()
+    each_row_block(total, tiles_ref.shape[1], rounded)
+
+
+def build_rest_kernel(list_ref, tiles_ref, half_ref, dense_ref, total, held, sems, *, blocks):
+    chunks = live_chunks(list_ref, tiles_ref)
+    run = add_tiles(
+        list_ref, tiles_ref, total, held, sems, (chunks + 1) // 2, chunks, first_block=0, blocks=blocks, steps=1
+    )
+
+    def widened(down):
+        total[down, :] = half_ref[down, :].astype(jnp.float32)
+
+    def rounded(down):
+        dense_ref[down, :] = total[down, :].astype(jnp.bfloat16)
+
+    each_row_block(total, tiles_ref.shape[1], widened)
+    run()
+    each_row_block(total, tiles_ref.shape[1], rounded)
+
+
+def build_whole_kernel(list_ref, tiles_ref, dense_ref, total, held, sems, *, blocks, steps):
+    chunks = live_chunks(list_ref, tiles_ref)
+    first_block = pl.program_id(0) * blocks
+    run = add_tiles(
+        list_ref, tiles_ref, total, held, sems, 0, chunks, first_block=first_block, blocks=blocks, steps=steps
+    )
+
+    def clear(down):
+        total[down, :] = jnp.zeros((down.size, total.shape[1]), jnp.float32)
+
+    def rounded(down):
+        dense_ref[down, :] = total[down, :].astype(jnp.bfloat16)
+
+    each_row_block(total, tiles_ref.shape[1], clear)
+    run()
+    each_row_block(total, tiles_ref.shape[1], rounded)
+
+
+def build_stages(packed, tiles, row_blocks, col_blocks, per_strip):
     capacity, side, _ = tiles.shape
     blocks = min(strips_per_step * per_strip, col_blocks)
     steps = col_blocks // blocks
     high, wide = row_blocks * side, blocks * side
     total = ((high + side, wide), jnp.float32)
-    held = ((chunk_slots, chunk_tiles, side, side), jnp.bfloat16)
-    block = ((high, wide), jnp.bfloat16)
-    return pl.pallas_call(
-        functools.partial(build_kernel, blocks=blocks, steps=steps),
-        out_shape=jax.ShapeDtypeStruct((high, col_blocks * side), jnp.bfloat16),
-        grid_spec=pltpu.PrefetchScalarGridSpec(
-            num_scalar_prefetch=1,
-            grid=(steps,),
-            in_specs=[pl.BlockSpec(memory_space=pltpu.HBM)],
-            out_specs=pl.BlockSpec((high, wide), lambda i, *_: (0, i)),
-            scratch_shapes=[
-                pltpu.VMEM(*total),
-                pltpu.VMEM(*held),
-                pltpu.SemaphoreType.DMA((chunk_slots,)),
-            ],
-        ),
-        compiler_params=pltpu.CompilerParams(vmem_limit_bytes=46 * mib),
-        cost_estimate=pl.CostEstimate(
-            flops=capacity * side * side,
-            bytes_accessed=2 * (capacity * side * side + high * col_blocks * side),
-            transcendentals=0,
-        ),
-        name="build_dense",
-    )(packed, tiles)
+    held = ((min(chunk_slots, capacity // chunk_tiles), chunk_tiles, side, side), jnp.bfloat16)
+    cost = pl.CostEstimate(
+        flops=capacity * side * side, bytes_accessed=capacity * side * side + high * wide, transcendentals=0
+    )
+    held_scratch = [pltpu.VMEM(*held), pltpu.SemaphoreType.DMA((held[0][0],))]
+    dense_shape = jax.ShapeDtypeStruct((high, col_blocks * side), jnp.bfloat16)
+    whole = pl.BlockSpec(memory_space=pltpu.VMEM)
+    apart = pl.BlockSpec(memory_space=pl.ANY)
+    listed = pl.BlockSpec(memory_space=pltpu.SMEM)
+    if steps > 1:
+        block = ((high, wide), jnp.bfloat16)
+        return [
+            lambda _: pl.pallas_call(
+                functools.partial(build_whole_kernel, blocks=blocks, steps=steps),
+                out_shape=dense_shape,
+                grid_spec=pltpu.PrefetchScalarGridSpec(
+                    num_scalar_prefetch=1,
+                    grid=(steps,),
+                    in_specs=[apart],
+                    out_specs=pl.BlockSpec((high, wide), lambda i, *_: (0, i)),
+                    scratch_shapes=[pltpu.VMEM(*total)] + held_scratch,
+                ),
+                compiler_params=pltpu.CompilerParams(
+                    vmem_limit_bytes=scratch_bytes(total, held, block, block) + 4 * mib
+                ),
+                cost_estimate=cost,
+                name="build_whole",
+            )(packed, tiles)
+        ]
+    params = pltpu.CompilerParams(vmem_limit_bytes=build_grant * mib)
+    scratch = [pltpu.VMEM(*total)] + held_scratch
+    return [
+        lambda _: pl.pallas_call(
+            functools.partial(build_first_kernel, blocks=blocks),
+            out_shape=dense_shape,
+            in_specs=[listed, apart],
+            out_specs=whole,
+            scratch_shapes=scratch,
+            compiler_params=params,
+            cost_estimate=cost,
+            name="build_first",
+        )(packed, tiles),
+        lambda half: pl.pallas_call(
+            functools.partial(build_rest_kernel, blocks=blocks),
+            out_shape=dense_shape,
+            in_specs=[listed, apart, whole],
+            out_specs=whole,
+            scratch_shapes=scratch,
+            compiler_params=params,
+            cost_estimate=cost,
+            name="build_rest",
+        )(packed, tiles, half),
+    ]
 
 
 def ring_place(row, count):
@@ -365,20 +440,27 @@
     return lax.ppermute(value, axis, [(i, i ^ partner) for i in range(lax.axis_size(axis))])
 
 
-def gathered_shards(own, beside):
+def gathered_shards(own, stages, cotangent):
     reach = lax.axis_size("row") // 2
     rows = own.shape[0]
     shards = [(((0, 0, 0, rows),), own)]
     up = down = own
+    beside = None
+    cotangents = [cotangent]
     for step in range(1, reach + 1):
         up = around(up, 1)
+        if step < reach:
+            down = around(down, -1)
+        if step <= len(stages):
+            up, down, beside = lax.optimization_barrier((up, down, stages[step - 1](beside)))
+        elif step == len(stages) + 1:
+            others = [swapped(cotangent, "col", partner) for partner in range(2, lax.axis_size("col"), 2)]
+            up, down, others = lax.optimization_barrier((up, down, others))
+            cotangents += others
         shards.append((((-step, 0, 0, rows),), up))
         if step < reach:
-            down = around(down, -1)
             shards.append((((step, 0, 0, rows),), down))
-        if step == 1:
-            up, down, beside = lax.optimization_barrier((up, down, beside))
-    return shards, beside
+    return shards, beside, cotangents
 
 
 def added(first, second):
@@ -393,8 +475,7 @@
     above, below, terms = backward_product(dense, own, sibling, chunk, first, row_count, col_count)
     above, below, terms, cell = lax.optimization_barrier((above, below, terms, dense))
     up, down = around(above, 1), around(below, -1)
-    up, down, opposite = lax.optimization_barrier((up, down, around(terms, reach)))
-    all_terms = [(0, 0, terms), (reach, 0, opposite)]
+    all_terms = [(0, 0, terms)]
 
     ups = tuple((offset, "zeros" if offset > 1 else "") for offset in range(reach - 1, 0, -1))
     downs = tuple((-offset, "zeros") for offset in range(reach - 2, 0, -1))
@@ -405,6 +486,9 @@
         up = around(added(ups[step - 1], up), 1)
         if step < reach - 1:
             down = around(added(downs[step - 1], down), -1)
+        if step == 1:
+            up, down, opposite = lax.optimization_barrier((up, down, around(terms, reach)))
+            all_terms.append((reach, 0, opposite))
     chunk = summed_terms(all_terms, size)
     chunks = [chunk] + [swapped(chunk, "col", partner) for partner in range(1, col_count)]
     return [mine, up, down], chunks
@@ -414,13 +498,12 @@
     node_rows, width = features.shape
     capacity, side = adj_tiles.shape[2:4]
     tiles = adj_tiles.reshape(capacity, side, side)
-    packed = ((tile_counts[:, :, None] << 16) | (tile_rows << 8) | tile_cols).reshape(capacity)
+    packed = jnp.concatenate([tile_rows, tile_cols, tile_counts[:, :, None]], axis=2).reshape(2 * capacity + 1)
     row_count = lax.axis_size("row")
     col_count = lax.axis_size("col")
     per_strip = node_rows // side
-    dense = build_dense(packed, tiles, col_count * per_strip, row_count * per_strip, per_strip)
-    cotangents = [out_grad] + [swapped(out_grad, "col", partner) for partner in range(2, col_count, 2)]
-    shards, (dense, cotangents) = gathered_shards(features, (dense, cotangents))
+    stages = build_stages(packed, tiles, col_count * per_strip, row_count * per_strip, per_strip)
+    shards, dense, cotangents = gathered_shards(features, stages, out_grad)
 
     for_sibling = forward_product(dense, shards, 1, row_count, col_count)
     for_sibling, cell = lax.optimization_barrier((for_sibling, dense))

time: 72.2 us -> 70.6 us (0.978); the launches traced: 72.7 us -> 69.5 us
  starting transfers between devices: 30.2 us -> 24.1 us
  Pallas kernels: 8.13 us -> 11.9 us
  waiting for transfers between devices: 31.9 us -> 31 us
    ppermute x15, starting transfers between devices: 25 us -> 18.5 us  [around(): lax.ppermute(value, 'row', [(order[i], order[(i + step) % count]) for i i...]
    pallas_call x1 -> x2, Pallas kernels: 3.11 us -> 6.84 us  [the longest x1 3.44 us: build_stages(): pl.pallas_call(functools.partial(build_first_kernel, blocks=blocks), out_...]
    ppermute x15, waiting for transfers between devices: 19.1 us -> 17.7 us  [around(): lax.ppermute(value, 'row', [(order[i], order[(i + step) % count]) for i i...]
  transfers between devices with their start and end apart: 22 -> 22, of which waited for: 13 -> 12; matrix products, arithmetic and copies ran while one was open for 1% -> 1% of each run, Pallas kernels for 7% -> 13%
where the time goes in v7:
time: 70.6 us; the launch traced here: 69.5 us
  waiting for transfers between devices  31 us (44%)
  starting transfers between devices  24.1 us (34%)
  Pallas kernels  11.9 us (17%)
  between operations  1.48 us (2%)
  other arithmetic  0.99 us (1%)
    ppermute x15, starting transfers between devices, around(): lax.ppermute(value, 'row', [(order[i], order[(i + step) % count]) for i i...  18.5 us
    ppermute x15, waiting for transfers between devices, around(): lax.ppermute(value, 'row', [(order[i], order[(i + step) % count]) for i i...  17.7 us
    ppermute x7, waiting for transfers between devices, swapped(): lax.ppermute(value, axis, [(i, i ^ partner) for i in range(lax.axis_size(...  13.3 us
    ppermute x7, starting transfers between devices, swapped(): lax.ppermute(value, axis, [(i, i ^ partner) for i in range(lax.axis_size(...  5.59 us
    pallas_call x1, Pallas kernels, build_stages(): pl.pallas_call(functools.partial(build_first_kernel, blocks=blocks), out_...  3.44 us
    pallas_call x1, Pallas kernels, build_stages(): pl.pallas_call(functools.partial(build_rest_kernel, blocks=blocks), out_s...  3.4 us
    pallas_call x2, Pallas kernels, backward_product(): pl.pallas_call(functools.partial(backward_kernel, outputs=outputs, row_co...  1.72 us
    pallas_call x2, Pallas kernels, forward_product(): pl.pallas_call(functools.partial(forward_kernel, pieces=pieces, sibling=s...  1.42 us
  transfers between devices with their start and end apart: 22, of which 12 were waited for; matrix products, arithmetic and copies ran while one was open for 1% of the time, Pallas kernels for 13%

profile of v7, /device:TPU:0, one launch (start us, length us, event | category | flops | bytes accessed | tf_op | source)
XLA Modules:
  0.0 69.5 jit_solution(10922966719966961080)
XLA Ops:
  0.6 3.1 %collective-permute-start = (bf16[256,256]{1,0:T(8,128)(2,1)}, bf16[256,256]{1,0:T(8,128)(2,1)S(1)}, u32[]{:S(2)}, u32[]{:S(2)}) collective-permute-start(bf16[256,256]{1,0:T(8,128)(2,1)} %refs_0_.3), channel_id=1, source_target_pairs={{0,8},{8,16},{16,24},{24,28},{28,20},{20,12},{12,4},{4,0},{1,9},{9... | collective-permute-start | bytes 393224 | tf_op jit(solution)/shard_map/ppermute | solution.py:436
  3.7 0.0 collective-permute-start.1
  4.4 0.7 %add_reduce_fusion.list_ref = s32[513]{0:T(1024)S(1)} fusion(s32[1,1,1]{2,1,0:T(1,128)} %bitcast.2, s32[1,1,256]{2,1,0:T(1,128)} %param.11, s32[1,1,256]{2,1,0:T(1,128)} %param.10), kind=kLoop, calls=%fused_computation.6 | loop fusion | flops 1026 | bytes 4104 | tf_op jit(solution)/shard_map/concatenate | solution.py:501
  5.1 0.0 copy-start.2
  5.1 3.4 %build_first.1.half_ref = bf16[1024,2048]{1,0:T(8,128)(2,1)S(1)} custom-call(s32[513]{0:T(1024)S(1)} %add_reduce_fusion.list_ref, bf16[256,128,128]{2,1,0:T(8,128)(2,1)} %bitcast.3), custom_call_target="tpu_custom_call" | custom-call | flops 4194304 | bytes 6291456 | tf_op jit(solution)/shard_map/build_first/pallas_call | solution.py:174
  8.5 0.0 copy-start
  8.6 0.0 collective-permute-done.refs_1_
  8.6 0.3 collective-permute-done.1.refs_2_
  8.9 1.6 %collective-permute-start.2 = (bf16[256,256]{1,0:T(8,128)(2,1)S(1)}, bf16[256,256]{1,0:T(8,128)(2,1)S(1)}, u32[]{:S(2)}, u32[]{:S(2)}) collective-permute-start(bf16[256,256]{1,0:T(8,128)(2,1)S(1)} %collective-permute-done.refs_1_), channel_id=1, source_target_pairs={{0,8},{8,16},{16,24},{24,28},{28,20},{20,12},{12,4},{4,0},{1,9},{9... | collective-permute-start | bytes 393224 | tf_op jit(solution)/shard_map/ppermute | solution.py:436
  10.5 0.4 collective-permute-start.3
  10.9 0.0 copy-done.2
  10.9 2.4 %collective-permute-start.6 = (bf16[256,256]{1,0:T(8,128)(2,1)S(1)}, bf16[256,256]{1,0:T(8,128)(2,1)S(1)}, u32[]{:S(2)}, u32[]{:S(2)}) collective-permute-start(bf16[256,256]{1,0:T(8,128)(2,1)S(1)} %copy-done.2), channel_id=1, source_target_pairs={{0,2},{1,3},{2,0},{3,1},{4,6},{5,7},{6,4},{7,5},{8,10},{9,11},{10,... | collective-permute-start | bytes 393224 | tf_op jit(solution)/shard_map/ppermute | solution.py:440
  13.3 3.4 %build_rest.1.dense_ref = bf16[1024,2048]{1,0:T(8,128)(2,1)S(1)} custom-call(s32[513]{0:T(1024)S(1)} %add_reduce_fusion.list_ref, bf16[256,128,128]{2,1,0:T(8,128)(2,1)} %bitcast.4, bf16[1024,2048]{1,0:T(8,128)(2,1)S(1)} %build_first.1.half_ref), custom_call_target="tpu_custom_call" | custom-call | flops 4194304 | bytes 6291456 | tf_op jit(solution)/shard_map/build_rest/pallas_call | solution.py:184
  16.8 0.0 collective-permute-done.2.refs_3_
  16.8 0.0 collective-permute-done.3.refs_4_
  16.8 0.7 %collective-permute-start.4 = (bf16[256,256]{1,0:T(8,128)(2,1)S(1)}, bf16[256,256]{1,0:T(8,128)(2,1)S(1)}, u32[]{:S(2)}, u32[]{:S(2)}) collective-permute-start(bf16[256,256]{1,0:T(8,128)(2,1)S(1)} %collective-permute-done.2.refs_3_), channel_id=1, source_target_pairs={{0,8},{8,16},{16,24},{24,28},{28,20},{20,12},{12,4},{4,0},{1,9},{9... | collective-permute-start | bytes 393224 | tf_op jit(solution)/shard_map/ppermute | solution.py:436
  17.5 1.4 %collective-permute-start.5 = (bf16[256,256]{1,0:T(8,128)(2,1)S(1)}, bf16[256,256]{1,0:T(8,128)(2,1)S(1)}, u32[]{:S(2)}, u32[]{:S(2)}) collective-permute-start(bf16[256,256]{1,0:T(8,128)(2,1)S(1)} %collective-permute-done.3.refs_4_), channel_id=1, source_target_pairs={{0,4},{8,0},{16,8},{24,16},{28,24},{20,28},{12,20},{4,12},{1,5},{9... | collective-permute-start | bytes 393224 | tf_op jit(solution)/shard_map/ppermute | solution.py:436
  18.9 0.0 collective-permute-done.6.refs_4_
  18.9 2.9 %collective-permute-done.4.refs_5_ = bf16[256,256]{1,0:T(8,128)(2,1)S(1)} collective-permute-done((bf16[256,256]{1,0:T(8,128)(2,1)S(1)}, bf16[256,256]{1,0:T(8,128)(2,1)S(1)}, u32[]{:S(2)}, u32[]{:S(2)}) %collective-permute-start.4) | collective-permute-done | bytes 131104 | tf_op jit(solution)/shard_map/ppermute | solution.py:436
  21.8 0.7 collective-permute-done.5.refs_6_
  22.5 2.0 %collective-permute-start.7 = (bf16[256,256]{1,0:T(8,128)(2,1)S(1)}, bf16[256,256]{1,0:T(8,128)(2,1)S(1)}, u32[]{:S(2)}, u32[]{:S(2)}) collective-permute-start(bf16[256,256]{1,0:T(8,128)(2,1)S(1)} %collective-permute-done.4.refs_5_), channel_id=1, source_target_pairs={{0,8},{8,16},{16,24},{24,28},{28,20},{20,12},{12,4},{4,0},{1,9},{9... | collective-permute-start | bytes 393224 | tf_op jit(solution)/shard_map/ppermute | solution.py:436
  24.5 2.9 %collective-permute-done.7.refs_7_ = bf16[256,256]{1,0:T(8,128)(2,1)S(1)} collective-permute-done((bf16[256,256]{1,0:T(8,128)(2,1)S(1)}, bf16[256,256]{1,0:T(8,128)(2,1)S(1)}, u32[]{:S(2)}, u32[]{:S(2)}) %collective-permute-start.7) | collective-permute-done | bytes 131104 | tf_op jit(solution)/shard_map/ppermute | solution.py:436
  27.4 0.0 copy-done
  27.4 0.7 %forward_product.2 = bf16[512,256]{1,0:T(8,128)(2,1)S(1)} custom-call(bf16[1024,2048]{1,0:T(8,128)(2,1)S(1)} %build_rest.1.dense_ref, bf16[256,256]{1,0:T(8,128)(2,1)S(1)} %copy-done, bf16[256,256]{1,0:T(8,128)(2,1)S(1)} %collective-permute-done.refs_1_, bf16[256,256]{1,0:T(8,128)(2,1)S(1)} %collective-permute-done.1.refs_2_, ...), custom_call_target="tpu_custom_call" | custom-call | flops 536870912 | bytes 3407872 | tf_op jit(solution)/shard_map/forward_product/pallas_call | solution.py:236
  28.1 0.0 copy-start.1
  28.2 0.1 collective-permute-start.8
  28.2 0.7 %forward_product.3 = bf16[512,256]{1,0:T(8,128)(2,1)S(1)} custom-call(bf16[1024,2048]{1,0:T(8,128)(2,1)S(1)} %build_rest.1.dense_ref, bf16[256,256]{1,0:T(8,128)(2,1)S(1)} %copy-done, bf16[256,256]{1,0:T(8,128)(2,1)S(1)} %collective-permute-done.refs_1_, bf16[256,256]{1,0:T(8,128)(2,1)S(1)} %collective-permute-done.1.refs_2_, ...), custom_call_target="tpu_custom_call" | custom-call | flops 536870912 | bytes 3407872 | tf_op jit(solution)/shard_map/forward_product/pallas_call | solution.py:236
  28.9 0.8 %collective-permute-done.8 = bf16[512,256]{1,0:T(8,128)(2,1)S(1)} collective-permute-done((bf16[512,256]{1,0:T(8,128)(2,1)S(1)}, bf16[512,256]{1,0:T(8,128)(2,1)S(1)}, u32[]{:S(2)}, u32[]{:S(2)}) %collective-permute-start.8) | collective-permute-done | bytes 262176 | tf_op jit(solution)/shard_map/ppermute | solution.py:440
  29.8 0.1 add_convert_fusion.refs_0_
  29.8 1.1 %collective-permute-start.9 = (bf16[512,256]{1,0:T(8,128)(2,1)S(1)}, bf16[512,256]{1,0:T(8,128)(2,1)S(1)}, u32[]{:S(2)}, u32[]{:S(2)}) collective-permute-start(bf16[512,256]{1,0:T(8,128)(2,1)S(1)} %add_convert_fusion.refs_0_), channel_id=1, source_target_pairs={{0,2},{1,3},{2,0},{3,1},{4,6},{5,7},{6,4},{7,5},{8,10},{9,11},{10,... | collective-permute-start | bytes 786440 | tf_op jit(solution)/shard_map/ppermute | solution.py:440
  30.9 7.3 %collective-permute-done.9.refs_1_ = bf16[512,256]{1,0:T(8,128)(2,1)S(1)} collective-permute-done((bf16[512,256]{1,0:T(8,128)(2,1)S(1)}, bf16[512,256]{1,0:T(8,128)(2,1)S(1)}, u32[]{:S(2)}, u32[]{:S(2)}) %collective-permute-start.9) | collective-permute-done | bytes 262176 | tf_op jit(solution)/shard_map/ppermute | solution.py:440
  38.2 0.0 copy-done.1
  38.2 1.0 %middle.1 = (bf16[256,256]{1,0:T(8,128)(2,1)}, bf16[640,256]{1,0:T(8,128)(2,1)S(1)}, f32[64,256]{1,0:T(8,128)S(1)}) custom-call(bf16[512,256]{1,0:T(8,128)(2,1)S(1)} %add_convert_fusion.refs_0_, bf16[512,256]{1,0:T(8,128)(2,1)S(1)} %collective-permute-done.9.refs_1_, bf16[256,256]{1,0:T(8,128)(2,1)S(1)} %copy-done.1, bf16[256,256]{1,0:T(8,128)(2,1)S(1)} %copy-done.2, ...), custom_call_target="tpu_custom_call" | custom-call | flops 335544320 | bytes 1572864 | tf_op jit(solution)/shard_map/middle/pallas_call | solution.py:293
  39.3 0.1 collective-permute-start.10
  39.3 1.6 %collective-permute-done.10.sibling_ref = bf16[640,256]{1,0:T(8,128)(2,1)S(1)} collective-permute-done((bf16[640,256]{1,0:T(8,128)(2,1)S(1)}, bf16[640,256]{1,0:T(8,128)(2,1)S(1)}, u32[]{:S(2)}, u32[]{:S(2)}) %collective-permute-start.10) | collective-permute-done | bytes 327712 | tf_op jit(solution)/shard_map/ppermute | solution.py:440
  40.9 0.6 backward_product.2
  41.5 1.4 %collective-permute-start.13 = (bf16[320,256]{1,0:T(8,128)(2,1)S(1)}, bf16[320,256]{1,0:T(8,128)(2,1)S(1)}, u32[]{:S(2)}, u32[]{:S(2)}) collective-permute-start(bf16[320,256]{1,0:T(8,128)(2,1)S(1)} %get-tuple-element.59), channel_id=1, source_target_pairs={{0,4},{8,0},{16,8},{24,16},{28,24},{20,28},{12,20},{4,12},{1,5},{9... | collective-permute-start | bytes 491528 | tf_op jit(solution)/shard_map/ppermute | solution.py:436
  43.0 0.7 %collective-permute-start.11 = (bf16[320,256]{1,0:T(8,128)(2,1)S(1)}, bf16[320,256]{1,0:T(8,128)(2,1)S(1)}, u32[]{:S(2)}, u32[]{:S(2)}) collective-permute-start(bf16[320,256]{1,0:T(8,128)(2,1)S(1)} %get-tuple-element.57), channel_id=1, source_target_pairs={{0,8},{8,16},{16,24},{24,28},{28,20},{20,12},{12,4},{4,0},{1,9},{9... | collective-permute-start | bytes 491528 | tf_op jit(solution)/shard_map/ppermute | solution.py:436
  43.7 1.1 %backward_product.3 = (bf16[320,256]{1,0:T(8,128)(2,1)S(1)}, bf16[320,256]{1,0:T(8,128)(2,1)S(1)}, bf16[256,256]{1,0:T(8,128)(2,1)S(1)}, bf16[320,256]{1,0:T(8,1...) custom-call(bf16[1024,2048]{1,0:T(8,128)(2,1)S(1)} %build_rest.1.dense_ref, ...), custom_call_target="tpu_custom_call" | custom-call | flops 134217728 | bytes 786432 | tf_op jit(solution)/shard_map/backward_product/pallas_call | solution.py:355
  44.8 3.3 %collective-permute-done.13.refs_2_ = bf16[320,256]{1,0:T(8,128)(2,1)S(1)} collective-permute-done((bf16[320,256]{1,0:T(8,128)(2,1)S(1)}, bf16[320,256]{1,0:T(8,128)(2,1)S(1)}, u32[]{:S(2)}, u32[]{:S(2)}) %collective-permute-start.13) | collective-permute-done | bytes 163872 | tf_op jit(solution)/shard_map/ppermute | solution.py:436
  48.2 1.1 %collective-permute-start.14 = (bf16[320,256]{1,0:T(8,128)(2,1)S(1)}, bf16[320,256]{1,0:T(8,128)(2,1)S(1)}, u32[]{:S(2)}, u32[]{:S(2)}) collective-permute-start(bf16[320,256]{1,0:T(8,128)(2,1)S(1)} %add_convert_fusion.3), channel_id=1, source_target_pairs={{0,4},{8,0},{16,8},{24,16},{28,24},{20,28},{12,20},{4,12},{1,5},{9... | collective-permute-start | bytes 491528 | tf_op jit(solution)/shard_map/ppermute | solution.py:436
  49.3 0.0 collective-permute-done.11.refs_1_
  49.4 1.0 %collective-permute-start.12 = (bf16[320,256]{1,0:T(8,128)(2,1)S(1)}, bf16[320,256]{1,0:T(8,128)(2,1)S(1)}, u32[]{:S(2)}, u32[]{:S(2)}) collective-permute-start(bf16[320,256]{1,0:T(8,128)(2,1)S(1)} %add_convert_fusion.4), channel_id=1, source_target_pairs={{0,8},{8,16},{16,24},{24,28},{28,20},{20,12},{12,4},{4,0},{1,9},{9... | collective-permute-start | bytes 491528 | tf_op jit(solution)/shard_map/ppermute | solution.py:436
  50.3 2.8 %collective-permute-start.15 = (bf16[64,256]{1,0:T(8,128)(2,1)S(1)}, bf16[64,256]{1,0:T(8,128)(2,1)S(1)}, u32[]{:S(2)}, u32[]{:S(2)}) collective-permute-start(bf16[64,256]{1,0:T(8,128)(2,1)S(1)} %get-tuple-element.60.refs_0_), channel_id=1, source_target_pairs={{0,28},{8,20},{16,12},{24,4},{28,0},{20,8},{12,16},{4,24},{1,29},{... | collective-permute-start | bytes 98312 | tf_op jit(solution)/shard_map/ppermute | solution.py:436
  53.2 4.0 %collective-permute-done.15.refs_3_ = bf16[64,256]{1,0:T(8,128)(2,1)S(1)} collective-permute-done((bf16[64,256]{1,0:T(8,128)(2,1)S(1)}, bf16[64,256]{1,0:T(8,128)(2,1)S(1)}, u32[]{:S(2)}, u32[]{:S(2)}) %collective-permute-start.15) | collective-permute-done | bytes 32800 | tf_op jit(solution)/shard_map/ppermute | solution.py:436
  57.1 0.0 collective-permute-done.14.refs_5_
  57.2 0.0 collective-permute-done.12.refs_4_
  57.2 0.1 collective-permute-start.16
  57.3 2.1 %collective-permute-start.18 = (bf16[320,256]{1,0:T(8,128)(2,1)S(1)}, bf16[320,256]{1,0:T(8,128)(2,1)S(1)}, u32[]{:S(2)}, u32[]{:S(2)}) collective-permute-start(bf16[320,256]{1,0:T(8,128)(2,1)S(1)} %add_convert_fusion.1), channel_id=1, source_target_pairs={{0,4},{8,0},{16,8},{24,16},{28,24},{20,28},{12,20},{4,12},{1,5},{9... | collective-permute-start | bytes 491528 | tf_op jit(solution)/shard_map/ppermute | solution.py:436
  59.4 3.5 %collective-permute-done.16.refs_6_ = bf16[320,256]{1,0:T(8,128)(2,1)S(1)} collective-permute-done((bf16[320,256]{1,0:T(8,128)(2,1)S(1)}, bf16[320,256]{1,0:T(8,128)(2,1)S(1)}, u32[]{:S(2)}, u32[]{:S(2)}) %collective-permute-start.16) | collective-permute-done | bytes 163872 | tf_op jit(solution)/shard_map/ppermute | solution.py:436
  63.0 0.1 collective-permute-start.17
  63.0 0.0 collective-permute-done.18.refs_7_.refs_2_
  63.0 0.1 summed_terms.1.refs_3_
  63.1 0.1 collective-permute-start.19
  63.2 0.8 %collective-permute-start.20 = (f32[64,256]{1,0:T(8,128)S(1)}, f32[64,256]{1,0:T(8,128)S(1)}, u32[]{:S(2)}, u32[]{:S(2)}) collective-permute-start(f32[64,256]{1,0:T(8,128)S(1)} %summed_terms.1.refs_3_), channel_id=1, source_target_pairs={{0,2},{1,3},{2,0},{3,1},{4,6},{5,7},{6,4},{7,5},{8,10},{9,11},{10,... | collective-permute-start | bytes 196616 | tf_op jit(solution)/shard_map/ppermute | solution.py:440
  64.1 1.0 %collective-permute-start.21 = (f32[64,256]{1,0:T(8,128)S(1)}, f32[64,256]{1,0:T(8,128)S(1)}, u32[]{:S(2)}, u32[]{:S(2)}) collective-permute-start(f32[64,256]{1,0:T(8,128)S(1)} %summed_terms.1.refs_3_), channel_id=1, source_target_pairs={{0,3},{1,2},{2,1},{3,0},{4,7},{5,6},{6,5},{7,4},{8,11},{9,10},{10,... | collective-permute-start | bytes 196616 | tf_op jit(solution)/shard_map/ppermute | solution.py:440
  65.1 0.0 collective-permute-done.19.refs_4_
  65.1 3.1 %collective-permute-done.20.refs_5_ = f32[64,256]{1,0:T(8,128)S(1)} collective-permute-done((f32[64,256]{1,0:T(8,128)S(1)}, f32[64,256]{1,0:T(8,128)S(1)}, u32[]{:S(2)}, u32[]{:S(2)}) %collective-permute-start.20) | collective-permute-done | bytes 65568 | tf_op jit(solution)/shard_map/ppermute | solution.py:440
  68.2 0.5 collective-permute-done.21.refs_6_
  68.7 0.0 collective-permute-done.17.refs_1_
  68.7 0.8 %finish.1 = (bf16[256,256]{1,0:T(8,128)(2,1)}, f32[256,256]{1,0:T(8,128)}) custom-call(bf16[256,256]{1,0:T(8,128)(2,1)S(1)} %get-tuple-element.53.refs_0_, bf16[256,256]{1,0:T(8,128)(2,1)S(1)} %collective-permute-done.17.refs_1_, bf16[320,256]{1,0:T(8,128)(2,1)S(1)} %collective-permute-done.18.refs_7_.refs_2_, f32[64,256]{1,0:T(8,128)S(1)} %summed_terms.1.refs_3_, ...), custom_call_target="tpu_custom_call" | custom-call | flops 196608 | bytes 1048576 | tf_op jit(solution)/shard_map/finish/pallas_call | solution.py:417
  (5 shorter events, 0.2 us)
Async XLA Ops:
  0.6 7.9 %collective-permute-start = (bf16[256,256]{1,0:T(8,128)(2,1)}, bf16[256,256]{1,0:T(8,128)(2,1)S(1)}, u32[]{:S(2)}, u32[]{:S(2)}) collective-permute-start(bf16[256,256]{1,0:T(8,128)(2,1)} %refs_0_.3), channel_id=1, source_target_pairs={{0,8},{8,16},{16,24},{24,28},{28,20},{20,12},{12,4},{4,0},{1,9},{9... | collective-permute-start | bytes 393224 | tf_op jit(solution)/shard_map/ppermute | solution.py:436
  3.7 5.2 %collective-permute-start.1 = (bf16[256,256]{1,0:T(8,128)(2,1)}, bf16[256,256]{1,0:T(8,128)(2,1)S(1)}, u32[]{:S(2)}, u32[]{:S(2)}) collective-permute-start(bf16[256,256]{1,0:T(8,128)(2,1)} %refs_0_.3), channel_id=1, source_target_pairs={{0,4},{8,0},{16,8},{24,16},{28,24},{20,28},{12,20},{4,12},{1,5},{9... | collective-permute-start | bytes 393224 | tf_op jit(solution)/shard_map/ppermute | solution.py:436
  5.1 5.8 %copy-start.2 = (bf16[256,256]{1,0:T(8,128)(2,1)S(1)}, bf16[256,256]{1,0:T(8,128)(2,1)}, u32[]{:S(2)}) copy-start(bf16[256,256]{1,0:T(8,128)(2,1)} %refs_3_.1) | copy-start | bytes 393220
  8.5 18.9 %copy-start = (bf16[256,256]{1,0:T(8,128)(2,1)S(1)}, bf16[256,256]{1,0:T(8,128)(2,1)}, u32[]{:S(2)}) copy-start(bf16[256,256]{1,0:T(8,128)(2,1)} %refs_0_.3) | copy-start | bytes 393220
  8.9 7.9 %collective-permute-start.2 = (bf16[256,256]{1,0:T(8,128)(2,1)S(1)}, bf16[256,256]{1,0:T(8,128)(2,1)S(1)}, u32[]{:S(2)}, u32[]{:S(2)}) collective-permute-start(bf16[256,256]{1,0:T(8,128)(2,1)S(1)} %collective-permute-done.refs_1_), channel_id=1, source_target_pairs={{0,8},{8,16},{16,24},{24,28},{28,20},{20,12},{12,4},{4,0},{1,9},{9... | collective-permute-start | bytes 393224 | tf_op jit(solution)/shard_map/ppermute | solution.py:436
  10.5 6.3 %collective-permute-start.3 = (bf16[256,256]{1,0:T(8,128)(2,1)S(1)}, bf16[256,256]{1,0:T(8,128)(2,1)S(1)}, u32[]{:S(2)}, u32[]{:S(2)}) collective-permute-start(bf16[256,256]{1,0:T(8,128)(2,1)S(1)} %collective-permute-done.1.refs_2_), channel_id=1, source_target_pairs={{0,4},{8,0},{16,8},{24,16},{28,24},{20,28},{12,20},{4,12},{1,5},{9... | collective-permute-start | bytes 393224 | tf_op jit(solution)/shard_map/ppermute | solution.py:436
  10.9 7.9 %collective-permute-start.6 = (bf16[256,256]{1,0:T(8,128)(2,1)S(1)}, bf16[256,256]{1,0:T(8,128)(2,1)S(1)}, u32[]{:S(2)}, u32[]{:S(2)}) collective-permute-start(bf16[256,256]{1,0:T(8,128)(2,1)S(1)} %copy-done.2), channel_id=1, source_target_pairs={{0,2},{1,3},{2,0},{3,1},{4,6},{5,7},{6,4},{7,5},{8,10},{9,11},{10,... | collective-permute-start | bytes 393224 | tf_op jit(solution)/shard_map/ppermute | solution.py:440
  16.8 5.0 %collective-permute-start.4 = (bf16[256,256]{1,0:T(8,128)(2,1)S(1)}, bf16[256,256]{1,0:T(8,128)(2,1)S(1)}, u32[]{:S(2)}, u32[]{:S(2)}) collective-permute-start(bf16[256,256]{1,0:T(8,128)(2,1)S(1)} %collective-permute-done.2.refs_3_), channel_id=1, source_target_pairs={{0,8},{8,16},{16,24},{24,28},{28,20},{20,12},{12,4},{4,0},{1,9},{9... | collective-permute-start | bytes 393224 | tf_op jit(solution)/shard_map/ppermute | solution.py:436
  17.5 5.0 %collective-permute-start.5 = (bf16[256,256]{1,0:T(8,128)(2,1)S(1)}, bf16[256,256]{1,0:T(8,128)(2,1)S(1)}, u32[]{:S(2)}, u32[]{:S(2)}) collective-permute-start(bf16[256,256]{1,0:T(8,128)(2,1)S(1)} %collective-permute-done.3.refs_4_), channel_id=1, source_target_pairs={{0,4},{8,0},{16,8},{24,16},{28,24},{20,28},{12,20},{4,12},{1,5},{9... | collective-permute-start | bytes 393224 | tf_op jit(solution)/shard_map/ppermute | solution.py:436
  22.5 5.0 %collective-permute-start.7 = (bf16[256,256]{1,0:T(8,128)(2,1)S(1)}, bf16[256,256]{1,0:T(8,128)(2,1)S(1)}, u32[]{:S(2)}, u32[]{:S(2)}) collective-permute-start(bf16[256,256]{1,0:T(8,128)(2,1)S(1)} %collective-permute-done.4.refs_5_), channel_id=1, source_target_pairs={{0,8},{8,16},{16,24},{24,28},{28,20},{20,12},{12,4},{4,0},{1,9},{9... | collective-permute-start | bytes 393224 | tf_op jit(solution)/shard_map/ppermute | solution.py:436
  28.1 10.1 %copy-start.1 = (bf16[256,256]{1,0:T(8,128)(2,1)S(1)}, bf16[256,256]{1,0:T(8,128)(2,1)}, u32[]{:S(2)}) copy-start(bf16[256,256]{1,0:T(8,128)(2,1)} %refs_2_.1) | copy-start | bytes 393220
  28.2 1.6 %collective-permute-start.8 = (bf16[512,256]{1,0:T(8,128)(2,1)S(1)}, bf16[512,256]{1,0:T(8,128)(2,1)S(1)}, u32[]{:S(2)}, u32[]{:S(2)}) collective-permute-start(bf16[512,256]{1,0:T(8,128)(2,1)S(1)} %forward_product.2), channel_id=1, source_target_pairs={{0,1},{1,0},{2,3},{3,2},{4,5},{5,4},{6,7},{7,6},{8,9},{9,8},{10,11... | collective-permute-start | bytes 786440 | tf_op jit(solution)/shard_map/ppermute | solution.py:440
  29.8 8.4 %collective-permute-start.9 = (bf16[512,256]{1,0:T(8,128)(2,1)S(1)}, bf16[512,256]{1,0:T(8,128)(2,1)S(1)}, u32[]{:S(2)}, u32[]{:S(2)}) collective-permute-start(bf16[512,256]{1,0:T(8,128)(2,1)S(1)} %add_convert_fusion.refs_0_), channel_id=1, source_target_pairs={{0,2},{1,3},{2,0},{3,1},{4,6},{5,7},{6,4},{7,5},{8,10},{9,11},{10,... | collective-permute-start | bytes 786440 | tf_op jit(solution)/shard_map/ppermute | solution.py:440
  39.3 1.7 %collective-permute-start.10 = (bf16[640,256]{1,0:T(8,128)(2,1)S(1)}, bf16[640,256]{1,0:T(8,128)(2,1)S(1)}, u32[]{:S(2)}, u32[]{:S(2)}) collective-permute-start(bf16[640,256]{1,0:T(8,128)(2,1)S(1)} %get-tuple-element.47.own_ref), channel_id=1, source_target_pairs={{0,1},{1,0},{2,3},{3,2},{4,5},{5,4},{6,7},{7,6},{8,9},{9,8},{10,11... | collective-permute-start | bytes 983048 | tf_op jit(solution)/shard_map/ppermute | solution.py:440
  41.5 6.6 %collective-permute-start.13 = (bf16[320,256]{1,0:T(8,128)(2,1)S(1)}, bf16[320,256]{1,0:T(8,128)(2,1)S(1)}, u32[]{:S(2)}, u32[]{:S(2)}) collective-permute-start(bf16[320,256]{1,0:T(8,128)(2,1)S(1)} %get-tuple-element.59), channel_id=1, source_target_pairs={{0,4},{8,0},{16,8},{24,16},{28,24},{20,28},{12,20},{4,12},{1,5},{9... | collective-permute-start | bytes 491528 | tf_op jit(solution)/shard_map/ppermute | solution.py:436
  43.0 6.3 %collective-permute-start.11 = (bf16[320,256]{1,0:T(8,128)(2,1)S(1)}, bf16[320,256]{1,0:T(8,128)(2,1)S(1)}, u32[]{:S(2)}, u32[]{:S(2)}) collective-permute-start(bf16[320,256]{1,0:T(8,128)(2,1)S(1)} %get-tuple-element.57), channel_id=1, source_target_pairs={{0,8},{8,16},{16,24},{24,28},{28,20},{20,12},{12,4},{4,0},{1,9},{9... | collective-permute-start | bytes 491528 | tf_op jit(solution)/shard_map/ppermute | solution.py:436
  48.2 9.0 %collective-permute-start.14 = (bf16[320,256]{1,0:T(8,128)(2,1)S(1)}, bf16[320,256]{1,0:T(8,128)(2,1)S(1)}, u32[]{:S(2)}, u32[]{:S(2)}) collective-permute-start(bf16[320,256]{1,0:T(8,128)(2,1)S(1)} %add_convert_fusion.3), channel_id=1, source_target_pairs={{0,4},{8,0},{16,8},{24,16},{28,24},{20,28},{12,20},{4,12},{1,5},{9... | collective-permute-start | bytes 491528 | tf_op jit(solution)/shard_map/ppermute | solution.py:436
  49.4 7.8 %collective-permute-start.12 = (bf16[320,256]{1,0:T(8,128)(2,1)S(1)}, bf16[320,256]{1,0:T(8,128)(2,1)S(1)}, u32[]{:S(2)}, u32[]{:S(2)}) collective-permute-start(bf16[320,256]{1,0:T(8,128)(2,1)S(1)} %add_convert_fusion.4), channel_id=1, source_target_pairs={{0,8},{8,16},{16,24},{24,28},{28,20},{20,12},{12,4},{4,0},{1,9},{9... | collective-permute-start | bytes 491528 | tf_op jit(solution)/shard_map/ppermute | solution.py:436
  50.3 6.8 %collective-permute-start.15 = (bf16[64,256]{1,0:T(8,128)(2,1)S(1)}, bf16[64,256]{1,0:T(8,128)(2,1)S(1)}, u32[]{:S(2)}, u32[]{:S(2)}) collective-permute-start(bf16[64,256]{1,0:T(8,128)(2,1)S(1)} %get-tuple-element.60.refs_0_), channel_id=1, source_target_pairs={{0,28},{8,20},{16,12},{24,4},{28,0},{20,8},{12,16},{4,24},{1,29},{... | collective-permute-start | bytes 98312 | tf_op jit(solution)/shard_map/ppermute | solution.py:436
  57.2 5.7 %collective-permute-start.16 = (bf16[320,256]{1,0:T(8,128)(2,1)S(1)}, bf16[320,256]{1,0:T(8,128)(2,1)S(1)}, u32[]{:S(2)}, u32[]{:S(2)}) collective-permute-start(bf16[320,256]{1,0:T(8,128)(2,1)S(1)} %add_convert_fusion.2), channel_id=1, source_target_pairs={{0,8},{8,16},{16,24},{24,28},{28,20},{20,12},{12,4},{4,0},{1,9},{9... | collective-permute-start | bytes 491528 | tf_op jit(solution)/shard_map/ppermute | solution.py:436
  57.3 5.7 %collective-permute-start.18 = (bf16[320,256]{1,0:T(8,128)(2,1)S(1)}, bf16[320,256]{1,0:T(8,128)(2,1)S(1)}, u32[]{:S(2)}, u32[]{:S(2)}) collective-permute-start(bf16[320,256]{1,0:T(8,128)(2,1)S(1)} %add_convert_fusion.1), channel_id=1, source_target_pairs={{0,4},{8,0},{16,8},{24,16},{28,24},{20,28},{12,20},{4,12},{1,5},{9... | collective-permute-start | bytes 491528 | tf_op jit(solution)/shard_map/ppermute | solution.py:436
  63.0 5.7 %collective-permute-start.17 = (bf16[256,256]{1,0:T(8,128)(2,1)S(1)}, bf16[256,256]{1,0:T(8,128)(2,1)S(1)}, u32[]{:S(2)}, u32[]{:S(2)}) collective-permute-start(bf16[256,256]{1,0:T(8,128)(2,1)S(1)} %add_convert_fusion.5), channel_id=1, source_target_pairs={{0,8},{8,16},{16,24},{24,28},{28,20},{20,12},{12,4},{4,0},{1,9},{9... | collective-permute-start | bytes 393224 | tf_op jit(solution)/shard_map/ppermute | solution.py:436
  63.1 1.9 %collective-permute-start.19 = (f32[64,256]{1,0:T(8,128)S(1)}, f32[64,256]{1,0:T(8,128)S(1)}, u32[]{:S(2)}, u32[]{:S(2)}) collective-permute-start(f32[64,256]{1,0:T(8,128)S(1)} %summed_terms.1.refs_3_), channel_id=1, source_target_pairs={{0,1},{1,0},{2,3},{3,2},{4,5},{5,4},{6,7},{7,6},{8,9},{9,8},{10,11... | collective-permute-start | bytes 196616 | tf_op jit(solution)/shard_map/ppermute | solution.py:440
  63.2 5.0 %collective-permute-start.20 = (f32[64,256]{1,0:T(8,128)S(1)}, f32[64,256]{1,0:T(8,128)S(1)}, u32[]{:S(2)}, u32[]{:S(2)}) collective-permute-start(f32[64,256]{1,0:T(8,128)S(1)} %summed_terms.1.refs_3_), channel_id=1, source_target_pairs={{0,2},{1,3},{2,0},{3,1},{4,6},{5,7},{6,4},{7,5},{8,10},{9,11},{10,... | collective-permute-start | bytes 196616 | tf_op jit(solution)/shard_map/ppermute | solution.py:440
  64.1 4.6 %collective-permute-start.21 = (f32[64,256]{1,0:T(8,128)S(1)}, f32[64,256]{1,0:T(8,128)S(1)}, u32[]{:S(2)}, u32[]{:S(2)}) collective-permute-start(f32[64,256]{1,0:T(8,128)S(1)} %summed_terms.1.refs_3_), channel_id=1, source_target_pairs={{0,3},{1,2},{2,1},{3,0},{4,7},{5,6},{6,5},{7,4},{8,11},{9,10},{10,... | collective-permute-start | bytes 196616 | tf_op jit(solution)/shard_map/ppermute | solution.py:440

commit v8 on v7

--- a/solution.py
+++ b/solution.py
@@ -19,7 +19,7 @@
     return sum(math.prod(shape) * jnp.dtype(kind).itemsize for shape, kind in shapes)
 
 
-def add_tiles(list_ref, tiles_ref, total, held, sems, begin, end, *, first_block, blocks, steps):
+def add_tiles(list_ref, tiles_ref, total, seen, held, sems, begin, end, *, base, first_block, blocks, steps):
     side = tiles_ref.shape[1]
     capacity = tiles_ref.shape[0]
     count = list_ref[2 * capacity]
@@ -37,6 +37,13 @@
         return carry
 
     lax.fori_loop(begin, jnp.minimum(end, begin + slots), start, 0)
+
+    def forget(index, carry):
+        for turn in range(8):
+            seen[index * 8 + turn] = 0
+        return carry
+
+    lax.fori_loop(0, seen.shape[0] // 8, forget, 0)
 
     def target(place):
         col = list_ref[capacity + place] - first_block
@@ -56,11 +63,16 @@
                 (pl.ds(pl.multiple_of(row * side, side), side), pl.ds(pl.multiple_of(col * side, side), side))
                 for row, col in spots
             ]
-            first, second = total[at[0]], total[at[1]]
+            first, second = (
+                jnp.where(seen[row * blocks + col] != 0, total[spot], base(row, col))
+                for (row, col), spot in zip(spots, at)
+            )
             tiles = [held[slot, lane + turn].astype(jnp.float32) for turn in range(2)]
             same = (spots[0][0] == spots[1][0]) & (spots[0][1] == spots[1][1])
             total[at[0]] = first + tiles[0]
             total[at[1]] = second + tiles[1] + jnp.where(same, tiles[0], 0.0)
+            for row, col in spots:
+                seen[row * blocks + col] = 1
 
         @pl.when(index + slots < end)
         def _():
@@ -68,12 +80,24 @@
 
         return carry
 
-    return lambda: lax.fori_loop(begin, end, chunk_step, 0)
-
-
-def each_row_block(total, side, action):
-    def step(block, carry):
-        action(pl.ds(pl.multiple_of(block * side, side), side))
+    lax.fori_loop(begin, end, chunk_step, 0)
+
+
+def round_blocks(dense_ref, total, seen, side, blocks, unseen):
+    def step(row, carry):
+        down = pl.ds(pl.multiple_of(row * side, side), side)
+        for col in range(blocks):
+            along = pl.ds(col * side, side)
+            touched = seen[row * blocks + col] != 0
+
+            @pl.when(touched)
+            def _():
+                dense_ref[down, along] = total[down, along].astype(jnp.bfloat16)
+
+            @pl.when(jnp.logical_not(touched))
+            def _():
+                dense_ref[down, along] = unseen(down, along)
+
         return carry
 
     lax.fori_loop(0, total.shape[0] // side - 1, step, 0)
@@ -83,54 +107,43 @@
     return (list_ref[2 * tiles_ref.shape[0]] + chunk_tiles - 1) // chunk_tiles
 
 
-def build_first_kernel(list_ref, tiles_ref, dense_ref, total, held, sems, *, blocks):
+def build_first_kernel(list_ref, tiles_ref, dense_ref, total, seen, held, sems, *, blocks):
+    side = tiles_ref.shape[1]
     half = (live_chunks(list_ref, tiles_ref) + 1) // 2
-    run = add_tiles(list_ref, tiles_ref, total, held, sems, 0, half, first_block=0, blocks=blocks, steps=1)
-
-    def clear(down):
-        total[down, :] = jnp.zeros((down.size, total.shape[1]), jnp.float32)
-
-    def rounded(down):
-        dense_ref[down, :] = total[down, :].astype(jnp.bfloat16)
-
-    each_row_block(total, tiles_ref.shape[1], clear)
-    run()
-    each_row_block(total, tiles_ref.shape[1], rounded)
-
-
-def build_rest_kernel(list_ref, tiles_ref, half_ref, dense_ref, total, held, sems, *, blocks):
+    add_tiles(
+        list_ref, tiles_ref, total, seen, held, sems, 0, half,
+        base=lambda row, col: 0.0, first_block=0, blocks=blocks, steps=1,
+    )
+    round_blocks(
+        dense_ref, total, seen, side, blocks, lambda down, along: jnp.zeros((side, side), jnp.bfloat16)
+    )
+
+
+def build_rest_kernel(list_ref, tiles_ref, half_ref, dense_ref, total, seen, held, sems, *, blocks):
+    side = tiles_ref.shape[1]
     chunks = live_chunks(list_ref, tiles_ref)
-    run = add_tiles(
-        list_ref, tiles_ref, total, held, sems, (chunks + 1) // 2, chunks, first_block=0, blocks=blocks, steps=1
-    )
-
-    def widened(down):
-        total[down, :] = half_ref[down, :].astype(jnp.float32)
-
-    def rounded(down):
-        dense_ref[down, :] = total[down, :].astype(jnp.bfloat16)
-
-    each_row_block(total, tiles_ref.shape[1], widened)
-    run()
-    each_row_block(total, tiles_ref.shape[1], rounded)
-
-
-def build_whole_kernel(list_ref, tiles_ref, dense_ref, total, held, sems, *, blocks, steps):
-    chunks = live_chunks(list_ref, tiles_ref)
-    first_block = pl.program_id(0) * blocks
-    run = add_tiles(
-        list_ref, tiles_ref, total, held, sems, 0, chunks, first_block=first_block, blocks=blocks, steps=steps
-    )
-
-    def clear(down):
-        total[down, :] = jnp.zeros((down.size, total.shape[1]), jnp.float32)
-
-    def rounded(down):
-        dense_ref[down, :] = total[down, :].astype(jnp.bfloat16)
-
-    each_row_block(total, tiles_ref.shape[1], clear)
-    run()
-    each_row_block(total, tiles_ref.shape[1], rounded)
+    last = half_ref.shape[0] // side - 1
+
+    def base(row, col):
+        down = pl.ds(pl.multiple_of(jnp.minimum(row, last) * side, side), side)
+        return half_ref[down, pl.ds(pl.multiple_of(col * side, side), side)].astype(jnp.float32)
+
+    add_tiles(
+        list_ref, tiles_ref, total, seen, held, sems, (chunks + 1) // 2, chunks,
+        base=base, first_block=0, blocks=blocks, steps=1,
+    )
+    round_blocks(dense_ref, total, seen, side, blocks, lambda down, along: half_ref[down, along])
+
+
+def build_whole_kernel(list_ref, tiles_ref, dense_ref, total, seen, held, sems, *, blocks, steps):
+    side = tiles_ref.shape[1]
+    add_tiles(
+        list_ref, tiles_ref, total, seen, held, sems, 0, live_chunks(list_ref, tiles_ref),
+        base=lambda row, col: 0.0, first_block=pl.program_id(0) * blocks, blocks=blocks, steps=steps,
+    )
+    round_blocks(
+        dense_ref, total, seen, side, blocks, lambda down, along: jnp.zeros((side, side), jnp.bfloat16)
+    )
 
 
 def build_stages(packed, tiles, row_blocks, col_blocks, per_strip):
@@ -143,7 +156,12 @@
     cost = pl.CostEstimate(
         flops=capacity * side * side, bytes_accessed=capacity * side * side + high * wide, transcendentals=0
     )
-    held_scratch = [pltpu.VMEM(*held), pltpu.SemaphoreType.DMA((held[0][0],))]
+    scratch = [
+        pltpu.VMEM(*total),
+        pltpu.SMEM((-(-(row_blocks + 1) * blocks // 8) * 8,), jnp.int32),
+        pltpu.VMEM(*held),
+        pltpu.SemaphoreType.DMA((held[0][0],)),
+    ]
     dense_shape = jax.ShapeDtypeStruct((high, col_blocks * side), jnp.bfloat16)
     whole = pl.BlockSpec(memory_space=pltpu.VMEM)
     apart = pl.BlockSpec(memory_space=pl.ANY)
@@ -159,7 +177,7 @@
                     grid=(steps,),
                     in_specs=[apart],
                     out_specs=pl.BlockSpec((high, wide), lambda i, *_: (0, i)),
-                    scratch_shapes=[pltpu.VMEM(*total)] + held_scratch,
+                    scratch_shapes=scratch,
                 ),
                 compiler_params=pltpu.CompilerParams(
                     vmem_limit_bytes=scratch_bytes(total, held, block, block) + 4 * mib
@@ -169,7 +187,6 @@
             )(packed, tiles)
         ]
     params = pltpu.CompilerParams(vmem_limit_bytes=build_grant * mib)
-    scratch = [pltpu.VMEM(*total)] + held_scratch
     return [
         lambda _: pl.pallas_call(
             functools.partial(build_first_kernel, blocks=blocks),
@@ -453,9 +470,9 @@
             down = around(down, -1)
         if step <= len(stages):
             up, down, beside = lax.optimization_barrier((up, down, stages[step - 1](beside)))
-        elif step == len(stages) + 1:
+        elif step == reach:
             others = [swapped(cotangent, "col", partner) for partner in range(2, lax.axis_size("col"), 2)]
-            up, down, others = lax.optimization_barrier((up, down, others))
+            up, others = lax.optimization_barrier((up, others))
             cotangents += others
         shards.append((((-step, 0, 0, rows),), up))
         if step < reach:
@@ -483,12 +500,11 @@
     ups, downs, mine = strips[: reach - 1], strips[reach - 1 : -1], strips[-1]
     for step in range(1, reach):
         all_terms += [(-step, width, up), (step, width, down)]
+        if step == reach - 1:
+            all_terms.append((reach, 0, around(down[width:], -1)))
         up = around(added(ups[step - 1], up), 1)
         if step < reach - 1:
             down = around(added(downs[step - 1], down), -1)
-        if step == 1:
-            up, down, opposite = lax.optimization_barrier((up, down, around(terms, reach)))
-            all_terms.append((reach, 0, opposite))
     chunk = summed_terms(all_terms, size)
     chunks = [chunk] + [swapped(chunk, "col", partner) for partner in range(1, col_count)]
     return [mine, up, down], chunks

time: 70.6 us -> 75.1 us (1.064); the launches traced: 69.5 us -> 74.8 us
  Pallas kernels: 11.9 us -> 19 us
  starting transfers between devices: 24.1 us -> 21.5 us
  waiting for transfers between devices: 31 us -> 31.8 us
    pallas_call x1, Pallas kernels: 3.4 us -> 7.63 us  [build_stages(): pl.pallas_call(functools.partial(build_rest_kernel, blocks=blocks), out_s...]
    pallas_call x1, Pallas kernels: 3.44 us -> 6.39 us  [build_stages(): pl.pallas_call(functools.partial(build_first_kernel, blocks=blocks), out_...]
    ppermute x15, starting transfers between devices: 18.5 us -> 16 us  [around(): lax.ppermute(value, 'row', [(order[i], order[(i + step) % count]) for i i...]
    ppermute x15, waiting for transfers between devices: 17.7 us -> 18.6 us  [around(): lax.ppermute(value, 'row', [(order[i], order[(i + step) % count]) for i i...]
  transfers between devices with their start and end apart: 22 -> 22, of which waited for: 12 -> 12; matrix products, arithmetic and copies ran while one was open for 1% -> 1% of each run, Pallas kernels for 13% -> 21%
where the time goes in v8:
time: 75.1 us; the launch traced here: 74.8 us
  waiting for transfers between devices  31.8 us (42%)
  starting transfers between devices  21.5 us (29%)
  Pallas kernels  19 us (25%)
  between operations  1.48 us (2%)
  other arithmetic  0.98 us (1%)
    ppermute x15, waiting for transfers between devices, around(): lax.ppermute(value, 'row', [(order[i], order[(i + step) % count]) for i i...  18.6 us
    ppermute x15, starting transfers between devices, around(): lax.ppermute(value, 'row', [(order[i], order[(i + step) % count]) for i i...  16 us
    ppermute x7, waiting for transfers between devices, swapped(): lax.ppermute(value, axis, [(i, i ^ partner) for i in range(lax.axis_size(...  13.3 us
    pallas_call x1, Pallas kernels, build_stages(): pl.pallas_call(functools.partial(build_rest_kernel, blocks=blocks), out_s...  7.63 us
    pallas_call x1, Pallas kernels, build_stages(): pl.pallas_call(functools.partial(build_first_kernel, blocks=blocks), out_...  6.39 us
    ppermute x7, starting transfers between devices, swapped(): lax.ppermute(value, axis, [(i, i ^ partner) for i in range(lax.axis_size(...  5.46 us
    pallas_call x2, Pallas kernels, backward_product(): pl.pallas_call(functools.partial(backward_kernel, outputs=outputs, row_co...  1.73 us
  transfers between devices with their start and end apart: 22, of which 12 were waited for; matrix products, arithmetic and copies ran while one was open for 1% of the time, Pallas kernels for 21%

profile of v8, /device:TPU:0, one launch (start us, length us, event | category | flops | bytes accessed | tf_op | source)
XLA Modules:
  0.0 74.8 jit_solution(12358868534466785978)
XLA Ops:
  0.6 3.1 %collective-permute-start = (bf16[256,256]{1,0:T(8,128)(2,1)}, bf16[256,256]{1,0:T(8,128)(2,1)S(1)}, u32[]{:S(2)}, u32[]{:S(2)}) collective-permute-start(bf16[256,256]{1,0:T(8,128)(2,1)} %refs_0_.3), channel_id=1, source_target_pairs={{0,8},{8,16},{16,24},{24,28},{28,20},{20,12},{12,4},{4,0},{1,9},{9... | collective-permute-start | bytes 393224 | tf_op jit(solution)/shard_map/ppermute | solution.py:453
  3.7 0.0 collective-permute-start.1
  4.4 0.7 add_reduce_fusion.list_ref
  5.1 6.4 %build_first.1.half_ref = bf16[1024,2048]{1,0:T(8,128)(2,1)S(1)} custom-call(s32[513]{0:T(1024)S(1)} %add_reduce_fusion.list_ref, bf16[256,128,128]{2,1,0:T(8,128)(2,1)} %bitcast.3), custom_call_target="tpu_custom_call" | custom-call | flops 4194304 | bytes 6291456 | tf_op jit(solution)/shard_map/build_first/pallas_call | solution.py:191
  11.5 0.0 copy-start.2
  11.5 0.0 copy-start
  11.5 0.0 collective-permute-done.refs_1_
  11.5 0.0 collective-permute-done.1.refs_2_
  11.5 0.5 collective-permute-start.2
  12.0 1.6 %collective-permute-start.3 = (bf16[256,256]{1,0:T(8,128)(2,1)S(1)}, bf16[256,256]{1,0:T(8,128)(2,1)S(1)}, u32[]{:S(2)}, u32[]{:S(2)}) collective-permute-start(bf16[256,256]{1,0:T(8,128)(2,1)S(1)} %collective-permute-done.1.refs_2_), channel_id=1, source_target_pairs={{0,4},{8,0},{16,8},{24,16},{28,24},{20,28},{12,20},{4,12},{1,5},{9... | collective-permute-start | bytes 393224 | tf_op jit(solution)/shard_map/ppermute | solution.py:453
  13.6 7.6 %build_rest.1.dense_ref = bf16[1024,2048]{1,0:T(8,128)(2,1)S(1)} custom-call(s32[513]{0:T(1024)S(1)} %add_reduce_fusion.list_ref, bf16[256,128,128]{2,1,0:T(8,128)(2,1)} %bitcast.4, bf16[1024,2048]{1,0:T(8,128)(2,1)S(1)} %build_first.1.half_ref), custom_call_target="tpu_custom_call" | custom-call | flops 4194304 | bytes 6291456 | tf_op jit(solution)/shard_map/build_rest/pallas_call | solution.py:201
  21.2 0.0 collective-permute-done.2.refs_3_
  21.3 0.0 collective-permute-done.3.refs_4_
  21.3 0.1 collective-permute-start.4
  21.3 0.0 copy-done.2
  21.3 2.0 %collective-permute-start.7 = (bf16[256,256]{1,0:T(8,128)(2,1)S(1)}, bf16[256,256]{1,0:T(8,128)(2,1)S(1)}, u32[]{:S(2)}, u32[]{:S(2)}) collective-permute-start(bf16[256,256]{1,0:T(8,128)(2,1)S(1)} %copy-done.2), channel_id=1, source_target_pairs={{0,2},{1,3},{2,0},{3,1},{4,6},{5,7},{6,4},{7,5},{8,10},{9,11},{10,... | collective-permute-start | bytes 393224 | tf_op jit(solution)/shard_map/ppermute | solution.py:457
  23.4 2.9 %collective-permute-done.4.refs_5_ = bf16[256,256]{1,0:T(8,128)(2,1)S(1)} collective-permute-done((bf16[256,256]{1,0:T(8,128)(2,1)S(1)}, bf16[256,256]{1,0:T(8,128)(2,1)S(1)}, u32[]{:S(2)}, u32[]{:S(2)}) %collective-permute-start.4) | collective-permute-done | bytes 131104 | tf_op jit(solution)/shard_map/ppermute | solution.py:453
  26.3 1.1 %collective-permute-start.6 = (bf16[256,256]{1,0:T(8,128)(2,1)S(1)}, bf16[256,256]{1,0:T(8,128)(2,1)S(1)}, u32[]{:S(2)}, u32[]{:S(2)}) collective-permute-start(bf16[256,256]{1,0:T(8,128)(2,1)S(1)} %collective-permute-done.4.refs_5_), channel_id=1, source_target_pairs={{0,8},{8,16},{16,24},{24,28},{28,20},{20,12},{12,4},{4,0},{1,9},{9... | collective-permute-start | bytes 393224 | tf_op jit(solution)/shard_map/ppermute | solution.py:453
  27.4 0.9 %collective-permute-start.5 = (bf16[256,256]{1,0:T(8,128)(2,1)S(1)}, bf16[256,256]{1,0:T(8,128)(2,1)S(1)}, u32[]{:S(2)}, u32[]{:S(2)}) collective-permute-start(bf16[256,256]{1,0:T(8,128)(2,1)S(1)} %collective-permute-done.3.refs_4_), channel_id=1, source_target_pairs={{0,4},{8,0},{16,8},{24,16},{28,24},{20,28},{12,20},{4,12},{1,5},{9... | collective-permute-start | bytes 393224 | tf_op jit(solution)/shard_map/ppermute | solution.py:453
  28.3 0.0 collective-permute-done.7.refs_4_
  28.3 2.9 %collective-permute-done.6.refs_7_ = bf16[256,256]{1,0:T(8,128)(2,1)S(1)} collective-permute-done((bf16[256,256]{1,0:T(8,128)(2,1)S(1)}, bf16[256,256]{1,0:T(8,128)(2,1)S(1)}, u32[]{:S(2)}, u32[]{:S(2)}) %collective-permute-start.6) | collective-permute-done | bytes 131104 | tf_op jit(solution)/shard_map/ppermute | solution.py:453
  31.3 1.1 %collective-permute-done.5.refs_6_ = bf16[256,256]{1,0:T(8,128)(2,1)S(1)} collective-permute-done((bf16[256,256]{1,0:T(8,128)(2,1)S(1)}, bf16[256,256]{1,0:T(8,128)(2,1)S(1)}, u32[]{:S(2)}, u32[]{:S(2)}) %collective-permute-start.5) | collective-permute-done | bytes 131104 | tf_op jit(solution)/shard_map/ppermute | solution.py:453
  32.4 0.0 copy-done
  32.4 0.7 forward_product.2
  33.1 0.0 copy-start.1
  33.1 0.1 collective-permute-start.8
  33.2 0.7 forward_product.3
  33.9 0.8 %collective-permute-done.8 = bf16[512,256]{1,0:T(8,128)(2,1)S(1)} collective-permute-done((bf16[512,256]{1,0:T(8,128)(2,1)S(1)}, bf16[512,256]{1,0:T(8,128)(2,1)S(1)}, u32[]{:S(2)}, u32[]{:S(2)}) %collective-permute-start.8) | collective-permute-done | bytes 262176 | tf_op jit(solution)/shard_map/ppermute | solution.py:457
  34.7 0.1 add_convert_fusion.refs_0_
  34.8 1.4 %collective-permute-start.9 = (bf16[512,256]{1,0:T(8,128)(2,1)S(1)}, bf16[512,256]{1,0:T(8,128)(2,1)S(1)}, u32[]{:S(2)}, u32[]{:S(2)}) collective-permute-start(bf16[512,256]{1,0:T(8,128)(2,1)S(1)} %add_convert_fusion.refs_0_), channel_id=1, source_target_pairs={{0,2},{1,3},{2,0},{3,1},{4,6},{5,7},{6,4},{7,5},{8,10},{9,11},{10,... | collective-permute-start | bytes 786440 | tf_op jit(solution)/shard_map/ppermute | solution.py:457
  36.2 7.1 %collective-permute-done.9.refs_1_ = bf16[512,256]{1,0:T(8,128)(2,1)S(1)} collective-permute-done((bf16[512,256]{1,0:T(8,128)(2,1)S(1)}, bf16[512,256]{1,0:T(8,128)(2,1)S(1)}, u32[]{:S(2)}, u32[]{:S(2)}) %collective-permute-start.9) | collective-permute-done | bytes 262176 | tf_op jit(solution)/shard_map/ppermute | solution.py:457
  43.2 0.0 copy-done.1
  43.2 1.0 %middle.1 = (bf16[256,256]{1,0:T(8,128)(2,1)}, bf16[640,256]{1,0:T(8,128)(2,1)S(1)}, f32[64,256]{1,0:T(8,128)S(1)}) custom-call(bf16[512,256]{1,0:T(8,128)(2,1)S(1)} %add_convert_fusion.refs_0_, bf16[512,256]{1,0:T(8,128)(2,1)S(1)} %collective-permute-done.9.refs_1_, bf16[256,256]{1,0:T(8,128)(2,1)S(1)} %copy-done.1, bf16[256,256]{1,0:T(8,128)(2,1)S(1)} %copy-done.2, ...), custom_call_target="tpu_custom_call" | custom-call | flops 335544320 | bytes 1572864 | tf_op jit(solution)/shard_map/middle/pallas_call | solution.py:310
  44.2 0.1 collective-permute-start.10
  44.3 1.6 %collective-permute-done.10.sibling_ref = bf16[640,256]{1,0:T(8,128)(2,1)S(1)} collective-permute-done((bf16[640,256]{1,0:T(8,128)(2,1)S(1)}, bf16[640,256]{1,0:T(8,128)(2,1)S(1)}, u32[]{:S(2)}, u32[]{:S(2)}) %collective-permute-start.10) | collective-permute-done | bytes 327712 | tf_op jit(solution)/shard_map/ppermute | solution.py:457
  45.9 0.6 backward_product.2
  46.5 0.2 collective-permute-start.11
  46.7 1.9 %collective-permute-start.15 = (bf16[320,256]{1,0:T(8,128)(2,1)S(1)}, bf16[320,256]{1,0:T(8,128)(2,1)S(1)}, u32[]{:S(2)}, u32[]{:S(2)}) collective-permute-start(bf16[320,256]{1,0:T(8,128)(2,1)S(1)} %get-tuple-element.55), channel_id=1, source_target_pairs={{0,4},{8,0},{16,8},{24,16},{28,24},{20,28},{12,20},{4,12},{1,5},{9... | collective-permute-start | bytes 491528 | tf_op jit(solution)/shard_map/ppermute | solution.py:453
  48.6 1.1 %backward_product.3 = (bf16[320,256]{1,0:T(8,128)(2,1)S(1)}, bf16[320,256]{1,0:T(8,128)(2,1)S(1)}, bf16[256,256]{1,0:T(8,128)(2,1)S(1)}, bf16[320,256]{1,0:T(8,1...) custom-call(bf16[1024,2048]{1,0:T(8,128)(2,1)S(1)} %build_rest.1.dense_ref, ...), custom_call_target="tpu_custom_call" | custom-call | flops 134217728 | bytes 786432 | tf_op jit(solution)/shard_map/backward_product/pallas_call | solution.py:372
  49.7 3.1 %collective-permute-done.11.refs_1_ = bf16[320,256]{1,0:T(8,128)(2,1)S(1)} collective-permute-done((bf16[320,256]{1,0:T(8,128)(2,1)S(1)}, bf16[320,256]{1,0:T(8,128)(2,1)S(1)}, u32[]{:S(2)}, u32[]{:S(2)}) %collective-permute-start.11) | collective-permute-done | bytes 163872 | tf_op jit(solution)/shard_map/ppermute | solution.py:453
  52.9 0.3 collective-permute-start.12
  53.2 0.0 collective-permute-done.15.refs_2_
  53.2 1.8 %collective-permute-start.16 = (bf16[320,256]{1,0:T(8,128)(2,1)S(1)}, bf16[320,256]{1,0:T(8,128)(2,1)S(1)}, u32[]{:S(2)}, u32[]{:S(2)}) collective-permute-start(bf16[320,256]{1,0:T(8,128)(2,1)S(1)} %add_convert_fusion.2), channel_id=1, source_target_pairs={{0,4},{8,0},{16,8},{24,16},{28,24},{20,28},{12,20},{4,12},{1,5},{9... | collective-permute-start | bytes 491528 | tf_op jit(solution)/shard_map/ppermute | solution.py:453
  55.0 3.3 %collective-permute-done.12.refs_3_ = bf16[320,256]{1,0:T(8,128)(2,1)S(1)} collective-permute-done((bf16[320,256]{1,0:T(8,128)(2,1)S(1)}, bf16[320,256]{1,0:T(8,128)(2,1)S(1)}, u32[]{:S(2)}, u32[]{:S(2)}) %collective-permute-start.12) | collective-permute-done | bytes 163872 | tf_op jit(solution)/shard_map/ppermute | solution.py:453
  58.4 0.5 collective-permute-start.13
  58.9 0.0 collective-permute-done.16.refs_4_
  58.9 1.6 %collective-permute-start.17 = (bf16[320,256]{1,0:T(8,128)(2,1)S(1)}, bf16[320,256]{1,0:T(8,128)(2,1)S(1)}, u32[]{:S(2)}, u32[]{:S(2)}) collective-permute-start(bf16[320,256]{1,0:T(8,128)(2,1)S(1)} %add_convert_fusion.1), channel_id=1, source_target_pairs={{0,4},{8,0},{16,8},{24,16},{28,24},{20,28},{12,20},{4,12},{1,5},{9... | collective-permute-start | bytes 491528 | tf_op jit(solution)/shard_map/ppermute | solution.py:453
  60.6 3.2 %collective-permute-done.13.refs_5_ = bf16[320,256]{1,0:T(8,128)(2,1)S(1)} collective-permute-done((bf16[320,256]{1,0:T(8,128)(2,1)S(1)}, bf16[320,256]{1,0:T(8,128)(2,1)S(1)}, u32[]{:S(2)}, u32[]{:S(2)}) %collective-permute-start.13) | collective-permute-done | bytes 163872 | tf_op jit(solution)/shard_map/ppermute | solution.py:453
  63.8 0.5 collective-permute-start.14
  64.3 0.0 collective-permute-done.17.refs_6_.refs_2_
  64.3 1.9 %collective-permute-start.18 = (bf16[64,256]{1,0:T(8,128)(2,1)S(1)}, bf16[64,256]{1,0:T(8,128)(2,1)S(1)}, u32[]{:S(2)}, u32[]{:S(2)}) collective-permute-start(bf16[64,256]{1,0:T(8,128)(2,1)S(1)} %slice.9), channel_id=1, source_target_pairs={{0,4},{8,0},{16,8},{24,16},{28,24},{20,28},{12,20},{4,12},{1,5},{9... | collective-permute-start | bytes 98312 | tf_op jit(solution)/shard_map/ppermute | solution.py:453
  66.2 2.0 %collective-permute-done.18.refs_7_ = bf16[64,256]{1,0:T(8,128)(2,1)S(1)} collective-permute-done((bf16[64,256]{1,0:T(8,128)(2,1)S(1)}, bf16[64,256]{1,0:T(8,128)(2,1)S(1)}, u32[]{:S(2)}, u32[]{:S(2)}) %collective-permute-start.18) | collective-permute-done | bytes 32800 | tf_op jit(solution)/shard_map/ppermute | solution.py:453
  68.2 0.1 summed_terms.1.refs_3_
  68.3 0.1 collective-permute-start.19
  68.4 1.6 %collective-permute-start.20 = (f32[64,256]{1,0:T(8,128)S(1)}, f32[64,256]{1,0:T(8,128)S(1)}, u32[]{:S(2)}, u32[]{:S(2)}) collective-permute-start(f32[64,256]{1,0:T(8,128)S(1)} %summed_terms.1.refs_3_), channel_id=1, source_target_pairs={{0,2},{1,3},{2,0},{3,1},{4,6},{5,7},{6,4},{7,5},{8,10},{9,11},{10,... | collective-permute-start | bytes 196616 | tf_op jit(solution)/shard_map/ppermute | solution.py:457
  70.0 0.3 collective-permute-start.21
  70.2 0.0 collective-permute-done.19.refs_4_
  70.2 2.6 %collective-permute-done.20.refs_5_ = f32[64,256]{1,0:T(8,128)S(1)} collective-permute-done((f32[64,256]{1,0:T(8,128)S(1)}, f32[64,256]{1,0:T(8,128)S(1)}, u32[]{:S(2)}, u32[]{:S(2)}) %collective-permute-start.20) | collective-permute-done | bytes 65568 | tf_op jit(solution)/shard_map/ppermute | solution.py:457
  72.9 1.1 %collective-permute-done.21.refs_6_ = f32[64,256]{1,0:T(8,128)S(1)} collective-permute-done((f32[64,256]{1,0:T(8,128)S(1)}, f32[64,256]{1,0:T(8,128)S(1)}, u32[]{:S(2)}, u32[]{:S(2)}) %collective-permute-start.21) | collective-permute-done | bytes 65568 | tf_op jit(solution)/shard_map/ppermute | solution.py:457
  74.0 0.0 collective-permute-done.14.refs_1_
  74.0 0.8 %finish.1 = (bf16[256,256]{1,0:T(8,128)(2,1)}, f32[256,256]{1,0:T(8,128)}) custom-call(bf16[256,256]{1,0:T(8,128)(2,1)S(1)} %get-tuple-element.48.refs_0_, bf16[256,256]{1,0:T(8,128)(2,1)S(1)} %collective-permute-done.14.refs_1_, bf16[320,256]{1,0:T(8,128)(2,1)S(1)} %collective-permute-done.17.refs_6_.refs_2_, f32[64,256]{1,0:T(8,128)S(1)} %summed_terms.1.refs_3_, ...), custom_call_target="tpu_custom_call" | custom-call | flops 196608 | bytes 1048576 | tf_op jit(solution)/shard_map/finish/pallas_call | solution.py:434
  (6 shorter events, 0.2 us)
Async XLA Ops:
  0.6 10.9 %collective-permute-start = (bf16[256,256]{1,0:T(8,128)(2,1)}, bf16[256,256]{1,0:T(8,128)(2,1)S(1)}, u32[]{:S(2)}, u32[]{:S(2)}) collective-permute-start(bf16[256,256]{1,0:T(8,128)(2,1)} %refs_0_.3), channel_id=1, source_target_pairs={{0,8},{8,16},{16,24},{24,28},{28,20},{20,12},{12,4},{4,0},{1,9},{9... | collective-permute-start | bytes 393224 | tf_op jit(solution)/shard_map/ppermute | solution.py:453
  3.7 7.8 %collective-permute-start.1 = (bf16[256,256]{1,0:T(8,128)(2,1)}, bf16[256,256]{1,0:T(8,128)(2,1)S(1)}, u32[]{:S(2)}, u32[]{:S(2)}) collective-permute-start(bf16[256,256]{1,0:T(8,128)(2,1)} %refs_0_.3), channel_id=1, source_target_pairs={{0,4},{8,0},{16,8},{24,16},{28,24},{20,28},{12,20},{4,12},{1,5},{9... | collective-permute-start | bytes 393224 | tf_op jit(solution)/shard_map/ppermute | solution.py:453
  11.5 9.9 %copy-start.2 = (bf16[256,256]{1,0:T(8,128)(2,1)S(1)}, bf16[256,256]{1,0:T(8,128)(2,1)}, u32[]{:S(2)}) copy-start(bf16[256,256]{1,0:T(8,128)(2,1)} %refs_3_.1) | copy-start | bytes 393220
  11.5 20.9 %copy-start = (bf16[256,256]{1,0:T(8,128)(2,1)S(1)}, bf16[256,256]{1,0:T(8,128)(2,1)}, u32[]{:S(2)}) copy-start(bf16[256,256]{1,0:T(8,128)(2,1)} %refs_0_.3) | copy-start | bytes 393220
  11.5 9.7 %collective-permute-start.2 = (bf16[256,256]{1,0:T(8,128)(2,1)S(1)}, bf16[256,256]{1,0:T(8,128)(2,1)S(1)}, u32[]{:S(2)}, u32[]{:S(2)}) collective-permute-start(bf16[256,256]{1,0:T(8,128)(2,1)S(1)} %collective-permute-done.refs_1_), channel_id=1, source_target_pairs={{0,8},{8,16},{16,24},{24,28},{28,20},{20,12},{12,4},{4,0},{1,9},{9... | collective-permute-start | bytes 393224 | tf_op jit(solution)/shard_map/ppermute | solution.py:453
  12.0 9.3 %collective-permute-start.3 = (bf16[256,256]{1,0:T(8,128)(2,1)S(1)}, bf16[256,256]{1,0:T(8,128)(2,1)S(1)}, u32[]{:S(2)}, u32[]{:S(2)}) collective-permute-start(bf16[256,256]{1,0:T(8,128)(2,1)S(1)} %collective-permute-done.1.refs_2_), channel_id=1, source_target_pairs={{0,4},{8,0},{16,8},{24,16},{28,24},{20,28},{12,20},{4,12},{1,5},{9... | collective-permute-start | bytes 393224 | tf_op jit(solution)/shard_map/ppermute | solution.py:453
  21.3 5.0 %collective-permute-start.4 = (bf16[256,256]{1,0:T(8,128)(2,1)S(1)}, bf16[256,256]{1,0:T(8,128)(2,1)S(1)}, u32[]{:S(2)}, u32[]{:S(2)}) collective-permute-start(bf16[256,256]{1,0:T(8,128)(2,1)S(1)} %collective-permute-done.2.refs_3_), channel_id=1, source_target_pairs={{0,8},{8,16},{16,24},{24,28},{28,20},{20,12},{12,4},{4,0},{1,9},{9... | collective-permute-start | bytes 393224 | tf_op jit(solution)/shard_map/ppermute | solution.py:453
  21.3 7.0 %collective-permute-start.7 = (bf16[256,256]{1,0:T(8,128)(2,1)S(1)}, bf16[256,256]{1,0:T(8,128)(2,1)S(1)}, u32[]{:S(2)}, u32[]{:S(2)}) collective-permute-start(bf16[256,256]{1,0:T(8,128)(2,1)S(1)} %copy-done.2), channel_id=1, source_target_pairs={{0,2},{1,3},{2,0},{3,1},{4,6},{5,7},{6,4},{7,5},{8,10},{9,11},{10,... | collective-permute-start | bytes 393224 | tf_op jit(solution)/shard_map/ppermute | solution.py:457
  26.3 5.0 %collective-permute-start.6 = (bf16[256,256]{1,0:T(8,128)(2,1)S(1)}, bf16[256,256]{1,0:T(8,128)(2,1)S(1)}, u32[]{:S(2)}, u32[]{:S(2)}) collective-permute-start(bf16[256,256]{1,0:T(8,128)(2,1)S(1)} %collective-permute-done.4.refs_5_), channel_id=1, source_target_pairs={{0,8},{8,16},{16,24},{24,28},{28,20},{20,12},{12,4},{4,0},{1,9},{9... | collective-permute-start | bytes 393224 | tf_op jit(solution)/shard_map/ppermute | solution.py:453
  27.4 5.0 %collective-permute-start.5 = (bf16[256,256]{1,0:T(8,128)(2,1)S(1)}, bf16[256,256]{1,0:T(8,128)(2,1)S(1)}, u32[]{:S(2)}, u32[]{:S(2)}) collective-permute-start(bf16[256,256]{1,0:T(8,128)(2,1)S(1)} %collective-permute-done.3.refs_4_), channel_id=1, source_target_pairs={{0,4},{8,0},{16,8},{24,16},{28,24},{20,28},{12,20},{4,12},{1,5},{9... | collective-permute-start | bytes 393224 | tf_op jit(solution)/shard_map/ppermute | solution.py:453
  33.1 10.1 %copy-start.1 = (bf16[256,256]{1,0:T(8,128)(2,1)S(1)}, bf16[256,256]{1,0:T(8,128)(2,1)}, u32[]{:S(2)}) copy-start(bf16[256,256]{1,0:T(8,128)(2,1)} %refs_2_.1) | copy-start | bytes 393220
  33.1 1.6 %collective-permute-start.8 = (bf16[512,256]{1,0:T(8,128)(2,1)S(1)}, bf16[512,256]{1,0:T(8,128)(2,1)S(1)}, u32[]{:S(2)}, u32[]{:S(2)}) collective-permute-start(bf16[512,256]{1,0:T(8,128)(2,1)S(1)} %forward_product.2), channel_id=1, source_target_pairs={{0,1},{1,0},{2,3},{3,2},{4,5},{5,4},{6,7},{7,6},{8,9},{9,8},{10,11... | collective-permute-start | bytes 786440 | tf_op jit(solution)/shard_map/ppermute | solution.py:457
  34.8 8.4 %collective-permute-start.9 = (bf16[512,256]{1,0:T(8,128)(2,1)S(1)}, bf16[512,256]{1,0:T(8,128)(2,1)S(1)}, u32[]{:S(2)}, u32[]{:S(2)}) collective-permute-start(bf16[512,256]{1,0:T(8,128)(2,1)S(1)} %add_convert_fusion.refs_0_), channel_id=1, source_target_pairs={{0,2},{1,3},{2,0},{3,1},{4,6},{5,7},{6,4},{7,5},{8,10},{9,11},{10,... | collective-permute-start | bytes 786440 | tf_op jit(solution)/shard_map/ppermute | solution.py:457
  44.2 1.7 %collective-permute-start.10 = (bf16[640,256]{1,0:T(8,128)(2,1)S(1)}, bf16[640,256]{1,0:T(8,128)(2,1)S(1)}, u32[]{:S(2)}, u32[]{:S(2)}) collective-permute-start(bf16[640,256]{1,0:T(8,128)(2,1)S(1)} %get-tuple-element.42.own_ref), channel_id=1, source_target_pairs={{0,1},{1,0},{2,3},{3,2},{4,5},{5,4},{6,7},{7,6},{8,9},{9,8},{10,11... | collective-permute-start | bytes 983048 | tf_op jit(solution)/shard_map/ppermute | solution.py:457
  46.5 6.3 %collective-permute-start.11 = (bf16[320,256]{1,0:T(8,128)(2,1)S(1)}, bf16[320,256]{1,0:T(8,128)(2,1)S(1)}, u32[]{:S(2)}, u32[]{:S(2)}) collective-permute-start(bf16[320,256]{1,0:T(8,128)(2,1)S(1)} %get-tuple-element.52), channel_id=1, source_target_pairs={{0,8},{8,16},{16,24},{24,28},{28,20},{20,12},{12,4},{4,0},{1,9},{9... | collective-permute-start | bytes 491528 | tf_op jit(solution)/shard_map/ppermute | solution.py:453
  46.7 6.5 %collective-permute-start.15 = (bf16[320,256]{1,0:T(8,128)(2,1)S(1)}, bf16[320,256]{1,0:T(8,128)(2,1)S(1)}, u32[]{:S(2)}, u32[]{:S(2)}) collective-permute-start(bf16[320,256]{1,0:T(8,128)(2,1)S(1)} %get-tuple-element.55), channel_id=1, source_target_pairs={{0,4},{8,0},{16,8},{24,16},{28,24},{20,28},{12,20},{4,12},{1,5},{9... | collective-permute-start | bytes 491528 | tf_op jit(solution)/shard_map/ppermute | solution.py:453
  52.9 5.5 %collective-permute-start.12 = (bf16[320,256]{1,0:T(8,128)(2,1)S(1)}, bf16[320,256]{1,0:T(8,128)(2,1)S(1)}, u32[]{:S(2)}, u32[]{:S(2)}) collective-permute-start(bf16[320,256]{1,0:T(8,128)(2,1)S(1)} %add_convert_fusion.4), channel_id=1, source_target_pairs={{0,8},{8,16},{16,24},{24,28},{28,20},{20,12},{12,4},{4,0},{1,9},{9... | collective-permute-start | bytes 491528 | tf_op jit(solution)/shard_map/ppermute | solution.py:453
  53.2 5.6 %collective-permute-start.16 = (bf16[320,256]{1,0:T(8,128)(2,1)S(1)}, bf16[320,256]{1,0:T(8,128)(2,1)S(1)}, u32[]{:S(2)}, u32[]{:S(2)}) collective-permute-start(bf16[320,256]{1,0:T(8,128)(2,1)S(1)} %add_convert_fusion.2), channel_id=1, source_target_pairs={{0,4},{8,0},{16,8},{24,16},{28,24},{20,28},{12,20},{4,12},{1,5},{9... | collective-permute-start | bytes 491528 | tf_op jit(solution)/shard_map/ppermute | solution.py:453
  58.4 5.4 %collective-permute-start.13 = (bf16[320,256]{1,0:T(8,128)(2,1)S(1)}, bf16[320,256]{1,0:T(8,128)(2,1)S(1)}, u32[]{:S(2)}, u32[]{:S(2)}) collective-permute-start(bf16[320,256]{1,0:T(8,128)(2,1)S(1)} %add_convert_fusion.3), channel_id=1, source_target_pairs={{0,8},{8,16},{16,24},{24,28},{28,20},{20,12},{12,4},{4,0},{1,9},{9... | collective-permute-start | bytes 491528 | tf_op jit(solution)/shard_map/ppermute | solution.py:453
  58.9 5.4 %collective-permute-start.17 = (bf16[320,256]{1,0:T(8,128)(2,1)S(1)}, bf16[320,256]{1,0:T(8,128)(2,1)S(1)}, u32[]{:S(2)}, u32[]{:S(2)}) collective-permute-start(bf16[320,256]{1,0:T(8,128)(2,1)S(1)} %add_convert_fusion.1), channel_id=1, source_target_pairs={{0,4},{8,0},{16,8},{24,16},{28,24},{20,28},{12,20},{4,12},{1,5},{9... | collective-permute-start | bytes 491528 | tf_op jit(solution)/shard_map/ppermute | solution.py:453
  63.8 10.2 %collective-permute-start.14 = (bf16[256,256]{1,0:T(8,128)(2,1)S(1)}, bf16[256,256]{1,0:T(8,128)(2,1)S(1)}, u32[]{:S(2)}, u32[]{:S(2)}) collective-permute-start(bf16[256,256]{1,0:T(8,128)(2,1)S(1)} %add_convert_fusion.5), channel_id=1, source_target_pairs={{0,8},{8,16},{16,24},{24,28},{28,20},{20,12},{12,4},{4,0},{1,9},{9... | collective-permute-start | bytes 393224 | tf_op jit(solution)/shard_map/ppermute | solution.py:453
  64.3 3.9 %collective-permute-start.18 = (bf16[64,256]{1,0:T(8,128)(2,1)S(1)}, bf16[64,256]{1,0:T(8,128)(2,1)S(1)}, u32[]{:S(2)}, u32[]{:S(2)}) collective-permute-start(bf16[64,256]{1,0:T(8,128)(2,1)S(1)} %slice.9), channel_id=1, source_target_pairs={{0,4},{8,0},{16,8},{24,16},{28,24},{20,28},{12,20},{4,12},{1,5},{9... | collective-permute-start | bytes 98312 | tf_op jit(solution)/shard_map/ppermute | solution.py:453
  68.3 1.9 %collective-permute-start.19 = (f32[64,256]{1,0:T(8,128)S(1)}, f32[64,256]{1,0:T(8,128)S(1)}, u32[]{:S(2)}, u32[]{:S(2)}) collective-permute-start(f32[64,256]{1,0:T(8,128)S(1)} %summed_terms.1.refs_3_), channel_id=1, source_target_pairs={{0,1},{1,0},{2,3},{3,2},{4,5},{5,4},{6,7},{7,6},{8,9},{9,8},{10,11... | collective-permute-start | bytes 196616 | tf_op jit(solution)/shard_map/ppermute | solution.py:457
  68.4 4.5 %collective-permute-start.20 = (f32[64,256]{1,0:T(8,128)S(1)}, f32[64,256]{1,0:T(8,128)S(1)}, u32[]{:S(2)}, u32[]{:S(2)}) collective-permute-start(f32[64,256]{1,0:T(8,128)S(1)} %summed_terms.1.refs_3_), channel_id=1, source_target_pairs={{0,2},{1,3},{2,0},{3,1},{4,6},{5,7},{6,4},{7,5},{8,10},{9,11},{10,... | collective-permute-start | bytes 196616 | tf_op jit(solution)/shard_map/ppermute | solution.py:457
  70.0 4.0 %collective-permute-start.21 = (f32[64,256]{1,0:T(8,128)S(1)}, f32[64,256]{1,0:T(8,128)S(1)}, u32[]{:S(2)}, u32[]{:S(2)}) collective-permute-start(f32[64,256]{1,0:T(8,128)S(1)} %summed_terms.1.refs_3_), channel_id=1, source_target_pairs={{0,3},{1,2},{2,1},{3,0},{4,7},{5,6},{6,5},{7,4},{8,11},{9,10},{10,... | collective-permute-start | bytes 196616 | tf_op jit(solution)/shard_map/ppermute | solution.py:457

commit v9 on v7

--- a/solution.py
+++ b/solution.py
@@ -133,7 +133,7 @@
     each_row_block(total, tiles_ref.shape[1], rounded)
 
 
-def build_stages(packed, tiles, row_blocks, col_blocks, per_strip):
+def build_stages(tiles, row_blocks, col_blocks, per_strip):
     capacity, side, _ = tiles.shape
     blocks = min(strips_per_step * per_strip, col_blocks)
     steps = col_blocks // blocks
@@ -151,7 +151,7 @@
     if steps > 1:
         block = ((high, wide), jnp.bfloat16)
         return [
-            lambda _: pl.pallas_call(
+            lambda packed: pl.pallas_call(
                 functools.partial(build_whole_kernel, blocks=blocks, steps=steps),
                 out_shape=dense_shape,
                 grid_spec=pltpu.PrefetchScalarGridSpec(
@@ -171,7 +171,7 @@
     params = pltpu.CompilerParams(vmem_limit_bytes=build_grant * mib)
     scratch = [pltpu.VMEM(*total)] + held_scratch
     return [
-        lambda _: pl.pallas_call(
+        lambda packed: (packed, pl.pallas_call(
             functools.partial(build_first_kernel, blocks=blocks),
             out_shape=dense_shape,
             in_specs=[listed, apart],
@@ -180,8 +180,8 @@
             compiler_params=params,
             cost_estimate=cost,
             name="build_first",
-        )(packed, tiles),
-        lambda half: pl.pallas_call(
+        )(packed, tiles)),
+        lambda state: pl.pallas_call(
             functools.partial(build_rest_kernel, blocks=blocks),
             out_shape=dense_shape,
             in_specs=[listed, apart, whole],
@@ -190,7 +190,7 @@
             compiler_params=params,
             cost_estimate=cost,
             name="build_rest",
-        )(packed, tiles, half),
+        )(state[0], tiles, state[1]),
     ]
 
 
@@ -440,27 +440,27 @@
     return lax.ppermute(value, axis, [(i, i ^ partner) for i in range(lax.axis_size(axis))])
 
 
-def gathered_shards(own, stages, cotangent):
+def gathered_shards(own, packed, stages, cotangent):
     reach = lax.axis_size("row") // 2
     rows = own.shape[0]
     shards = [(((0, 0, 0, rows),), own)]
     up = down = own
-    beside = None
-    cotangents = [cotangent]
+    dense = packed
+    others = [swapped(cotangent, "col", partner) for partner in range(2, lax.axis_size("col"), 2)]
     for step in range(1, reach + 1):
         up = around(up, 1)
         if step < reach:
             down = around(down, -1)
-        if step <= len(stages):
-            up, down, beside = lax.optimization_barrier((up, down, stages[step - 1](beside)))
-        elif step == len(stages) + 1:
-            others = [swapped(cotangent, "col", partner) for partner in range(2, lax.axis_size("col"), 2)]
-            up, down, others = lax.optimization_barrier((up, down, others))
-            cotangents += others
+        if step == 1:
+            up, down, dense, others = lax.optimization_barrier((up, down, dense, others))
+        elif step in (2, reach):
+            dense = stages.pop(0)(dense) if stages else dense
+        if 1 < step < reach:
+            up, down, dense = lax.optimization_barrier((up, down, dense))
         shards.append((((-step, 0, 0, rows),), up))
         if step < reach:
             shards.append((((step, 0, 0, rows),), down))
-    return shards, beside, cotangents
+    return shards, dense, [cotangent] + others
 
 
 def added(first, second):
@@ -483,12 +483,13 @@
     ups, downs, mine = strips[: reach - 1], strips[reach - 1 : -1], strips[-1]
     for step in range(1, reach):
         all_terms += [(-step, width, up), (step, width, down)]
+        relayed = around(down[width:], -2) if step == reach - 2 else None
         up = around(added(ups[step - 1], up), 1)
         if step < reach - 1:
             down = around(added(downs[step - 1], down), -1)
-        if step == 1:
-            up, down, opposite = lax.optimization_barrier((up, down, around(terms, reach)))
-            all_terms.append((reach, 0, opposite))
+        if relayed is not None:
+            up, down, relayed = lax.optimization_barrier((up, down, relayed))
+            all_terms.append((reach, 0, relayed))
     chunk = summed_terms(all_terms, size)
     chunks = [chunk] + [swapped(chunk, "col", partner) for partner in range(1, col_count)]
     return [mine, up, down], chunks
@@ -502,8 +503,8 @@
     row_count = lax.axis_size("row")
     col_count = lax.axis_size("col")
     per_strip = node_rows // side
-    stages = build_stages(packed, tiles, col_count * per_strip, row_count * per_strip, per_strip)
-    shards, dense, cotangents = gathered_shards(features, stages, out_grad)
+    stages = build_stages(tiles, col_count * per_strip, row_count * per_strip, per_strip)
+    shards, dense, cotangents = gathered_shards(features, packed, stages, out_grad)
 
     for_sibling = forward_product(dense, shards, 1, row_count, col_count)
     for_sibling, cell = lax.optimization_barrier((for_sibling, dense))

time: 70.6 us -> 69.5 us (0.984); the launches traced: 69.5 us -> 69.3 us
  starting transfers between devices: 24.1 us -> 21.7 us
  Pallas kernels: 11.9 us -> 13.4 us
    ppermute x15, starting transfers between devices: 18.5 us -> 16.6 us  [around(): lax.ppermute(value, 'row', [(order[i], order[(i + step) % count]) for i i...]
    ppermute x7, waiting for transfers between devices: 13.3 us -> 14.2 us  [swapped(): lax.ppermute(value, axis, [(i, i ^ partner) for i in range(lax.axis_size(...]
    pallas_call x1, Pallas kernels: 3.4 us -> 4.17 us  [build_stages(): pl.pallas_call(functools.partial(build_rest_kernel, blocks=blocks), out_s...]
    pallas_call x1, Pallas kernels: 3.44 us -> 4.18 us  [build_stages(): pl.pallas_call(functools.partial(build_first_kernel, blocks=blocks), out_...]
  transfers between devices with their start and end apart: 22 -> 22, of which waited for: 12 -> 12; matrix products, arithmetic and copies ran while one was open for 1% -> 1% of each run, Pallas kernels for 13% -> 15%
where the time goes in v9:
time: 69.5 us; the launch traced here: 69.3 us
  waiting for transfers between devices  31.7 us (46%)
  starting transfers between devices  21.7 us (31%)
  Pallas kernels  13.4 us (19%)
  between operations  1.47 us (2%)
  other arithmetic  0.98 us (1%)
    ppermute x15, waiting for transfers between devices, around(): lax.ppermute(value, 'row', [(order[i], order[(i + step) % count]) for i i...  17.5 us
    ppermute x15, starting transfers between devices, around(): lax.ppermute(value, 'row', [(order[i], order[(i + step) % count]) for i i...  16.6 us
    ppermute x7, waiting for transfers between devices, swapped(): lax.ppermute(value, axis, [(i, i ^ partner) for i in range(lax.axis_size(...  14.2 us
    ppermute x7, starting transfers between devices, swapped(): lax.ppermute(value, axis, [(i, i ^ partner) for i in range(lax.axis_size(...  5.14 us
    pallas_call x1, Pallas kernels, build_stages(): pl.pallas_call(functools.partial(build_first_kernel, blocks=blocks), out_...  4.18 us
    pallas_call x1, Pallas kernels, build_stages(): pl.pallas_call(functools.partial(build_rest_kernel, blocks=blocks), out_s...  4.17 us
    pallas_call x2, Pallas kernels, backward_product(): pl.pallas_call(functools.partial(backward_kernel, outputs=outputs, row_co...  1.74 us
    pallas_call x2, Pallas kernels, forward_product(): pl.pallas_call(functools.partial(forward_kernel, pieces=pieces, sibling=s...  1.42 us
  transfers between devices with their start and end apart: 22, of which 12 were waited for; matrix products, arithmetic and copies ran while one was open for 1% of the time, Pallas kernels for 15%

profile of v9, /device:TPU:0, one launch (start us, length us, event | category | flops | bytes accessed | tf_op | source)
XLA Modules:
  0.0 69.3 jit_solution(2759312621187495032)
XLA Ops:
  0.6 3.0 %collective-permute-start.2 = (bf16[256,256]{1,0:T(8,128)(2,1)}, bf16[256,256]{1,0:T(8,128)(2,1)S(1)}, u32[]{:S(2)}, u32[]{:S(2)}) collective-permute-start(bf16[256,256]{1,0:T(8,128)(2,1)} %refs_3_.1), channel_id=1, source_target_pairs={{0,2},{1,3},{2,0},{3,1},{4,6},{5,7},{6,4},{7,5},{8,10},{9,11},{10,... | collective-permute-start | bytes 393224 | tf_op jit(solution)/shard_map/ppermute | solution.py:440
  3.6 1.5 %collective-permute-start.1 = (bf16[256,256]{1,0:T(8,128)(2,1)}, bf16[256,256]{1,0:T(8,128)(2,1)S(1)}, u32[]{:S(2)}, u32[]{:S(2)}) collective-permute-start(bf16[256,256]{1,0:T(8,128)(2,1)} %refs_0_.3), channel_id=1, source_target_pairs={{0,4},{8,0},{16,8},{24,16},{28,24},{20,28},{12,20},{4,12},{1,5},{9... | collective-permute-start | bytes 393224 | tf_op jit(solution)/shard_map/ppermute | solution.py:436
  5.2 0.5 collective-permute-start
  6.3 0.7 %add_reduce_fusion.list_ref = s32[513]{0:T(1024)S(1)} fusion(s32[1,1,1]{2,1,0:T(1,128)} %bitcast.2, s32[1,1,256]{2,1,0:T(1,128)} %param.11, s32[1,1,256]{2,1,0:T(1,128)} %param.10), kind=kLoop, calls=%fused_computation.6 | loop fusion | flops 1026 | bytes 4104 | tf_op jit(solution)/shard_map/concatenate | solution.py:502
  7.0 0.3 collective-permute-done.2.refs_4_
  7.3 1.5 %collective-permute-done.1.refs_2_ = bf16[256,256]{1,0:T(8,128)(2,1)S(1)} collective-permute-done((bf16[256,256]{1,0:T(8,128)(2,1)}, bf16[256,256]{1,0:T(8,128)(2,1)S(1)}, u32[]{:S(2)}, u32[]{:S(2)}) %collective-permute-start.1) | collective-permute-done | bytes 131104 | tf_op jit(solution)/shard_map/ppermute | solution.py:436
  8.8 1.5 %collective-permute-done.refs_1_ = bf16[256,256]{1,0:T(8,128)(2,1)S(1)} collective-permute-done((bf16[256,256]{1,0:T(8,128)(2,1)}, bf16[256,256]{1,0:T(8,128)(2,1)S(1)}, u32[]{:S(2)}, u32[]{:S(2)}) %collective-permute-start) | collective-permute-done | bytes 131104 | tf_op jit(solution)/shard_map/ppermute | solution.py:436
  10.3 0.5 collective-permute-start.3
  10.8 1.5 %collective-permute-start.4 = (bf16[256,256]{1,0:T(8,128)(2,1)S(1)}, bf16[256,256]{1,0:T(8,128)(2,1)S(1)}, u32[]{:S(2)}, u32[]{:S(2)}) collective-permute-start(bf16[256,256]{1,0:T(8,128)(2,1)S(1)} %collective-permute-done.1.refs_2_), channel_id=1, source_target_pairs={{0,4},{8,0},{16,8},{24,16},{28,24},{20,28},{12,20},{4,12},{1,5},{9... | collective-permute-start | bytes 393224 | tf_op jit(solution)/shard_map/ppermute | solution.py:436
  12.4 4.2 %build_first.1.half_ref = bf16[1024,2048]{1,0:T(8,128)(2,1)S(1)} custom-call(s32[513]{0:T(1024)S(1)} %add_reduce_fusion.list_ref, bf16[256,128,128]{2,1,0:T(8,128)(2,1)} %bitcast.3), custom_call_target="tpu_custom_call" | custom-call | flops 4194304 | bytes 6291456 | tf_op jit(solution)/shard_map/build_first/pallas_call | solution.py:174
  16.5 0.0 copy-start
  16.6 0.0 collective-permute-done.3.refs_3_
  16.6 0.0 collective-permute-done.4.refs_4_
  16.6 0.8 %collective-permute-start.5 = (bf16[256,256]{1,0:T(8,128)(2,1)S(1)}, bf16[256,256]{1,0:T(8,128)(2,1)S(1)}, u32[]{:S(2)}, u32[]{:S(2)}) collective-permute-start(bf16[256,256]{1,0:T(8,128)(2,1)S(1)} %collective-permute-done.3.refs_3_), channel_id=1, source_target_pairs={{0,8},{8,16},{16,24},{24,28},{28,20},{20,12},{12,4},{4,0},{1,9},{9... | collective-permute-start | bytes 393224 | tf_op jit(solution)/shard_map/ppermute | solution.py:436
  17.4 1.3 %collective-permute-start.6 = (bf16[256,256]{1,0:T(8,128)(2,1)S(1)}, bf16[256,256]{1,0:T(8,128)(2,1)S(1)}, u32[]{:S(2)}, u32[]{:S(2)}) collective-permute-start(bf16[256,256]{1,0:T(8,128)(2,1)S(1)} %collective-permute-done.4.refs_4_), channel_id=1, source_target_pairs={{0,4},{8,0},{16,8},{24,16},{28,24},{20,28},{12,20},{4,12},{1,5},{9... | collective-permute-start | bytes 393224 | tf_op jit(solution)/shard_map/ppermute | solution.py:436
  18.7 3.8 %collective-permute-done.5.refs_5_ = bf16[256,256]{1,0:T(8,128)(2,1)S(1)} collective-permute-done((bf16[256,256]{1,0:T(8,128)(2,1)S(1)}, bf16[256,256]{1,0:T(8,128)(2,1)S(1)}, u32[]{:S(2)}, u32[]{:S(2)}) %collective-permute-start.5) | collective-permute-done | bytes 131104 | tf_op jit(solution)/shard_map/ppermute | solution.py:436
  22.5 0.0 collective-permute-done.6.refs_6_
  22.5 1.5 %collective-permute-start.7 = (bf16[256,256]{1,0:T(8,128)(2,1)S(1)}, bf16[256,256]{1,0:T(8,128)(2,1)S(1)}, u32[]{:S(2)}, u32[]{:S(2)}) collective-permute-start(bf16[256,256]{1,0:T(8,128)(2,1)S(1)} %collective-permute-done.5.refs_5_), channel_id=1, source_target_pairs={{0,8},{8,16},{16,24},{24,28},{28,20},{20,12},{12,4},{4,0},{1,9},{9... | collective-permute-start | bytes 393224 | tf_op jit(solution)/shard_map/ppermute | solution.py:436
  23.9 4.2 %build_rest.1.dense_ref = bf16[1024,2048]{1,0:T(8,128)(2,1)S(1)} custom-call(s32[513]{0:T(1024)S(1)} %add_reduce_fusion.list_ref, bf16[256,128,128]{2,1,0:T(8,128)(2,1)} %bitcast.4, bf16[1024,2048]{1,0:T(8,128)(2,1)S(1)} %build_first.1.half_ref), custom_call_target="tpu_custom_call" | custom-call | flops 4194304 | bytes 6291456 | tf_op jit(solution)/shard_map/build_rest/pallas_call | solution.py:184
  28.1 0.0 collective-permute-done.7.refs_7_
  28.1 0.0 copy-done
  28.1 0.7 %forward_product.2 = bf16[512,256]{1,0:T(8,128)(2,1)S(1)} custom-call(bf16[1024,2048]{1,0:T(8,128)(2,1)S(1)} %build_rest.1.dense_ref, bf16[256,256]{1,0:T(8,128)(2,1)S(1)} %copy-done, bf16[256,256]{1,0:T(8,128)(2,1)S(1)} %collective-permute-done.refs_1_, bf16[256,256]{1,0:T(8,128)(2,1)S(1)} %collective-permute-done.1.refs_2_, ...), custom_call_target="tpu_custom_call" | custom-call | flops 536870912 | bytes 3407872 | tf_op jit(solution)/shard_map/forward_product/pallas_call | solution.py:236
  28.9 0.0 copy-start.1
  28.9 0.0 copy-start.2
  28.9 0.1 collective-permute-start.8
  29.0 0.7 %forward_product.3 = bf16[512,256]{1,0:T(8,128)(2,1)S(1)} custom-call(bf16[1024,2048]{1,0:T(8,128)(2,1)S(1)} %build_rest.1.dense_ref, bf16[256,256]{1,0:T(8,128)(2,1)S(1)} %copy-done, bf16[256,256]{1,0:T(8,128)(2,1)S(1)} %collective-permute-done.refs_1_, bf16[256,256]{1,0:T(8,128)(2,1)S(1)} %collective-permute-done.1.refs_2_, ...), custom_call_target="tpu_custom_call" | custom-call | flops 536870912 | bytes 3407872 | tf_op jit(solution)/shard_map/forward_product/pallas_call | solution.py:236
  29.7 0.8 %collective-permute-done.8 = bf16[512,256]{1,0:T(8,128)(2,1)S(1)} collective-permute-done((bf16[512,256]{1,0:T(8,128)(2,1)S(1)}, bf16[512,256]{1,0:T(8,128)(2,1)S(1)}, u32[]{:S(2)}, u32[]{:S(2)}) %collective-permute-start.8) | collective-permute-done | bytes 262176 | tf_op jit(solution)/shard_map/ppermute | solution.py:440
  30.5 0.1 add_convert_fusion.refs_0_
  30.5 0.1 collective-permute-start.9
  30.6 8.3 %collective-permute-done.9.refs_1_ = bf16[512,256]{1,0:T(8,128)(2,1)S(1)} collective-permute-done((bf16[512,256]{1,0:T(8,128)(2,1)S(1)}, bf16[512,256]{1,0:T(8,128)(2,1)S(1)}, u32[]{:S(2)}, u32[]{:S(2)}) %collective-permute-start.9) | collective-permute-done | bytes 262176 | tf_op jit(solution)/shard_map/ppermute | solution.py:440
  39.0 0.0 copy-done.1
  39.0 0.0 copy-done.2
  39.0 1.0 %middle.1 = (bf16[256,256]{1,0:T(8,128)(2,1)}, bf16[640,256]{1,0:T(8,128)(2,1)S(1)}, f32[64,256]{1,0:T(8,128)S(1)}) custom-call(bf16[512,256]{1,0:T(8,128)(2,1)S(1)} %add_convert_fusion.refs_0_, bf16[512,256]{1,0:T(8,128)(2,1)S(1)} %collective-permute-done.9.refs_1_, bf16[256,256]{1,0:T(8,128)(2,1)S(1)} %copy-done.1, bf16[256,256]{1,0:T(8,128)(2,1)S(1)} %copy-done.2, ...), custom_call_target="tpu_custom_call" | custom-call | flops 335544320 | bytes 1572864 | tf_op jit(solution)/shard_map/middle/pallas_call | solution.py:293
  40.0 0.1 collective-permute-start.10
  40.0 1.6 %collective-permute-done.10.sibling_ref = bf16[640,256]{1,0:T(8,128)(2,1)S(1)} collective-permute-done((bf16[640,256]{1,0:T(8,128)(2,1)S(1)}, bf16[640,256]{1,0:T(8,128)(2,1)S(1)}, u32[]{:S(2)}, u32[]{:S(2)}) %collective-permute-start.10) | collective-permute-done | bytes 327712 | tf_op jit(solution)/shard_map/ppermute | solution.py:440
  41.7 0.6 backward_product.2
  42.3 0.8 %collective-permute-start.11 = (bf16[320,256]{1,0:T(8,128)(2,1)S(1)}, bf16[320,256]{1,0:T(8,128)(2,1)S(1)}, u32[]{:S(2)}, u32[]{:S(2)}) collective-permute-start(bf16[320,256]{1,0:T(8,128)(2,1)S(1)} %get-tuple-element.63), channel_id=1, source_target_pairs={{0,8},{8,16},{16,24},{24,28},{28,20},{20,12},{12,4},{4,0},{1,9},{9... | collective-permute-start | bytes 491528 | tf_op jit(solution)/shard_map/ppermute | solution.py:436
  43.1 1.3 %collective-permute-start.14 = (bf16[320,256]{1,0:T(8,128)(2,1)S(1)}, bf16[320,256]{1,0:T(8,128)(2,1)S(1)}, u32[]{:S(2)}, u32[]{:S(2)}) collective-permute-start(bf16[320,256]{1,0:T(8,128)(2,1)S(1)} %get-tuple-element.66), channel_id=1, source_target_pairs={{0,4},{8,0},{16,8},{24,16},{28,24},{20,28},{12,20},{4,12},{1,5},{9... | collective-permute-start | bytes 491528 | tf_op jit(solution)/shard_map/ppermute | solution.py:436
  44.4 1.1 %backward_product.3 = (bf16[320,256]{1,0:T(8,128)(2,1)S(1)}, bf16[320,256]{1,0:T(8,128)(2,1)S(1)}, bf16[256,256]{1,0:T(8,128)(2,1)S(1)}, bf16[320,256]{1,0:T(8,1...) custom-call(bf16[1024,2048]{1,0:T(8,128)(2,1)S(1)} %build_rest.1.dense_ref, ...), custom_call_target="tpu_custom_call" | custom-call | flops 134217728 | bytes 786432 | tf_op jit(solution)/shard_map/backward_product/pallas_call | solution.py:355
  45.5 3.1 %collective-permute-done.11.refs_1_ = bf16[320,256]{1,0:T(8,128)(2,1)S(1)} collective-permute-done((bf16[320,256]{1,0:T(8,128)(2,1)S(1)}, bf16[320,256]{1,0:T(8,128)(2,1)S(1)}, u32[]{:S(2)}, u32[]{:S(2)}) %collective-permute-start.11) | collective-permute-done | bytes 163872 | tf_op jit(solution)/shard_map/ppermute | solution.py:436
  48.6 0.8 %collective-permute-start.12 = (bf16[320,256]{1,0:T(8,128)(2,1)S(1)}, bf16[320,256]{1,0:T(8,128)(2,1)S(1)}, u32[]{:S(2)}, u32[]{:S(2)}) collective-permute-start(bf16[320,256]{1,0:T(8,128)(2,1)S(1)} %add_convert_fusion.4), channel_id=1, source_target_pairs={{0,8},{8,16},{16,24},{24,28},{28,20},{20,12},{12,4},{4,0},{1,9},{9... | collective-permute-start | bytes 491528 | tf_op jit(solution)/shard_map/ppermute | solution.py:436
  49.4 0.0 collective-permute-done.14.refs_2_
  49.5 1.3 %collective-permute-start.15 = (bf16[320,256]{1,0:T(8,128)(2,1)S(1)}, bf16[320,256]{1,0:T(8,128)(2,1)S(1)}, u32[]{:S(2)}, u32[]{:S(2)}) collective-permute-start(bf16[320,256]{1,0:T(8,128)(2,1)S(1)} %add_convert_fusion.2), channel_id=1, source_target_pairs={{0,4},{8,0},{16,8},{24,16},{28,24},{20,28},{12,20},{4,12},{1,5},{9... | collective-permute-start | bytes 491528 | tf_op jit(solution)/shard_map/ppermute | solution.py:436
  50.8 3.3 %collective-permute-done.12.refs_3_ = bf16[320,256]{1,0:T(8,128)(2,1)S(1)} collective-permute-done((bf16[320,256]{1,0:T(8,128)(2,1)S(1)}, bf16[320,256]{1,0:T(8,128)(2,1)S(1)}, u32[]{:S(2)}, u32[]{:S(2)}) %collective-permute-start.12) | collective-permute-done | bytes 163872 | tf_op jit(solution)/shard_map/ppermute | solution.py:436
  54.1 0.8 %collective-permute-start.13 = (bf16[320,256]{1,0:T(8,128)(2,1)S(1)}, bf16[320,256]{1,0:T(8,128)(2,1)S(1)}, u32[]{:S(2)}, u32[]{:S(2)}) collective-permute-start(bf16[320,256]{1,0:T(8,128)(2,1)S(1)} %add_convert_fusion.3), channel_id=1, source_target_pairs={{0,8},{8,16},{16,24},{24,28},{28,20},{20,12},{12,4},{4,0},{1,9},{9... | collective-permute-start | bytes 491528 | tf_op jit(solution)/shard_map/ppermute | solution.py:436
  54.9 0.0 collective-permute-done.15.refs_4_
  55.0 1.3 %collective-permute-start.16 = (bf16[320,256]{1,0:T(8,128)(2,1)S(1)}, bf16[320,256]{1,0:T(8,128)(2,1)S(1)}, u32[]{:S(2)}, u32[]{:S(2)}) collective-permute-start(bf16[320,256]{1,0:T(8,128)(2,1)S(1)} %add_convert_fusion.1), channel_id=1, source_target_pairs={{0,4},{8,0},{16,8},{24,16},{28,24},{20,28},{12,20},{4,12},{1,5},{9... | collective-permute-start | bytes 491528 | tf_op jit(solution)/shard_map/ppermute | solution.py:436
  56.3 1.3 %collective-permute-start.17 = (bf16[64,256]{1,0:T(8,128)(2,1)S(1)}, bf16[64,256]{1,0:T(8,128)(2,1)S(1)}, u32[]{:S(2)}, u32[]{:S(2)}) collective-permute-start(bf16[64,256]{1,0:T(8,128)(2,1)S(1)} %slice.8), channel_id=1, source_target_pairs={{0,12},{8,4},{16,0},{24,8},{28,16},{20,24},{12,28},{4,20},{1,13},{... | collective-permute-start | bytes 98312 | tf_op jit(solution)/shard_map/ppermute | solution.py:436
  57.6 4.4 %collective-permute-done.17.refs_5_ = bf16[64,256]{1,0:T(8,128)(2,1)S(1)} collective-permute-done((bf16[64,256]{1,0:T(8,128)(2,1)S(1)}, bf16[64,256]{1,0:T(8,128)(2,1)S(1)}, u32[]{:S(2)}, u32[]{:S(2)}) %collective-permute-start.17) | collective-permute-done | bytes 32800 | tf_op jit(solution)/shard_map/ppermute | solution.py:436
  61.9 0.0 collective-permute-done.13.refs_6_
  61.9 0.0 collective-permute-done.16.refs_7_.refs_2_
  62.0 1.4 %collective-permute-start.18 = (bf16[256,256]{1,0:T(8,128)(2,1)S(1)}, bf16[256,256]{1,0:T(8,128)(2,1)S(1)}, u32[]{:S(2)}, u32[]{:S(2)}) collective-permute-start(bf16[256,256]{1,0:T(8,128)(2,1)S(1)} %add_convert_fusion.5), channel_id=1, source_target_pairs={{0,8},{8,16},{16,24},{24,28},{28,20},{20,12},{12,4},{4,0},{1,9},{9... | collective-permute-start | bytes 393224 | tf_op jit(solution)/shard_map/ppermute | solution.py:436
  63.3 0.1 summed_terms.1.refs_3_
  63.4 0.1 collective-permute-start.21
  63.5 0.7 collective-permute-start.20
  64.2 1.2 %collective-permute-start.19 = (f32[64,256]{1,0:T(8,128)S(1)}, f32[64,256]{1,0:T(8,128)S(1)}, u32[]{:S(2)}, u32[]{:S(2)}) collective-permute-start(f32[64,256]{1,0:T(8,128)S(1)} %summed_terms.1.refs_3_), channel_id=1, source_target_pairs={{0,1},{1,0},{2,3},{3,2},{4,5},{5,4},{6,7},{7,6},{8,9},{9,8},{10,11... | collective-permute-start | bytes 196616 | tf_op jit(solution)/shard_map/ppermute | solution.py:440
  65.3 1.9 %collective-permute-done.21.refs_6_ = f32[64,256]{1,0:T(8,128)S(1)} collective-permute-done((f32[64,256]{1,0:T(8,128)S(1)}, f32[64,256]{1,0:T(8,128)S(1)}, u32[]{:S(2)}, u32[]{:S(2)}) %collective-permute-start.21) | collective-permute-done | bytes 65568 | tf_op jit(solution)/shard_map/ppermute | solution.py:440
  67.3 1.2 %collective-permute-done.20.refs_5_ = f32[64,256]{1,0:T(8,128)S(1)} collective-permute-done((f32[64,256]{1,0:T(8,128)S(1)}, f32[64,256]{1,0:T(8,128)S(1)}, u32[]{:S(2)}, u32[]{:S(2)}) %collective-permute-start.20) | collective-permute-done | bytes 65568 | tf_op jit(solution)/shard_map/ppermute | solution.py:440
  68.5 0.0 collective-permute-done.19.refs_4_
  68.5 0.0 collective-permute-done.18.refs_1_
  68.5 0.8 %finish.1 = (bf16[256,256]{1,0:T(8,128)(2,1)}, f32[256,256]{1,0:T(8,128)}) custom-call(bf16[256,256]{1,0:T(8,128)(2,1)S(1)} %get-tuple-element.59.refs_0_, bf16[256,256]{1,0:T(8,128)(2,1)S(1)} %collective-permute-done.18.refs_1_, bf16[320,256]{1,0:T(8,128)(2,1)S(1)} %collective-permute-done.16.refs_7_.refs_2_, f32[64,256]{1,0:T(8,128)S(1)} %summed_terms.1.refs_3_, ...), custom_call_target="tpu_custom_call" | custom-call | flops 196608 | bytes 1048576 | tf_op jit(solution)/shard_map/finish/pallas_call | solution.py:417
  (6 shorter events, 0.2 us)
Async XLA Ops:
  0.6 6.7 %collective-permute-start.2 = (bf16[256,256]{1,0:T(8,128)(2,1)}, bf16[256,256]{1,0:T(8,128)(2,1)S(1)}, u32[]{:S(2)}, u32[]{:S(2)}) collective-permute-start(bf16[256,256]{1,0:T(8,128)(2,1)} %refs_3_.1), channel_id=1, source_target_pairs={{0,2},{1,3},{2,0},{3,1},{4,6},{5,7},{6,4},{7,5},{8,10},{9,11},{10,... | collective-permute-start | bytes 393224 | tf_op jit(solution)/shard_map/ppermute | solution.py:440
  3.6 5.2 %collective-permute-start.1 = (bf16[256,256]{1,0:T(8,128)(2,1)}, bf16[256,256]{1,0:T(8,128)(2,1)S(1)}, u32[]{:S(2)}, u32[]{:S(2)}) collective-permute-start(bf16[256,256]{1,0:T(8,128)(2,1)} %refs_0_.3), channel_id=1, source_target_pairs={{0,4},{8,0},{16,8},{24,16},{28,24},{20,28},{12,20},{4,12},{1,5},{9... | collective-permute-start | bytes 393224 | tf_op jit(solution)/shard_map/ppermute | solution.py:436
  5.2 5.2 %collective-permute-start = (bf16[256,256]{1,0:T(8,128)(2,1)}, bf16[256,256]{1,0:T(8,128)(2,1)S(1)}, u32[]{:S(2)}, u32[]{:S(2)}) collective-permute-start(bf16[256,256]{1,0:T(8,128)(2,1)} %refs_0_.3), channel_id=1, source_target_pairs={{0,8},{8,16},{16,24},{24,28},{28,20},{20,12},{12,4},{4,0},{1,9},{9... | collective-permute-start | bytes 393224 | tf_op jit(solution)/shard_map/ppermute | solution.py:436
  10.3 6.2 %collective-permute-start.3 = (bf16[256,256]{1,0:T(8,128)(2,1)S(1)}, bf16[256,256]{1,0:T(8,128)(2,1)S(1)}, u32[]{:S(2)}, u32[]{:S(2)}) collective-permute-start(bf16[256,256]{1,0:T(8,128)(2,1)S(1)} %collective-permute-done.refs_1_), channel_id=1, source_target_pairs={{0,8},{8,16},{16,24},{24,28},{28,20},{20,12},{12,4},{4,0},{1,9},{9... | collective-permute-start | bytes 393224 | tf_op jit(solution)/shard_map/ppermute | solution.py:436
  10.8 5.7 %collective-permute-start.4 = (bf16[256,256]{1,0:T(8,128)(2,1)S(1)}, bf16[256,256]{1,0:T(8,128)(2,1)S(1)}, u32[]{:S(2)}, u32[]{:S(2)}) collective-permute-start(bf16[256,256]{1,0:T(8,128)(2,1)S(1)} %collective-permute-done.1.refs_2_), channel_id=1, source_target_pairs={{0,4},{8,0},{16,8},{24,16},{28,24},{20,28},{12,20},{4,12},{1,5},{9... | collective-permute-start | bytes 393224 | tf_op jit(solution)/shard_map/ppermute | solution.py:436
  16.5 11.6 %copy-start = (bf16[256,256]{1,0:T(8,128)(2,1)S(1)}, bf16[256,256]{1,0:T(8,128)(2,1)}, u32[]{:S(2)}) copy-start(bf16[256,256]{1,0:T(8,128)(2,1)} %refs_0_.3) | copy-start | bytes 393220
  16.6 5.9 %collective-permute-start.5 = (bf16[256,256]{1,0:T(8,128)(2,1)S(1)}, bf16[256,256]{1,0:T(8,128)(2,1)S(1)}, u32[]{:S(2)}, u32[]{:S(2)}) collective-permute-start(bf16[256,256]{1,0:T(8,128)(2,1)S(1)} %collective-permute-done.3.refs_3_), channel_id=1, source_target_pairs={{0,8},{8,16},{16,24},{24,28},{28,20},{20,12},{12,4},{4,0},{1,9},{9... | collective-permute-start | bytes 393224 | tf_op jit(solution)/shard_map/ppermute | solution.py:436
  17.4 5.1 %collective-permute-start.6 = (bf16[256,256]{1,0:T(8,128)(2,1)S(1)}, bf16[256,256]{1,0:T(8,128)(2,1)S(1)}, u32[]{:S(2)}, u32[]{:S(2)}) collective-permute-start(bf16[256,256]{1,0:T(8,128)(2,1)S(1)} %collective-permute-done.4.refs_4_), channel_id=1, source_target_pairs={{0,4},{8,0},{16,8},{24,16},{28,24},{20,28},{12,20},{4,12},{1,5},{9... | collective-permute-start | bytes 393224 | tf_op jit(solution)/shard_map/ppermute | solution.py:436
  22.5 5.7 %collective-permute-start.7 = (bf16[256,256]{1,0:T(8,128)(2,1)S(1)}, bf16[256,256]{1,0:T(8,128)(2,1)S(1)}, u32[]{:S(2)}, u32[]{:S(2)}) collective-permute-start(bf16[256,256]{1,0:T(8,128)(2,1)S(1)} %collective-permute-done.5.refs_5_), channel_id=1, source_target_pairs={{0,8},{8,16},{16,24},{24,28},{28,20},{20,12},{12,4},{4,0},{1,9},{9... | collective-permute-start | bytes 393224 | tf_op jit(solution)/shard_map/ppermute | solution.py:436
  28.9 10.1 %copy-start.1 = (bf16[256,256]{1,0:T(8,128)(2,1)S(1)}, bf16[256,256]{1,0:T(8,128)(2,1)}, u32[]{:S(2)}) copy-start(bf16[256,256]{1,0:T(8,128)(2,1)} %refs_2_.1) | copy-start | bytes 393220
  28.9 10.1 %copy-start.2 = (bf16[256,256]{1,0:T(8,128)(2,1)S(1)}, bf16[256,256]{1,0:T(8,128)(2,1)}, u32[]{:S(2)}) copy-start(bf16[256,256]{1,0:T(8,128)(2,1)} %refs_3_.1) | copy-start | bytes 393220
  28.9 1.6 %collective-permute-start.8 = (bf16[512,256]{1,0:T(8,128)(2,1)S(1)}, bf16[512,256]{1,0:T(8,128)(2,1)S(1)}, u32[]{:S(2)}, u32[]{:S(2)}) collective-permute-start(bf16[512,256]{1,0:T(8,128)(2,1)S(1)} %forward_product.2), channel_id=1, source_target_pairs={{0,1},{1,0},{2,3},{3,2},{4,5},{5,4},{6,7},{7,6},{8,9},{9,8},{10,11... | collective-permute-start | bytes 786440 | tf_op jit(solution)/shard_map/ppermute | solution.py:440
  30.5 8.4 %collective-permute-start.9 = (bf16[512,256]{1,0:T(8,128)(2,1)S(1)}, bf16[512,256]{1,0:T(8,128)(2,1)S(1)}, u32[]{:S(2)}, u32[]{:S(2)}) collective-permute-start(bf16[512,256]{1,0:T(8,128)(2,1)S(1)} %add_convert_fusion.refs_0_), channel_id=1, source_target_pairs={{0,2},{1,3},{2,0},{3,1},{4,6},{5,7},{6,4},{7,5},{8,10},{9,11},{10,... | collective-permute-start | bytes 786440 | tf_op jit(solution)/shard_map/ppermute | solution.py:440
  40.0 1.7 %collective-permute-start.10 = (bf16[640,256]{1,0:T(8,128)(2,1)S(1)}, bf16[640,256]{1,0:T(8,128)(2,1)S(1)}, u32[]{:S(2)}, u32[]{:S(2)}) collective-permute-start(bf16[640,256]{1,0:T(8,128)(2,1)S(1)} %get-tuple-element.53.own_ref), channel_id=1, source_target_pairs={{0,1},{1,0},{2,3},{3,2},{4,5},{5,4},{6,7},{7,6},{8,9},{9,8},{10,11... | collective-permute-start | bytes 983048 | tf_op jit(solution)/shard_map/ppermute | solution.py:440
  42.3 6.3 %collective-permute-start.11 = (bf16[320,256]{1,0:T(8,128)(2,1)S(1)}, bf16[320,256]{1,0:T(8,128)(2,1)S(1)}, u32[]{:S(2)}, u32[]{:S(2)}) collective-permute-start(bf16[320,256]{1,0:T(8,128)(2,1)S(1)} %get-tuple-element.63), channel_id=1, source_target_pairs={{0,8},{8,16},{16,24},{24,28},{28,20},{20,12},{12,4},{4,0},{1,9},{9... | collective-permute-start | bytes 491528 | tf_op jit(solution)/shard_map/ppermute | solution.py:436
  43.1 6.3 %collective-permute-start.14 = (bf16[320,256]{1,0:T(8,128)(2,1)S(1)}, bf16[320,256]{1,0:T(8,128)(2,1)S(1)}, u32[]{:S(2)}, u32[]{:S(2)}) collective-permute-start(bf16[320,256]{1,0:T(8,128)(2,1)S(1)} %get-tuple-element.66), channel_id=1, source_target_pairs={{0,4},{8,0},{16,8},{24,16},{28,24},{20,28},{12,20},{4,12},{1,5},{9... | collective-permute-start | bytes 491528 | tf_op jit(solution)/shard_map/ppermute | solution.py:436
  48.6 5.4 %collective-permute-start.12 = (bf16[320,256]{1,0:T(8,128)(2,1)S(1)}, bf16[320,256]{1,0:T(8,128)(2,1)S(1)}, u32[]{:S(2)}, u32[]{:S(2)}) collective-permute-start(bf16[320,256]{1,0:T(8,128)(2,1)S(1)} %add_convert_fusion.4), channel_id=1, source_target_pairs={{0,8},{8,16},{16,24},{24,28},{28,20},{20,12},{12,4},{4,0},{1,9},{9... | collective-permute-start | bytes 491528 | tf_op jit(solution)/shard_map/ppermute | solution.py:436
  49.5 5.5 %collective-permute-start.15 = (bf16[320,256]{1,0:T(8,128)(2,1)S(1)}, bf16[320,256]{1,0:T(8,128)(2,1)S(1)}, u32[]{:S(2)}, u32[]{:S(2)}) collective-permute-start(bf16[320,256]{1,0:T(8,128)(2,1)S(1)} %add_convert_fusion.2), channel_id=1, source_target_pairs={{0,4},{8,0},{16,8},{24,16},{28,24},{20,28},{12,20},{4,12},{1,5},{9... | collective-permute-start | bytes 491528 | tf_op jit(solution)/shard_map/ppermute | solution.py:436
  54.1 7.8 %collective-permute-start.13 = (bf16[320,256]{1,0:T(8,128)(2,1)S(1)}, bf16[320,256]{1,0:T(8,128)(2,1)S(1)}, u32[]{:S(2)}, u32[]{:S(2)}) collective-permute-start(bf16[320,256]{1,0:T(8,128)(2,1)S(1)} %add_convert_fusion.3), channel_id=1, source_target_pairs={{0,8},{8,16},{16,24},{24,28},{28,20},{20,12},{12,4},{4,0},{1,9},{9... | collective-permute-start | bytes 491528 | tf_op jit(solution)/shard_map/ppermute | solution.py:436
  55.0 7.0 %collective-permute-start.16 = (bf16[320,256]{1,0:T(8,128)(2,1)S(1)}, bf16[320,256]{1,0:T(8,128)(2,1)S(1)}, u32[]{:S(2)}, u32[]{:S(2)}) collective-permute-start(bf16[320,256]{1,0:T(8,128)(2,1)S(1)} %add_convert_fusion.1), channel_id=1, source_target_pairs={{0,4},{8,0},{16,8},{24,16},{28,24},{20,28},{12,20},{4,12},{1,5},{9... | collective-permute-start | bytes 491528 | tf_op jit(solution)/shard_map/ppermute | solution.py:436
  56.3 5.6 %collective-permute-start.17 = (bf16[64,256]{1,0:T(8,128)(2,1)S(1)}, bf16[64,256]{1,0:T(8,128)(2,1)S(1)}, u32[]{:S(2)}, u32[]{:S(2)}) collective-permute-start(bf16[64,256]{1,0:T(8,128)(2,1)S(1)} %slice.8), channel_id=1, source_target_pairs={{0,12},{8,4},{16,0},{24,8},{28,16},{20,24},{12,28},{4,20},{1,13},{... | collective-permute-start | bytes 98312 | tf_op jit(solution)/shard_map/ppermute | solution.py:436
  62.0 6.5 %collective-permute-start.18 = (bf16[256,256]{1,0:T(8,128)(2,1)S(1)}, bf16[256,256]{1,0:T(8,128)(2,1)S(1)}, u32[]{:S(2)}, u32[]{:S(2)}) collective-permute-start(bf16[256,256]{1,0:T(8,128)(2,1)S(1)} %add_convert_fusion.5), channel_id=1, source_target_pairs={{0,8},{8,16},{16,24},{24,28},{28,20},{20,12},{12,4},{4,0},{1,9},{9... | collective-permute-start | bytes 393224 | tf_op jit(solution)/shard_map/ppermute | solution.py:436
  63.4 3.8 %collective-permute-start.21 = (f32[64,256]{1,0:T(8,128)S(1)}, f32[64,256]{1,0:T(8,128)S(1)}, u32[]{:S(2)}, u32[]{:S(2)}) collective-permute-start(f32[64,256]{1,0:T(8,128)S(1)} %summed_terms.1.refs_3_), channel_id=1, source_target_pairs={{0,3},{1,2},{2,1},{3,0},{4,7},{5,6},{6,5},{7,4},{8,11},{9,10},{10,... | collective-permute-start | bytes 196616 | tf_op jit(solution)/shard_map/ppermute | solution.py:440
  63.5 5.0 %collective-permute-start.20 = (f32[64,256]{1,0:T(8,128)S(1)}, f32[64,256]{1,0:T(8,128)S(1)}, u32[]{:S(2)}, u32[]{:S(2)}) collective-permute-start(f32[64,256]{1,0:T(8,128)S(1)} %summed_terms.1.refs_3_), channel_id=1, source_target_pairs={{0,2},{1,3},{2,0},{3,1},{4,6},{5,7},{6,4},{7,5},{8,10},{9,11},{10,... | collective-permute-start | bytes 196616 | tf_op jit(solution)/shard_map/ppermute | solution.py:440
  64.2 4.3 %collective-permute-start.19 = (f32[64,256]{1,0:T(8,128)S(1)}, f32[64,256]{1,0:T(8,128)S(1)}, u32[]{:S(2)}, u32[]{:S(2)}) collective-permute-start(f32[64,256]{1,0:T(8,128)S(1)} %summed_terms.1.refs_3_), channel_id=1, source_target_pairs={{0,1},{1,0},{2,3},{3,2},{4,5},{5,4},{6,7},{7,6},{8,9},{9,8},{10,11... | collective-permute-start | bytes 196616 | tf_op jit(solution)/shard_map/ppermute | solution.py:440

commit v10 on v9

--- a/solution.py
+++ b/solution.py
@@ -248,6 +248,12 @@
     )(dense, *arrays)
 
 
+def partners_sum(values):
+    while len(values) > 1:
+        values = [values[i] + values[i + 1] for i in range(0, len(values), 2)]
+    return values[0]
+
+
 def middle_kernel(*refs, blocks, scale):
     sums, refs = refs[:blocks], refs[blocks:]
     weight_ref, refs = refs[0], refs[1:]
@@ -255,11 +261,11 @@
     weight = weight_ref[...]
     rows, width = act_ref.shape
     over_nodes = (((0,), (0,)), ((), ()))
-    terms = None
+    terms = []
     for index in range(blocks):
-        aggregate = sums[0][pl.ds(index * rows, rows), :].astype(jnp.float32)
-        for other in range(1, blocks):
-            aggregate += sums[other][pl.ds((index ^ other) * rows, rows), :].astype(jnp.float32)
+        aggregate = partners_sum(
+            [sums[other][pl.ds((index ^ other) * rows, rows), :].astype(jnp.float32) for other in range(blocks)]
+        )
         high = aggregate.astype(jnp.bfloat16)
         low = (aggregate - high.astype(jnp.float32)).astype(jnp.bfloat16)
         pre = jnp.dot(high, weight, preferred_element_type=jnp.float32)
@@ -274,12 +280,13 @@
             act_ref[...] = (pre * sig).astype(jnp.bfloat16)
         part = lax.dot_general(high, grad, over_nodes, preferred_element_type=jnp.float32)
         part += lax.dot_general(low, grad, over_nodes, preferred_element_type=jnp.float32)
-        terms = part if terms is None else terms + part
-    product[...] = terms * scale
+        terms.append(part)
+    product[...] = partners_sum(terms) * scale
     col = lax.axis_index("col")
     size = chunk_ref.shape[0]
-    chunk_ref[...] = product[pl.ds(pl.multiple_of(col * size, size), size), :]
-    sent = product[pl.ds(pl.multiple_of((col ^ 1) * size, size), size), :]
+    core = col & 1
+    chunk_ref[...] = product[pl.ds(pl.multiple_of(core * size, size), size), :]
+    sent = product[pl.ds(pl.multiple_of((core ^ 1) * size, size), size), :]
     high = sent.astype(jnp.bfloat16)
     low = (sent - high.astype(jnp.float32)).astype(jnp.bfloat16)
     message_ref[pl.ds(blocks * width, size), :] = high
@@ -289,7 +296,7 @@
 def middle(sums, weight, cotangents, total_nodes):
     rows, width = cotangents[0].shape
     blocks = len(cotangents)
-    size = width // (2 * blocks)
+    size = width // 2
     return pl.pallas_call(
         functools.partial(middle_kernel, blocks=blocks, scale=1.0 / math.sqrt(total_nodes)),
         out_shape=[
@@ -399,35 +406,48 @@
     )(*arrays)
 
 
-def finish_kernel(*refs, parts):
-    part_refs, chunk_refs, (features_ref, weight_ref) = refs[:parts], refs[parts:-2], refs[-2:]
+def finish_kernel(*refs):
+    *part_refs, features_ref = refs
     width = features_ref.shape[1]
     total = part_refs[0][pl.ds(0, width), :].astype(jnp.float32)
     for part_ref in part_refs[1:]:
         total += part_ref[pl.ds(0, width), :].astype(jnp.float32)
     features_ref[...] = total.astype(jnp.bfloat16).T
-    rows = chunk_refs[0].shape[0]
-    col = lax.axis_index("col")
-    for partner, chunk_ref in enumerate(chunk_refs):
-        weight_ref[pl.ds(pl.multiple_of((col ^ partner) * rows, rows), rows), :] = chunk_ref[...]
-
-
-def finish(parts, chunks):
+
+
+def finish(parts):
     width, rows = parts[0].shape
     return pl.pallas_call(
-        functools.partial(finish_kernel, parts=len(parts)),
-        out_shape=[
-            jax.ShapeDtypeStruct((rows, width), jnp.bfloat16),
-            jax.ShapeDtypeStruct((width, width), jnp.float32),
-        ],
-        in_specs=[pl.BlockSpec(memory_space=pltpu.VMEM)] * (len(parts) + len(chunks)),
-        out_specs=[pl.BlockSpec(memory_space=pltpu.VMEM)] * 2,
+        finish_kernel,
+        out_shape=jax.ShapeDtypeStruct((rows, width), jnp.bfloat16),
+        in_specs=[pl.BlockSpec(memory_space=pltpu.VMEM)] * len(parts),
+        out_specs=pl.BlockSpec(memory_space=pltpu.VMEM),
         compiler_params=pltpu.CompilerParams(vmem_limit_bytes=8 * mib),
         cost_estimate=pl.CostEstimate(
-            flops=len(parts) * rows * width, bytes_accessed=2 * (len(parts) + 5) * rows * width, transcendentals=0
+            flops=len(parts) * rows * width, bytes_accessed=2 * (len(parts) + 1) * rows * width, transcendentals=0
         ),
         name="finish",
-    )(*parts, *chunks)
+    )(*parts)
+
+
+def joined_kernel(own_ref, sibling_ref, weight_ref):
+    rows = own_ref.shape[0]
+    core = lax.axis_index("col") & 1
+    for turn, ref in enumerate((own_ref, sibling_ref)):
+        weight_ref[pl.ds(pl.multiple_of((core ^ turn) * rows, rows), rows), :] = ref[...]
+
+
+def joined(own, sibling):
+    rows, width = own.shape
+    return pl.pallas_call(
+        joined_kernel,
+        out_shape=jax.ShapeDtypeStruct((2 * rows, width), jnp.float32),
+        in_specs=[pl.BlockSpec(memory_space=pltpu.VMEM)] * 2,
+        out_specs=pl.BlockSpec(memory_space=pltpu.VMEM),
+        compiler_params=pltpu.CompilerParams(vmem_limit_bytes=8 * mib),
+        cost_estimate=pl.CostEstimate(flops=0, bytes_accessed=16 * rows * width, transcendentals=0),
+        name="joined",
+    )(own, sibling)
 
 
 def around(value, step):
@@ -443,23 +463,26 @@
 def gathered_shards(own, packed, stages, cotangent):
     reach = lax.axis_size("row") // 2
     rows = own.shape[0]
-    shards = [(((0, 0, 0, rows),), own)]
-    up = down = own
+    ups, downs = [own], [own]
+    for step in range(reach):
+        ups.append(around(ups[-1], 1))
     dense = packed
     others = [swapped(cotangent, "col", partner) for partner in range(2, lax.axis_size("col"), 2)]
-    for step in range(1, reach + 1):
-        up = around(up, 1)
-        if step < reach:
-            down = around(down, -1)
+    for step in range(1, reach):
+        down = around(downs[-1], -1)
         if step == 1:
-            up, down, dense, others = lax.optimization_barrier((up, down, dense, others))
-        elif step in (2, reach):
-            dense = stages.pop(0)(dense) if stages else dense
-        if 1 < step < reach:
-            up, down, dense = lax.optimization_barrier((up, down, dense))
-        shards.append((((-step, 0, 0, rows),), up))
-        if step < reach:
-            shards.append((((step, 0, 0, rows),), down))
+            down, dense, others = lax.optimization_barrier((down, dense, others))
+        elif step == 2:
+            dense = stages.pop(0)(dense)
+            down, dense = lax.optimization_barrier((down, dense))
+        elif step == reach - 1 and stages:
+            down, dense = lax.optimization_barrier((down, dense))
+        downs.append(down)
+    if stages:
+        dense = stages.pop(0)(dense)
+    shards = [(((0, 0, 0, rows),), own)]
+    shards += [(((-step, 0, 0, rows),), ups[step]) for step in range(1, reach + 1)]
+    shards += [(((step, 0, 0, rows),), downs[step]) for step in range(1, reach)]
     return shards, dense, [cotangent] + others
 
 
@@ -477,22 +500,17 @@
     up, down = around(above, 1), around(below, -1)
     all_terms = [(0, 0, terms)]
 
-    ups = tuple((offset, "zeros" if offset > 1 else "") for offset in range(reach - 1, 0, -1))
+    ups = tuple((offset, "zeros") for offset in range(reach - 1, 0, -1))
     downs = tuple((-offset, "zeros") for offset in range(reach - 2, 0, -1))
     strips = backward_product(cell, own, sibling, chunk, ups + downs + ((0, ""),), row_count, col_count)
     ups, downs, mine = strips[: reach - 1], strips[reach - 1 : -1], strips[-1]
     for step in range(1, reach):
         all_terms += [(-step, width, up), (step, width, down)]
-        relayed = around(down[width:], -2) if step == reach - 2 else None
         up = around(added(ups[step - 1], up), 1)
         if step < reach - 1:
             down = around(added(downs[step - 1], down), -1)
-        if relayed is not None:
-            up, down, relayed = lax.optimization_barrier((up, down, relayed))
-            all_terms.append((reach, 0, relayed))
-    chunk = summed_terms(all_terms, size)
-    chunks = [chunk] + [swapped(chunk, "col", partner) for partner in range(1, col_count)]
-    return [mine, up, down], chunks
+    all_terms.append((reach, width, up))
+    return [mine, up, down], summed_terms(all_terms, size)
 
 
 def per_device(features, weight, adj_tiles, tile_rows, tile_cols, tile_counts, out_grad):
@@ -512,9 +530,9 @@
     sums = [sums] + [swapped(sums, "col", partner) for partner in range(2, col_count, 2)]
     activations, message, chunk = middle(sums, weight, cotangents, node_rows * row_count * col_count)
     sibling = swapped(message, "col", 1)
-    parts, chunks = scattered_sums(dense, message, sibling, chunk)
-    grad_features, grad_weight = finish(parts, chunks)
-    return (activations, grad_features, grad_weight)
+    parts, half = scattered_sums(dense, message, sibling, chunk)
+    grad_weight = joined(half, swapped(half, "col", 1))
+    return (activations, finish(parts), grad_weight)
 
 
 def solution(mesh):

time: 69.5 us -> 68 us (0.978)
  Pallas kernels: 13.4 us -> 10.9 us
  waiting for transfers between devices: 31.7 us -> 32.9 us
    ppermute x15 -> x14, waiting for transfers between devices: 17.5 us -> 22.9 us  [around(): lax.ppermute(value, 'row', [(order[i], order[(i + step) % count]) for i i...]
    ppermute x7 -> x5, waiting for transfers between devices: 14.2 us -> 10 us  [swapped(): lax.ppermute(value, axis, [(i, i ^ partner) for i in range(lax.axis_size(...]
    pallas_call x1, Pallas kernels: 4.17 us -> 2.4 us  [build_stages(): pl.pallas_call(functools.partial(build_rest_kernel, blocks=blocks), out_s...]
    pallas_call x1, Pallas kernels: 4.18 us -> 2.65 us  [build_stages(): pl.pallas_call(functools.partial(build_first_kernel, blocks=blocks), out_...]
    ppermute x7 -> x5, starting transfers between devices: 5.14 us -> 3.63 us  [swapped(): lax.ppermute(value, axis, [(i, i ^ partner) for i in range(lax.axis_size(...]
    ppermute x15 -> x14, starting transfers between devices: 16.6 us -> 17.9 us  [around(): lax.ppermute(value, 'row', [(order[i], order[(i + step) % count]) for i i...]
    pallas_call x1 -> x2, Pallas kernels: 0.8 us -> 1.49 us  [the longest x1 0.76 us: finish(): pl.pallas_call(finish_kernel, out_shape=jax.ShapeDtypeStruct((rows, width...]
  transfers between devices with their start and end apart: 22 -> 19, of which waited for: 12 -> 11; matrix products, arithmetic and copies ran while one was open for 1% -> 1% of each run, Pallas kernels for 15% -> 11%
where the time goes in v10:
time: 68 us; the launch traced here: 67.8 us
  waiting for transfers between devices  32.9 us (48%)
  starting transfers between devices  21.5 us (32%)
  Pallas kernels  10.9 us (16%)
  between operations  1.47 us (2%)
  other arithmetic  1.01 us (1%)
    ppermute x14, waiting for transfers between devices, around(): lax.ppermute(value, 'row', [(order[i], order[(i + step) % count]) for i i...  22.9 us
    ppermute x14, starting transfers between devices, around(): lax.ppermute(value, 'row', [(order[i], order[(i + step) % count]) for i i...  17.9 us
    ppermute x5, waiting for transfers between devices, swapped(): lax.ppermute(value, axis, [(i, i ^ partner) for i in range(lax.axis_size(...  10 us
    ppermute x5, starting transfers between devices, swapped(): lax.ppermute(value, axis, [(i, i ^ partner) for i in range(lax.axis_size(...  3.63 us
    pallas_call x1, Pallas kernels, build_stages(): pl.pallas_call(functools.partial(build_first_kernel, blocks=blocks), out_...  2.65 us
    pallas_call x1, Pallas kernels, build_stages(): pl.pallas_call(functools.partial(build_rest_kernel, blocks=blocks), out_s...  2.4 us
    pallas_call x2, Pallas kernels, backward_product(): pl.pallas_call(functools.partial(backward_kernel, outputs=outputs, row_co...  1.76 us
    pallas_call x2, Pallas kernels, forward_product(): pl.pallas_call(functools.partial(forward_kernel, pieces=pieces, sibling=s...  1.42 us
  transfers between devices with their start and end apart: 19, of which 11 were waited for; matrix products, arithmetic and copies ran while one was open for 1% of the time, Pallas kernels for 11%

profile of v10, /device:TPU:0, one launch (start us, length us, event | category | flops | bytes accessed | tf_op | source)
XLA Modules:
  0.0 67.8 jit_solution(5183044424010092786)
XLA Ops:
  0.6 3.1 %collective-permute-start.4 = (bf16[256,256]{1,0:T(8,128)(2,1)}, bf16[256,256]{1,0:T(8,128)(2,1)S(1)}, u32[]{:S(2)}, u32[]{:S(2)}) collective-permute-start(bf16[256,256]{1,0:T(8,128)(2,1)} %refs_0_.3), channel_id=1, source_target_pairs={{0,8},{8,16},{16,24},{24,28},{28,20},{20,12},{12,4},{4,0},{1,9},{9... | collective-permute-start | bytes 393224 | tf_op jit(solution)/shard_map/ppermute | solution.py:456
  3.7 0.0 collective-permute-start
  3.7 1.9 %collective-permute-start.1 = (bf16[256,256]{1,0:T(8,128)(2,1)}, bf16[256,256]{1,0:T(8,128)(2,1)S(1)}, u32[]{:S(2)}, u32[]{:S(2)}) collective-permute-start(bf16[256,256]{1,0:T(8,128)(2,1)} %refs_3_.1), channel_id=1, source_target_pairs={{0,2},{1,3},{2,0},{3,1},{4,6},{5,7},{6,4},{7,5},{8,10},{9,11},{10,... | collective-permute-start | bytes 393224 | tf_op jit(solution)/shard_map/ppermute | solution.py:460
  5.6 1.7 %collective-permute-done.4.refs_1_ = bf16[256,256]{1,0:T(8,128)(2,1)S(1)} collective-permute-done((bf16[256,256]{1,0:T(8,128)(2,1)}, bf16[256,256]{1,0:T(8,128)(2,1)S(1)}, u32[]{:S(2)}, u32[]{:S(2)}) %collective-permute-start.4) | collective-permute-done | bytes 131104 | tf_op jit(solution)/shard_map/ppermute | solution.py:456
  7.4 1.8 %collective-permute-start.5 = (bf16[256,256]{1,0:T(8,128)(2,1)S(1)}, bf16[256,256]{1,0:T(8,128)(2,1)S(1)}, u32[]{:S(2)}, u32[]{:S(2)}) collective-permute-start(bf16[256,256]{1,0:T(8,128)(2,1)S(1)} %collective-permute-done.4.refs_1_), channel_id=1, source_target_pairs={{0,8},{8,16},{16,24},{24,28},{28,20},{20,12},{12,4},{4,0},{1,9},{9... | collective-permute-start | bytes 393224 | tf_op jit(solution)/shard_map/ppermute | solution.py:456
  9.8 0.7 %add_reduce_fusion.list_ref = s32[513]{0:T(1024)S(1)} fusion(s32[1,1,1]{2,1,0:T(1,128)} %bitcast.2, s32[1,1,256]{2,1,0:T(1,128)} %param.11, s32[1,1,256]{2,1,0:T(1,128)} %param.10), kind=kLoop, calls=%fused_computation.6 | loop fusion | flops 1026 | bytes 4104 | tf_op jit(solution)/shard_map/concatenate | solution.py:520
  10.5 0.0 collective-permute-done.refs_5_
  10.5 0.0 collective-permute-done.1.refs_4_
  10.5 0.3 collective-permute-start.2
  10.9 1.5 %collective-permute-done.5.refs_2_ = bf16[256,256]{1,0:T(8,128)(2,1)S(1)} collective-permute-done((bf16[256,256]{1,0:T(8,128)(2,1)S(1)}, bf16[256,256]{1,0:T(8,128)(2,1)S(1)}, u32[]{:S(2)}, u32[]{:S(2)}) %collective-permute-start.5) | collective-permute-done | bytes 131104 | tf_op jit(solution)/shard_map/ppermute | solution.py:456
  12.3 1.8 %collective-permute-start.6 = (bf16[256,256]{1,0:T(8,128)(2,1)S(1)}, bf16[256,256]{1,0:T(8,128)(2,1)S(1)}, u32[]{:S(2)}, u32[]{:S(2)}) collective-permute-start(bf16[256,256]{1,0:T(8,128)(2,1)S(1)} %collective-permute-done.5.refs_2_), channel_id=1, source_target_pairs={{0,8},{8,16},{16,24},{24,28},{28,20},{20,12},{12,4},{4,0},{1,9},{9... | collective-permute-start | bytes 393224 | tf_op jit(solution)/shard_map/ppermute | solution.py:456
  14.1 2.6 %build_first.1.half_ref = bf16[1024,2048]{1,0:T(8,128)(2,1)S(1)} custom-call(s32[513]{0:T(1024)S(1)} %add_reduce_fusion.list_ref, bf16[256,128,128]{2,1,0:T(8,128)(2,1)} %bitcast.3), custom_call_target="tpu_custom_call" | custom-call | flops 4194304 | bytes 6291456 | tf_op jit(solution)/shard_map/build_first/pallas_call | solution.py:174
  16.8 0.0 copy-start
  16.8 0.0 collective-permute-done.2.refs_6_
  16.8 0.5 collective-permute-start.3
  17.3 0.0 collective-permute-done.6.refs_3_
  17.3 1.7 %collective-permute-start.7 = (bf16[256,256]{1,0:T(8,128)(2,1)S(1)}, bf16[256,256]{1,0:T(8,128)(2,1)S(1)}, u32[]{:S(2)}, u32[]{:S(2)}) collective-permute-start(bf16[256,256]{1,0:T(8,128)(2,1)S(1)} %collective-permute-done.6.refs_3_), channel_id=1, source_target_pairs={{0,8},{8,16},{16,24},{24,28},{28,20},{20,12},{12,4},{4,0},{1,9},{9... | collective-permute-start | bytes 393224 | tf_op jit(solution)/shard_map/ppermute | solution.py:456
  19.1 2.8 %collective-permute-done.3.refs_7_ = bf16[256,256]{1,0:T(8,128)(2,1)S(1)} collective-permute-done((bf16[256,256]{1,0:T(8,128)(2,1)S(1)}, bf16[256,256]{1,0:T(8,128)(2,1)S(1)}, u32[]{:S(2)}, u32[]{:S(2)}) %collective-permute-start.3) | collective-permute-done | bytes 131104 | tf_op jit(solution)/shard_map/ppermute | solution.py:456
  21.9 2.4 %build_rest.1.dense_ref = bf16[1024,2048]{1,0:T(8,128)(2,1)S(1)} custom-call(s32[513]{0:T(1024)S(1)} %add_reduce_fusion.list_ref, bf16[256,128,128]{2,1,0:T(8,128)(2,1)} %bitcast.4, bf16[1024,2048]{1,0:T(8,128)(2,1)S(1)} %build_first.1.half_ref), custom_call_target="tpu_custom_call" | custom-call | flops 4194304 | bytes 6291456 | tf_op jit(solution)/shard_map/build_rest/pallas_call | solution.py:184
  24.3 0.0 collective-permute-done.7.refs_4_
  24.3 0.0 copy-done
  24.3 0.7 %forward_product.2 = bf16[512,256]{1,0:T(8,128)(2,1)S(1)} custom-call(bf16[1024,2048]{1,0:T(8,128)(2,1)S(1)} %build_rest.1.dense_ref, bf16[256,256]{1,0:T(8,128)(2,1)S(1)} %copy-done, bf16[256,256]{1,0:T(8,128)(2,1)S(1)} %collective-permute-done.4.refs_1_, bf16[256,256]{1,0:T(8,128)(2,1)S(1)} %collective-permute-done.5.refs_2_, ...), custom_call_target="tpu_custom_call" | custom-call | flops 536870912 | bytes 3407872 | tf_op jit(solution)/shard_map/forward_product/pallas_call | solution.py:236
  25.0 0.0 copy-start.1
  25.0 0.0 copy-start.2
  25.1 0.1 collective-permute-start.8
  25.1 0.7 %forward_product.3 = bf16[512,256]{1,0:T(8,128)(2,1)S(1)} custom-call(bf16[1024,2048]{1,0:T(8,128)(2,1)S(1)} %build_rest.1.dense_ref, bf16[256,256]{1,0:T(8,128)(2,1)S(1)} %copy-done, bf16[256,256]{1,0:T(8,128)(2,1)S(1)} %collective-permute-done.4.refs_1_, bf16[256,256]{1,0:T(8,128)(2,1)S(1)} %collective-permute-done.5.refs_2_, ...), custom_call_target="tpu_custom_call" | custom-call | flops 536870912 | bytes 3407872 | tf_op jit(solution)/shard_map/forward_product/pallas_call | solution.py:236
  25.9 0.8 %collective-permute-done.8 = bf16[512,256]{1,0:T(8,128)(2,1)S(1)} collective-permute-done((bf16[512,256]{1,0:T(8,128)(2,1)S(1)}, bf16[512,256]{1,0:T(8,128)(2,1)S(1)}, u32[]{:S(2)}, u32[]{:S(2)}) %collective-permute-start.8) | collective-permute-done | bytes 262176 | tf_op jit(solution)/shard_map/ppermute | solution.py:460
  26.7 0.1 add_convert_fusion.refs_0_
  26.7 1.5 %collective-permute-start.9 = (bf16[512,256]{1,0:T(8,128)(2,1)S(1)}, bf16[512,256]{1,0:T(8,128)(2,1)S(1)}, u32[]{:S(2)}, u32[]{:S(2)}) collective-permute-start(bf16[512,256]{1,0:T(8,128)(2,1)S(1)} %add_convert_fusion.refs_0_), channel_id=1, source_target_pairs={{0,2},{1,3},{2,0},{3,1},{4,6},{5,7},{6,4},{7,5},{8,10},{9,11},{10,... | collective-permute-start | bytes 786440 | tf_op jit(solution)/shard_map/ppermute | solution.py:460
  28.2 6.9 %collective-permute-done.9.refs_1_ = bf16[512,256]{1,0:T(8,128)(2,1)S(1)} collective-permute-done((bf16[512,256]{1,0:T(8,128)(2,1)S(1)}, bf16[512,256]{1,0:T(8,128)(2,1)S(1)}, u32[]{:S(2)}, u32[]{:S(2)}) %collective-permute-start.9) | collective-permute-done | bytes 262176 | tf_op jit(solution)/shard_map/ppermute | solution.py:460
  35.1 0.0 copy-done.1
  35.1 0.0 copy-done.2
  35.1 1.0 %middle.1 = (bf16[256,256]{1,0:T(8,128)(2,1)}, bf16[768,256]{1,0:T(8,128)(2,1)S(1)}, f32[128,256]{1,0:T(8,128)S(1)}) custom-call(bf16[512,256]{1,0:T(8,128)(2,1)S(1)} %add_convert_fusion.refs_0_, bf16[512,256]{1,0:T(8,128)(2,1)S(1)} %collective-permute-done.9.refs_1_, bf16[256,256]{1,0:T(8,128)(2,1)S(1)} %copy-done.1, bf16[256,256]{1,0:T(8,128)(2,1)S(1)} %copy-done.2, ...), custom_call_target="tpu_custom_call" | custom-call | flops 335544320 | bytes 1572864 | tf_op jit(solution)/shard_map/middle/pallas_call | solution.py:300
  36.2 0.1 collective-permute-start.10
  36.3 1.7 %collective-permute-done.10.sibling_ref = bf16[768,256]{1,0:T(8,128)(2,1)S(1)} collective-permute-done((bf16[768,256]{1,0:T(8,128)(2,1)S(1)}, bf16[768,256]{1,0:T(8,128)(2,1)S(1)}, u32[]{:S(2)}, u32[]{:S(2)}) %collective-permute-start.10) | collective-permute-done | bytes 393248 | tf_op jit(solution)/shard_map/ppermute | solution.py:460
  38.0 0.6 backward_product.2
  38.6 2.6 %collective-permute-start.11 = (bf16[384,256]{1,0:T(8,128)(2,1)S(1)}, bf16[384,256]{1,0:T(8,128)(2,1)S(1)}, u32[]{:S(2)}, u32[]{:S(2)}) collective-permute-start(bf16[384,256]{1,0:T(8,128)(2,1)S(1)} %get-tuple-element.52), channel_id=1, source_target_pairs={{0,8},{8,16},{16,24},{24,28},{28,20},{20,12},{12,4},{4,0},{1,9},{9... | collective-permute-start | bytes 589832 | tf_op jit(solution)/shard_map/ppermute | solution.py:456
  41.2 0.0 collective-permute-start.15
  41.2 1.1 %backward_product.3 = (bf16[384,256]{1,0:T(8,128)(2,1)S(1)}, bf16[384,256]{1,0:T(8,128)(2,1)S(1)}, bf16[384,256]{1,0:T(8,128)(2,1)S(1)}, bf16[384,256]{1,0:T(8,1...) custom-call(bf16[1024,2048]{1,0:T(8,128)(2,1)S(1)} %build_rest.1.dense_ref, ...), custom_call_target="tpu_custom_call" | custom-call | flops 134217728 | bytes 786432 | tf_op jit(solution)/shard_map/backward_product/pallas_call | solution.py:362
  42.3 3.3 %collective-permute-done.11.refs_1_ = bf16[384,256]{1,0:T(8,128)(2,1)S(1)} collective-permute-done((bf16[384,256]{1,0:T(8,128)(2,1)S(1)}, bf16[384,256]{1,0:T(8,128)(2,1)S(1)}, u32[]{:S(2)}, u32[]{:S(2)}) %collective-permute-start.11) | collective-permute-done | bytes 196640 | tf_op jit(solution)/shard_map/ppermute | solution.py:456
  45.7 2.5 %collective-permute-start.12 = (bf16[384,256]{1,0:T(8,128)(2,1)S(1)}, bf16[384,256]{1,0:T(8,128)(2,1)S(1)}, u32[]{:S(2)}, u32[]{:S(2)}) collective-permute-start(bf16[384,256]{1,0:T(8,128)(2,1)S(1)} %add_convert_fusion.5), channel_id=1, source_target_pairs={{0,8},{8,16},{16,24},{24,28},{28,20},{20,12},{12,4},{4,0},{1,9},{9... | collective-permute-start | bytes 589832 | tf_op jit(solution)/shard_map/ppermute | solution.py:456
  48.2 0.0 collective-permute-done.15.refs_2_
  48.3 1.0 %collective-permute-start.16 = (bf16[384,256]{1,0:T(8,128)(2,1)S(1)}, bf16[384,256]{1,0:T(8,128)(2,1)S(1)}, u32[]{:S(2)}, u32[]{:S(2)}) collective-permute-start(bf16[384,256]{1,0:T(8,128)(2,1)S(1)} %add_convert_fusion.2), channel_id=1, source_target_pairs={{0,4},{8,0},{16,8},{24,16},{28,24},{20,28},{12,20},{4,12},{1,5},{9... | collective-permute-start | bytes 589832 | tf_op jit(solution)/shard_map/ppermute | solution.py:456
  49.3 4.5 %collective-permute-done.12.refs_3_ = bf16[384,256]{1,0:T(8,128)(2,1)S(1)} collective-permute-done((bf16[384,256]{1,0:T(8,128)(2,1)S(1)}, bf16[384,256]{1,0:T(8,128)(2,1)S(1)}, u32[]{:S(2)}, u32[]{:S(2)}) %collective-permute-start.12) | collective-permute-done | bytes 196640 | tf_op jit(solution)/shard_map/ppermute | solution.py:456
  53.9 0.5 collective-permute-start.13
  54.4 0.0 collective-permute-done.16.refs_4_
  54.5 1.6 %collective-permute-start.17 = (bf16[384,256]{1,0:T(8,128)(2,1)S(1)}, bf16[384,256]{1,0:T(8,128)(2,1)S(1)}, u32[]{:S(2)}, u32[]{:S(2)}) collective-permute-start(bf16[384,256]{1,0:T(8,128)(2,1)S(1)} %add_convert_fusion.1), channel_id=1, source_target_pairs={{0,4},{8,0},{16,8},{24,16},{28,24},{20,28},{12,20},{4,12},{1,5},{9... | collective-permute-start | bytes 589832 | tf_op jit(solution)/shard_map/ppermute | solution.py:456
  56.1 3.7 %collective-permute-done.13.refs_5_ = bf16[384,256]{1,0:T(8,128)(2,1)S(1)} collective-permute-done((bf16[384,256]{1,0:T(8,128)(2,1)S(1)}, bf16[384,256]{1,0:T(8,128)(2,1)S(1)}, u32[]{:S(2)}, u32[]{:S(2)}) %collective-permute-start.13) | collective-permute-done | bytes 196640 | tf_op jit(solution)/shard_map/ppermute | solution.py:456
  59.8 0.3 collective-permute-start.14
  60.2 0.0 collective-permute-done.17.refs_2_.refs_6_
  60.2 5.4 %collective-permute-done.14.refs_1_.refs_7_ = bf16[384,256]{1,0:T(8,128)(2,1)S(1)} collective-permute-done((bf16[384,256]{1,0:T(8,128)(2,1)S(1)}, bf16[384,256]{1,0:T(8,128)(2,1)S(1)}, u32[]{:S(2)}, u32[]{:S(2)}) %collective-permute-start.14) | collective-permute-done | bytes 196640 | tf_op jit(solution)/shard_map/ppermute | solution.py:456
  65.6 0.1 summed_terms.1.own_ref
  65.7 0.1 collective-permute-start.18
  65.8 0.8 %finish.1 = bf16[256,256]{1,0:T(8,128)(2,1)} custom-call(bf16[256,256]{1,0:T(8,128)(2,1)S(1)} %get-tuple-element.48.refs_0_, bf16[384,256]{1,0:T(8,128)(2,1)S(1)} %collective-permute-done.14.refs_1_.refs_7_, bf16[384,256]{1,0:T(8,128)(2,1)S(1)} %collective-permute-done.17.refs_2_.refs_6_), custom_call_target="tpu_custom_call" | custom-call | flops 196608 | bytes 524288 | tf_op jit(solution)/shard_map/finish/pallas_call | solution.py:420
  66.5 0.6 collective-permute-done.18.sibling_ref
  67.1 0.7 %joined.1 = f32[256,256]{1,0:T(8,128)} custom-call(f32[128,256]{1,0:T(8,128)S(1)} %summed_terms.1.own_ref, f32[128,256]{1,0:T(8,128)S(1)} %collective-permute-done.18.sibling_ref), custom_call_target="tpu_custom_call" | custom-call | bytes 524288 | tf_op jit(solution)/shard_map/joined/pallas_call | solution.py:442
  (5 shorter events, 0.2 us)
Async XLA Ops:
  0.6 6.7 %collective-permute-start.4 = (bf16[256,256]{1,0:T(8,128)(2,1)}, bf16[256,256]{1,0:T(8,128)(2,1)S(1)}, u32[]{:S(2)}, u32[]{:S(2)}) collective-permute-start(bf16[256,256]{1,0:T(8,128)(2,1)} %refs_0_.3), channel_id=1, source_target_pairs={{0,8},{8,16},{16,24},{24,28},{28,20},{20,12},{12,4},{4,0},{1,9},{9... | collective-permute-start | bytes 393224 | tf_op jit(solution)/shard_map/ppermute | solution.py:456
  3.7 6.8 %collective-permute-start = (bf16[256,256]{1,0:T(8,128)(2,1)}, bf16[256,256]{1,0:T(8,128)(2,1)S(1)}, u32[]{:S(2)}, u32[]{:S(2)}) collective-permute-start(bf16[256,256]{1,0:T(8,128)(2,1)} %refs_0_.3), channel_id=1, source_target_pairs={{0,4},{8,0},{16,8},{24,16},{28,24},{20,28},{12,20},{4,12},{1,5},{9... | collective-permute-start | bytes 393224 | tf_op jit(solution)/shard_map/ppermute | solution.py:456
  3.7 6.8 %collective-permute-start.1 = (bf16[256,256]{1,0:T(8,128)(2,1)}, bf16[256,256]{1,0:T(8,128)(2,1)S(1)}, u32[]{:S(2)}, u32[]{:S(2)}) collective-permute-start(bf16[256,256]{1,0:T(8,128)(2,1)} %refs_3_.1), channel_id=1, source_target_pairs={{0,2},{1,3},{2,0},{3,1},{4,6},{5,7},{6,4},{7,5},{8,10},{9,11},{10,... | collective-permute-start | bytes 393224 | tf_op jit(solution)/shard_map/ppermute | solution.py:460
  7.4 5.0 %collective-permute-start.5 = (bf16[256,256]{1,0:T(8,128)(2,1)S(1)}, bf16[256,256]{1,0:T(8,128)(2,1)S(1)}, u32[]{:S(2)}, u32[]{:S(2)}) collective-permute-start(bf16[256,256]{1,0:T(8,128)(2,1)S(1)} %collective-permute-done.4.refs_1_), channel_id=1, source_target_pairs={{0,8},{8,16},{16,24},{24,28},{28,20},{20,12},{12,4},{4,0},{1,9},{9... | collective-permute-start | bytes 393224 | tf_op jit(solution)/shard_map/ppermute | solution.py:456
  10.5 6.3 %collective-permute-start.2 = (bf16[256,256]{1,0:T(8,128)(2,1)S(1)}, bf16[256,256]{1,0:T(8,128)(2,1)S(1)}, u32[]{:S(2)}, u32[]{:S(2)}) collective-permute-start(bf16[256,256]{1,0:T(8,128)(2,1)S(1)} %collective-permute-done.refs_5_), channel_id=1, source_target_pairs={{0,4},{8,0},{16,8},{24,16},{28,24},{20,28},{12,20},{4,12},{1,5},{9... | collective-permute-start | bytes 393224 | tf_op jit(solution)/shard_map/ppermute | solution.py:456
  12.3 5.0 %collective-permute-start.6 = (bf16[256,256]{1,0:T(8,128)(2,1)S(1)}, bf16[256,256]{1,0:T(8,128)(2,1)S(1)}, u32[]{:S(2)}, u32[]{:S(2)}) collective-permute-start(bf16[256,256]{1,0:T(8,128)(2,1)S(1)} %collective-permute-done.5.refs_2_), channel_id=1, source_target_pairs={{0,8},{8,16},{16,24},{24,28},{28,20},{20,12},{12,4},{4,0},{1,9},{9... | collective-permute-start | bytes 393224 | tf_op jit(solution)/shard_map/ppermute | solution.py:456
  16.8 7.5 %copy-start = (bf16[256,256]{1,0:T(8,128)(2,1)S(1)}, bf16[256,256]{1,0:T(8,128)(2,1)}, u32[]{:S(2)}) copy-start(bf16[256,256]{1,0:T(8,128)(2,1)} %refs_0_.3) | copy-start | bytes 393220
  16.8 5.1 %collective-permute-start.3 = (bf16[256,256]{1,0:T(8,128)(2,1)S(1)}, bf16[256,256]{1,0:T(8,128)(2,1)S(1)}, u32[]{:S(2)}, u32[]{:S(2)}) collective-permute-start(bf16[256,256]{1,0:T(8,128)(2,1)S(1)} %collective-permute-done.2.refs_6_), channel_id=1, source_target_pairs={{0,4},{8,0},{16,8},{24,16},{28,24},{20,28},{12,20},{4,12},{1,5},{9... | collective-permute-start | bytes 393224 | tf_op jit(solution)/shard_map/ppermute | solution.py:456
  17.3 6.9 %collective-permute-start.7 = (bf16[256,256]{1,0:T(8,128)(2,1)S(1)}, bf16[256,256]{1,0:T(8,128)(2,1)S(1)}, u32[]{:S(2)}, u32[]{:S(2)}) collective-permute-start(bf16[256,256]{1,0:T(8,128)(2,1)S(1)} %collective-permute-done.6.refs_3_), channel_id=1, source_target_pairs={{0,8},{8,16},{16,24},{24,28},{28,20},{20,12},{12,4},{4,0},{1,9},{9... | collective-permute-start | bytes 393224 | tf_op jit(solution)/shard_map/ppermute | solution.py:456
  25.0 10.1 %copy-start.1 = (bf16[256,256]{1,0:T(8,128)(2,1)S(1)}, bf16[256,256]{1,0:T(8,128)(2,1)}, u32[]{:S(2)}) copy-start(bf16[256,256]{1,0:T(8,128)(2,1)} %refs_2_.1) | copy-start | bytes 393220
  25.0 10.1 %copy-start.2 = (bf16[256,256]{1,0:T(8,128)(2,1)S(1)}, bf16[256,256]{1,0:T(8,128)(2,1)}, u32[]{:S(2)}) copy-start(bf16[256,256]{1,0:T(8,128)(2,1)} %refs_3_.1) | copy-start | bytes 393220
  25.1 1.6 %collective-permute-start.8 = (bf16[512,256]{1,0:T(8,128)(2,1)S(1)}, bf16[512,256]{1,0:T(8,128)(2,1)S(1)}, u32[]{:S(2)}, u32[]{:S(2)}) collective-permute-start(bf16[512,256]{1,0:T(8,128)(2,1)S(1)} %forward_product.2), channel_id=1, source_target_pairs={{0,1},{1,0},{2,3},{3,2},{4,5},{5,4},{6,7},{7,6},{8,9},{9,8},{10,11... | collective-permute-start | bytes 786440 | tf_op jit(solution)/shard_map/ppermute | solution.py:460
  26.7 8.4 %collective-permute-start.9 = (bf16[512,256]{1,0:T(8,128)(2,1)S(1)}, bf16[512,256]{1,0:T(8,128)(2,1)S(1)}, u32[]{:S(2)}, u32[]{:S(2)}) collective-permute-start(bf16[512,256]{1,0:T(8,128)(2,1)S(1)} %add_convert_fusion.refs_0_), channel_id=1, source_target_pairs={{0,2},{1,3},{2,0},{3,1},{4,6},{5,7},{6,4},{7,5},{8,10},{9,11},{10,... | collective-permute-start | bytes 786440 | tf_op jit(solution)/shard_map/ppermute | solution.py:460
  36.2 1.8 %collective-permute-start.10 = (bf16[768,256]{1,0:T(8,128)(2,1)S(1)}, bf16[768,256]{1,0:T(8,128)(2,1)S(1)}, u32[]{:S(2)}, u32[]{:S(2)}) collective-permute-start(bf16[768,256]{1,0:T(8,128)(2,1)S(1)} %get-tuple-element.42.own_ref), channel_id=1, source_target_pairs={{0,1},{1,0},{2,3},{3,2},{4,5},{5,4},{6,7},{7,6},{8,9},{9,8},{10,11... | collective-permute-start | bytes 1179656 | tf_op jit(solution)/shard_map/ppermute | solution.py:460
  38.6 7.0 %collective-permute-start.11 = (bf16[384,256]{1,0:T(8,128)(2,1)S(1)}, bf16[384,256]{1,0:T(8,128)(2,1)S(1)}, u32[]{:S(2)}, u32[]{:S(2)}) collective-permute-start(bf16[384,256]{1,0:T(8,128)(2,1)S(1)} %get-tuple-element.52), channel_id=1, source_target_pairs={{0,8},{8,16},{16,24},{24,28},{28,20},{20,12},{12,4},{4,0},{1,9},{9... | collective-permute-start | bytes 589832 | tf_op jit(solution)/shard_map/ppermute | solution.py:456
  41.2 7.0 %collective-permute-start.15 = (bf16[384,256]{1,0:T(8,128)(2,1)S(1)}, bf16[384,256]{1,0:T(8,128)(2,1)S(1)}, u32[]{:S(2)}, u32[]{:S(2)}) collective-permute-start(bf16[384,256]{1,0:T(8,128)(2,1)S(1)} %get-tuple-element.55), channel_id=1, source_target_pairs={{0,4},{8,0},{16,8},{24,16},{28,24},{20,28},{12,20},{4,12},{1,5},{9... | collective-permute-start | bytes 589832 | tf_op jit(solution)/shard_map/ppermute | solution.py:456
  45.7 8.2 %collective-permute-start.12 = (bf16[384,256]{1,0:T(8,128)(2,1)S(1)}, bf16[384,256]{1,0:T(8,128)(2,1)S(1)}, u32[]{:S(2)}, u32[]{:S(2)}) collective-permute-start(bf16[384,256]{1,0:T(8,128)(2,1)S(1)} %add_convert_fusion.5), channel_id=1, source_target_pairs={{0,8},{8,16},{16,24},{24,28},{28,20},{20,12},{12,4},{4,0},{1,9},{9... | collective-permute-start | bytes 589832 | tf_op jit(solution)/shard_map/ppermute | solution.py:456
  48.3 6.2 %collective-permute-start.16 = (bf16[384,256]{1,0:T(8,128)(2,1)S(1)}, bf16[384,256]{1,0:T(8,128)(2,1)S(1)}, u32[]{:S(2)}, u32[]{:S(2)}) collective-permute-start(bf16[384,256]{1,0:T(8,128)(2,1)S(1)} %add_convert_fusion.2), channel_id=1, source_target_pairs={{0,4},{8,0},{16,8},{24,16},{28,24},{20,28},{12,20},{4,12},{1,5},{9... | collective-permute-start | bytes 589832 | tf_op jit(solution)/shard_map/ppermute | solution.py:456
  53.9 5.9 %collective-permute-start.13 = (bf16[384,256]{1,0:T(8,128)(2,1)S(1)}, bf16[384,256]{1,0:T(8,128)(2,1)S(1)}, u32[]{:S(2)}, u32[]{:S(2)}) collective-permute-start(bf16[384,256]{1,0:T(8,128)(2,1)S(1)} %add_convert_fusion.4), channel_id=1, source_target_pairs={{0,8},{8,16},{16,24},{24,28},{28,20},{20,12},{12,4},{4,0},{1,9},{9... | collective-permute-start | bytes 589832 | tf_op jit(solution)/shard_map/ppermute | solution.py:456
  54.5 5.7 %collective-permute-start.17 = (bf16[384,256]{1,0:T(8,128)(2,1)S(1)}, bf16[384,256]{1,0:T(8,128)(2,1)S(1)}, u32[]{:S(2)}, u32[]{:S(2)}) collective-permute-start(bf16[384,256]{1,0:T(8,128)(2,1)S(1)} %add_convert_fusion.1), channel_id=1, source_target_pairs={{0,4},{8,0},{16,8},{24,16},{28,24},{20,28},{12,20},{4,12},{1,5},{9... | collective-permute-start | bytes 589832 | tf_op jit(solution)/shard_map/ppermute | solution.py:456
  59.8 5.7 %collective-permute-start.14 = (bf16[384,256]{1,0:T(8,128)(2,1)S(1)}, bf16[384,256]{1,0:T(8,128)(2,1)S(1)}, u32[]{:S(2)}, u32[]{:S(2)}) collective-permute-start(bf16[384,256]{1,0:T(8,128)(2,1)S(1)} %add_convert_fusion.3), channel_id=1, source_target_pairs={{0,8},{8,16},{16,24},{24,28},{28,20},{20,12},{12,4},{4,0},{1,9},{9... | collective-permute-start | bytes 589832 | tf_op jit(solution)/shard_map/ppermute | solution.py:456
  65.7 1.4 %collective-permute-start.18 = (f32[128,256]{1,0:T(8,128)S(1)}, f32[128,256]{1,0:T(8,128)S(1)}, u32[]{:S(2)}, u32[]{:S(2)}) collective-permute-start(f32[128,256]{1,0:T(8,128)S(1)} %summed_terms.1.own_ref), channel_id=1, source_target_pairs={{0,1},{1,0},{2,3},{3,2},{4,5},{5,4},{6,7},{7,6},{8,9},{9,8},{10,11... | collective-permute-start | bytes 393224 | tf_op jit(solution)/shard_map/ppermute | solution.py:460

commit v11 on v10

--- a/solution.py
+++ b/solution.py
@@ -83,9 +83,13 @@
     return (list_ref[2 * tiles_ref.shape[0]] + chunk_tiles - 1) // chunk_tiles
 
 
+def first_chunks(list_ref, tiles_ref):
+    return (live_chunks(list_ref, tiles_ref) * 3 + 7) // 8
+
+
 def build_first_kernel(list_ref, tiles_ref, dense_ref, total, held, sems, *, blocks):
-    half = (live_chunks(list_ref, tiles_ref) + 1) // 2
-    run = add_tiles(list_ref, tiles_ref, total, held, sems, 0, half, first_block=0, blocks=blocks, steps=1)
+    part = first_chunks(list_ref, tiles_ref)
+    run = add_tiles(list_ref, tiles_ref, total, held, sems, 0, part, first_block=0, blocks=blocks, steps=1)
 
     def clear(down):
         total[down, :] = jnp.zeros((down.size, total.shape[1]), jnp.float32)
@@ -101,7 +105,8 @@
 def build_rest_kernel(list_ref, tiles_ref, half_ref, dense_ref, total, held, sems, *, blocks):
     chunks = live_chunks(list_ref, tiles_ref)
     run = add_tiles(
-        list_ref, tiles_ref, total, held, sems, (chunks + 1) // 2, chunks, first_block=0, blocks=blocks, steps=1
+        list_ref, tiles_ref, total, held, sems, first_chunks(list_ref, tiles_ref), chunks,
+        first_block=0, blocks=blocks, steps=1,
     )
 
     def widened(down):
@@ -463,20 +468,22 @@
 def gathered_shards(own, packed, stages, cotangent):
     reach = lax.axis_size("row") // 2
     rows = own.shape[0]
-    ups, downs = [own], [own]
-    for step in range(reach):
-        ups.append(around(ups[-1], 1))
-    dense = packed
-    others = [swapped(cotangent, "col", partner) for partner in range(2, lax.axis_size("col"), 2)]
-    for step in range(1, reach):
+    ups, downs, dense = [own], [own], packed
+    others = []
+    for step in range(1, reach + 1):
+        up = around(ups[-1], 1)
+        if step == reach - 1:
+            up, dense, others = lax.optimization_barrier((up, dense, others))
+        ups.append(up)
+        if step == reach:
+            break
         down = around(downs[-1], -1)
         if step == 1:
-            down, dense, others = lax.optimization_barrier((down, dense, others))
+            down, dense = lax.optimization_barrier((down, dense))
         elif step == 2:
             dense = stages.pop(0)(dense)
-            down, dense = lax.optimization_barrier((down, dense))
-        elif step == reach - 1 and stages:
-            down, dense = lax.optimization_barrier((down, dense))
+            down, dense, cotangent = lax.optimization_barrier((down, dense, cotangent))
+            others = [swapped(cotangent, "col", partner) for partner in range(2, lax.axis_size("col"), 2)]
         downs.append(down)
     if stages:
         dense = stages.pop(0)(dense)

time: 68 us -> 67.1 us (0.987)
  starting transfers between devices: 21.5 us -> 20.8 us
    ppermute x14, starting transfers between devices: 17.9 us -> 17 us  [around(): lax.ppermute(value, 'row', [(order[i], order[(i + step) % count]) for i i...]
  transfers between devices with their start and end apart: 19 -> 19, of which waited for: 11 -> 14; matrix products, arithmetic and copies ran while one was open for 1% -> 1% of each run, Pallas kernels for 11% -> 11%
where the time goes in v11:
time: 67.1 us; the launch traced here: 66.9 us
  waiting for transfers between devices  32.8 us (49%)
  starting transfers between devices  20.8 us (31%)
  Pallas kernels  10.9 us (16%)
  between operations  1.43 us (2%)
  other arithmetic  1.01 us (2%)
    ppermute x14, waiting for transfers between devices, around(): lax.ppermute(value, 'row', [(order[i], order[(i + step) % count]) for i i...  22.9 us
    ppermute x14, starting transfers between devices, around(): lax.ppermute(value, 'row', [(order[i], order[(i + step) % count]) for i i...  17 us
    ppermute x5, waiting for transfers between devices, swapped(): lax.ppermute(value, axis, [(i, i ^ partner) for i in range(lax.axis_size(...  9.92 us
    ppermute x5, starting transfers between devices, swapped(): lax.ppermute(value, axis, [(i, i ^ partner) for i in range(lax.axis_size(...  3.84 us
    pallas_call x1, Pallas kernels, build_stages(): pl.pallas_call(functools.partial(build_first_kernel, blocks=blocks), out_...  2.66 us
    pallas_call x1, Pallas kernels, build_stages(): pl.pallas_call(functools.partial(build_rest_kernel, blocks=blocks), out_s...  2.39 us
    pallas_call x2, Pallas kernels, backward_product(): pl.pallas_call(functools.partial(backward_kernel, outputs=outputs, row_co...  1.75 us
    pallas_call x2, Pallas kernels, forward_product(): pl.pallas_call(functools.partial(forward_kernel, pieces=pieces, sibling=s...  1.42 us
  transfers between devices with their start and end apart: 19, of which 14 were waited for; matrix products, arithmetic and copies ran while one was open for 1% of the time, Pallas kernels for 11%

profile of v11, /device:TPU:0, one launch (start us, length us, event | category | flops | bytes accessed | tf_op | source)
XLA Modules:
  0.0 66.9 jit_solution(17493422922142147422)
XLA Ops:
  0.6 3.0 %collective-permute-start.3 = (bf16[256,256]{1,0:T(8,128)(2,1)}, bf16[256,256]{1,0:T(8,128)(2,1)S(1)}, u32[]{:S(2)}, u32[]{:S(2)}) collective-permute-start(bf16[256,256]{1,0:T(8,128)(2,1)} %refs_0_.3), channel_id=1, source_target_pairs={{0,4},{8,0},{16,8},{24,16},{28,24},{20,28},{12,20},{4,12},{1,5},{9... | collective-permute-start | bytes 393224 | tf_op jit(solution)/shard_map/ppermute | solution.py:461
  3.6 0.1 collective-permute-start
  4.4 0.7 %add_reduce_fusion.list_ref = s32[513]{0:T(1024)S(1)} fusion(s32[1,1,1]{2,1,0:T(1,128)} %bitcast.2, s32[1,1,256]{2,1,0:T(1,128)} %param.11, s32[1,1,256]{2,1,0:T(1,128)} %param.10), kind=kLoop, calls=%fused_computation.6 | loop fusion | flops 1026 | bytes 4104 | tf_op jit(solution)/shard_map/concatenate | solution.py:527
  5.1 2.3 %collective-permute-done.3.refs_5_ = bf16[256,256]{1,0:T(8,128)(2,1)S(1)} collective-permute-done((bf16[256,256]{1,0:T(8,128)(2,1)}, bf16[256,256]{1,0:T(8,128)(2,1)S(1)}, u32[]{:S(2)}, u32[]{:S(2)}) %collective-permute-start.3) | collective-permute-done | bytes 131104 | tf_op jit(solution)/shard_map/ppermute | solution.py:461
  7.4 1.7 %collective-permute-start.4 = (bf16[256,256]{1,0:T(8,128)(2,1)S(1)}, bf16[256,256]{1,0:T(8,128)(2,1)S(1)}, u32[]{:S(2)}, u32[]{:S(2)}) collective-permute-start(bf16[256,256]{1,0:T(8,128)(2,1)S(1)} %collective-permute-done.3.refs_5_), channel_id=1, source_target_pairs={{0,4},{8,0},{16,8},{24,16},{28,24},{20,28},{12,20},{4,12},{1,5},{9... | collective-permute-start | bytes 393224 | tf_op jit(solution)/shard_map/ppermute | solution.py:461
  9.1 0.0 collective-permute-done.refs_1_
  9.1 0.3 collective-permute-start.1
  9.4 0.0 copy-start.2
  9.4 2.7 %build_first.1.half_ref = bf16[1024,2048]{1,0:T(8,128)(2,1)S(1)} custom-call(s32[513]{0:T(1024)S(1)} %add_reduce_fusion.list_ref, bf16[256,128,128]{2,1,0:T(8,128)(2,1)} %bitcast.3), custom_call_target="tpu_custom_call" | custom-call | flops 4194304 | bytes 6291456 | tf_op jit(solution)/shard_map/build_first/pallas_call | solution.py:179
  12.1 0.0 copy-start
  12.1 0.3 collective-permute-done.4.refs_6_
  12.4 1.7 %collective-permute-done.1.refs_2_ = bf16[256,256]{1,0:T(8,128)(2,1)S(1)} collective-permute-done((bf16[256,256]{1,0:T(8,128)(2,1)S(1)}, bf16[256,256]{1,0:T(8,128)(2,1)S(1)}, u32[]{:S(2)}, u32[]{:S(2)}) %collective-permute-start.1) | collective-permute-done | bytes 131104 | tf_op jit(solution)/shard_map/ppermute | solution.py:461
  14.1 0.9 %collective-permute-start.2 = (bf16[256,256]{1,0:T(8,128)(2,1)S(1)}, bf16[256,256]{1,0:T(8,128)(2,1)S(1)}, u32[]{:S(2)}, u32[]{:S(2)}) collective-permute-start(bf16[256,256]{1,0:T(8,128)(2,1)S(1)} %collective-permute-done.1.refs_2_), channel_id=1, source_target_pairs={{0,8},{8,16},{16,24},{24,28},{28,20},{20,12},{12,4},{4,0},{1,9},{9... | collective-permute-start | bytes 393224 | tf_op jit(solution)/shard_map/ppermute | solution.py:461
  15.0 0.0 copy-done.2
  15.0 1.1 %collective-permute-start.5 = (bf16[256,256]{1,0:T(8,128)(2,1)S(1)}, bf16[256,256]{1,0:T(8,128)(2,1)S(1)}, u32[]{:S(2)}, u32[]{:S(2)}) collective-permute-start(bf16[256,256]{1,0:T(8,128)(2,1)S(1)} %copy-done.2), channel_id=1, source_target_pairs={{0,2},{1,3},{2,0},{3,1},{4,6},{5,7},{6,4},{7,5},{8,10},{9,11},{10,... | collective-permute-start | bytes 393224 | tf_op jit(solution)/shard_map/ppermute | solution.py:465
  16.1 1.5 %collective-permute-start.7 = (bf16[256,256]{1,0:T(8,128)(2,1)S(1)}, bf16[256,256]{1,0:T(8,128)(2,1)S(1)}, u32[]{:S(2)}, u32[]{:S(2)}) collective-permute-start(bf16[256,256]{1,0:T(8,128)(2,1)S(1)} %collective-permute-done.4.refs_6_), channel_id=1, source_target_pairs={{0,4},{8,0},{16,8},{24,16},{28,24},{20,28},{12,20},{4,12},{1,5},{9... | collective-permute-start | bytes 393224 | tf_op jit(solution)/shard_map/ppermute | solution.py:461
  17.6 2.1 %collective-permute-done.2.refs_3_ = bf16[256,256]{1,0:T(8,128)(2,1)S(1)} collective-permute-done((bf16[256,256]{1,0:T(8,128)(2,1)S(1)}, bf16[256,256]{1,0:T(8,128)(2,1)S(1)}, u32[]{:S(2)}, u32[]{:S(2)}) %collective-permute-start.2) | collective-permute-done | bytes 131104 | tf_op jit(solution)/shard_map/ppermute | solution.py:461
  19.7 0.2 collective-permute-done.5.refs_4_
  19.9 1.2 %collective-permute-start.6 = (bf16[256,256]{1,0:T(8,128)(2,1)S(1)}, bf16[256,256]{1,0:T(8,128)(2,1)S(1)}, u32[]{:S(2)}, u32[]{:S(2)}) collective-permute-start(bf16[256,256]{1,0:T(8,128)(2,1)S(1)} %collective-permute-done.2.refs_3_), channel_id=1, source_target_pairs={{0,8},{8,16},{16,24},{24,28},{28,20},{20,12},{12,4},{4,0},{1,9},{9... | collective-permute-start | bytes 393224 | tf_op jit(solution)/shard_map/ppermute | solution.py:461
  21.1 2.4 %build_rest.1.dense_ref = bf16[1024,2048]{1,0:T(8,128)(2,1)S(1)} custom-call(s32[513]{0:T(1024)S(1)} %add_reduce_fusion.list_ref, bf16[256,128,128]{2,1,0:T(8,128)(2,1)} %bitcast.4, bf16[1024,2048]{1,0:T(8,128)(2,1)S(1)} %build_first.1.half_ref), custom_call_target="tpu_custom_call" | custom-call | flops 4194304 | bytes 6291456 | tf_op jit(solution)/shard_map/build_rest/pallas_call | solution.py:189
  23.5 0.0 collective-permute-done.7.refs_7_
  23.5 1.4 %collective-permute-done.6.refs_4_ = bf16[256,256]{1,0:T(8,128)(2,1)S(1)} collective-permute-done((bf16[256,256]{1,0:T(8,128)(2,1)S(1)}, bf16[256,256]{1,0:T(8,128)(2,1)S(1)}, u32[]{:S(2)}, u32[]{:S(2)}) %collective-permute-start.6) | collective-permute-done | bytes 131104 | tf_op jit(solution)/shard_map/ppermute | solution.py:461
  24.9 0.0 copy-done
  24.9 0.7 %forward_product.2 = bf16[512,256]{1,0:T(8,128)(2,1)S(1)} custom-call(bf16[1024,2048]{1,0:T(8,128)(2,1)S(1)} %build_rest.1.dense_ref, bf16[256,256]{1,0:T(8,128)(2,1)S(1)} %copy-done, bf16[256,256]{1,0:T(8,128)(2,1)S(1)} %collective-permute-done.refs_1_, bf16[256,256]{1,0:T(8,128)(2,1)S(1)} %collective-permute-done.1.refs_2_, ...), custom_call_target="tpu_custom_call" | custom-call | flops 536870912 | bytes 3407872 | tf_op jit(solution)/shard_map/forward_product/pallas_call | solution.py:241
  25.6 0.0 copy-start.1
  25.6 0.1 collective-permute-start.8
  25.7 0.7 %forward_product.3 = bf16[512,256]{1,0:T(8,128)(2,1)S(1)} custom-call(bf16[1024,2048]{1,0:T(8,128)(2,1)S(1)} %build_rest.1.dense_ref, bf16[256,256]{1,0:T(8,128)(2,1)S(1)} %copy-done, bf16[256,256]{1,0:T(8,128)(2,1)S(1)} %collective-permute-done.refs_1_, bf16[256,256]{1,0:T(8,128)(2,1)S(1)} %collective-permute-done.1.refs_2_, ...), custom_call_target="tpu_custom_call" | custom-call | flops 536870912 | bytes 3407872 | tf_op jit(solution)/shard_map/forward_product/pallas_call | solution.py:241
  26.4 0.8 %collective-permute-done.8 = bf16[512,256]{1,0:T(8,128)(2,1)S(1)} collective-permute-done((bf16[512,256]{1,0:T(8,128)(2,1)S(1)}, bf16[512,256]{1,0:T(8,128)(2,1)S(1)}, u32[]{:S(2)}, u32[]{:S(2)}) %collective-permute-start.8) | collective-permute-done | bytes 262176 | tf_op jit(solution)/shard_map/ppermute | solution.py:465
  27.2 0.1 add_convert_fusion.refs_0_
  27.3 2.5 %collective-permute-start.9 = (bf16[512,256]{1,0:T(8,128)(2,1)S(1)}, bf16[512,256]{1,0:T(8,128)(2,1)S(1)}, u32[]{:S(2)}, u32[]{:S(2)}) collective-permute-start(bf16[512,256]{1,0:T(8,128)(2,1)S(1)} %add_convert_fusion.refs_0_), channel_id=1, source_target_pairs={{0,2},{1,3},{2,0},{3,1},{4,6},{5,7},{6,4},{7,5},{8,10},{9,11},{10,... | collective-permute-start | bytes 786440 | tf_op jit(solution)/shard_map/ppermute | solution.py:465
  29.8 6.6 %collective-permute-done.9.refs_1_ = bf16[512,256]{1,0:T(8,128)(2,1)S(1)} collective-permute-done((bf16[512,256]{1,0:T(8,128)(2,1)S(1)}, bf16[512,256]{1,0:T(8,128)(2,1)S(1)}, u32[]{:S(2)}, u32[]{:S(2)}) %collective-permute-start.9) | collective-permute-done | bytes 262176 | tf_op jit(solution)/shard_map/ppermute | solution.py:465
  36.4 0.0 copy-done.1
  36.4 1.0 %middle.1 = (bf16[256,256]{1,0:T(8,128)(2,1)}, bf16[768,256]{1,0:T(8,128)(2,1)S(1)}, f32[128,256]{1,0:T(8,128)S(1)}) custom-call(bf16[512,256]{1,0:T(8,128)(2,1)S(1)} %add_convert_fusion.refs_0_, bf16[512,256]{1,0:T(8,128)(2,1)S(1)} %collective-permute-done.9.refs_1_, bf16[256,256]{1,0:T(8,128)(2,1)S(1)} %copy-done.1, bf16[256,256]{1,0:T(8,128)(2,1)S(1)} %copy-done.2, ...), custom_call_target="tpu_custom_call" | custom-call | flops 335544320 | bytes 1572864 | tf_op jit(solution)/shard_map/middle/pallas_call | solution.py:305
  37.5 0.1 collective-permute-start.10
  37.5 1.7 %collective-permute-done.10.sibling_ref = bf16[768,256]{1,0:T(8,128)(2,1)S(1)} collective-permute-done((bf16[768,256]{1,0:T(8,128)(2,1)S(1)}, bf16[768,256]{1,0:T(8,128)(2,1)S(1)}, u32[]{:S(2)}, u32[]{:S(2)}) %collective-permute-start.10) | collective-permute-done | bytes 393248 | tf_op jit(solution)/shard_map/ppermute | solution.py:465
  39.3 0.6 backward_product.2
  39.9 1.9 %collective-permute-start.11 = (bf16[384,256]{1,0:T(8,128)(2,1)S(1)}, bf16[384,256]{1,0:T(8,128)(2,1)S(1)}, u32[]{:S(2)}, u32[]{:S(2)}) collective-permute-start(bf16[384,256]{1,0:T(8,128)(2,1)S(1)} %get-tuple-element.54), channel_id=1, source_target_pairs={{0,8},{8,16},{16,24},{24,28},{28,20},{20,12},{12,4},{4,0},{1,9},{9... | collective-permute-start | bytes 589832 | tf_op jit(solution)/shard_map/ppermute | solution.py:461
  41.7 0.2 collective-permute-start.15
  41.9 1.1 %backward_product.3 = (bf16[384,256]{1,0:T(8,128)(2,1)S(1)}, bf16[384,256]{1,0:T(8,128)(2,1)S(1)}, bf16[384,256]{1,0:T(8,128)(2,1)S(1)}, bf16[384,256]{1,0:T(8,1...) custom-call(bf16[1024,2048]{1,0:T(8,128)(2,1)S(1)} %build_rest.1.dense_ref, ...), custom_call_target="tpu_custom_call" | custom-call | flops 134217728 | bytes 786432 | tf_op jit(solution)/shard_map/backward_product/pallas_call | solution.py:367
  43.1 3.8 %collective-permute-done.11.refs_1_ = bf16[384,256]{1,0:T(8,128)(2,1)S(1)} collective-permute-done((bf16[384,256]{1,0:T(8,128)(2,1)S(1)}, bf16[384,256]{1,0:T(8,128)(2,1)S(1)}, u32[]{:S(2)}, u32[]{:S(2)}) %collective-permute-start.11) | collective-permute-done | bytes 196640 | tf_op jit(solution)/shard_map/ppermute | solution.py:461
  46.9 1.9 %collective-permute-start.12 = (bf16[384,256]{1,0:T(8,128)(2,1)S(1)}, bf16[384,256]{1,0:T(8,128)(2,1)S(1)}, u32[]{:S(2)}, u32[]{:S(2)}) collective-permute-start(bf16[384,256]{1,0:T(8,128)(2,1)S(1)} %add_convert_fusion.5), channel_id=1, source_target_pairs={{0,8},{8,16},{16,24},{24,28},{28,20},{20,12},{12,4},{4,0},{1,9},{9... | collective-permute-start | bytes 589832 | tf_op jit(solution)/shard_map/ppermute | solution.py:461
  48.8 0.0 collective-permute-done.15.refs_2_
  48.8 0.3 collective-permute-start.16
  49.1 4.0 %collective-permute-done.12.refs_3_ = bf16[384,256]{1,0:T(8,128)(2,1)S(1)} collective-permute-done((bf16[384,256]{1,0:T(8,128)(2,1)S(1)}, bf16[384,256]{1,0:T(8,128)(2,1)S(1)}, u32[]{:S(2)}, u32[]{:S(2)}) %collective-permute-start.12) | collective-permute-done | bytes 196640 | tf_op jit(solution)/shard_map/ppermute | solution.py:461
  53.1 1.9 %collective-permute-start.13 = (bf16[384,256]{1,0:T(8,128)(2,1)S(1)}, bf16[384,256]{1,0:T(8,128)(2,1)S(1)}, u32[]{:S(2)}, u32[]{:S(2)}) collective-permute-start(bf16[384,256]{1,0:T(8,128)(2,1)S(1)} %add_convert_fusion.4), channel_id=1, source_target_pairs={{0,8},{8,16},{16,24},{24,28},{28,20},{20,12},{12,4},{4,0},{1,9},{9... | collective-permute-start | bytes 589832 | tf_op jit(solution)/shard_map/ppermute | solution.py:461
  55.0 0.0 collective-permute-done.16.refs_4_
  55.1 0.3 collective-permute-start.17
  55.3 3.5 %collective-permute-done.13.refs_5_ = bf16[384,256]{1,0:T(8,128)(2,1)S(1)} collective-permute-done((bf16[384,256]{1,0:T(8,128)(2,1)S(1)}, bf16[384,256]{1,0:T(8,128)(2,1)S(1)}, u32[]{:S(2)}, u32[]{:S(2)}) %collective-permute-start.13) | collective-permute-done | bytes 196640 | tf_op jit(solution)/shard_map/ppermute | solution.py:461
  58.9 1.9 %collective-permute-start.14 = (bf16[384,256]{1,0:T(8,128)(2,1)S(1)}, bf16[384,256]{1,0:T(8,128)(2,1)S(1)}, u32[]{:S(2)}, u32[]{:S(2)}) collective-permute-start(bf16[384,256]{1,0:T(8,128)(2,1)S(1)} %add_convert_fusion.3), channel_id=1, source_target_pairs={{0,8},{8,16},{16,24},{24,28},{28,20},{20,12},{12,4},{4,0},{1,9},{9... | collective-permute-start | bytes 589832 | tf_op jit(solution)/shard_map/ppermute | solution.py:461
  60.8 0.0 collective-permute-done.17.refs_2_.refs_6_
  60.8 3.9 %collective-permute-done.14.refs_1_.refs_7_ = bf16[384,256]{1,0:T(8,128)(2,1)S(1)} collective-permute-done((bf16[384,256]{1,0:T(8,128)(2,1)S(1)}, bf16[384,256]{1,0:T(8,128)(2,1)S(1)}, u32[]{:S(2)}, u32[]{:S(2)}) %collective-permute-start.14) | collective-permute-done | bytes 196640 | tf_op jit(solution)/shard_map/ppermute | solution.py:461
  64.6 0.1 summed_terms.1.own_ref
  64.8 0.1 collective-permute-start.18
  64.8 0.8 %finish.1 = bf16[256,256]{1,0:T(8,128)(2,1)} custom-call(bf16[256,256]{1,0:T(8,128)(2,1)S(1)} %get-tuple-element.50.refs_0_, bf16[384,256]{1,0:T(8,128)(2,1)S(1)} %collective-permute-done.14.refs_1_.refs_7_, bf16[384,256]{1,0:T(8,128)(2,1)S(1)} %collective-permute-done.17.refs_2_.refs_6_), custom_call_target="tpu_custom_call" | custom-call | flops 196608 | bytes 524288 | tf_op jit(solution)/shard_map/finish/pallas_call | solution.py:425
  65.6 0.6 collective-permute-done.18.sibling_ref
  66.2 0.7 %joined.1 = f32[256,256]{1,0:T(8,128)} custom-call(f32[128,256]{1,0:T(8,128)S(1)} %summed_terms.1.own_ref, f32[128,256]{1,0:T(8,128)S(1)} %collective-permute-done.18.sibling_ref), custom_call_target="tpu_custom_call" | custom-call | bytes 524288 | tf_op jit(solution)/shard_map/joined/pallas_call | solution.py:447
  (5 shorter events, 0.2 us)
Async XLA Ops:
  0.6 6.8 %collective-permute-start.3 = (bf16[256,256]{1,0:T(8,128)(2,1)}, bf16[256,256]{1,0:T(8,128)(2,1)S(1)}, u32[]{:S(2)}, u32[]{:S(2)}) collective-permute-start(bf16[256,256]{1,0:T(8,128)(2,1)} %refs_0_.3), channel_id=1, source_target_pairs={{0,4},{8,0},{16,8},{24,16},{28,24},{20,28},{12,20},{4,12},{1,5},{9... | collective-permute-start | bytes 393224 | tf_op jit(solution)/shard_map/ppermute | solution.py:461
  3.6 5.5 %collective-permute-start = (bf16[256,256]{1,0:T(8,128)(2,1)}, bf16[256,256]{1,0:T(8,128)(2,1)S(1)}, u32[]{:S(2)}, u32[]{:S(2)}) collective-permute-start(bf16[256,256]{1,0:T(8,128)(2,1)} %refs_0_.3), channel_id=1, source_target_pairs={{0,8},{8,16},{16,24},{24,28},{28,20},{20,12},{12,4},{4,0},{1,9},{9... | collective-permute-start | bytes 393224 | tf_op jit(solution)/shard_map/ppermute | solution.py:461
  7.4 5.0 %collective-permute-start.4 = (bf16[256,256]{1,0:T(8,128)(2,1)S(1)}, bf16[256,256]{1,0:T(8,128)(2,1)S(1)}, u32[]{:S(2)}, u32[]{:S(2)}) collective-permute-start(bf16[256,256]{1,0:T(8,128)(2,1)S(1)} %collective-permute-done.3.refs_5_), channel_id=1, source_target_pairs={{0,4},{8,0},{16,8},{24,16},{28,24},{20,28},{12,20},{4,12},{1,5},{9... | collective-permute-start | bytes 393224 | tf_op jit(solution)/shard_map/ppermute | solution.py:461
  9.1 5.0 %collective-permute-start.1 = (bf16[256,256]{1,0:T(8,128)(2,1)S(1)}, bf16[256,256]{1,0:T(8,128)(2,1)S(1)}, u32[]{:S(2)}, u32[]{:S(2)}) collective-permute-start(bf16[256,256]{1,0:T(8,128)(2,1)S(1)} %collective-permute-done.refs_1_), channel_id=1, source_target_pairs={{0,8},{8,16},{16,24},{24,28},{28,20},{20,12},{12,4},{4,0},{1,9},{9... | collective-permute-start | bytes 393224 | tf_op jit(solution)/shard_map/ppermute | solution.py:461
  9.4 5.5 %copy-start.2 = (bf16[256,256]{1,0:T(8,128)(2,1)S(1)}, bf16[256,256]{1,0:T(8,128)(2,1)}, u32[]{:S(2)}) copy-start(bf16[256,256]{1,0:T(8,128)(2,1)} %refs_3_) | copy-start | bytes 393220
  12.1 12.8 %copy-start = (bf16[256,256]{1,0:T(8,128)(2,1)S(1)}, bf16[256,256]{1,0:T(8,128)(2,1)}, u32[]{:S(2)}) copy-start(bf16[256,256]{1,0:T(8,128)(2,1)} %refs_0_.3) | copy-start | bytes 393220
  14.1 5.6 %collective-permute-start.2 = (bf16[256,256]{1,0:T(8,128)(2,1)S(1)}, bf16[256,256]{1,0:T(8,128)(2,1)S(1)}, u32[]{:S(2)}, u32[]{:S(2)}) collective-permute-start(bf16[256,256]{1,0:T(8,128)(2,1)S(1)} %collective-permute-done.1.refs_2_), channel_id=1, source_target_pairs={{0,8},{8,16},{16,24},{24,28},{28,20},{20,12},{12,4},{4,0},{1,9},{9... | collective-permute-start | bytes 393224 | tf_op jit(solution)/shard_map/ppermute | solution.py:461
  15.0 5.0 %collective-permute-start.5 = (bf16[256,256]{1,0:T(8,128)(2,1)S(1)}, bf16[256,256]{1,0:T(8,128)(2,1)S(1)}, u32[]{:S(2)}, u32[]{:S(2)}) collective-permute-start(bf16[256,256]{1,0:T(8,128)(2,1)S(1)} %copy-done.2), channel_id=1, source_target_pairs={{0,2},{1,3},{2,0},{3,1},{4,6},{5,7},{6,4},{7,5},{8,10},{9,11},{10,... | collective-permute-start | bytes 393224 | tf_op jit(solution)/shard_map/ppermute | solution.py:465
  16.1 7.5 %collective-permute-start.7 = (bf16[256,256]{1,0:T(8,128)(2,1)S(1)}, bf16[256,256]{1,0:T(8,128)(2,1)S(1)}, u32[]{:S(2)}, u32[]{:S(2)}) collective-permute-start(bf16[256,256]{1,0:T(8,128)(2,1)S(1)} %collective-permute-done.4.refs_6_), channel_id=1, source_target_pairs={{0,4},{8,0},{16,8},{24,16},{28,24},{20,28},{12,20},{4,12},{1,5},{9... | collective-permute-start | bytes 393224 | tf_op jit(solution)/shard_map/ppermute | solution.py:461
  19.9 5.0 %collective-permute-start.6 = (bf16[256,256]{1,0:T(8,128)(2,1)S(1)}, bf16[256,256]{1,0:T(8,128)(2,1)S(1)}, u32[]{:S(2)}, u32[]{:S(2)}) collective-permute-start(bf16[256,256]{1,0:T(8,128)(2,1)S(1)} %collective-permute-done.2.refs_3_), channel_id=1, source_target_pairs={{0,8},{8,16},{16,24},{24,28},{28,20},{20,12},{12,4},{4,0},{1,9},{9... | collective-permute-start | bytes 393224 | tf_op jit(solution)/shard_map/ppermute | solution.py:461
  25.6 10.8 %copy-start.1 = (bf16[256,256]{1,0:T(8,128)(2,1)S(1)}, bf16[256,256]{1,0:T(8,128)(2,1)}, u32[]{:S(2)}) copy-start(bf16[256,256]{1,0:T(8,128)(2,1)} %refs_2_.1) | copy-start | bytes 393220
  25.6 1.6 %collective-permute-start.8 = (bf16[512,256]{1,0:T(8,128)(2,1)S(1)}, bf16[512,256]{1,0:T(8,128)(2,1)S(1)}, u32[]{:S(2)}, u32[]{:S(2)}) collective-permute-start(bf16[512,256]{1,0:T(8,128)(2,1)S(1)} %forward_product.2), channel_id=1, source_target_pairs={{0,1},{1,0},{2,3},{3,2},{4,5},{5,4},{6,7},{7,6},{8,9},{9,8},{10,11... | collective-permute-start | bytes 786440 | tf_op jit(solution)/shard_map/ppermute | solution.py:465
  27.3 9.1 %collective-permute-start.9 = (bf16[512,256]{1,0:T(8,128)(2,1)S(1)}, bf16[512,256]{1,0:T(8,128)(2,1)S(1)}, u32[]{:S(2)}, u32[]{:S(2)}) collective-permute-start(bf16[512,256]{1,0:T(8,128)(2,1)S(1)} %add_convert_fusion.refs_0_), channel_id=1, source_target_pairs={{0,2},{1,3},{2,0},{3,1},{4,6},{5,7},{6,4},{7,5},{8,10},{9,11},{10,... | collective-permute-start | bytes 786440 | tf_op jit(solution)/shard_map/ppermute | solution.py:465
  37.5 1.8 %collective-permute-start.10 = (bf16[768,256]{1,0:T(8,128)(2,1)S(1)}, bf16[768,256]{1,0:T(8,128)(2,1)S(1)}, u32[]{:S(2)}, u32[]{:S(2)}) collective-permute-start(bf16[768,256]{1,0:T(8,128)(2,1)S(1)} %get-tuple-element.44.own_ref), channel_id=1, source_target_pairs={{0,1},{1,0},{2,3},{3,2},{4,5},{5,4},{6,7},{7,6},{8,9},{9,8},{10,11... | collective-permute-start | bytes 1179656 | tf_op jit(solution)/shard_map/ppermute | solution.py:465
  39.9 7.0 %collective-permute-start.11 = (bf16[384,256]{1,0:T(8,128)(2,1)S(1)}, bf16[384,256]{1,0:T(8,128)(2,1)S(1)}, u32[]{:S(2)}, u32[]{:S(2)}) collective-permute-start(bf16[384,256]{1,0:T(8,128)(2,1)S(1)} %get-tuple-element.54), channel_id=1, source_target_pairs={{0,8},{8,16},{16,24},{24,28},{28,20},{20,12},{12,4},{4,0},{1,9},{9... | collective-permute-start | bytes 589832 | tf_op jit(solution)/shard_map/ppermute | solution.py:461
  41.7 7.0 %collective-permute-start.15 = (bf16[384,256]{1,0:T(8,128)(2,1)S(1)}, bf16[384,256]{1,0:T(8,128)(2,1)S(1)}, u32[]{:S(2)}, u32[]{:S(2)}) collective-permute-start(bf16[384,256]{1,0:T(8,128)(2,1)S(1)} %get-tuple-element.57), channel_id=1, source_target_pairs={{0,4},{8,0},{16,8},{24,16},{28,24},{20,28},{12,20},{4,12},{1,5},{9... | collective-permute-start | bytes 589832 | tf_op jit(solution)/shard_map/ppermute | solution.py:461
  46.9 6.2 %collective-permute-start.12 = (bf16[384,256]{1,0:T(8,128)(2,1)S(1)}, bf16[384,256]{1,0:T(8,128)(2,1)S(1)}, u32[]{:S(2)}, u32[]{:S(2)}) collective-permute-start(bf16[384,256]{1,0:T(8,128)(2,1)S(1)} %add_convert_fusion.5), channel_id=1, source_target_pairs={{0,8},{8,16},{16,24},{24,28},{28,20},{20,12},{12,4},{4,0},{1,9},{9... | collective-permute-start | bytes 589832 | tf_op jit(solution)/shard_map/ppermute | solution.py:461
  48.8 6.2 %collective-permute-start.16 = (bf16[384,256]{1,0:T(8,128)(2,1)S(1)}, bf16[384,256]{1,0:T(8,128)(2,1)S(1)}, u32[]{:S(2)}, u32[]{:S(2)}) collective-permute-start(bf16[384,256]{1,0:T(8,128)(2,1)S(1)} %add_convert_fusion.2), channel_id=1, source_target_pairs={{0,4},{8,0},{16,8},{24,16},{28,24},{20,28},{12,20},{4,12},{1,5},{9... | collective-permute-start | bytes 589832 | tf_op jit(solution)/shard_map/ppermute | solution.py:461
  53.1 5.7 %collective-permute-start.13 = (bf16[384,256]{1,0:T(8,128)(2,1)S(1)}, bf16[384,256]{1,0:T(8,128)(2,1)S(1)}, u32[]{:S(2)}, u32[]{:S(2)}) collective-permute-start(bf16[384,256]{1,0:T(8,128)(2,1)S(1)} %add_convert_fusion.4), channel_id=1, source_target_pairs={{0,8},{8,16},{16,24},{24,28},{28,20},{20,12},{12,4},{4,0},{1,9},{9... | collective-permute-start | bytes 589832 | tf_op jit(solution)/shard_map/ppermute | solution.py:461
  55.1 5.7 %collective-permute-start.17 = (bf16[384,256]{1,0:T(8,128)(2,1)S(1)}, bf16[384,256]{1,0:T(8,128)(2,1)S(1)}, u32[]{:S(2)}, u32[]{:S(2)}) collective-permute-start(bf16[384,256]{1,0:T(8,128)(2,1)S(1)} %add_convert_fusion.1), channel_id=1, source_target_pairs={{0,4},{8,0},{16,8},{24,16},{28,24},{20,28},{12,20},{4,12},{1,5},{9... | collective-permute-start | bytes 589832 | tf_op jit(solution)/shard_map/ppermute | solution.py:461
  58.9 5.7 %collective-permute-start.14 = (bf16[384,256]{1,0:T(8,128)(2,1)S(1)}, bf16[384,256]{1,0:T(8,128)(2,1)S(1)}, u32[]{:S(2)}, u32[]{:S(2)}) collective-permute-start(bf16[384,256]{1,0:T(8,128)(2,1)S(1)} %add_convert_fusion.3), channel_id=1, source_target_pairs={{0,8},{8,16},{16,24},{24,28},{28,20},{20,12},{12,4},{4,0},{1,9},{9... | collective-permute-start | bytes 589832 | tf_op jit(solution)/shard_map/ppermute | solution.py:461
  64.8 1.4 %collective-permute-start.18 = (f32[128,256]{1,0:T(8,128)S(1)}, f32[128,256]{1,0:T(8,128)S(1)}, u32[]{:S(2)}, u32[]{:S(2)}) collective-permute-start(f32[128,256]{1,0:T(8,128)S(1)} %summed_terms.1.own_ref), channel_id=1, source_target_pairs={{0,1},{1,0},{2,3},{3,2},{4,5},{5,4},{6,7},{7,6},{8,9},{9,8},{10,11... | collective-permute-start | bytes 393224 | tf_op jit(solution)/shard_map/ppermute | solution.py:465

commit v12 on v11

--- a/solution.py
+++ b/solution.py
@@ -199,12 +199,22 @@
     ]
 
 
-def ring_place(row, count):
-    return jnp.where(lax.rem(row, 2) == 0, row // 2, count - 1 - row // 2)
+def ring_order(count, core):
+    order = list(range(0, count, 2)) + list(range(count - 1, 0, -2))
+    return order if core == 0 else order[:1] + order[:0:-1]
+
+
+def turned(place, count):
+    return jnp.where(lax.axis_index("col") & 1 == 1, lax.rem(count - place, count), place)
+
+
+def ring_place(count):
+    row = lax.axis_index("row")
+    return turned(jnp.where(lax.rem(row, 2) == 0, row // 2, count - 1 - row // 2), count)
 
 
 def ring_row(place, count):
-    place = lax.rem(place + 2 * count, count)
+    place = turned(lax.rem(place + 2 * count, count), count)
     return jnp.where(place < count // 2, 2 * place, 2 * (count - 1 - place) + 1)
 
 
@@ -213,7 +223,7 @@
     count = lax.axis_size("col")
     rows = dense_ref.shape[0] // count
     block = dense_ref.shape[1] // row_count
-    place = ring_place(lax.axis_index("row"), row_count)
+    place = ring_place(row_count)
     col = lax.axis_index("col") ^ sibling
     operands = []
     for piece, ref in zip(pieces, piece_refs):
@@ -342,7 +352,7 @@
     terms = (chunk_ref[...] + (high + low)).astype(jnp.bfloat16)
     for copy in copies:
         copy.wait()
-    place = ring_place(lax.axis_index("row"), row_count)
+    place = ring_place(row_count)
     for (offset, tail), out_ref in zip(outputs, out_refs):
         if tail != "terms alone":
             along = pl.ds(pl.multiple_of(ring_row(place + offset, row_count) * wide, wide), wide)
@@ -381,7 +391,7 @@
 def terms_kernel(*refs, offsets, first_rows):
     term_refs, out_ref, places = refs[:-2], refs[-2], refs[-1]
     row_count, size, _ = places.shape
-    place = ring_place(lax.axis_index("row"), row_count)
+    place = ring_place(row_count)
     for offset, first, ref in zip(offsets, first_rows, term_refs):
         places[ring_row(place + offset, row_count)] = ref[pl.ds(first, size), :].astype(jnp.float32)
     total = places[0]
@@ -456,9 +466,13 @@
 
 
 def around(value, step):
-    count = lax.axis_size("row")
-    order = list(range(0, count, 2)) + list(range(count - 1, 0, -2))
-    return lax.ppermute(value, "row", [(order[i], order[(i + step) % count]) for i in range(count)])
+    row_count, col_count = lax.axis_size("row"), lax.axis_size("col")
+    pairs = []
+    for col in range(col_count):
+        order = ring_order(row_count, col % 2)
+        for place, row in enumerate(order):
+            pairs.append((row * col_count + col, order[(place + step) % row_count] * col_count + col))
+    return lax.ppermute(value, ("row", "col"), pairs)
 
 
 def swapped(value, axis, partner):

time: 67.1 us -> 68.7 us (1.024)
  waiting for transfers between devices: 32.8 us -> 37.1 us
  starting transfers between devices: 20.8 us -> 17.7 us
    ppermute x14, waiting for transfers between devices: 22.9 us -> 26.9 us  [around(): return lax.ppermute(value, ('row', 'col'), pairs)]
    ppermute x14, starting transfers between devices: 17 us -> 14.5 us  [around(): return lax.ppermute(value, ('row', 'col'), pairs)]
  transfers between devices with their start and end apart: 19 -> 19, of which waited for: 14 -> 16; matrix products, arithmetic and copies ran while one was open for 1% -> 1% of each run, Pallas kernels for 11% -> 12%
where the time goes in v12:
time: 68.7 us
  waiting for transfers between devices  37.1 us (54%)
  starting transfers between devices  17.7 us (26%)
  Pallas kernels  11.4 us (17%)
  between operations  1.43 us (2%)
  other arithmetic  1.01 us (1%)
    ppermute x14, waiting for transfers between devices, around(): return lax.ppermute(value, ('row', 'col'), pairs)  26.9 us
    ppermute x14, starting transfers between devices, around(): return lax.ppermute(value, ('row', 'col'), pairs)  14.5 us
    ppermute x5, waiting for transfers between devices, swapped(): lax.ppermute(value, axis, [(i, i ^ partner) for i in range(lax.axis_size(...  10.2 us
    ppermute x5, starting transfers between devices, swapped(): lax.ppermute(value, axis, [(i, i ^ partner) for i in range(lax.axis_size(...  3.26 us
    pallas_call x1, Pallas kernels, build_stages(): pl.pallas_call(functools.partial(build_rest_kernel, blocks=blocks), out_s...  2.9 us
    pallas_call x1, Pallas kernels, build_stages(): pl.pallas_call(functools.partial(build_first_kernel, blocks=blocks), out_...  2.65 us
    pallas_call x2, Pallas kernels, backward_product(): pl.pallas_call(functools.partial(backward_kernel, outputs=outputs, row_co...  1.76 us
    pallas_call x2, Pallas kernels, forward_product(): pl.pallas_call(functools.partial(forward_kernel, pieces=pieces, sibling=s...  1.44 us
  transfers between devices with their start and end apart: 19, of which 16 were waited for; matrix products, arithmetic and copies ran while one was open for 1% of the time, Pallas kernels for 12%

profile of v12, /device:TPU:0, one launch (start us, length us, event | category | flops | bytes accessed | tf_op | source)
XLA Modules:
  0.0 68.7 jit_solution(7961252932913036190)
XLA Ops:
  0.6 3.0 %collective-permute-start.3 = (bf16[256,256]{1,0:T(8,128)(2,1)}, bf16[256,256]{1,0:T(8,128)(2,1)S(1)}, u32[]{:S(2)}, u32[]{:S(2)}) collective-permute-start(bf16[256,256]{1,0:T(8,128)(2,1)} %refs_0_.3), channel_id=1, source_target_pairs={{0,4},{8,0},{16,8},{24,16},{28,24},{20,28},{12,20},{4,12},{1,9},{5... | collective-permute-start | bytes 393224 | tf_op jit(solution)/shard_map/ppermute | solution.py:475
  3.6 0.1 collective-permute-start
  4.4 0.7 %add_reduce_fusion.list_ref = s32[513]{0:T(1024)S(1)} fusion(s32[1,1,1]{2,1,0:T(1,128)} %bitcast.2, s32[1,1,256]{2,1,0:T(1,128)} %param.11, s32[1,1,256]{2,1,0:T(1,128)} %param.10), kind=kLoop, calls=%fused_computation.6 | loop fusion | flops 1026 | bytes 4104 | tf_op jit(solution)/shard_map/concatenate | solution.py:541
  5.1 2.6 %collective-permute-done.3.refs_5_ = bf16[256,256]{1,0:T(8,128)(2,1)S(1)} collective-permute-done((bf16[256,256]{1,0:T(8,128)(2,1)}, bf16[256,256]{1,0:T(8,128)(2,1)S(1)}, u32[]{:S(2)}, u32[]{:S(2)}) %collective-permute-start.3) | collective-permute-done | bytes 131104 | tf_op jit(solution)/shard_map/ppermute | solution.py:475
  7.7 1.5 %collective-permute-start.4 = (bf16[256,256]{1,0:T(8,128)(2,1)S(1)}, bf16[256,256]{1,0:T(8,128)(2,1)S(1)}, u32[]{:S(2)}, u32[]{:S(2)}) collective-permute-start(bf16[256,256]{1,0:T(8,128)(2,1)S(1)} %collective-permute-done.3.refs_5_), channel_id=1, source_target_pairs={{0,4},{8,0},{16,8},{24,16},{28,24},{20,28},{12,20},{4,12},{1,9},{5... | collective-permute-start | bytes 393224 | tf_op jit(solution)/shard_map/ppermute | solution.py:475
  9.2 0.0 collective-permute-done.refs_1_
  9.2 0.9 %collective-permute-start.1 = (bf16[256,256]{1,0:T(8,128)(2,1)S(1)}, bf16[256,256]{1,0:T(8,128)(2,1)S(1)}, u32[]{:S(2)}, u32[]{:S(2)}) collective-permute-start(bf16[256,256]{1,0:T(8,128)(2,1)S(1)} %collective-permute-done.refs_1_), channel_id=1, source_target_pairs={{0,8},{8,16},{16,24},{24,28},{28,20},{20,12},{12,4},{4,0},{1,5},{5... | collective-permute-start | bytes 393224 | tf_op jit(solution)/shard_map/ppermute | solution.py:475
  10.1 0.0 copy-start.2
  10.1 2.7 %build_first.1.half_ref = bf16[1024,2048]{1,0:T(8,128)(2,1)S(1)} custom-call(s32[513]{0:T(1024)S(1)} %add_reduce_fusion.list_ref, bf16[256,128,128]{2,1,0:T(8,128)(2,1)} %bitcast.3), custom_call_target="tpu_custom_call" | custom-call | flops 4194304 | bytes 6291456 | tf_op jit(solution)/shard_map/build_first/pallas_call | solution.py:179
  12.8 0.0 copy-start
  12.8 1.1 %collective-permute-done.4.refs_6_ = bf16[256,256]{1,0:T(8,128)(2,1)S(1)} collective-permute-done((bf16[256,256]{1,0:T(8,128)(2,1)S(1)}, bf16[256,256]{1,0:T(8,128)(2,1)S(1)}, u32[]{:S(2)}, u32[]{:S(2)}) %collective-permute-start.4) | collective-permute-done | bytes 131104 | tf_op jit(solution)/shard_map/ppermute | solution.py:475
  13.9 0.3 collective-permute-done.1.refs_2_
  14.2 1.5 %collective-permute-start.2 = (bf16[256,256]{1,0:T(8,128)(2,1)S(1)}, bf16[256,256]{1,0:T(8,128)(2,1)S(1)}, u32[]{:S(2)}, u32[]{:S(2)}) collective-permute-start(bf16[256,256]{1,0:T(8,128)(2,1)S(1)} %collective-permute-done.1.refs_2_), channel_id=1, source_target_pairs={{0,8},{8,16},{16,24},{24,28},{28,20},{20,12},{12,4},{4,0},{1,5},{5... | collective-permute-start | bytes 393224 | tf_op jit(solution)/shard_map/ppermute | solution.py:475
  15.6 0.0 copy-done.2
  15.7 1.5 %collective-permute-start.5 = (bf16[256,256]{1,0:T(8,128)(2,1)S(1)}, bf16[256,256]{1,0:T(8,128)(2,1)S(1)}, u32[]{:S(2)}, u32[]{:S(2)}) collective-permute-start(bf16[256,256]{1,0:T(8,128)(2,1)S(1)} %copy-done.2), channel_id=1, source_target_pairs={{0,2},{1,3},{2,0},{3,1},{4,6},{5,7},{6,4},{7,5},{8,10},{9,11},{10,... | collective-permute-start | bytes 393224 | tf_op jit(solution)/shard_map/ppermute | solution.py:479
  17.1 0.7 collective-permute-start.7
  17.8 2.5 %collective-permute-done.2.refs_3_ = bf16[256,256]{1,0:T(8,128)(2,1)S(1)} collective-permute-done((bf16[256,256]{1,0:T(8,128)(2,1)S(1)}, bf16[256,256]{1,0:T(8,128)(2,1)S(1)}, u32[]{:S(2)}, u32[]{:S(2)}) %collective-permute-start.2) | collective-permute-done | bytes 131104 | tf_op jit(solution)/shard_map/ppermute | solution.py:475
  20.3 0.3 collective-permute-done.5.refs_4_
  20.6 1.6 %collective-permute-start.6 = (bf16[256,256]{1,0:T(8,128)(2,1)S(1)}, bf16[256,256]{1,0:T(8,128)(2,1)S(1)}, u32[]{:S(2)}, u32[]{:S(2)}) collective-permute-start(bf16[256,256]{1,0:T(8,128)(2,1)S(1)} %collective-permute-done.2.refs_3_), channel_id=1, source_target_pairs={{0,8},{8,16},{16,24},{24,28},{28,20},{20,12},{12,4},{4,0},{1,5},{5... | collective-permute-start | bytes 393224 | tf_op jit(solution)/shard_map/ppermute | solution.py:475
  22.2 2.9 %build_rest.1.dense_ref = bf16[1024,2048]{1,0:T(8,128)(2,1)S(1)} custom-call(s32[513]{0:T(1024)S(1)} %add_reduce_fusion.list_ref, bf16[256,128,128]{2,1,0:T(8,128)(2,1)} %bitcast.4, bf16[1024,2048]{1,0:T(8,128)(2,1)S(1)} %build_first.1.half_ref), custom_call_target="tpu_custom_call" | custom-call | flops 4194304 | bytes 6291456 | tf_op jit(solution)/shard_map/build_rest/pallas_call | solution.py:189
  25.1 0.0 collective-permute-done.7.refs_7_
  25.1 0.5 collective-permute-done.6.refs_4_
  25.6 0.0 copy-done
  25.6 0.7 %forward_product.2 = bf16[512,256]{1,0:T(8,128)(2,1)S(1)} custom-call(bf16[1024,2048]{1,0:T(8,128)(2,1)S(1)} %build_rest.1.dense_ref, bf16[256,256]{1,0:T(8,128)(2,1)S(1)} %copy-done, bf16[256,256]{1,0:T(8,128)(2,1)S(1)} %collective-permute-done.refs_1_, bf16[256,256]{1,0:T(8,128)(2,1)S(1)} %collective-permute-done.1.refs_2_, ...), custom_call_target="tpu_custom_call" | custom-call | flops 536870912 | bytes 3407872 | tf_op jit(solution)/shard_map/forward_product/pallas_call | solution.py:251
  26.3 0.0 copy-start.1
  26.3 0.1 collective-permute-start.8
  26.4 0.7 %forward_product.3 = bf16[512,256]{1,0:T(8,128)(2,1)S(1)} custom-call(bf16[1024,2048]{1,0:T(8,128)(2,1)S(1)} %build_rest.1.dense_ref, bf16[256,256]{1,0:T(8,128)(2,1)S(1)} %copy-done, bf16[256,256]{1,0:T(8,128)(2,1)S(1)} %collective-permute-done.refs_1_, bf16[256,256]{1,0:T(8,128)(2,1)S(1)} %collective-permute-done.1.refs_2_, ...), custom_call_target="tpu_custom_call" | custom-call | flops 536870912 | bytes 3407872 | tf_op jit(solution)/shard_map/forward_product/pallas_call | solution.py:251
  27.1 0.8 %collective-permute-done.8 = bf16[512,256]{1,0:T(8,128)(2,1)S(1)} collective-permute-done((bf16[512,256]{1,0:T(8,128)(2,1)S(1)}, bf16[512,256]{1,0:T(8,128)(2,1)S(1)}, u32[]{:S(2)}, u32[]{:S(2)}) %collective-permute-start.8) | collective-permute-done | bytes 262176 | tf_op jit(solution)/shard_map/ppermute | solution.py:479
  27.9 0.1 add_convert_fusion.refs_0_
  28.0 1.6 %collective-permute-start.9 = (bf16[512,256]{1,0:T(8,128)(2,1)S(1)}, bf16[512,256]{1,0:T(8,128)(2,1)S(1)}, u32[]{:S(2)}, u32[]{:S(2)}) collective-permute-start(bf16[512,256]{1,0:T(8,128)(2,1)S(1)} %add_convert_fusion.refs_0_), channel_id=1, source_target_pairs={{0,2},{1,3},{2,0},{3,1},{4,6},{5,7},{6,4},{7,5},{8,10},{9,11},{10,... | collective-permute-start | bytes 786440 | tf_op jit(solution)/shard_map/ppermute | solution.py:479
  29.6 6.9 %collective-permute-done.9.refs_1_ = bf16[512,256]{1,0:T(8,128)(2,1)S(1)} collective-permute-done((bf16[512,256]{1,0:T(8,128)(2,1)S(1)}, bf16[512,256]{1,0:T(8,128)(2,1)S(1)}, u32[]{:S(2)}, u32[]{:S(2)}) %collective-permute-start.9) | collective-permute-done | bytes 262176 | tf_op jit(solution)/shard_map/ppermute | solution.py:479
  36.4 0.0 copy-done.1
  36.4 1.0 %middle.1 = (bf16[256,256]{1,0:T(8,128)(2,1)}, bf16[768,256]{1,0:T(8,128)(2,1)S(1)}, f32[128,256]{1,0:T(8,128)S(1)}) custom-call(bf16[512,256]{1,0:T(8,128)(2,1)S(1)} %add_convert_fusion.refs_0_, bf16[512,256]{1,0:T(8,128)(2,1)S(1)} %collective-permute-done.9.refs_1_, bf16[256,256]{1,0:T(8,128)(2,1)S(1)} %copy-done.1, bf16[256,256]{1,0:T(8,128)(2,1)S(1)} %copy-done.2, ...), custom_call_target="tpu_custom_call" | custom-call | flops 335544320 | bytes 1572864 | tf_op jit(solution)/shard_map/middle/pallas_call | solution.py:315
  37.4 0.1 collective-permute-start.10
  37.5 1.7 %collective-permute-done.10.sibling_ref = bf16[768,256]{1,0:T(8,128)(2,1)S(1)} collective-permute-done((bf16[768,256]{1,0:T(8,128)(2,1)S(1)}, bf16[768,256]{1,0:T(8,128)(2,1)S(1)}, u32[]{:S(2)}, u32[]{:S(2)}) %collective-permute-start.10) | collective-permute-done | bytes 393248 | tf_op jit(solution)/shard_map/ppermute | solution.py:479
  39.2 0.6 backward_product.2
  39.9 1.8 %collective-permute-start.11 = (bf16[384,256]{1,0:T(8,128)(2,1)S(1)}, bf16[384,256]{1,0:T(8,128)(2,1)S(1)}, u32[]{:S(2)}, u32[]{:S(2)}) collective-permute-start(bf16[384,256]{1,0:T(8,128)(2,1)S(1)} %get-tuple-element.54), channel_id=1, source_target_pairs={{0,8},{8,16},{16,24},{24,28},{28,20},{20,12},{12,4},{4,0},{1,5},{5... | collective-permute-start | bytes 589832 | tf_op jit(solution)/shard_map/ppermute | solution.py:475
  41.6 0.3 collective-permute-start.15
  41.9 1.1 %backward_product.3 = (bf16[384,256]{1,0:T(8,128)(2,1)S(1)}, bf16[384,256]{1,0:T(8,128)(2,1)S(1)}, bf16[384,256]{1,0:T(8,128)(2,1)S(1)}, bf16[384,256]{1,0:T(8,1...) custom-call(bf16[1024,2048]{1,0:T(8,128)(2,1)S(1)} %build_rest.1.dense_ref, ...), custom_call_target="tpu_custom_call" | custom-call | flops 134217728 | bytes 786432 | tf_op jit(solution)/shard_map/backward_product/pallas_call | solution.py:377
  43.1 4.2 %collective-permute-done.11.refs_1_ = bf16[384,256]{1,0:T(8,128)(2,1)S(1)} collective-permute-done((bf16[384,256]{1,0:T(8,128)(2,1)S(1)}, bf16[384,256]{1,0:T(8,128)(2,1)S(1)}, u32[]{:S(2)}, u32[]{:S(2)}) %collective-permute-start.11) | collective-permute-done | bytes 196640 | tf_op jit(solution)/shard_map/ppermute | solution.py:475
  47.4 1.4 %collective-permute-start.12 = (bf16[384,256]{1,0:T(8,128)(2,1)S(1)}, bf16[384,256]{1,0:T(8,128)(2,1)S(1)}, u32[]{:S(2)}, u32[]{:S(2)}) collective-permute-start(bf16[384,256]{1,0:T(8,128)(2,1)S(1)} %add_convert_fusion.5), channel_id=1, source_target_pairs={{0,8},{8,16},{16,24},{24,28},{28,20},{20,12},{12,4},{4,0},{1,5},{5... | collective-permute-start | bytes 589832 | tf_op jit(solution)/shard_map/ppermute | solution.py:475
  48.7 0.0 collective-permute-done.15.refs_2_
  48.8 0.8 %collective-permute-start.16 = (bf16[384,256]{1,0:T(8,128)(2,1)S(1)}, bf16[384,256]{1,0:T(8,128)(2,1)S(1)}, u32[]{:S(2)}, u32[]{:S(2)}) collective-permute-start(bf16[384,256]{1,0:T(8,128)(2,1)S(1)} %add_convert_fusion.2), channel_id=1, source_target_pairs={{0,4},{8,0},{16,8},{24,16},{28,24},{20,28},{12,20},{4,12},{1,9},{5... | collective-permute-start | bytes 589832 | tf_op jit(solution)/shard_map/ppermute | solution.py:475
  49.6 4.8 %collective-permute-done.12.refs_3_ = bf16[384,256]{1,0:T(8,128)(2,1)S(1)} collective-permute-done((bf16[384,256]{1,0:T(8,128)(2,1)S(1)}, bf16[384,256]{1,0:T(8,128)(2,1)S(1)}, u32[]{:S(2)}, u32[]{:S(2)}) %collective-permute-start.12) | collective-permute-done | bytes 196640 | tf_op jit(solution)/shard_map/ppermute | solution.py:475
  54.5 0.6 collective-permute-start.13
  55.0 1.5 %collective-permute-done.16.refs_4_ = bf16[384,256]{1,0:T(8,128)(2,1)S(1)} collective-permute-done((bf16[384,256]{1,0:T(8,128)(2,1)S(1)}, bf16[384,256]{1,0:T(8,128)(2,1)S(1)}, u32[]{:S(2)}, u32[]{:S(2)}) %collective-permute-start.16) | collective-permute-done | bytes 196640 | tf_op jit(solution)/shard_map/ppermute | solution.py:475
  56.5 0.1 collective-permute-start.17
  56.7 4.0 %collective-permute-done.13.refs_5_ = bf16[384,256]{1,0:T(8,128)(2,1)S(1)} collective-permute-done((bf16[384,256]{1,0:T(8,128)(2,1)S(1)}, bf16[384,256]{1,0:T(8,128)(2,1)S(1)}, u32[]{:S(2)}, u32[]{:S(2)}) %collective-permute-start.13) | collective-permute-done | bytes 196640 | tf_op jit(solution)/shard_map/ppermute | solution.py:475
  60.7 0.3 collective-permute-start.14
  61.1 2.3 %collective-permute-done.17.refs_2_.refs_6_ = bf16[384,256]{1,0:T(8,128)(2,1)S(1)} collective-permute-done((bf16[384,256]{1,0:T(8,128)(2,1)S(1)}, bf16[384,256]{1,0:T(8,128)(2,1)S(1)}, u32[]{:S(2)}, u32[]{:S(2)}) %collective-permute-start.17) | collective-permute-done | bytes 196640 | tf_op jit(solution)/shard_map/ppermute | solution.py:475
  63.4 3.0 %collective-permute-done.14.refs_1_.refs_7_ = bf16[384,256]{1,0:T(8,128)(2,1)S(1)} collective-permute-done((bf16[384,256]{1,0:T(8,128)(2,1)S(1)}, bf16[384,256]{1,0:T(8,128)(2,1)S(1)}, u32[]{:S(2)}, u32[]{:S(2)}) %collective-permute-start.14) | collective-permute-done | bytes 196640 | tf_op jit(solution)/shard_map/ppermute | solution.py:475
  66.4 0.1 summed_terms.1.own_ref
  66.6 0.1 collective-permute-start.18
  66.7 0.8 %finish.1 = bf16[256,256]{1,0:T(8,128)(2,1)} custom-call(bf16[256,256]{1,0:T(8,128)(2,1)S(1)} %get-tuple-element.50.refs_0_, bf16[384,256]{1,0:T(8,128)(2,1)S(1)} %collective-permute-done.14.refs_1_.refs_7_, bf16[384,256]{1,0:T(8,128)(2,1)S(1)} %collective-permute-done.17.refs_2_.refs_6_), custom_call_target="tpu_custom_call" | custom-call | flops 196608 | bytes 524288 | tf_op jit(solution)/shard_map/finish/pallas_call | solution.py:435
  67.4 0.6 collective-permute-done.18.sibling_ref
  68.0 0.7 %joined.1 = f32[256,256]{1,0:T(8,128)} custom-call(f32[128,256]{1,0:T(8,128)S(1)} %summed_terms.1.own_ref, f32[128,256]{1,0:T(8,128)S(1)} %collective-permute-done.18.sibling_ref), custom_call_target="tpu_custom_call" | custom-call | bytes 524288 | tf_op jit(solution)/shard_map/joined/pallas_call | solution.py:457
  (5 shorter events, 0.2 us)
Async XLA Ops:
  0.6 7.1 %collective-permute-start.3 = (bf16[256,256]{1,0:T(8,128)(2,1)}, bf16[256,256]{1,0:T(8,128)(2,1)S(1)}, u32[]{:S(2)}, u32[]{:S(2)}) collective-permute-start(bf16[256,256]{1,0:T(8,128)(2,1)} %refs_0_.3), channel_id=1, source_target_pairs={{0,4},{8,0},{16,8},{24,16},{28,24},{20,28},{12,20},{4,12},{1,9},{5... | collective-permute-start | bytes 393224 | tf_op jit(solution)/shard_map/ppermute | solution.py:475
  3.6 5.5 %collective-permute-start = (bf16[256,256]{1,0:T(8,128)(2,1)}, bf16[256,256]{1,0:T(8,128)(2,1)S(1)}, u32[]{:S(2)}, u32[]{:S(2)}) collective-permute-start(bf16[256,256]{1,0:T(8,128)(2,1)} %refs_0_.3), channel_id=1, source_target_pairs={{0,8},{8,16},{16,24},{24,28},{28,20},{20,12},{12,4},{4,0},{1,5},{5... | collective-permute-start | bytes 393224 | tf_op jit(solution)/shard_map/ppermute | solution.py:475
  7.7 6.2 %collective-permute-start.4 = (bf16[256,256]{1,0:T(8,128)(2,1)S(1)}, bf16[256,256]{1,0:T(8,128)(2,1)S(1)}, u32[]{:S(2)}, u32[]{:S(2)}) collective-permute-start(bf16[256,256]{1,0:T(8,128)(2,1)S(1)} %collective-permute-done.3.refs_5_), channel_id=1, source_target_pairs={{0,4},{8,0},{16,8},{24,16},{28,24},{20,28},{12,20},{4,12},{1,9},{5... | collective-permute-start | bytes 393224 | tf_op jit(solution)/shard_map/ppermute | solution.py:475
  9.2 5.0 %collective-permute-start.1 = (bf16[256,256]{1,0:T(8,128)(2,1)S(1)}, bf16[256,256]{1,0:T(8,128)(2,1)S(1)}, u32[]{:S(2)}, u32[]{:S(2)}) collective-permute-start(bf16[256,256]{1,0:T(8,128)(2,1)S(1)} %collective-permute-done.refs_1_), channel_id=1, source_target_pairs={{0,8},{8,16},{16,24},{24,28},{28,20},{20,12},{12,4},{4,0},{1,5},{5... | collective-permute-start | bytes 393224 | tf_op jit(solution)/shard_map/ppermute | solution.py:475
  10.1 5.5 %copy-start.2 = (bf16[256,256]{1,0:T(8,128)(2,1)S(1)}, bf16[256,256]{1,0:T(8,128)(2,1)}, u32[]{:S(2)}) copy-start(bf16[256,256]{1,0:T(8,128)(2,1)} %refs_3_) | copy-start | bytes 393220
  12.8 12.8 %copy-start = (bf16[256,256]{1,0:T(8,128)(2,1)S(1)}, bf16[256,256]{1,0:T(8,128)(2,1)}, u32[]{:S(2)}) copy-start(bf16[256,256]{1,0:T(8,128)(2,1)} %refs_0_.3) | copy-start | bytes 393220
  14.2 6.2 %collective-permute-start.2 = (bf16[256,256]{1,0:T(8,128)(2,1)S(1)}, bf16[256,256]{1,0:T(8,128)(2,1)S(1)}, u32[]{:S(2)}, u32[]{:S(2)}) collective-permute-start(bf16[256,256]{1,0:T(8,128)(2,1)S(1)} %collective-permute-done.1.refs_2_), channel_id=1, source_target_pairs={{0,8},{8,16},{16,24},{24,28},{28,20},{20,12},{12,4},{4,0},{1,5},{5... | collective-permute-start | bytes 393224 | tf_op jit(solution)/shard_map/ppermute | solution.py:475
  15.7 5.0 %collective-permute-start.5 = (bf16[256,256]{1,0:T(8,128)(2,1)S(1)}, bf16[256,256]{1,0:T(8,128)(2,1)S(1)}, u32[]{:S(2)}, u32[]{:S(2)}) collective-permute-start(bf16[256,256]{1,0:T(8,128)(2,1)S(1)} %copy-done.2), channel_id=1, source_target_pairs={{0,2},{1,3},{2,0},{3,1},{4,6},{5,7},{6,4},{7,5},{8,10},{9,11},{10,... | collective-permute-start | bytes 393224 | tf_op jit(solution)/shard_map/ppermute | solution.py:479
  17.1 8.0 %collective-permute-start.7 = (bf16[256,256]{1,0:T(8,128)(2,1)S(1)}, bf16[256,256]{1,0:T(8,128)(2,1)S(1)}, u32[]{:S(2)}, u32[]{:S(2)}) collective-permute-start(bf16[256,256]{1,0:T(8,128)(2,1)S(1)} %collective-permute-done.4.refs_6_), channel_id=1, source_target_pairs={{0,4},{8,0},{16,8},{24,16},{28,24},{20,28},{12,20},{4,12},{1,9},{5... | collective-permute-start | bytes 393224 | tf_op jit(solution)/shard_map/ppermute | solution.py:475
  20.6 5.0 %collective-permute-start.6 = (bf16[256,256]{1,0:T(8,128)(2,1)S(1)}, bf16[256,256]{1,0:T(8,128)(2,1)S(1)}, u32[]{:S(2)}, u32[]{:S(2)}) collective-permute-start(bf16[256,256]{1,0:T(8,128)(2,1)S(1)} %collective-permute-done.2.refs_3_), channel_id=1, source_target_pairs={{0,8},{8,16},{16,24},{24,28},{28,20},{20,12},{12,4},{4,0},{1,5},{5... | collective-permute-start | bytes 393224 | tf_op jit(solution)/shard_map/ppermute | solution.py:475
  26.3 10.1 %copy-start.1 = (bf16[256,256]{1,0:T(8,128)(2,1)S(1)}, bf16[256,256]{1,0:T(8,128)(2,1)}, u32[]{:S(2)}) copy-start(bf16[256,256]{1,0:T(8,128)(2,1)} %refs_2_.1) | copy-start | bytes 393220
  26.3 1.6 %collective-permute-start.8 = (bf16[512,256]{1,0:T(8,128)(2,1)S(1)}, bf16[512,256]{1,0:T(8,128)(2,1)S(1)}, u32[]{:S(2)}, u32[]{:S(2)}) collective-permute-start(bf16[512,256]{1,0:T(8,128)(2,1)S(1)} %forward_product.2), channel_id=1, source_target_pairs={{0,1},{1,0},{2,3},{3,2},{4,5},{5,4},{6,7},{7,6},{8,9},{9,8},{10,11... | collective-permute-start | bytes 786440 | tf_op jit(solution)/shard_map/ppermute | solution.py:479
  28.0 8.4 %collective-permute-start.9 = (bf16[512,256]{1,0:T(8,128)(2,1)S(1)}, bf16[512,256]{1,0:T(8,128)(2,1)S(1)}, u32[]{:S(2)}, u32[]{:S(2)}) collective-permute-start(bf16[512,256]{1,0:T(8,128)(2,1)S(1)} %add_convert_fusion.refs_0_), channel_id=1, source_target_pairs={{0,2},{1,3},{2,0},{3,1},{4,6},{5,7},{6,4},{7,5},{8,10},{9,11},{10,... | collective-permute-start | bytes 786440 | tf_op jit(solution)/shard_map/ppermute | solution.py:479
  37.4 1.8 %collective-permute-start.10 = (bf16[768,256]{1,0:T(8,128)(2,1)S(1)}, bf16[768,256]{1,0:T(8,128)(2,1)S(1)}, u32[]{:S(2)}, u32[]{:S(2)}) collective-permute-start(bf16[768,256]{1,0:T(8,128)(2,1)S(1)} %get-tuple-element.44.own_ref), channel_id=1, source_target_pairs={{0,1},{1,0},{2,3},{3,2},{4,5},{5,4},{6,7},{7,6},{8,9},{9,8},{10,11... | collective-permute-start | bytes 1179656 | tf_op jit(solution)/shard_map/ppermute | solution.py:479
  39.9 7.5 %collective-permute-start.11 = (bf16[384,256]{1,0:T(8,128)(2,1)S(1)}, bf16[384,256]{1,0:T(8,128)(2,1)S(1)}, u32[]{:S(2)}, u32[]{:S(2)}) collective-permute-start(bf16[384,256]{1,0:T(8,128)(2,1)S(1)} %get-tuple-element.54), channel_id=1, source_target_pairs={{0,8},{8,16},{16,24},{24,28},{28,20},{20,12},{12,4},{4,0},{1,5},{5... | collective-permute-start | bytes 589832 | tf_op jit(solution)/shard_map/ppermute | solution.py:475
  41.6 7.1 %collective-permute-start.15 = (bf16[384,256]{1,0:T(8,128)(2,1)S(1)}, bf16[384,256]{1,0:T(8,128)(2,1)S(1)}, u32[]{:S(2)}, u32[]{:S(2)}) collective-permute-start(bf16[384,256]{1,0:T(8,128)(2,1)S(1)} %get-tuple-element.57), channel_id=1, source_target_pairs={{0,4},{8,0},{16,8},{24,16},{28,24},{20,28},{12,20},{4,12},{1,9},{5... | collective-permute-start | bytes 589832 | tf_op jit(solution)/shard_map/ppermute | solution.py:475
  47.4 7.0 %collective-permute-start.12 = (bf16[384,256]{1,0:T(8,128)(2,1)S(1)}, bf16[384,256]{1,0:T(8,128)(2,1)S(1)}, u32[]{:S(2)}, u32[]{:S(2)}) collective-permute-start(bf16[384,256]{1,0:T(8,128)(2,1)S(1)} %add_convert_fusion.5), channel_id=1, source_target_pairs={{0,8},{8,16},{16,24},{24,28},{28,20},{20,12},{12,4},{4,0},{1,5},{5... | collective-permute-start | bytes 589832 | tf_op jit(solution)/shard_map/ppermute | solution.py:475
  48.8 7.7 %collective-permute-start.16 = (bf16[384,256]{1,0:T(8,128)(2,1)S(1)}, bf16[384,256]{1,0:T(8,128)(2,1)S(1)}, u32[]{:S(2)}, u32[]{:S(2)}) collective-permute-start(bf16[384,256]{1,0:T(8,128)(2,1)S(1)} %add_convert_fusion.2), channel_id=1, source_target_pairs={{0,4},{8,0},{16,8},{24,16},{28,24},{20,28},{12,20},{4,12},{1,9},{5... | collective-permute-start | bytes 589832 | tf_op jit(solution)/shard_map/ppermute | solution.py:475
  54.5 6.2 %collective-permute-start.13 = (bf16[384,256]{1,0:T(8,128)(2,1)S(1)}, bf16[384,256]{1,0:T(8,128)(2,1)S(1)}, u32[]{:S(2)}, u32[]{:S(2)}) collective-permute-start(bf16[384,256]{1,0:T(8,128)(2,1)S(1)} %add_convert_fusion.4), channel_id=1, source_target_pairs={{0,8},{8,16},{16,24},{24,28},{28,20},{20,12},{12,4},{4,0},{1,5},{5... | collective-permute-start | bytes 589832 | tf_op jit(solution)/shard_map/ppermute | solution.py:475
  56.5 6.9 %collective-permute-start.17 = (bf16[384,256]{1,0:T(8,128)(2,1)S(1)}, bf16[384,256]{1,0:T(8,128)(2,1)S(1)}, u32[]{:S(2)}, u32[]{:S(2)}) collective-permute-start(bf16[384,256]{1,0:T(8,128)(2,1)S(1)} %add_convert_fusion.1), channel_id=1, source_target_pairs={{0,4},{8,0},{16,8},{24,16},{28,24},{20,28},{12,20},{4,12},{1,9},{5... | collective-permute-start | bytes 589832 | tf_op jit(solution)/shard_map/ppermute | solution.py:475
  60.7 5.7 %collective-permute-start.14 = (bf16[384,256]{1,0:T(8,128)(2,1)S(1)}, bf16[384,256]{1,0:T(8,128)(2,1)S(1)}, u32[]{:S(2)}, u32[]{:S(2)}) collective-permute-start(bf16[384,256]{1,0:T(8,128)(2,1)S(1)} %add_convert_fusion.3), channel_id=1, source_target_pairs={{0,8},{8,16},{16,24},{24,28},{28,20},{20,12},{12,4},{4,0},{1,5},{5... | collective-permute-start | bytes 589832 | tf_op jit(solution)/shard_map/ppermute | solution.py:475
  66.6 1.4 %collective-permute-start.18 = (f32[128,256]{1,0:T(8,128)S(1)}, f32[128,256]{1,0:T(8,128)S(1)}, u32[]{:S(2)}, u32[]{:S(2)}) collective-permute-start(f32[128,256]{1,0:T(8,128)S(1)} %summed_terms.1.own_ref), channel_id=1, source_target_pairs={{0,1},{1,0},{2,3},{3,2},{4,5},{5,4},{6,7},{7,6},{8,9},{9,8},{10,11... | collective-permute-start | bytes 393224 | tf_op jit(solution)/shard_map/ppermute | solution.py:479

commit v13 on v11

--- a/solution.py
+++ b/solution.py
@@ -343,30 +343,31 @@
     for copy in copies:
         copy.wait()
     place = ring_place(lax.axis_index("row"), row_count)
-    for (offset, tail), out_ref in zip(outputs, out_refs):
-        if tail != "terms alone":
-            along = pl.ds(pl.multiple_of(ring_row(place + offset, row_count) * wide, wide), wide)
-            part = jnp.dot(depth[...], dense_ref[:, along], preferred_element_type=jnp.float32)
-            out_ref[pl.ds(0, width), :] = part.astype(jnp.bfloat16)
-        if tail == "terms alone":
-            out_ref[...] = terms
-        elif tail == "terms":
-            out_ref[pl.ds(width, size), :] = terms
-        elif tail == "zeros":
-            out_ref[pl.ds(width, size), :] = jnp.zeros_like(terms)
+    strips = {}
+    for (offset, layout), out_ref in zip(outputs, out_refs):
+        start = 0
+        for kind, first, high in layout:
+            if kind == "strip" and offset not in strips:
+                along = pl.ds(pl.multiple_of(ring_row(place + offset, row_count) * wide, wide), wide)
+                part = jnp.dot(depth[...], dense_ref[:, along], preferred_element_type=jnp.float32)
+                strips[offset] = part.astype(jnp.bfloat16)
+            source = {"strip": strips.get(offset), "terms": terms, "zeros": jnp.zeros_like(terms)}[kind]
+            out_ref[start : start + high, :] = source[first : first + high, :]
+            start += high
 
 
 def backward_product(dense, own, sibling, chunk, outputs, row_count, col_count):
     high, deep = dense.shape
     size, width = chunk.shape
     wide = deep // row_count
-    heights = {"": width, "terms alone": size, "terms": width + size, "zeros": width + size}
     cell = ((high, deep), jnp.bfloat16)
     depth = ((width, high), jnp.bfloat16)
     out = ((len(outputs), width + size, wide), jnp.float32)
     return pl.pallas_call(
         functools.partial(backward_kernel, outputs=outputs, row_count=row_count),
-        out_shape=[jax.ShapeDtypeStruct((heights[tail], wide), jnp.bfloat16) for _, tail in outputs],
+        out_shape=[
+            jax.ShapeDtypeStruct((sum(high for _, _, high in layout), wide), jnp.bfloat16) for _, layout in outputs
+        ],
         in_specs=[pl.BlockSpec(memory_space=pltpu.VMEM)] * 4,
         out_specs=[pl.BlockSpec(memory_space=pltpu.VMEM)] * len(outputs),
         scratch_shapes=[pltpu.VMEM(*depth), pltpu.SemaphoreType.DMA((col_count,))],
@@ -378,52 +379,55 @@
     )(dense, own, sibling, chunk)
 
 
-def terms_kernel(*refs, offsets, first_rows):
+def terms_kernel(*refs, pieces):
     term_refs, out_ref, places = refs[:-2], refs[-2], refs[-1]
-    row_count, size, _ = places.shape
+    row_count = places.shape[0]
     place = ring_place(lax.axis_index("row"), row_count)
-    for offset, first, ref in zip(offsets, first_rows, term_refs):
-        places[ring_row(place + offset, row_count)] = ref[pl.ds(first, size), :].astype(jnp.float32)
+    for (offset, first, high, at), ref in zip(pieces, term_refs):
+        places[ring_row(place + offset, row_count), pl.ds(at, high), :] = ref[pl.ds(first, high), :].astype(jnp.float32)
     total = places[0]
     for index in range(1, row_count):
         total += places[index]
     out_ref[...] = total
 
 
-def summed_terms(terms, size):
-    offsets = tuple(offset for offset, _, _ in terms)
-    first_rows = tuple(first for _, first, _ in terms)
-    arrays = [array for _, _, array in terms]
+def summed_terms(terms, size, row_count):
+    pieces = tuple(piece for *piece, _ in terms)
+    arrays = [array for *_, array in terms]
     width = arrays[0].shape[1]
     return pl.pallas_call(
-        functools.partial(terms_kernel, offsets=offsets, first_rows=first_rows),
+        functools.partial(terms_kernel, pieces=pieces),
         out_shape=jax.ShapeDtypeStruct((size, width), jnp.float32),
         in_specs=[pl.BlockSpec(memory_space=pltpu.VMEM)] * len(arrays),
         out_specs=pl.BlockSpec(memory_space=pltpu.VMEM),
-        scratch_shapes=[pltpu.VMEM((len(arrays), size, width), jnp.float32)],
+        scratch_shapes=[pltpu.VMEM((row_count, size, width), jnp.float32)],
         compiler_params=pltpu.CompilerParams(
-            vmem_limit_bytes=scratch_bytes(*((array.shape, array.dtype) for array in arrays)) + 8 * mib
+            vmem_limit_bytes=scratch_bytes(*((array.shape, array.dtype) for array in arrays))
+            + scratch_bytes(((row_count, size, width), jnp.float32))
+            + 6 * mib
         ),
         cost_estimate=pl.CostEstimate(
-            flops=len(arrays) * size * width, bytes_accessed=2 * len(arrays) * size * width, transcendentals=0
+            flops=row_count * size * width, bytes_accessed=2 * row_count * size * width, transcendentals=0
         ),
         name="summed_terms",
     )(*arrays)
 
 
-def finish_kernel(*refs):
+def finish_kernel(*refs, firsts):
     *part_refs, features_ref = refs
     width = features_ref.shape[1]
-    total = part_refs[0][pl.ds(0, width), :].astype(jnp.float32)
-    for part_ref in part_refs[1:]:
-        total += part_ref[pl.ds(0, width), :].astype(jnp.float32)
+    total = jnp.zeros(features_ref.shape[::-1], jnp.float32)
+    for first, part_ref in zip(firsts, part_refs):
+        total += part_ref[pl.ds(first, width), :].astype(jnp.float32)
     features_ref[...] = total.astype(jnp.bfloat16).T
 
 
 def finish(parts):
+    firsts = tuple(first for first, _ in parts)
+    parts = [array for _, array in parts]
     width, rows = parts[0].shape
     return pl.pallas_call(
-        finish_kernel,
+        functools.partial(finish_kernel, firsts=firsts),
         out_shape=jax.ShapeDtypeStruct((rows, width), jnp.bfloat16),
         in_specs=[pl.BlockSpec(memory_space=pltpu.VMEM)] * len(parts),
         out_specs=pl.BlockSpec(memory_space=pltpu.VMEM),
@@ -493,31 +497,41 @@
     return shards, dense, [cotangent] + others
 
 
-def added(first, second):
-    return (first.astype(jnp.float32) + second[: first.shape[0]].astype(jnp.float32)).astype(jnp.bfloat16)
+def added(first, second, at=0):
+    spare = first.shape[0] - at - second.shape[0]
+    second = jnp.pad(second.astype(jnp.float32), ((at, spare), (0, 0)))
+    return (first.astype(jnp.float32) + second).astype(jnp.bfloat16)
 
 
 def scattered_sums(dense, own, sibling, chunk):
     row_count, col_count = lax.axis_size("row"), lax.axis_size("col")
     size, width = chunk.shape
+    half, half_size = width // 2, size // 2
     reach = row_count // 2
-    first = ((reach, "terms"), (1 - reach, "terms"), (0, "terms alone"))
+    strip, terms, zeros = ("strip", 0, width), ("terms", 0, size), ("zeros", 0, size)
+    first = (
+        (reach, (terms, ("strip", 0, half))),
+        (reach, (("strip", half, half), terms)),
+        (0, (terms,)),
+    )
     above, below, terms = backward_product(dense, own, sibling, chunk, first, row_count, col_count)
     above, below, terms, cell = lax.optimization_barrier((above, below, terms, dense))
     up, down = around(above, 1), around(below, -1)
-    all_terms = [(0, 0, terms)]
-
-    ups = tuple((offset, "zeros") for offset in range(reach - 1, 0, -1))
-    downs = tuple((-offset, "zeros") for offset in range(reach - 2, 0, -1))
-    strips = backward_product(cell, own, sibling, chunk, ups + downs + ((0, ""),), row_count, col_count)
+    all_terms = [(0, 0, size, 0, terms)]
+
+    few_zeros = ("zeros", 0, half_size)
+    ups = tuple((offset, (zeros if offset > 1 else few_zeros, strip)) for offset in range(reach - 1, 0, -1))
+    downs = tuple((-offset, (strip, zeros if offset > 1 else few_zeros)) for offset in range(reach - 1, 0, -1))
+    strips = backward_product(cell, own, sibling, chunk, ups + downs + ((0, (strip,)),), row_count, col_count)
     ups, downs, mine = strips[: reach - 1], strips[reach - 1 : -1], strips[-1]
     for step in range(1, reach):
-        all_terms += [(-step, width, up), (step, width, down)]
+        all_terms += [(-step, 0, size, 0, up), (step, down.shape[0] - size, size, 0, down)]
+        if step == reach - 1:
+            up, down = up[half_size:], down[: width + half_size]
         up = around(added(ups[step - 1], up), 1)
-        if step < reach - 1:
-            down = around(added(downs[step - 1], down), -1)
-    all_terms.append((reach, width, up))
-    return [mine, up, down], summed_terms(all_terms, size)
+        down = around(added(downs[step - 1], down, half if step == 1 else 0), -1)
+    all_terms += [(reach, 0, half_size, half_size, up), (reach, width, half_size, 0, down)]
+    return [(0, mine), (half_size, up), (0, down)], summed_terms(all_terms, size, row_count)
 
 
 def per_device(features, weight, adj_tiles, tile_rows, tile_cols, tile_counts, out_grad):

time: 67.1 us -> 66 us (0.984)
  waiting for transfers between devices: 32.8 us -> 28.8 us
  Pallas kernels: 10.9 us -> 14.2 us
    ppermute x14 -> x15, waiting for transfers between devices: 22.9 us -> 18.9 us  [around(): lax.ppermute(value, 'row', [(order[i], order[(i + step) % count]) for i i...]
    pallas_call x1, Pallas kernels: 2.39 us -> 4.7 us  [build_stages(): pl.pallas_call(functools.partial(build_rest_kernel, blocks=blocks), out_s...]
    pallas_call x1, Pallas kernels: 2.66 us -> 3.69 us  [build_stages(): pl.pallas_call(functools.partial(build_first_kernel, blocks=blocks), out_...]
    ppermute x14 -> x15, starting transfers between devices: 17 us -> 16.8 us  [around(): lax.ppermute(value, 'row', [(order[i], order[(i + step) % count]) for i i...]
  transfers between devices with their start and end apart: 19 -> 20, of which waited for: 14 -> 13; matrix products, arithmetic and copies ran while one was open for 1% -> 1% of each run, Pallas kernels for 11% -> 17%
where the time goes in v13:
time: 66 us; the launch traced here: 65.8 us
  waiting for transfers between devices  28.8 us (44%)
  starting transfers between devices  20.3 us (31%)
  Pallas kernels  14.2 us (22%)
  between operations  1.46 us (2%)
  other arithmetic  1.04 us (2%)
    ppermute x15, waiting for transfers between devices, around(): lax.ppermute(value, 'row', [(order[i], order[(i + step) % count]) for i i...  18.9 us
    ppermute x15, starting transfers between devices, around(): lax.ppermute(value, 'row', [(order[i], order[(i + step) % count]) for i i...  16.8 us
    ppermute x5, waiting for transfers between devices, swapped(): lax.ppermute(value, axis, [(i, i ^ partner) for i in range(lax.axis_size(...  9.93 us
    pallas_call x1, Pallas kernels, build_stages(): pl.pallas_call(functools.partial(build_rest_kernel, blocks=blocks), out_s...  4.7 us
    pallas_call x1, Pallas kernels, build_stages(): pl.pallas_call(functools.partial(build_first_kernel, blocks=blocks), out_...  3.69 us
    ppermute x5, starting transfers between devices, swapped(): lax.ppermute(value, axis, [(i, i ^ partner) for i in range(lax.axis_size(...  3.43 us
    pallas_call x2, Pallas kernels, backward_product(): pl.pallas_call(functools.partial(backward_kernel, outputs=outputs, row_co...  1.74 us
    pallas_call x2, Pallas kernels, forward_product(): pl.pallas_call(functools.partial(forward_kernel, pieces=pieces, sibling=s...  1.43 us
  transfers between devices with their start and end apart: 20, of which 13 were waited for; matrix products, arithmetic and copies ran while one was open for 1% of the time, Pallas kernels for 17%

profile of v13, /device:TPU:0, one launch (start us, length us, event | category | flops | bytes accessed | tf_op | source)
XLA Modules:
  0.0 65.8 jit_solution(12097121251757945829)
XLA Ops:
  0.6 3.0 %collective-permute-start.3 = (bf16[256,256]{1,0:T(8,128)(2,1)}, bf16[256,256]{1,0:T(8,128)(2,1)S(1)}, u32[]{:S(2)}, u32[]{:S(2)}) collective-permute-start(bf16[256,256]{1,0:T(8,128)(2,1)} %refs_0_.3), channel_id=1, source_target_pairs={{0,4},{8,0},{16,8},{24,16},{28,24},{20,28},{12,20},{4,12},{1,5},{9... | collective-permute-start | bytes 393224 | tf_op jit(solution)/shard_map/ppermute | solution.py:465
  3.6 0.1 collective-permute-start
  4.4 0.7 %add_reduce_fusion.list_ref = s32[513]{0:T(1024)S(1)} fusion(s32[1,1,1]{2,1,0:T(1,128)} %bitcast.2, s32[1,1,256]{2,1,0:T(1,128)} %param.11, s32[1,1,256]{2,1,0:T(1,128)} %param.10), kind=kLoop, calls=%fused_computation.7 | loop fusion | flops 1026 | bytes 4104 | tf_op jit(solution)/shard_map/concatenate | solution.py:541
  5.1 2.3 %collective-permute-done.3.refs_5_ = bf16[256,256]{1,0:T(8,128)(2,1)S(1)} collective-permute-done((bf16[256,256]{1,0:T(8,128)(2,1)}, bf16[256,256]{1,0:T(8,128)(2,1)S(1)}, u32[]{:S(2)}, u32[]{:S(2)}) %collective-permute-start.3) | collective-permute-done | bytes 131104 | tf_op jit(solution)/shard_map/ppermute | solution.py:465
  7.4 1.7 %collective-permute-start.4 = (bf16[256,256]{1,0:T(8,128)(2,1)S(1)}, bf16[256,256]{1,0:T(8,128)(2,1)S(1)}, u32[]{:S(2)}, u32[]{:S(2)}) collective-permute-start(bf16[256,256]{1,0:T(8,128)(2,1)S(1)} %collective-permute-done.3.refs_5_), channel_id=1, source_target_pairs={{0,4},{8,0},{16,8},{24,16},{28,24},{20,28},{12,20},{4,12},{1,5},{9... | collective-permute-start | bytes 393224 | tf_op jit(solution)/shard_map/ppermute | solution.py:465
  9.1 0.0 collective-permute-done.refs_1_
  9.1 0.3 collective-permute-start.1
  9.4 0.0 copy-start.2
  9.4 3.7 %build_first.1.half_ref = bf16[1024,2048]{1,0:T(8,128)(2,1)S(1)} custom-call(s32[513]{0:T(1024)S(1)} %add_reduce_fusion.list_ref, bf16[256,128,128]{2,1,0:T(8,128)(2,1)} %bitcast.3), custom_call_target="tpu_custom_call" | custom-call | flops 4194304 | bytes 6291456 | tf_op jit(solution)/shard_map/build_first/pallas_call | solution.py:179
  13.1 0.0 copy-start
  13.2 0.0 collective-permute-done.4.refs_6_
  13.2 0.9 %collective-permute-done.1.refs_2_ = bf16[256,256]{1,0:T(8,128)(2,1)S(1)} collective-permute-done((bf16[256,256]{1,0:T(8,128)(2,1)S(1)}, bf16[256,256]{1,0:T(8,128)(2,1)S(1)}, u32[]{:S(2)}, u32[]{:S(2)}) %collective-permute-start.1) | collective-permute-done | bytes 131104 | tf_op jit(solution)/shard_map/ppermute | solution.py:465
  14.1 0.3 collective-permute-start.2
  14.4 0.0 copy-done.2
  14.4 1.7 %collective-permute-start.5 = (bf16[256,256]{1,0:T(8,128)(2,1)S(1)}, bf16[256,256]{1,0:T(8,128)(2,1)S(1)}, u32[]{:S(2)}, u32[]{:S(2)}) collective-permute-start(bf16[256,256]{1,0:T(8,128)(2,1)S(1)} %copy-done.2), channel_id=1, source_target_pairs={{0,2},{1,3},{2,0},{3,1},{4,6},{5,7},{6,4},{7,5},{8,10},{9,11},{10,... | collective-permute-start | bytes 393224 | tf_op jit(solution)/shard_map/ppermute | solution.py:469
  16.1 1.5 %collective-permute-start.7 = (bf16[256,256]{1,0:T(8,128)(2,1)S(1)}, bf16[256,256]{1,0:T(8,128)(2,1)S(1)}, u32[]{:S(2)}, u32[]{:S(2)}) collective-permute-start(bf16[256,256]{1,0:T(8,128)(2,1)S(1)} %collective-permute-done.4.refs_6_), channel_id=1, source_target_pairs={{0,4},{8,0},{16,8},{24,16},{28,24},{20,28},{12,20},{4,12},{1,5},{9... | collective-permute-start | bytes 393224 | tf_op jit(solution)/shard_map/ppermute | solution.py:465
  17.6 2.0 %collective-permute-done.2.refs_3_ = bf16[256,256]{1,0:T(8,128)(2,1)S(1)} collective-permute-done((bf16[256,256]{1,0:T(8,128)(2,1)S(1)}, bf16[256,256]{1,0:T(8,128)(2,1)S(1)}, u32[]{:S(2)}, u32[]{:S(2)}) %collective-permute-start.2) | collective-permute-done | bytes 131104 | tf_op jit(solution)/shard_map/ppermute | solution.py:465
  19.6 0.0 collective-permute-done.5.refs_4_
  19.6 1.5 %collective-permute-start.6 = (bf16[256,256]{1,0:T(8,128)(2,1)S(1)}, bf16[256,256]{1,0:T(8,128)(2,1)S(1)}, u32[]{:S(2)}, u32[]{:S(2)}) collective-permute-start(bf16[256,256]{1,0:T(8,128)(2,1)S(1)} %collective-permute-done.2.refs_3_), channel_id=1, source_target_pairs={{0,8},{8,16},{16,24},{24,28},{28,20},{20,12},{12,4},{4,0},{1,9},{9... | collective-permute-start | bytes 393224 | tf_op jit(solution)/shard_map/ppermute | solution.py:465
  21.1 4.7 %build_rest.1.dense_ref = bf16[1024,2048]{1,0:T(8,128)(2,1)S(1)} custom-call(s32[513]{0:T(1024)S(1)} %add_reduce_fusion.list_ref, bf16[256,128,128]{2,1,0:T(8,128)(2,1)} %bitcast.4, bf16[1024,2048]{1,0:T(8,128)(2,1)S(1)} %build_first.1.half_ref), custom_call_target="tpu_custom_call" | custom-call | flops 4194304 | bytes 6291456 | tf_op jit(solution)/shard_map/build_rest/pallas_call | solution.py:189
  25.8 0.0 collective-permute-done.7.refs_7_
  25.8 0.0 collective-permute-done.6.refs_4_
  25.8 0.0 copy-done
  25.9 0.7 %forward_product.2 = bf16[512,256]{1,0:T(8,128)(2,1)S(1)} custom-call(bf16[1024,2048]{1,0:T(8,128)(2,1)S(1)} %build_rest.1.dense_ref, bf16[256,256]{1,0:T(8,128)(2,1)S(1)} %copy-done, bf16[256,256]{1,0:T(8,128)(2,1)S(1)} %collective-permute-done.refs_1_, bf16[256,256]{1,0:T(8,128)(2,1)S(1)} %collective-permute-done.1.refs_2_, ...), custom_call_target="tpu_custom_call" | custom-call | flops 536870912 | bytes 3407872 | tf_op jit(solution)/shard_map/forward_product/pallas_call | solution.py:241
  26.6 0.0 copy-start.1
  26.6 0.1 collective-permute-start.8
  26.7 0.7 %forward_product.3 = bf16[512,256]{1,0:T(8,128)(2,1)S(1)} custom-call(bf16[1024,2048]{1,0:T(8,128)(2,1)S(1)} %build_rest.1.dense_ref, bf16[256,256]{1,0:T(8,128)(2,1)S(1)} %copy-done, bf16[256,256]{1,0:T(8,128)(2,1)S(1)} %collective-permute-done.refs_1_, bf16[256,256]{1,0:T(8,128)(2,1)S(1)} %collective-permute-done.1.refs_2_, ...), custom_call_target="tpu_custom_call" | custom-call | flops 536870912 | bytes 3407872 | tf_op jit(solution)/shard_map/forward_product/pallas_call | solution.py:241
  27.4 0.8 %collective-permute-done.8 = bf16[512,256]{1,0:T(8,128)(2,1)S(1)} collective-permute-done((bf16[512,256]{1,0:T(8,128)(2,1)S(1)}, bf16[512,256]{1,0:T(8,128)(2,1)S(1)}, u32[]{:S(2)}, u32[]{:S(2)}) %collective-permute-start.8) | collective-permute-done | bytes 262176 | tf_op jit(solution)/shard_map/ppermute | solution.py:469
  28.2 0.1 add_convert_fusion.refs_0_
  28.3 1.6 %collective-permute-start.9 = (bf16[512,256]{1,0:T(8,128)(2,1)S(1)}, bf16[512,256]{1,0:T(8,128)(2,1)S(1)}, u32[]{:S(2)}, u32[]{:S(2)}) collective-permute-start(bf16[512,256]{1,0:T(8,128)(2,1)S(1)} %add_convert_fusion.refs_0_), channel_id=1, source_target_pairs={{0,2},{1,3},{2,0},{3,1},{4,6},{5,7},{6,4},{7,5},{8,10},{9,11},{10,... | collective-permute-start | bytes 786440 | tf_op jit(solution)/shard_map/ppermute | solution.py:469
  29.8 6.8 %collective-permute-done.9.refs_1_ = bf16[512,256]{1,0:T(8,128)(2,1)S(1)} collective-permute-done((bf16[512,256]{1,0:T(8,128)(2,1)S(1)}, bf16[512,256]{1,0:T(8,128)(2,1)S(1)}, u32[]{:S(2)}, u32[]{:S(2)}) %collective-permute-start.9) | collective-permute-done | bytes 262176 | tf_op jit(solution)/shard_map/ppermute | solution.py:469
  36.7 0.0 copy-done.1
  36.7 1.0 %middle.1 = (bf16[256,256]{1,0:T(8,128)(2,1)}, bf16[768,256]{1,0:T(8,128)(2,1)S(1)}, f32[128,256]{1,0:T(8,128)S(1)}) custom-call(bf16[512,256]{1,0:T(8,128)(2,1)S(1)} %add_convert_fusion.refs_0_, bf16[512,256]{1,0:T(8,128)(2,1)S(1)} %collective-permute-done.9.refs_1_, bf16[256,256]{1,0:T(8,128)(2,1)S(1)} %copy-done.1, bf16[256,256]{1,0:T(8,128)(2,1)S(1)} %copy-done.2, ...), custom_call_target="tpu_custom_call" | custom-call | flops 335544320 | bytes 1572864 | tf_op jit(solution)/shard_map/middle/pallas_call | solution.py:305
  37.7 0.1 collective-permute-start.10
  37.8 1.7 %collective-permute-done.10.sibling_ref = bf16[768,256]{1,0:T(8,128)(2,1)S(1)} collective-permute-done((bf16[768,256]{1,0:T(8,128)(2,1)S(1)}, bf16[768,256]{1,0:T(8,128)(2,1)S(1)}, u32[]{:S(2)}, u32[]{:S(2)}) %collective-permute-start.10) | collective-permute-done | bytes 393248 | tf_op jit(solution)/shard_map/ppermute | solution.py:469
  39.5 0.5 backward_product.2
  40.0 0.4 collective-permute-start.15
  40.3 1.7 %collective-permute-start.11 = (bf16[256,256]{1,0:T(8,128)(2,1)S(1)}, bf16[256,256]{1,0:T(8,128)(2,1)S(1)}, u32[]{:S(2)}, u32[]{:S(2)}) collective-permute-start(bf16[256,256]{1,0:T(8,128)(2,1)S(1)} %get-tuple-element.55), channel_id=1, source_target_pairs={{0,8},{8,16},{16,24},{24,28},{28,20},{20,12},{12,4},{4,0},{1,9},{9... | collective-permute-start | bytes 393224 | tf_op jit(solution)/shard_map/ppermute | solution.py:465
  42.0 1.3 %backward_product.3 = (bf16[384,256]{1,0:T(8,128)(2,1)S(1)}, bf16[384,256]{1,0:T(8,128)(2,1)S(1)}, bf16[320,256]{1,0:T(8,128)(2,1)S(1)}, bf16[384,256]{1,0:T(8,1...) custom-call(bf16[1024,2048]{1,0:T(8,128)(2,1)S(1)} %build_rest.1.dense_ref, ...), custom_call_target="tpu_custom_call" | custom-call | flops 134217728 | bytes 917504 | tf_op jit(solution)/shard_map/backward_product/pallas_call | solution.py:366
  43.3 2.2 %collective-permute-done.15.refs_2_ = bf16[256,256]{1,0:T(8,128)(2,1)S(1)} collective-permute-done((bf16[256,256]{1,0:T(8,128)(2,1)S(1)}, bf16[256,256]{1,0:T(8,128)(2,1)S(1)}, u32[]{:S(2)}, u32[]{:S(2)}) %collective-permute-start.15) | collective-permute-done | bytes 131104 | tf_op jit(solution)/shard_map/ppermute | solution.py:465
  45.6 0.4 collective-permute-start.16
  46.0 0.0 collective-permute-done.11.refs_1_
  46.0 1.8 %collective-permute-start.12 = (bf16[384,256]{1,0:T(8,128)(2,1)S(1)}, bf16[384,256]{1,0:T(8,128)(2,1)S(1)}, u32[]{:S(2)}, u32[]{:S(2)}) collective-permute-start(bf16[384,256]{1,0:T(8,128)(2,1)S(1)} %add_convert_fusion.4), channel_id=1, source_target_pairs={{0,8},{8,16},{16,24},{24,28},{28,20},{20,12},{12,4},{4,0},{1,9},{9... | collective-permute-start | bytes 589832 | tf_op jit(solution)/shard_map/ppermute | solution.py:465
  47.8 4.0 %collective-permute-done.16.refs_4_ = bf16[384,256]{1,0:T(8,128)(2,1)S(1)} collective-permute-done((bf16[384,256]{1,0:T(8,128)(2,1)S(1)}, bf16[384,256]{1,0:T(8,128)(2,1)S(1)}, u32[]{:S(2)}, u32[]{:S(2)}) %collective-permute-start.16) | collective-permute-done | bytes 196640 | tf_op jit(solution)/shard_map/ppermute | solution.py:465
  51.8 0.1 add_convert_fusion.1
  51.8 0.4 collective-permute-start.17
  52.2 0.0 collective-permute-done.12.refs_3_
  52.2 0.1 add_convert_fusion.3
  52.2 1.8 %collective-permute-start.13 = (bf16[384,256]{1,0:T(8,128)(2,1)S(1)}, bf16[384,256]{1,0:T(8,128)(2,1)S(1)}, u32[]{:S(2)}, u32[]{:S(2)}) collective-permute-start(bf16[384,256]{1,0:T(8,128)(2,1)S(1)} %add_convert_fusion.3), channel_id=1, source_target_pairs={{0,8},{8,16},{16,24},{24,28},{28,20},{20,12},{12,4},{4,0},{1,9},{9... | collective-permute-start | bytes 589832 | tf_op jit(solution)/shard_map/ppermute | solution.py:465
  54.0 3.5 %collective-permute-done.17.refs_6_ = bf16[384,256]{1,0:T(8,128)(2,1)S(1)} collective-permute-done((bf16[384,256]{1,0:T(8,128)(2,1)S(1)}, bf16[384,256]{1,0:T(8,128)(2,1)S(1)}, u32[]{:S(2)}, u32[]{:S(2)}) %collective-permute-start.17) | collective-permute-done | bytes 196640 | tf_op jit(solution)/shard_map/ppermute | solution.py:465
  57.6 0.4 collective-permute-start.18
  58.0 0.2 collective-permute-done.13.refs_5_
  58.2 1.6 %collective-permute-start.14 = (bf16[320,256]{1,0:T(8,128)(2,1)S(1)}, bf16[320,256]{1,0:T(8,128)(2,1)S(1)}, u32[]{:S(2)}, u32[]{:S(2)}) collective-permute-start(bf16[320,256]{1,0:T(8,128)(2,1)S(1)} %add_convert_fusion.6), channel_id=1, source_target_pairs={{0,8},{8,16},{16,24},{24,28},{28,20},{20,12},{12,4},{4,0},{1,9},{9... | collective-permute-start | bytes 491528 | tf_op jit(solution)/shard_map/ppermute | solution.py:465
  59.8 3.2 %collective-permute-done.18.refs_2_.refs_8_ = bf16[320,256]{1,0:T(8,128)(2,1)S(1)} collective-permute-done((bf16[320,256]{1,0:T(8,128)(2,1)S(1)}, bf16[320,256]{1,0:T(8,128)(2,1)S(1)}, u32[]{:S(2)}, u32[]{:S(2)}) %collective-permute-start.18) | collective-permute-done | bytes 163872 | tf_op jit(solution)/shard_map/ppermute | solution.py:465
  63.0 0.6 collective-permute-done.14.refs_1_.refs_7_
  63.5 0.1 summed_terms.1.own_ref
  63.7 0.1 collective-permute-start.19
  63.8 0.8 %finish.1 = bf16[256,256]{1,0:T(8,128)(2,1)} custom-call(bf16[256,256]{1,0:T(8,128)(2,1)S(1)} %get-tuple-element.51.refs_0_, bf16[320,256]{1,0:T(8,128)(2,1)S(1)} %collective-permute-done.14.refs_1_.refs_7_, bf16[320,256]{1,0:T(8,128)(2,1)S(1)} %collective-permute-done.18.refs_2_.refs_8_), custom_call_target="tpu_custom_call" | custom-call | flops 196608 | bytes 524288 | tf_op jit(solution)/shard_map/finish/pallas_call | solution.py:429
  64.5 0.6 collective-permute-done.19.sibling_ref
  65.1 0.7 %joined.1 = f32[256,256]{1,0:T(8,128)} custom-call(f32[128,256]{1,0:T(8,128)S(1)} %summed_terms.1.own_ref, f32[128,256]{1,0:T(8,128)S(1)} %collective-permute-done.19.sibling_ref), custom_call_target="tpu_custom_call" | custom-call | bytes 524288 | tf_op jit(solution)/shard_map/joined/pallas_call | solution.py:451
  (4 shorter events, 0.2 us)
Async XLA Ops:
  0.6 6.8 %collective-permute-start.3 = (bf16[256,256]{1,0:T(8,128)(2,1)}, bf16[256,256]{1,0:T(8,128)(2,1)S(1)}, u32[]{:S(2)}, u32[]{:S(2)}) collective-permute-start(bf16[256,256]{1,0:T(8,128)(2,1)} %refs_0_.3), channel_id=1, source_target_pairs={{0,4},{8,0},{16,8},{24,16},{28,24},{20,28},{12,20},{4,12},{1,5},{9... | collective-permute-start | bytes 393224 | tf_op jit(solution)/shard_map/ppermute | solution.py:465
  3.6 5.5 %collective-permute-start = (bf16[256,256]{1,0:T(8,128)(2,1)}, bf16[256,256]{1,0:T(8,128)(2,1)S(1)}, u32[]{:S(2)}, u32[]{:S(2)}) collective-permute-start(bf16[256,256]{1,0:T(8,128)(2,1)} %refs_0_.3), channel_id=1, source_target_pairs={{0,8},{8,16},{16,24},{24,28},{28,20},{20,12},{12,4},{4,0},{1,9},{9... | collective-permute-start | bytes 393224 | tf_op jit(solution)/shard_map/ppermute | solution.py:465
  7.4 5.7 %collective-permute-start.4 = (bf16[256,256]{1,0:T(8,128)(2,1)S(1)}, bf16[256,256]{1,0:T(8,128)(2,1)S(1)}, u32[]{:S(2)}, u32[]{:S(2)}) collective-permute-start(bf16[256,256]{1,0:T(8,128)(2,1)S(1)} %collective-permute-done.3.refs_5_), channel_id=1, source_target_pairs={{0,4},{8,0},{16,8},{24,16},{28,24},{20,28},{12,20},{4,12},{1,5},{9... | collective-permute-start | bytes 393224 | tf_op jit(solution)/shard_map/ppermute | solution.py:465
  9.1 5.0 %collective-permute-start.1 = (bf16[256,256]{1,0:T(8,128)(2,1)S(1)}, bf16[256,256]{1,0:T(8,128)(2,1)S(1)}, u32[]{:S(2)}, u32[]{:S(2)}) collective-permute-start(bf16[256,256]{1,0:T(8,128)(2,1)S(1)} %collective-permute-done.refs_1_), channel_id=1, source_target_pairs={{0,8},{8,16},{16,24},{24,28},{28,20},{20,12},{12,4},{4,0},{1,9},{9... | collective-permute-start | bytes 393224 | tf_op jit(solution)/shard_map/ppermute | solution.py:465
  9.4 5.0 %copy-start.2 = (bf16[256,256]{1,0:T(8,128)(2,1)S(1)}, bf16[256,256]{1,0:T(8,128)(2,1)}, u32[]{:S(2)}) copy-start(bf16[256,256]{1,0:T(8,128)(2,1)} %refs_3_) | copy-start | bytes 393220
  13.1 12.7 %copy-start = (bf16[256,256]{1,0:T(8,128)(2,1)S(1)}, bf16[256,256]{1,0:T(8,128)(2,1)}, u32[]{:S(2)}) copy-start(bf16[256,256]{1,0:T(8,128)(2,1)} %refs_0_.3) | copy-start | bytes 393220
  14.1 5.6 %collective-permute-start.2 = (bf16[256,256]{1,0:T(8,128)(2,1)S(1)}, bf16[256,256]{1,0:T(8,128)(2,1)S(1)}, u32[]{:S(2)}, u32[]{:S(2)}) collective-permute-start(bf16[256,256]{1,0:T(8,128)(2,1)S(1)} %collective-permute-done.1.refs_2_), channel_id=1, source_target_pairs={{0,8},{8,16},{16,24},{24,28},{28,20},{20,12},{12,4},{4,0},{1,9},{9... | collective-permute-start | bytes 393224 | tf_op jit(solution)/shard_map/ppermute | solution.py:465
  14.4 5.2 %collective-permute-start.5 = (bf16[256,256]{1,0:T(8,128)(2,1)S(1)}, bf16[256,256]{1,0:T(8,128)(2,1)S(1)}, u32[]{:S(2)}, u32[]{:S(2)}) collective-permute-start(bf16[256,256]{1,0:T(8,128)(2,1)S(1)} %copy-done.2), channel_id=1, source_target_pairs={{0,2},{1,3},{2,0},{3,1},{4,6},{5,7},{6,4},{7,5},{8,10},{9,11},{10,... | collective-permute-start | bytes 393224 | tf_op jit(solution)/shard_map/ppermute | solution.py:469
  16.1 9.8 %collective-permute-start.7 = (bf16[256,256]{1,0:T(8,128)(2,1)S(1)}, bf16[256,256]{1,0:T(8,128)(2,1)S(1)}, u32[]{:S(2)}, u32[]{:S(2)}) collective-permute-start(bf16[256,256]{1,0:T(8,128)(2,1)S(1)} %collective-permute-done.4.refs_6_), channel_id=1, source_target_pairs={{0,4},{8,0},{16,8},{24,16},{28,24},{20,28},{12,20},{4,12},{1,5},{9... | collective-permute-start | bytes 393224 | tf_op jit(solution)/shard_map/ppermute | solution.py:465
  19.6 6.2 %collective-permute-start.6 = (bf16[256,256]{1,0:T(8,128)(2,1)S(1)}, bf16[256,256]{1,0:T(8,128)(2,1)S(1)}, u32[]{:S(2)}, u32[]{:S(2)}) collective-permute-start(bf16[256,256]{1,0:T(8,128)(2,1)S(1)} %collective-permute-done.2.refs_3_), channel_id=1, source_target_pairs={{0,8},{8,16},{16,24},{24,28},{28,20},{20,12},{12,4},{4,0},{1,9},{9... | collective-permute-start | bytes 393224 | tf_op jit(solution)/shard_map/ppermute | solution.py:465
  26.6 10.1 %copy-start.1 = (bf16[256,256]{1,0:T(8,128)(2,1)S(1)}, bf16[256,256]{1,0:T(8,128)(2,1)}, u32[]{:S(2)}) copy-start(bf16[256,256]{1,0:T(8,128)(2,1)} %refs_2_.1) | copy-start | bytes 393220
  26.6 1.6 %collective-permute-start.8 = (bf16[512,256]{1,0:T(8,128)(2,1)S(1)}, bf16[512,256]{1,0:T(8,128)(2,1)S(1)}, u32[]{:S(2)}, u32[]{:S(2)}) collective-permute-start(bf16[512,256]{1,0:T(8,128)(2,1)S(1)} %forward_product.2), channel_id=1, source_target_pairs={{0,1},{1,0},{2,3},{3,2},{4,5},{5,4},{6,7},{7,6},{8,9},{9,8},{10,11... | collective-permute-start | bytes 786440 | tf_op jit(solution)/shard_map/ppermute | solution.py:469
  28.3 8.4 %collective-permute-start.9 = (bf16[512,256]{1,0:T(8,128)(2,1)S(1)}, bf16[512,256]{1,0:T(8,128)(2,1)S(1)}, u32[]{:S(2)}, u32[]{:S(2)}) collective-permute-start(bf16[512,256]{1,0:T(8,128)(2,1)S(1)} %add_convert_fusion.refs_0_), channel_id=1, source_target_pairs={{0,2},{1,3},{2,0},{3,1},{4,6},{5,7},{6,4},{7,5},{8,10},{9,11},{10,... | collective-permute-start | bytes 786440 | tf_op jit(solution)/shard_map/ppermute | solution.py:469
  37.7 1.8 %collective-permute-start.10 = (bf16[768,256]{1,0:T(8,128)(2,1)S(1)}, bf16[768,256]{1,0:T(8,128)(2,1)S(1)}, u32[]{:S(2)}, u32[]{:S(2)}) collective-permute-start(bf16[768,256]{1,0:T(8,128)(2,1)S(1)} %get-tuple-element.45.own_ref), channel_id=1, source_target_pairs={{0,1},{1,0},{2,3},{3,2},{4,5},{5,4},{6,7},{7,6},{8,9},{9,8},{10,11... | collective-permute-start | bytes 1179656 | tf_op jit(solution)/shard_map/ppermute | solution.py:469
  40.0 5.6 %collective-permute-start.15 = (bf16[256,256]{1,0:T(8,128)(2,1)S(1)}, bf16[256,256]{1,0:T(8,128)(2,1)S(1)}, u32[]{:S(2)}, u32[]{:S(2)}) collective-permute-start(bf16[256,256]{1,0:T(8,128)(2,1)S(1)} %get-tuple-element.59), channel_id=1, source_target_pairs={{0,4},{8,0},{16,8},{24,16},{28,24},{20,28},{12,20},{4,12},{1,5},{9... | collective-permute-start | bytes 393224 | tf_op jit(solution)/shard_map/ppermute | solution.py:465
  40.3 5.6 %collective-permute-start.11 = (bf16[256,256]{1,0:T(8,128)(2,1)S(1)}, bf16[256,256]{1,0:T(8,128)(2,1)S(1)}, u32[]{:S(2)}, u32[]{:S(2)}) collective-permute-start(bf16[256,256]{1,0:T(8,128)(2,1)S(1)} %get-tuple-element.55), channel_id=1, source_target_pairs={{0,8},{8,16},{16,24},{24,28},{28,20},{20,12},{12,4},{4,0},{1,9},{9... | collective-permute-start | bytes 393224 | tf_op jit(solution)/shard_map/ppermute | solution.py:465
  45.6 6.2 %collective-permute-start.16 = (bf16[384,256]{1,0:T(8,128)(2,1)S(1)}, bf16[384,256]{1,0:T(8,128)(2,1)S(1)}, u32[]{:S(2)}, u32[]{:S(2)}) collective-permute-start(bf16[384,256]{1,0:T(8,128)(2,1)S(1)} %add_convert_fusion.2), channel_id=1, source_target_pairs={{0,4},{8,0},{16,8},{24,16},{28,24},{20,28},{12,20},{4,12},{1,5},{9... | collective-permute-start | bytes 589832 | tf_op jit(solution)/shard_map/ppermute | solution.py:465
  46.0 6.2 %collective-permute-start.12 = (bf16[384,256]{1,0:T(8,128)(2,1)S(1)}, bf16[384,256]{1,0:T(8,128)(2,1)S(1)}, u32[]{:S(2)}, u32[]{:S(2)}) collective-permute-start(bf16[384,256]{1,0:T(8,128)(2,1)S(1)} %add_convert_fusion.4), channel_id=1, source_target_pairs={{0,8},{8,16},{16,24},{24,28},{28,20},{20,12},{12,4},{4,0},{1,9},{9... | collective-permute-start | bytes 589832 | tf_op jit(solution)/shard_map/ppermute | solution.py:465
  51.8 5.7 %collective-permute-start.17 = (bf16[384,256]{1,0:T(8,128)(2,1)S(1)}, bf16[384,256]{1,0:T(8,128)(2,1)S(1)}, u32[]{:S(2)}, u32[]{:S(2)}) collective-permute-start(bf16[384,256]{1,0:T(8,128)(2,1)S(1)} %add_convert_fusion.1), channel_id=1, source_target_pairs={{0,4},{8,0},{16,8},{24,16},{28,24},{20,28},{12,20},{4,12},{1,5},{9... | collective-permute-start | bytes 589832 | tf_op jit(solution)/shard_map/ppermute | solution.py:465
  52.2 5.9 %collective-permute-start.13 = (bf16[384,256]{1,0:T(8,128)(2,1)S(1)}, bf16[384,256]{1,0:T(8,128)(2,1)S(1)}, u32[]{:S(2)}, u32[]{:S(2)}) collective-permute-start(bf16[384,256]{1,0:T(8,128)(2,1)S(1)} %add_convert_fusion.3), channel_id=1, source_target_pairs={{0,8},{8,16},{16,24},{24,28},{28,20},{20,12},{12,4},{4,0},{1,9},{9... | collective-permute-start | bytes 589832 | tf_op jit(solution)/shard_map/ppermute | solution.py:465
  57.6 5.4 %collective-permute-start.18 = (bf16[320,256]{1,0:T(8,128)(2,1)S(1)}, bf16[320,256]{1,0:T(8,128)(2,1)S(1)}, u32[]{:S(2)}, u32[]{:S(2)}) collective-permute-start(bf16[320,256]{1,0:T(8,128)(2,1)S(1)} %add_convert_fusion.5), channel_id=1, source_target_pairs={{0,4},{8,0},{16,8},{24,16},{28,24},{20,28},{12,20},{4,12},{1,5},{9... | collective-permute-start | bytes 491528 | tf_op jit(solution)/shard_map/ppermute | solution.py:465
  58.2 5.4 %collective-permute-start.14 = (bf16[320,256]{1,0:T(8,128)(2,1)S(1)}, bf16[320,256]{1,0:T(8,128)(2,1)S(1)}, u32[]{:S(2)}, u32[]{:S(2)}) collective-permute-start(bf16[320,256]{1,0:T(8,128)(2,1)S(1)} %add_convert_fusion.6), channel_id=1, source_target_pairs={{0,8},{8,16},{16,24},{24,28},{28,20},{20,12},{12,4},{4,0},{1,9},{9... | collective-permute-start | bytes 491528 | tf_op jit(solution)/shard_map/ppermute | solution.py:465
  63.7 1.4 %collective-permute-start.19 = (f32[128,256]{1,0:T(8,128)S(1)}, f32[128,256]{1,0:T(8,128)S(1)}, u32[]{:S(2)}, u32[]{:S(2)}) collective-permute-start(f32[128,256]{1,0:T(8,128)S(1)} %summed_terms.1.own_ref), channel_id=1, source_target_pairs={{0,1},{1,0},{2,3},{3,2},{4,5},{5,4},{6,7},{7,6},{8,9},{9,8},{10,11... | collective-permute-start | bytes 393224 | tf_op jit(solution)/shard_map/ppermute | solution.py:469

commit v14 on v13

--- a/solution.py
+++ b/solution.py
@@ -50,17 +50,20 @@
     def chunk_step(index, carry):
         fetch(index).wait()
         slot = lax.rem(index - begin, slots)
-        for lane in range(0, chunk_tiles, 2):
-            spots = [target(index * chunk_tiles + lane + turn) for turn in range(2)]
-            at = [
-                (pl.ds(pl.multiple_of(row * side, side), side), pl.ds(pl.multiple_of(col * side, side), side))
-                for row, col in spots
-            ]
-            first, second = total[at[0]], total[at[1]]
-            tiles = [held[slot, lane + turn].astype(jnp.float32) for turn in range(2)]
-            same = (spots[0][0] == spots[1][0]) & (spots[0][1] == spots[1][1])
-            total[at[0]] = first + tiles[0]
-            total[at[1]] = second + tiles[1] + jnp.where(same, tiles[0], 0.0)
+        spots = [target(index * chunk_tiles + lane) for lane in range(chunk_tiles)]
+        at = [
+            (pl.ds(pl.multiple_of(row * side, side), side), pl.ds(pl.multiple_of(col * side, side), side))
+            for row, col in spots
+        ]
+        current = total[at[0]]
+        for lane in range(chunk_tiles):
+            last = lane == chunk_tiles - 1
+            following = None if last else total[at[lane + 1]]
+            current = current + held[slot, lane].astype(jnp.float32)
+            total[at[lane]] = current
+            if not last:
+                same = (spots[lane][0] == spots[lane + 1][0]) & (spots[lane][1] == spots[lane + 1][1])
+                current = jnp.where(same, current, following)
 
         @pl.when(index + slots < end)
         def _():
@@ -506,7 +509,7 @@
 def scattered_sums(dense, own, sibling, chunk):
     row_count, col_count = lax.axis_size("row"), lax.axis_size("col")
     size, width = chunk.shape
-    half, half_size = width // 2, size // 2
+    half = width // 2
     reach = row_count // 2
     strip, terms, zeros = ("strip", 0, width), ("terms", 0, size), ("zeros", 0, size)
     first = (
@@ -519,19 +522,18 @@
     up, down = around(above, 1), around(below, -1)
     all_terms = [(0, 0, size, 0, terms)]
 
-    few_zeros = ("zeros", 0, half_size)
-    ups = tuple((offset, (zeros if offset > 1 else few_zeros, strip)) for offset in range(reach - 1, 0, -1))
-    downs = tuple((-offset, (strip, zeros if offset > 1 else few_zeros)) for offset in range(reach - 1, 0, -1))
+    ups = tuple((offset, (zeros, strip) if offset > 1 else (strip,)) for offset in range(reach - 1, 0, -1))
+    downs = tuple((-offset, (strip, zeros)) for offset in range(reach - 1, 0, -1))
     strips = backward_product(cell, own, sibling, chunk, ups + downs + ((0, (strip,)),), row_count, col_count)
     ups, downs, mine = strips[: reach - 1], strips[reach - 1 : -1], strips[-1]
     for step in range(1, reach):
         all_terms += [(-step, 0, size, 0, up), (step, down.shape[0] - size, size, 0, down)]
         if step == reach - 1:
-            up, down = up[half_size:], down[: width + half_size]
+            up = up[size:]
         up = around(added(ups[step - 1], up), 1)
         down = around(added(downs[step - 1], down, half if step == 1 else 0), -1)
-    all_terms += [(reach, 0, half_size, half_size, up), (reach, width, half_size, 0, down)]
-    return [(0, mine), (half_size, up), (0, down)], summed_terms(all_terms, size, row_count)
+    all_terms.append((reach, width, size, 0, down))
+    return [(0, mine), (0, up), (0, down)], summed_terms(all_terms, size, row_count)
 
 
 def per_device(features, weight, adj_tiles, tile_rows, tile_cols, tile_counts, out_grad):

time: 66 us -> 65.2 us (0.988)
  Pallas kernels: 14.2 us -> 10.9 us
  waiting for transfers between devices: 28.8 us -> 31.3 us
    ppermute x15, waiting for transfers between devices: 18.9 us -> 21.4 us  [around(): lax.ppermute(value, 'row', [(order[i], order[(i + step) % count]) for i i...]
    pallas_call x1, Pallas kernels: 4.7 us -> 2.41 us  [build_stages(): pl.pallas_call(functools.partial(build_rest_kernel, blocks=blocks), out_s...]
    pallas_call x1, Pallas kernels: 3.69 us -> 2.68 us  [build_stages(): pl.pallas_call(functools.partial(build_first_kernel, blocks=blocks), out_...]
  transfers between devices with their start and end apart: 20 -> 20, of which waited for: 13 -> 13; matrix products, arithmetic and copies ran while one was open for 1% -> 1% of each run, Pallas kernels for 17% -> 12%
where the time goes in v14:
time: 65.2 us; the launch traced here: 65.5 us
  waiting for transfers between devices  31.3 us (48%)
  starting transfers between devices  20.8 us (32%)
  Pallas kernels  10.9 us (17%)
  between operations  1.44 us (2%)
  other arithmetic  1.04 us (2%)
    ppermute x15, waiting for transfers between devices, around(): lax.ppermute(value, 'row', [(order[i], order[(i + step) % count]) for i i...  21.4 us
    ppermute x15, starting transfers between devices, around(): lax.ppermute(value, 'row', [(order[i], order[(i + step) % count]) for i i...  17.4 us
    ppermute x5, waiting for transfers between devices, swapped(): lax.ppermute(value, axis, [(i, i ^ partner) for i in range(lax.axis_size(...  9.92 us
    ppermute x5, starting transfers between devices, swapped(): lax.ppermute(value, axis, [(i, i ^ partner) for i in range(lax.axis_size(...  3.43 us
    pallas_call x1, Pallas kernels, build_stages(): pl.pallas_call(functools.partial(build_first_kernel, blocks=blocks), out_...  2.68 us
    pallas_call x1, Pallas kernels, build_stages(): pl.pallas_call(functools.partial(build_rest_kernel, blocks=blocks), out_s...  2.41 us
    pallas_call x2, Pallas kernels, backward_product(): pl.pallas_call(functools.partial(backward_kernel, outputs=outputs, row_co...  1.74 us
    pallas_call x2, Pallas kernels, forward_product(): pl.pallas_call(functools.partial(forward_kernel, pieces=pieces, sibling=s...  1.42 us
  transfers between devices with their start and end apart: 20, of which 13 were waited for; matrix products, arithmetic and copies ran while one was open for 1% of the time, Pallas kernels for 12%

profile of v14, /device:TPU:0, one launch (start us, length us, event | category | flops | bytes accessed | tf_op | source)
XLA Modules:
  0.0 65.5 jit_solution(8183844555864743456)
XLA Ops:
  0.6 3.0 %collective-permute-start.3 = (bf16[256,256]{1,0:T(8,128)(2,1)}, bf16[256,256]{1,0:T(8,128)(2,1)S(1)}, u32[]{:S(2)}, u32[]{:S(2)}) collective-permute-start(bf16[256,256]{1,0:T(8,128)(2,1)} %refs_0_.3), channel_id=1, source_target_pairs={{0,4},{8,0},{16,8},{24,16},{28,24},{20,28},{12,20},{4,12},{1,5},{9... | collective-permute-start | bytes 393224 | tf_op jit(solution)/shard_map/ppermute | solution.py:468
  3.6 0.1 collective-permute-start
  4.4 0.7 %add_reduce_fusion.list_ref = s32[513]{0:T(1024)S(1)} fusion(s32[1,1,1]{2,1,0:T(1,128)} %bitcast.2, s32[1,1,256]{2,1,0:T(1,128)} %param.11, s32[1,1,256]{2,1,0:T(1,128)} %param.10), kind=kLoop, calls=%fused_computation.7 | loop fusion | flops 1026 | bytes 4104 | tf_op jit(solution)/shard_map/concatenate | solution.py:543
  5.1 2.3 %collective-permute-done.3.refs_5_ = bf16[256,256]{1,0:T(8,128)(2,1)S(1)} collective-permute-done((bf16[256,256]{1,0:T(8,128)(2,1)}, bf16[256,256]{1,0:T(8,128)(2,1)S(1)}, u32[]{:S(2)}, u32[]{:S(2)}) %collective-permute-start.3) | collective-permute-done | bytes 131104 | tf_op jit(solution)/shard_map/ppermute | solution.py:468
  7.4 1.7 %collective-permute-start.4 = (bf16[256,256]{1,0:T(8,128)(2,1)S(1)}, bf16[256,256]{1,0:T(8,128)(2,1)S(1)}, u32[]{:S(2)}, u32[]{:S(2)}) collective-permute-start(bf16[256,256]{1,0:T(8,128)(2,1)S(1)} %collective-permute-done.3.refs_5_), channel_id=1, source_target_pairs={{0,4},{8,0},{16,8},{24,16},{28,24},{20,28},{12,20},{4,12},{1,5},{9... | collective-permute-start | bytes 393224 | tf_op jit(solution)/shard_map/ppermute | solution.py:468
  9.1 0.0 collective-permute-done.refs_1_
  9.1 0.3 collective-permute-start.1
  9.4 0.0 copy-start.2
  9.4 2.7 %build_first.1.half_ref = bf16[1024,2048]{1,0:T(8,128)(2,1)S(1)} custom-call(s32[513]{0:T(1024)S(1)} %add_reduce_fusion.list_ref, bf16[256,128,128]{2,1,0:T(8,128)(2,1)} %bitcast.3), custom_call_target="tpu_custom_call" | custom-call | flops 4194304 | bytes 6291456 | tf_op jit(solution)/shard_map/build_first/pallas_call | solution.py:182
  12.1 0.0 copy-start
  12.2 0.2 collective-permute-done.4.refs_6_
  12.4 1.7 %collective-permute-done.1.refs_2_ = bf16[256,256]{1,0:T(8,128)(2,1)S(1)} collective-permute-done((bf16[256,256]{1,0:T(8,128)(2,1)S(1)}, bf16[256,256]{1,0:T(8,128)(2,1)S(1)}, u32[]{:S(2)}, u32[]{:S(2)}) %collective-permute-start.1) | collective-permute-done | bytes 131104 | tf_op jit(solution)/shard_map/ppermute | solution.py:468
  14.1 0.3 collective-permute-start.2
  14.4 0.0 copy-done.2
  14.4 1.7 %collective-permute-start.5 = (bf16[256,256]{1,0:T(8,128)(2,1)S(1)}, bf16[256,256]{1,0:T(8,128)(2,1)S(1)}, u32[]{:S(2)}, u32[]{:S(2)}) collective-permute-start(bf16[256,256]{1,0:T(8,128)(2,1)S(1)} %copy-done.2), channel_id=1, source_target_pairs={{0,2},{1,3},{2,0},{3,1},{4,6},{5,7},{6,4},{7,5},{8,10},{9,11},{10,... | collective-permute-start | bytes 393224 | tf_op jit(solution)/shard_map/ppermute | solution.py:472
  16.1 1.5 %collective-permute-start.7 = (bf16[256,256]{1,0:T(8,128)(2,1)S(1)}, bf16[256,256]{1,0:T(8,128)(2,1)S(1)}, u32[]{:S(2)}, u32[]{:S(2)}) collective-permute-start(bf16[256,256]{1,0:T(8,128)(2,1)S(1)} %collective-permute-done.4.refs_6_), channel_id=1, source_target_pairs={{0,4},{8,0},{16,8},{24,16},{28,24},{20,28},{12,20},{4,12},{1,5},{9... | collective-permute-start | bytes 393224 | tf_op jit(solution)/shard_map/ppermute | solution.py:468
  17.6 2.0 %collective-permute-done.2.refs_3_ = bf16[256,256]{1,0:T(8,128)(2,1)S(1)} collective-permute-done((bf16[256,256]{1,0:T(8,128)(2,1)S(1)}, bf16[256,256]{1,0:T(8,128)(2,1)S(1)}, u32[]{:S(2)}, u32[]{:S(2)}) %collective-permute-start.2) | collective-permute-done | bytes 131104 | tf_op jit(solution)/shard_map/ppermute | solution.py:468
  19.6 0.0 collective-permute-done.5.refs_4_
  19.6 1.5 %collective-permute-start.6 = (bf16[256,256]{1,0:T(8,128)(2,1)S(1)}, bf16[256,256]{1,0:T(8,128)(2,1)S(1)}, u32[]{:S(2)}, u32[]{:S(2)}) collective-permute-start(bf16[256,256]{1,0:T(8,128)(2,1)S(1)} %collective-permute-done.2.refs_3_), channel_id=1, source_target_pairs={{0,8},{8,16},{16,24},{24,28},{28,20},{20,12},{12,4},{4,0},{1,9},{9... | collective-permute-start | bytes 393224 | tf_op jit(solution)/shard_map/ppermute | solution.py:468
  21.1 2.4 %build_rest.1.dense_ref = bf16[1024,2048]{1,0:T(8,128)(2,1)S(1)} custom-call(s32[513]{0:T(1024)S(1)} %add_reduce_fusion.list_ref, bf16[256,128,128]{2,1,0:T(8,128)(2,1)} %bitcast.4, bf16[1024,2048]{1,0:T(8,128)(2,1)S(1)} %build_first.1.half_ref), custom_call_target="tpu_custom_call" | custom-call | flops 4194304 | bytes 6291456 | tf_op jit(solution)/shard_map/build_rest/pallas_call | solution.py:192
  23.5 0.0 collective-permute-done.7.refs_7_
  23.6 1.0 %collective-permute-done.6.refs_4_ = bf16[256,256]{1,0:T(8,128)(2,1)S(1)} collective-permute-done((bf16[256,256]{1,0:T(8,128)(2,1)S(1)}, bf16[256,256]{1,0:T(8,128)(2,1)S(1)}, u32[]{:S(2)}, u32[]{:S(2)}) %collective-permute-start.6) | collective-permute-done | bytes 131104 | tf_op jit(solution)/shard_map/ppermute | solution.py:468
  24.6 0.0 copy-done
  24.6 0.7 %forward_product.2 = bf16[512,256]{1,0:T(8,128)(2,1)S(1)} custom-call(bf16[1024,2048]{1,0:T(8,128)(2,1)S(1)} %build_rest.1.dense_ref, bf16[256,256]{1,0:T(8,128)(2,1)S(1)} %copy-done, bf16[256,256]{1,0:T(8,128)(2,1)S(1)} %collective-permute-done.refs_1_, bf16[256,256]{1,0:T(8,128)(2,1)S(1)} %collective-permute-done.1.refs_2_, ...), custom_call_target="tpu_custom_call" | custom-call | flops 536870912 | bytes 3407872 | tf_op jit(solution)/shard_map/forward_product/pallas_call | solution.py:244
  25.3 0.0 copy-start.1
  25.3 0.1 collective-permute-start.8
  25.4 0.7 %forward_product.3 = bf16[512,256]{1,0:T(8,128)(2,1)S(1)} custom-call(bf16[1024,2048]{1,0:T(8,128)(2,1)S(1)} %build_rest.1.dense_ref, bf16[256,256]{1,0:T(8,128)(2,1)S(1)} %copy-done, bf16[256,256]{1,0:T(8,128)(2,1)S(1)} %collective-permute-done.refs_1_, bf16[256,256]{1,0:T(8,128)(2,1)S(1)} %collective-permute-done.1.refs_2_, ...), custom_call_target="tpu_custom_call" | custom-call | flops 536870912 | bytes 3407872 | tf_op jit(solution)/shard_map/forward_product/pallas_call | solution.py:244
  26.1 0.8 %collective-permute-done.8 = bf16[512,256]{1,0:T(8,128)(2,1)S(1)} collective-permute-done((bf16[512,256]{1,0:T(8,128)(2,1)S(1)}, bf16[512,256]{1,0:T(8,128)(2,1)S(1)}, u32[]{:S(2)}, u32[]{:S(2)}) %collective-permute-start.8) | collective-permute-done | bytes 262176 | tf_op jit(solution)/shard_map/ppermute | solution.py:472
  26.9 0.1 add_convert_fusion.refs_0_
  27.0 1.6 %collective-permute-start.9 = (bf16[512,256]{1,0:T(8,128)(2,1)S(1)}, bf16[512,256]{1,0:T(8,128)(2,1)S(1)}, u32[]{:S(2)}, u32[]{:S(2)}) collective-permute-start(bf16[512,256]{1,0:T(8,128)(2,1)S(1)} %add_convert_fusion.refs_0_), channel_id=1, source_target_pairs={{0,2},{1,3},{2,0},{3,1},{4,6},{5,7},{6,4},{7,5},{8,10},{9,11},{10,... | collective-permute-start | bytes 786440 | tf_op jit(solution)/shard_map/ppermute | solution.py:472
  28.5 6.8 %collective-permute-done.9.refs_1_ = bf16[512,256]{1,0:T(8,128)(2,1)S(1)} collective-permute-done((bf16[512,256]{1,0:T(8,128)(2,1)S(1)}, bf16[512,256]{1,0:T(8,128)(2,1)S(1)}, u32[]{:S(2)}, u32[]{:S(2)}) %collective-permute-start.9) | collective-permute-done | bytes 262176 | tf_op jit(solution)/shard_map/ppermute | solution.py:472
  35.4 0.0 copy-done.1
  35.4 1.0 %middle.1 = (bf16[256,256]{1,0:T(8,128)(2,1)}, bf16[768,256]{1,0:T(8,128)(2,1)S(1)}, f32[128,256]{1,0:T(8,128)S(1)}) custom-call(bf16[512,256]{1,0:T(8,128)(2,1)S(1)} %add_convert_fusion.refs_0_, bf16[512,256]{1,0:T(8,128)(2,1)S(1)} %collective-permute-done.9.refs_1_, bf16[256,256]{1,0:T(8,128)(2,1)S(1)} %copy-done.1, bf16[256,256]{1,0:T(8,128)(2,1)S(1)} %copy-done.2, ...), custom_call_target="tpu_custom_call" | custom-call | flops 335544320 | bytes 1572864 | tf_op jit(solution)/shard_map/middle/pallas_call | solution.py:308
  36.4 0.1 collective-permute-start.10
  36.5 1.7 %collective-permute-done.10.sibling_ref = bf16[768,256]{1,0:T(8,128)(2,1)S(1)} collective-permute-done((bf16[768,256]{1,0:T(8,128)(2,1)S(1)}, bf16[768,256]{1,0:T(8,128)(2,1)S(1)}, u32[]{:S(2)}, u32[]{:S(2)}) %collective-permute-start.10) | collective-permute-done | bytes 393248 | tf_op jit(solution)/shard_map/ppermute | solution.py:472
  38.2 0.5 backward_product.2
  38.7 1.8 %collective-permute-start.15 = (bf16[256,256]{1,0:T(8,128)(2,1)S(1)}, bf16[256,256]{1,0:T(8,128)(2,1)S(1)}, u32[]{:S(2)}, u32[]{:S(2)}) collective-permute-start(bf16[256,256]{1,0:T(8,128)(2,1)S(1)} %get-tuple-element.59), channel_id=1, source_target_pairs={{0,4},{8,0},{16,8},{24,16},{28,24},{20,28},{12,20},{4,12},{1,5},{9... | collective-permute-start | bytes 393224 | tf_op jit(solution)/shard_map/ppermute | solution.py:468
  40.5 0.3 collective-permute-start.11
  40.8 1.3 %backward_product.3 = (bf16[384,256]{1,0:T(8,128)(2,1)S(1)}, bf16[384,256]{1,0:T(8,128)(2,1)S(1)}, bf16[256,256]{1,0:T(8,128)(2,1)S(1)}, bf16[384,256]{1,0:T(8,1...) custom-call(bf16[1024,2048]{1,0:T(8,128)(2,1)S(1)} %build_rest.1.dense_ref, ...), custom_call_target="tpu_custom_call" | custom-call | flops 134217728 | bytes 917504 | tf_op jit(solution)/shard_map/backward_product/pallas_call | solution.py:369
  42.0 2.4 %collective-permute-done.15.refs_2_ = bf16[256,256]{1,0:T(8,128)(2,1)S(1)} collective-permute-done((bf16[256,256]{1,0:T(8,128)(2,1)S(1)}, bf16[256,256]{1,0:T(8,128)(2,1)S(1)}, u32[]{:S(2)}, u32[]{:S(2)}) %collective-permute-start.15) | collective-permute-done | bytes 131104 | tf_op jit(solution)/shard_map/ppermute | solution.py:468
  44.5 1.6 %collective-permute-start.16 = (bf16[384,256]{1,0:T(8,128)(2,1)S(1)}, bf16[384,256]{1,0:T(8,128)(2,1)S(1)}, u32[]{:S(2)}, u32[]{:S(2)}) collective-permute-start(bf16[384,256]{1,0:T(8,128)(2,1)S(1)} %add_convert_fusion.3), channel_id=1, source_target_pairs={{0,4},{8,0},{16,8},{24,16},{28,24},{20,28},{12,20},{4,12},{1,5},{9... | collective-permute-start | bytes 589832 | tf_op jit(solution)/shard_map/ppermute | solution.py:468
  46.1 0.0 collective-permute-done.11.refs_1_
  46.1 0.5 collective-permute-start.12
  46.7 4.2 %collective-permute-done.16.refs_4_ = bf16[384,256]{1,0:T(8,128)(2,1)S(1)} collective-permute-done((bf16[384,256]{1,0:T(8,128)(2,1)S(1)}, bf16[384,256]{1,0:T(8,128)(2,1)S(1)}, u32[]{:S(2)}, u32[]{:S(2)}) %collective-permute-start.16) | collective-permute-done | bytes 196640 | tf_op jit(solution)/shard_map/ppermute | solution.py:468
  50.9 0.1 add_convert_fusion.2
  50.9 1.4 %collective-permute-start.17 = (bf16[384,256]{1,0:T(8,128)(2,1)S(1)}, bf16[384,256]{1,0:T(8,128)(2,1)S(1)}, u32[]{:S(2)}, u32[]{:S(2)}) collective-permute-start(bf16[384,256]{1,0:T(8,128)(2,1)S(1)} %add_convert_fusion.2), channel_id=1, source_target_pairs={{0,4},{8,0},{16,8},{24,16},{28,24},{20,28},{12,20},{4,12},{1,5},{9... | collective-permute-start | bytes 589832 | tf_op jit(solution)/shard_map/ppermute | solution.py:468
  52.3 0.0 collective-permute-done.12.refs_3_
  52.3 0.1 add_convert_fusion.4
  52.4 1.1 %collective-permute-start.13 = (bf16[384,256]{1,0:T(8,128)(2,1)S(1)}, bf16[384,256]{1,0:T(8,128)(2,1)S(1)}, u32[]{:S(2)}, u32[]{:S(2)}) collective-permute-start(bf16[384,256]{1,0:T(8,128)(2,1)S(1)} %add_convert_fusion.4), channel_id=1, source_target_pairs={{0,8},{8,16},{16,24},{24,28},{28,20},{20,12},{12,4},{4,0},{1,9},{9... | collective-permute-start | bytes 589832 | tf_op jit(solution)/shard_map/ppermute | solution.py:468
  53.5 4.0 %collective-permute-done.17.refs_6_ = bf16[384,256]{1,0:T(8,128)(2,1)S(1)} collective-permute-done((bf16[384,256]{1,0:T(8,128)(2,1)S(1)}, bf16[384,256]{1,0:T(8,128)(2,1)S(1)}, u32[]{:S(2)}, u32[]{:S(2)}) %collective-permute-start.17) | collective-permute-done | bytes 196640 | tf_op jit(solution)/shard_map/ppermute | solution.py:468
  57.4 0.1 add_convert_fusion.1
  57.5 0.6 collective-permute-start.18
  58.1 0.0 collective-permute-done.13.refs_5_
  58.1 1.5 %collective-permute-start.14 = (bf16[256,256]{1,0:T(8,128)(2,1)S(1)}, bf16[256,256]{1,0:T(8,128)(2,1)S(1)}, u32[]{:S(2)}, u32[]{:S(2)}) collective-permute-start(bf16[256,256]{1,0:T(8,128)(2,1)S(1)} %add_convert_fusion.6), channel_id=1, source_target_pairs={{0,8},{8,16},{16,24},{24,28},{28,20},{20,12},{12,4},{4,0},{1,9},{9... | collective-permute-start | bytes 393224 | tf_op jit(solution)/shard_map/ppermute | solution.py:468
  59.7 3.5 %collective-permute-done.18.refs_2_.refs_7_ = bf16[384,256]{1,0:T(8,128)(2,1)S(1)} collective-permute-done((bf16[384,256]{1,0:T(8,128)(2,1)S(1)}, bf16[384,256]{1,0:T(8,128)(2,1)S(1)}, u32[]{:S(2)}, u32[]{:S(2)}) %collective-permute-start.18) | collective-permute-done | bytes 196640 | tf_op jit(solution)/shard_map/ppermute | solution.py:468
  63.2 0.1 summed_terms.1.own_ref
  63.4 0.1 collective-permute-start.19
  63.4 0.0 collective-permute-done.14.refs_1_
  63.4 0.8 %finish.1 = bf16[256,256]{1,0:T(8,128)(2,1)} custom-call(bf16[256,256]{1,0:T(8,128)(2,1)S(1)} %get-tuple-element.51.refs_0_, bf16[256,256]{1,0:T(8,128)(2,1)S(1)} %collective-permute-done.14.refs_1_, bf16[384,256]{1,0:T(8,128)(2,1)S(1)} %collective-permute-done.18.refs_2_.refs_7_), custom_call_target="tpu_custom_call" | custom-call | flops 196608 | bytes 524288 | tf_op jit(solution)/shard_map/finish/pallas_call | solution.py:432
  64.2 0.6 collective-permute-done.19.sibling_ref
  64.8 0.7 %joined.1 = f32[256,256]{1,0:T(8,128)} custom-call(f32[128,256]{1,0:T(8,128)S(1)} %summed_terms.1.own_ref, f32[128,256]{1,0:T(8,128)S(1)} %collective-permute-done.19.sibling_ref), custom_call_target="tpu_custom_call" | custom-call | bytes 524288 | tf_op jit(solution)/shard_map/joined/pallas_call | solution.py:454
  (3 shorter events, 0.1 us)
Async XLA Ops:
  0.6 6.8 %collective-permute-start.3 = (bf16[256,256]{1,0:T(8,128)(2,1)}, bf16[256,256]{1,0:T(8,128)(2,1)S(1)}, u32[]{:S(2)}, u32[]{:S(2)}) collective-permute-start(bf16[256,256]{1,0:T(8,128)(2,1)} %refs_0_.3), channel_id=1, source_target_pairs={{0,4},{8,0},{16,8},{24,16},{28,24},{20,28},{12,20},{4,12},{1,5},{9... | collective-permute-start | bytes 393224 | tf_op jit(solution)/shard_map/ppermute | solution.py:468
  3.6 5.5 %collective-permute-start = (bf16[256,256]{1,0:T(8,128)(2,1)}, bf16[256,256]{1,0:T(8,128)(2,1)S(1)}, u32[]{:S(2)}, u32[]{:S(2)}) collective-permute-start(bf16[256,256]{1,0:T(8,128)(2,1)} %refs_0_.3), channel_id=1, source_target_pairs={{0,8},{8,16},{16,24},{24,28},{28,20},{20,12},{12,4},{4,0},{1,9},{9... | collective-permute-start | bytes 393224 | tf_op jit(solution)/shard_map/ppermute | solution.py:468
  7.4 5.0 %collective-permute-start.4 = (bf16[256,256]{1,0:T(8,128)(2,1)S(1)}, bf16[256,256]{1,0:T(8,128)(2,1)S(1)}, u32[]{:S(2)}, u32[]{:S(2)}) collective-permute-start(bf16[256,256]{1,0:T(8,128)(2,1)S(1)} %collective-permute-done.3.refs_5_), channel_id=1, source_target_pairs={{0,4},{8,0},{16,8},{24,16},{28,24},{20,28},{12,20},{4,12},{1,5},{9... | collective-permute-start | bytes 393224 | tf_op jit(solution)/shard_map/ppermute | solution.py:468
  9.1 5.0 %collective-permute-start.1 = (bf16[256,256]{1,0:T(8,128)(2,1)S(1)}, bf16[256,256]{1,0:T(8,128)(2,1)S(1)}, u32[]{:S(2)}, u32[]{:S(2)}) collective-permute-start(bf16[256,256]{1,0:T(8,128)(2,1)S(1)} %collective-permute-done.refs_1_), channel_id=1, source_target_pairs={{0,8},{8,16},{16,24},{24,28},{28,20},{20,12},{12,4},{4,0},{1,9},{9... | collective-permute-start | bytes 393224 | tf_op jit(solution)/shard_map/ppermute | solution.py:468
  9.4 5.0 %copy-start.2 = (bf16[256,256]{1,0:T(8,128)(2,1)S(1)}, bf16[256,256]{1,0:T(8,128)(2,1)}, u32[]{:S(2)}) copy-start(bf16[256,256]{1,0:T(8,128)(2,1)} %refs_3_) | copy-start | bytes 393220
  12.1 12.4 %copy-start = (bf16[256,256]{1,0:T(8,128)(2,1)S(1)}, bf16[256,256]{1,0:T(8,128)(2,1)}, u32[]{:S(2)}) copy-start(bf16[256,256]{1,0:T(8,128)(2,1)} %refs_0_.3) | copy-start | bytes 393220
  14.1 5.5 %collective-permute-start.2 = (bf16[256,256]{1,0:T(8,128)(2,1)S(1)}, bf16[256,256]{1,0:T(8,128)(2,1)S(1)}, u32[]{:S(2)}, u32[]{:S(2)}) collective-permute-start(bf16[256,256]{1,0:T(8,128)(2,1)S(1)} %collective-permute-done.1.refs_2_), channel_id=1, source_target_pairs={{0,8},{8,16},{16,24},{24,28},{28,20},{20,12},{12,4},{4,0},{1,9},{9... | collective-permute-start | bytes 393224 | tf_op jit(solution)/shard_map/ppermute | solution.py:468
  14.4 5.2 %collective-permute-start.5 = (bf16[256,256]{1,0:T(8,128)(2,1)S(1)}, bf16[256,256]{1,0:T(8,128)(2,1)S(1)}, u32[]{:S(2)}, u32[]{:S(2)}) collective-permute-start(bf16[256,256]{1,0:T(8,128)(2,1)S(1)} %copy-done.2), channel_id=1, source_target_pairs={{0,2},{1,3},{2,0},{3,1},{4,6},{5,7},{6,4},{7,5},{8,10},{9,11},{10,... | collective-permute-start | bytes 393224 | tf_op jit(solution)/shard_map/ppermute | solution.py:472
  16.1 7.5 %collective-permute-start.7 = (bf16[256,256]{1,0:T(8,128)(2,1)S(1)}, bf16[256,256]{1,0:T(8,128)(2,1)S(1)}, u32[]{:S(2)}, u32[]{:S(2)}) collective-permute-start(bf16[256,256]{1,0:T(8,128)(2,1)S(1)} %collective-permute-done.4.refs_6_), channel_id=1, source_target_pairs={{0,4},{8,0},{16,8},{24,16},{28,24},{20,28},{12,20},{4,12},{1,5},{9... | collective-permute-start | bytes 393224 | tf_op jit(solution)/shard_map/ppermute | solution.py:468
  19.6 5.0 %collective-permute-start.6 = (bf16[256,256]{1,0:T(8,128)(2,1)S(1)}, bf16[256,256]{1,0:T(8,128)(2,1)S(1)}, u32[]{:S(2)}, u32[]{:S(2)}) collective-permute-start(bf16[256,256]{1,0:T(8,128)(2,1)S(1)} %collective-permute-done.2.refs_3_), channel_id=1, source_target_pairs={{0,8},{8,16},{16,24},{24,28},{28,20},{20,12},{12,4},{4,0},{1,9},{9... | collective-permute-start | bytes 393224 | tf_op jit(solution)/shard_map/ppermute | solution.py:468
  25.3 10.1 %copy-start.1 = (bf16[256,256]{1,0:T(8,128)(2,1)S(1)}, bf16[256,256]{1,0:T(8,128)(2,1)}, u32[]{:S(2)}) copy-start(bf16[256,256]{1,0:T(8,128)(2,1)} %refs_2_.1) | copy-start | bytes 393220
  25.3 1.6 %collective-permute-start.8 = (bf16[512,256]{1,0:T(8,128)(2,1)S(1)}, bf16[512,256]{1,0:T(8,128)(2,1)S(1)}, u32[]{:S(2)}, u32[]{:S(2)}) collective-permute-start(bf16[512,256]{1,0:T(8,128)(2,1)S(1)} %forward_product.2), channel_id=1, source_target_pairs={{0,1},{1,0},{2,3},{3,2},{4,5},{5,4},{6,7},{7,6},{8,9},{9,8},{10,11... | collective-permute-start | bytes 786440 | tf_op jit(solution)/shard_map/ppermute | solution.py:472
  27.0 8.4 %collective-permute-start.9 = (bf16[512,256]{1,0:T(8,128)(2,1)S(1)}, bf16[512,256]{1,0:T(8,128)(2,1)S(1)}, u32[]{:S(2)}, u32[]{:S(2)}) collective-permute-start(bf16[512,256]{1,0:T(8,128)(2,1)S(1)} %add_convert_fusion.refs_0_), channel_id=1, source_target_pairs={{0,2},{1,3},{2,0},{3,1},{4,6},{5,7},{6,4},{7,5},{8,10},{9,11},{10,... | collective-permute-start | bytes 786440 | tf_op jit(solution)/shard_map/ppermute | solution.py:472
  36.4 1.8 %collective-permute-start.10 = (bf16[768,256]{1,0:T(8,128)(2,1)S(1)}, bf16[768,256]{1,0:T(8,128)(2,1)S(1)}, u32[]{:S(2)}, u32[]{:S(2)}) collective-permute-start(bf16[768,256]{1,0:T(8,128)(2,1)S(1)} %get-tuple-element.45.own_ref), channel_id=1, source_target_pairs={{0,1},{1,0},{2,3},{3,2},{4,5},{5,4},{6,7},{7,6},{8,9},{9,8},{10,11... | collective-permute-start | bytes 1179656 | tf_op jit(solution)/shard_map/ppermute | solution.py:472
  38.7 5.8 %collective-permute-start.15 = (bf16[256,256]{1,0:T(8,128)(2,1)S(1)}, bf16[256,256]{1,0:T(8,128)(2,1)S(1)}, u32[]{:S(2)}, u32[]{:S(2)}) collective-permute-start(bf16[256,256]{1,0:T(8,128)(2,1)S(1)} %get-tuple-element.59), channel_id=1, source_target_pairs={{0,4},{8,0},{16,8},{24,16},{28,24},{20,28},{12,20},{4,12},{1,5},{9... | collective-permute-start | bytes 393224 | tf_op jit(solution)/shard_map/ppermute | solution.py:468
  40.5 5.6 %collective-permute-start.11 = (bf16[256,256]{1,0:T(8,128)(2,1)S(1)}, bf16[256,256]{1,0:T(8,128)(2,1)S(1)}, u32[]{:S(2)}, u32[]{:S(2)}) collective-permute-start(bf16[256,256]{1,0:T(8,128)(2,1)S(1)} %get-tuple-element.55), channel_id=1, source_target_pairs={{0,8},{8,16},{16,24},{24,28},{28,20},{20,12},{12,4},{4,0},{1,9},{9... | collective-permute-start | bytes 393224 | tf_op jit(solution)/shard_map/ppermute | solution.py:468
  44.5 6.4 %collective-permute-start.16 = (bf16[384,256]{1,0:T(8,128)(2,1)S(1)}, bf16[384,256]{1,0:T(8,128)(2,1)S(1)}, u32[]{:S(2)}, u32[]{:S(2)}) collective-permute-start(bf16[384,256]{1,0:T(8,128)(2,1)S(1)} %add_convert_fusion.3), channel_id=1, source_target_pairs={{0,4},{8,0},{16,8},{24,16},{28,24},{20,28},{12,20},{4,12},{1,5},{9... | collective-permute-start | bytes 589832 | tf_op jit(solution)/shard_map/ppermute | solution.py:468
  46.1 6.2 %collective-permute-start.12 = (bf16[384,256]{1,0:T(8,128)(2,1)S(1)}, bf16[384,256]{1,0:T(8,128)(2,1)S(1)}, u32[]{:S(2)}, u32[]{:S(2)}) collective-permute-start(bf16[384,256]{1,0:T(8,128)(2,1)S(1)} %add_convert_fusion.5), channel_id=1, source_target_pairs={{0,8},{8,16},{16,24},{24,28},{28,20},{20,12},{12,4},{4,0},{1,9},{9... | collective-permute-start | bytes 589832 | tf_op jit(solution)/shard_map/ppermute | solution.py:468
  50.9 6.5 %collective-permute-start.17 = (bf16[384,256]{1,0:T(8,128)(2,1)S(1)}, bf16[384,256]{1,0:T(8,128)(2,1)S(1)}, u32[]{:S(2)}, u32[]{:S(2)}) collective-permute-start(bf16[384,256]{1,0:T(8,128)(2,1)S(1)} %add_convert_fusion.2), channel_id=1, source_target_pairs={{0,4},{8,0},{16,8},{24,16},{28,24},{20,28},{12,20},{4,12},{1,5},{9... | collective-permute-start | bytes 589832 | tf_op jit(solution)/shard_map/ppermute | solution.py:468
  52.4 5.7 %collective-permute-start.13 = (bf16[384,256]{1,0:T(8,128)(2,1)S(1)}, bf16[384,256]{1,0:T(8,128)(2,1)S(1)}, u32[]{:S(2)}, u32[]{:S(2)}) collective-permute-start(bf16[384,256]{1,0:T(8,128)(2,1)S(1)} %add_convert_fusion.4), channel_id=1, source_target_pairs={{0,8},{8,16},{16,24},{24,28},{28,20},{20,12},{12,4},{4,0},{1,9},{9... | collective-permute-start | bytes 589832 | tf_op jit(solution)/shard_map/ppermute | solution.py:468
  57.5 5.7 %collective-permute-start.18 = (bf16[384,256]{1,0:T(8,128)(2,1)S(1)}, bf16[384,256]{1,0:T(8,128)(2,1)S(1)}, u32[]{:S(2)}, u32[]{:S(2)}) collective-permute-start(bf16[384,256]{1,0:T(8,128)(2,1)S(1)} %add_convert_fusion.1), channel_id=1, source_target_pairs={{0,4},{8,0},{16,8},{24,16},{28,24},{20,28},{12,20},{4,12},{1,5},{9... | collective-permute-start | bytes 589832 | tf_op jit(solution)/shard_map/ppermute | solution.py:468
  58.1 5.3 %collective-permute-start.14 = (bf16[256,256]{1,0:T(8,128)(2,1)S(1)}, bf16[256,256]{1,0:T(8,128)(2,1)S(1)}, u32[]{:S(2)}, u32[]{:S(2)}) collective-permute-start(bf16[256,256]{1,0:T(8,128)(2,1)S(1)} %add_convert_fusion.6), channel_id=1, source_target_pairs={{0,8},{8,16},{16,24},{24,28},{28,20},{20,12},{12,4},{4,0},{1,9},{9... | collective-permute-start | bytes 393224 | tf_op jit(solution)/shard_map/ppermute | solution.py:468
  63.4 1.4 %collective-permute-start.19 = (f32[128,256]{1,0:T(8,128)S(1)}, f32[128,256]{1,0:T(8,128)S(1)}, u32[]{:S(2)}, u32[]{:S(2)}) collective-permute-start(f32[128,256]{1,0:T(8,128)S(1)} %summed_terms.1.own_ref), channel_id=1, source_target_pairs={{0,1},{1,0},{2,3},{3,2},{4,5},{5,4},{6,7},{7,6},{8,9},{9,8},{10,11... | collective-permute-start | bytes 393224 | tf_op jit(solution)/shard_map/ppermute | solution.py:472

commit v15 on v14

--- a/solution.py
+++ b/solution.py
@@ -9,7 +9,7 @@
 from jax.sharding import PartitionSpec as P
 
 chunk_tiles = 16
-chunk_slots = 8
+chunk_slots = 16
 build_grant = 44
 strips_per_step = 8
 mib = 1024 * 1024
@@ -87,7 +87,7 @@
 
 
 def first_chunks(list_ref, tiles_ref):
-    return (live_chunks(list_ref, tiles_ref) * 3 + 7) // 8
+    return (live_chunks(list_ref, tiles_ref) * 7 + 15) // 16
 
 
 def build_first_kernel(list_ref, tiles_ref, dense_ref, total, held, sems, *, blocks):

time: 65.2 us -> 65.2 us (level); the launches traced: 65.5 us -> 64.5 us
  waiting for transfers between devices: 31.3 us -> 29.3 us
  Pallas kernels: 10.9 us -> 11.9 us
    ppermute x15, waiting for transfers between devices: 21.4 us -> 19.7 us  [around(): lax.ppermute(value, 'row', [(order[i], order[(i + step) % count]) for i i...]
  transfers between devices with their start and end apart: 20 -> 20, of which waited for: 13 -> 13; matrix products, arithmetic and copies ran while one was open for 1% -> 2% of each run, Pallas kernels for 12% -> 14%
where the time goes in v15:
time: 65.2 us; the launch traced here: 64.5 us
  waiting for transfers between devices  29.3 us (45%)
  starting transfers between devices  20.9 us (32%)
  Pallas kernels  11.9 us (18%)
  between operations  1.44 us (2%)
  other arithmetic  1.04 us (2%)
    ppermute x15, waiting for transfers between devices, around(): lax.ppermute(value, 'row', [(order[i], order[(i + step) % count]) for i i...  19.7 us
    ppermute x15, starting transfers between devices, around(): lax.ppermute(value, 'row', [(order[i], order[(i + step) % count]) for i i...  17.3 us
    ppermute x5, waiting for transfers between devices, swapped(): lax.ppermute(value, axis, [(i, i ^ partner) for i in range(lax.axis_size(...  9.56 us
    ppermute x5, starting transfers between devices, swapped(): lax.ppermute(value, axis, [(i, i ^ partner) for i in range(lax.axis_size(...  3.58 us
    pallas_call x1, Pallas kernels, build_stages(): pl.pallas_call(functools.partial(build_rest_kernel, blocks=blocks), out_s...  3.03 us
    pallas_call x1, Pallas kernels, build_stages(): pl.pallas_call(functools.partial(build_first_kernel, blocks=blocks), out_...  3.02 us
    pallas_call x2, Pallas kernels, backward_product(): pl.pallas_call(functools.partial(backward_kernel, outputs=outputs, row_co...  1.74 us
    pallas_call x2, Pallas kernels, forward_product(): pl.pallas_call(functools.partial(forward_kernel, pieces=pieces, sibling=s...  1.42 us
  transfers between devices with their start and end apart: 20, of which 13 were waited for; matrix products, arithmetic and copies ran while one was open for 2% of the time, Pallas kernels for 14%

profile of v15, /device:TPU:0, one launch (start us, length us, event | category | flops | bytes accessed | tf_op | source)
XLA Modules:
  0.0 64.5 jit_solution(17757859165449273192)
XLA Ops:
  0.6 3.0 %collective-permute-start.3 = (bf16[256,256]{1,0:T(8,128)(2,1)}, bf16[256,256]{1,0:T(8,128)(2,1)S(1)}, u32[]{:S(2)}, u32[]{:S(2)}) collective-permute-start(bf16[256,256]{1,0:T(8,128)(2,1)} %refs_0_.3), channel_id=1, source_target_pairs={{0,4},{8,0},{16,8},{24,16},{28,24},{20,28},{12,20},{4,12},{1,5},{9... | collective-permute-start | bytes 393224 | tf_op jit(solution)/shard_map/ppermute | solution.py:468
  3.6 0.1 collective-permute-start
  4.4 0.7 %add_reduce_fusion.list_ref = s32[513]{0:T(1024)S(1)} fusion(s32[1,1,1]{2,1,0:T(1,128)} %bitcast.2, s32[1,1,256]{2,1,0:T(1,128)} %param.11, s32[1,1,256]{2,1,0:T(1,128)} %param.10), kind=kLoop, calls=%fused_computation.7 | loop fusion | flops 1026 | bytes 4104 | tf_op jit(solution)/shard_map/concatenate | solution.py:543
  5.1 2.3 %collective-permute-done.3.refs_5_ = bf16[256,256]{1,0:T(8,128)(2,1)S(1)} collective-permute-done((bf16[256,256]{1,0:T(8,128)(2,1)}, bf16[256,256]{1,0:T(8,128)(2,1)S(1)}, u32[]{:S(2)}, u32[]{:S(2)}) %collective-permute-start.3) | collective-permute-done | bytes 131104 | tf_op jit(solution)/shard_map/ppermute | solution.py:468
  7.4 1.7 %collective-permute-start.4 = (bf16[256,256]{1,0:T(8,128)(2,1)S(1)}, bf16[256,256]{1,0:T(8,128)(2,1)S(1)}, u32[]{:S(2)}, u32[]{:S(2)}) collective-permute-start(bf16[256,256]{1,0:T(8,128)(2,1)S(1)} %collective-permute-done.3.refs_5_), channel_id=1, source_target_pairs={{0,4},{8,0},{16,8},{24,16},{28,24},{20,28},{12,20},{4,12},{1,5},{9... | collective-permute-start | bytes 393224 | tf_op jit(solution)/shard_map/ppermute | solution.py:468
  9.1 0.0 collective-permute-done.refs_1_
  9.1 0.3 collective-permute-start.1
  9.4 0.0 copy-start.2
  9.4 3.0 %build_first.1.half_ref = bf16[1024,2048]{1,0:T(8,128)(2,1)S(1)} custom-call(s32[513]{0:T(1024)S(1)} %add_reduce_fusion.list_ref, bf16[256,128,128]{2,1,0:T(8,128)(2,1)} %bitcast.3), custom_call_target="tpu_custom_call" | custom-call | flops 4194304 | bytes 6291456 | tf_op jit(solution)/shard_map/build_first/pallas_call | solution.py:182
  12.5 0.0 copy-start
  12.5 0.0 collective-permute-done.4.refs_6_
  12.5 1.6 %collective-permute-done.1.refs_2_ = bf16[256,256]{1,0:T(8,128)(2,1)S(1)} collective-permute-done((bf16[256,256]{1,0:T(8,128)(2,1)S(1)}, bf16[256,256]{1,0:T(8,128)(2,1)S(1)}, u32[]{:S(2)}, u32[]{:S(2)}) %collective-permute-start.1) | collective-permute-done | bytes 131104 | tf_op jit(solution)/shard_map/ppermute | solution.py:468
  14.1 0.3 collective-permute-start.2
  14.4 0.0 copy-done.2
  14.4 1.7 %collective-permute-start.5 = (bf16[256,256]{1,0:T(8,128)(2,1)S(1)}, bf16[256,256]{1,0:T(8,128)(2,1)S(1)}, u32[]{:S(2)}, u32[]{:S(2)}) collective-permute-start(bf16[256,256]{1,0:T(8,128)(2,1)S(1)} %copy-done.2), channel_id=1, source_target_pairs={{0,2},{1,3},{2,0},{3,1},{4,6},{5,7},{6,4},{7,5},{8,10},{9,11},{10,... | collective-permute-start | bytes 393224 | tf_op jit(solution)/shard_map/ppermute | solution.py:472
  16.1 1.5 %collective-permute-start.7 = (bf16[256,256]{1,0:T(8,128)(2,1)S(1)}, bf16[256,256]{1,0:T(8,128)(2,1)S(1)}, u32[]{:S(2)}, u32[]{:S(2)}) collective-permute-start(bf16[256,256]{1,0:T(8,128)(2,1)S(1)} %collective-permute-done.4.refs_6_), channel_id=1, source_target_pairs={{0,4},{8,0},{16,8},{24,16},{28,24},{20,28},{12,20},{4,12},{1,5},{9... | collective-permute-start | bytes 393224 | tf_op jit(solution)/shard_map/ppermute | solution.py:468
  17.6 1.4 %collective-permute-done.2.refs_3_ = bf16[256,256]{1,0:T(8,128)(2,1)S(1)} collective-permute-done((bf16[256,256]{1,0:T(8,128)(2,1)S(1)}, bf16[256,256]{1,0:T(8,128)(2,1)S(1)}, u32[]{:S(2)}, u32[]{:S(2)}) %collective-permute-start.2) | collective-permute-done | bytes 131104 | tf_op jit(solution)/shard_map/ppermute | solution.py:468
  19.0 0.3 collective-permute-done.5.refs_4_
  19.4 1.7 %collective-permute-start.6 = (bf16[256,256]{1,0:T(8,128)(2,1)S(1)}, bf16[256,256]{1,0:T(8,128)(2,1)S(1)}, u32[]{:S(2)}, u32[]{:S(2)}) collective-permute-start(bf16[256,256]{1,0:T(8,128)(2,1)S(1)} %collective-permute-done.2.refs_3_), channel_id=1, source_target_pairs={{0,8},{8,16},{16,24},{24,28},{28,20},{20,12},{12,4},{4,0},{1,9},{9... | collective-permute-start | bytes 393224 | tf_op jit(solution)/shard_map/ppermute | solution.py:468
  21.1 3.0 %build_rest.1.dense_ref = bf16[1024,2048]{1,0:T(8,128)(2,1)S(1)} custom-call(s32[513]{0:T(1024)S(1)} %add_reduce_fusion.list_ref, bf16[256,128,128]{2,1,0:T(8,128)(2,1)} %bitcast.4, bf16[1024,2048]{1,0:T(8,128)(2,1)S(1)} %build_first.1.half_ref), custom_call_target="tpu_custom_call" | custom-call | flops 4194304 | bytes 6291456 | tf_op jit(solution)/shard_map/build_rest/pallas_call | solution.py:192
  24.2 0.0 collective-permute-done.7.refs_7_
  24.2 0.2 collective-permute-done.6.refs_4_
  24.4 0.0 copy-done
  24.4 0.7 %forward_product.2 = bf16[512,256]{1,0:T(8,128)(2,1)S(1)} custom-call(bf16[1024,2048]{1,0:T(8,128)(2,1)S(1)} %build_rest.1.dense_ref, bf16[256,256]{1,0:T(8,128)(2,1)S(1)} %copy-done, bf16[256,256]{1,0:T(8,128)(2,1)S(1)} %collective-permute-done.refs_1_, bf16[256,256]{1,0:T(8,128)(2,1)S(1)} %collective-permute-done.1.refs_2_, ...), custom_call_target="tpu_custom_call" | custom-call | flops 536870912 | bytes 3407872 | tf_op jit(solution)/shard_map/forward_product/pallas_call | solution.py:244
  25.1 0.0 copy-start.1
  25.1 0.1 collective-permute-start.8
  25.2 0.7 %forward_product.3 = bf16[512,256]{1,0:T(8,128)(2,1)S(1)} custom-call(bf16[1024,2048]{1,0:T(8,128)(2,1)S(1)} %build_rest.1.dense_ref, bf16[256,256]{1,0:T(8,128)(2,1)S(1)} %copy-done, bf16[256,256]{1,0:T(8,128)(2,1)S(1)} %collective-permute-done.refs_1_, bf16[256,256]{1,0:T(8,128)(2,1)S(1)} %collective-permute-done.1.refs_2_, ...), custom_call_target="tpu_custom_call" | custom-call | flops 536870912 | bytes 3407872 | tf_op jit(solution)/shard_map/forward_product/pallas_call | solution.py:244
  25.9 0.8 %collective-permute-done.8 = bf16[512,256]{1,0:T(8,128)(2,1)S(1)} collective-permute-done((bf16[512,256]{1,0:T(8,128)(2,1)S(1)}, bf16[512,256]{1,0:T(8,128)(2,1)S(1)}, u32[]{:S(2)}, u32[]{:S(2)}) %collective-permute-start.8) | collective-permute-done | bytes 262176 | tf_op jit(solution)/shard_map/ppermute | solution.py:472
  26.7 0.1 add_convert_fusion.refs_0_
  26.8 1.7 %collective-permute-start.9 = (bf16[512,256]{1,0:T(8,128)(2,1)S(1)}, bf16[512,256]{1,0:T(8,128)(2,1)S(1)}, u32[]{:S(2)}, u32[]{:S(2)}) collective-permute-start(bf16[512,256]{1,0:T(8,128)(2,1)S(1)} %add_convert_fusion.refs_0_), channel_id=1, source_target_pairs={{0,2},{1,3},{2,0},{3,1},{4,6},{5,7},{6,4},{7,5},{8,10},{9,11},{10,... | collective-permute-start | bytes 786440 | tf_op jit(solution)/shard_map/ppermute | solution.py:472
  28.5 6.7 %collective-permute-done.9.refs_1_ = bf16[512,256]{1,0:T(8,128)(2,1)S(1)} collective-permute-done((bf16[512,256]{1,0:T(8,128)(2,1)S(1)}, bf16[512,256]{1,0:T(8,128)(2,1)S(1)}, u32[]{:S(2)}, u32[]{:S(2)}) %collective-permute-start.9) | collective-permute-done | bytes 262176 | tf_op jit(solution)/shard_map/ppermute | solution.py:472
  35.2 0.0 copy-done.1
  35.2 1.0 %middle.1 = (bf16[256,256]{1,0:T(8,128)(2,1)}, bf16[768,256]{1,0:T(8,128)(2,1)S(1)}, f32[128,256]{1,0:T(8,128)S(1)}) custom-call(bf16[512,256]{1,0:T(8,128)(2,1)S(1)} %add_convert_fusion.refs_0_, bf16[512,256]{1,0:T(8,128)(2,1)S(1)} %collective-permute-done.9.refs_1_, bf16[256,256]{1,0:T(8,128)(2,1)S(1)} %copy-done.1, bf16[256,256]{1,0:T(8,128)(2,1)S(1)} %copy-done.2, ...), custom_call_target="tpu_custom_call" | custom-call | flops 335544320 | bytes 1572864 | tf_op jit(solution)/shard_map/middle/pallas_call | solution.py:308
  36.2 0.1 collective-permute-start.10
  36.3 1.7 %collective-permute-done.10.sibling_ref = bf16[768,256]{1,0:T(8,128)(2,1)S(1)} collective-permute-done((bf16[768,256]{1,0:T(8,128)(2,1)S(1)}, bf16[768,256]{1,0:T(8,128)(2,1)S(1)}, u32[]{:S(2)}, u32[]{:S(2)}) %collective-permute-start.10) | collective-permute-done | bytes 393248 | tf_op jit(solution)/shard_map/ppermute | solution.py:472
  38.0 0.5 backward_product.2
  38.5 1.9 %collective-permute-start.15 = (bf16[256,256]{1,0:T(8,128)(2,1)S(1)}, bf16[256,256]{1,0:T(8,128)(2,1)S(1)}, u32[]{:S(2)}, u32[]{:S(2)}) collective-permute-start(bf16[256,256]{1,0:T(8,128)(2,1)S(1)} %get-tuple-element.59), channel_id=1, source_target_pairs={{0,4},{8,0},{16,8},{24,16},{28,24},{20,28},{12,20},{4,12},{1,5},{9... | collective-permute-start | bytes 393224 | tf_op jit(solution)/shard_map/ppermute | solution.py:468
  40.3 0.2 collective-permute-start.11
  40.5 1.3 %backward_product.3 = (bf16[384,256]{1,0:T(8,128)(2,1)S(1)}, bf16[384,256]{1,0:T(8,128)(2,1)S(1)}, bf16[256,256]{1,0:T(8,128)(2,1)S(1)}, bf16[384,256]{1,0:T(8,1...) custom-call(bf16[1024,2048]{1,0:T(8,128)(2,1)S(1)} %build_rest.1.dense_ref, ...), custom_call_target="tpu_custom_call" | custom-call | flops 134217728 | bytes 917504 | tf_op jit(solution)/shard_map/backward_product/pallas_call | solution.py:369
  41.8 2.2 %collective-permute-done.15.refs_2_ = bf16[256,256]{1,0:T(8,128)(2,1)S(1)} collective-permute-done((bf16[256,256]{1,0:T(8,128)(2,1)S(1)}, bf16[256,256]{1,0:T(8,128)(2,1)S(1)}, u32[]{:S(2)}, u32[]{:S(2)}) %collective-permute-start.15) | collective-permute-done | bytes 131104 | tf_op jit(solution)/shard_map/ppermute | solution.py:468
  44.1 1.8 %collective-permute-start.16 = (bf16[384,256]{1,0:T(8,128)(2,1)S(1)}, bf16[384,256]{1,0:T(8,128)(2,1)S(1)}, u32[]{:S(2)}, u32[]{:S(2)}) collective-permute-start(bf16[384,256]{1,0:T(8,128)(2,1)S(1)} %add_convert_fusion.3), channel_id=1, source_target_pairs={{0,4},{8,0},{16,8},{24,16},{28,24},{20,28},{12,20},{4,12},{1,5},{9... | collective-permute-start | bytes 589832 | tf_op jit(solution)/shard_map/ppermute | solution.py:468
  46.0 0.0 collective-permute-done.11.refs_1_
  46.0 0.3 collective-permute-start.12
  46.3 4.2 %collective-permute-done.16.refs_4_ = bf16[384,256]{1,0:T(8,128)(2,1)S(1)} collective-permute-done((bf16[384,256]{1,0:T(8,128)(2,1)S(1)}, bf16[384,256]{1,0:T(8,128)(2,1)S(1)}, u32[]{:S(2)}, u32[]{:S(2)}) %collective-permute-start.16) | collective-permute-done | bytes 196640 | tf_op jit(solution)/shard_map/ppermute | solution.py:468
  50.5 0.1 add_convert_fusion.2
  50.5 1.6 %collective-permute-start.17 = (bf16[384,256]{1,0:T(8,128)(2,1)S(1)}, bf16[384,256]{1,0:T(8,128)(2,1)S(1)}, u32[]{:S(2)}, u32[]{:S(2)}) collective-permute-start(bf16[384,256]{1,0:T(8,128)(2,1)S(1)} %add_convert_fusion.2), channel_id=1, source_target_pairs={{0,4},{8,0},{16,8},{24,16},{28,24},{20,28},{12,20},{4,12},{1,5},{9... | collective-permute-start | bytes 589832 | tf_op jit(solution)/shard_map/ppermute | solution.py:468
  52.2 0.0 collective-permute-done.12.refs_3_
  52.2 0.1 add_convert_fusion.4
  52.2 0.5 collective-permute-start.13
  52.7 3.5 %collective-permute-done.17.refs_6_ = bf16[384,256]{1,0:T(8,128)(2,1)S(1)} collective-permute-done((bf16[384,256]{1,0:T(8,128)(2,1)S(1)}, bf16[384,256]{1,0:T(8,128)(2,1)S(1)}, u32[]{:S(2)}, u32[]{:S(2)}) %collective-permute-start.17) | collective-permute-done | bytes 196640 | tf_op jit(solution)/shard_map/ppermute | solution.py:468
  56.3 0.1 add_convert_fusion.1
  56.3 1.6 %collective-permute-start.18 = (bf16[384,256]{1,0:T(8,128)(2,1)S(1)}, bf16[384,256]{1,0:T(8,128)(2,1)S(1)}, u32[]{:S(2)}, u32[]{:S(2)}) collective-permute-start(bf16[384,256]{1,0:T(8,128)(2,1)S(1)} %add_convert_fusion.1), channel_id=1, source_target_pairs={{0,4},{8,0},{16,8},{24,16},{28,24},{20,28},{12,20},{4,12},{1,5},{9... | collective-permute-start | bytes 589832 | tf_op jit(solution)/shard_map/ppermute | solution.py:468
  58.0 0.0 collective-permute-done.13.refs_5_
  58.0 0.6 collective-permute-start.14
  58.6 3.5 %collective-permute-done.18.refs_2_.refs_7_ = bf16[384,256]{1,0:T(8,128)(2,1)S(1)} collective-permute-done((bf16[384,256]{1,0:T(8,128)(2,1)S(1)}, bf16[384,256]{1,0:T(8,128)(2,1)S(1)}, u32[]{:S(2)}, u32[]{:S(2)}) %collective-permute-start.18) | collective-permute-done | bytes 196640 | tf_op jit(solution)/shard_map/ppermute | solution.py:468
  62.0 0.1 summed_terms.1.own_ref
  62.2 0.1 collective-permute-start.19
  62.3 0.8 %collective-permute-done.14.refs_1_ = bf16[256,256]{1,0:T(8,128)(2,1)S(1)} collective-permute-done((bf16[256,256]{1,0:T(8,128)(2,1)S(1)}, bf16[256,256]{1,0:T(8,128)(2,1)S(1)}, u32[]{:S(2)}, u32[]{:S(2)}) %collective-permute-start.14) | collective-permute-done | bytes 131104 | tf_op jit(solution)/shard_map/ppermute | solution.py:468
  63.0 0.8 %finish.1 = bf16[256,256]{1,0:T(8,128)(2,1)} custom-call(bf16[256,256]{1,0:T(8,128)(2,1)S(1)} %get-tuple-element.51.refs_0_, bf16[256,256]{1,0:T(8,128)(2,1)S(1)} %collective-permute-done.14.refs_1_, bf16[384,256]{1,0:T(8,128)(2,1)S(1)} %collective-permute-done.18.refs_2_.refs_7_), custom_call_target="tpu_custom_call" | custom-call | flops 196608 | bytes 524288 | tf_op jit(solution)/shard_map/finish/pallas_call | solution.py:432
  63.8 0.0 collective-permute-done.19.sibling_ref
  63.8 0.7 %joined.1 = f32[256,256]{1,0:T(8,128)} custom-call(f32[128,256]{1,0:T(8,128)S(1)} %summed_terms.1.own_ref, f32[128,256]{1,0:T(8,128)S(1)} %collective-permute-done.19.sibling_ref), custom_call_target="tpu_custom_call" | custom-call | bytes 524288 | tf_op jit(solution)/shard_map/joined/pallas_call | solution.py:454
  (3 shorter events, 0.1 us)
Async XLA Ops:
  0.6 6.8 %collective-permute-start.3 = (bf16[256,256]{1,0:T(8,128)(2,1)}, bf16[256,256]{1,0:T(8,128)(2,1)S(1)}, u32[]{:S(2)}, u32[]{:S(2)}) collective-permute-start(bf16[256,256]{1,0:T(8,128)(2,1)} %refs_0_.3), channel_id=1, source_target_pairs={{0,4},{8,0},{16,8},{24,16},{28,24},{20,28},{12,20},{4,12},{1,5},{9... | collective-permute-start | bytes 393224 | tf_op jit(solution)/shard_map/ppermute | solution.py:468
  3.6 5.5 %collective-permute-start = (bf16[256,256]{1,0:T(8,128)(2,1)}, bf16[256,256]{1,0:T(8,128)(2,1)S(1)}, u32[]{:S(2)}, u32[]{:S(2)}) collective-permute-start(bf16[256,256]{1,0:T(8,128)(2,1)} %refs_0_.3), channel_id=1, source_target_pairs={{0,8},{8,16},{16,24},{24,28},{28,20},{20,12},{12,4},{4,0},{1,9},{9... | collective-permute-start | bytes 393224 | tf_op jit(solution)/shard_map/ppermute | solution.py:468
  7.4 5.1 %collective-permute-start.4 = (bf16[256,256]{1,0:T(8,128)(2,1)S(1)}, bf16[256,256]{1,0:T(8,128)(2,1)S(1)}, u32[]{:S(2)}, u32[]{:S(2)}) collective-permute-start(bf16[256,256]{1,0:T(8,128)(2,1)S(1)} %collective-permute-done.3.refs_5_), channel_id=1, source_target_pairs={{0,4},{8,0},{16,8},{24,16},{28,24},{20,28},{12,20},{4,12},{1,5},{9... | collective-permute-start | bytes 393224 | tf_op jit(solution)/shard_map/ppermute | solution.py:468
  9.1 5.0 %collective-permute-start.1 = (bf16[256,256]{1,0:T(8,128)(2,1)S(1)}, bf16[256,256]{1,0:T(8,128)(2,1)S(1)}, u32[]{:S(2)}, u32[]{:S(2)}) collective-permute-start(bf16[256,256]{1,0:T(8,128)(2,1)S(1)} %collective-permute-done.refs_1_), channel_id=1, source_target_pairs={{0,8},{8,16},{16,24},{24,28},{28,20},{20,12},{12,4},{4,0},{1,9},{9... | collective-permute-start | bytes 393224 | tf_op jit(solution)/shard_map/ppermute | solution.py:468
  9.4 5.0 %copy-start.2 = (bf16[256,256]{1,0:T(8,128)(2,1)S(1)}, bf16[256,256]{1,0:T(8,128)(2,1)}, u32[]{:S(2)}) copy-start(bf16[256,256]{1,0:T(8,128)(2,1)} %refs_3_) | copy-start | bytes 393220
  12.5 11.9 %copy-start = (bf16[256,256]{1,0:T(8,128)(2,1)S(1)}, bf16[256,256]{1,0:T(8,128)(2,1)}, u32[]{:S(2)}) copy-start(bf16[256,256]{1,0:T(8,128)(2,1)} %refs_0_.3) | copy-start | bytes 393220
  14.1 5.0 %collective-permute-start.2 = (bf16[256,256]{1,0:T(8,128)(2,1)S(1)}, bf16[256,256]{1,0:T(8,128)(2,1)S(1)}, u32[]{:S(2)}, u32[]{:S(2)}) collective-permute-start(bf16[256,256]{1,0:T(8,128)(2,1)S(1)} %collective-permute-done.1.refs_2_), channel_id=1, source_target_pairs={{0,8},{8,16},{16,24},{24,28},{28,20},{20,12},{12,4},{4,0},{1,9},{9... | collective-permute-start | bytes 393224 | tf_op jit(solution)/shard_map/ppermute | solution.py:468
  14.4 5.0 %collective-permute-start.5 = (bf16[256,256]{1,0:T(8,128)(2,1)S(1)}, bf16[256,256]{1,0:T(8,128)(2,1)S(1)}, u32[]{:S(2)}, u32[]{:S(2)}) collective-permute-start(bf16[256,256]{1,0:T(8,128)(2,1)S(1)} %copy-done.2), channel_id=1, source_target_pairs={{0,2},{1,3},{2,0},{3,1},{4,6},{5,7},{6,4},{7,5},{8,10},{9,11},{10,... | collective-permute-start | bytes 393224 | tf_op jit(solution)/shard_map/ppermute | solution.py:472
  16.1 8.1 %collective-permute-start.7 = (bf16[256,256]{1,0:T(8,128)(2,1)S(1)}, bf16[256,256]{1,0:T(8,128)(2,1)S(1)}, u32[]{:S(2)}, u32[]{:S(2)}) collective-permute-start(bf16[256,256]{1,0:T(8,128)(2,1)S(1)} %collective-permute-done.4.refs_6_), channel_id=1, source_target_pairs={{0,4},{8,0},{16,8},{24,16},{28,24},{20,28},{12,20},{4,12},{1,5},{9... | collective-permute-start | bytes 393224 | tf_op jit(solution)/shard_map/ppermute | solution.py:468
  19.4 5.0 %collective-permute-start.6 = (bf16[256,256]{1,0:T(8,128)(2,1)S(1)}, bf16[256,256]{1,0:T(8,128)(2,1)S(1)}, u32[]{:S(2)}, u32[]{:S(2)}) collective-permute-start(bf16[256,256]{1,0:T(8,128)(2,1)S(1)} %collective-permute-done.2.refs_3_), channel_id=1, source_target_pairs={{0,8},{8,16},{16,24},{24,28},{28,20},{20,12},{12,4},{4,0},{1,9},{9... | collective-permute-start | bytes 393224 | tf_op jit(solution)/shard_map/ppermute | solution.py:468
  25.1 10.1 %copy-start.1 = (bf16[256,256]{1,0:T(8,128)(2,1)S(1)}, bf16[256,256]{1,0:T(8,128)(2,1)}, u32[]{:S(2)}) copy-start(bf16[256,256]{1,0:T(8,128)(2,1)} %refs_2_.1) | copy-start | bytes 393220
  25.1 1.6 %collective-permute-start.8 = (bf16[512,256]{1,0:T(8,128)(2,1)S(1)}, bf16[512,256]{1,0:T(8,128)(2,1)S(1)}, u32[]{:S(2)}, u32[]{:S(2)}) collective-permute-start(bf16[512,256]{1,0:T(8,128)(2,1)S(1)} %forward_product.2), channel_id=1, source_target_pairs={{0,1},{1,0},{2,3},{3,2},{4,5},{5,4},{6,7},{7,6},{8,9},{9,8},{10,11... | collective-permute-start | bytes 786440 | tf_op jit(solution)/shard_map/ppermute | solution.py:472
  26.8 8.4 %collective-permute-start.9 = (bf16[512,256]{1,0:T(8,128)(2,1)S(1)}, bf16[512,256]{1,0:T(8,128)(2,1)S(1)}, u32[]{:S(2)}, u32[]{:S(2)}) collective-permute-start(bf16[512,256]{1,0:T(8,128)(2,1)S(1)} %add_convert_fusion.refs_0_), channel_id=1, source_target_pairs={{0,2},{1,3},{2,0},{3,1},{4,6},{5,7},{6,4},{7,5},{8,10},{9,11},{10,... | collective-permute-start | bytes 786440 | tf_op jit(solution)/shard_map/ppermute | solution.py:472
  36.2 1.8 %collective-permute-start.10 = (bf16[768,256]{1,0:T(8,128)(2,1)S(1)}, bf16[768,256]{1,0:T(8,128)(2,1)S(1)}, u32[]{:S(2)}, u32[]{:S(2)}) collective-permute-start(bf16[768,256]{1,0:T(8,128)(2,1)S(1)} %get-tuple-element.45.own_ref), channel_id=1, source_target_pairs={{0,1},{1,0},{2,3},{3,2},{4,5},{5,4},{6,7},{7,6},{8,9},{9,8},{10,11... | collective-permute-start | bytes 1179656 | tf_op jit(solution)/shard_map/ppermute | solution.py:472
  38.5 5.6 %collective-permute-start.15 = (bf16[256,256]{1,0:T(8,128)(2,1)S(1)}, bf16[256,256]{1,0:T(8,128)(2,1)S(1)}, u32[]{:S(2)}, u32[]{:S(2)}) collective-permute-start(bf16[256,256]{1,0:T(8,128)(2,1)S(1)} %get-tuple-element.59), channel_id=1, source_target_pairs={{0,4},{8,0},{16,8},{24,16},{28,24},{20,28},{12,20},{4,12},{1,5},{9... | collective-permute-start | bytes 393224 | tf_op jit(solution)/shard_map/ppermute | solution.py:468
  40.3 5.6 %collective-permute-start.11 = (bf16[256,256]{1,0:T(8,128)(2,1)S(1)}, bf16[256,256]{1,0:T(8,128)(2,1)S(1)}, u32[]{:S(2)}, u32[]{:S(2)}) collective-permute-start(bf16[256,256]{1,0:T(8,128)(2,1)S(1)} %get-tuple-element.55), channel_id=1, source_target_pairs={{0,8},{8,16},{16,24},{24,28},{28,20},{20,12},{12,4},{4,0},{1,9},{9... | collective-permute-start | bytes 393224 | tf_op jit(solution)/shard_map/ppermute | solution.py:468
  44.1 6.4 %collective-permute-start.16 = (bf16[384,256]{1,0:T(8,128)(2,1)S(1)}, bf16[384,256]{1,0:T(8,128)(2,1)S(1)}, u32[]{:S(2)}, u32[]{:S(2)}) collective-permute-start(bf16[384,256]{1,0:T(8,128)(2,1)S(1)} %add_convert_fusion.3), channel_id=1, source_target_pairs={{0,4},{8,0},{16,8},{24,16},{28,24},{20,28},{12,20},{4,12},{1,5},{9... | collective-permute-start | bytes 589832 | tf_op jit(solution)/shard_map/ppermute | solution.py:468
  46.0 6.2 %collective-permute-start.12 = (bf16[384,256]{1,0:T(8,128)(2,1)S(1)}, bf16[384,256]{1,0:T(8,128)(2,1)S(1)}, u32[]{:S(2)}, u32[]{:S(2)}) collective-permute-start(bf16[384,256]{1,0:T(8,128)(2,1)S(1)} %add_convert_fusion.5), channel_id=1, source_target_pairs={{0,8},{8,16},{16,24},{24,28},{28,20},{20,12},{12,4},{4,0},{1,9},{9... | collective-permute-start | bytes 589832 | tf_op jit(solution)/shard_map/ppermute | solution.py:468
  50.5 5.7 %collective-permute-start.17 = (bf16[384,256]{1,0:T(8,128)(2,1)S(1)}, bf16[384,256]{1,0:T(8,128)(2,1)S(1)}, u32[]{:S(2)}, u32[]{:S(2)}) collective-permute-start(bf16[384,256]{1,0:T(8,128)(2,1)S(1)} %add_convert_fusion.2), channel_id=1, source_target_pairs={{0,4},{8,0},{16,8},{24,16},{28,24},{20,28},{12,20},{4,12},{1,5},{9... | collective-permute-start | bytes 589832 | tf_op jit(solution)/shard_map/ppermute | solution.py:468
  52.2 5.7 %collective-permute-start.13 = (bf16[384,256]{1,0:T(8,128)(2,1)S(1)}, bf16[384,256]{1,0:T(8,128)(2,1)S(1)}, u32[]{:S(2)}, u32[]{:S(2)}) collective-permute-start(bf16[384,256]{1,0:T(8,128)(2,1)S(1)} %add_convert_fusion.4), channel_id=1, source_target_pairs={{0,8},{8,16},{16,24},{24,28},{28,20},{20,12},{12,4},{4,0},{1,9},{9... | collective-permute-start | bytes 589832 | tf_op jit(solution)/shard_map/ppermute | solution.py:468
  56.3 5.7 %collective-permute-start.18 = (bf16[384,256]{1,0:T(8,128)(2,1)S(1)}, bf16[384,256]{1,0:T(8,128)(2,1)S(1)}, u32[]{:S(2)}, u32[]{:S(2)}) collective-permute-start(bf16[384,256]{1,0:T(8,128)(2,1)S(1)} %add_convert_fusion.1), channel_id=1, source_target_pairs={{0,4},{8,0},{16,8},{24,16},{28,24},{20,28},{12,20},{4,12},{1,5},{9... | collective-permute-start | bytes 589832 | tf_op jit(solution)/shard_map/ppermute | solution.py:468
  58.0 5.0 %collective-permute-start.14 = (bf16[256,256]{1,0:T(8,128)(2,1)S(1)}, bf16[256,256]{1,0:T(8,128)(2,1)S(1)}, u32[]{:S(2)}, u32[]{:S(2)}) collective-permute-start(bf16[256,256]{1,0:T(8,128)(2,1)S(1)} %add_convert_fusion.6), channel_id=1, source_target_pairs={{0,8},{8,16},{16,24},{24,28},{28,20},{20,12},{12,4},{4,0},{1,9},{9... | collective-permute-start | bytes 393224 | tf_op jit(solution)/shard_map/ppermute | solution.py:468
  62.2 1.6 %collective-permute-start.19 = (f32[128,256]{1,0:T(8,128)S(1)}, f32[128,256]{1,0:T(8,128)S(1)}, u32[]{:S(2)}, u32[]{:S(2)}) collective-permute-start(f32[128,256]{1,0:T(8,128)S(1)} %summed_terms.1.own_ref), channel_id=1, source_target_pairs={{0,1},{1,0},{2,3},{3,2},{4,5},{5,4},{6,7},{7,6},{8,9},{9,8},{10,11... | collective-permute-start | bytes 393224 | tf_op jit(solution)/shard_map/ppermute | solution.py:472

commit v16 on v15

--- a/solution.py
+++ b/solution.py
@@ -11,6 +11,7 @@
 chunk_tiles = 16
 chunk_slots = 16
 build_grant = 44
+build_cuts = (5, 10, 16)
 strips_per_step = 8
 mib = 1024 * 1024
 
@@ -86,12 +87,12 @@
     return (list_ref[2 * tiles_ref.shape[0]] + chunk_tiles - 1) // chunk_tiles
 
 
-def first_chunks(list_ref, tiles_ref):
-    return (live_chunks(list_ref, tiles_ref) * 7 + 15) // 16
-
-
-def build_first_kernel(list_ref, tiles_ref, dense_ref, total, held, sems, *, blocks):
-    part = first_chunks(list_ref, tiles_ref)
+def cut_chunks(list_ref, tiles_ref, cut):
+    return (live_chunks(list_ref, tiles_ref) * cut + 15) // 16
+
+
+def build_first_kernel(list_ref, tiles_ref, dense_ref, total, held, sems, *, blocks, cuts):
+    part = cut_chunks(list_ref, tiles_ref, cuts[1])
     run = add_tiles(list_ref, tiles_ref, total, held, sems, 0, part, first_block=0, blocks=blocks, steps=1)
 
     def clear(down):
@@ -105,11 +106,10 @@
     each_row_block(total, tiles_ref.shape[1], rounded)
 
 
-def build_rest_kernel(list_ref, tiles_ref, half_ref, dense_ref, total, held, sems, *, blocks):
-    chunks = live_chunks(list_ref, tiles_ref)
+def build_more_kernel(list_ref, tiles_ref, half_ref, dense_ref, total, held, sems, *, blocks, cuts):
+    begin, end = (cut_chunks(list_ref, tiles_ref, cut) for cut in cuts)
     run = add_tiles(
-        list_ref, tiles_ref, total, held, sems, first_chunks(list_ref, tiles_ref), chunks,
-        first_block=0, blocks=blocks, steps=1,
+        list_ref, tiles_ref, total, held, sems, begin, end, first_block=0, blocks=blocks, steps=1
     )
 
     def widened(down):
@@ -178,9 +178,10 @@
         ]
     params = pltpu.CompilerParams(vmem_limit_bytes=build_grant * mib)
     scratch = [pltpu.VMEM(*total)] + held_scratch
-    return [
-        lambda packed: (packed, pl.pallas_call(
-            functools.partial(build_first_kernel, blocks=blocks),
+
+    def first(packed):
+        half = pl.pallas_call(
+            functools.partial(build_first_kernel, blocks=blocks, cuts=(0, build_cuts[0])),
             out_shape=dense_shape,
             in_specs=[listed, apart],
             out_specs=whole,
@@ -188,18 +189,24 @@
             compiler_params=params,
             cost_estimate=cost,
             name="build_first",
-        )(packed, tiles)),
-        lambda state: pl.pallas_call(
-            functools.partial(build_rest_kernel, blocks=blocks),
+        )(packed, tiles)
+        return packed, half
+
+    def more(state, begin, end):
+        packed, half = state
+        dense = pl.pallas_call(
+            functools.partial(build_more_kernel, blocks=blocks, cuts=(begin, end)),
             out_shape=dense_shape,
             in_specs=[listed, apart, whole],
             out_specs=whole,
             scratch_shapes=scratch,
             compiler_params=params,
             cost_estimate=cost,
-            name="build_rest",
-        )(state[0], tiles, state[1]),
-    ]
+            name="build_more",
+        )(packed, tiles, half)
+        return (packed, dense) if end < 16 else dense
+
+    return [first] + [functools.partial(more, begin=begin, end=end) for begin, end in zip(build_cuts, build_cuts[1:])]
 
 
 def ring_place(row, count):
@@ -480,6 +487,8 @@
     for step in range(1, reach + 1):
         up = around(ups[-1], 1)
         if step == reach - 1:
+            if len(stages) > 1:
+                dense = stages.pop(0)(dense)
             up, dense, others = lax.optimization_barrier((up, dense, others))
         ups.append(up)
         if step == reach:

time: 65.2 us -> 66 us (1.012); the launches traced: 64.5 us -> 66.2 us
  Pallas kernels: 11.9 us -> 14.4 us
  starting transfers between devices: 20.9 us -> 18.7 us
  waiting for transfers between devices: 29.3 us -> 30.6 us
    pallas_call x2 -> x3, Pallas kernels: 6.05 us -> 8.54 us  [the longest x2 5.52 us: more(): pl.pallas_call(functools.partial(build_more_kernel, blocks=blocks, cuts=(...]
    ppermute x5, starting transfers between devices: 3.58 us -> 2.13 us  [swapped(): lax.ppermute(value, axis, [(i, i ^ partner) for i in range(lax.axis_size(...]
    ppermute x5, waiting for transfers between devices: 9.56 us -> 10.7 us  [swapped(): lax.ppermute(value, axis, [(i, i ^ partner) for i in range(lax.axis_size(...]
    ppermute x15, starting transfers between devices: 17.3 us -> 16.5 us  [around(): lax.ppermute(value, 'row', [(order[i], order[(i + step) % count]) for i i...]
  transfers between devices with their start and end apart: 20 -> 20, of which waited for: 13 -> 11; matrix products, arithmetic and copies ran while one was open for 2% -> 1% of each run, Pallas kernels for 14% -> 17%
where the time goes in v16:
time: 66 us; the launch traced here: 66.2 us
  waiting for transfers between devices  30.6 us (46%)
  starting transfers between devices  18.7 us (28%)
  Pallas kernels  14.4 us (22%)
  between operations  1.49 us (2%)
  other arithmetic  1.04 us (2%)
    ppermute x15, waiting for transfers between devices, around(): lax.ppermute(value, 'row', [(order[i], order[(i + step) % count]) for i i...  19.9 us
    ppermute x15, starting transfers between devices, around(): lax.ppermute(value, 'row', [(order[i], order[(i + step) % count]) for i i...  16.5 us
    ppermute x5, waiting for transfers between devices, swapped(): lax.ppermute(value, axis, [(i, i ^ partner) for i in range(lax.axis_size(...  10.7 us
    pallas_call x2, Pallas kernels, more(): pl.pallas_call(functools.partial(build_more_kernel, blocks=blocks, cuts=(...  5.52 us
    pallas_call x1, Pallas kernels, first(): pl.pallas_call(functools.partial(build_first_kernel, blocks=blocks, cuts=...  3.03 us
    ppermute x5, starting transfers between devices, swapped(): lax.ppermute(value, axis, [(i, i ^ partner) for i in range(lax.axis_size(...  2.13 us
    pallas_call x2, Pallas kernels, backward_product(): pl.pallas_call(functools.partial(backward_kernel, outputs=outputs, row_co...  1.75 us
    pallas_call x2, Pallas kernels, forward_product(): pl.pallas_call(functools.partial(forward_kernel, pieces=pieces, sibling=s...  1.42 us
  transfers between devices with their start and end apart: 20, of which 11 were waited for; matrix products, arithmetic and copies ran while one was open for 1% of the time, Pallas kernels for 17%

profile of v16, /device:TPU:0, one launch (start us, length us, event | category | flops | bytes accessed | tf_op | source)
XLA Modules:
  0.0 66.2 jit_solution(5555062067066830768)
XLA Ops:
  0.6 3.0 %collective-permute-start.3 = (bf16[256,256]{1,0:T(8,128)(2,1)}, bf16[256,256]{1,0:T(8,128)(2,1)S(1)}, u32[]{:S(2)}, u32[]{:S(2)}) collective-permute-start(bf16[256,256]{1,0:T(8,128)(2,1)} %refs_0_.3), channel_id=1, source_target_pairs={{0,4},{8,0},{16,8},{24,16},{28,24},{20,28},{12,20},{4,12},{1,5},{9... | collective-permute-start | bytes 393224 | tf_op jit(solution)/shard_map/ppermute | solution.py:475
  3.6 0.1 collective-permute-start
  4.4 0.7 %add_reduce_fusion.list_ref = s32[513]{0:T(1024)S(1)} fusion(s32[1,1,1]{2,1,0:T(1,128)} %bitcast.2, s32[1,1,256]{2,1,0:T(1,128)} %param.11, s32[1,1,256]{2,1,0:T(1,128)} %param.10), kind=kLoop, calls=%fused_computation.7 | loop fusion | flops 1026 | bytes 4104 | tf_op jit(solution)/shard_map/concatenate | solution.py:552
  5.1 2.3 %collective-permute-done.3.refs_5_ = bf16[256,256]{1,0:T(8,128)(2,1)S(1)} collective-permute-done((bf16[256,256]{1,0:T(8,128)(2,1)}, bf16[256,256]{1,0:T(8,128)(2,1)S(1)}, u32[]{:S(2)}, u32[]{:S(2)}) %collective-permute-start.3) | collective-permute-done | bytes 131104 | tf_op jit(solution)/shard_map/ppermute | solution.py:475
  7.4 1.7 %collective-permute-start.4 = (bf16[256,256]{1,0:T(8,128)(2,1)S(1)}, bf16[256,256]{1,0:T(8,128)(2,1)S(1)}, u32[]{:S(2)}, u32[]{:S(2)}) collective-permute-start(bf16[256,256]{1,0:T(8,128)(2,1)S(1)} %collective-permute-done.3.refs_5_), channel_id=1, source_target_pairs={{0,4},{8,0},{16,8},{24,16},{28,24},{20,28},{12,20},{4,12},{1,5},{9... | collective-permute-start | bytes 393224 | tf_op jit(solution)/shard_map/ppermute | solution.py:475
  9.1 0.0 collective-permute-done.refs_1_
  9.1 0.3 collective-permute-start.1
  9.4 0.0 copy-start.2
  9.4 3.0 %build_first.1.half_ref = bf16[1024,2048]{1,0:T(8,128)(2,1)S(1)} custom-call(s32[513]{0:T(1024)S(1)} %add_reduce_fusion.list_ref, bf16[256,128,128]{2,1,0:T(8,128)(2,1)} %bitcast.3), custom_call_target="tpu_custom_call" | custom-call | flops 4194304 | bytes 6291456 | tf_op jit(solution)/shard_map/build_first/pallas_call | solution.py:183
  12.5 0.0 collective-permute-done.4.refs_6_
  12.5 1.6 %collective-permute-done.1.refs_2_ = bf16[256,256]{1,0:T(8,128)(2,1)S(1)} collective-permute-done((bf16[256,256]{1,0:T(8,128)(2,1)S(1)}, bf16[256,256]{1,0:T(8,128)(2,1)S(1)}, u32[]{:S(2)}, u32[]{:S(2)}) %collective-permute-start.1) | collective-permute-done | bytes 131104 | tf_op jit(solution)/shard_map/ppermute | solution.py:475
  14.1 0.3 collective-permute-start.2
  14.4 0.0 copy-done.2
  14.4 1.7 %collective-permute-start.5 = (bf16[256,256]{1,0:T(8,128)(2,1)S(1)}, bf16[256,256]{1,0:T(8,128)(2,1)S(1)}, u32[]{:S(2)}, u32[]{:S(2)}) collective-permute-start(bf16[256,256]{1,0:T(8,128)(2,1)S(1)} %copy-done.2), channel_id=1, source_target_pairs={{0,2},{1,3},{2,0},{3,1},{4,6},{5,7},{6,4},{7,5},{8,10},{9,11},{10,... | collective-permute-start | bytes 393224 | tf_op jit(solution)/shard_map/ppermute | solution.py:479
  16.1 1.5 %collective-permute-start.7 = (bf16[256,256]{1,0:T(8,128)(2,1)S(1)}, bf16[256,256]{1,0:T(8,128)(2,1)S(1)}, u32[]{:S(2)}, u32[]{:S(2)}) collective-permute-start(bf16[256,256]{1,0:T(8,128)(2,1)S(1)} %collective-permute-done.4.refs_6_), channel_id=1, source_target_pairs={{0,4},{8,0},{16,8},{24,16},{28,24},{20,28},{12,20},{4,12},{1,5},{9... | collective-permute-start | bytes 393224 | tf_op jit(solution)/shard_map/ppermute | solution.py:475
  17.6 2.8 %build_more.2.half_ref = bf16[1024,2048]{1,0:T(8,128)(2,1)S(1)} custom-call(s32[513]{0:T(1024)S(1)} %add_reduce_fusion.list_ref, bf16[256,128,128]{2,1,0:T(8,128)(2,1)} %bitcast.4, bf16[1024,2048]{1,0:T(8,128)(2,1)S(1)} %build_first.1.half_ref), custom_call_target="tpu_custom_call" | custom-call | flops 4194304 | bytes 6291456 | tf_op jit(solution)/shard_map/build_more/pallas_call | solution.py:197
  20.4 0.0 copy-start
  20.4 0.0 collective-permute-done.2.refs_3_
  20.4 0.0 collective-permute-done.5.refs_4_
  20.4 1.0 %collective-permute-start.6 = (bf16[256,256]{1,0:T(8,128)(2,1)S(1)}, bf16[256,256]{1,0:T(8,128)(2,1)S(1)}, u32[]{:S(2)}, u32[]{:S(2)}) collective-permute-start(bf16[256,256]{1,0:T(8,128)(2,1)S(1)} %collective-permute-done.2.refs_3_), channel_id=1, source_target_pairs={{0,8},{8,16},{16,24},{24,28},{28,20},{20,12},{12,4},{4,0},{1,9},{9... | collective-permute-start | bytes 393224 | tf_op jit(solution)/shard_map/ppermute | solution.py:475
  21.4 2.8 %build_more.3.dense_ref = bf16[1024,2048]{1,0:T(8,128)(2,1)S(1)} custom-call(s32[513]{0:T(1024)S(1)} %add_reduce_fusion.list_ref, bf16[256,128,128]{2,1,0:T(8,128)(2,1)} %bitcast.5, bf16[1024,2048]{1,0:T(8,128)(2,1)S(1)} %build_more.2.half_ref), custom_call_target="tpu_custom_call" | custom-call | flops 4194304 | bytes 6291456 | tf_op jit(solution)/shard_map/build_more/pallas_call | solution.py:197
  24.2 0.0 collective-permute-done.7.refs_7_
  24.2 1.6 %collective-permute-done.6.refs_4_ = bf16[256,256]{1,0:T(8,128)(2,1)S(1)} collective-permute-done((bf16[256,256]{1,0:T(8,128)(2,1)S(1)}, bf16[256,256]{1,0:T(8,128)(2,1)S(1)}, u32[]{:S(2)}, u32[]{:S(2)}) %collective-permute-start.6) | collective-permute-done | bytes 131104 | tf_op jit(solution)/shard_map/ppermute | solution.py:475
  25.8 0.0 copy-done
  25.8 0.7 %forward_product.2 = bf16[512,256]{1,0:T(8,128)(2,1)S(1)} custom-call(bf16[1024,2048]{1,0:T(8,128)(2,1)S(1)} %build_more.3.dense_ref, bf16[256,256]{1,0:T(8,128)(2,1)S(1)} %copy-done, bf16[256,256]{1,0:T(8,128)(2,1)S(1)} %collective-permute-done.refs_1_, bf16[256,256]{1,0:T(8,128)(2,1)S(1)} %collective-permute-done.1.refs_2_, ...), custom_call_target="tpu_custom_call" | custom-call | flops 536870912 | bytes 3407872 | tf_op jit(solution)/shard_map/forward_product/pallas_call | solution.py:251
  26.5 0.0 copy-start.1
  26.5 0.1 collective-permute-start.8
  26.6 0.7 %forward_product.3 = bf16[512,256]{1,0:T(8,128)(2,1)S(1)} custom-call(bf16[1024,2048]{1,0:T(8,128)(2,1)S(1)} %build_more.3.dense_ref, bf16[256,256]{1,0:T(8,128)(2,1)S(1)} %copy-done, bf16[256,256]{1,0:T(8,128)(2,1)S(1)} %collective-permute-done.refs_1_, bf16[256,256]{1,0:T(8,128)(2,1)S(1)} %collective-permute-done.1.refs_2_, ...), custom_call_target="tpu_custom_call" | custom-call | flops 536870912 | bytes 3407872 | tf_op jit(solution)/shard_map/forward_product/pallas_call | solution.py:251
  27.3 0.8 %collective-permute-done.8 = bf16[512,256]{1,0:T(8,128)(2,1)S(1)} collective-permute-done((bf16[512,256]{1,0:T(8,128)(2,1)S(1)}, bf16[512,256]{1,0:T(8,128)(2,1)S(1)}, u32[]{:S(2)}, u32[]{:S(2)}) %collective-permute-start.8) | collective-permute-done | bytes 262176 | tf_op jit(solution)/shard_map/ppermute | solution.py:479
  28.1 0.1 add_convert_fusion.refs_0_
  28.2 0.3 collective-permute-start.9
  28.5 8.1 %collective-permute-done.9.refs_1_ = bf16[512,256]{1,0:T(8,128)(2,1)S(1)} collective-permute-done((bf16[512,256]{1,0:T(8,128)(2,1)S(1)}, bf16[512,256]{1,0:T(8,128)(2,1)S(1)}, u32[]{:S(2)}, u32[]{:S(2)}) %collective-permute-start.9) | collective-permute-done | bytes 262176 | tf_op jit(solution)/shard_map/ppermute | solution.py:479
  36.6 0.0 copy-done.1
  36.6 1.0 %middle.1 = (bf16[256,256]{1,0:T(8,128)(2,1)}, bf16[768,256]{1,0:T(8,128)(2,1)S(1)}, f32[128,256]{1,0:T(8,128)S(1)}) custom-call(bf16[512,256]{1,0:T(8,128)(2,1)S(1)} %add_convert_fusion.refs_0_, bf16[512,256]{1,0:T(8,128)(2,1)S(1)} %collective-permute-done.9.refs_1_, bf16[256,256]{1,0:T(8,128)(2,1)S(1)} %copy-done.1, bf16[256,256]{1,0:T(8,128)(2,1)S(1)} %copy-done.2, ...), custom_call_target="tpu_custom_call" | custom-call | flops 335544320 | bytes 1572864 | tf_op jit(solution)/shard_map/middle/pallas_call | solution.py:315
  37.6 0.1 collective-permute-start.10
  37.7 1.7 %collective-permute-done.10.sibling_ref = bf16[768,256]{1,0:T(8,128)(2,1)S(1)} collective-permute-done((bf16[768,256]{1,0:T(8,128)(2,1)S(1)}, bf16[768,256]{1,0:T(8,128)(2,1)S(1)}, u32[]{:S(2)}, u32[]{:S(2)}) %collective-permute-start.10) | collective-permute-done | bytes 393248 | tf_op jit(solution)/shard_map/ppermute | solution.py:479
  39.4 0.5 backward_product.2
  39.9 2.1 %collective-permute-start.15 = (bf16[256,256]{1,0:T(8,128)(2,1)S(1)}, bf16[256,256]{1,0:T(8,128)(2,1)S(1)}, u32[]{:S(2)}, u32[]{:S(2)}) collective-permute-start(bf16[256,256]{1,0:T(8,128)(2,1)S(1)} %get-tuple-element.59), channel_id=1, source_target_pairs={{0,4},{8,0},{16,8},{24,16},{28,24},{20,28},{12,20},{4,12},{1,5},{9... | collective-permute-start | bytes 393224 | tf_op jit(solution)/shard_map/ppermute | solution.py:475
  42.0 0.0 collective-permute-start.11
  42.0 1.3 %backward_product.3 = (bf16[384,256]{1,0:T(8,128)(2,1)S(1)}, bf16[384,256]{1,0:T(8,128)(2,1)S(1)}, bf16[256,256]{1,0:T(8,128)(2,1)S(1)}, bf16[384,256]{1,0:T(8,1...) custom-call(bf16[1024,2048]{1,0:T(8,128)(2,1)S(1)} %build_more.3.dense_ref, ...), custom_call_target="tpu_custom_call" | custom-call | flops 134217728 | bytes 917504 | tf_op jit(solution)/shard_map/backward_product/pallas_call | solution.py:376
  43.3 2.2 %collective-permute-done.15.refs_2_ = bf16[256,256]{1,0:T(8,128)(2,1)S(1)} collective-permute-done((bf16[256,256]{1,0:T(8,128)(2,1)S(1)}, bf16[256,256]{1,0:T(8,128)(2,1)S(1)}, u32[]{:S(2)}, u32[]{:S(2)}) %collective-permute-start.15) | collective-permute-done | bytes 131104 | tf_op jit(solution)/shard_map/ppermute | solution.py:475
  45.5 2.1 %collective-permute-start.16 = (bf16[384,256]{1,0:T(8,128)(2,1)S(1)}, bf16[384,256]{1,0:T(8,128)(2,1)S(1)}, u32[]{:S(2)}, u32[]{:S(2)}) collective-permute-start(bf16[384,256]{1,0:T(8,128)(2,1)S(1)} %add_convert_fusion.3), channel_id=1, source_target_pairs={{0,4},{8,0},{16,8},{24,16},{28,24},{20,28},{12,20},{4,12},{1,5},{9... | collective-permute-start | bytes 589832 | tf_op jit(solution)/shard_map/ppermute | solution.py:475
  47.6 0.0 collective-permute-done.11.refs_1_
  47.7 0.1 collective-permute-start.12
  47.7 4.0 %collective-permute-done.16.refs_4_ = bf16[384,256]{1,0:T(8,128)(2,1)S(1)} collective-permute-done((bf16[384,256]{1,0:T(8,128)(2,1)S(1)}, bf16[384,256]{1,0:T(8,128)(2,1)S(1)}, u32[]{:S(2)}, u32[]{:S(2)}) %collective-permute-start.16) | collective-permute-done | bytes 196640 | tf_op jit(solution)/shard_map/ppermute | solution.py:475
  51.7 0.1 add_convert_fusion.2
  51.8 2.1 %collective-permute-start.17 = (bf16[384,256]{1,0:T(8,128)(2,1)S(1)}, bf16[384,256]{1,0:T(8,128)(2,1)S(1)}, u32[]{:S(2)}, u32[]{:S(2)}) collective-permute-start(bf16[384,256]{1,0:T(8,128)(2,1)S(1)} %add_convert_fusion.2), channel_id=1, source_target_pairs={{0,4},{8,0},{16,8},{24,16},{28,24},{20,28},{12,20},{4,12},{1,5},{9... | collective-permute-start | bytes 589832 | tf_op jit(solution)/shard_map/ppermute | solution.py:475
  53.8 0.0 collective-permute-done.12.refs_3_
  53.8 0.1 add_convert_fusion.4
  53.9 0.1 collective-permute-start.13
  54.0 3.5 %collective-permute-done.17.refs_6_ = bf16[384,256]{1,0:T(8,128)(2,1)S(1)} collective-permute-done((bf16[384,256]{1,0:T(8,128)(2,1)S(1)}, bf16[384,256]{1,0:T(8,128)(2,1)S(1)}, u32[]{:S(2)}, u32[]{:S(2)}) %collective-permute-start.17) | collective-permute-done | bytes 196640 | tf_op jit(solution)/shard_map/ppermute | solution.py:475
  57.5 0.1 add_convert_fusion.1
  57.5 2.1 %collective-permute-start.18 = (bf16[384,256]{1,0:T(8,128)(2,1)S(1)}, bf16[384,256]{1,0:T(8,128)(2,1)S(1)}, u32[]{:S(2)}, u32[]{:S(2)}) collective-permute-start(bf16[384,256]{1,0:T(8,128)(2,1)S(1)} %add_convert_fusion.1), channel_id=1, source_target_pairs={{0,4},{8,0},{16,8},{24,16},{28,24},{20,28},{12,20},{4,12},{1,5},{9... | collective-permute-start | bytes 589832 | tf_op jit(solution)/shard_map/ppermute | solution.py:475
  59.6 0.0 collective-permute-done.13.refs_5_
  59.7 0.1 collective-permute-start.14
  59.7 3.5 %collective-permute-done.18.refs_2_.refs_7_ = bf16[384,256]{1,0:T(8,128)(2,1)S(1)} collective-permute-done((bf16[384,256]{1,0:T(8,128)(2,1)S(1)}, bf16[384,256]{1,0:T(8,128)(2,1)S(1)}, u32[]{:S(2)}, u32[]{:S(2)}) %collective-permute-start.18) | collective-permute-done | bytes 196640 | tf_op jit(solution)/shard_map/ppermute | solution.py:475
  63.3 0.1 summed_terms.1.own_ref
  63.4 0.1 collective-permute-start.19
  63.5 1.2 %collective-permute-done.14.refs_1_ = bf16[256,256]{1,0:T(8,128)(2,1)S(1)} collective-permute-done((bf16[256,256]{1,0:T(8,128)(2,1)S(1)}, bf16[256,256]{1,0:T(8,128)(2,1)S(1)}, u32[]{:S(2)}, u32[]{:S(2)}) %collective-permute-start.14) | collective-permute-done | bytes 131104 | tf_op jit(solution)/shard_map/ppermute | solution.py:475
  64.7 0.8 %finish.1 = bf16[256,256]{1,0:T(8,128)(2,1)} custom-call(bf16[256,256]{1,0:T(8,128)(2,1)S(1)} %get-tuple-element.51.refs_0_, bf16[256,256]{1,0:T(8,128)(2,1)S(1)} %collective-permute-done.14.refs_1_, bf16[384,256]{1,0:T(8,128)(2,1)S(1)} %collective-permute-done.18.refs_2_.refs_7_), custom_call_target="tpu_custom_call" | custom-call | flops 196608 | bytes 524288 | tf_op jit(solution)/shard_map/finish/pallas_call | solution.py:439
  65.5 0.0 collective-permute-done.19.sibling_ref
  65.5 0.7 %joined.1 = f32[256,256]{1,0:T(8,128)} custom-call(f32[128,256]{1,0:T(8,128)S(1)} %summed_terms.1.own_ref, f32[128,256]{1,0:T(8,128)S(1)} %collective-permute-done.19.sibling_ref), custom_call_target="tpu_custom_call" | custom-call | bytes 524288 | tf_op jit(solution)/shard_map/joined/pallas_call | solution.py:461
  (3 shorter events, 0.1 us)
Async XLA Ops:
  0.6 6.8 %collective-permute-start.3 = (bf16[256,256]{1,0:T(8,128)(2,1)}, bf16[256,256]{1,0:T(8,128)(2,1)S(1)}, u32[]{:S(2)}, u32[]{:S(2)}) collective-permute-start(bf16[256,256]{1,0:T(8,128)(2,1)} %refs_0_.3), channel_id=1, source_target_pairs={{0,4},{8,0},{16,8},{24,16},{28,24},{20,28},{12,20},{4,12},{1,5},{9... | collective-permute-start | bytes 393224 | tf_op jit(solution)/shard_map/ppermute | solution.py:475
  3.6 5.5 %collective-permute-start = (bf16[256,256]{1,0:T(8,128)(2,1)}, bf16[256,256]{1,0:T(8,128)(2,1)S(1)}, u32[]{:S(2)}, u32[]{:S(2)}) collective-permute-start(bf16[256,256]{1,0:T(8,128)(2,1)} %refs_0_.3), channel_id=1, source_target_pairs={{0,8},{8,16},{16,24},{24,28},{28,20},{20,12},{12,4},{4,0},{1,9},{9... | collective-permute-start | bytes 393224 | tf_op jit(solution)/shard_map/ppermute | solution.py:475
  7.4 5.1 %collective-permute-start.4 = (bf16[256,256]{1,0:T(8,128)(2,1)S(1)}, bf16[256,256]{1,0:T(8,128)(2,1)S(1)}, u32[]{:S(2)}, u32[]{:S(2)}) collective-permute-start(bf16[256,256]{1,0:T(8,128)(2,1)S(1)} %collective-permute-done.3.refs_5_), channel_id=1, source_target_pairs={{0,4},{8,0},{16,8},{24,16},{28,24},{20,28},{12,20},{4,12},{1,5},{9... | collective-permute-start | bytes 393224 | tf_op jit(solution)/shard_map/ppermute | solution.py:475
  9.1 5.0 %collective-permute-start.1 = (bf16[256,256]{1,0:T(8,128)(2,1)S(1)}, bf16[256,256]{1,0:T(8,128)(2,1)S(1)}, u32[]{:S(2)}, u32[]{:S(2)}) collective-permute-start(bf16[256,256]{1,0:T(8,128)(2,1)S(1)} %collective-permute-done.refs_1_), channel_id=1, source_target_pairs={{0,8},{8,16},{16,24},{24,28},{28,20},{20,12},{12,4},{4,0},{1,9},{9... | collective-permute-start | bytes 393224 | tf_op jit(solution)/shard_map/ppermute | solution.py:475
  9.4 5.0 %copy-start.2 = (bf16[256,256]{1,0:T(8,128)(2,1)S(1)}, bf16[256,256]{1,0:T(8,128)(2,1)}, u32[]{:S(2)}) copy-start(bf16[256,256]{1,0:T(8,128)(2,1)} %refs_3_) | copy-start | bytes 393220
  14.1 6.3 %collective-permute-start.2 = (bf16[256,256]{1,0:T(8,128)(2,1)S(1)}, bf16[256,256]{1,0:T(8,128)(2,1)S(1)}, u32[]{:S(2)}, u32[]{:S(2)}) collective-permute-start(bf16[256,256]{1,0:T(8,128)(2,1)S(1)} %collective-permute-done.1.refs_2_), channel_id=1, source_target_pairs={{0,8},{8,16},{16,24},{24,28},{28,20},{20,12},{12,4},{4,0},{1,9},{9... | collective-permute-start | bytes 393224 | tf_op jit(solution)/shard_map/ppermute | solution.py:475
  14.4 6.0 %collective-permute-start.5 = (bf16[256,256]{1,0:T(8,128)(2,1)S(1)}, bf16[256,256]{1,0:T(8,128)(2,1)S(1)}, u32[]{:S(2)}, u32[]{:S(2)}) collective-permute-start(bf16[256,256]{1,0:T(8,128)(2,1)S(1)} %copy-done.2), channel_id=1, source_target_pairs={{0,2},{1,3},{2,0},{3,1},{4,6},{5,7},{6,4},{7,5},{8,10},{9,11},{10,... | collective-permute-start | bytes 393224 | tf_op jit(solution)/shard_map/ppermute | solution.py:479
  16.1 8.1 %collective-permute-start.7 = (bf16[256,256]{1,0:T(8,128)(2,1)S(1)}, bf16[256,256]{1,0:T(8,128)(2,1)S(1)}, u32[]{:S(2)}, u32[]{:S(2)}) collective-permute-start(bf16[256,256]{1,0:T(8,128)(2,1)S(1)} %collective-permute-done.4.refs_6_), channel_id=1, source_target_pairs={{0,4},{8,0},{16,8},{24,16},{28,24},{20,28},{12,20},{4,12},{1,5},{9... | collective-permute-start | bytes 393224 | tf_op jit(solution)/shard_map/ppermute | solution.py:475
  20.4 5.5 %copy-start = (bf16[256,256]{1,0:T(8,128)(2,1)S(1)}, bf16[256,256]{1,0:T(8,128)(2,1)}, u32[]{:S(2)}) copy-start(bf16[256,256]{1,0:T(8,128)(2,1)} %refs_0_.3) | copy-start | bytes 393220
  20.4 5.4 %collective-permute-start.6 = (bf16[256,256]{1,0:T(8,128)(2,1)S(1)}, bf16[256,256]{1,0:T(8,128)(2,1)S(1)}, u32[]{:S(2)}, u32[]{:S(2)}) collective-permute-start(bf16[256,256]{1,0:T(8,128)(2,1)S(1)} %collective-permute-done.2.refs_3_), channel_id=1, source_target_pairs={{0,8},{8,16},{16,24},{24,28},{28,20},{20,12},{12,4},{4,0},{1,9},{9... | collective-permute-start | bytes 393224 | tf_op jit(solution)/shard_map/ppermute | solution.py:475
  26.5 10.1 %copy-start.1 = (bf16[256,256]{1,0:T(8,128)(2,1)S(1)}, bf16[256,256]{1,0:T(8,128)(2,1)}, u32[]{:S(2)}) copy-start(bf16[256,256]{1,0:T(8,128)(2,1)} %refs_2_.1) | copy-start | bytes 393220
  26.5 1.6 %collective-permute-start.8 = (bf16[512,256]{1,0:T(8,128)(2,1)S(1)}, bf16[512,256]{1,0:T(8,128)(2,1)S(1)}, u32[]{:S(2)}, u32[]{:S(2)}) collective-permute-start(bf16[512,256]{1,0:T(8,128)(2,1)S(1)} %forward_product.2), channel_id=1, source_target_pairs={{0,1},{1,0},{2,3},{3,2},{4,5},{5,4},{6,7},{7,6},{8,9},{9,8},{10,11... | collective-permute-start | bytes 786440 | tf_op jit(solution)/shard_map/ppermute | solution.py:479
  28.2 8.4 %collective-permute-start.9 = (bf16[512,256]{1,0:T(8,128)(2,1)S(1)}, bf16[512,256]{1,0:T(8,128)(2,1)S(1)}, u32[]{:S(2)}, u32[]{:S(2)}) collective-permute-start(bf16[512,256]{1,0:T(8,128)(2,1)S(1)} %add_convert_fusion.refs_0_), channel_id=1, source_target_pairs={{0,2},{1,3},{2,0},{3,1},{4,6},{5,7},{6,4},{7,5},{8,10},{9,11},{10,... | collective-permute-start | bytes 786440 | tf_op jit(solution)/shard_map/ppermute | solution.py:479
  37.6 1.8 %collective-permute-start.10 = (bf16[768,256]{1,0:T(8,128)(2,1)S(1)}, bf16[768,256]{1,0:T(8,128)(2,1)S(1)}, u32[]{:S(2)}, u32[]{:S(2)}) collective-permute-start(bf16[768,256]{1,0:T(8,128)(2,1)S(1)} %get-tuple-element.45.own_ref), channel_id=1, source_target_pairs={{0,1},{1,0},{2,3},{3,2},{4,5},{5,4},{6,7},{7,6},{8,9},{9,8},{10,11... | collective-permute-start | bytes 1179656 | tf_op jit(solution)/shard_map/ppermute | solution.py:479
  39.9 5.6 %collective-permute-start.15 = (bf16[256,256]{1,0:T(8,128)(2,1)S(1)}, bf16[256,256]{1,0:T(8,128)(2,1)S(1)}, u32[]{:S(2)}, u32[]{:S(2)}) collective-permute-start(bf16[256,256]{1,0:T(8,128)(2,1)S(1)} %get-tuple-element.59), channel_id=1, source_target_pairs={{0,4},{8,0},{16,8},{24,16},{28,24},{20,28},{12,20},{4,12},{1,5},{9... | collective-permute-start | bytes 393224 | tf_op jit(solution)/shard_map/ppermute | solution.py:475
  42.0 5.6 %collective-permute-start.11 = (bf16[256,256]{1,0:T(8,128)(2,1)S(1)}, bf16[256,256]{1,0:T(8,128)(2,1)S(1)}, u32[]{:S(2)}, u32[]{:S(2)}) collective-permute-start(bf16[256,256]{1,0:T(8,128)(2,1)S(1)} %get-tuple-element.55), channel_id=1, source_target_pairs={{0,8},{8,16},{16,24},{24,28},{28,20},{20,12},{12,4},{4,0},{1,9},{9... | collective-permute-start | bytes 393224 | tf_op jit(solution)/shard_map/ppermute | solution.py:475
  45.5 6.2 %collective-permute-start.16 = (bf16[384,256]{1,0:T(8,128)(2,1)S(1)}, bf16[384,256]{1,0:T(8,128)(2,1)S(1)}, u32[]{:S(2)}, u32[]{:S(2)}) collective-permute-start(bf16[384,256]{1,0:T(8,128)(2,1)S(1)} %add_convert_fusion.3), channel_id=1, source_target_pairs={{0,4},{8,0},{16,8},{24,16},{28,24},{20,28},{12,20},{4,12},{1,5},{9... | collective-permute-start | bytes 589832 | tf_op jit(solution)/shard_map/ppermute | solution.py:475
  47.7 6.2 %collective-permute-start.12 = (bf16[384,256]{1,0:T(8,128)(2,1)S(1)}, bf16[384,256]{1,0:T(8,128)(2,1)S(1)}, u32[]{:S(2)}, u32[]{:S(2)}) collective-permute-start(bf16[384,256]{1,0:T(8,128)(2,1)S(1)} %add_convert_fusion.5), channel_id=1, source_target_pairs={{0,8},{8,16},{16,24},{24,28},{28,20},{20,12},{12,4},{4,0},{1,9},{9... | collective-permute-start | bytes 589832 | tf_op jit(solution)/shard_map/ppermute | solution.py:475
  51.8 5.7 %collective-permute-start.17 = (bf16[384,256]{1,0:T(8,128)(2,1)S(1)}, bf16[384,256]{1,0:T(8,128)(2,1)S(1)}, u32[]{:S(2)}, u32[]{:S(2)}) collective-permute-start(bf16[384,256]{1,0:T(8,128)(2,1)S(1)} %add_convert_fusion.2), channel_id=1, source_target_pairs={{0,4},{8,0},{16,8},{24,16},{28,24},{20,28},{12,20},{4,12},{1,5},{9... | collective-permute-start | bytes 589832 | tf_op jit(solution)/shard_map/ppermute | solution.py:475
  53.9 5.7 %collective-permute-start.13 = (bf16[384,256]{1,0:T(8,128)(2,1)S(1)}, bf16[384,256]{1,0:T(8,128)(2,1)S(1)}, u32[]{:S(2)}, u32[]{:S(2)}) collective-permute-start(bf16[384,256]{1,0:T(8,128)(2,1)S(1)} %add_convert_fusion.4), channel_id=1, source_target_pairs={{0,8},{8,16},{16,24},{24,28},{28,20},{20,12},{12,4},{4,0},{1,9},{9... | collective-permute-start | bytes 589832 | tf_op jit(solution)/shard_map/ppermute | solution.py:475
  57.5 5.7 %collective-permute-start.18 = (bf16[384,256]{1,0:T(8,128)(2,1)S(1)}, bf16[384,256]{1,0:T(8,128)(2,1)S(1)}, u32[]{:S(2)}, u32[]{:S(2)}) collective-permute-start(bf16[384,256]{1,0:T(8,128)(2,1)S(1)} %add_convert_fusion.1), channel_id=1, source_target_pairs={{0,4},{8,0},{16,8},{24,16},{28,24},{20,28},{12,20},{4,12},{1,5},{9... | collective-permute-start | bytes 589832 | tf_op jit(solution)/shard_map/ppermute | solution.py:475
  59.7 5.0 %collective-permute-start.14 = (bf16[256,256]{1,0:T(8,128)(2,1)S(1)}, bf16[256,256]{1,0:T(8,128)(2,1)S(1)}, u32[]{:S(2)}, u32[]{:S(2)}) collective-permute-start(bf16[256,256]{1,0:T(8,128)(2,1)S(1)} %add_convert_fusion.6), channel_id=1, source_target_pairs={{0,8},{8,16},{16,24},{24,28},{28,20},{20,12},{12,4},{4,0},{1,9},{9... | collective-permute-start | bytes 393224 | tf_op jit(solution)/shard_map/ppermute | solution.py:475
  63.4 2.1 %collective-permute-start.19 = (f32[128,256]{1,0:T(8,128)S(1)}, f32[128,256]{1,0:T(8,128)S(1)}, u32[]{:S(2)}, u32[]{:S(2)}) collective-permute-start(f32[128,256]{1,0:T(8,128)S(1)} %summed_terms.1.own_ref), channel_id=1, source_target_pairs={{0,1},{1,0},{2,3},{3,2},{4,5},{5,4},{6,7},{7,6},{8,9},{9,8},{10,11... | collective-permute-start | bytes 393224 | tf_op jit(solution)/shard_map/ppermute | solution.py:479

commit v17 on v15

--- a/solution.py
+++ b/solution.py
@@ -46,6 +46,9 @@
             col = jnp.where(live, col, 0)
         row = jnp.where(live, list_ref[place], row_blocks)
         return row, col
+
+    down, along = (lax.broadcasted_iota(jnp.int32, (side, side), axis) for axis in range(2))
+    unit = (down == along).astype(jnp.float32).astype(jnp.bfloat16)
 
     def chunk_step(index, carry):
         fetch(index).wait()
@@ -59,7 +62,7 @@
         for lane in range(chunk_tiles):
             last = lane == chunk_tiles - 1
             following = None if last else total[at[lane + 1]]
-            current = current + held[slot, lane].astype(jnp.float32)
+            current = current + jnp.dot(held[slot, lane], unit, preferred_element_type=jnp.float32)
             total[at[lane]] = current
             if not last:
                 same = (spots[lane][0] == spots[lane + 1][0]) & (spots[lane][1] == spots[lane + 1][1])

time: 65.2 us -> 66.6 us (1.021)
  Pallas kernels: 11.9 us -> 13.1 us
  starting transfers between devices: 20.9 us -> 20.1 us
    ppermute x5, waiting for transfers between devices: 9.56 us -> 10.9 us  [swapped(): lax.ppermute(value, axis, [(i, i ^ partner) for i in range(lax.axis_size(...]
    ppermute x15, waiting for transfers between devices: 19.7 us -> 18.8 us  [around(): lax.ppermute(value, 'row', [(order[i], order[(i + step) % count]) for i i...]
    pallas_call x1, Pallas kernels: 3.02 us -> 3.82 us  [build_stages(): pl.pallas_call(functools.partial(build_first_kernel, blocks=blocks), out_...]
  transfers between devices with their start and end apart: 20 -> 20, of which waited for: 13 -> 13; matrix products, arithmetic and copies ran while one was open for 2% -> 1% of each run, Pallas kernels for 14% -> 16%
where the time goes in v17:
time: 66.6 us; the launch traced here: 65.4 us
  waiting for transfers between devices  29.7 us (45%)
  starting transfers between devices  20.1 us (30%)
  Pallas kernels  13.1 us (20%)
  between operations  1.45 us (2%)
  other arithmetic  1.04 us (2%)
    ppermute x15, waiting for transfers between devices, around(): lax.ppermute(value, 'row', [(order[i], order[(i + step) % count]) for i i...  18.8 us
    ppermute x15, starting transfers between devices, around(): lax.ppermute(value, 'row', [(order[i], order[(i + step) % count]) for i i...  16.8 us
    ppermute x5, waiting for transfers between devices, swapped(): lax.ppermute(value, axis, [(i, i ^ partner) for i in range(lax.axis_size(...  10.9 us
    pallas_call x1, Pallas kernels, build_stages(): pl.pallas_call(functools.partial(build_first_kernel, blocks=blocks), out_...  3.82 us
    pallas_call x1, Pallas kernels, build_stages(): pl.pallas_call(functools.partial(build_rest_kernel, blocks=blocks), out_s...  3.43 us
    ppermute x5, starting transfers between devices, swapped(): lax.ppermute(value, axis, [(i, i ^ partner) for i in range(lax.axis_size(...  3.29 us
    pallas_call x2, Pallas kernels, backward_product(): pl.pallas_call(functools.partial(backward_kernel, outputs=outputs, row_co...  1.74 us
    pallas_call x2, Pallas kernels, forward_product(): pl.pallas_call(functools.partial(forward_kernel, pieces=pieces, sibling=s...  1.42 us
  transfers between devices with their start and end apart: 20, of which 13 were waited for; matrix products, arithmetic and copies ran while one was open for 1% of the time, Pallas kernels for 16%

profile of v17, /device:TPU:0, one launch (start us, length us, event | category | flops | bytes accessed | tf_op | source)
XLA Modules:
  0.0 65.4 jit_solution(12964400581312253969)
XLA Ops:
  0.6 3.0 %collective-permute-start.3 = (bf16[256,256]{1,0:T(8,128)(2,1)}, bf16[256,256]{1,0:T(8,128)(2,1)S(1)}, u32[]{:S(2)}, u32[]{:S(2)}) collective-permute-start(bf16[256,256]{1,0:T(8,128)(2,1)} %refs_0_.3), channel_id=1, source_target_pairs={{0,4},{8,0},{16,8},{24,16},{28,24},{20,28},{12,20},{4,12},{1,5},{9... | collective-permute-start | bytes 393224 | tf_op jit(solution)/shard_map/ppermute | solution.py:471
  3.6 0.1 collective-permute-start
  4.4 0.7 %add_reduce_fusion.list_ref = s32[513]{0:T(1024)S(1)} fusion(s32[1,1,1]{2,1,0:T(1,128)} %bitcast.2, s32[1,1,256]{2,1,0:T(1,128)} %param.11, s32[1,1,256]{2,1,0:T(1,128)} %param.10), kind=kLoop, calls=%fused_computation.7 | loop fusion | flops 1026 | bytes 4104 | tf_op jit(solution)/shard_map/concatenate | solution.py:546
  5.1 2.3 %collective-permute-done.3.refs_5_ = bf16[256,256]{1,0:T(8,128)(2,1)S(1)} collective-permute-done((bf16[256,256]{1,0:T(8,128)(2,1)}, bf16[256,256]{1,0:T(8,128)(2,1)S(1)}, u32[]{:S(2)}, u32[]{:S(2)}) %collective-permute-start.3) | collective-permute-done | bytes 131104 | tf_op jit(solution)/shard_map/ppermute | solution.py:471
  7.4 1.7 %collective-permute-start.4 = (bf16[256,256]{1,0:T(8,128)(2,1)S(1)}, bf16[256,256]{1,0:T(8,128)(2,1)S(1)}, u32[]{:S(2)}, u32[]{:S(2)}) collective-permute-start(bf16[256,256]{1,0:T(8,128)(2,1)S(1)} %collective-permute-done.3.refs_5_), channel_id=1, source_target_pairs={{0,4},{8,0},{16,8},{24,16},{28,24},{20,28},{12,20},{4,12},{1,5},{9... | collective-permute-start | bytes 393224 | tf_op jit(solution)/shard_map/ppermute | solution.py:471
  9.1 0.0 collective-permute-done.refs_1_
  9.1 0.3 collective-permute-start.1
  9.4 0.0 copy-start.2
  9.4 3.8 %build_first.1.half_ref = bf16[1024,2048]{1,0:T(8,128)(2,1)S(1)} custom-call(s32[513]{0:T(1024)S(1)} %add_reduce_fusion.list_ref, bf16[256,128,128]{2,1,0:T(8,128)(2,1)} %bitcast.3), custom_call_target="tpu_custom_call" | custom-call | flops 4194304 | bytes 6291456 | tf_op jit(solution)/shard_map/build_first/pallas_call | solution.py:185
  13.3 0.0 copy-start
  13.3 0.0 collective-permute-done.4.refs_6_
  13.3 0.8 %collective-permute-done.1.refs_2_ = bf16[256,256]{1,0:T(8,128)(2,1)S(1)} collective-permute-done((bf16[256,256]{1,0:T(8,128)(2,1)S(1)}, bf16[256,256]{1,0:T(8,128)(2,1)S(1)}, u32[]{:S(2)}, u32[]{:S(2)}) %collective-permute-start.1) | collective-permute-done | bytes 131104 | tf_op jit(solution)/shard_map/ppermute | solution.py:471
  14.1 1.0 %collective-permute-start.2 = (bf16[256,256]{1,0:T(8,128)(2,1)S(1)}, bf16[256,256]{1,0:T(8,128)(2,1)S(1)}, u32[]{:S(2)}, u32[]{:S(2)}) collective-permute-start(bf16[256,256]{1,0:T(8,128)(2,1)S(1)} %collective-permute-done.1.refs_2_), channel_id=1, source_target_pairs={{0,8},{8,16},{16,24},{24,28},{28,20},{20,12},{12,4},{4,0},{1,9},{9... | collective-permute-start | bytes 393224 | tf_op jit(solution)/shard_map/ppermute | solution.py:471
  15.1 0.0 copy-done.2
  15.1 1.5 %collective-permute-start.5 = (bf16[256,256]{1,0:T(8,128)(2,1)S(1)}, bf16[256,256]{1,0:T(8,128)(2,1)S(1)}, u32[]{:S(2)}, u32[]{:S(2)}) collective-permute-start(bf16[256,256]{1,0:T(8,128)(2,1)S(1)} %copy-done.2), channel_id=1, source_target_pairs={{0,2},{1,3},{2,0},{3,1},{4,6},{5,7},{6,4},{7,5},{8,10},{9,11},{10,... | collective-permute-start | bytes 393224 | tf_op jit(solution)/shard_map/ppermute | solution.py:475
  16.6 1.0 %collective-permute-start.7 = (bf16[256,256]{1,0:T(8,128)(2,1)S(1)}, bf16[256,256]{1,0:T(8,128)(2,1)S(1)}, u32[]{:S(2)}, u32[]{:S(2)}) collective-permute-start(bf16[256,256]{1,0:T(8,128)(2,1)S(1)} %collective-permute-done.4.refs_6_), channel_id=1, source_target_pairs={{0,4},{8,0},{16,8},{24,16},{28,24},{20,28},{12,20},{4,12},{1,5},{9... | collective-permute-start | bytes 393224 | tf_op jit(solution)/shard_map/ppermute | solution.py:471
  17.6 1.4 %collective-permute-done.2.refs_3_ = bf16[256,256]{1,0:T(8,128)(2,1)S(1)} collective-permute-done((bf16[256,256]{1,0:T(8,128)(2,1)S(1)}, bf16[256,256]{1,0:T(8,128)(2,1)S(1)}, u32[]{:S(2)}, u32[]{:S(2)}) %collective-permute-start.2) | collective-permute-done | bytes 131104 | tf_op jit(solution)/shard_map/ppermute | solution.py:471
  19.0 1.0 %collective-permute-done.5.refs_4_ = bf16[256,256]{1,0:T(8,128)(2,1)S(1)} collective-permute-done((bf16[256,256]{1,0:T(8,128)(2,1)S(1)}, bf16[256,256]{1,0:T(8,128)(2,1)S(1)}, u32[]{:S(2)}, u32[]{:S(2)}) %collective-permute-start.5) | collective-permute-done | bytes 131104 | tf_op jit(solution)/shard_map/ppermute | solution.py:475
  20.1 1.1 %collective-permute-start.6 = (bf16[256,256]{1,0:T(8,128)(2,1)S(1)}, bf16[256,256]{1,0:T(8,128)(2,1)S(1)}, u32[]{:S(2)}, u32[]{:S(2)}) collective-permute-start(bf16[256,256]{1,0:T(8,128)(2,1)S(1)} %collective-permute-done.2.refs_3_), channel_id=1, source_target_pairs={{0,8},{8,16},{16,24},{24,28},{28,20},{20,12},{12,4},{4,0},{1,9},{9... | collective-permute-start | bytes 393224 | tf_op jit(solution)/shard_map/ppermute | solution.py:471
  21.1 3.4 %build_rest.1.dense_ref = bf16[1024,2048]{1,0:T(8,128)(2,1)S(1)} custom-call(s32[513]{0:T(1024)S(1)} %add_reduce_fusion.list_ref, bf16[256,128,128]{2,1,0:T(8,128)(2,1)} %bitcast.4, bf16[1024,2048]{1,0:T(8,128)(2,1)S(1)} %build_first.1.half_ref), custom_call_target="tpu_custom_call" | custom-call | flops 4194304 | bytes 6291456 | tf_op jit(solution)/shard_map/build_rest/pallas_call | solution.py:195
  24.6 0.0 collective-permute-done.7.refs_7_
  24.6 0.4 collective-permute-done.6.refs_4_
  25.0 0.0 copy-done
  25.0 0.7 %forward_product.2 = bf16[512,256]{1,0:T(8,128)(2,1)S(1)} custom-call(bf16[1024,2048]{1,0:T(8,128)(2,1)S(1)} %build_rest.1.dense_ref, bf16[256,256]{1,0:T(8,128)(2,1)S(1)} %copy-done, bf16[256,256]{1,0:T(8,128)(2,1)S(1)} %collective-permute-done.refs_1_, bf16[256,256]{1,0:T(8,128)(2,1)S(1)} %collective-permute-done.1.refs_2_, ...), custom_call_target="tpu_custom_call" | custom-call | flops 536870912 | bytes 3407872 | tf_op jit(solution)/shard_map/forward_product/pallas_call | solution.py:247
  25.7 0.0 copy-start.1
  25.8 0.1 collective-permute-start.8
  25.8 0.7 %forward_product.3 = bf16[512,256]{1,0:T(8,128)(2,1)S(1)} custom-call(bf16[1024,2048]{1,0:T(8,128)(2,1)S(1)} %build_rest.1.dense_ref, bf16[256,256]{1,0:T(8,128)(2,1)S(1)} %copy-done, bf16[256,256]{1,0:T(8,128)(2,1)S(1)} %collective-permute-done.refs_1_, bf16[256,256]{1,0:T(8,128)(2,1)S(1)} %collective-permute-done.1.refs_2_, ...), custom_call_target="tpu_custom_call" | custom-call | flops 536870912 | bytes 3407872 | tf_op jit(solution)/shard_map/forward_product/pallas_call | solution.py:247
  26.6 0.8 %collective-permute-done.8 = bf16[512,256]{1,0:T(8,128)(2,1)S(1)} collective-permute-done((bf16[512,256]{1,0:T(8,128)(2,1)S(1)}, bf16[512,256]{1,0:T(8,128)(2,1)S(1)}, u32[]{:S(2)}, u32[]{:S(2)}) %collective-permute-start.8) | collective-permute-done | bytes 262176 | tf_op jit(solution)/shard_map/ppermute | solution.py:475
  27.4 0.1 add_convert_fusion.refs_0_
  27.4 1.6 %collective-permute-start.9 = (bf16[512,256]{1,0:T(8,128)(2,1)S(1)}, bf16[512,256]{1,0:T(8,128)(2,1)S(1)}, u32[]{:S(2)}, u32[]{:S(2)}) collective-permute-start(bf16[512,256]{1,0:T(8,128)(2,1)S(1)} %add_convert_fusion.refs_0_), channel_id=1, source_target_pairs={{0,2},{1,3},{2,0},{3,1},{4,6},{5,7},{6,4},{7,5},{8,10},{9,11},{10,... | collective-permute-start | bytes 786440 | tf_op jit(solution)/shard_map/ppermute | solution.py:475
  29.0 6.8 %collective-permute-done.9.refs_1_ = bf16[512,256]{1,0:T(8,128)(2,1)S(1)} collective-permute-done((bf16[512,256]{1,0:T(8,128)(2,1)S(1)}, bf16[512,256]{1,0:T(8,128)(2,1)S(1)}, u32[]{:S(2)}, u32[]{:S(2)}) %collective-permute-start.9) | collective-permute-done | bytes 262176 | tf_op jit(solution)/shard_map/ppermute | solution.py:475
  35.8 0.0 copy-done.1
  35.8 1.0 %middle.1 = (bf16[256,256]{1,0:T(8,128)(2,1)}, bf16[768,256]{1,0:T(8,128)(2,1)S(1)}, f32[128,256]{1,0:T(8,128)S(1)}) custom-call(bf16[512,256]{1,0:T(8,128)(2,1)S(1)} %add_convert_fusion.refs_0_, bf16[512,256]{1,0:T(8,128)(2,1)S(1)} %collective-permute-done.9.refs_1_, bf16[256,256]{1,0:T(8,128)(2,1)S(1)} %copy-done.1, bf16[256,256]{1,0:T(8,128)(2,1)S(1)} %copy-done.2, ...), custom_call_target="tpu_custom_call" | custom-call | flops 335544320 | bytes 1572864 | tf_op jit(solution)/shard_map/middle/pallas_call | solution.py:311
  36.9 0.1 collective-permute-start.10
  37.0 1.7 %collective-permute-done.10.sibling_ref = bf16[768,256]{1,0:T(8,128)(2,1)S(1)} collective-permute-done((bf16[768,256]{1,0:T(8,128)(2,1)S(1)}, bf16[768,256]{1,0:T(8,128)(2,1)S(1)}, u32[]{:S(2)}, u32[]{:S(2)}) %collective-permute-start.10) | collective-permute-done | bytes 393248 | tf_op jit(solution)/shard_map/ppermute | solution.py:475
  38.7 0.5 backward_product.2
  39.1 1.1 %collective-permute-start.15 = (bf16[256,256]{1,0:T(8,128)(2,1)S(1)}, bf16[256,256]{1,0:T(8,128)(2,1)S(1)}, u32[]{:S(2)}, u32[]{:S(2)}) collective-permute-start(bf16[256,256]{1,0:T(8,128)(2,1)S(1)} %get-tuple-element.59), channel_id=1, source_target_pairs={{0,4},{8,0},{16,8},{24,16},{28,24},{20,28},{12,20},{4,12},{1,5},{9... | collective-permute-start | bytes 393224 | tf_op jit(solution)/shard_map/ppermute | solution.py:471
  40.2 1.1 %collective-permute-start.11 = (bf16[256,256]{1,0:T(8,128)(2,1)S(1)}, bf16[256,256]{1,0:T(8,128)(2,1)S(1)}, u32[]{:S(2)}, u32[]{:S(2)}) collective-permute-start(bf16[256,256]{1,0:T(8,128)(2,1)S(1)} %get-tuple-element.55), channel_id=1, source_target_pairs={{0,8},{8,16},{16,24},{24,28},{28,20},{20,12},{12,4},{4,0},{1,9},{9... | collective-permute-start | bytes 393224 | tf_op jit(solution)/shard_map/ppermute | solution.py:471
  41.3 1.3 %backward_product.3 = (bf16[384,256]{1,0:T(8,128)(2,1)S(1)}, bf16[384,256]{1,0:T(8,128)(2,1)S(1)}, bf16[256,256]{1,0:T(8,128)(2,1)S(1)}, bf16[384,256]{1,0:T(8,1...) custom-call(bf16[1024,2048]{1,0:T(8,128)(2,1)S(1)} %build_rest.1.dense_ref, ...), custom_call_target="tpu_custom_call" | custom-call | flops 134217728 | bytes 917504 | tf_op jit(solution)/shard_map/backward_product/pallas_call | solution.py:372
  42.6 2.4 %collective-permute-done.15.refs_2_ = bf16[256,256]{1,0:T(8,128)(2,1)S(1)} collective-permute-done((bf16[256,256]{1,0:T(8,128)(2,1)S(1)}, bf16[256,256]{1,0:T(8,128)(2,1)S(1)}, u32[]{:S(2)}, u32[]{:S(2)}) %collective-permute-start.15) | collective-permute-done | bytes 131104 | tf_op jit(solution)/shard_map/ppermute | solution.py:471
  45.1 0.8 %collective-permute-start.16 = (bf16[384,256]{1,0:T(8,128)(2,1)S(1)}, bf16[384,256]{1,0:T(8,128)(2,1)S(1)}, u32[]{:S(2)}, u32[]{:S(2)}) collective-permute-start(bf16[384,256]{1,0:T(8,128)(2,1)S(1)} %add_convert_fusion.3), channel_id=1, source_target_pairs={{0,4},{8,0},{16,8},{24,16},{28,24},{20,28},{12,20},{4,12},{1,5},{9... | collective-permute-start | bytes 589832 | tf_op jit(solution)/shard_map/ppermute | solution.py:471
  45.8 0.0 collective-permute-done.11.refs_1_
  45.9 1.4 %collective-permute-start.12 = (bf16[384,256]{1,0:T(8,128)(2,1)S(1)}, bf16[384,256]{1,0:T(8,128)(2,1)S(1)}, u32[]{:S(2)}, u32[]{:S(2)}) collective-permute-start(bf16[384,256]{1,0:T(8,128)(2,1)S(1)} %add_convert_fusion.5), channel_id=1, source_target_pairs={{0,8},{8,16},{16,24},{24,28},{28,20},{20,12},{12,4},{4,0},{1,9},{9... | collective-permute-start | bytes 589832 | tf_op jit(solution)/shard_map/ppermute | solution.py:471
  47.2 4.3 %collective-permute-done.16.refs_4_ = bf16[384,256]{1,0:T(8,128)(2,1)S(1)} collective-permute-done((bf16[384,256]{1,0:T(8,128)(2,1)S(1)}, bf16[384,256]{1,0:T(8,128)(2,1)S(1)}, u32[]{:S(2)}, u32[]{:S(2)}) %collective-permute-start.16) | collective-permute-done | bytes 196640 | tf_op jit(solution)/shard_map/ppermute | solution.py:471
  51.6 0.1 add_convert_fusion.2
  51.6 0.4 collective-permute-start.17
  52.0 0.0 collective-permute-done.12.refs_3_
  52.1 0.1 add_convert_fusion.4
  52.1 1.7 %collective-permute-start.13 = (bf16[384,256]{1,0:T(8,128)(2,1)S(1)}, bf16[384,256]{1,0:T(8,128)(2,1)S(1)}, u32[]{:S(2)}, u32[]{:S(2)}) collective-permute-start(bf16[384,256]{1,0:T(8,128)(2,1)S(1)} %add_convert_fusion.4), channel_id=1, source_target_pairs={{0,8},{8,16},{16,24},{24,28},{28,20},{20,12},{12,4},{4,0},{1,9},{9... | collective-permute-start | bytes 589832 | tf_op jit(solution)/shard_map/ppermute | solution.py:471
  53.8 3.5 %collective-permute-done.17.refs_6_ = bf16[384,256]{1,0:T(8,128)(2,1)S(1)} collective-permute-done((bf16[384,256]{1,0:T(8,128)(2,1)S(1)}, bf16[384,256]{1,0:T(8,128)(2,1)S(1)}, u32[]{:S(2)}, u32[]{:S(2)}) %collective-permute-start.17) | collective-permute-done | bytes 196640 | tf_op jit(solution)/shard_map/ppermute | solution.py:471
  57.3 0.1 add_convert_fusion.1
  57.4 0.4 collective-permute-start.18
  57.8 0.0 collective-permute-done.13.refs_5_
  57.9 1.7 %collective-permute-start.14 = (bf16[256,256]{1,0:T(8,128)(2,1)S(1)}, bf16[256,256]{1,0:T(8,128)(2,1)S(1)}, u32[]{:S(2)}, u32[]{:S(2)}) collective-permute-start(bf16[256,256]{1,0:T(8,128)(2,1)S(1)} %add_convert_fusion.6), channel_id=1, source_target_pairs={{0,8},{8,16},{16,24},{24,28},{28,20},{20,12},{12,4},{4,0},{1,9},{9... | collective-permute-start | bytes 393224 | tf_op jit(solution)/shard_map/ppermute | solution.py:471
  59.6 3.5 %collective-permute-done.18.refs_2_.refs_7_ = bf16[384,256]{1,0:T(8,128)(2,1)S(1)} collective-permute-done((bf16[384,256]{1,0:T(8,128)(2,1)S(1)}, bf16[384,256]{1,0:T(8,128)(2,1)S(1)}, u32[]{:S(2)}, u32[]{:S(2)}) %collective-permute-start.18) | collective-permute-done | bytes 196640 | tf_op jit(solution)/shard_map/ppermute | solution.py:471
  63.1 0.1 summed_terms.1.own_ref
  63.3 0.1 collective-permute-start.19
  63.3 0.0 collective-permute-done.14.refs_1_
  63.3 0.8 %finish.1 = bf16[256,256]{1,0:T(8,128)(2,1)} custom-call(bf16[256,256]{1,0:T(8,128)(2,1)S(1)} %get-tuple-element.51.refs_0_, bf16[256,256]{1,0:T(8,128)(2,1)S(1)} %collective-permute-done.14.refs_1_, bf16[384,256]{1,0:T(8,128)(2,1)S(1)} %collective-permute-done.18.refs_2_.refs_7_), custom_call_target="tpu_custom_call" | custom-call | flops 196608 | bytes 524288 | tf_op jit(solution)/shard_map/finish/pallas_call | solution.py:435
  64.1 0.6 collective-permute-done.19.sibling_ref
  64.7 0.7 %joined.1 = f32[256,256]{1,0:T(8,128)} custom-call(f32[128,256]{1,0:T(8,128)S(1)} %summed_terms.1.own_ref, f32[128,256]{1,0:T(8,128)S(1)} %collective-permute-done.19.sibling_ref), custom_call_target="tpu_custom_call" | custom-call | bytes 524288 | tf_op jit(solution)/shard_map/joined/pallas_call | solution.py:457
  (3 shorter events, 0.1 us)
Async XLA Ops:
  0.6 6.8 %collective-permute-start.3 = (bf16[256,256]{1,0:T(8,128)(2,1)}, bf16[256,256]{1,0:T(8,128)(2,1)S(1)}, u32[]{:S(2)}, u32[]{:S(2)}) collective-permute-start(bf16[256,256]{1,0:T(8,128)(2,1)} %refs_0_.3), channel_id=1, source_target_pairs={{0,4},{8,0},{16,8},{24,16},{28,24},{20,28},{12,20},{4,12},{1,5},{9... | collective-permute-start | bytes 393224 | tf_op jit(solution)/shard_map/ppermute | solution.py:471
  3.6 5.5 %collective-permute-start = (bf16[256,256]{1,0:T(8,128)(2,1)}, bf16[256,256]{1,0:T(8,128)(2,1)S(1)}, u32[]{:S(2)}, u32[]{:S(2)}) collective-permute-start(bf16[256,256]{1,0:T(8,128)(2,1)} %refs_0_.3), channel_id=1, source_target_pairs={{0,8},{8,16},{16,24},{24,28},{28,20},{20,12},{12,4},{4,0},{1,9},{9... | collective-permute-start | bytes 393224 | tf_op jit(solution)/shard_map/ppermute | solution.py:471
  7.4 5.9 %collective-permute-start.4 = (bf16[256,256]{1,0:T(8,128)(2,1)S(1)}, bf16[256,256]{1,0:T(8,128)(2,1)S(1)}, u32[]{:S(2)}, u32[]{:S(2)}) collective-permute-start(bf16[256,256]{1,0:T(8,128)(2,1)S(1)} %collective-permute-done.3.refs_5_), channel_id=1, source_target_pairs={{0,4},{8,0},{16,8},{24,16},{28,24},{20,28},{12,20},{4,12},{1,5},{9... | collective-permute-start | bytes 393224 | tf_op jit(solution)/shard_map/ppermute | solution.py:471
  9.1 5.0 %collective-permute-start.1 = (bf16[256,256]{1,0:T(8,128)(2,1)S(1)}, bf16[256,256]{1,0:T(8,128)(2,1)S(1)}, u32[]{:S(2)}, u32[]{:S(2)}) collective-permute-start(bf16[256,256]{1,0:T(8,128)(2,1)S(1)} %collective-permute-done.refs_1_), channel_id=1, source_target_pairs={{0,8},{8,16},{16,24},{24,28},{28,20},{20,12},{12,4},{4,0},{1,9},{9... | collective-permute-start | bytes 393224 | tf_op jit(solution)/shard_map/ppermute | solution.py:471
  9.4 5.6 %copy-start.2 = (bf16[256,256]{1,0:T(8,128)(2,1)S(1)}, bf16[256,256]{1,0:T(8,128)(2,1)}, u32[]{:S(2)}) copy-start(bf16[256,256]{1,0:T(8,128)(2,1)} %refs_3_) | copy-start | bytes 393220
  13.3 11.7 %copy-start = (bf16[256,256]{1,0:T(8,128)(2,1)S(1)}, bf16[256,256]{1,0:T(8,128)(2,1)}, u32[]{:S(2)}) copy-start(bf16[256,256]{1,0:T(8,128)(2,1)} %refs_0_.3) | copy-start | bytes 393220
  14.1 5.0 %collective-permute-start.2 = (bf16[256,256]{1,0:T(8,128)(2,1)S(1)}, bf16[256,256]{1,0:T(8,128)(2,1)S(1)}, u32[]{:S(2)}, u32[]{:S(2)}) collective-permute-start(bf16[256,256]{1,0:T(8,128)(2,1)S(1)} %collective-permute-done.1.refs_2_), channel_id=1, source_target_pairs={{0,8},{8,16},{16,24},{24,28},{28,20},{20,12},{12,4},{4,0},{1,9},{9... | collective-permute-start | bytes 393224 | tf_op jit(solution)/shard_map/ppermute | solution.py:471
  15.1 5.0 %collective-permute-start.5 = (bf16[256,256]{1,0:T(8,128)(2,1)S(1)}, bf16[256,256]{1,0:T(8,128)(2,1)S(1)}, u32[]{:S(2)}, u32[]{:S(2)}) collective-permute-start(bf16[256,256]{1,0:T(8,128)(2,1)S(1)} %copy-done.2), channel_id=1, source_target_pairs={{0,2},{1,3},{2,0},{3,1},{4,6},{5,7},{6,4},{7,5},{8,10},{9,11},{10,... | collective-permute-start | bytes 393224 | tf_op jit(solution)/shard_map/ppermute | solution.py:475
  16.6 8.0 %collective-permute-start.7 = (bf16[256,256]{1,0:T(8,128)(2,1)S(1)}, bf16[256,256]{1,0:T(8,128)(2,1)S(1)}, u32[]{:S(2)}, u32[]{:S(2)}) collective-permute-start(bf16[256,256]{1,0:T(8,128)(2,1)S(1)} %collective-permute-done.4.refs_6_), channel_id=1, source_target_pairs={{0,4},{8,0},{16,8},{24,16},{28,24},{20,28},{12,20},{4,12},{1,5},{9... | collective-permute-start | bytes 393224 | tf_op jit(solution)/shard_map/ppermute | solution.py:471
  20.1 5.0 %collective-permute-start.6 = (bf16[256,256]{1,0:T(8,128)(2,1)S(1)}, bf16[256,256]{1,0:T(8,128)(2,1)S(1)}, u32[]{:S(2)}, u32[]{:S(2)}) collective-permute-start(bf16[256,256]{1,0:T(8,128)(2,1)S(1)} %collective-permute-done.2.refs_3_), channel_id=1, source_target_pairs={{0,8},{8,16},{16,24},{24,28},{28,20},{20,12},{12,4},{4,0},{1,9},{9... | collective-permute-start | bytes 393224 | tf_op jit(solution)/shard_map/ppermute | solution.py:471
  25.7 10.1 %copy-start.1 = (bf16[256,256]{1,0:T(8,128)(2,1)S(1)}, bf16[256,256]{1,0:T(8,128)(2,1)}, u32[]{:S(2)}) copy-start(bf16[256,256]{1,0:T(8,128)(2,1)} %refs_2_.1) | copy-start | bytes 393220
  25.8 1.6 %collective-permute-start.8 = (bf16[512,256]{1,0:T(8,128)(2,1)S(1)}, bf16[512,256]{1,0:T(8,128)(2,1)S(1)}, u32[]{:S(2)}, u32[]{:S(2)}) collective-permute-start(bf16[512,256]{1,0:T(8,128)(2,1)S(1)} %forward_product.2), channel_id=1, source_target_pairs={{0,1},{1,0},{2,3},{3,2},{4,5},{5,4},{6,7},{7,6},{8,9},{9,8},{10,11... | collective-permute-start | bytes 786440 | tf_op jit(solution)/shard_map/ppermute | solution.py:475
  27.4 8.4 %collective-permute-start.9 = (bf16[512,256]{1,0:T(8,128)(2,1)S(1)}, bf16[512,256]{1,0:T(8,128)(2,1)S(1)}, u32[]{:S(2)}, u32[]{:S(2)}) collective-permute-start(bf16[512,256]{1,0:T(8,128)(2,1)S(1)} %add_convert_fusion.refs_0_), channel_id=1, source_target_pairs={{0,2},{1,3},{2,0},{3,1},{4,6},{5,7},{6,4},{7,5},{8,10},{9,11},{10,... | collective-permute-start | bytes 786440 | tf_op jit(solution)/shard_map/ppermute | solution.py:475
  36.9 1.8 %collective-permute-start.10 = (bf16[768,256]{1,0:T(8,128)(2,1)S(1)}, bf16[768,256]{1,0:T(8,128)(2,1)S(1)}, u32[]{:S(2)}, u32[]{:S(2)}) collective-permute-start(bf16[768,256]{1,0:T(8,128)(2,1)S(1)} %get-tuple-element.45.own_ref), channel_id=1, source_target_pairs={{0,1},{1,0},{2,3},{3,2},{4,5},{5,4},{6,7},{7,6},{8,9},{9,8},{10,11... | collective-permute-start | bytes 1179656 | tf_op jit(solution)/shard_map/ppermute | solution.py:475
  39.1 5.9 %collective-permute-start.15 = (bf16[256,256]{1,0:T(8,128)(2,1)S(1)}, bf16[256,256]{1,0:T(8,128)(2,1)S(1)}, u32[]{:S(2)}, u32[]{:S(2)}) collective-permute-start(bf16[256,256]{1,0:T(8,128)(2,1)S(1)} %get-tuple-element.59), channel_id=1, source_target_pairs={{0,4},{8,0},{16,8},{24,16},{28,24},{20,28},{12,20},{4,12},{1,5},{9... | collective-permute-start | bytes 393224 | tf_op jit(solution)/shard_map/ppermute | solution.py:471
  40.2 5.6 %collective-permute-start.11 = (bf16[256,256]{1,0:T(8,128)(2,1)S(1)}, bf16[256,256]{1,0:T(8,128)(2,1)S(1)}, u32[]{:S(2)}, u32[]{:S(2)}) collective-permute-start(bf16[256,256]{1,0:T(8,128)(2,1)S(1)} %get-tuple-element.55), channel_id=1, source_target_pairs={{0,8},{8,16},{16,24},{24,28},{28,20},{20,12},{12,4},{4,0},{1,9},{9... | collective-permute-start | bytes 393224 | tf_op jit(solution)/shard_map/ppermute | solution.py:471
  45.1 6.5 %collective-permute-start.16 = (bf16[384,256]{1,0:T(8,128)(2,1)S(1)}, bf16[384,256]{1,0:T(8,128)(2,1)S(1)}, u32[]{:S(2)}, u32[]{:S(2)}) collective-permute-start(bf16[384,256]{1,0:T(8,128)(2,1)S(1)} %add_convert_fusion.3), channel_id=1, source_target_pairs={{0,4},{8,0},{16,8},{24,16},{28,24},{20,28},{12,20},{4,12},{1,5},{9... | collective-permute-start | bytes 589832 | tf_op jit(solution)/shard_map/ppermute | solution.py:471
  45.9 6.2 %collective-permute-start.12 = (bf16[384,256]{1,0:T(8,128)(2,1)S(1)}, bf16[384,256]{1,0:T(8,128)(2,1)S(1)}, u32[]{:S(2)}, u32[]{:S(2)}) collective-permute-start(bf16[384,256]{1,0:T(8,128)(2,1)S(1)} %add_convert_fusion.5), channel_id=1, source_target_pairs={{0,8},{8,16},{16,24},{24,28},{28,20},{20,12},{12,4},{4,0},{1,9},{9... | collective-permute-start | bytes 589832 | tf_op jit(solution)/shard_map/ppermute | solution.py:471
  51.6 5.7 %collective-permute-start.17 = (bf16[384,256]{1,0:T(8,128)(2,1)S(1)}, bf16[384,256]{1,0:T(8,128)(2,1)S(1)}, u32[]{:S(2)}, u32[]{:S(2)}) collective-permute-start(bf16[384,256]{1,0:T(8,128)(2,1)S(1)} %add_convert_fusion.2), channel_id=1, source_target_pairs={{0,4},{8,0},{16,8},{24,16},{28,24},{20,28},{12,20},{4,12},{1,5},{9... | collective-permute-start | bytes 589832 | tf_op jit(solution)/shard_map/ppermute | solution.py:471
  52.1 5.7 %collective-permute-start.13 = (bf16[384,256]{1,0:T(8,128)(2,1)S(1)}, bf16[384,256]{1,0:T(8,128)(2,1)S(1)}, u32[]{:S(2)}, u32[]{:S(2)}) collective-permute-start(bf16[384,256]{1,0:T(8,128)(2,1)S(1)} %add_convert_fusion.4), channel_id=1, source_target_pairs={{0,8},{8,16},{16,24},{24,28},{28,20},{20,12},{12,4},{4,0},{1,9},{9... | collective-permute-start | bytes 589832 | tf_op jit(solution)/shard_map/ppermute | solution.py:471
  57.4 5.7 %collective-permute-start.18 = (bf16[384,256]{1,0:T(8,128)(2,1)S(1)}, bf16[384,256]{1,0:T(8,128)(2,1)S(1)}, u32[]{:S(2)}, u32[]{:S(2)}) collective-permute-start(bf16[384,256]{1,0:T(8,128)(2,1)S(1)} %add_convert_fusion.1), channel_id=1, source_target_pairs={{0,4},{8,0},{16,8},{24,16},{28,24},{20,28},{12,20},{4,12},{1,5},{9... | collective-permute-start | bytes 589832 | tf_op jit(solution)/shard_map/ppermute | solution.py:471
  57.9 5.4 %collective-permute-start.14 = (bf16[256,256]{1,0:T(8,128)(2,1)S(1)}, bf16[256,256]{1,0:T(8,128)(2,1)S(1)}, u32[]{:S(2)}, u32[]{:S(2)}) collective-permute-start(bf16[256,256]{1,0:T(8,128)(2,1)S(1)} %add_convert_fusion.6), channel_id=1, source_target_pairs={{0,8},{8,16},{16,24},{24,28},{28,20},{20,12},{12,4},{4,0},{1,9},{9... | collective-permute-start | bytes 393224 | tf_op jit(solution)/shard_map/ppermute | solution.py:471
  63.3 1.4 %collective-permute-start.19 = (f32[128,256]{1,0:T(8,128)S(1)}, f32[128,256]{1,0:T(8,128)S(1)}, u32[]{:S(2)}, u32[]{:S(2)}) collective-permute-start(f32[128,256]{1,0:T(8,128)S(1)} %summed_terms.1.own_ref), channel_id=1, source_target_pairs={{0,1},{1,0},{2,3},{3,2},{4,5},{5,4},{6,7},{7,6},{8,9},{9,8},{10,11... | collective-permute-start | bytes 393224 | tf_op jit(solution)/shard_map/ppermute | solution.py:475

commit v18 on v13

--- a/solution.py
+++ b/solution.py
@@ -9,7 +9,7 @@
 from jax.sharding import PartitionSpec as P
 
 chunk_tiles = 16
-chunk_slots = 8
+chunk_slots = 16
 build_grant = 44
 strips_per_step = 8
 mib = 1024 * 1024
@@ -84,7 +84,7 @@
 
 
 def first_chunks(list_ref, tiles_ref):
-    return (live_chunks(list_ref, tiles_ref) * 3 + 7) // 8
+    return (live_chunks(list_ref, tiles_ref) * 7 + 15) // 16
 
 
 def build_first_kernel(list_ref, tiles_ref, dense_ref, total, held, sems, *, blocks):
@@ -506,7 +506,7 @@
 def scattered_sums(dense, own, sibling, chunk):
     row_count, col_count = lax.axis_size("row"), lax.axis_size("col")
     size, width = chunk.shape
-    half, half_size = width // 2, size // 2
+    half = width // 2
     reach = row_count // 2
     strip, terms, zeros = ("strip", 0, width), ("terms", 0, size), ("zeros", 0, size)
     first = (
@@ -519,19 +519,18 @@
     up, down = around(above, 1), around(below, -1)
     all_terms = [(0, 0, size, 0, terms)]
 
-    few_zeros = ("zeros", 0, half_size)
-    ups = tuple((offset, (zeros if offset > 1 else few_zeros, strip)) for offset in range(reach - 1, 0, -1))
-    downs = tuple((-offset, (strip, zeros if offset > 1 else few_zeros)) for offset in range(reach - 1, 0, -1))
+    ups = tuple((offset, (zeros, strip) if offset > 1 else (strip,)) for offset in range(reach - 1, 0, -1))
+    downs = tuple((-offset, (strip, zeros)) for offset in range(reach - 1, 0, -1))
     strips = backward_product(cell, own, sibling, chunk, ups + downs + ((0, (strip,)),), row_count, col_count)
     ups, downs, mine = strips[: reach - 1], strips[reach - 1 : -1], strips[-1]
     for step in range(1, reach):
         all_terms += [(-step, 0, size, 0, up), (step, down.shape[0] - size, size, 0, down)]
         if step == reach - 1:
-            up, down = up[half_size:], down[: width + half_size]
+            up = up[size:]
         up = around(added(ups[step - 1], up), 1)
         down = around(added(downs[step - 1], down, half if step == 1 else 0), -1)
-    all_terms += [(reach, 0, half_size, half_size, up), (reach, width, half_size, 0, down)]
-    return [(0, mine), (half_size, up), (0, down)], summed_terms(all_terms, size, row_count)
+    all_terms.append((reach, width, size, 0, down))
+    return [(0, mine), (0, up), (0, down)], summed_terms(all_terms, size, row_count)
 
 
 def per_device(features, weight, adj_tiles, tile_rows, tile_cols, tile_counts, out_grad):

time: 66 us -> 65.3 us (0.989)
  Pallas kernels: 14.2 us -> 11.3 us
  waiting for transfers between devices: 28.8 us -> 30.5 us
    pallas_call x1, Pallas kernels: 4.7 us -> 2.73 us  [build_stages(): pl.pallas_call(functools.partial(build_rest_kernel, blocks=blocks), out_s...]
    ppermute x15, waiting for transfers between devices: 18.9 us -> 20.6 us  [around(): lax.ppermute(value, 'row', [(order[i], order[(i + step) % count]) for i i...]
    pallas_call x1, Pallas kernels: 3.69 us -> 2.72 us  [build_stages(): pl.pallas_call(functools.partial(build_first_kernel, blocks=blocks), out_...]
  transfers between devices with their start and end apart: 20 -> 20, of which waited for: 13 -> 13; matrix products, arithmetic and copies ran while one was open for 1% -> 1% of each run, Pallas kernels for 17% -> 13%
where the time goes in v18:
time: 65.3 us; the launch traced here: 65.2 us
  waiting for transfers between devices  30.5 us (47%)
  starting transfers between devices  20.9 us (32%)
  Pallas kernels  11.3 us (17%)
  between operations  1.44 us (2%)
  other arithmetic  1.04 us (2%)
    ppermute x15, waiting for transfers between devices, around(): lax.ppermute(value, 'row', [(order[i], order[(i + step) % count]) for i i...  20.6 us
    ppermute x15, starting transfers between devices, around(): lax.ppermute(value, 'row', [(order[i], order[(i + step) % count]) for i i...  17.4 us
    ppermute x5, waiting for transfers between devices, swapped(): lax.ppermute(value, axis, [(i, i ^ partner) for i in range(lax.axis_size(...  9.81 us
    ppermute x5, starting transfers between devices, swapped(): lax.ppermute(value, axis, [(i, i ^ partner) for i in range(lax.axis_size(...  3.53 us
    pallas_call x1, Pallas kernels, build_stages(): pl.pallas_call(functools.partial(build_rest_kernel, blocks=blocks), out_s...  2.73 us
    pallas_call x1, Pallas kernels, build_stages(): pl.pallas_call(functools.partial(build_first_kernel, blocks=blocks), out_...  2.72 us
    pallas_call x2, Pallas kernels, backward_product(): pl.pallas_call(functools.partial(backward_kernel, outputs=outputs, row_co...  1.74 us
    pallas_call x2, Pallas kernels, forward_product(): pl.pallas_call(functools.partial(forward_kernel, pieces=pieces, sibling=s...  1.42 us
  transfers between devices with their start and end apart: 20, of which 13 were waited for; matrix products, arithmetic and copies ran while one was open for 1% of the time, Pallas kernels for 13%

profile of v18, /device:TPU:0, one launch (start us, length us, event | category | flops | bytes accessed | tf_op | source)
XLA Modules:
  0.0 65.2 jit_solution(13596417279600748199)
XLA Ops:
  0.6 3.0 %collective-permute-start.3 = (bf16[256,256]{1,0:T(8,128)(2,1)}, bf16[256,256]{1,0:T(8,128)(2,1)S(1)}, u32[]{:S(2)}, u32[]{:S(2)}) collective-permute-start(bf16[256,256]{1,0:T(8,128)(2,1)} %refs_0_.3), channel_id=1, source_target_pairs={{0,4},{8,0},{16,8},{24,16},{28,24},{20,28},{12,20},{4,12},{1,5},{9... | collective-permute-start | bytes 393224 | tf_op jit(solution)/shard_map/ppermute | solution.py:465
  3.6 0.1 collective-permute-start
  4.4 0.7 %add_reduce_fusion.list_ref = s32[513]{0:T(1024)S(1)} fusion(s32[1,1,1]{2,1,0:T(1,128)} %bitcast.2, s32[1,1,256]{2,1,0:T(1,128)} %param.11, s32[1,1,256]{2,1,0:T(1,128)} %param.10), kind=kLoop, calls=%fused_computation.7 | loop fusion | flops 1026 | bytes 4104 | tf_op jit(solution)/shard_map/concatenate | solution.py:540
  5.1 2.3 %collective-permute-done.3.refs_5_ = bf16[256,256]{1,0:T(8,128)(2,1)S(1)} collective-permute-done((bf16[256,256]{1,0:T(8,128)(2,1)}, bf16[256,256]{1,0:T(8,128)(2,1)S(1)}, u32[]{:S(2)}, u32[]{:S(2)}) %collective-permute-start.3) | collective-permute-done | bytes 131104 | tf_op jit(solution)/shard_map/ppermute | solution.py:465
  7.4 1.7 %collective-permute-start.4 = (bf16[256,256]{1,0:T(8,128)(2,1)S(1)}, bf16[256,256]{1,0:T(8,128)(2,1)S(1)}, u32[]{:S(2)}, u32[]{:S(2)}) collective-permute-start(bf16[256,256]{1,0:T(8,128)(2,1)S(1)} %collective-permute-done.3.refs_5_), channel_id=1, source_target_pairs={{0,4},{8,0},{16,8},{24,16},{28,24},{20,28},{12,20},{4,12},{1,5},{9... | collective-permute-start | bytes 393224 | tf_op jit(solution)/shard_map/ppermute | solution.py:465
  9.1 0.0 collective-permute-done.refs_1_
  9.1 0.3 collective-permute-start.1
  9.4 0.0 copy-start.2
  9.4 2.7 %build_first.1.half_ref = bf16[1024,2048]{1,0:T(8,128)(2,1)S(1)} custom-call(s32[513]{0:T(1024)S(1)} %add_reduce_fusion.list_ref, bf16[256,128,128]{2,1,0:T(8,128)(2,1)} %bitcast.3), custom_call_target="tpu_custom_call" | custom-call | flops 4194304 | bytes 6291456 | tf_op jit(solution)/shard_map/build_first/pallas_call | solution.py:179
  12.2 0.0 copy-start
  12.2 0.2 collective-permute-done.4.refs_6_
  12.4 1.7 %collective-permute-done.1.refs_2_ = bf16[256,256]{1,0:T(8,128)(2,1)S(1)} collective-permute-done((bf16[256,256]{1,0:T(8,128)(2,1)S(1)}, bf16[256,256]{1,0:T(8,128)(2,1)S(1)}, u32[]{:S(2)}, u32[]{:S(2)}) %collective-permute-start.1) | collective-permute-done | bytes 131104 | tf_op jit(solution)/shard_map/ppermute | solution.py:465
  14.1 0.3 collective-permute-start.2
  14.4 0.0 copy-done.2
  14.4 1.7 %collective-permute-start.5 = (bf16[256,256]{1,0:T(8,128)(2,1)S(1)}, bf16[256,256]{1,0:T(8,128)(2,1)S(1)}, u32[]{:S(2)}, u32[]{:S(2)}) collective-permute-start(bf16[256,256]{1,0:T(8,128)(2,1)S(1)} %copy-done.2), channel_id=1, source_target_pairs={{0,2},{1,3},{2,0},{3,1},{4,6},{5,7},{6,4},{7,5},{8,10},{9,11},{10,... | collective-permute-start | bytes 393224 | tf_op jit(solution)/shard_map/ppermute | solution.py:469
  16.1 1.5 %collective-permute-start.7 = (bf16[256,256]{1,0:T(8,128)(2,1)S(1)}, bf16[256,256]{1,0:T(8,128)(2,1)S(1)}, u32[]{:S(2)}, u32[]{:S(2)}) collective-permute-start(bf16[256,256]{1,0:T(8,128)(2,1)S(1)} %collective-permute-done.4.refs_6_), channel_id=1, source_target_pairs={{0,4},{8,0},{16,8},{24,16},{28,24},{20,28},{12,20},{4,12},{1,5},{9... | collective-permute-start | bytes 393224 | tf_op jit(solution)/shard_map/ppermute | solution.py:465
  17.6 2.0 %collective-permute-done.2.refs_3_ = bf16[256,256]{1,0:T(8,128)(2,1)S(1)} collective-permute-done((bf16[256,256]{1,0:T(8,128)(2,1)S(1)}, bf16[256,256]{1,0:T(8,128)(2,1)S(1)}, u32[]{:S(2)}, u32[]{:S(2)}) %collective-permute-start.2) | collective-permute-done | bytes 131104 | tf_op jit(solution)/shard_map/ppermute | solution.py:465
  19.5 0.0 collective-permute-done.5.refs_4_
  19.5 1.8 %collective-permute-start.6 = (bf16[256,256]{1,0:T(8,128)(2,1)S(1)}, bf16[256,256]{1,0:T(8,128)(2,1)S(1)}, u32[]{:S(2)}, u32[]{:S(2)}) collective-permute-start(bf16[256,256]{1,0:T(8,128)(2,1)S(1)} %collective-permute-done.2.refs_3_), channel_id=1, source_target_pairs={{0,8},{8,16},{16,24},{24,28},{28,20},{20,12},{12,4},{4,0},{1,9},{9... | collective-permute-start | bytes 393224 | tf_op jit(solution)/shard_map/ppermute | solution.py:465
  21.3 2.7 %build_rest.1.dense_ref = bf16[1024,2048]{1,0:T(8,128)(2,1)S(1)} custom-call(s32[513]{0:T(1024)S(1)} %add_reduce_fusion.list_ref, bf16[256,128,128]{2,1,0:T(8,128)(2,1)} %bitcast.4, bf16[1024,2048]{1,0:T(8,128)(2,1)S(1)} %build_first.1.half_ref), custom_call_target="tpu_custom_call" | custom-call | flops 4194304 | bytes 6291456 | tf_op jit(solution)/shard_map/build_rest/pallas_call | solution.py:189
  24.1 0.0 collective-permute-done.7.refs_7_
  24.1 0.4 collective-permute-done.6.refs_4_
  24.5 0.0 copy-done
  24.5 0.7 %forward_product.2 = bf16[512,256]{1,0:T(8,128)(2,1)S(1)} custom-call(bf16[1024,2048]{1,0:T(8,128)(2,1)S(1)} %build_rest.1.dense_ref, bf16[256,256]{1,0:T(8,128)(2,1)S(1)} %copy-done, bf16[256,256]{1,0:T(8,128)(2,1)S(1)} %collective-permute-done.refs_1_, bf16[256,256]{1,0:T(8,128)(2,1)S(1)} %collective-permute-done.1.refs_2_, ...), custom_call_target="tpu_custom_call" | custom-call | flops 536870912 | bytes 3407872 | tf_op jit(solution)/shard_map/forward_product/pallas_call | solution.py:241
  25.2 0.0 copy-start.1
  25.2 0.1 collective-permute-start.8
  25.3 0.7 %forward_product.3 = bf16[512,256]{1,0:T(8,128)(2,1)S(1)} custom-call(bf16[1024,2048]{1,0:T(8,128)(2,1)S(1)} %build_rest.1.dense_ref, bf16[256,256]{1,0:T(8,128)(2,1)S(1)} %copy-done, bf16[256,256]{1,0:T(8,128)(2,1)S(1)} %collective-permute-done.refs_1_, bf16[256,256]{1,0:T(8,128)(2,1)S(1)} %collective-permute-done.1.refs_2_, ...), custom_call_target="tpu_custom_call" | custom-call | flops 536870912 | bytes 3407872 | tf_op jit(solution)/shard_map/forward_product/pallas_call | solution.py:241
  26.0 0.8 %collective-permute-done.8 = bf16[512,256]{1,0:T(8,128)(2,1)S(1)} collective-permute-done((bf16[512,256]{1,0:T(8,128)(2,1)S(1)}, bf16[512,256]{1,0:T(8,128)(2,1)S(1)}, u32[]{:S(2)}, u32[]{:S(2)}) %collective-permute-start.8) | collective-permute-done | bytes 262176 | tf_op jit(solution)/shard_map/ppermute | solution.py:469
  26.8 0.1 add_convert_fusion.refs_0_
  26.9 1.7 %collective-permute-start.9 = (bf16[512,256]{1,0:T(8,128)(2,1)S(1)}, bf16[512,256]{1,0:T(8,128)(2,1)S(1)}, u32[]{:S(2)}, u32[]{:S(2)}) collective-permute-start(bf16[512,256]{1,0:T(8,128)(2,1)S(1)} %add_convert_fusion.refs_0_), channel_id=1, source_target_pairs={{0,2},{1,3},{2,0},{3,1},{4,6},{5,7},{6,4},{7,5},{8,10},{9,11},{10,... | collective-permute-start | bytes 786440 | tf_op jit(solution)/shard_map/ppermute | solution.py:469
  28.6 6.7 %collective-permute-done.9.refs_1_ = bf16[512,256]{1,0:T(8,128)(2,1)S(1)} collective-permute-done((bf16[512,256]{1,0:T(8,128)(2,1)S(1)}, bf16[512,256]{1,0:T(8,128)(2,1)S(1)}, u32[]{:S(2)}, u32[]{:S(2)}) %collective-permute-start.9) | collective-permute-done | bytes 262176 | tf_op jit(solution)/shard_map/ppermute | solution.py:469
  35.3 0.0 copy-done.1
  35.3 1.0 %middle.1 = (bf16[256,256]{1,0:T(8,128)(2,1)}, bf16[768,256]{1,0:T(8,128)(2,1)S(1)}, f32[128,256]{1,0:T(8,128)S(1)}) custom-call(bf16[512,256]{1,0:T(8,128)(2,1)S(1)} %add_convert_fusion.refs_0_, bf16[512,256]{1,0:T(8,128)(2,1)S(1)} %collective-permute-done.9.refs_1_, bf16[256,256]{1,0:T(8,128)(2,1)S(1)} %copy-done.1, bf16[256,256]{1,0:T(8,128)(2,1)S(1)} %copy-done.2, ...), custom_call_target="tpu_custom_call" | custom-call | flops 335544320 | bytes 1572864 | tf_op jit(solution)/shard_map/middle/pallas_call | solution.py:305
  36.4 0.1 collective-permute-start.10
  36.4 1.7 %collective-permute-done.10.sibling_ref = bf16[768,256]{1,0:T(8,128)(2,1)S(1)} collective-permute-done((bf16[768,256]{1,0:T(8,128)(2,1)S(1)}, bf16[768,256]{1,0:T(8,128)(2,1)S(1)}, u32[]{:S(2)}, u32[]{:S(2)}) %collective-permute-start.10) | collective-permute-done | bytes 393248 | tf_op jit(solution)/shard_map/ppermute | solution.py:469
  38.1 0.5 backward_product.2
  38.6 1.7 %collective-permute-start.15 = (bf16[256,256]{1,0:T(8,128)(2,1)S(1)}, bf16[256,256]{1,0:T(8,128)(2,1)S(1)}, u32[]{:S(2)}, u32[]{:S(2)}) collective-permute-start(bf16[256,256]{1,0:T(8,128)(2,1)S(1)} %get-tuple-element.59), channel_id=1, source_target_pairs={{0,4},{8,0},{16,8},{24,16},{28,24},{20,28},{12,20},{4,12},{1,5},{9... | collective-permute-start | bytes 393224 | tf_op jit(solution)/shard_map/ppermute | solution.py:465
  40.3 0.5 collective-permute-start.11
  40.8 1.3 %backward_product.3 = (bf16[384,256]{1,0:T(8,128)(2,1)S(1)}, bf16[384,256]{1,0:T(8,128)(2,1)S(1)}, bf16[256,256]{1,0:T(8,128)(2,1)S(1)}, bf16[384,256]{1,0:T(8,1...) custom-call(bf16[1024,2048]{1,0:T(8,128)(2,1)S(1)} %build_rest.1.dense_ref, ...), custom_call_target="tpu_custom_call" | custom-call | flops 134217728 | bytes 917504 | tf_op jit(solution)/shard_map/backward_product/pallas_call | solution.py:366
  42.1 2.4 %collective-permute-done.15.refs_2_ = bf16[256,256]{1,0:T(8,128)(2,1)S(1)} collective-permute-done((bf16[256,256]{1,0:T(8,128)(2,1)S(1)}, bf16[256,256]{1,0:T(8,128)(2,1)S(1)}, u32[]{:S(2)}, u32[]{:S(2)}) %collective-permute-start.15) | collective-permute-done | bytes 131104 | tf_op jit(solution)/shard_map/ppermute | solution.py:465
  44.6 1.4 %collective-permute-start.16 = (bf16[384,256]{1,0:T(8,128)(2,1)S(1)}, bf16[384,256]{1,0:T(8,128)(2,1)S(1)}, u32[]{:S(2)}, u32[]{:S(2)}) collective-permute-start(bf16[384,256]{1,0:T(8,128)(2,1)S(1)} %add_convert_fusion.3), channel_id=1, source_target_pairs={{0,4},{8,0},{16,8},{24,16},{28,24},{20,28},{12,20},{4,12},{1,5},{9... | collective-permute-start | bytes 589832 | tf_op jit(solution)/shard_map/ppermute | solution.py:465
  46.0 0.0 collective-permute-done.11.refs_1_
  46.0 0.8 %collective-permute-start.12 = (bf16[384,256]{1,0:T(8,128)(2,1)S(1)}, bf16[384,256]{1,0:T(8,128)(2,1)S(1)}, u32[]{:S(2)}, u32[]{:S(2)}) collective-permute-start(bf16[384,256]{1,0:T(8,128)(2,1)S(1)} %add_convert_fusion.5), channel_id=1, source_target_pairs={{0,8},{8,16},{16,24},{24,28},{28,20},{20,12},{12,4},{4,0},{1,9},{9... | collective-permute-start | bytes 589832 | tf_op jit(solution)/shard_map/ppermute | solution.py:465
  46.8 4.5 %collective-permute-done.16.refs_4_ = bf16[384,256]{1,0:T(8,128)(2,1)S(1)} collective-permute-done((bf16[384,256]{1,0:T(8,128)(2,1)S(1)}, bf16[384,256]{1,0:T(8,128)(2,1)S(1)}, u32[]{:S(2)}, u32[]{:S(2)}) %collective-permute-start.16) | collective-permute-done | bytes 196640 | tf_op jit(solution)/shard_map/ppermute | solution.py:465
  51.3 0.1 add_convert_fusion.2
  51.3 0.9 %collective-permute-start.17 = (bf16[384,256]{1,0:T(8,128)(2,1)S(1)}, bf16[384,256]{1,0:T(8,128)(2,1)S(1)}, u32[]{:S(2)}, u32[]{:S(2)}) collective-permute-start(bf16[384,256]{1,0:T(8,128)(2,1)S(1)} %add_convert_fusion.2), channel_id=1, source_target_pairs={{0,4},{8,0},{16,8},{24,16},{28,24},{20,28},{12,20},{4,12},{1,5},{9... | collective-permute-start | bytes 589832 | tf_op jit(solution)/shard_map/ppermute | solution.py:465
  52.2 0.0 collective-permute-done.12.refs_3_
  52.2 0.1 add_convert_fusion.4
  52.2 1.3 %collective-permute-start.13 = (bf16[384,256]{1,0:T(8,128)(2,1)S(1)}, bf16[384,256]{1,0:T(8,128)(2,1)S(1)}, u32[]{:S(2)}, u32[]{:S(2)}) collective-permute-start(bf16[384,256]{1,0:T(8,128)(2,1)S(1)} %add_convert_fusion.4), channel_id=1, source_target_pairs={{0,8},{8,16},{16,24},{24,28},{28,20},{20,12},{12,4},{4,0},{1,9},{9... | collective-permute-start | bytes 589832 | tf_op jit(solution)/shard_map/ppermute | solution.py:465
  53.5 3.6 %collective-permute-done.17.refs_6_ = bf16[384,256]{1,0:T(8,128)(2,1)S(1)} collective-permute-done((bf16[384,256]{1,0:T(8,128)(2,1)S(1)}, bf16[384,256]{1,0:T(8,128)(2,1)S(1)}, u32[]{:S(2)}, u32[]{:S(2)}) %collective-permute-start.17) | collective-permute-done | bytes 196640 | tf_op jit(solution)/shard_map/ppermute | solution.py:465
  57.1 0.1 add_convert_fusion.1
  57.2 0.8 %collective-permute-start.18 = (bf16[384,256]{1,0:T(8,128)(2,1)S(1)}, bf16[384,256]{1,0:T(8,128)(2,1)S(1)}, u32[]{:S(2)}, u32[]{:S(2)}) collective-permute-start(bf16[384,256]{1,0:T(8,128)(2,1)S(1)} %add_convert_fusion.1), channel_id=1, source_target_pairs={{0,4},{8,0},{16,8},{24,16},{28,24},{20,28},{12,20},{4,12},{1,5},{9... | collective-permute-start | bytes 589832 | tf_op jit(solution)/shard_map/ppermute | solution.py:465
  58.0 0.0 collective-permute-done.13.refs_5_
  58.0 1.3 %collective-permute-start.14 = (bf16[256,256]{1,0:T(8,128)(2,1)S(1)}, bf16[256,256]{1,0:T(8,128)(2,1)S(1)}, u32[]{:S(2)}, u32[]{:S(2)}) collective-permute-start(bf16[256,256]{1,0:T(8,128)(2,1)S(1)} %add_convert_fusion.6), channel_id=1, source_target_pairs={{0,8},{8,16},{16,24},{24,28},{28,20},{20,12},{12,4},{4,0},{1,9},{9... | collective-permute-start | bytes 393224 | tf_op jit(solution)/shard_map/ppermute | solution.py:465
  59.3 3.5 %collective-permute-done.18.refs_2_.refs_7_ = bf16[384,256]{1,0:T(8,128)(2,1)S(1)} collective-permute-done((bf16[384,256]{1,0:T(8,128)(2,1)S(1)}, bf16[384,256]{1,0:T(8,128)(2,1)S(1)}, u32[]{:S(2)}, u32[]{:S(2)}) %collective-permute-start.18) | collective-permute-done | bytes 196640 | tf_op jit(solution)/shard_map/ppermute | solution.py:465
  62.9 0.1 summed_terms.1.own_ref
  63.0 0.1 collective-permute-start.19
  63.1 0.0 collective-permute-done.14.refs_1_
  63.1 0.8 %finish.1 = bf16[256,256]{1,0:T(8,128)(2,1)} custom-call(bf16[256,256]{1,0:T(8,128)(2,1)S(1)} %get-tuple-element.51.refs_0_, bf16[256,256]{1,0:T(8,128)(2,1)S(1)} %collective-permute-done.14.refs_1_, bf16[384,256]{1,0:T(8,128)(2,1)S(1)} %collective-permute-done.18.refs_2_.refs_7_), custom_call_target="tpu_custom_call" | custom-call | flops 196608 | bytes 524288 | tf_op jit(solution)/shard_map/finish/pallas_call | solution.py:429
  63.9 0.6 collective-permute-done.19.sibling_ref
  64.4 0.7 %joined.1 = f32[256,256]{1,0:T(8,128)} custom-call(f32[128,256]{1,0:T(8,128)S(1)} %summed_terms.1.own_ref, f32[128,256]{1,0:T(8,128)S(1)} %collective-permute-done.19.sibling_ref), custom_call_target="tpu_custom_call" | custom-call | bytes 524288 | tf_op jit(solution)/shard_map/joined/pallas_call | solution.py:451
  (3 shorter events, 0.1 us)
Async XLA Ops:
  0.6 6.8 %collective-permute-start.3 = (bf16[256,256]{1,0:T(8,128)(2,1)}, bf16[256,256]{1,0:T(8,128)(2,1)S(1)}, u32[]{:S(2)}, u32[]{:S(2)}) collective-permute-start(bf16[256,256]{1,0:T(8,128)(2,1)} %refs_0_.3), channel_id=1, source_target_pairs={{0,4},{8,0},{16,8},{24,16},{28,24},{20,28},{12,20},{4,12},{1,5},{9... | collective-permute-start | bytes 393224 | tf_op jit(solution)/shard_map/ppermute | solution.py:465
  3.6 5.5 %collective-permute-start = (bf16[256,256]{1,0:T(8,128)(2,1)}, bf16[256,256]{1,0:T(8,128)(2,1)S(1)}, u32[]{:S(2)}, u32[]{:S(2)}) collective-permute-start(bf16[256,256]{1,0:T(8,128)(2,1)} %refs_0_.3), channel_id=1, source_target_pairs={{0,8},{8,16},{16,24},{24,28},{28,20},{20,12},{12,4},{4,0},{1,9},{9... | collective-permute-start | bytes 393224 | tf_op jit(solution)/shard_map/ppermute | solution.py:465
  7.4 5.0 %collective-permute-start.4 = (bf16[256,256]{1,0:T(8,128)(2,1)S(1)}, bf16[256,256]{1,0:T(8,128)(2,1)S(1)}, u32[]{:S(2)}, u32[]{:S(2)}) collective-permute-start(bf16[256,256]{1,0:T(8,128)(2,1)S(1)} %collective-permute-done.3.refs_5_), channel_id=1, source_target_pairs={{0,4},{8,0},{16,8},{24,16},{28,24},{20,28},{12,20},{4,12},{1,5},{9... | collective-permute-start | bytes 393224 | tf_op jit(solution)/shard_map/ppermute | solution.py:465
  9.1 5.0 %collective-permute-start.1 = (bf16[256,256]{1,0:T(8,128)(2,1)S(1)}, bf16[256,256]{1,0:T(8,128)(2,1)S(1)}, u32[]{:S(2)}, u32[]{:S(2)}) collective-permute-start(bf16[256,256]{1,0:T(8,128)(2,1)S(1)} %collective-permute-done.refs_1_), channel_id=1, source_target_pairs={{0,8},{8,16},{16,24},{24,28},{28,20},{20,12},{12,4},{4,0},{1,9},{9... | collective-permute-start | bytes 393224 | tf_op jit(solution)/shard_map/ppermute | solution.py:465
  9.4 5.0 %copy-start.2 = (bf16[256,256]{1,0:T(8,128)(2,1)S(1)}, bf16[256,256]{1,0:T(8,128)(2,1)}, u32[]{:S(2)}) copy-start(bf16[256,256]{1,0:T(8,128)(2,1)} %refs_3_) | copy-start | bytes 393220
  12.2 12.3 %copy-start = (bf16[256,256]{1,0:T(8,128)(2,1)S(1)}, bf16[256,256]{1,0:T(8,128)(2,1)}, u32[]{:S(2)}) copy-start(bf16[256,256]{1,0:T(8,128)(2,1)} %refs_0_.3) | copy-start | bytes 393220
  14.1 5.5 %collective-permute-start.2 = (bf16[256,256]{1,0:T(8,128)(2,1)S(1)}, bf16[256,256]{1,0:T(8,128)(2,1)S(1)}, u32[]{:S(2)}, u32[]{:S(2)}) collective-permute-start(bf16[256,256]{1,0:T(8,128)(2,1)S(1)} %collective-permute-done.1.refs_2_), channel_id=1, source_target_pairs={{0,8},{8,16},{16,24},{24,28},{28,20},{20,12},{12,4},{4,0},{1,9},{9... | collective-permute-start | bytes 393224 | tf_op jit(solution)/shard_map/ppermute | solution.py:465
  14.4 5.1 %collective-permute-start.5 = (bf16[256,256]{1,0:T(8,128)(2,1)S(1)}, bf16[256,256]{1,0:T(8,128)(2,1)S(1)}, u32[]{:S(2)}, u32[]{:S(2)}) collective-permute-start(bf16[256,256]{1,0:T(8,128)(2,1)S(1)} %copy-done.2), channel_id=1, source_target_pairs={{0,2},{1,3},{2,0},{3,1},{4,6},{5,7},{6,4},{7,5},{8,10},{9,11},{10,... | collective-permute-start | bytes 393224 | tf_op jit(solution)/shard_map/ppermute | solution.py:469
  16.1 8.0 %collective-permute-start.7 = (bf16[256,256]{1,0:T(8,128)(2,1)S(1)}, bf16[256,256]{1,0:T(8,128)(2,1)S(1)}, u32[]{:S(2)}, u32[]{:S(2)}) collective-permute-start(bf16[256,256]{1,0:T(8,128)(2,1)S(1)} %collective-permute-done.4.refs_6_), channel_id=1, source_target_pairs={{0,4},{8,0},{16,8},{24,16},{28,24},{20,28},{12,20},{4,12},{1,5},{9... | collective-permute-start | bytes 393224 | tf_op jit(solution)/shard_map/ppermute | solution.py:465
  19.5 5.0 %collective-permute-start.6 = (bf16[256,256]{1,0:T(8,128)(2,1)S(1)}, bf16[256,256]{1,0:T(8,128)(2,1)S(1)}, u32[]{:S(2)}, u32[]{:S(2)}) collective-permute-start(bf16[256,256]{1,0:T(8,128)(2,1)S(1)} %collective-permute-done.2.refs_3_), channel_id=1, source_target_pairs={{0,8},{8,16},{16,24},{24,28},{28,20},{20,12},{12,4},{4,0},{1,9},{9... | collective-permute-start | bytes 393224 | tf_op jit(solution)/shard_map/ppermute | solution.py:465
  25.2 10.1 %copy-start.1 = (bf16[256,256]{1,0:T(8,128)(2,1)S(1)}, bf16[256,256]{1,0:T(8,128)(2,1)}, u32[]{:S(2)}) copy-start(bf16[256,256]{1,0:T(8,128)(2,1)} %refs_2_.1) | copy-start | bytes 393220
  25.2 1.6 %collective-permute-start.8 = (bf16[512,256]{1,0:T(8,128)(2,1)S(1)}, bf16[512,256]{1,0:T(8,128)(2,1)S(1)}, u32[]{:S(2)}, u32[]{:S(2)}) collective-permute-start(bf16[512,256]{1,0:T(8,128)(2,1)S(1)} %forward_product.2), channel_id=1, source_target_pairs={{0,1},{1,0},{2,3},{3,2},{4,5},{5,4},{6,7},{7,6},{8,9},{9,8},{10,11... | collective-permute-start | bytes 786440 | tf_op jit(solution)/shard_map/ppermute | solution.py:469
  26.9 8.4 %collective-permute-start.9 = (bf16[512,256]{1,0:T(8,128)(2,1)S(1)}, bf16[512,256]{1,0:T(8,128)(2,1)S(1)}, u32[]{:S(2)}, u32[]{:S(2)}) collective-permute-start(bf16[512,256]{1,0:T(8,128)(2,1)S(1)} %add_convert_fusion.refs_0_), channel_id=1, source_target_pairs={{0,2},{1,3},{2,0},{3,1},{4,6},{5,7},{6,4},{7,5},{8,10},{9,11},{10,... | collective-permute-start | bytes 786440 | tf_op jit(solution)/shard_map/ppermute | solution.py:469
  36.4 1.8 %collective-permute-start.10 = (bf16[768,256]{1,0:T(8,128)(2,1)S(1)}, bf16[768,256]{1,0:T(8,128)(2,1)S(1)}, u32[]{:S(2)}, u32[]{:S(2)}) collective-permute-start(bf16[768,256]{1,0:T(8,128)(2,1)S(1)} %get-tuple-element.45.own_ref), channel_id=1, source_target_pairs={{0,1},{1,0},{2,3},{3,2},{4,5},{5,4},{6,7},{7,6},{8,9},{9,8},{10,11... | collective-permute-start | bytes 1179656 | tf_op jit(solution)/shard_map/ppermute | solution.py:469
  38.6 5.9 %collective-permute-start.15 = (bf16[256,256]{1,0:T(8,128)(2,1)S(1)}, bf16[256,256]{1,0:T(8,128)(2,1)S(1)}, u32[]{:S(2)}, u32[]{:S(2)}) collective-permute-start(bf16[256,256]{1,0:T(8,128)(2,1)S(1)} %get-tuple-element.59), channel_id=1, source_target_pairs={{0,4},{8,0},{16,8},{24,16},{28,24},{20,28},{12,20},{4,12},{1,5},{9... | collective-permute-start | bytes 393224 | tf_op jit(solution)/shard_map/ppermute | solution.py:465
  40.3 5.6 %collective-permute-start.11 = (bf16[256,256]{1,0:T(8,128)(2,1)S(1)}, bf16[256,256]{1,0:T(8,128)(2,1)S(1)}, u32[]{:S(2)}, u32[]{:S(2)}) collective-permute-start(bf16[256,256]{1,0:T(8,128)(2,1)S(1)} %get-tuple-element.55), channel_id=1, source_target_pairs={{0,8},{8,16},{16,24},{24,28},{28,20},{20,12},{12,4},{4,0},{1,9},{9... | collective-permute-start | bytes 393224 | tf_op jit(solution)/shard_map/ppermute | solution.py:465
  44.6 6.7 %collective-permute-start.16 = (bf16[384,256]{1,0:T(8,128)(2,1)S(1)}, bf16[384,256]{1,0:T(8,128)(2,1)S(1)}, u32[]{:S(2)}, u32[]{:S(2)}) collective-permute-start(bf16[384,256]{1,0:T(8,128)(2,1)S(1)} %add_convert_fusion.3), channel_id=1, source_target_pairs={{0,4},{8,0},{16,8},{24,16},{28,24},{20,28},{12,20},{4,12},{1,5},{9... | collective-permute-start | bytes 589832 | tf_op jit(solution)/shard_map/ppermute | solution.py:465
  46.0 6.2 %collective-permute-start.12 = (bf16[384,256]{1,0:T(8,128)(2,1)S(1)}, bf16[384,256]{1,0:T(8,128)(2,1)S(1)}, u32[]{:S(2)}, u32[]{:S(2)}) collective-permute-start(bf16[384,256]{1,0:T(8,128)(2,1)S(1)} %add_convert_fusion.5), channel_id=1, source_target_pairs={{0,8},{8,16},{16,24},{24,28},{28,20},{20,12},{12,4},{4,0},{1,9},{9... | collective-permute-start | bytes 589832 | tf_op jit(solution)/shard_map/ppermute | solution.py:465
  51.3 5.8 %collective-permute-start.17 = (bf16[384,256]{1,0:T(8,128)(2,1)S(1)}, bf16[384,256]{1,0:T(8,128)(2,1)S(1)}, u32[]{:S(2)}, u32[]{:S(2)}) collective-permute-start(bf16[384,256]{1,0:T(8,128)(2,1)S(1)} %add_convert_fusion.2), channel_id=1, source_target_pairs={{0,4},{8,0},{16,8},{24,16},{28,24},{20,28},{12,20},{4,12},{1,5},{9... | collective-permute-start | bytes 589832 | tf_op jit(solution)/shard_map/ppermute | solution.py:465
  52.2 5.7 %collective-permute-start.13 = (bf16[384,256]{1,0:T(8,128)(2,1)S(1)}, bf16[384,256]{1,0:T(8,128)(2,1)S(1)}, u32[]{:S(2)}, u32[]{:S(2)}) collective-permute-start(bf16[384,256]{1,0:T(8,128)(2,1)S(1)} %add_convert_fusion.4), channel_id=1, source_target_pairs={{0,8},{8,16},{16,24},{24,28},{28,20},{20,12},{12,4},{4,0},{1,9},{9... | collective-permute-start | bytes 589832 | tf_op jit(solution)/shard_map/ppermute | solution.py:465
  57.2 5.7 %collective-permute-start.18 = (bf16[384,256]{1,0:T(8,128)(2,1)S(1)}, bf16[384,256]{1,0:T(8,128)(2,1)S(1)}, u32[]{:S(2)}, u32[]{:S(2)}) collective-permute-start(bf16[384,256]{1,0:T(8,128)(2,1)S(1)} %add_convert_fusion.1), channel_id=1, source_target_pairs={{0,4},{8,0},{16,8},{24,16},{28,24},{20,28},{12,20},{4,12},{1,5},{9... | collective-permute-start | bytes 589832 | tf_op jit(solution)/shard_map/ppermute | solution.py:465
  58.0 5.1 %collective-permute-start.14 = (bf16[256,256]{1,0:T(8,128)(2,1)S(1)}, bf16[256,256]{1,0:T(8,128)(2,1)S(1)}, u32[]{:S(2)}, u32[]{:S(2)}) collective-permute-start(bf16[256,256]{1,0:T(8,128)(2,1)S(1)} %add_convert_fusion.6), channel_id=1, source_target_pairs={{0,8},{8,16},{16,24},{24,28},{28,20},{20,12},{12,4},{4,0},{1,9},{9... | collective-permute-start | bytes 393224 | tf_op jit(solution)/shard_map/ppermute | solution.py:465
  63.0 1.4 %collective-permute-start.19 = (f32[128,256]{1,0:T(8,128)S(1)}, f32[128,256]{1,0:T(8,128)S(1)}, u32[]{:S(2)}, u32[]{:S(2)}) collective-permute-start(f32[128,256]{1,0:T(8,128)S(1)} %summed_terms.1.own_ref), channel_id=1, source_target_pairs={{0,1},{1,0},{2,3},{3,2},{4,5},{5,4},{6,7},{7,6},{8,9},{9,8},{10,11... | collective-permute-start | bytes 393224 | tf_op jit(solution)/shard_map/ppermute | solution.py:469
